TPU v7x, 32 devices: a whole 2x2x4 slice. The times are simulated.
32 devices in a mesh: dp: 16 (over z, x, core), shard: 2 (over y).
Axes of the slice: x: 2, y: 2, z: 4, core: 2. Of those that a mesh axis runs over, the one named last changes fastest.
Arguments:
- tokens: bfloat16 [32, 128, 576], P(('dp', 'shard')), may hold values from -6 to 6
- segments: int32 [32, 128], P(('dp', 'shard')), may hold values from 0 to 1, never falling along the last dimension, each value on 1 to 96 neighbouring positions
- cotangent: bfloat16 [32, 128, 576], P(('dp', 'shard')), may hold values from -6 to 6
- w_qkv: float32 [576, 960], P('shard'), may hold values from -0.25 to 0.25
- w_out: float32 [576, 576], P('shard'), may hold values from -1 to 1
- w_gate_up: float32 [576, 3072], P('shard'), may hold values from -0.25 to 0.25
- w_down: float32 [1536, 576], P('shard'), may hold values from -0.15625 to 0.15625
- norm_gains: float32 [2, 576], P(None, 'shard'), may hold values from 0.5 to 1.5
- first_qkv: float32 [576, 960], P('shard'), may hold values from -12 to 12
- first_out: float32 [576, 576], P('shard'), may hold values from -8 to 8
- first_gate_up: float32 [576, 3072], P('shard'), may hold values from -16 to 16
- first_down: float32 [1536, 576], P('shard'), may hold values from -24 to 24
- first_gains: float32 [2, 576], P(None, 'shard'), may hold values from -32 to 32
- second_qkv: float32 [576, 960], P('shard'), may hold values from 18.432 to 73.728
- second_out: float32 [576, 576], P('shard'), may hold values from 8.192 to 32.768
- second_gate_up: float32 [576, 3072], P('shard'), may hold values from 32.768 to 131.072
- second_down: float32 [1536, 576], P('shard'), may hold values from 73.728 to 294.912
- second_gains: float32 [2, 576], P(None, 'shard'), may hold values from 102.4 to 409.6
Outputs:
- output: bfloat16 [32, 128, 576], P(('dp', 'shard'))
- token_grad: bfloat16 [32, 128, 576], P(('dp', 'shard'))
- new_first_qkv: float32 [576, 960], P('shard')
- new_first_out: float32 [576, 576], P('shard')
- new_first_gate_up: float32 [576, 3072], P('shard')
- new_first_down: float32 [1536, 576], P('shard')
- new_first_gains: float32 [2, 576], P(None, 'shard')
- new_second_qkv: float32 [576, 960], P('shard')
- new_second_out: float32 [576, 576], P('shard')
- new_second_gate_up: float32 [576, 3072], P('shard')
- new_second_down: float32 [1536, 576], P('shard')
- new_second_gains: float32 [2, 576], P(None, 'shard')
- new_qkv: float32 [576, 960], P('shard')
- new_out: float32 [576, 576], P('shard')
- new_gate_up: float32 [576, 3072], P('shard')
- new_down: float32 [1536, 576], P('shard')
- new_gains: float32 [2, 576], P(None, 'shard')
Inputs may be any that keep to these rules, and one draw needn't show every extreme that they name: `segments`: within each sequence segment numbers start at 0, never fall and rise by at most one from token to token; each document has at most 96 tokens.
All inputs are finite; a program needn't handle non-finite values.
Results may differ from a plain program's by a relative error of at most 0.012.
The roundings to bfloat16 on the way count: a program that leaves them out, or rounds other values in their place, can miss the bound.
Values may be sent and summed in bfloat16 or wider, within the bound.
No kernel may reach another device: no remote copies, remote signals or barrier semaphores. Data moves between devices by JAX's collectives and lax.ppermute only.
A program may use at most 192 MiB of HBM per device.

v0:
```python
import jax
import jax.numpy as jnp
from jax import lax
from jax.sharding import PartitionSpec as P

HEADS = 9
KV_HEADS = 3
HEAD = 64
FF = 1536
STEP = 10


EPS_NORM = 1e-05
ROPE_BASE = 100000.0
BETA_ONE = 0.9
BETA_TWO = 0.95
RATE_MATRIX = 0.1
RATE_GAIN = 0.3
DECAY_MATRIX = 0.1
EPS_ADAM = 1e-08
MASKED = -1e30


def doc_positions(segments):
    seq_length = segments.shape[-1]
    token_index = jnp.arange(seq_length, dtype=jnp.int32)
    earlier = jnp.concatenate([segments[..., :1] - 1, segments[..., :-1]], axis=-1)
    starts = jnp.where(segments != earlier, token_index, jnp.zeros_like(token_index))
    return token_index - lax.cummax(starts, axis=segments.ndim - 1)


def rope_tables(segments):
    positions = doc_positions(segments).astype(jnp.float32)
    half_size = HEAD // 2
    frequency = ROPE_BASE ** (-(jnp.arange(half_size, dtype=jnp.float32) * 2.0 / HEAD))
    angles = positions[..., None] * frequency
    return (jnp.cos(angles), jnp.sin(angles))


def rotate(values, cosine, sine_table):
    half_size = values.shape[-1] // 2
    first_half = values[..., :half_size]
    second_half = values[..., half_size:]
    return jnp.concatenate(
        [
            first_half * cosine - second_half * sine_table,
            second_half * cosine + first_half * sine_table,
        ],
        axis=-1,
    )


def unrotate(grad_values, cosine, sine_table):
    half_size = grad_values.shape[-1] // 2
    first_half = grad_values[..., :half_size]
    second_half = grad_values[..., half_size:]
    return jnp.concatenate(
        [
            first_half * cosine + second_half * sine_table,
            second_half * cosine - first_half * sine_table,
        ],
        axis=-1,
    )


def norm_back(grad_normed, normed, scale_rows):
    return scale_rows * (
        grad_normed - normed * jnp.mean(grad_normed * normed, axis=-1, keepdims=True)
    )


def adamw(weight, first_moment, second_moment, gradient, step_rate, weight_decay):
    first_new = BETA_ONE * first_moment + (1.0 - BETA_ONE) * gradient
    second_new = BETA_TWO * second_moment + (1.0 - BETA_TWO) * gradient * gradient
    fix_one = 1.0 - BETA_ONE**STEP
    fix_two = 1.0 - BETA_TWO**STEP
    update = first_new / fix_one / (jnp.sqrt(second_new / fix_two) + EPS_ADAM)
    return (first_new, second_new, weight - step_rate * (update + weight_decay * weight))


def owner_blocks(grad_values, groups):
    pieces = [matrix.reshape(groups, -1) for matrix in grad_values[:4]]
    gain_grads = grad_values[4]
    pieces.append(gain_grads.reshape(2, groups, -1).transpose(1, 0, 2).reshape(groups, -1))
    return jnp.concatenate(pieces, axis=1)


def per_device(
    tokens,
    segments,
    cotangent,
    w_qkv,
    w_out,
    w_gate_up,
    w_down,
    norm_gains,
    first_qkv,
    first_out,
    first_gate_up,
    first_down,
    first_gains,
    second_qkv,
    second_out,
    second_gate_up,
    second_down,
    second_gains,
):
    mat_qkv, mat_out, mat_gate_up, mat_down, gains_full = (
        lax.all_gather(w_qkv.astype(jnp.bfloat16), "shard", axis=0, tiled=True),
        lax.all_gather(w_out.astype(jnp.bfloat16), "shard", axis=0, tiled=True),
        lax.all_gather(w_gate_up.astype(jnp.bfloat16), "shard", axis=0, tiled=True),
        lax.all_gather(w_down.astype(jnp.bfloat16), "shard", axis=0, tiled=True),
        lax.all_gather(norm_gains.astype(jnp.bfloat16), "shard", axis=1, tiled=True),
    )
    gain_one = gains_full[0].astype(jnp.float32)
    gain_two = gains_full[1].astype(jnp.float32)
    seq_count, seq_length, model_width = tokens.shape
    group_size = HEADS // KV_HEADS
    scale_score = float(HEAD) ** (-0.5)
    token_values = tokens.astype(jnp.float32)
    scale_one = lax.rsqrt(jnp.mean(token_values * token_values, axis=-1, keepdims=True) + EPS_NORM)
    normed_one = token_values * scale_one
    normed_one_low = (normed_one * gain_one).astype(jnp.bfloat16)
    projected = jnp.einsum(
        "bld,de->ble", normed_one_low, mat_qkv, preferred_element_type=jnp.float32
    )
    query_part = projected[..., : HEADS * HEAD].reshape(
        seq_count, seq_length, KV_HEADS, group_size, HEAD
    )
    key_part = projected[..., HEADS * HEAD : (HEADS + KV_HEADS) * HEAD].reshape(
        seq_count, seq_length, KV_HEADS, HEAD
    )
    value_part = projected[..., (HEADS + KV_HEADS) * HEAD :].reshape(
        seq_count, seq_length, KV_HEADS, HEAD
    )
    cosine, sine_table = rope_tables(segments)
    cos_query = cosine[:, :, None, None]
    sin_query = sine_table[:, :, None, None]
    cos_key = cosine[:, :, None]
    sin_key = sine_table[:, :, None]
    query_low = rotate(query_part, cos_query, sin_query).astype(jnp.bfloat16)
    key_low = rotate(key_part, cos_key, sin_key).astype(jnp.bfloat16)
    value_low = value_part.astype(jnp.bfloat16)
    token_index = jnp.arange(seq_length, dtype=jnp.int32)
    allowed = (segments[:, :, None] == segments[:, None, :]) & (
        token_index[:, None] >= token_index[None, :]
    )

    def masked_scores():
        raw_scores = (
            jnp.einsum("blhrc,bmhc->bhrlm", query_low, key_low, preferred_element_type=jnp.float32)
            * scale_score
        )
        return jnp.where(allowed[:, None, None], raw_scores, MASKED)

    scores = masked_scores()
    row_top = jnp.max(scores, axis=-1, keepdims=True)
    exponent = jnp.exp(scores - row_top)
    row_total = jnp.sum(exponent, axis=-1, keepdims=True)
    log_total = row_top + jnp.log(row_total)
    probs_low = (exponent / row_total).astype(jnp.bfloat16)
    attended = jnp.einsum(
        "bhrlm,bmhc->blhrc", probs_low, value_low, preferred_element_type=jnp.float32
    )
    attended_low = attended.reshape(seq_count, seq_length, HEADS * HEAD).astype(jnp.bfloat16)
    branch = jnp.einsum("blk,kd->bld", attended_low, mat_out, preferred_element_type=jnp.float32)
    middle = token_values + branch
    scale_two = lax.rsqrt(jnp.mean(middle * middle, axis=-1, keepdims=True) + EPS_NORM)
    normed_two = middle * scale_two
    normed_two_low = (normed_two * gain_two).astype(jnp.bfloat16)
    gate_up_out = jnp.einsum(
        "bld,de->ble", normed_two_low, mat_gate_up, preferred_element_type=jnp.float32
    )
    gate_part = gate_up_out[..., :FF]
    up_part = gate_up_out[..., FF:]
    sigmoid_gate = jax.nn.sigmoid(gate_part)
    hidden_low = (gate_part * sigmoid_gate * up_part).astype(jnp.bfloat16)
    result = jnp.einsum("blf,fd->bld", hidden_low, mat_down, preferred_element_type=jnp.float32)
    output = (middle + result).astype(jnp.bfloat16)
    grad_result = cotangent.astype(jnp.float32)
    grad_down = jnp.einsum("blf,bld->fd", hidden_low, cotangent, preferred_element_type=jnp.float32)
    grad_hidden = jnp.einsum("bld,fd->blf", cotangent, mat_down, preferred_element_type=jnp.float32)
    grad_gate = grad_hidden * up_part * sigmoid_gate * (1.0 + gate_part * (1.0 - sigmoid_gate))
    grad_up = grad_hidden * gate_part * sigmoid_gate
    grad_gated_low = jnp.concatenate([grad_gate, grad_up], axis=-1).astype(jnp.bfloat16)
    grad_gate_up = jnp.einsum(
        "bld,ble->de", normed_two_low, grad_gated_low, preferred_element_type=jnp.float32
    )
    grad_normed_two = jnp.einsum(
        "ble,de->bld", grad_gated_low, mat_gate_up, preferred_element_type=jnp.float32
    )
    grad_gain_two = jnp.sum(grad_normed_two * normed_two, axis=(0, 1))
    grad_middle = grad_result + norm_back(grad_normed_two * gain_two, normed_two, scale_two)
    grad_branch_low = grad_middle.astype(jnp.bfloat16)
    grad_out = jnp.einsum(
        "blk,bld->kd", attended_low, grad_branch_low, preferred_element_type=jnp.float32
    )
    grad_attended = jnp.einsum(
        "bld,kd->blk", grad_branch_low, mat_out, preferred_element_type=jnp.float32
    )
    grad_attended_low = grad_attended.astype(jnp.bfloat16).reshape(
        seq_count, seq_length, KV_HEADS, group_size, HEAD
    )
    attn_probs = jnp.exp(masked_scores() - log_total)
    probs_again = attn_probs.astype(jnp.bfloat16)
    grad_probs = jnp.einsum(
        "blhrc,bmhc->bhrlm", grad_attended_low, value_low, preferred_element_type=jnp.float32
    )
    row_delta = jnp.sum(attn_probs * grad_probs, axis=-1, keepdims=True)
    grad_scores_low = (attn_probs * (grad_probs - row_delta)).astype(jnp.bfloat16)
    grad_value = jnp.einsum(
        "bhrlm,blhrc->bmhc", probs_again, grad_attended_low, preferred_element_type=jnp.float32
    )
    grad_query = (
        jnp.einsum(
            "bhrlm,bmhc->blhrc", grad_scores_low, key_low, preferred_element_type=jnp.float32
        )
        * scale_score
    )
    grad_key = (
        jnp.einsum(
            "bhrlm,blhrc->bmhc", grad_scores_low, query_low, preferred_element_type=jnp.float32
        )
        * scale_score
    )
    grad_query = unrotate(grad_query, cos_query, sin_query).reshape(
        seq_count, seq_length, HEADS * HEAD
    )
    grad_key = unrotate(grad_key, cos_key, sin_key).reshape(seq_count, seq_length, KV_HEADS * HEAD)
    grad_projected_low = jnp.concatenate(
        [grad_query, grad_key, grad_value.reshape(seq_count, seq_length, KV_HEADS * HEAD)], axis=-1
    ).astype(jnp.bfloat16)
    grad_qkv = jnp.einsum(
        "bld,ble->de", normed_one_low, grad_projected_low, preferred_element_type=jnp.float32
    )
    grad_normed_one = jnp.einsum(
        "ble,de->bld", grad_projected_low, mat_qkv, preferred_element_type=jnp.float32
    )
    grad_gain_one = jnp.sum(grad_normed_one * normed_one, axis=(0, 1))
    token_grad = (
        grad_middle + norm_back(grad_normed_one * gain_one, normed_one, scale_one)
    ).astype(jnp.bfloat16)
    groups = lax.axis_size("shard")
    replicas = lax.axis_size("dp")
    blocks = owner_blocks(
        (grad_qkv, grad_out, grad_gate_up, grad_down, jnp.stack([grad_gain_one, grad_gain_two])),
        groups,
    )
    block_length = blocks.shape[1]
    piece_length = -(-block_length // replicas)
    padded_length = piece_length * replicas
    blocks = jnp.pad(blocks, ((0, 0), (0, padded_length - block_length)))
    arranged = blocks.reshape(groups, replicas, piece_length).transpose(1, 0, 2)
    traded = lax.all_to_all(arranged, "dp", split_axis=0, concat_axis=0, tiled=True)
    replica_sum = jnp.sum(traded, axis=0)
    piece_sum = lax.psum_scatter(replica_sum, "shard", scatter_dimension=0, tiled=True).reshape(
        piece_length
    )
    owned = lax.all_gather(piece_sum, "dp", axis=0, tiled=True)
    masters = (w_qkv, w_out, w_gate_up, w_down, norm_gains)
    owned_grads = []
    offset = 0
    for weight in masters:
        entry_count = weight.shape[0] * weight.shape[1]
        owned_grads.append(owned[offset : offset + entry_count].reshape(weight.shape))
        offset = offset + entry_count
    one_qkv, two_qkv, next_qkv = adamw(
        w_qkv, first_qkv, second_qkv, owned_grads[0], RATE_MATRIX, DECAY_MATRIX
    )
    one_out, two_out, next_out = adamw(
        w_out, first_out, second_out, owned_grads[1], RATE_MATRIX, DECAY_MATRIX
    )
    one_gate_up, two_gate_up, next_gate_up = adamw(
        w_gate_up, first_gate_up, second_gate_up, owned_grads[2], RATE_MATRIX, DECAY_MATRIX
    )
    one_down, two_down, next_down = adamw(
        w_down, first_down, second_down, owned_grads[3], RATE_MATRIX, DECAY_MATRIX
    )
    one_gains, two_gains, next_gains = adamw(
        norm_gains, first_gains, second_gains, owned_grads[4], RATE_GAIN, 0.0
    )
    return (
        output,
        token_grad,
        one_qkv,
        one_out,
        one_gate_up,
        one_down,
        one_gains,
        two_qkv,
        two_out,
        two_gate_up,
        two_down,
        two_gains,
        next_qkv,
        next_out,
        next_gate_up,
        next_down,
        next_gains,
    )


def solution(mesh):
    return jax.shard_map(
        per_device,
        mesh=mesh,
        in_specs=(
            P(("dp", "shard"), None, None),
            P(("dp", "shard"), None),
            P(("dp", "shard"), None, None),
            P("shard", None),
            P("shard", None),
            P("shard", None),
            P("shard", None),
            P(None, "shard"),
            P("shard", None),
            P("shard", None),
            P("shard", None),
            P("shard", None),
            P(None, "shard"),
            P("shard", None),
            P("shard", None),
            P("shard", None),
            P("shard", None),
            P(None, "shard"),
        ),
        out_specs=(
            P(("dp", "shard"), None, None),
            P(("dp", "shard"), None, None),
            P("shard", None),
            P("shard", None),
            P("shard", None),
            P("shard", None),
            P(None, "shard"),
            P("shard", None),
            P("shard", None),
            P("shard", None),
            P("shard", None),
            P(None, "shard"),
            P("shard", None),
            P("shard", None),
            P("shard", None),
            P("shard", None),
            P(None, "shard"),
        ),
        check_vma=False,
    )
```

profile of v0, /device:TPU:0, one launch (start us, length us, event | category | flops | bytes accessed | tf_op | source)
XLA Modules:
  0.0 936.8 jit_solution(14043071552615770470)
XLA Ops:
  7.2 2.2 convert_element_type.133
  9.5 3.5 convert_element_type.145
  15.5 5.2 all-gather.1
  21.7 19.3 %all_gather.20 = bf16[576,576]{1,0:T(8,128)(2,1)S(1)} all-gather(bf16[288,576]{1,0:T(8,128)(2,1)S(1)} %convert_element_type.141), channel_id=1, replica_groups=mesh['dp'=16,'shard'=2] {'shard'}, dimensions={0}, use_global_device_ids=true | all-gather | bytes 995328 | tf_op jit(solution)/shard_map/all_gather | solution.py:110
  41.1 2.5 all-gather.6.cloned.1.call-done
  43.6 2.0 convolution_bitcast_fusion.3
  46.9 48.1 %all-gather.8.cloned.1.call-done = bf16[576,3072]{1,0:T(8,128)(2,1)} async-done(((bf16[288,3072]{1,0:T(8,128)(2,1)}), bf16[576,3072]{1,0:T(8,128)(2,1)}) %all-gather.8.cloned.1.call-update) | async-done | bytes 3538960 | tf_op jit(solution)/shard_map/all_gather | solution.py:111
  95.1 4.1 convolution_bitcast_fusion
  99.2 27.5 %all-gather.10.cloned.1.call-done = bf16[1536,576]{0,1:T(8,128)(2,1)} async-done(((bf16[768,576]{0,1:T(8,128)(2,1)}), bf16[1536,576]{0,1:T(8,128)(2,1)}) %all-gather.10.cloned.1.call-update) | async-done | bytes 1769488 | tf_op jit(solution)/shard_map/all_gather | solution.py:112
  126.7 2.8 fusion.25
  134.0 4.0 fusion.14
  139.4 3.5 reshape.591
  142.8 4.0 constant_dynamic-update-slice_fusion.4
  146.9 2.3 reshape.592
  149.2 11.9 %reshape.593 = f32[2,884736]{1,0:T(2,128)} reshape(f32[576,3072]{1,0:T(8,128)} %fusion.14) | data formatting | bytes 14155776 | tf_op jit(solution)/shard_map/reshape | solution.py:82
  161.1 2.7 fusion.21
  163.8 5.5 reshape.594
  169.3 3.5 fusion.32
  175.7 2.2 constant_dynamic-update-slice_fusion.3
  177.8 6.7 constant_dynamic-update-slice_fusion.2
  184.5 2.3 constant_dynamic-update-slice_fusion.1
  187.4 32.1 %reshape.655 = f32[3540096]{0:T(1024)} reshape(f32[2,1770048]{1,0:T(2,128)} %constant_dynamic-update-slice_fusion) | data formatting | bytes 28320768
  219.5 19.2 %reshape.596 = f32[2,16,110628]{2,1,0:T(8,128)} reshape(f32[3540096]{0:T(1024)} %reshape.655) | data formatting | bytes 28320768 | tf_op jit(solution)/shard_map/reshape | solution.py:253
  238.7 24.1 %copy.75 = f32[16,2,110628]{2,1,0:T(2,128)S(1)} copy(f32[16,2,110628]{2,0,1:T(8,128)} %bitcast.172) | data formatting | bytes 28320768 | tf_op jit(solution)/shard_map/transpose | solution.py:253
  262.8 314.1 %all_to_all.5 = f32[16,2,110628]{2,1,0:T(2,128)} all-to-all(f32[16,2,110628]{2,1,0:T(2,128)S(1)} %copy.75), channel_id=1, replica_groups=mesh['dp'=16,'shard'=2] {'dp'}, dimensions={0} | all-to-all | bytes 28320768 | tf_op jit(solution)/shard_map/all_to_all | solution.py:254
  576.9 10.3 %reduce_sum.89 = f32[2,110628]{1,0:T(2,128)} reduce(f32[16,2,110628]{2,1,0:T(2,128)} %all_to_all.5, f32[]{:T(128)} %constant.20.clone.1), dimensions={0}, to_apply=%region_10.11 | reduce | flops 3318840 | bytes 15045412 | tf_op jit(solution)/shard_map/reduce_sum | solution.py:255
  589.2 33.3 %all-reduce.7.cloned.1.call-done = f32[2,110628]{1,0:T(2,128)} async-done(((f32[2,110628]{1,0:T(2,128)}), f32[2,110628]{1,0:T(2,128)}) %all-reduce.7.cloned.1.call-update) | async-done | bytes 885040
  622.5 3.1 dynamic-slice_reduce_fusion
  625.6 3.1 broadcast.236
  628.7 4.6 dynamic-update-slice
  636.6 1.8 copy.76
  638.4 3.4 copy.77
  644.0 141.6 %all-reduce.5.cloned.1.call-done = f32[1770048]{0:T(1024)} async-done(((f32[1770048]{0:T(1024)}), f32[1770048]{0:T(1024)}) %all-reduce.5.cloned.1.call-update) | async-done | bytes 7080208
  785.6 27.1 %reshape.618 = f32[1,1770048]{1,0:T(1,128)S(1)} reshape(f32[1770048]{0:T(1024)} %all-reduce.5.cloned.1.call-done) | data formatting | bytes 14160384
  812.7 38.4 %slice_reduce_fusion = f32[884736]{0:T(1024)} fusion(f32[1,1770048]{1,0:T(1,128)S(1)} %reshape.618), kind=kLoop, calls=%fused_computation.3 | loop fusion | bytes 7077888 | tf_op jit(solution)/shard_map/slice | solution.py:265
  851.1 19.6 %slice_reduce_fusion.1 = f32[442368]{0:T(1024)} fusion(f32[1,1770048]{1,0:T(1,128)S(1)} %reshape.618), kind=kLoop, calls=%fused_computation.11 | loop fusion | bytes 3538944 | tf_op jit(solution)/shard_map/slice | solution.py:265
  870.7 12.4 %slice_reduce_fusion.2 = f32[276480]{0:T(1024)} fusion(f32[1,1770048]{1,0:T(1,128)S(1)} %reshape.618), kind=kLoop, calls=%fused_computation.35 | loop fusion | bytes 2211840 | tf_op jit(solution)/shard_map/slice | solution.py:265
  883.1 7.7 slice_reduce_fusion.3
  890.8 3.0 reshape.600
  893.8 3.0 reshape.601
  896.8 6.8 multiply_subtract_fusion.1
  903.6 2.8 copy.80
  906.3 2.8 copy.81
  909.1 2.8 copy.82
  911.8 2.6 reshape.598
  914.4 2.2 reshape.599
  916.7 8.1 multiply_subtract_fusion
  925.0 2.5 multiply_subtract_fusion.2
  (145 shorter events, 23.4 us)
Async XLA Ops:
  7.2 36.4 %all-gather.6.cloned.1.call-start = ((), (), s32[]{:S(2)}) async-start(), calls=%async_computation.1 | async-start | bytes 1769472 | tf_op jit(solution)/shard_map/all_gather | solution.py:109
  9.4 85.6 %all-gather.8.cloned.1.call-start = ((), (), s32[]{:S(2)}) async-start(), calls=%async_computation.2 | async-start | bytes 5308416 | tf_op jit(solution)/shard_map/all_gather | solution.py:111
  12.9 1.5 copy-start.2
  13.0 2.5 copy-start.29
  13.0 7.9 copy-start.9
  13.0 8.0 copy-start.31
  13.0 8.6 copy-start.12
  13.0 113.6 %all-gather.10.cloned.1.call-start = ((), (), s32[]{:S(2)}) async-start(), calls=%async_computation.3 | async-start | bytes 2654208 | tf_op jit(solution)/shard_map/all_gather | solution.py:112
  15.4 607.0 %all-reduce.7.cloned.1.call-start = ((), (), s32[]{:S(2)}) async-start(), calls=%async_computation.5 | async-start | bytes 1771520
  21.0 148.3 %copy-start.32 = (f32[128]{0:T(128)}, f32[128]{0:T(128)S(1)}, u32[]{:S(2)}) copy-start(f32[128]{0:T(128)S(1)} %add_rsqrt_fusion.1) | copy-start | bytes 1540
  46.9 87.1 %copy-start = (f32[1,128,576]{1,2,0:T(8,128)}, f32[1,128,576]{1,2,0:T(8,128)S(1)}, u32[]{:S(2)}) copy-start(f32[1,128,576]{1,2,0:T(8,128)S(1)} %get-tuple-element.105) | copy-start | bytes 884740
  95.1 31.6 %copy-start.23 = (bf16[1,128,576]{1,2,0:T(8,128)(2,1)S(1)}, bf16[1,128,576]{1,2,0:T(8,128)(2,1)}, u32[]{:S(2)}) copy-start(bf16[1,128,576]{1,2,0:T(8,128)(2,1)} %param.20) | copy-start | bytes 442372
  126.7 3.0 copy-start.11
  129.5 31.6 %copy-start.17 = (bf16[1,128,1536]{2,1,0:T(8,128)(2,1)}, bf16[1,128,1536]{2,1,0:T(8,128)(2,1)S(1)}, u32[]{:S(2)}) copy-start(bf16[1,128,1536]{2,1,0:T(8,128)(2,1)S(1)} %get-tuple-element.91) | copy-start | bytes 1179652
  131.0 1.6 copy-start.7
  132.6 5.7 copy-start.26
  138.2 0.7 copy-start.24
  138.2 0.6 copy-start.27
  142.8 4.0 copy-start.4
  184.5 2.3 copy-start.28
  576.9 10.4 %copy-start.37 = (u32[32]{0:T(128)S(1)}, u32[32]{0:T(128)}, u32[]{:S(2)}) copy-start(u32[32]{0:T(128)} %constant.49) | copy-start | bytes 388
  576.9 11.0 %copy-start.36 = (u32[32]{0:T(128)S(1)}, u32[32]{0:T(128)}, u32[]{:S(2)}) copy-start(u32[32]{0:T(128)} %constant.43) | copy-start | bytes 388
  587.3 198.3 %all-reduce.5.cloned.1.call-start = ((), (), s32[]{:S(2)}) async-start(), calls=%async_computation.4 | async-start | bytes 14163968
  633.4 1.5 copy-start.3
  634.8 1.8 copy-start.15
  638.4 3.5 copy-start.38
  638.4 3.5 copy-start.8
  638.4 3.5 copy-start.10
  638.4 3.5 copy-start.25
  638.4 3.5 copy-start.33
  638.4 4.3 copy-start.1
  638.4 4.3 copy-start.16
  638.4 4.3 copy-start.18
  916.6 8.1 copy-start.5
  916.6 8.1 copy-start.6
  916.6 8.1 copy-start.19
  916.7 8.3 copy-start.20
  924.9 2.5 copy-start.13
  924.9 2.5 copy-start.14
  925.0 2.5 copy-start.21
  925.0 2.8 copy-start.22
  927.7 1.7 copy-start.30
  927.7 1.7 copy-start.34
  927.7 1.7 copy-start.35
Sparse Core Ops, SparseCore 0:
  10.1 33.4 all-gather.5
  45.7 49.3 all-gather.7
  97.2 29.4 all-gather.9
  587.4 35.0 all-reduce.6
  633.5 152.0 all-reduce.4
where the time goes:
time: 946 us; the launch traced here: 937 us
  blocking collectives  339 us (36%)
  local copies, waits for them, and re-layouts  264 us (28%)
  waiting for transfers between devices  253 us (27%)
  other arithmetic  39.5 us (4%)
  matrix products  26 us (3%)
  between operations  15.3 us (2%)
    all_to_all x1, blocking collectives, per_device(): lax.all_to_all(arranged, 'dp', split_axis=0, concat_axis=0, tiled=True)  314 us
    unnamed x7, waiting for transfers between devices  175 us
    unnamed x96, local copies, waits for them, and re-layouts  106 us
    slice x5, local copies, waits for them, and re-layouts, per_device(): owned_grads.append(owned[offset:offset + entry_count].reshape(weight.shape))  78.1 us
    all_gather x1, waiting for transfers between devices, per_device(): lax.all_gather(w_gate_up.astype(jnp.bfloat16), 'shard', axis=0, tiled=True)  48.1 us
    all_gather x1, waiting for transfers between devices, per_device(): lax.all_gather(w_down.astype(jnp.bfloat16), 'shard', axis=0, tiled=True)  27.5 us
    transpose x1, local copies, waits for them, and re-layouts, per_device(): arranged = blocks.reshape(groups, replicas, piece_length).transpose(1, 0, 2)  24.1 us
    reshape x4, local copies, waits for them, and re-layouts, owner_blocks(): pieces = [matrix.reshape(groups, -1) for matrix in grad_values[:4]]  23.2 us
  transfers between devices with their start and end apart: 5, of which 5 were waited for; matrix products, arithmetic and copies ran while one was open for 2% of the time, Pallas kernels for 0%

commit v1 on v0

v1 whole, which is shorter than its diff:
```python
import functools

import jax
import jax.numpy as jnp
from jax import lax
from jax.experimental import pallas as pl
from jax.experimental.pallas import tpu as pltpu
from jax.sharding import PartitionSpec as P

HEADS = 9
KV_HEADS = 3
GROUP = HEADS // KV_HEADS
HEAD = 64
FF = 1536
STEP = 10
QUERY = HEADS * HEAD
ROPED = (HEADS + KV_HEADS) * HEAD
QKV = (HEADS + 2 * KV_HEADS) * HEAD
LANES = 128

EPS_NORM = 1e-05
ROPE_BASE = 100000.0
BETA_ONE = 0.9
BETA_TWO = 0.95
RATE_MATRIX = 0.1
RATE_GAIN = 0.3
DECAY_MATRIX = 0.1
EPS_ADAM = 1e-08
MASKED = -1e30
SCALE = float(HEAD) ** (-0.5)
VMEM_LIMIT = 56 * 1024 * 1024
F32 = jnp.float32
BF16 = jnp.bfloat16


def doc_positions(segments):
    seq_length = segments.shape[-1]
    token_index = jnp.arange(seq_length, dtype=jnp.int32)
    earlier = jnp.concatenate([segments[..., :1] - 1, segments[..., :-1]], axis=-1)
    starts = jnp.where(segments != earlier, token_index, jnp.zeros_like(token_index))
    return token_index - lax.cummax(starts, axis=segments.ndim - 1)


def rope_tables(segments):
    positions = doc_positions(segments).astype(F32)
    half_size = HEAD // 2
    frequency = ROPE_BASE ** (-(jnp.arange(half_size, dtype=F32) * 2.0 / HEAD))
    angles = positions[:, None] * frequency
    cosine, sine = jnp.cos(angles), jnp.sin(angles)
    return (
        jnp.concatenate([cosine] * 4, axis=-1),
        jnp.concatenate([-sine, sine, -sine, sine], axis=-1),
    )


def rotate_block(values, cosine, signed_sine):
    lane = lax.broadcasted_iota(jnp.int32, values.shape, 1)
    swapped = jnp.where(
        lane % HEAD < HEAD // 2,
        pltpu.roll(values, LANES - HEAD // 2, 1),
        pltpu.roll(values, HEAD // 2, 1),
    )
    return values * cosine + swapped * signed_sine


def adamw(weight, first_moment, second_moment, gradient, step_rate, weight_decay):
    first_new = BETA_ONE * first_moment + (1.0 - BETA_ONE) * gradient
    second_new = BETA_TWO * second_moment + (1.0 - BETA_TWO) * gradient * gradient
    fix_one = 1.0 - BETA_ONE**STEP
    fix_two = 1.0 - BETA_TWO**STEP
    update = first_new / fix_one / (jnp.sqrt(second_new / fix_two) + EPS_ADAM)
    return (first_new, second_new, weight - step_rate * (update + weight_decay * weight))


def dot(left, right):
    return lax.dot_general(left, right, (((1,), (0,)), ((), ())), preferred_element_type=F32)


def dot_right_t(left, right):
    return lax.dot_general(left, right, (((1,), (1,)), ((), ())), preferred_element_type=F32)


def dot_left_t(left, right):
    return lax.dot_general(left, right, (((0,), (0,)), ((), ())), preferred_element_type=F32)


def norm_scale(values):
    return lax.rsqrt(jnp.mean(values * values, axis=-1, keepdims=True) + EPS_NORM)


def norm_back(grad_normed, normed, scale_rows):
    return scale_rows * (
        grad_normed - normed * jnp.mean(grad_normed * normed, axis=-1, keepdims=True)
    )


class Weight:
    def __init__(self, shape, whole=None, own=None, parts=(), rels=(), place=None):
        self.shape, self.place, self.rels = shape, place, rels
        self.arrays = [whole] if whole is not None else [own, *parts]
        self.split = whole is None

    def scratch(self):
        return [pltpu.VMEM(self.shape, BF16)] if self.split else []

    def load(self, idx, refs, scratch):
        if not self.split:
            return refs[0]
        full, own, parts = scratch[0], refs[0], refs[1:]
        rows = own.shape[0]
        full[pl.ds(pl.multiple_of(idx[0] * rows, 16), rows), :] = own[...].astype(BF16)
        base = (1 - idx[0]) * rows
        for part, (core, x) in zip(parts, self.rels):
            row, col = self.place(idx[1] ^ core, idx[2] ^ x)
            height, width = part.shape
            row = pl.multiple_of(base + row, 16)
            if width == self.shape[1]:
                full[pl.ds(row, height), :] = part[...]
            else:
                full[pl.ds(row, height), pl.ds(pl.multiple_of(col, LANES), width)] = part[...]
        return full


def call(body, idx, arrays, weights, outs, scratch, flops, name):
    counts = [len(w.arrays) for w in weights]
    flat = list(arrays) + [a for w in weights for a in w.arrays]
    weight_scratch = [w.scratch() for w in weights]

    def kernel(*refs):
        refs = list(refs)
        idx_ref = refs.pop(0)
        take = lambda n: [refs.pop(0) for _ in range(n)]
        array_refs = take(len(arrays))
        weight_refs = [take(n) for n in counts]
        out_refs = take(len(outs))
        own_scratch = take(len(scratch))
        scratch_refs = [take(len(s)) for s in weight_scratch]
        loads = [
            functools.partial(w.load, idx_ref, r, s)
            for w, r, s in zip(weights, weight_refs, scratch_refs)
        ]
        body(idx_ref, array_refs, loads, out_refs, own_scratch)

    moved = sum(a.size * a.dtype.itemsize for a in flat)
    moved += sum(o.size * o.dtype.itemsize for o in outs)
    return pl.pallas_call(
        kernel,
        out_shape=tuple(outs),
        in_specs=[pl.BlockSpec(memory_space=pltpu.SMEM)]
        + [pl.BlockSpec(memory_space=pltpu.VMEM)] * len(flat),
        out_specs=tuple([pl.BlockSpec(memory_space=pltpu.VMEM)] * len(outs)),
        scratch_shapes=list(scratch) + [s for group in weight_scratch for s in group],
        compiler_params=pltpu.CompilerParams(vmem_limit_bytes=VMEM_LIMIT),
        cost_estimate=pl.CostEstimate(flops=flops, bytes_accessed=moved, transcendentals=0),
        name=name,
    )(idx, *flat)


def sds(shape, dtype):
    return jax.ShapeDtypeStruct(shape, dtype)


class Pieces:
    def __init__(self, rows, height, width, place):
        self.rows, self.height, self.width, self.place = rows, height, width, place

    def outs(self):
        return [sds((2, 8, self.height, self.width), BF16)] * 2

    def emit(self, idx, full, outs):
        for other_core, out in enumerate((outs[1], outs[0])):
            for owner in range(2):
                for slot in range(8):
                    row, col = self.place(
                        idx[1] ^ other_core, idx[2] ^ (slot >> 2), idx[3] ^ (slot & 3)
                    )
                    row = pl.multiple_of((idx[0] ^ owner) * self.rows + row, 8)
                    rows = pl.ds(row, self.height)
                    if self.width == full.shape[1]:
                        piece = full[rows, :]
                    else:
                        piece = full[rows, pl.ds(pl.multiple_of(col, LANES), self.width)]
                    out[owner, slot] = piece.astype(BF16)


def attention_mask(segment_column, segment_row):
    seq_length = segment_column.shape[0]
    shape = (seq_length, seq_length)
    token = lax.broadcasted_iota(jnp.int32, shape, 0)
    seen = lax.broadcasted_iota(jnp.int32, shape, 1)
    allowed = (segment_column == segment_row) & (token >= seen)
    return jnp.concatenate([allowed] * GROUP, axis=0)


def head_stack(values, kv_head):
    first = kv_head * GROUP
    return jnp.concatenate(
        [values[:, (first + i) * HEAD : (first + i + 1) * HEAD] for i in range(GROUP)], axis=0
    )


def softmax_rows(query, key, allowed):
    scores = jnp.where(allowed, dot_right_t(query, key) * SCALE, MASKED)
    top = jnp.max(scores, axis=-1, keepdims=True)
    exponent = jnp.exp(scores - top)
    return exponent / jnp.sum(exponent, axis=-1, keepdims=True)


def attention_forward(idx, tokens, tables, segs, gains, w_qkv):
    seq_length, width = tokens.shape

    def body(idx_ref, arrays, loads, outs, scratch):
        x_ref, cos_ref, sin_ref, col_ref, row_ref, gains_ref = arrays
        qkv_ref, o_ref = outs
        x = x_ref[...].astype(F32)
        h1 = (x * norm_scale(x) * gains_ref[0:1, :]).astype(BF16)
        projected = dot(h1, loads[0]()[...])
        for start in range(0, ROPED, LANES):
            block = projected[:, start : start + LANES]
            qkv_ref[:, start : start + LANES] = rotate_block(
                block, cos_ref[...], sin_ref[...]
            ).astype(BF16)
        qkv_ref[:, ROPED:QKV] = projected[:, ROPED:QKV].astype(BF16)
        allowed = attention_mask(col_ref[...], row_ref[...])
        qkv = qkv_ref[...]
        for kv in range(KV_HEADS):
            key = qkv[:, QUERY + kv * HEAD : QUERY + (kv + 1) * HEAD]
            value = qkv[:, ROPED + kv * HEAD : ROPED + (kv + 1) * HEAD]
            probs = softmax_rows(head_stack(qkv, kv), key, allowed).astype(BF16)
            attended = dot(probs, value).astype(BF16)
            for i in range(GROUP):
                start = (kv * GROUP + i) * HEAD
                o_ref[:, start : start + HEAD] = attended[i * seq_length : (i + 1) * seq_length]

    outs = [sds((seq_length, QKV), BF16), sds((seq_length, QUERY), BF16)]
    return call(
        body, idx, [tokens, *tables, *segs, gains], [w_qkv], outs, [], 2 * 128 * 576 * 960, "attention"
    )


def feed_forward(idx, tokens, attended, gains, cotangent, w_out, w_gate_up, pieces):
    seq_length, width = tokens.shape

    def body(idx_ref, arrays, loads, outs, scratch):
        x_ref, o_ref, gains_ref, y_ref = arrays
        u_ref, h2_ref, ab_ref, z_ref = outs[:4]
        u = x_ref[...].astype(F32) + dot(o_ref[...], loads[0]()[...])
        u_ref[...] = u
        h2 = (u * norm_scale(u) * gains_ref[1:2, :]).astype(BF16)
        h2_ref[...] = h2
        ab = dot(h2, loads[1]()[...])
        ab_ref[...] = ab
        gate, up = ab[:, :FF], ab[:, FF:]
        z = (gate * jax.nn.sigmoid(gate) * up).astype(BF16)
        z_ref[...] = z
        if pieces is None:
            outs[4][...] = dot_left_t(z, y_ref[...])
        else:
            scratch[0][...] = dot_left_t(z, y_ref[...]).astype(BF16)
            pieces.emit(idx_ref, scratch[0], outs[4:])

    outs = [
        sds((seq_length, width), F32),
        sds((seq_length, width), BF16),
        sds((seq_length, 2 * FF), F32),
        sds((seq_length, FF), BF16),
    ]
    outs += [sds((FF, width), F32)] if pieces is None else pieces.outs()
    scratch = [] if pieces is None else [pltpu.VMEM((FF, width), BF16)]
    return call(
        body,
        idx,
        [tokens, attended, gains, cotangent],
        [w_out, w_gate_up],
        outs,
        scratch,
        2 * 128 * 576 * 5200,
        "feed_forward",
    )


def feed_back(idx, ab, normed_low, cotangent, w_down, pieces):
    seq_length, width = cotangent.shape

    def body(idx_ref, arrays, loads, outs, scratch):
        ab_ref, h2_ref, y_ref = arrays
        gg_ref = outs[0]
        gate, up = ab_ref[:, :FF], ab_ref[:, FF:]
        sig = jax.nn.sigmoid(gate)
        grad_hidden = dot_right_t(y_ref[...], loads[0]()[...])
        gg_ref[:, :FF] = (grad_hidden * up * sig * (1.0 + gate * (1.0 - sig))).astype(BF16)
        gg_ref[:, FF:] = (grad_hidden * gate * sig).astype(BF16)
        grad = dot_left_t(h2_ref[...], gg_ref[...])
        if pieces is None:
            outs[1][...] = grad
        else:
            scratch[0][...] = grad.astype(BF16)
            pieces.emit(idx_ref, scratch[0], outs[1:])

    outs = [sds((seq_length, 2 * FF), BF16)]
    outs += [sds((width, 2 * FF), F32)] if pieces is None else pieces.outs()
    scratch = [] if pieces is None else [pltpu.VMEM((width, 2 * FF), BF16)]
    return call(
        body, idx, [ab, normed_low, cotangent], [w_down], outs, scratch, 2 * 128 * 576 * 4700, "feed_back"
    )


def attention_back(
    idx, tokens, cotangent, middle, gated, qkv, attended, tables, segs, gains, w_gate_up, w_out, pieces
):
    seq_length, width = tokens.shape

    def body(idx_ref, arrays, loads, outs, scratch):
        x_ref, y_ref, u_ref, gg_ref, qkv_ref, o_ref = arrays[:6]
        cos_ref, sin_ref, col_ref, row_ref, gains_ref = arrays[6:]
        gu_ref, gp_ref, gain_ref = outs[:3]
        full, grad_proj = scratch
        u = u_ref[...]
        scale_two = norm_scale(u)
        normed = u * scale_two
        grad_normed = dot_right_t(gg_ref[...], loads[0]()[...])
        gain_ref[...] = jnp.sum(grad_normed * normed, axis=0, keepdims=True)
        gu = y_ref[...].astype(F32) + norm_back(
            grad_normed * gains_ref[1:2, :], normed, scale_two
        )
        gu_ref[...] = gu
        gu_low = gu.astype(BF16)
        go = dot_right_t(gu_low, loads[1]()[...]).astype(BF16)
        allowed = attention_mask(col_ref[...], row_ref[...])
        qkv_values = qkv_ref[...]
        for kv in range(KV_HEADS):
            key = qkv_values[:, QUERY + kv * HEAD : QUERY + (kv + 1) * HEAD]
            value = qkv_values[:, ROPED + kv * HEAD : ROPED + (kv + 1) * HEAD]
            query = head_stack(qkv_values, kv)
            grad_out = head_stack(go, kv)
            probs = softmax_rows(query, key, allowed)
            grad_probs = dot_right_t(grad_out, value)
            row_delta = jnp.sum(probs * grad_probs, axis=-1, keepdims=True)
            gs = (probs * (grad_probs - row_delta)).astype(BF16)
            grad_query = dot(gs, key) * SCALE
            for i in range(GROUP):
                start = (kv * GROUP + i) * HEAD
                grad_proj[:, start : start + HEAD] = grad_query[
                    i * seq_length : (i + 1) * seq_length
                ]
            start = QUERY + kv * HEAD
            grad_proj[:, start : start + HEAD] = dot_left_t(gs, query) * SCALE
            start = ROPED + kv * HEAD
            grad_proj[:, start : start + HEAD] = dot_left_t(probs.astype(BF16), grad_out)
        for start in range(0, ROPED, LANES):
            gp_ref[:, start : start + LANES] = rotate_block(
                grad_proj[:, start : start + LANES], cos_ref[...], -sin_ref[...]
            ).astype(BF16)
        gp_ref[:, ROPED:QKV] = grad_proj[:, ROPED:QKV].astype(BF16)
        x = x_ref[...].astype(F32)
        h1 = (x * norm_scale(x) * gains_ref[0:1, :]).astype(BF16)
        full[:, :QKV] = dot_left_t(h1, gp_ref[...])
        full[:, QKV:] = dot_left_t(o_ref[...], gu_low)
        if pieces is None:
            outs[3][...] = full[...]
        else:
            pieces.emit(idx_ref, full, outs[3:])

    outs = [sds((seq_length, width), F32), sds((seq_length, QKV), BF16), sds((1, width), F32)]
    outs += [sds((width, QKV + width), F32)] if pieces is None else pieces.outs()
    scratch = [pltpu.VMEM((width, QKV + width), F32), pltpu.VMEM((seq_length, QKV), F32)]
    return call(
        body,
        idx,
        [tokens, cotangent, middle, gated, qkv, attended, *tables, *segs, gains],
        [w_gate_up, w_out],
        outs,
        scratch,
        2 * 128 * 576 * 6500,
        "attention_back",
    )


def finish_tokens(idx, tokens, middle, hidden, grad_middle, grad_proj, gains, w_down, w_qkv):
    seq_length, width = tokens.shape

    def body(idx_ref, arrays, loads, outs, scratch):
        x_ref, u_ref, z_ref, gu_ref, gp_ref, gains_ref = arrays
        out_ref, grad_ref, gain_ref = outs
        out_ref[...] = (u_ref[...] + dot(z_ref[...], loads[0]()[...])).astype(BF16)
        x = x_ref[...].astype(F32)
        scale_one = norm_scale(x)
        normed = x * scale_one
        grad_normed = dot_right_t(gp_ref[...], loads[1]()[...])
        gain_ref[...] = jnp.sum(grad_normed * normed, axis=0, keepdims=True)
        grad_ref[...] = (
            gu_ref[...] + norm_back(grad_normed * gains_ref[0:1, :], normed, scale_one)
        ).astype(BF16)

    outs = [sds((seq_length, width), BF16), sds((seq_length, width), BF16), sds((1, width), F32)]
    return call(
        body,
        idx,
        [tokens, middle, hidden, grad_middle, grad_proj, gains],
        [w_down, w_qkv],
        outs,
        [],
        2 * 128 * 576 * 2500,
        "finish_tokens",
    )


def update_state(idx, parts, weights, firsts, seconds, blocks, assemble, name):
    count = len(weights)
    height, width = parts[0].shape[1:]
    full_shape, put = assemble

    def kernel(idx_ref, *refs):
        part_refs = refs[:4]
        w_refs = refs[4 : 4 + count]
        f_refs = refs[4 + count : 4 + 2 * count]
        s_refs = refs[4 + 2 * count : 4 + 3 * count]
        outs = refs[4 + 3 * count : 4 + 6 * count]
        full = refs[4 + 6 * count]
        rel = pl.program_id(0) ^ (idx_ref[1] * 2 + idx_ref[2])
        for k in range(4):

            @pl.when(rel == k)
            def _(k=k):
                for z in range(4):
                    put(full, z, part_refs[k][idx_ref[3] ^ z].astype(F32))

        start = 0
        for i in range(count):
            columns = w_refs[i].shape[1]
            first, second, new = adamw(
                w_refs[i][...],
                f_refs[i][...],
                s_refs[i][...],
                full[:, start : start + columns],
                RATE_MATRIX,
                DECAY_MATRIX,
            )
            start += columns
            outs[i][...] = first
            outs[count + i][...] = second
            outs[2 * count + i][...] = new

    state = [*weights, *firsts, *seconds]
    state_specs = [pl.BlockSpec(*blocks[i]) for i in range(count)] * 3
    moved = sum(a.size * 8 for a in state)
    return pl.pallas_call(
        kernel,
        grid_spec=pltpu.PrefetchScalarGridSpec(
            num_scalar_prefetch=1,
            grid=(4,),
            in_specs=[pl.BlockSpec((4, height, width), lambda t, _: (0, 0, 0))] * 4 + state_specs,
            out_specs=tuple(state_specs),
            scratch_shapes=[pltpu.VMEM(full_shape, F32)],
        ),
        out_shape=tuple(sds(a.shape, F32) for a in state),
        compiler_params=pltpu.CompilerParams(vmem_limit_bytes=VMEM_LIMIT),
        cost_estimate=pl.CostEstimate(flops=0, bytes_accessed=moved, transcendentals=0),
        name=name,
    )(idx, *parts, *state)


def swap(values, axis, mask):
    size = lax.axis_size(axis)
    return lax.ppermute(values, axis, [(i, i ^ mask) for i in range(size)])


def sum_and_share(send, keep):
    arrived = swap(send, "dp", 1)
    across = (keep[1].astype(F32) + arrived[1].astype(F32)).astype(BF16)
    arrived_across = swap(across, "shard", 1)
    total = keep[0].astype(F32) + arrived[0].astype(F32) + arrived_across.astype(F32)
    arrived_x = swap(total[4:].astype(BF16), "dp", 2)
    total = total[:4] + arrived_x.astype(F32)
    arrived_z = [swap(total[m].astype(BF16), "dp", 4 * m) for m in (1, 2, 3)]
    piece = total[0] + sum(a.astype(F32) for a in arrived_z)
    piece = piece.astype(BF16)
    near = jnp.stack([piece] + [swap(piece, "dp", 4 * m) for m in (1, 2, 3)])
    near_x = swap(near, "dp", 2)
    return [near, near_x, swap(near, "dp", 1), swap(near_x, "dp", 1)]


def gather_two(own, place, shape, core):
    rows = own.shape[0] // 2
    mine = lax.dynamic_slice_in_dim(own, core * rows, rows, 0).astype(BF16)
    near = swap(mine, "shard", 1)
    far = swap(near, "dp", 1)
    return Weight(shape, own=own, parts=[near, far], rels=[(0, 0), (1, 0)], place=place)


def gather_four(own, mine, place, shape):
    near = swap(mine, "shard", 1)
    near_x = swap(near, "dp", 2)
    parts = [near, near_x, swap(near, "dp", 1), swap(near_x, "dp", 1)]
    rels = [(0, 0), (0, 1), (1, 0), (1, 1)]
    return Weight(shape, own=own, parts=parts, rels=rels, place=place)


def per_device(
    tokens,
    segments,
    cotangent,
    w_qkv,
    w_out,
    w_gate_up,
    w_down,
    norm_gains,
    first_qkv,
    first_out,
    first_gate_up,
    first_down,
    first_gains,
    second_qkv,
    second_out,
    second_gate_up,
    second_down,
    second_gains,
):
    groups = lax.axis_size("shard")
    replicas = lax.axis_size("dp")
    fast = groups == 2 and replicas == 16
    place_dp = lax.axis_index("dp")
    owner = lax.axis_index("shard")
    core, x_bit, z_bits = place_dp & 1, (place_dp >> 1) & 1, place_dp >> 2
    idx = jnp.stack([owner, core, x_bit, z_bits]).astype(jnp.int32)
    x, y = tokens[0], cotangent[0]
    width = x.shape[1]
    rows, down_rows = w_qkv.shape[0], w_down.shape[0]
    masters = (w_qkv, w_out, w_gate_up, w_down)
    shapes = [(m.shape[0] * groups, m.shape[1]) for m in masters]
    if fast:
        own_gains = norm_gains.astype(BF16)
        other_gains = swap(own_gains, "shard", 1)
        gains = jnp.where(
            owner == 0,
            jnp.concatenate([own_gains, other_gains], axis=1),
            jnp.concatenate([other_gains, own_gains], axis=1),
        ).astype(F32)
        half = rows // 2
        mat_qkv = gather_two(w_qkv, lambda c, x: (c * half, 0), shapes[0], core)
        mat_out = gather_two(w_out, lambda c, x: (c * half, 0), shapes[1], core)
        mine = lax.dynamic_slice_in_dim(w_gate_up, core * half, half, 0)
        mine = jnp.where(x_bit == 0, mine[:, :FF], mine[:, FF:]).astype(BF16)
        mat_gate_up = gather_four(w_gate_up, mine, lambda c, x: (c * half, x * FF), shapes[2])
        quarter = down_rows // 4
        mine = lax.dynamic_slice_in_dim(
            w_down, (core * 2 + x_bit) * quarter, quarter, 0
        ).astype(BF16)
        mat_down = gather_four(w_down, mine, lambda c, x: ((c * 2 + x) * quarter, 0), shapes[3])
        eighth = rows // 4
        cut_qkv_out = Pieces(rows, eighth, 384, lambda c, x, z: ((c * 2 + x) * eighth, z * 384))
        cut_gate_up = Pieces(rows, half, 384, lambda c, x, z: (c * half, (x * 4 + z) * 384))
        thin = down_rows // 16
        cut_down = Pieces(down_rows, thin, width, lambda c, x, z: ((c * 8 + x * 4 + z) * thin, 0))
    else:
        gains = lax.all_gather(norm_gains.astype(BF16), "shard", axis=1, tiled=True).astype(F32)
        mat_qkv, mat_out, mat_gate_up, mat_down = [
            Weight(s, whole=lax.all_gather(m.astype(BF16), "shard", axis=0, tiled=True))
            for s, m in zip(shapes, masters)
        ]
        cut_qkv_out = cut_gate_up = cut_down = None

    tables = rope_tables(segments[0])
    segs = (segments.reshape(-1, 1), segments.reshape(1, -1))
    qkv, attended = attention_forward(idx, x, tables, segs, gains, mat_qkv)
    middle, normed_low, ab, hidden, *grad_down = feed_forward(
        idx, x, attended, gains, y, mat_out, mat_gate_up, cut_down
    )
    gated, *grad_gate_up = feed_back(idx, ab, normed_low, y, mat_down, cut_gate_up)
    grad_middle, grad_proj, grad_gain_two, *grad_qkv_out = attention_back(
        idx, x, y, middle, gated, qkv, attended, tables, segs, gains, mat_gate_up, mat_out, cut_qkv_out
    )
    output, token_grad, grad_gain_one = finish_tokens(
        idx, x, middle, hidden, grad_middle, grad_proj, gains, mat_down, mat_qkv
    )
    gain_grads = lax.psum(
        jnp.concatenate([grad_gain_one, grad_gain_two], axis=0), ("dp", "shard")
    )
    gain_grads = lax.dynamic_slice_in_dim(
        gain_grads, owner * norm_gains.shape[1], norm_gains.shape[1], 1
    )
    one_gains, two_gains, next_gains = adamw(
        norm_gains, first_gains, second_gains, gain_grads, RATE_GAIN, 0.0
    )
    if fast:

        def put_rows(full, z, piece):
            full[pl.ds(z * thin, thin), :] = piece

        def put_columns(full, z, piece):
            full[:, pl.ds(z * 384, 384)] = piece

        by_row = lambda t, _: (t, 0)
        one_down, two_down, next_down = update_state(
            idx,
            sum_and_share(*grad_down),
            [w_down],
            [first_down],
            [second_down],
            [((quarter, width), by_row)],
            ((quarter, width), put_rows),
            "update_down",
        )
        one_gate_up, two_gate_up, next_gate_up = update_state(
            idx,
            sum_and_share(*grad_gate_up),
            [w_gate_up],
            [first_gate_up],
            [second_gate_up],
            [((half, FF), lambda t, _: (t // 2, t % 2))],
            ((half, FF), put_columns),
            "update_gate_up",
        )
        one_qkv, one_out, two_qkv, two_out, next_qkv, next_out = update_state(
            idx,
            sum_and_share(*grad_qkv_out),
            [w_qkv, w_out],
            [first_qkv, first_out],
            [second_qkv, second_out],
            [((eighth, QKV), by_row), ((eighth, width), by_row)],
            ((eighth, QKV + width), put_columns),
            "update_qkv_out",
        )
    else:
        sums = lax.psum((grad_qkv_out[0], grad_gate_up[0], grad_down[0]), ("dp", "shard"))
        mine = [lax.dynamic_slice_in_dim(g, owner * (g.shape[0] // groups), g.shape[0] // groups, 0) for g in sums]
        one_qkv, two_qkv, next_qkv = adamw(
            w_qkv, first_qkv, second_qkv, mine[0][:, :QKV], RATE_MATRIX, DECAY_MATRIX
        )
        one_out, two_out, next_out = adamw(
            w_out, first_out, second_out, mine[0][:, QKV:], RATE_MATRIX, DECAY_MATRIX
        )
        one_gate_up, two_gate_up, next_gate_up = adamw(
            w_gate_up, first_gate_up, second_gate_up, mine[1], RATE_MATRIX, DECAY_MATRIX
        )
        one_down, two_down, next_down = adamw(
            w_down, first_down, second_down, mine[2], RATE_MATRIX, DECAY_MATRIX
        )
    return (
        output[None],
        token_grad[None],
        one_qkv,
        one_out,
        one_gate_up,
        one_down,
        one_gains,
        two_qkv,
        two_out,
        two_gate_up,
        two_down,
        two_gains,
        next_qkv,
        next_out,
        next_gate_up,
        next_down,
        next_gains,
    )


def solution(mesh):
    return jax.shard_map(
        per_device,
        mesh=mesh,
        in_specs=(
            P(("dp", "shard"), None, None),
            P(("dp", "shard"), None),
            P(("dp", "shard"), None, None),
            P("shard", None),
            P("shard", None),
            P("shard", None),
            P("shard", None),
            P(None, "shard"),
            P("shard", None),
            P("shard", None),
            P("shard", None),
            P("shard", None),
            P(None, "shard"),
            P("shard", None),
            P("shard", None),
            P("shard", None),
            P("shard", None),
            P(None, "shard"),
        ),
        out_specs=(
            P(("dp", "shard"), None, None),
            P(("dp", "shard"), None, None),
            P("shard", None),
            P("shard", None),
            P("shard", None),
            P("shard", None),
            P(None, "shard"),
            P("shard", None),
            P("shard", None),
            P("shard", None),
            P("shard", None),
            P(None, "shard"),
            P("shard", None),
            P("shard", None),
            P("shard", None),
            P("shard", None),
            P(None, "shard"),
        ),
        check_vma=False,
    )
```

time: 946 us -> 264 us (0.28)
  blocking collectives: 339 us -> 38.8 us
  local copies, waits for them, and re-layouts: 264 us -> 27 us
  waiting for transfers between devices: 253 us -> 68.7 us
  starting transfers between devices: 0.21 us -> 57.9 us
  Pallas kernels: 0 us -> 56.8 us
  other arithmetic: 39.5 us -> 13.1 us
  matrix products: 26 us -> 0 us
  between operations: 15.3 us -> 1.04 us
    all_to_all x1 -> x0, blocking collectives: 314 us -> none  [per_device(): lax.all_to_all(arranged, 'dp', split_axis=0, concat_axis=0, tiled=True)]
    unnamed x7 -> x0, waiting for transfers between devices: 175 us -> none
    unnamed x96 -> x50, local copies, waits for them, and re-layouts: 106 us -> 22.4 us
    all_gather x3 -> x0, waiting for transfers between devices: 78.1 us -> none  [the longest x1 48.1 us: per_device(): lax.all_gather(w_gate_up.astype(jnp.bfloat16), 'shard', axis=0, tiled=True)]
    slice x8 -> x3, local copies, waits for them, and re-layouts: 78.1 us -> 0.11 us  [sum_and_share(): arrived_x = swap(total[4:].astype(BF16), 'dp', 2)]
    ppermute x0 -> x49, waiting for transfers between devices: none -> 68.7 us  [swap(): return lax.ppermute(values, axis, [(i, i ^ mask) for i in range(size)])]
    ppermute x0 -> x49, starting transfers between devices: none -> 57.9 us  [swap(): return lax.ppermute(values, axis, [(i, i ^ mask) for i in range(size)])]
    pallas_call x0 -> x8, Pallas kernels: none -> 56.8 us  [the longest x5 31.9 us: call(): pl.pallas_call(kernel, out_shape=tuple(outs), in_specs=[pl.BlockSpec(memo...]
  transfers between devices with their start and end apart: 5 -> 49, of which waited for: 5 -> 17; matrix products, arithmetic and copies ran while one was open for 2% -> 14% of each run, Pallas kernels for 0% -> 15%
where the time goes in v1:
time: 264 us; the launch traced here: 263 us
  waiting for transfers between devices  68.7 us (26%)
  starting transfers between devices  57.9 us (22%)
  Pallas kernels  56.8 us (22%)
  blocking collectives  38.8 us (15%)
  local copies, waits for them, and re-layouts  27 us (10%)
  other arithmetic  13.1 us (5%)
    ppermute x49, waiting for transfers between devices, swap(): return lax.ppermute(values, axis, [(i, i ^ mask) for i in range(size)])  68.7 us
    ppermute x49, starting transfers between devices, swap(): return lax.ppermute(values, axis, [(i, i ^ mask) for i in range(size)])  57.9 us
    psum x1, blocking collectives, per_device(): lax.psum(jnp.concatenate([grad_gain_one, grad_gain_two], axis=0), ('dp',...  38.8 us
    pallas_call x5, Pallas kernels, call(): pl.pallas_call(kernel, out_shape=tuple(outs), in_specs=[pl.BlockSpec(memo...  31.9 us
    pallas_call x3, Pallas kernels, update_state(): pl.pallas_call(kernel, grid_spec=pltpu.PrefetchScalarGridSpec(num_scalar_...  24.8 us
    unnamed x50, local copies, waits for them, and re-layouts  22.4 us
  transfers between devices with their start and end apart: 49, of which 17 were waited for; matrix products, arithmetic and copies ran while one was open for 14% of the time, Pallas kernels for 15%

profile of v1, /device:TPU:0, one launch (start us, length us, event | category | flops | bytes accessed | tf_op | source)
XLA Modules:
  0.0 263.3 jit_solution(949488361115860964)
XLA Ops:
  1.3 3.0 %collective-permute-start = (bf16[2,288]{1,0:T(2,128)(2,1)S(1)}, bf16[2,288]{1,0:T(2,128)(2,1)S(1)}, u32[]{:S(2)}, u32[]{:S(2)}) collective-permute-start(bf16[2,288]{1,0:T(2,128)(2,1)S(1)} %convert_element_type.185), channel_id=1, source_target_pairs={{0,1},{1,0},{2,3},{3,2},{4,5},{5,4},{6,7},{7,6},{8,9},{9,8},{10,11... | collective-permute-start | bytes 3464 | tf_op jit(solution)/shard_map/ppermute | solution.py:465
  4.3 1.7 dynamic-slice_convert_fusion.2
  7.5 2.1 collective-permute-start.5
  10.8 1.9 copy.76.refs_4_.refs_7_
  13.5 2.0 collective-permute-start.9
  15.6 7.7 %collective-permute-done.5.refs_9_.refs_13_ = bf16[144,1536]{1,0:T(8,128)(2,1)S(1)} collective-permute-done((bf16[144,1536]{1,0:T(8,128)(2,1)S(1)}, bf16[144,1536]{1,0:T(8,128)(2,1)S(1)}, u32[]{:S(2)}, u32[]{:S(2)}) %collective-permute-start.5) | collective-permute-done | bytes 442400 | tf_op jit(solution)/shard_map/ppermute | solution.py:465
  25.2 8.1 %collective-permute-done.9.refs_5_.refs_8_ = bf16[192,576]{1,0:T(8,128)(2,1)S(1)} collective-permute-done((bf16[192,576]{1,0:T(8,128)(2,1)}, bf16[192,576]{1,0:T(8,128)(2,1)S(1)}, u32[]{:S(2)}, u32[]{:S(2)}) %collective-permute-start.9) | collective-permute-done | bytes 221216 | tf_op jit(solution)/shard_map/ppermute | solution.py:465
  36.5 1.9 pad_maximum_fusion.3
  41.8 1.7 copy.69
  43.5 1.7 copy.74
  45.9 3.8 %attention.1 = (bf16[128,960]{1,0:T(8,128)(2,1)}, bf16[128,576]{1,0:T(8,128)(2,1)}) custom-call(s32[4]{0:T(128)} %pad_add_fusion.refs_0_.idx_ref, bf16[128,576]{1,0:T(8,128)(2,1)} %bitcast.74, f32[128,128]{1,0:T(8,128)} %get-tuple-element.151.refs_2_.refs_7_, f32[128,128]{1,0:T(8,128)} %get-tuple-element.152.refs_3_.refs_8_, s32[128,1]{1,0:T(8,128)} %copy.73.refs_4_.refs_9_, ...), custom_call_target="tpu_custom_call" | custom-call | flops 141557760 | bytes 2336256 | tf_op jit(solution)/shard_map/attention/pallas_call | solution.py:146
  50.6 6.5 %feed_forward.1 = (f32[128,576]{1,0:T(8,128)}, bf16[128,576]{1,0:T(8,128)(2,1)}, f32[128,3072]{1,0:T(8,128)}, bf16[128,1536]{1,0:T(8,128)(2,1)}, bf16[2,8,48,576...) custom-call(s32[4]{0:T(128)} %pad_add_fusion.refs_0_.idx_ref, bf16[128,576]{1,0:T(8,128)(2,1)} %bitcast.75, ...), custom_call_target="tpu_custom_call" | custom-call | flops 766771200 | bytes 10928640 | tf_op jit(solution)/shard_map/feed_forward/pallas_call | solution.py:146
  57.1 6.6 %feed_back.1 = (bf16[128,3072]{1,0:T(8,128)(2,1)}, bf16[2,8,144,384]{3,2,1,0:T(8,128)(2,1)}, bf16[2,8,144,384]{3,2,1,0:T(8,128)(2,1)}) custom-call(s32[4]{0:T(128)} %pad_add_fusion.refs_0_.idx_ref, f32[128,3072]{1,0:T(8,128)} %get-tuple-element.51.refs_1_, bf16[128,576]{1,0:T(8,128)(2,1)} %get-tuple-element.52.refs_2_, bf16[128,576]{1,0:T(8,128)(2,1)} %bitcast.79, ...), custom_call_target="tpu_custom_call" | custom-call | flops 693043200 | bytes 8847360 | tf_op jit(solution)/shard_map/feed_back/pallas_call | solution.py:146
  64.3 10.2 %attention_back.1 = (f32[128,576]{1,0:T(8,128)}, bf16[128,960]{1,0:T(8,128)(2,1)}, f32[1,576]{1,0:T(1,128)}, bf16[2,8,72,384]{3,2,1,0:T(8,128)(2,1)}, bf16[2,8,72,384]{3,2,1,0:T(8,128)(2,1)}) custom-call(s32[4]{0:T(128)} %pad_add_fusion.refs_0_.idx_ref, bf16[128,576]{1,0:T(8,128)(2,1)} %bitcast.76, bf16[128,576]{1,0:T(8,128)(2,1)} %bitcast.80, ...), custom_call_target="tpu_custom_call" | custom-call | flops 958464000 | bytes 10522368 | tf_op jit(solution)/shard_map/attention_back/pallas_call | solution.py:146
  80.8 8.3 %collective-permute-done.38 = bf16[8,48,576]{2,1,0:T(8,128)(2,1)S(1)} collective-permute-done((bf16[8,48,576]{2,1,0:T(8,128)(2,1)S(1)}, bf16[8,48,576]{2,1,0:T(8,128)(2,1)S(1)}, u32[]{:S(2)}, u32[]{:S(2)}) %collective-permute-start.38) | collective-permute-done | bytes 442400 | tf_op jit(solution)/shard_map/ppermute | solution.py:465
  89.3 1.6 collective-permute-start.39
  90.9 7.7 %collective-permute-done.14 = bf16[8,72,384]{2,1,0:T(8,128)(2,1)S(1)} collective-permute-done((bf16[8,72,384]{2,1,0:T(8,128)(2,1)S(1)}, bf16[8,72,384]{2,1,0:T(8,128)(2,1)S(1)}, u32[]{:S(2)}, u32[]{:S(2)}) %collective-permute-start.14) | collective-permute-done | bytes 442400 | tf_op jit(solution)/shard_map/ppermute | solution.py:465
  98.7 1.6 collective-permute-start.15
  100.4 16.7 %collective-permute-done.26 = bf16[8,144,384]{2,1,0:T(8,128)(2,1)S(1)} collective-permute-done((bf16[8,144,384]{2,1,0:T(8,128)(2,1)S(1)}, bf16[8,144,384]{2,1,0:T(8,128)(2,1)S(1)}, u32[]{:S(2)}, u32[]{:S(2)}) %collective-permute-start.26) | collective-permute-done | bytes 884768 | tf_op jit(solution)/shard_map/ppermute | solution.py:465
  119.0 1.6 collective-permute-start.40
  120.6 2.5 collective-permute-start.42
  123.2 6.0 %collective-permute-done.27 = bf16[4,144,384]{2,1,0:T(8,128)(2,1)S(1)} collective-permute-done((bf16[4,144,384]{2,1,0:T(8,128)(2,1)S(1)}, bf16[4,144,384]{2,1,0:T(8,128)(2,1)S(1)}, u32[]{:S(2)}, u32[]{:S(2)}) %collective-permute-start.27) | collective-permute-done | bytes 442400 | tf_op jit(solution)/shard_map/ppermute | solution.py:465
  129.4 1.6 collective-permute-start.28
  131.0 2.5 collective-permute-start.30
  133.6 1.8 collective-permute-done.28
  135.4 2.6 collective-permute-start.41
  139.4 3.7 %collective-permute-start.16 = (bf16[72,384]{1,0:T(8,128)(2,1)S(1)}, bf16[72,384]{1,0:T(8,128)(2,1)S(1)}, u32[]{:S(2)}, u32[]{:S(2)}) collective-permute-start(bf16[72,384]{1,0:T(8,128)(2,1)S(1)} %get-tuple-element.145), channel_id=1, source_target_pairs={{0,8},{2,10},{4,12},{6,14},{8,0},{10,2},{12,4},{14,6},{16,24},{18,... | collective-permute-start | bytes 165896 | tf_op jit(solution)/shard_map/ppermute | solution.py:465
  143.1 1.6 collective-permute-done.29
  144.8 3.3 %collective-permute-start.18 = (bf16[72,384]{1,0:T(8,128)(2,1)S(1)}, bf16[72,384]{1,0:T(8,128)(2,1)S(1)}, u32[]{:S(2)}, u32[]{:S(2)}) collective-permute-start(bf16[72,384]{1,0:T(8,128)(2,1)S(1)} %get-tuple-element.146), channel_id=1, source_target_pairs={{0,24},{2,26},{4,28},{6,30},{8,16},{10,18},{12,20},{14,22},{16,8},... | collective-permute-start | bytes 165896 | tf_op jit(solution)/shard_map/ppermute | solution.py:465
  148.7 3.9 %collective-permute-start.31 = (bf16[144,384]{1,0:T(8,128)(2,1)S(1)}, bf16[144,384]{1,0:T(8,128)(2,1)S(1)}, u32[]{:S(2)}, u32[]{:S(2)}) collective-permute-start(bf16[144,384]{1,0:T(8,128)(2,1)S(1)} %fusion.5), channel_id=1, source_target_pairs={{0,8},{2,10},{4,12},{6,14},{8,0},{10,2},{12,4},{14,6},{16,24},{18,... | collective-permute-start | bytes 331784 | tf_op jit(solution)/shard_map/ppermute | solution.py:465
  152.6 2.3 collective-permute-done.33
  154.9 3.3 %collective-permute-start.17 = (bf16[72,384]{1,0:T(8,128)(2,1)S(1)}, bf16[72,384]{1,0:T(8,128)(2,1)S(1)}, u32[]{:S(2)}, u32[]{:S(2)}) collective-permute-start(bf16[72,384]{1,0:T(8,128)(2,1)S(1)} %get-tuple-element.147), channel_id=1, source_target_pairs={{0,16},{2,18},{4,20},{6,22},{8,24},{10,26},{12,28},{14,30},{16,0},... | collective-permute-start | bytes 165896 | tf_op jit(solution)/shard_map/ppermute | solution.py:465
  159.5 1.6 collective-permute-start.45
  162.0 2.8 %collective-permute-start.43 = (bf16[48,576]{1,0:T(8,128)(2,1)S(1)}, bf16[48,576]{1,0:T(8,128)(2,1)S(1)}, u32[]{:S(2)}, u32[]{:S(2)}) collective-permute-start(bf16[48,576]{1,0:T(8,128)(2,1)S(1)} %fusion.7), channel_id=1, source_target_pairs={{0,8},{2,10},{4,12},{6,14},{8,0},{10,2},{12,4},{14,6},{16,24},{18,... | collective-permute-start | bytes 165896 | tf_op jit(solution)/shard_map/ppermute | solution.py:465
  166.3 1.6 collective-permute-start.21
  168.7 2.1 collective-permute-start.19
  175.9 1.8 copy.80.refs_5_
  177.7 1.8 copy.81.refs_6_
  179.4 4.7 %finish_tokens.1 = (bf16[128,576]{1,0:T(8,128)(2,1)}, bf16[128,576]{1,0:T(8,128)(2,1)}, f32[1,576]{1,0:T(1,128)}) custom-call(s32[4]{0:T(128)} %pad_add_fusion.refs_0_.idx_ref, bf16[128,576]{1,0:T(8,128)(2,1)} %bitcast.77, f32[128,576]{1,0:T(8,128)} %get-tuple-element.49.refs_3_.refs_2_, bf16[128,1536]{1,0:T(8,128)(2,1)} %get-tuple-element.50.refs_3_, ...), custom_call_target="tpu_custom_call" | custom-call | flops 368640000 | bytes 5991168 | tf_op jit(solution)/shard_map/finish_tokens/pallas_call | solution.py:146
  184.1 1.7 copy.82
  185.8 1.7 copy.83
  188.2 38.8 %psum.7 = f32[2,576]{1,0:T(2,128)S(1)} all-reduce(f32[2,576]{1,0:T(2,128)S(1)} %pad_maximum_fusion.5), channel_id=1, replica_groups=mesh['dp'=16,'shard'=2] {'dp','shard'}, use_global_device_ids=true, to_apply=%region_1.2 | all-reduce | flops 1152 | bytes 9216 | tf_op jit(solution)/shard_map/psum | solution.py:576
  229.7 7.2 %update_down.1 = (f32[768,576]{1,0:T(8,128)}, f32[768,576]{1,0:T(8,128)}, f32[768,576]{1,0:T(8,128)}) custom-call(s32[4]{0:T(128)} %pad_add_fusion.refs_0_.idx_ref, bf16[4,48,576]{2,1,0:T(8,128)(2,1)} %pad_maximum_fusion.1.refs_0_, bf16[4,48,576]{2,1,0:T(8,128)(2,1)} %collective-permute-done.46.refs_1_, bf16[4,48,576]{2,1,0:T(8,128)(2,1)} %collective-permute-done.47.refs_2_, ...), custom_call_target="tpu_custom_call" | custom-call | bytes 10616832 | tf_op jit(solution)/shard_map/update_down/pallas_call | solution.py:447
  236.9 2.8 %copy.84 = f32[768,576]{0,1:T(8,128)} copy(f32[768,576]{1,0:T(8,128)} %get-tuple-element.118) | data formatting | bytes 3538944
  239.7 2.9 %copy.85 = f32[768,576]{0,1:T(8,128)} copy(f32[768,576]{1,0:T(8,128)} %get-tuple-element.123) | data formatting | bytes 3538944
  242.6 1.7 copy.86
  245.6 7.4 %update_qkv_out.1 = (f32[288,960]{1,0:T(8,128)}, f32[288,576]{1,0:T(8,128)}, f32[288,960]{1,0:T(8,128)}, f32[288,576]{1,0:T(8,128)}, f32[288,960]{1,0:T(8,128)}, /*index=5*/f32[288,576]{1,0:T(8,128)}) custom-call(s32[4]{0:T(128)} %pad_add_fusion.refs_0_.idx_ref, bf16[4,72,384]{2,1,0:T(8,128)(2,1)} %pad_maximum_fusion.2.refs_0_, ...), custom_call_target="tpu_custom_call" | custom-call | bytes 10616832 | tf_op jit(solution)/shard_map/update_qkv_out/pallas_call | solution.py:447
  253.0 10.3 %update_gate_up.1 = (f32[288,3072]{1,0:T(8,128)}, f32[288,3072]{1,0:T(8,128)}, f32[288,3072]{1,0:T(8,128)}) custom-call(s32[4]{0:T(128)} %pad_add_fusion.refs_0_.idx_ref, bf16[4,144,384]{2,1,0:T(8,128)(2,1)} %pad_maximum_fusion.refs_0_, bf16[4,144,384]{2,1,0:T(8,128)(2,1)} %collective-permute-done.34.refs_1_, ...), custom_call_target="tpu_custom_call" | custom-call | bytes 21233664 | tf_op jit(solution)/shard_map/update_gate_up/pallas_call | solution.py:447
  (149 shorter events, 40.2 us)
Async XLA Ops:
  1.3 33.5 %collective-permute-start = (bf16[2,288]{1,0:T(2,128)(2,1)S(1)}, bf16[2,288]{1,0:T(2,128)(2,1)S(1)}, u32[]{:S(2)}, u32[]{:S(2)}) collective-permute-start(bf16[2,288]{1,0:T(2,128)(2,1)S(1)} %convert_element_type.185), channel_id=1, source_target_pairs={{0,1},{1,0},{2,3},{3,2},{4,5},{5,4},{6,7},{7,6},{8,9},{9,8},{10,11... | collective-permute-start | bytes 3464 | tf_op jit(solution)/shard_map/ppermute | solution.py:465
  6.0 32.4 %collective-permute-start.3 = (bf16[144,576]{1,0:T(8,128)(2,1)}, bf16[144,576]{1,0:T(8,128)(2,1)}, u32[]{:S(2)}, u32[]{:S(2)}) collective-permute-start(bf16[144,576]{1,0:T(8,128)(2,1)} %dynamic-slice_convert_fusion.2), channel_id=1, source_target_pairs={{0,1},{1,0},{2,3},{3,2},{4,5},{5,4},{6,7},{7,6},{8,9},{9,8},{10,11... | collective-permute-start | bytes 497672 | tf_op jit(solution)/shard_map/ppermute | solution.py:465
  7.5 15.7 %collective-permute-start.5 = (bf16[144,1536]{1,0:T(8,128)(2,1)S(1)}, bf16[144,1536]{1,0:T(8,128)(2,1)S(1)}, u32[]{:S(2)}, u32[]{:S(2)}) collective-permute-start(bf16[144,1536]{1,0:T(8,128)(2,1)S(1)} %fusion.1), channel_id=1, source_target_pairs={{0,1},{1,0},{2,3},{3,2},{4,5},{5,4},{6,7},{7,6},{8,9},{9,8},{10,11... | collective-permute-start | bytes 1327112 | tf_op jit(solution)/shard_map/ppermute | solution.py:465
  10.7 24.1 %collective-permute-start.1 = (bf16[144,960]{1,0:T(8,128)(2,1)S(1)}, bf16[144,960]{1,0:T(8,128)(2,1)}, u32[]{:S(2)}, u32[]{:S(2)}) collective-permute-start(bf16[144,960]{1,0:T(8,128)(2,1)S(1)} %dynamic-slice_convert_fusion), channel_id=1, source_target_pairs={{0,1},{1,0},{2,3},{3,2},{4,5},{5,4},{6,7},{7,6},{8,9},{9,8},{10,11... | collective-permute-start | bytes 829448 | tf_op jit(solution)/shard_map/ppermute | solution.py:465
  13.5 19.9 %collective-permute-start.9 = (bf16[192,576]{1,0:T(8,128)(2,1)}, bf16[192,576]{1,0:T(8,128)(2,1)S(1)}, u32[]{:S(2)}, u32[]{:S(2)}) collective-permute-start(bf16[192,576]{1,0:T(8,128)(2,1)} %dynamic-slice_convert_fusion.1), channel_id=1, source_target_pairs={{0,1},{1,0},{2,3},{3,2},{4,5},{5,4},{6,7},{7,6},{8,9},{9,8},{10,11... | collective-permute-start | bytes 663560 | tf_op jit(solution)/shard_map/ppermute | solution.py:465
  23.2 12.1 %collective-permute-start.6 = (bf16[144,1536]{1,0:T(8,128)(2,1)S(1)}, bf16[144,1536]{1,0:T(8,128)(2,1)S(1)}, u32[]{:S(2)}, u32[]{:S(2)}) collective-permute-start(bf16[144,1536]{1,0:T(8,128)(2,1)S(1)} %collective-permute-done.5.refs_9_.refs_13_), channel_id=1, source_target_pairs={{0,4},{2,6},{4,0},{6,2},{8,12},{10,14},{12,8},{14,10},{16,20},{18,... | collective-permute-start | bytes 1327112 | tf_op jit(solution)/shard_map/ppermute | solution.py:465
  33.4 6.6 %collective-permute-start.10 = (bf16[192,576]{1,0:T(8,128)(2,1)S(1)}, bf16[192,576]{1,0:T(8,128)(2,1)}, u32[]{:S(2)}, u32[]{:S(2)}) collective-permute-start(bf16[192,576]{1,0:T(8,128)(2,1)S(1)} %collective-permute-done.9.refs_5_.refs_8_), channel_id=1, source_target_pairs={{0,4},{2,6},{4,0},{6,2},{8,12},{10,14},{12,8},{14,10},{16,20},{18,... | collective-permute-start | bytes 663560 | tf_op jit(solution)/shard_map/ppermute | solution.py:465
  34.9 5.1 %collective-permute-start.2 = (bf16[144,960]{1,0:T(8,128)(2,1)}, bf16[144,960]{1,0:T(8,128)(2,1)}, u32[]{:S(2)}, u32[]{:S(2)}) collective-permute-start(bf16[144,960]{1,0:T(8,128)(2,1)} %collective-permute-done.1.refs_8_.refs_13_), channel_id=1, source_target_pairs={{0,2},{2,0},{4,6},{6,4},{8,10},{10,8},{12,14},{14,12},{16,18},{18,... | collective-permute-start | bytes 829448 | tf_op jit(solution)/shard_map/ppermute | solution.py:465
  34.9 14.9 %collective-permute-start.7 = (bf16[144,1536]{1,0:T(8,128)(2,1)S(1)}, bf16[144,1536]{1,0:T(8,128)(2,1)S(1)}, u32[]{:S(2)}, u32[]{:S(2)}) collective-permute-start(bf16[144,1536]{1,0:T(8,128)(2,1)S(1)} %collective-permute-done.5.refs_9_.refs_13_), channel_id=1, source_target_pairs={{0,2},{2,0},{4,6},{6,4},{8,10},{10,8},{12,14},{14,12},{16,18},{18,... | collective-permute-start | bytes 1327112 | tf_op jit(solution)/shard_map/ppermute | solution.py:465
  35.4 14.4 %collective-permute-start.8 = (bf16[144,1536]{1,0:T(8,128)(2,1)S(1)}, bf16[144,1536]{1,0:T(8,128)(2,1)}, u32[]{:S(2)}, u32[]{:S(2)}) collective-permute-start(bf16[144,1536]{1,0:T(8,128)(2,1)S(1)} %collective-permute-done.6.refs_10_.refs_14_), channel_id=1, source_target_pairs={{0,2},{2,0},{4,6},{6,4},{8,10},{10,8},{12,14},{14,12},{16,18},{18,... | collective-permute-start | bytes 1327112 | tf_op jit(solution)/shard_map/ppermute | solution.py:465
  38.4 11.4 %collective-permute-start.4 = (bf16[144,576]{1,0:T(8,128)(2,1)}, bf16[144,576]{1,0:T(8,128)(2,1)}, u32[]{:S(2)}, u32[]{:S(2)}) collective-permute-start(bf16[144,576]{1,0:T(8,128)(2,1)} %collective-permute-done.3.refs_6_.refs_18_), channel_id=1, source_target_pairs={{0,2},{2,0},{4,6},{6,4},{8,10},{10,8},{12,14},{14,12},{16,18},{18,... | collective-permute-start | bytes 497672 | tf_op jit(solution)/shard_map/ppermute | solution.py:465
  40.0 17.1 %collective-permute-start.11 = (bf16[192,576]{1,0:T(8,128)(2,1)S(1)}, bf16[192,576]{1,0:T(8,128)(2,1)}, u32[]{:S(2)}, u32[]{:S(2)}) collective-permute-start(bf16[192,576]{1,0:T(8,128)(2,1)S(1)} %collective-permute-done.9.refs_5_.refs_8_), channel_id=1, source_target_pairs={{0,2},{2,0},{4,6},{6,4},{8,10},{10,8},{12,14},{14,12},{16,18},{18,... | collective-permute-start | bytes 663560 | tf_op jit(solution)/shard_map/ppermute | solution.py:465
  40.0 17.1 %collective-permute-start.12 = (bf16[192,576]{1,0:T(8,128)(2,1)}, bf16[192,576]{1,0:T(8,128)(2,1)}, u32[]{:S(2)}, u32[]{:S(2)}) collective-permute-start(bf16[192,576]{1,0:T(8,128)(2,1)} %collective-permute-done.10.refs_6_.refs_9_), channel_id=1, source_target_pairs={{0,2},{2,0},{4,6},{6,4},{8,10},{10,8},{12,14},{14,12},{16,18},{18,... | collective-permute-start | bytes 663560 | tf_op jit(solution)/shard_map/ppermute | solution.py:465
  63.8 15.4 %collective-permute-start.25 = (bf16[2,8,144,384]{3,2,1,0:T(8,128)(2,1)}, bf16[2,8,144,384]{3,2,1,0:T(8,128)(2,1)S(1)}, u32[]{:S(2)}, u32[]{:S(2)}) collective-permute-start(bf16[2,8,144,384]{3,2,1,0:T(8,128)(2,1)} %get-tuple-element.64), channel_id=1, source_target_pairs={{0,2},{2,0},{4,6},{6,4},{8,10},{10,8},{12,14},{14,12},{16,18},{18,... | collective-permute-start | bytes 5308424 | tf_op jit(solution)/shard_map/ppermute | solution.py:465
  63.8 10.9 %collective-permute-start.37 = (bf16[2,8,48,576]{3,2,1,0:T(8,128)(2,1)S(1)}, bf16[2,8,48,576]{3,2,1,0:T(8,128)(2,1)S(1)}, u32[]{:S(2)}, u32[]{:S(2)}) collective-permute-start(bf16[2,8,48,576]{3,2,1,0:T(8,128)(2,1)S(1)} %copy-done.19), channel_id=1, source_target_pairs={{0,2},{2,0},{4,6},{6,4},{8,10},{10,8},{12,14},{14,12},{16,18},{18,... | collective-permute-start | bytes 2654216 | tf_op jit(solution)/shard_map/ppermute | solution.py:465
  74.5 2.7 %collective-permute-start.13 = (bf16[2,8,72,384]{3,2,1,0:T(8,128)(2,1)}, bf16[2,8,72,384]{3,2,1,0:T(8,128)(2,1)S(1)}, u32[]{:S(2)}, u32[]{:S(2)}) collective-permute-start(bf16[2,8,72,384]{3,2,1,0:T(8,128)(2,1)} %get-tuple-element.60), channel_id=1, source_target_pairs={{0,2},{2,0},{4,6},{6,4},{8,10},{10,8},{12,14},{14,12},{16,18},{18,... | collective-permute-start | bytes 2654216 | tf_op jit(solution)/shard_map/ppermute | solution.py:465
  75.0 14.1 %collective-permute-start.38 = (bf16[8,48,576]{2,1,0:T(8,128)(2,1)S(1)}, bf16[8,48,576]{2,1,0:T(8,128)(2,1)S(1)}, u32[]{:S(2)}, u32[]{:S(2)}) collective-permute-start(bf16[8,48,576]{2,1,0:T(8,128)(2,1)S(1)} %fusion.2), channel_id=1, source_target_pairs={{0,1},{1,0},{2,3},{3,2},{4,5},{5,4},{6,7},{7,6},{8,9},{9,8},{10,11... | collective-permute-start | bytes 1327112 | tf_op jit(solution)/shard_map/ppermute | solution.py:465
  78.4 20.2 %collective-permute-start.14 = (bf16[8,72,384]{2,1,0:T(8,128)(2,1)S(1)}, bf16[8,72,384]{2,1,0:T(8,128)(2,1)S(1)}, u32[]{:S(2)}, u32[]{:S(2)}) collective-permute-start(bf16[8,72,384]{2,1,0:T(8,128)(2,1)S(1)} %fusion.3), channel_id=1, source_target_pairs={{0,1},{1,0},{2,3},{3,2},{4,5},{5,4},{6,7},{7,6},{8,9},{9,8},{10,11... | collective-permute-start | bytes 1327112 | tf_op jit(solution)/shard_map/ppermute | solution.py:465
  79.4 37.6 %collective-permute-start.26 = (bf16[8,144,384]{2,1,0:T(8,128)(2,1)S(1)}, bf16[8,144,384]{2,1,0:T(8,128)(2,1)S(1)}, u32[]{:S(2)}, u32[]{:S(2)}) collective-permute-start(bf16[8,144,384]{2,1,0:T(8,128)(2,1)S(1)} %fusion), channel_id=1, source_target_pairs={{0,1},{1,0},{2,3},{3,2},{4,5},{5,4},{6,7},{7,6},{8,9},{9,8},{10,11... | collective-permute-start | bytes 2654216 | tf_op jit(solution)/shard_map/ppermute | solution.py:465
  89.3 11.0 %collective-permute-start.39 = (bf16[4,48,576]{2,1,0:T(8,128)(2,1)S(1)}, bf16[4,48,576]{2,1,0:T(8,128)(2,1)S(1)}, u32[]{:S(2)}, u32[]{:S(2)}) collective-permute-start(bf16[4,48,576]{2,1,0:T(8,128)(2,1)S(1)} %slice.218), channel_id=1, source_target_pairs={{0,4},{2,6},{4,0},{6,2},{8,12},{10,14},{12,8},{14,10},{16,20},{18,... | collective-permute-start | bytes 663560 | tf_op jit(solution)/shard_map/ppermute | solution.py:465
  98.7 24.4 %collective-permute-start.15 = (bf16[4,72,384]{2,1,0:T(8,128)(2,1)S(1)}, bf16[4,72,384]{2,1,0:T(8,128)(2,1)S(1)}, u32[]{:S(2)}, u32[]{:S(2)}) collective-permute-start(bf16[4,72,384]{2,1,0:T(8,128)(2,1)S(1)} %slice.219), channel_id=1, source_target_pairs={{0,4},{2,6},{4,0},{6,2},{8,12},{10,14},{12,8},{14,10},{16,20},{18,... | collective-permute-start | bytes 663560 | tf_op jit(solution)/shard_map/ppermute | solution.py:465
  117.4 11.8 %collective-permute-start.27 = (bf16[4,144,384]{2,1,0:T(8,128)(2,1)S(1)}, bf16[4,144,384]{2,1,0:T(8,128)(2,1)S(1)}, u32[]{:S(2)}, u32[]{:S(2)}) collective-permute-start(bf16[4,144,384]{2,1,0:T(8,128)(2,1)S(1)} %slice.217), channel_id=1, source_target_pairs={{0,4},{2,6},{4,0},{6,2},{8,12},{10,14},{12,8},{14,10},{16,20},{18,... | collective-permute-start | bytes 1327112 | tf_op jit(solution)/shard_map/ppermute | solution.py:465
  119.0 29.2 %collective-permute-start.40 = (bf16[48,576]{1,0:T(8,128)(2,1)S(1)}, bf16[48,576]{1,0:T(8,128)(2,1)S(1)}, u32[]{:S(2)}, u32[]{:S(2)}) collective-permute-start(bf16[48,576]{1,0:T(8,128)(2,1)S(1)} %get-tuple-element.142), channel_id=1, source_target_pairs={{0,8},{2,10},{4,12},{6,14},{8,0},{10,2},{12,4},{14,6},{16,24},{18,... | collective-permute-start | bytes 165896 | tf_op jit(solution)/shard_map/ppermute | solution.py:465
  120.6 28.1 %collective-permute-start.42 = (bf16[48,576]{1,0:T(8,128)(2,1)S(1)}, bf16[48,576]{1,0:T(8,128)(2,1)S(1)}, u32[]{:S(2)}, u32[]{:S(2)}) collective-permute-start(bf16[48,576]{1,0:T(8,128)(2,1)S(1)} %get-tuple-element.143), channel_id=1, source_target_pairs={{0,24},{2,26},{4,28},{6,30},{8,16},{10,18},{12,20},{14,22},{16,8},... | collective-permute-start | bytes 165896 | tf_op jit(solution)/shard_map/ppermute | solution.py:465
  129.4 6.1 %collective-permute-start.28 = (bf16[144,384]{1,0:T(8,128)(2,1)S(1)}, bf16[144,384]{1,0:T(8,128)(2,1)S(1)}, u32[]{:S(2)}, u32[]{:S(2)}) collective-permute-start(bf16[144,384]{1,0:T(8,128)(2,1)S(1)} %get-tuple-element.139), channel_id=1, source_target_pairs={{0,8},{2,10},{4,12},{6,14},{8,0},{10,2},{12,4},{14,6},{16,24},{18,... | collective-permute-start | bytes 331784 | tf_op jit(solution)/shard_map/ppermute | solution.py:465
  131.0 8.4 %collective-permute-start.30 = (bf16[144,384]{1,0:T(8,128)(2,1)S(1)}, bf16[144,384]{1,0:T(8,128)(2,1)S(1)}, u32[]{:S(2)}, u32[]{:S(2)}) collective-permute-start(bf16[144,384]{1,0:T(8,128)(2,1)S(1)} %get-tuple-element.140), channel_id=1, source_target_pairs={{0,24},{2,26},{4,28},{6,30},{8,16},{10,18},{12,20},{14,22},{16,8},... | collective-permute-start | bytes 331784 | tf_op jit(solution)/shard_map/ppermute | solution.py:465
  133.5 11.3 %collective-permute-start.29 = (bf16[144,384]{1,0:T(8,128)(2,1)S(1)}, bf16[144,384]{1,0:T(8,128)(2,1)S(1)}, u32[]{:S(2)}, u32[]{:S(2)}) collective-permute-start(bf16[144,384]{1,0:T(8,128)(2,1)S(1)} %get-tuple-element.141), channel_id=1, source_target_pairs={{0,16},{2,18},{4,20},{6,22},{8,24},{10,26},{12,28},{14,30},{16,0},... | collective-permute-start | bytes 331784 | tf_op jit(solution)/shard_map/ppermute | solution.py:465
  135.4 13.3 %collective-permute-start.41 = (bf16[48,576]{1,0:T(8,128)(2,1)S(1)}, bf16[48,576]{1,0:T(8,128)(2,1)S(1)}, u32[]{:S(2)}, u32[]{:S(2)}) collective-permute-start(bf16[48,576]{1,0:T(8,128)(2,1)S(1)} %get-tuple-element.144), channel_id=1, source_target_pairs={{0,16},{2,18},{4,20},{6,22},{8,24},{10,26},{12,28},{14,30},{16,0},... | collective-permute-start | bytes 165896 | tf_op jit(solution)/shard_map/ppermute | solution.py:465
  139.4 22.5 %collective-permute-start.16 = (bf16[72,384]{1,0:T(8,128)(2,1)S(1)}, bf16[72,384]{1,0:T(8,128)(2,1)S(1)}, u32[]{:S(2)}, u32[]{:S(2)}) collective-permute-start(bf16[72,384]{1,0:T(8,128)(2,1)S(1)} %get-tuple-element.145), channel_id=1, source_target_pairs={{0,8},{2,10},{4,12},{6,14},{8,0},{10,2},{12,4},{14,6},{16,24},{18,... | collective-permute-start | bytes 165896 | tf_op jit(solution)/shard_map/ppermute | solution.py:465
  144.8 20.0 %collective-permute-start.18 = (bf16[72,384]{1,0:T(8,128)(2,1)S(1)}, bf16[72,384]{1,0:T(8,128)(2,1)S(1)}, u32[]{:S(2)}, u32[]{:S(2)}) collective-permute-start(bf16[72,384]{1,0:T(8,128)(2,1)S(1)} %get-tuple-element.146), channel_id=1, source_target_pairs={{0,24},{2,26},{4,28},{6,30},{8,16},{10,18},{12,20},{14,22},{16,8},... | collective-permute-start | bytes 165896 | tf_op jit(solution)/shard_map/ppermute | solution.py:465
  148.1 6.8 %collective-permute-start.33 = (bf16[144,384]{1,0:T(8,128)(2,1)S(1)}, bf16[144,384]{1,0:T(8,128)(2,1)S(1)}, u32[]{:S(2)}, u32[]{:S(2)}) collective-permute-start(bf16[144,384]{1,0:T(8,128)(2,1)S(1)} %fusion.5), channel_id=1, source_target_pairs={{0,24},{2,26},{4,28},{6,30},{8,16},{10,18},{12,20},{14,22},{16,8},... | collective-permute-start | bytes 331784 | tf_op jit(solution)/shard_map/ppermute | solution.py:465
  148.7 10.8 %collective-permute-start.32 = (bf16[144,384]{1,0:T(8,128)(2,1)S(1)}, bf16[144,384]{1,0:T(8,128)(2,1)S(1)}, u32[]{:S(2)}, u32[]{:S(2)}) collective-permute-start(bf16[144,384]{1,0:T(8,128)(2,1)S(1)} %fusion.5), channel_id=1, source_target_pairs={{0,16},{2,18},{4,20},{6,22},{8,24},{10,26},{12,28},{14,30},{16,0},... | collective-permute-start | bytes 331784 | tf_op jit(solution)/shard_map/ppermute | solution.py:465
  148.7 12.4 %collective-permute-start.31 = (bf16[144,384]{1,0:T(8,128)(2,1)S(1)}, bf16[144,384]{1,0:T(8,128)(2,1)S(1)}, u32[]{:S(2)}, u32[]{:S(2)}) collective-permute-start(bf16[144,384]{1,0:T(8,128)(2,1)S(1)} %fusion.5), channel_id=1, source_target_pairs={{0,8},{2,10},{4,12},{6,14},{8,0},{10,2},{12,4},{14,6},{16,24},{18,... | collective-permute-start | bytes 331784 | tf_op jit(solution)/shard_map/ppermute | solution.py:465
  154.9 11.3 %collective-permute-start.17 = (bf16[72,384]{1,0:T(8,128)(2,1)S(1)}, bf16[72,384]{1,0:T(8,128)(2,1)S(1)}, u32[]{:S(2)}, u32[]{:S(2)}) collective-permute-start(bf16[72,384]{1,0:T(8,128)(2,1)S(1)} %get-tuple-element.147), channel_id=1, source_target_pairs={{0,16},{2,18},{4,20},{6,22},{8,24},{10,26},{12,28},{14,30},{16,0},... | collective-permute-start | bytes 165896 | tf_op jit(solution)/shard_map/ppermute | solution.py:465
  159.5 8.5 %collective-permute-start.45 = (bf16[48,576]{1,0:T(8,128)(2,1)S(1)}, bf16[48,576]{1,0:T(8,128)(2,1)S(1)}, u32[]{:S(2)}, u32[]{:S(2)}) collective-permute-start(bf16[48,576]{1,0:T(8,128)(2,1)S(1)} %fusion.7), channel_id=1, source_target_pairs={{0,24},{2,26},{4,28},{6,30},{8,16},{10,18},{12,20},{14,22},{16,8},... | collective-permute-start | bytes 165896 | tf_op jit(solution)/shard_map/ppermute | solution.py:465
  161.1 7.6 %collective-permute-start.44 = (bf16[48,576]{1,0:T(8,128)(2,1)S(1)}, bf16[48,576]{1,0:T(8,128)(2,1)S(1)}, u32[]{:S(2)}, u32[]{:S(2)}) collective-permute-start(bf16[48,576]{1,0:T(8,128)(2,1)S(1)} %fusion.7), channel_id=1, source_target_pairs={{0,16},{2,18},{4,20},{6,22},{8,24},{10,26},{12,28},{14,30},{16,0},... | collective-permute-start | bytes 165896 | tf_op jit(solution)/shard_map/ppermute | solution.py:465
  162.0 8.8 %collective-permute-start.43 = (bf16[48,576]{1,0:T(8,128)(2,1)S(1)}, bf16[48,576]{1,0:T(8,128)(2,1)S(1)}, u32[]{:S(2)}, u32[]{:S(2)}) collective-permute-start(bf16[48,576]{1,0:T(8,128)(2,1)S(1)} %fusion.7), channel_id=1, source_target_pairs={{0,8},{2,10},{4,12},{6,14},{8,0},{10,2},{12,4},{14,6},{16,24},{18,... | collective-permute-start | bytes 165896 | tf_op jit(solution)/shard_map/ppermute | solution.py:465
  164.7 10.7 %collective-permute-start.34 = (bf16[4,144,384]{2,1,0:T(8,128)(2,1)}, bf16[4,144,384]{2,1,0:T(8,128)(2,1)}, u32[]{:S(2)}, u32[]{:S(2)}) collective-permute-start(bf16[4,144,384]{2,1,0:T(8,128)(2,1)} %pad_maximum_fusion.refs_0_), channel_id=1, source_target_pairs={{0,4},{2,6},{4,0},{6,2},{8,12},{10,14},{12,8},{14,10},{16,20},{18,... | collective-permute-start | bytes 1327112 | tf_op jit(solution)/shard_map/ppermute | solution.py:465
  166.3 6.0 %collective-permute-start.21 = (bf16[72,384]{1,0:T(8,128)(2,1)S(1)}, bf16[72,384]{1,0:T(8,128)(2,1)S(1)}, u32[]{:S(2)}, u32[]{:S(2)}) collective-permute-start(bf16[72,384]{1,0:T(8,128)(2,1)S(1)} %fusion.9), channel_id=1, source_target_pairs={{0,24},{2,26},{4,28},{6,30},{8,16},{10,18},{12,20},{14,22},{16,8},... | collective-permute-start | bytes 165896 | tf_op jit(solution)/shard_map/ppermute | solution.py:465
  168.0 5.6 %collective-permute-start.20 = (bf16[72,384]{1,0:T(8,128)(2,1)S(1)}, bf16[72,384]{1,0:T(8,128)(2,1)S(1)}, u32[]{:S(2)}, u32[]{:S(2)}) collective-permute-start(bf16[72,384]{1,0:T(8,128)(2,1)S(1)} %fusion.9), channel_id=1, source_target_pairs={{0,16},{2,18},{4,20},{6,22},{8,24},{10,26},{12,28},{14,30},{16,0},... | collective-permute-start | bytes 165896 | tf_op jit(solution)/shard_map/ppermute | solution.py:465
  168.7 4.8 %collective-permute-start.19 = (bf16[72,384]{1,0:T(8,128)(2,1)S(1)}, bf16[72,384]{1,0:T(8,128)(2,1)S(1)}, u32[]{:S(2)}, u32[]{:S(2)}) collective-permute-start(bf16[72,384]{1,0:T(8,128)(2,1)S(1)} %fusion.9), channel_id=1, source_target_pairs={{0,8},{2,10},{4,12},{6,14},{8,0},{10,2},{12,4},{14,6},{16,24},{18,... | collective-permute-start | bytes 165896 | tf_op jit(solution)/shard_map/ppermute | solution.py:465
  171.5 55.5 %collective-permute-start.47 = (bf16[4,48,576]{2,1,0:T(8,128)(2,1)}, bf16[4,48,576]{2,1,0:T(8,128)(2,1)}, u32[]{:S(2)}, u32[]{:S(2)}) collective-permute-start(bf16[4,48,576]{2,1,0:T(8,128)(2,1)} %pad_maximum_fusion.1.refs_0_), channel_id=1, source_target_pairs={{0,2},{2,0},{4,6},{6,4},{8,10},{10,8},{12,14},{14,12},{16,18},{18,... | collective-permute-start | bytes 663560 | tf_op jit(solution)/shard_map/ppermute | solution.py:465
  172.3 54.7 %collective-permute-start.46 = (bf16[4,48,576]{2,1,0:T(8,128)(2,1)}, bf16[4,48,576]{2,1,0:T(8,128)(2,1)}, u32[]{:S(2)}, u32[]{:S(2)}) collective-permute-start(bf16[4,48,576]{2,1,0:T(8,128)(2,1)} %pad_maximum_fusion.1.refs_0_), channel_id=1, source_target_pairs={{0,4},{2,6},{4,0},{6,2},{8,12},{10,14},{12,8},{14,10},{16,20},{18,... | collective-permute-start | bytes 663560 | tf_op jit(solution)/shard_map/ppermute | solution.py:465
  174.3 53.3 %collective-permute-start.22 = (bf16[4,72,384]{2,1,0:T(8,128)(2,1)}, bf16[4,72,384]{2,1,0:T(8,128)(2,1)}, u32[]{:S(2)}, u32[]{:S(2)}) collective-permute-start(bf16[4,72,384]{2,1,0:T(8,128)(2,1)} %pad_maximum_fusion.2.refs_0_), channel_id=1, source_target_pairs={{0,4},{2,6},{4,0},{6,2},{8,12},{10,14},{12,8},{14,10},{16,20},{18,... | collective-permute-start | bytes 663560 | tf_op jit(solution)/shard_map/ppermute | solution.py:465
  175.4 77.6 %collective-permute-start.35 = (bf16[4,144,384]{2,1,0:T(8,128)(2,1)}, bf16[4,144,384]{2,1,0:T(8,128)(2,1)}, u32[]{:S(2)}, u32[]{:S(2)}) collective-permute-start(bf16[4,144,384]{2,1,0:T(8,128)(2,1)} %pad_maximum_fusion.refs_0_), channel_id=1, source_target_pairs={{0,2},{2,0},{4,6},{6,4},{8,10},{10,8},{12,14},{14,12},{16,18},{18,... | collective-permute-start | bytes 1327112 | tf_op jit(solution)/shard_map/ppermute | solution.py:465
  175.4 77.6 %collective-permute-start.36 = (bf16[4,144,384]{2,1,0:T(8,128)(2,1)}, bf16[4,144,384]{2,1,0:T(8,128)(2,1)}, u32[]{:S(2)}, u32[]{:S(2)}) collective-permute-start(bf16[4,144,384]{2,1,0:T(8,128)(2,1)} %collective-permute-done.34.refs_1_), channel_id=1, source_target_pairs={{0,2},{2,0},{4,6},{6,4},{8,10},{10,8},{12,14},{14,12},{16,18},{18,... | collective-permute-start | bytes 1327112 | tf_op jit(solution)/shard_map/ppermute | solution.py:465
  227.0 17.3 %collective-permute-start.23 = (bf16[4,72,384]{2,1,0:T(8,128)(2,1)}, bf16[4,72,384]{2,1,0:T(8,128)(2,1)S(1)}, u32[]{:S(2)}, u32[]{:S(2)}) collective-permute-start(bf16[4,72,384]{2,1,0:T(8,128)(2,1)} %pad_maximum_fusion.2.refs_0_), channel_id=1, source_target_pairs={{0,2},{2,0},{4,6},{6,4},{8,10},{10,8},{12,14},{14,12},{16,18},{18,... | collective-permute-start | bytes 663560 | tf_op jit(solution)/shard_map/ppermute | solution.py:465
  227.5 16.7 %collective-permute-start.24 = (bf16[4,72,384]{2,1,0:T(8,128)(2,1)}, bf16[4,72,384]{2,1,0:T(8,128)(2,1)S(1)}, u32[]{:S(2)}, u32[]{:S(2)}) collective-permute-start(bf16[4,72,384]{2,1,0:T(8,128)(2,1)} %collective-permute-done.22.refs_1_), channel_id=1, source_target_pairs={{0,2},{2,0},{4,6},{6,4},{8,10},{10,8},{12,14},{14,12},{16,18},{18,... | collective-permute-start | bytes 663560 | tf_op jit(solution)/shard_map/ppermute | solution.py:465
  (21 other events, 351.8 us)

commit v2 on v1

v2 whole, which is shorter than its diff:
```python
import functools

import jax
import jax.numpy as jnp
import numpy as np
from jax import lax
from jax.experimental import pallas as pl
from jax.experimental.pallas import tpu as pltpu
from jax.sharding import PartitionSpec as P

HEADS = 9
KV_HEADS = 3
GROUP = HEADS // KV_HEADS
HEAD = 64
FF = 1536
STEP = 10
QUERY = HEADS * HEAD
ROPED = (HEADS + KV_HEADS) * HEAD
QKV = (HEADS + 2 * KV_HEADS) * HEAD
LANES = 128

EPS_NORM = 1e-05
ROPE_BASE = 100000.0
BETA_ONE = 0.9
BETA_TWO = 0.95
RATE_MATRIX = 0.1
RATE_GAIN = 0.3
DECAY_MATRIX = 0.1
EPS_ADAM = 1e-08
MASKED = -1e30
SCALE = float(HEAD) ** (-0.5)
VMEM_LIMIT = 56 * 1024 * 1024
HALF = 144
CUT_ROWS = 72
CUT_COLUMNS = 384
F32 = jnp.float32
BF16 = jnp.bfloat16


def rotate_block(values, cosine, signed_sine):
    lane = lax.broadcasted_iota(jnp.int32, values.shape, 1)
    swapped = jnp.where(
        lane % HEAD < HEAD // 2,
        pltpu.roll(values, LANES - HEAD // 2, 1),
        pltpu.roll(values, HEAD // 2, 1),
    )
    return values * cosine + swapped * signed_sine


def adamw(weight, first_moment, second_moment, gradient, step_rate, weight_decay):
    first_new = BETA_ONE * first_moment + (1.0 - BETA_ONE) * gradient
    second_new = BETA_TWO * second_moment + (1.0 - BETA_TWO) * gradient * gradient
    fix_one = 1.0 - BETA_ONE**STEP
    fix_two = 1.0 - BETA_TWO**STEP
    update = first_new / fix_one / (jnp.sqrt(second_new / fix_two) + EPS_ADAM)
    return (first_new, second_new, weight - step_rate * (update + weight_decay * weight))


def dot(left, right):
    return lax.dot_general(left, right, (((1,), (0,)), ((), ())), preferred_element_type=F32)


def dot_right_t(left, right):
    return lax.dot_general(left, right, (((1,), (1,)), ((), ())), preferred_element_type=F32)


def dot_left_t(left, right):
    return lax.dot_general(left, right, (((0,), (0,)), ((), ())), preferred_element_type=F32)


def norm_scale(values):
    return lax.rsqrt(jnp.mean(values * values, axis=-1, keepdims=True) + EPS_NORM)


def norm_back(grad_normed, normed, scale_rows):
    return scale_rows * (
        grad_normed - normed * jnp.mean(grad_normed * normed, axis=-1, keepdims=True)
    )


class Weight:
    def __init__(self, shape, whole=None, own=None, parts=(), place=None, own_place=None):
        self.shape, self.place, self.own_place = shape, place, own_place
        self.parts = parts
        self.arrays = [whole] if whole is not None else [own] + [p[0] for p in parts]
        self.split = whole is None

    def scratch(self):
        return [pltpu.VMEM(self.shape, BF16)] if self.split else []

    def load(self, idx, refs, scratch):
        if not self.split:
            return refs[0]
        full = scratch[0]
        self.put(full, self.own_place(idx[0]), refs[0][...].astype(BF16))
        for ref, (_, columns, (core, x)) in zip(refs[1:], self.parts):
            value = ref[...] if columns is None else ref[:HALF, columns[0] : columns[1]]
            self.put(full, self.place(1 - idx[0], idx[1] ^ core, idx[2] ^ x), value)
        return full

    def put(self, full, position, value):
        rows, columns = slice(None), slice(None)
        if value.shape[0] < self.shape[0]:
            rows = pl.ds(pl.multiple_of(position[0], 16), value.shape[0])
        if value.shape[1] < self.shape[1]:
            columns = pl.ds(pl.multiple_of(position[1], LANES), value.shape[1])
        full[rows, columns] = value


def call(body, idx, arrays, weights, outs, scratch, flops, name):
    counts = [len(w.arrays) for w in weights]
    flat = list(arrays) + [a for w in weights for a in w.arrays]
    weight_scratch = [w.scratch() for w in weights]

    def kernel(*refs):
        refs = list(refs)
        idx_ref = refs.pop(0)
        take = lambda n: [refs.pop(0) for _ in range(n)]
        array_refs = take(len(arrays))
        weight_refs = [take(n) for n in counts]
        out_refs = take(len(outs))
        own_scratch = take(len(scratch))
        scratch_refs = [take(len(s)) for s in weight_scratch]
        loads = [
            functools.partial(w.load, idx_ref, r, s)
            for w, r, s in zip(weights, weight_refs, scratch_refs)
        ]
        body(idx_ref, array_refs, loads, out_refs, own_scratch)

    moved = sum(a.size * a.dtype.itemsize for a in flat)
    moved += sum(o.size * o.dtype.itemsize for o in outs)
    return pl.pallas_call(
        kernel,
        out_shape=tuple(outs),
        in_specs=[pl.BlockSpec(memory_space=pltpu.SMEM)]
        + [pl.BlockSpec(memory_space=pltpu.VMEM)] * len(flat),
        out_specs=tuple([pl.BlockSpec(memory_space=pltpu.VMEM)] * len(outs)),
        scratch_shapes=list(scratch) + [s for group in weight_scratch for s in group],
        compiler_params=pltpu.CompilerParams(vmem_limit_bytes=VMEM_LIMIT),
        cost_estimate=pl.CostEstimate(flops=flops, bytes_accessed=moved, transcendentals=0),
        name=name,
    )(idx, *flat)


def sds(shape, dtype):
    return jax.ShapeDtypeStruct(shape, dtype)


class Pieces:
    def __init__(self, place, parts=1, extra=0):
        self.place, self.parts, self.extra = place, parts, extra

    def outs(self):
        return [sds((self.parts, 2, 8, CUT_ROWS + self.extra, CUT_COLUMNS), BF16)] * 2

    def scratch(self, columns):
        return pltpu.VMEM((8, CUT_ROWS, columns), BF16)

    def store(self, blocks, grad, start=0):
        for i in range(8):
            rows = grad[i * CUT_ROWS : (i + 1) * CUT_ROWS].astype(BF16)
            blocks[i, :, start : start + grad.shape[1]] = rows

    def emit(self, idx, blocks, outs, under=None):
        for other_core, out in enumerate((outs[1], outs[0])):
            for part in range(self.parts):
                for owner in range(2):
                    for slot in range(8):
                        z = ((slot >> 1) & 1) | ((slot & 1) << 1)
                        block, column = self.place(
                            idx[0] ^ owner, idx[1] ^ other_core, idx[2] ^ (slot >> 2), idx[3] ^ z, part
                        )
                        columns = pl.ds(pl.multiple_of(column * CUT_COLUMNS, LANES), CUT_COLUMNS)
                        piece = blocks[block, :, columns]
                        if under is not None:
                            piece = jnp.concatenate(
                                [piece.astype(F32), under[idx[0] ^ owner]], axis=0
                            ).astype(BF16)
                        out[part, owner, slot] = piece


def head_stack(values, kv_head):
    first = kv_head * GROUP
    return jnp.concatenate(
        [values[:, (first + i) * HEAD : (first + i + 1) * HEAD] for i in range(GROUP)], axis=0
    )


def softmax_rows(query, key, allowed):
    scores = jnp.where(allowed, dot_right_t(query, key) * SCALE, MASKED)
    top = jnp.max(scores, axis=-1, keepdims=True)
    exponent = jnp.exp(scores - top)
    return exponent / jnp.sum(exponent, axis=-1, keepdims=True)


def pack_weights(idx, w_qkv, w_out, w_gate_up, down_t, norm_gains):
    width = w_out.shape[1]

    def kernel(idx_ref, q_ref, o_ref, g_ref, d_ref, gains_ref, qo_out, g_out, d_out):
        g_out[...] = g_ref[...].astype(BF16)
        qo_out[:HALF, :QKV] = q_ref[...].astype(BF16)
        qo_out[:HALF, QKV:] = o_ref[...].astype(BF16)
        qo_out[HALF:, :] = jnp.zeros((16, QKV + width), BF16)
        qo_out[HALF : HALF + 2, : gains_ref.shape[1]] = gains_ref[...].astype(BF16)
        d_out[...] = d_ref[...].astype(BF16)

    outs = (
        sds((HALF + 16, QKV + width), BF16),
        sds((HALF, FF), BF16),
        sds((HALF, down_t.shape[1]), BF16),
    )
    return pl.pallas_call(
        kernel,
        grid_spec=pltpu.PrefetchScalarGridSpec(
            num_scalar_prefetch=1,
            grid=(1,),
            in_specs=[
                pl.BlockSpec((HALF, QKV), lambda t, i: (i[1], 0)),
                pl.BlockSpec((HALF, width), lambda t, i: (i[1], 0)),
                pl.BlockSpec((HALF, FF), lambda t, i: (i[1], i[2])),
                pl.BlockSpec((HALF, down_t.shape[1]), lambda t, i: (i[1] * 2 + i[2], 0)),
                pl.BlockSpec(norm_gains.shape, lambda t, i: (0, 0)),
            ],
            out_specs=tuple(pl.BlockSpec(o.shape, lambda t, i: (0, 0)) for o in outs),
        ),
        out_shape=outs,
        compiler_params=pltpu.CompilerParams(vmem_limit_bytes=VMEM_LIMIT),
        name="pack_weights",
    )(idx, w_qkv, w_out, w_gate_up, down_t, norm_gains)


def attention_forward(idx, tokens_t, segments, frequency, gains, w_qkv):
    width, seq_length = tokens_t.shape
    split_gains = len(gains) > 1

    def body(idx_ref, arrays, loads, outs, scratch):
        x_ref, seg_ref, freq_ref = arrays[:3]
        qkv_ref, o_ref, cos_ref, sin_ref, allowed_ref, gains_ref = outs
        if split_gains:
            own = arrays[3][...].astype(BF16).astype(F32)
            other = arrays[4][HALF : HALF + 8, : width // 2].astype(F32)[:2]
            gains_ref[...] = jnp.where(
                idx_ref[0] == 0,
                jnp.concatenate([own, other], axis=1),
                jnp.concatenate([other, own], axis=1),
            )
        else:
            gains_ref[...] = arrays[3][...]
        seen_doc = jnp.broadcast_to(seg_ref[...], (seq_length, seq_length))
        own_doc = seen_doc.T
        token = lax.broadcasted_iota(jnp.int32, (seq_length, seq_length), 0)
        seen = lax.broadcasted_iota(jnp.int32, (seq_length, seq_length), 1)
        begin = jnp.sum((seen_doc < own_doc).astype(F32), axis=-1, keepdims=True)
        angles = (token.astype(F32) - begin) * freq_ref[...]
        cosine, sine = jnp.cos(angles), jnp.sin(angles)
        sine = jnp.where(seen % HEAD < HEAD // 2, -sine, sine)
        cos_ref[...] = cosine
        sin_ref[...] = sine
        allowed = ((seen_doc == own_doc) & (token >= seen)).astype(F32)
        allowed_ref[...] = allowed
        allowed = jnp.concatenate([allowed] * GROUP, axis=0) > 0.5
        x = x_ref[...].astype(F32).T
        h1 = (x * norm_scale(x) * gains_ref[0:1, :]).astype(BF16)
        projected = dot(h1, loads[0]()[...])
        for start in range(0, ROPED, LANES):
            block = projected[:, start : start + LANES]
            qkv_ref[:, start : start + LANES] = rotate_block(block, cosine, sine).astype(BF16)
        qkv_ref[:, ROPED:QKV] = projected[:, ROPED:QKV].astype(BF16)
        qkv = qkv_ref[...]
        for kv in range(KV_HEADS):
            key = qkv[:, QUERY + kv * HEAD : QUERY + (kv + 1) * HEAD]
            value = qkv[:, ROPED + kv * HEAD : ROPED + (kv + 1) * HEAD]
            probs = softmax_rows(head_stack(qkv, kv), key, allowed).astype(BF16)
            attended = dot(probs, value).astype(BF16)
            for i in range(GROUP):
                start = (kv * GROUP + i) * HEAD
                o_ref[:, start : start + HEAD] = attended[i * seq_length : (i + 1) * seq_length]

    square = sds((seq_length, seq_length), F32)
    outs = [sds((seq_length, QKV), BF16), sds((seq_length, QUERY), BF16)]
    outs += [square, square, square, sds((2, width), F32)]
    return call(
        body,
        idx,
        [tokens_t, segments, frequency, *gains],
        [w_qkv],
        outs,
        [],
        2 * 128 * 576 * 960,
        "attention",
    )


def feed_forward(idx, tokens_t, attended, gains, cotangent_t, w_out, w_gate_up, pieces):
    width, seq_length = tokens_t.shape

    def body(idx_ref, arrays, loads, outs, scratch):
        x_ref, o_ref, gains_ref, y_ref = arrays
        u_ref, h2_ref, ab_ref, z_ref = outs[:4]
        u = x_ref[...].astype(F32).T + dot(o_ref[...], loads[0]()[...])
        u_ref[...] = u
        h2 = (u * norm_scale(u) * gains_ref[1:2, :]).astype(BF16)
        h2_ref[...] = h2
        ab = dot(h2, loads[1]()[...])
        ab_ref[...] = ab
        gate, up = ab[:, :FF], ab[:, FF:]
        z = (gate * jax.nn.sigmoid(gate) * up).astype(BF16)
        z_ref[...] = z
        grad = dot(y_ref[...], z)
        if pieces is None:
            outs[4][...] = grad
        else:
            pieces.store(scratch[0], grad)
            pieces.emit(idx_ref, scratch[0], outs[4:])

    outs = [
        sds((seq_length, width), F32),
        sds((seq_length, width), BF16),
        sds((seq_length, 2 * FF), F32),
        sds((seq_length, FF), BF16),
    ]
    outs += [sds((width, FF), F32)] if pieces is None else pieces.outs()
    scratch = [] if pieces is None else [pieces.scratch(FF)]
    return call(
        body,
        idx,
        [tokens_t, attended, gains, cotangent_t],
        [w_out, w_gate_up],
        outs,
        scratch,
        2 * 128 * 576 * 5200,
        "feed_forward",
    )


def feed_back(idx, ab, normed_low, hidden, middle, cotangent_t, down_t, pieces):
    width, seq_length = cotangent_t.shape

    def body(idx_ref, arrays, loads, outs, scratch):
        ab_ref, h2_ref, z_ref, u_ref, y_ref = arrays
        gg_ref, out_ref = outs[:2]
        down = loads[0]()
        gate, up = ab_ref[:, :FF], ab_ref[:, FF:]
        sig = jax.nn.sigmoid(gate)
        grad_hidden = dot_left_t(y_ref[...], down[...])
        gg_ref[:, :FF] = (grad_hidden * up * sig * (1.0 + gate * (1.0 - sig))).astype(BF16)
        gg_ref[:, FF:] = (grad_hidden * gate * sig).astype(BF16)
        grad = dot_left_t(h2_ref[...], gg_ref[...])
        if pieces is None:
            outs[2][...] = grad
        else:
            pieces.store(scratch[0], grad)
            pieces.emit(idx_ref, scratch[0], outs[2:])
        out_ref[...] = (u_ref[...] + dot_right_t(z_ref[...], down[...])).T.astype(BF16)

    outs = [sds((seq_length, 2 * FF), BF16), sds((width, seq_length), BF16)]
    outs += [sds((width, 2 * FF), F32)] if pieces is None else pieces.outs()
    scratch = [] if pieces is None else [pieces.scratch(2 * FF)]
    return call(
        body,
        idx,
        [ab, normed_low, hidden, middle, cotangent_t],
        [down_t],
        outs,
        scratch,
        2 * 128 * 576 * 6200,
        "feed_back",
    )


def attention_back(
    idx, tokens_t, cotangent_t, middle, gated, qkv, attended, tables, gains, weights, pieces
):
    width, seq_length = tokens_t.shape

    def body(idx_ref, arrays, loads, outs, scratch):
        x_ref, y_ref, u_ref, gg_ref, qkv_ref, o_ref = arrays[:6]
        cos_ref, sin_ref, allowed_ref, gains_ref = arrays[6:]
        grad_ref = outs[0]
        grad_proj, gp_ref, gain_rows, *blocks = scratch
        u = u_ref[...]
        scale_two = norm_scale(u)
        normed = u * scale_two
        grad_normed = dot_right_t(gg_ref[...], loads[0]()[...])
        grad_gain_two = jnp.sum(grad_normed * normed, axis=0, keepdims=True)
        gu = y_ref[...].astype(F32).T + norm_back(
            grad_normed * gains_ref[1:2, :], normed, scale_two
        )
        gu_low = gu.astype(BF16)
        go = dot_right_t(gu_low, loads[1]()[...]).astype(BF16)
        allowed = jnp.concatenate([allowed_ref[...]] * GROUP, axis=0) > 0.5
        qkv_values = qkv_ref[...]
        for kv in range(KV_HEADS):
            key = qkv_values[:, QUERY + kv * HEAD : QUERY + (kv + 1) * HEAD]
            value = qkv_values[:, ROPED + kv * HEAD : ROPED + (kv + 1) * HEAD]
            query = head_stack(qkv_values, kv)
            grad_out = head_stack(go, kv)
            probs = softmax_rows(query, key, allowed)
            grad_probs = dot_right_t(grad_out, value)
            row_delta = jnp.sum(probs * grad_probs, axis=-1, keepdims=True)
            gs = (probs * (grad_probs - row_delta)).astype(BF16)
            grad_query = dot(gs, key) * SCALE
            for i in range(GROUP):
                start = (kv * GROUP + i) * HEAD
                grad_proj[:, start : start + HEAD] = grad_query[
                    i * seq_length : (i + 1) * seq_length
                ]
            start = QUERY + kv * HEAD
            grad_proj[:, start : start + HEAD] = dot_left_t(gs, query) * SCALE
            start = ROPED + kv * HEAD
            grad_proj[:, start : start + HEAD] = dot_left_t(probs.astype(BF16), grad_out)
        for start in range(0, ROPED, LANES):
            gp_ref[:, start : start + LANES] = rotate_block(
                grad_proj[:, start : start + LANES], cos_ref[...], -sin_ref[...]
            ).astype(BF16)
        gp_ref[:, ROPED:QKV] = grad_proj[:, ROPED:QKV].astype(BF16)
        x = x_ref[...].astype(F32).T
        scale_one = norm_scale(x)
        normed = x * scale_one
        h1 = (normed * gains_ref[0:1, :]).astype(BF16)
        grad_qkv = dot_left_t(h1, gp_ref[...])
        grad_out = dot_left_t(o_ref[...], gu_low)
        grad_normed = dot_right_t(gp_ref[...], loads[2]()[...])
        grad_gain_one = jnp.sum(grad_normed * normed, axis=0, keepdims=True)
        if pieces is None:
            outs[1][:, :QKV] = grad_qkv
            outs[1][:, QKV:] = grad_out
            outs[2][0:1, :] = grad_gain_one
            outs[2][1:2, :] = grad_gain_two
        else:
            pieces.store(blocks[0], grad_qkv)
            pieces.store(blocks[0], grad_out, QKV)
            half = width // 2
            gain_rows[...] = jnp.zeros_like(gain_rows)
            for owner in range(2):
                columns = slice(owner * half, (owner + 1) * half)
                gain_rows[owner, 0:1, :half] = grad_gain_one[:, columns]
                gain_rows[owner, 1:2, :half] = grad_gain_two[:, columns]
            pieces.emit(idx_ref, blocks[0], outs[1:], gain_rows)
        grad_ref[...] = (
            (gu + norm_back(grad_normed * gains_ref[0:1, :], normed, scale_one)).T
        ).astype(BF16)

    outs = [sds((width, seq_length), BF16)]
    scratch = [
        pltpu.VMEM((seq_length, QKV), F32),
        pltpu.VMEM((seq_length, QKV), BF16),
        pltpu.VMEM((2, 8, CUT_COLUMNS), F32),
    ]
    if pieces is None:
        outs += [sds((width, QKV + width), F32), sds((2, width), F32)]
    else:
        outs += pieces.outs()
        scratch += [pieces.scratch(QKV + width)]
    return call(
        body,
        idx,
        [tokens_t, cotangent_t, middle, gated, qkv, attended, *tables, gains],
        weights,
        outs,
        scratch,
        2 * 128 * 576 * 8000,
        "attention_back",
    )


def update_state(summed, parts, blocks, puts, state, shape, name, gains=()):
    count = len(state) // 3
    height, width = summed.shape[2:]
    by_z = summed.reshape(4, 4, *summed.shape[1:])

    def kernel(*refs):
        part_refs, refs = refs[: len(parts)], refs[len(parts) :]
        state_refs, refs = refs[: 3 * count], refs[3 * count :]
        gain_refs, refs = refs[: len(gains)], refs[len(gains) :]
        outs, refs = refs[: 3 * count], refs[3 * count :]
        gain_outs, full = refs[: len(gains)], refs[-1]
        for ref, put in zip(part_refs, puts):
            for z in range(4):
                put(full, z, ref[z, 0, 0].astype(F32))
        start = 0
        for i in range(count):
            columns = state_refs[i].shape[1]
            first, second, new = adamw(
                state_refs[i][...],
                state_refs[count + i][...],
                state_refs[2 * count + i][...],
                full[: state_refs[i].shape[0], start : start + columns],
                RATE_MATRIX,
                DECAY_MATRIX,
            )
            start += columns
            outs[i][...] = first
            outs[count + i][...] = second
            outs[2 * count + i][...] = new
        if gains:

            @pl.when(pl.program_id(0) == 0)
            def _():
                gradient = full[CUT_ROWS : CUT_ROWS + 2, : gain_refs[0].shape[1]]
                first, second, new = adamw(
                    gain_refs[0][...], gain_refs[1][...], gain_refs[2][...], gradient, RATE_GAIN, 0.0
                )
                gain_outs[0][...] = first
                gain_outs[1][...] = second
                gain_outs[2][...] = new

    state_specs = [pl.BlockSpec(*blocks[i]) for i in range(count)] * 3
    gain_specs = [pl.BlockSpec(g.shape, lambda t: (0, 0)) for g in gains]
    part_specs = [
        pl.BlockSpec((4, 1, 1, height, width), lambda t, p=p: (0, t, p, 0, 0)) for p in parts
    ]
    moved = sum(a.size * 8 for a in state)
    return pl.pallas_call(
        kernel,
        grid=(4,),
        in_specs=part_specs + state_specs + gain_specs,
        out_specs=tuple(state_specs + gain_specs),
        scratch_shapes=[pltpu.VMEM(shape, F32)],
        out_shape=tuple(sds(a.shape, F32) for a in [*state, *gains]),
        compiler_params=pltpu.CompilerParams(vmem_limit_bytes=VMEM_LIMIT),
        cost_estimate=pl.CostEstimate(flops=0, bytes_accessed=moved, transcendentals=0),
        name=name,
    )(*[by_z] * len(parts), *state, *gains)


def swap(values, axis, mask):
    size = lax.axis_size(axis)
    return lax.ppermute(values, axis, [(i, i ^ mask) for i in range(size)])


def sum_over_plane(keep, arrived, across_first):
    total = keep.astype(F32) + arrived.astype(F32)
    if across_first:
        total = total[0] + swap(total[1].astype(BF16), "shard", 1).astype(F32)
        return total[:4] + swap(total[4:].astype(BF16), "dp", 2).astype(F32)
    total = total[:, :4] + swap(total[:, 4:].astype(BF16), "dp", 2).astype(F32)
    return total[0] + swap(total[1].astype(BF16), "shard", 1).astype(F32)


def sum_over_line(totals):
    totals = totals[:, :2] + swap(totals[:, 2:].astype(BF16), "dp", 4).astype(F32)
    piece = totals[:, 0] + swap(totals[:, 1].astype(BF16), "dp", 8).astype(F32)
    return lax.all_gather(piece.astype(BF16), "dp", axis=0)


def spread(mine):
    near = swap(mine, "shard", 1)
    near_x = swap(near, "dp", 2)
    return [
        (near, None, (0, 0)),
        (near_x, None, (0, 1)),
        (swap(near, "dp", 1), None, (1, 0)),
        (swap(near_x, "dp", 1), None, (1, 1)),
    ]


def per_device(
    tokens,
    segments,
    cotangent,
    w_qkv,
    w_out,
    w_gate_up,
    w_down,
    norm_gains,
    first_qkv,
    first_out,
    first_gate_up,
    first_down,
    first_gains,
    second_qkv,
    second_out,
    second_gate_up,
    second_down,
    second_gains,
):
    groups = lax.axis_size("shard")
    replicas = lax.axis_size("dp")
    fast = groups == 2 and replicas == 16
    place_dp = lax.axis_index("dp")
    owner = lax.axis_index("shard")
    idx = jnp.stack([owner, place_dp & 1, (place_dp >> 1) & 1, place_dp >> 2]).astype(jnp.int32)
    x_t, y_t = tokens[0].T, cotangent[0].T
    width, seq_length = x_t.shape
    rows, down_rows = w_qkv.shape[0], w_down.shape[0]
    down_t, first_down_t, second_down_t = w_down.T, first_down.T, second_down.T
    half_size = HEAD // 2
    frequency = ROPE_BASE ** (-(np.arange(half_size) * 2.0 / HEAD))
    frequency = jnp.asarray(np.tile(frequency, 4)[None], F32)
    if fast:
        qo, gate_up, down = pack_weights(idx, w_qkv, w_out, w_gate_up, down_t, norm_gains)
        gate_up_parts = spread(gate_up)
        qo_near = swap(qo, "shard", 1)
        qo_far = swap(qo_near, "dp", 1)
        down_parts = spread(down)
        gains = (norm_gains, qo_near)
        by_rows = lambda o, c, x: (o * rows + c * HALF, 0)
        own_rows = lambda o: (o * rows, 0)
        rels = ((0, 0), (1, 0))
        mat_qkv = Weight(
            (width, QKV),
            own=w_qkv,
            parts=[(a, (0, QKV), r) for a, r in zip((qo_near, qo_far), rels)],
            place=by_rows,
            own_place=own_rows,
        )
        mat_out = Weight(
            (width, width),
            own=w_out,
            parts=[(a, (QKV, QKV + width), r) for a, r in zip((qo_near, qo_far), rels)],
            place=by_rows,
            own_place=own_rows,
        )
        mat_gate_up = Weight(
            (width, 2 * FF),
            own=w_gate_up,
            parts=gate_up_parts,
            place=lambda o, c, x: (o * rows + c * HALF, x * FF),
            own_place=own_rows,
        )
        mat_down = Weight(
            (width, FF),
            own=down_t,
            parts=down_parts,
            place=lambda o, c, x: ((c * 2 + x) * HALF, o * down_rows),
            own_place=lambda o: (0, o * down_rows),
        )
        cut_qkv_out = Pieces(lambda o, c, x, z, p: (o * 4 + c * 2 + x, z), extra=8)
        cut_gate_up = Pieces(lambda o, c, x, z, p: (o * 4 + c * 2 + p, x * 4 + z), parts=2)
        cut_down = Pieces(lambda o, c, x, z, p: (c * 4 + x * 2 + (z >> 1), o * 2 + (z & 1)))
    else:
        gains = (
            lax.all_gather(norm_gains.astype(BF16), "shard", axis=1, tiled=True).astype(F32),
        )
        mat_qkv, mat_out, mat_gate_up, mat_down = [
            lax.all_gather(m.astype(BF16), "shard", axis=0, tiled=True)
            for m in (w_qkv, w_out, w_gate_up, w_down)
        ]
        mat_qkv, mat_out, mat_gate_up, mat_down = [
            Weight(m.shape, whole=m) for m in (mat_qkv, mat_out, mat_gate_up, mat_down.T)
        ]
        cut_qkv_out = cut_gate_up = cut_down = None

    qkv, attended, *tables, gains = attention_forward(idx, x_t, segments, frequency, gains, mat_qkv)
    middle, normed_low, ab, hidden, *grad_down = feed_forward(
        idx, x_t, attended, gains, y_t, mat_out, mat_gate_up, cut_down
    )
    gated, output, *grad_gate_up = feed_back(
        idx, ab, normed_low, hidden, middle, y_t, mat_down, cut_gate_up
    )
    token_grad, *grad_qkv_out = attention_back(
        idx,
        x_t,
        y_t,
        middle,
        gated,
        qkv,
        attended,
        tables,
        gains,
        [mat_gate_up, mat_out, mat_qkv],
        cut_qkv_out,
    )
    if fast:

        def put_down(full, z, piece):
            full[(z >> 1) * CUT_ROWS : ((z >> 1) + 1) * CUT_ROWS, pl.ds((z & 1) * 384, 384)] = piece

        def put_upper(full, z, piece):
            full[:CUT_ROWS, pl.ds(z * 384, 384)] = piece

        def put_lower(full, z, piece):
            full[CUT_ROWS:, pl.ds(z * 384, 384)] = piece

        def put_columns(full, z, piece):
            full[:, pl.ds(z * 384, 384)] = piece

        arrived_down = swap(grad_down[0], "dp", 1)
        plane_down = sum_over_plane(grad_down[1][0], arrived_down[0], True)
        arrived_gate_up = swap(grad_gate_up[0], "dp", 1)
        plane_upper = sum_over_plane(grad_gate_up[1][0], arrived_gate_up[0], False)
        plane_lower = sum_over_plane(grad_gate_up[1][1], arrived_gate_up[1], True)
        summed = sum_over_line(jnp.stack([plane_down, plane_upper, plane_lower]))
        arrived_qkv_out = swap(grad_qkv_out[0], "dp", 1)
        plane_qkv_out = sum_over_plane(grad_qkv_out[1][0], arrived_qkv_out[0], False)
        summed_qkv_out = sum_over_line(plane_qkv_out[None])
        by_row = lambda t: ((t % 2) * 2 + t // 2, 0)
        one_down, two_down, next_down = update_state(
            summed,
            (0,),
            [((HALF, down_rows), by_row)],
            (put_down,),
            [down_t, first_down_t, second_down_t],
            (HALF, down_rows),
            "update_down",
        )
        one_gate_up, two_gate_up, next_gate_up = update_state(
            summed,
            (1, 2),
            [((HALF, FF), lambda t: (t % 2, t // 2))],
            (put_upper, put_lower),
            [w_gate_up, first_gate_up, second_gate_up],
            (HALF, FF),
            "update_gate_up",
        )
        updated = update_state(
            summed_qkv_out,
            (0,),
            [((CUT_ROWS, QKV), by_row), ((CUT_ROWS, width), by_row)],
            (put_columns,),
            [w_qkv, w_out, first_qkv, first_out, second_qkv, second_out],
            (CUT_ROWS + 8, QKV + width),
            "update_qkv_out",
            (norm_gains, first_gains, second_gains),
        )
        one_qkv, one_out, two_qkv, two_out, next_qkv, next_out = updated[:6]
        one_gains, two_gains, next_gains = updated[6:]
    else:
        sums = lax.psum((*grad_qkv_out, grad_gate_up[0], grad_down[0].T), ("dp", "shard"))
        grad_qkv_out, grad_gains, grad_gate_up, grad_down = sums

        def own(grad, axis=0):
            size = grad.shape[axis] // groups
            return lax.dynamic_slice_in_dim(grad, owner * size, size, axis)

        one_qkv, two_qkv, next_qkv = adamw(
            w_qkv, first_qkv, second_qkv, own(grad_qkv_out[:, :QKV]), RATE_MATRIX, DECAY_MATRIX
        )
        one_out, two_out, next_out = adamw(
            w_out, first_out, second_out, own(grad_qkv_out[:, QKV:]), RATE_MATRIX, DECAY_MATRIX
        )
        one_gate_up, two_gate_up, next_gate_up = adamw(
            w_gate_up, first_gate_up, second_gate_up, own(grad_gate_up), RATE_MATRIX, DECAY_MATRIX
        )
        one_down, two_down, next_down = [
            a.T
            for a in adamw(
                w_down, first_down, second_down, own(grad_down), RATE_MATRIX, DECAY_MATRIX
            )
        ]
        one_gains, two_gains, next_gains = adamw(
            norm_gains, first_gains, second_gains, own(grad_gains, 1), RATE_GAIN, 0.0
        )
    one_down, two_down, next_down = one_down.T, two_down.T, next_down.T
    return (
        output.T[None],
        token_grad.T[None],
        one_qkv,
        one_out,
        one_gate_up,
        one_down,
        one_gains,
        two_qkv,
        two_out,
        two_gate_up,
        two_down,
        two_gains,
        next_qkv,
        next_out,
        next_gate_up,
        next_down,
        next_gains,
    )


def solution(mesh):
    return jax.shard_map(
        per_device,
        mesh=mesh,
        in_specs=(
            P(("dp", "shard"), None, None),
            P(("dp", "shard"), None),
            P(("dp", "shard"), None, None),
            P("shard", None),
            P("shard", None),
            P("shard", None),
            P("shard", None),
            P(None, "shard"),
            P("shard", None),
            P("shard", None),
            P("shard", None),
            P("shard", None),
            P(None, "shard"),
            P("shard", None),
            P("shard", None),
            P("shard", None),
            P("shard", None),
            P(None, "shard"),
        ),
        out_specs=(
            P(("dp", "shard"), None, None),
            P(("dp", "shard"), None, None),
            P("shard", None),
            P("shard", None),
            P("shard", None),
            P("shard", None),
            P(None, "shard"),
            P("shard", None),
            P("shard", None),
            P("shard", None),
            P("shard", None),
            P(None, "shard"),
            P("shard", None),
            P("shard", None),
            P("shard", None),
            P("shard", None),
            P(None, "shard"),
        ),
        check_vma=False,
    )
```

time: 264 us -> 226 us (0.86)
  starting transfers between devices: 57.9 us -> 27.9 us
  waiting for transfers between devices: 68.7 us -> 98.1 us
  local copies, waits for them, and re-layouts: 27 us -> 2.76 us
  blocking collectives: 38.8 us -> 22.8 us
  between operations: 1.04 us -> 14.3 us
  other arithmetic: 13.1 us -> 4.17 us
    psum x1 -> x0, blocking collectives: 38.8 us -> none  [per_device(): lax.psum(jnp.concatenate([grad_gain_one, grad_gain_two], axis=0), ('dp',...]
    ppermute x49 -> x25, starting transfers between devices: 57.9 us -> 27.9 us  [swap(): return lax.ppermute(values, axis, [(i, i ^ mask) for i in range(size)])]
    ppermute x49 -> x25, waiting for transfers between devices: 68.7 us -> 98.1 us  [swap(): return lax.ppermute(values, axis, [(i, i ^ mask) for i in range(size)])]
    all_gather x0 -> x1, blocking collectives: none -> 22.8 us  [sum_over_line(): return lax.all_gather(piece.astype(BF16), 'dp', axis=0)]
    unnamed x50 -> x24, local copies, waits for them, and re-layouts: 22.4 us -> 2.35 us
    convert_element_type x10 -> x2, other arithmetic: 4.69 us -> 0.73 us  [sum_over_line(): return lax.all_gather(piece.astype(BF16), 'dp', axis=0)]
    convert_element_type x6, local copies, waits for them, and re-layouts: 3.66 us -> 0.19 us  [the longest x2 0.1 us: sum_over_plane(): total = total[0] + swap(total[1].astype(BF16), 'shard', 1).astype(F32)]
    pallas_call x5 -> x4, Pallas kernels: 31.9 us -> 29.4 us  [call(): pl.pallas_call(kernel, out_shape=tuple(outs), in_specs=[pl.BlockSpec(memo...]
  transfers between devices with their start and end apart: 49 -> 26, of which waited for: 17 -> 18; matrix products, arithmetic and copies ran while one was open for 14% -> 1% of each run, Pallas kernels for 15% -> 16%
where the time goes in v2:
time: 226 us; the launch traced here: 225 us
  waiting for transfers between devices  98.1 us (43%)
  Pallas kernels  55 us (24%)
  starting transfers between devices  27.9 us (12%)
  blocking collectives  22.8 us (10%)
  between operations  14.3 us (6%)
  other arithmetic  4.17 us (2%)
  local copies, waits for them, and re-layouts  2.76 us (1%)
    ppermute x25, waiting for transfers between devices, swap(): return lax.ppermute(values, axis, [(i, i ^ mask) for i in range(size)])  98.1 us
    pallas_call x4, Pallas kernels, call(): pl.pallas_call(kernel, out_shape=tuple(outs), in_specs=[pl.BlockSpec(memo...  29.4 us
    ppermute x25, starting transfers between devices, swap(): return lax.ppermute(values, axis, [(i, i ^ mask) for i in range(size)])  27.9 us
    all_gather x1, blocking collectives, sum_over_line(): return lax.all_gather(piece.astype(BF16), 'dp', axis=0)  22.8 us
    pallas_call x3, Pallas kernels, update_state(): pl.pallas_call(kernel, grid=(4,), in_specs=part_specs + state_specs + gai...  22.2 us
  transfers between devices with their start and end apart: 26, of which 18 were waited for; matrix products, arithmetic and copies ran while one was open for 1% of the time, Pallas kernels for 16%

profile of v2, /device:TPU:0, one launch (start us, length us, event | category | flops | bytes accessed | tf_op | source)
XLA Modules:
  0.0 225.1 jit_solution(9333346952996977480)
XLA Ops:
  7.2 0.7 pad_add_fusion.idx_ref.refs_0_
  7.9 3.3 %pack_weights.1 = (bf16[160,1536]{1,0:T(8,128)(2,1)}, bf16[144,1536]{1,0:T(8,128)(2,1)}, bf16[144,768]{1,0:T(8,128)(2,1)}) custom-call(s32[4]{0:T(128)} %pad_add_fusion.idx_ref.refs_0_, f32[288,960]{1,0:T(8,128)} %refs_1_.1, f32[288,576]{1,0:T(8,128)} %refs_2_.4, f32[288,3072]{1,0:T(8,128)} %refs_2_.5, f32[576,768]{1,0:T(8,128)} %bitcast.85, f32[2,288]{1,0:T(2,128)} %refs_7_.1), custom_call_target="tpu_custom_call" | custom-call | tf_op jit(solution)/shard_map/pack_weights/pallas_call | solution.py:212
  11.2 3.0 %collective-permute-start.2 = (bf16[144,1536]{1,0:T(8,128)(2,1)}, bf16[144,1536]{1,0:T(8,128)(2,1)S(1)}, u32[]{:S(2)}, u32[]{:S(2)}) collective-permute-start(bf16[144,1536]{1,0:T(8,128)(2,1)} %get-tuple-element.57), channel_id=1, source_target_pairs={{0,1},{1,0},{2,3},{3,2},{4,5},{5,4},{6,7},{7,6},{8,9},{9,8},{10,11... | collective-permute-start | bytes 1327112 | tf_op jit(solution)/shard_map/ppermute | solution.py:529
  14.2 11.2 %collective-permute-done.2.refs_9_.refs_12_ = bf16[144,1536]{1,0:T(8,128)(2,1)S(1)} collective-permute-done((bf16[144,1536]{1,0:T(8,128)(2,1)}, bf16[144,1536]{1,0:T(8,128)(2,1)S(1)}, u32[]{:S(2)}, u32[]{:S(2)}) %collective-permute-start.2) | collective-permute-done | bytes 442400 | tf_op jit(solution)/shard_map/ppermute | solution.py:529
  25.4 2.0 collective-permute-start.3
  27.5 7.7 %collective-permute-done.refs_5_.refs_7_.refs_6_.refs_17_.refs_20_ = bf16[160,1536]{1,0:T(8,128)(2,1)S(1)} collective-permute-done((bf16[160,1536]{1,0:T(8,128)(2,1)}, bf16[160,1536]{1,0:T(8,128)(2,1)S(1)}, u32[]{:S(2)}, u32[]{:S(2)}) %collective-permute-start) | collective-permute-done | bytes 491552 | tf_op jit(solution)/shard_map/ppermute | solution.py:529
  35.1 0.5 collective-permute-start.4
  35.9 1.5 collective-permute-start.6
  37.5 6.5 %collective-permute-done.6.refs_7_ = bf16[144,768]{1,0:T(8,128)(2,1)S(1)} collective-permute-done((bf16[144,768]{1,0:T(8,128)(2,1)}, bf16[144,768]{1,0:T(8,128)(2,1)S(1)}, u32[]{:S(2)}, u32[]{:S(2)}) %collective-permute-start.6) | collective-permute-done | bytes 221216 | tf_op jit(solution)/shard_map/ppermute | solution.py:529
  44.0 1.4 collective-permute-start.7
  45.4 0.8 copy-done.1
  46.2 4.3 %attention.1 = (bf16[128,960]{1,0:T(8,128)(2,1)}, bf16[128,576]{1,0:T(8,128)(2,1)}, f32[128,128]{1,0:T(8,128)}, f32[128,128]{1,0:T(8,128)}, f32[128,128]{1,0:T(8,128)}, /*index=5*/f32[2,576]{1,0:T(2,128)}) custom-call(s32[4]{0:T(128)} %pad_add_fusion.idx_ref.refs_0_, bf16[576,128]{1,0:T(8,128)(2,1)} %bitcast.91, s32[1,128]{1,0:T(1,128)} %refs_2_.3, ...), custom_call_target="tpu_custom_call" | custom-call | flops 141557760 | bytes 3325696 | tf_op jit(solution)/shard_map/attention/pallas_call | solution.py:132
  50.5 0.7 copy-done.5
  51.4 6.7 %feed_forward.1 = (f32[128,576]{1,0:T(8,128)}, bf16[128,576]{1,0:T(8,128)(2,1)}, f32[128,3072]{1,0:T(8,128)}, bf16[128,1536]{1,0:T(8,128)(2,1)}, bf16[1,2,8,72,3...) custom-call(s32[4]{0:T(128)} %pad_add_fusion.idx_ref.refs_0_, bf16[576,128]{1,0:T(8,128)(2,1)} %bitcast.92, ...), custom_call_target="tpu_custom_call" | custom-call | flops 766771200 | bytes 11579904 | tf_op jit(solution)/shard_map/feed_forward/pallas_call | solution.py:132
  58.7 1.9 collective-permute-done.8.refs_9_
  60.6 0.6 collective-permute-done.9.refs_10_
  61.3 0.6 copy-done.11
  61.9 6.8 %feed_back.1 = (bf16[128,3072]{1,0:T(8,128)(2,1)}, bf16[576,128]{1,0:T(8,128)(2,1)}, bf16[2,2,8,72,384]{4,3,2,1,0:T(8,128)(2,1)}, bf16[2,2,8,72,384]{4,3,2,1,0:T(8,128)(2,1)}) custom-call(s32[4]{0:T(128)} %pad_add_fusion.idx_ref.refs_0_, f32[128,3072]{1,0:T(8,128)} %get-tuple-element.58.refs_1_, bf16[128,576]{1,0:T(8,128)(2,1)} %get-tuple-element.59.refs_2_, ...), custom_call_target="tpu_custom_call" | custom-call | flops 914227200 | bytes 9682944 | tf_op jit(solution)/shard_map/feed_back/pallas_call | solution.py:132
  69.1 1.6 collective-permute-start.16
  70.7 10.9 %collective-permute-done.16 = bf16[8,72,384]{2,1,0:T(8,128)(2,1)S(1)} collective-permute-done((bf16[8,72,384]{2,1,0:T(8,128)(2,1)S(1)}, bf16[8,72,384]{2,1,0:T(8,128)(2,1)S(1)}, u32[]{:S(2)}, u32[]{:S(2)}) %collective-permute-start.16) | collective-permute-done | bytes 442400 | tf_op jit(solution)/shard_map/ppermute | solution.py:529
  81.8 0.7 collective-permute-start.17
  82.9 1.5 collective-permute-start.19
  84.4 5.9 %collective-permute-done.17 = bf16[4,72,384]{2,1,0:T(8,128)(2,1)S(1)} collective-permute-done((bf16[4,72,384]{2,1,0:T(8,128)(2,1)S(1)}, bf16[4,72,384]{2,1,0:T(8,128)(2,1)S(1)}, u32[]{:S(2)}, u32[]{:S(2)}) %collective-permute-start.17) | collective-permute-done | bytes 221216 | tf_op jit(solution)/shard_map/ppermute | solution.py:529
  90.3 1.6 collective-permute-start.21
  91.9 6.3 %collective-permute-done.19 = bf16[2,4,72,384]{3,2,1,0:T(8,128)(2,1)S(1)} collective-permute-done((bf16[2,4,72,384]{3,2,1,0:T(8,128)(2,1)S(1)}, bf16[2,4,72,384]{3,2,1,0:T(8,128)(2,1)S(1)}, u32[]{:S(2)}, u32[]{:S(2)}) %collective-permute-start.19) | collective-permute-done | bytes 442400 | tf_op jit(solution)/shard_map/ppermute | solution.py:529
  98.4 1.6 collective-permute-start.20
  100.1 0.6 collective-permute-start.22
  100.7 3.7 %collective-permute-done.20 = bf16[4,72,384]{2,1,0:T(8,128)(2,1)S(1)} collective-permute-done((bf16[4,72,384]{2,1,0:T(8,128)(2,1)S(1)}, bf16[4,72,384]{2,1,0:T(8,128)(2,1)S(1)}, u32[]{:S(2)}, u32[]{:S(2)}) %collective-permute-start.20) | collective-permute-done | bytes 221216 | tf_op jit(solution)/shard_map/ppermute | solution.py:529
  104.4 1.7 collective-permute-done.22
  106.3 1.7 collective-permute-start.23
  107.9 5.6 %collective-permute-done.23 = bf16[3,2,72,384]{3,2,1,0:T(8,128)(2,1)S(1)} collective-permute-done((bf16[3,2,72,384]{3,2,1,0:T(8,128)(2,1)S(1)}, bf16[3,2,72,384]{3,2,1,0:T(8,128)(2,1)S(1)}, u32[]{:S(2)}, u32[]{:S(2)}) %collective-permute-start.23) | collective-permute-done | bytes 331808 | tf_op jit(solution)/shard_map/ppermute | solution.py:529
  113.7 3.4 %collective-permute-start.24 = (bf16[3,72,384]{2,1,0:T(8,128)(2,1)S(1)}, bf16[3,72,384]{2,1,0:T(8,128)(2,1)S(1)}, u32[]{:S(2)}, u32[]{:S(2)}) collective-permute-start(bf16[3,72,384]{2,1,0:T(8,128)(2,1)S(1)} %fusion.14), channel_id=1, source_target_pairs={{0,16},{2,18},{4,20},{6,22},{8,24},{10,26},{12,28},{14,30},{16,0},... | collective-permute-start | bytes 497672 | tf_op jit(solution)/shard_map/ppermute | solution.py:529
  117.0 5.1 %collective-permute-done.24 = bf16[3,72,384]{2,1,0:T(8,128)(2,1)S(1)} collective-permute-done((bf16[3,72,384]{2,1,0:T(8,128)(2,1)S(1)}, bf16[3,72,384]{2,1,0:T(8,128)(2,1)S(1)}, u32[]{:S(2)}, u32[]{:S(2)}) %collective-permute-start.24) | collective-permute-done | bytes 165920 | tf_op jit(solution)/shard_map/ppermute | solution.py:529
  122.1 0.7 fusion.11
  122.9 11.6 %attention_back.1 = (bf16[576,128]{1,0:T(8,128)(2,1)}, bf16[1,2,8,80,384]{4,3,2,1,0:T(8,128)(2,1)}, bf16[1,2,8,80,384]{4,3,2,1,0:T(8,128)(2,1)}) custom-call(s32[4]{0:T(128)} %pad_add_fusion.idx_ref.refs_0_, bf16[576,128]{1,0:T(8,128)(2,1)} %bitcast.93, bf16[576,128]{1,0:T(8,128)(2,1)} %bitcast.96, f32[128,576]{1,0:T(8,128)} %get-tuple-element.61.refs_4_.refs_3_, ...), custom_call_target="tpu_custom_call" | custom-call | flops 1179648000 | bytes 13128192 | tf_op jit(solution)/shard_map/attention_back/pallas_call | solution.py:132
  134.5 2.8 %collective-permute-done.10 = bf16[1,2,8,80,384]{4,3,2,1,0:T(8,128)(2,1)S(1)} collective-permute-done((bf16[1,2,8,80,384]{4,3,2,1,0:T(8,128)(2,1)}, bf16[1,2,8,80,384]{4,3,2,1,0:T(8,128)(2,1)S(1)}, u32[]{:S(2)}, u32[]{:S(2)}) %collective-permute-start.10) | collective-permute-done | bytes 983072 | tf_op jit(solution)/shard_map/ppermute | solution.py:529
  137.3 1.4 add_bitcast_fusion
  138.8 0.6 collective-permute-start.11
  139.4 14.9 %collective-permute-done.11 = bf16[2,4,80,384]{3,2,1,0:T(8,128)(2,1)S(1)} collective-permute-done((bf16[2,4,80,384]{3,2,1,0:T(8,128)(2,1)S(1)}, bf16[2,4,80,384]{3,2,1,0:T(8,128)(2,1)S(1)}, u32[]{:S(2)}, u32[]{:S(2)}) %collective-permute-start.11) | collective-permute-done | bytes 491552 | tf_op jit(solution)/shard_map/ppermute | solution.py:529
  154.4 3.1 %collective-permute-start.12 = (bf16[4,80,384]{2,1,0:T(8,128)(2,1)S(1)}, bf16[4,80,384]{2,1,0:T(8,128)(2,1)S(1)}, u32[]{:S(2)}, u32[]{:S(2)}) collective-permute-start(bf16[4,80,384]{2,1,0:T(8,128)(2,1)S(1)} %fusion.12), channel_id=1, source_target_pairs={{0,1},{1,0},{2,3},{3,2},{4,5},{5,4},{6,7},{7,6},{8,9},{9,8},{10,11... | collective-permute-start | bytes 737288 | tf_op jit(solution)/shard_map/ppermute | solution.py:529
  157.5 4.2 %collective-permute-done.12 = bf16[4,80,384]{2,1,0:T(8,128)(2,1)S(1)} collective-permute-done((bf16[4,80,384]{2,1,0:T(8,128)(2,1)S(1)}, bf16[4,80,384]{2,1,0:T(8,128)(2,1)S(1)}, u32[]{:S(2)}, u32[]{:S(2)}) %collective-permute-start.12) | collective-permute-done | bytes 245792 | tf_op jit(solution)/shard_map/ppermute | solution.py:529
  161.8 5.5 %collective-permute-done.13 = bf16[1,2,80,384]{3,2,1,0:T(8,128)(2,1)S(1)} collective-permute-done((bf16[1,2,80,384]{3,2,1,0:T(8,128)(2,1)S(1)}, bf16[1,2,80,384]{3,2,1,0:T(8,128)(2,1)S(1)}, u32[]{:S(2)}, u32[]{:S(2)}) %collective-permute-start.13) | collective-permute-done | bytes 122912 | tf_op jit(solution)/shard_map/ppermute | solution.py:529
  167.3 2.4 %collective-permute-start.14 = (bf16[1,80,384]{2,1,0:T(8,128)(2,1)S(1)}, bf16[1,80,384]{2,1,0:T(8,128)(2,1)S(1)}, u32[]{:S(2)}, u32[]{:S(2)}) collective-permute-start(bf16[1,80,384]{2,1,0:T(8,128)(2,1)S(1)} %fusion.17), channel_id=1, source_target_pairs={{0,16},{2,18},{4,20},{6,22},{8,24},{10,26},{12,28},{14,30},{16,0},... | collective-permute-start | bytes 184328 | tf_op jit(solution)/shard_map/ppermute | solution.py:529
  169.8 3.4 %collective-permute-done.14 = bf16[1,80,384]{2,1,0:T(8,128)(2,1)S(1)} collective-permute-done((bf16[1,80,384]{2,1,0:T(8,128)(2,1)S(1)}, bf16[1,80,384]{2,1,0:T(8,128)(2,1)S(1)}, u32[]{:S(2)}, u32[]{:S(2)}) %collective-permute-start.14) | collective-permute-done | bytes 61472 | tf_op jit(solution)/shard_map/ppermute | solution.py:529
  173.2 22.8 %all-gather = bf16[16,80,384]{2,1,0:T(8,128)(2,1)} all-gather(bf16[1,80,384]{2,1,0:T(8,128)(2,1)S(1)} %fusion.16), channel_id=2, replica_groups=mesh['dp'=16,'shard'=2] {'dp'}, dimensions={0}, use_global_device_ids=true | all-gather | bytes 1044480 | tf_op jit(solution)/shard_map/all_gather | solution.py:544
  196.0 6.9 %update_qkv_out.1 = (f32[288,960]{1,0:T(8,128)}, f32[288,576]{1,0:T(8,128)}, f32[288,960]{1,0:T(8,128)}, f32[288,576]{1,0:T(8,128)}, f32[288,960]{1,0:T(8,128)},...) custom-call(bf16[4,4,1,80,384]{4,3,2,1,0:T(8,128)(2,1)} %bitcast.88, ...), custom_call_target="tpu_custom_call" | custom-call | bytes 10616832 | tf_op jit(solution)/shard_map/update_qkv_out/pallas_call | solution.py:514
  202.9 9.2 %update_gate_up.1 = (f32[288,3072]{1,0:T(8,128)}, f32[288,3072]{1,0:T(8,128)}, f32[288,3072]{1,0:T(8,128)}) custom-call(bf16[4,4,3,72,384]{4,3,2,1,0:T(8,128)(2,1)} %bitcast.82, bf16[4,4,3,72,384]{4,3,2,1,0:T(8,128)(2,1)} %bitcast.83, f32[288,3072]{1,0:T(8,128)} %refs_2_.5, f32[288,3072]{1,0:T(8,128)} %refs_3_.4, f32[288,3072]{1,0:T(8,128)} %refs_4_.5), custom_call_target="tpu_custom_call" | custom-call | bytes 21233664 | tf_op jit(solution)/shard_map/update_gate_up/pallas_call | solution.py:514
  212.1 6.1 %update_down.1 = (f32[576,768]{1,0:T(8,128)}, f32[576,768]{1,0:T(8,128)}, f32[576,768]{1,0:T(8,128)}) custom-call(bf16[4,4,3,72,384]{4,3,2,1,0:T(8,128)(2,1)} %bitcast.84, f32[576,768]{1,0:T(8,128)} %bitcast.87, f32[576,768]{1,0:T(8,128)} %bitcast.89, f32[576,768]{1,0:T(8,128)} %bitcast.90), custom_call_target="tpu_custom_call" | custom-call | bytes 10616832 | tf_op jit(solution)/shard_map/update_down/pallas_call | solution.py:514
  (67 shorter events, 3.4 us)
Async XLA Ops:
  7.2 195.7 %all-gather.4.cloned.1.call-start = ((), (), s32[]{:S(2)}) async-start(), calls=%async_computation | async-start | bytes 2820096 | tf_op jit(solution)/shard_map/all_gather | solution.py:544
  11.2 14.2 %collective-permute-start.2 = (bf16[144,1536]{1,0:T(8,128)(2,1)}, bf16[144,1536]{1,0:T(8,128)(2,1)S(1)}, u32[]{:S(2)}, u32[]{:S(2)}) collective-permute-start(bf16[144,1536]{1,0:T(8,128)(2,1)} %get-tuple-element.57), channel_id=1, source_target_pairs={{0,1},{1,0},{2,3},{3,2},{4,5},{5,4},{6,7},{7,6},{8,9},{9,8},{10,11... | collective-permute-start | bytes 1327112 | tf_op jit(solution)/shard_map/ppermute | solution.py:529
  14.2 20.9 %collective-permute-start = (bf16[160,1536]{1,0:T(8,128)(2,1)}, bf16[160,1536]{1,0:T(8,128)(2,1)S(1)}, u32[]{:S(2)}, u32[]{:S(2)}) collective-permute-start(bf16[160,1536]{1,0:T(8,128)(2,1)} %get-tuple-element.54), channel_id=1, source_target_pairs={{0,1},{1,0},{2,3},{3,2},{4,5},{5,4},{6,7},{7,6},{8,9},{9,8},{10,11... | collective-permute-start | bytes 1474568 | tf_op jit(solution)/shard_map/ppermute | solution.py:529
  25.4 25.1 %copy-start.3 = (bf16[144,1536]{1,0:T(8,128)(2,1)}, bf16[144,1536]{1,0:T(8,128)(2,1)S(1)}, u32[]{:S(2)}) copy-start(bf16[144,1536]{1,0:T(8,128)(2,1)S(1)} %collective-permute-done.2.refs_9_.refs_12_) | copy-start | bytes 1327108
  25.4 10.5 %collective-permute-start.3 = (bf16[144,1536]{1,0:T(8,128)(2,1)S(1)}, bf16[144,1536]{1,0:T(8,128)(2,1)S(1)}, u32[]{:S(2)}, u32[]{:S(2)}) collective-permute-start(bf16[144,1536]{1,0:T(8,128)(2,1)S(1)} %collective-permute-done.2.refs_9_.refs_12_), channel_id=1, source_target_pairs={{0,4},{2,6},{4,0},{6,2},{8,12},{10,14},{12,8},{14,10},{16,20},{18,... | collective-permute-start | bytes 1327112 | tf_op jit(solution)/shard_map/ppermute | solution.py:529
  35.1 10.3 %copy-start = (bf16[160,1536]{1,0:T(8,128)(2,1)}, bf16[160,1536]{1,0:T(8,128)(2,1)S(1)}, u32[]{:S(2)}) copy-start(bf16[160,1536]{1,0:T(8,128)(2,1)S(1)} %collective-permute-done.refs_5_.refs_7_.refs_6_.refs_17_.refs_20_) | copy-start | bytes 1474564
  35.1 10.3 %collective-permute-start.1 = (bf16[160,1536]{1,0:T(8,128)(2,1)S(1)}, bf16[160,1536]{1,0:T(8,128)(2,1)S(1)}, u32[]{:S(2)}, u32[]{:S(2)}) collective-permute-start(bf16[160,1536]{1,0:T(8,128)(2,1)S(1)} %collective-permute-done.refs_5_.refs_7_.refs_6_.refs_17_.refs_20_), channel_id=1, source_target_pairs={{0,2},{2,0},{4,6},{6,4},{8,10},{10,8},{12,14},{14,12},{16,18},{18,... | collective-permute-start | bytes 1474568 | tf_op jit(solution)/shard_map/ppermute | solution.py:529
  35.1 15.4 %collective-permute-start.4 = (bf16[144,1536]{1,0:T(8,128)(2,1)S(1)}, bf16[144,1536]{1,0:T(8,128)(2,1)S(1)}, u32[]{:S(2)}, u32[]{:S(2)}) collective-permute-start(bf16[144,1536]{1,0:T(8,128)(2,1)S(1)} %collective-permute-done.2.refs_9_.refs_12_), channel_id=1, source_target_pairs={{0,2},{2,0},{4,6},{6,4},{8,10},{10,8},{12,14},{14,12},{16,18},{18,... | collective-permute-start | bytes 1327112 | tf_op jit(solution)/shard_map/ppermute | solution.py:529
  35.9 14.6 %copy-start.4 = (bf16[144,1536]{1,0:T(8,128)(2,1)}, bf16[144,1536]{1,0:T(8,128)(2,1)S(1)}, u32[]{:S(2)}) copy-start(bf16[144,1536]{1,0:T(8,128)(2,1)S(1)} %collective-permute-done.3.refs_10_.refs_13_) | copy-start | bytes 1327108
  35.9 14.6 %collective-permute-start.5 = (bf16[144,1536]{1,0:T(8,128)(2,1)S(1)}, bf16[144,1536]{1,0:T(8,128)(2,1)S(1)}, u32[]{:S(2)}, u32[]{:S(2)}) collective-permute-start(bf16[144,1536]{1,0:T(8,128)(2,1)S(1)} %collective-permute-done.3.refs_10_.refs_13_), channel_id=1, source_target_pairs={{0,2},{2,0},{4,6},{6,4},{8,10},{10,8},{12,14},{14,12},{16,18},{18,... | collective-permute-start | bytes 1327112 | tf_op jit(solution)/shard_map/ppermute | solution.py:529
  35.9 8.1 %collective-permute-start.6 = (bf16[144,768]{1,0:T(8,128)(2,1)}, bf16[144,768]{1,0:T(8,128)(2,1)S(1)}, u32[]{:S(2)}, u32[]{:S(2)}) collective-permute-start(bf16[144,768]{1,0:T(8,128)(2,1)} %get-tuple-element.62), channel_id=1, source_target_pairs={{0,1},{1,0},{2,3},{3,2},{4,5},{5,4},{6,7},{7,6},{8,9},{9,8},{10,11... | collective-permute-start | bytes 663560 | tf_op jit(solution)/shard_map/ppermute | solution.py:529
  44.0 17.2 %copy-start.8 = (bf16[144,768]{1,0:T(8,128)(2,1)}, bf16[144,768]{1,0:T(8,128)(2,1)S(1)}, u32[]{:S(2)}) copy-start(bf16[144,768]{1,0:T(8,128)(2,1)S(1)} %collective-permute-done.6.refs_7_) | copy-start | bytes 663556
  44.0 14.7 %collective-permute-start.7 = (bf16[144,768]{1,0:T(8,128)(2,1)S(1)}, bf16[144,768]{1,0:T(8,128)(2,1)S(1)}, u32[]{:S(2)}, u32[]{:S(2)}) collective-permute-start(bf16[144,768]{1,0:T(8,128)(2,1)S(1)} %collective-permute-done.6.refs_7_), channel_id=1, source_target_pairs={{0,4},{2,6},{4,0},{6,2},{8,12},{10,14},{12,8},{14,10},{16,20},{18,... | collective-permute-start | bytes 663560 | tf_op jit(solution)/shard_map/ppermute | solution.py:529
  45.4 0.8 copy-start.1
  50.5 0.8 copy-start.5
  50.5 0.9 copy-start.6
  58.1 10.7 %collective-permute-start.15 = (bf16[1,2,8,72,384]{4,3,2,1,0:T(8,128)(2,1)}, bf16[1,2,8,72,384]{4,3,2,1,0:T(8,128)(2,1)S(1)}, u32[]{:S(2)}, u32[]{:S(2)}) collective-permute-start(bf16[1,2,8,72,384]{4,3,2,1,0:T(8,128)(2,1)} %get-tuple-element.75), channel_id=1, source_target_pairs={{0,2},{2,0},{4,6},{6,4},{8,10},{10,8},{12,14},{14,12},{16,18},{18,... | collective-permute-start | bytes 2654216 | tf_op jit(solution)/shard_map/ppermute | solution.py:529
  58.1 2.5 %collective-permute-start.8 = (bf16[144,768]{1,0:T(8,128)(2,1)S(1)}, bf16[144,768]{1,0:T(8,128)(2,1)S(1)}, u32[]{:S(2)}, u32[]{:S(2)}) collective-permute-start(bf16[144,768]{1,0:T(8,128)(2,1)S(1)} %collective-permute-done.6.refs_7_), channel_id=1, source_target_pairs={{0,2},{2,0},{4,6},{6,4},{8,10},{10,8},{12,14},{14,12},{16,18},{18,... | collective-permute-start | bytes 663560 | tf_op jit(solution)/shard_map/ppermute | solution.py:529
  58.7 2.6 %copy-start.9 = (bf16[144,768]{1,0:T(8,128)(2,1)}, bf16[144,768]{1,0:T(8,128)(2,1)S(1)}, u32[]{:S(2)}) copy-start(bf16[144,768]{1,0:T(8,128)(2,1)S(1)} %collective-permute-done.7.refs_8_) | copy-start | bytes 663556
  58.7 2.5 %collective-permute-start.9 = (bf16[144,768]{1,0:T(8,128)(2,1)S(1)}, bf16[144,768]{1,0:T(8,128)(2,1)S(1)}, u32[]{:S(2)}, u32[]{:S(2)}) collective-permute-start(bf16[144,768]{1,0:T(8,128)(2,1)S(1)} %collective-permute-done.7.refs_8_), channel_id=1, source_target_pairs={{0,2},{2,0},{4,6},{6,4},{8,10},{10,8},{12,14},{14,12},{16,18},{18,... | collective-permute-start | bytes 663560 | tf_op jit(solution)/shard_map/ppermute | solution.py:529
  60.6 0.7 copy-start.10
  61.2 0.7 copy-start.11
  61.9 7.0 %copy-start.7 = (bf16[1,2,8,72,384]{4,3,2,1,0:T(8,128)(2,1)S(1)}, bf16[1,2,8,72,384]{4,3,2,1,0:T(8,128)(2,1)}, u32[]{:S(2)}) copy-start(bf16[1,2,8,72,384]{4,3,2,1,0:T(8,128)(2,1)} %get-tuple-element.74) | copy-start | bytes 2654212
  68.7 13.7 %collective-permute-start.18 = (bf16[2,2,8,72,384]{4,3,2,1,0:T(8,128)(2,1)}, bf16[2,2,8,72,384]{4,3,2,1,0:T(8,128)(2,1)S(1)}, u32[]{:S(2)}, u32[]{:S(2)}) collective-permute-start(bf16[2,2,8,72,384]{4,3,2,1,0:T(8,128)(2,1)} %get-tuple-element.77), channel_id=1, source_target_pairs={{0,2},{2,0},{4,6},{6,4},{8,10},{10,8},{12,14},{14,12},{16,18},{18,... | collective-permute-start | bytes 5308424 | tf_op jit(solution)/shard_map/ppermute | solution.py:529
  69.1 13.4 %copy-start.2 = (bf16[2,2,8,72,384]{4,3,2,1,0:T(8,128)(2,1)S(1)}, bf16[2,2,8,72,384]{4,3,2,1,0:T(8,128)(2,1)}, u32[]{:S(2)}) copy-start(bf16[2,2,8,72,384]{4,3,2,1,0:T(8,128)(2,1)} %get-tuple-element.76) | copy-start | bytes 5308420
  69.1 12.5 %collective-permute-start.16 = (bf16[8,72,384]{2,1,0:T(8,128)(2,1)S(1)}, bf16[8,72,384]{2,1,0:T(8,128)(2,1)S(1)}, u32[]{:S(2)}, u32[]{:S(2)}) collective-permute-start(bf16[8,72,384]{2,1,0:T(8,128)(2,1)S(1)} %fusion.4), channel_id=1, source_target_pairs={{0,1},{1,0},{2,3},{3,2},{4,5},{5,4},{6,7},{7,6},{8,9},{9,8},{10,11... | collective-permute-start | bytes 1327112 | tf_op jit(solution)/shard_map/ppermute | solution.py:529
  81.8 8.4 %collective-permute-start.17 = (bf16[4,72,384]{2,1,0:T(8,128)(2,1)S(1)}, bf16[4,72,384]{2,1,0:T(8,128)(2,1)S(1)}, u32[]{:S(2)}, u32[]{:S(2)}) collective-permute-start(bf16[4,72,384]{2,1,0:T(8,128)(2,1)S(1)} %slice.222), channel_id=1, source_target_pairs={{0,4},{2,6},{4,0},{6,2},{8,12},{10,14},{12,8},{14,10},{16,20},{18,... | collective-permute-start | bytes 663560 | tf_op jit(solution)/shard_map/ppermute | solution.py:529
  82.9 15.3 %collective-permute-start.19 = (bf16[2,4,72,384]{3,2,1,0:T(8,128)(2,1)S(1)}, bf16[2,4,72,384]{3,2,1,0:T(8,128)(2,1)S(1)}, u32[]{:S(2)}, u32[]{:S(2)}) collective-permute-start(bf16[2,4,72,384]{3,2,1,0:T(8,128)(2,1)S(1)} %slice.219), channel_id=1, source_target_pairs={{0,4},{2,6},{4,0},{6,2},{8,12},{10,14},{12,8},{14,10},{16,20},{18,... | collective-permute-start | bytes 1327112 | tf_op jit(solution)/shard_map/ppermute | solution.py:529
  90.3 9.6 %collective-permute-start.21 = (bf16[8,72,384]{2,1,0:T(8,128)(2,1)S(1)}, bf16[8,72,384]{2,1,0:T(8,128)(2,1)S(1)}, u32[]{:S(2)}, u32[]{:S(2)}) collective-permute-start(bf16[8,72,384]{2,1,0:T(8,128)(2,1)S(1)} %fusion.5), channel_id=1, source_target_pairs={{0,1},{1,0},{2,3},{3,2},{4,5},{5,4},{6,7},{7,6},{8,9},{9,8},{10,11... | collective-permute-start | bytes 1327112 | tf_op jit(solution)/shard_map/ppermute | solution.py:529
  98.4 6.0 %collective-permute-start.20 = (bf16[4,72,384]{2,1,0:T(8,128)(2,1)S(1)}, bf16[4,72,384]{2,1,0:T(8,128)(2,1)S(1)}, u32[]{:S(2)}, u32[]{:S(2)}) collective-permute-start(bf16[4,72,384]{2,1,0:T(8,128)(2,1)S(1)} %fusion.13), channel_id=1, source_target_pairs={{0,1},{1,0},{2,3},{3,2},{4,5},{5,4},{6,7},{7,6},{8,9},{9,8},{10,11... | collective-permute-start | bytes 663560 | tf_op jit(solution)/shard_map/ppermute | solution.py:529
  100.1 6.0 %collective-permute-start.22 = (bf16[4,72,384]{2,1,0:T(8,128)(2,1)S(1)}, bf16[4,72,384]{2,1,0:T(8,128)(2,1)S(1)}, u32[]{:S(2)}, u32[]{:S(2)}) collective-permute-start(bf16[4,72,384]{2,1,0:T(8,128)(2,1)S(1)} %slice.221), channel_id=1, source_target_pairs={{0,4},{2,6},{4,0},{6,2},{8,12},{10,14},{12,8},{14,10},{16,20},{18,... | collective-permute-start | bytes 663560 | tf_op jit(solution)/shard_map/ppermute | solution.py:529
  106.3 7.3 %collective-permute-start.23 = (bf16[3,2,72,384]{3,2,1,0:T(8,128)(2,1)S(1)}, bf16[3,2,72,384]{3,2,1,0:T(8,128)(2,1)S(1)}, u32[]{:S(2)}, u32[]{:S(2)}) collective-permute-start(bf16[3,2,72,384]{3,2,1,0:T(8,128)(2,1)S(1)} %slice.220), channel_id=1, source_target_pairs={{0,8},{2,10},{4,12},{6,14},{8,0},{10,2},{12,4},{14,6},{16,24},{18,... | collective-permute-start | bytes 995336 | tf_op jit(solution)/shard_map/ppermute | solution.py:529
  113.7 8.5 %collective-permute-start.24 = (bf16[3,72,384]{2,1,0:T(8,128)(2,1)S(1)}, bf16[3,72,384]{2,1,0:T(8,128)(2,1)S(1)}, u32[]{:S(2)}, u32[]{:S(2)}) collective-permute-start(bf16[3,72,384]{2,1,0:T(8,128)(2,1)S(1)} %fusion.14), channel_id=1, source_target_pairs={{0,16},{2,18},{4,20},{6,22},{8,24},{10,26},{12,28},{14,30},{16,0},... | collective-permute-start | bytes 497672 | tf_op jit(solution)/shard_map/ppermute | solution.py:529
  134.4 2.8 %collective-permute-start.10 = (bf16[1,2,8,80,384]{4,3,2,1,0:T(8,128)(2,1)}, bf16[1,2,8,80,384]{4,3,2,1,0:T(8,128)(2,1)S(1)}, u32[]{:S(2)}, u32[]{:S(2)}) collective-permute-start(bf16[1,2,8,80,384]{4,3,2,1,0:T(8,128)(2,1)} %get-tuple-element.71), channel_id=1, source_target_pairs={{0,2},{2,0},{4,6},{6,4},{8,10},{10,8},{12,14},{14,12},{16,18},{18,... | collective-permute-start | bytes 2949128 | tf_op jit(solution)/shard_map/ppermute | solution.py:529
  138.8 15.5 %collective-permute-start.11 = (bf16[2,4,80,384]{3,2,1,0:T(8,128)(2,1)S(1)}, bf16[2,4,80,384]{3,2,1,0:T(8,128)(2,1)S(1)}, u32[]{:S(2)}, u32[]{:S(2)}) collective-permute-start(bf16[2,4,80,384]{3,2,1,0:T(8,128)(2,1)S(1)} %slice.218), channel_id=1, source_target_pairs={{0,4},{2,6},{4,0},{6,2},{8,12},{10,14},{12,8},{14,10},{16,20},{18,... | collective-permute-start | bytes 1474568 | tf_op jit(solution)/shard_map/ppermute | solution.py:529
  154.4 7.2 %collective-permute-start.12 = (bf16[4,80,384]{2,1,0:T(8,128)(2,1)S(1)}, bf16[4,80,384]{2,1,0:T(8,128)(2,1)S(1)}, u32[]{:S(2)}, u32[]{:S(2)}) collective-permute-start(bf16[4,80,384]{2,1,0:T(8,128)(2,1)S(1)} %fusion.12), channel_id=1, source_target_pairs={{0,1},{1,0},{2,3},{3,2},{4,5},{5,4},{6,7},{7,6},{8,9},{9,8},{10,11... | collective-permute-start | bytes 737288 | tf_op jit(solution)/shard_map/ppermute | solution.py:529
  161.7 5.6 %collective-permute-start.13 = (bf16[1,2,80,384]{3,2,1,0:T(8,128)(2,1)S(1)}, bf16[1,2,80,384]{3,2,1,0:T(8,128)(2,1)S(1)}, u32[]{:S(2)}, u32[]{:S(2)}) collective-permute-start(bf16[1,2,80,384]{3,2,1,0:T(8,128)(2,1)S(1)} %slice.223), channel_id=1, source_target_pairs={{0,8},{2,10},{4,12},{6,14},{8,0},{10,2},{12,4},{14,6},{16,24},{18,... | collective-permute-start | bytes 368648 | tf_op jit(solution)/shard_map/ppermute | solution.py:529
  167.3 5.8 %collective-permute-start.14 = (bf16[1,80,384]{2,1,0:T(8,128)(2,1)S(1)}, bf16[1,80,384]{2,1,0:T(8,128)(2,1)S(1)}, u32[]{:S(2)}, u32[]{:S(2)}) collective-permute-start(bf16[1,80,384]{2,1,0:T(8,128)(2,1)S(1)} %fusion.17), channel_id=1, source_target_pairs={{0,16},{2,18},{4,20},{6,22},{8,24},{10,26},{12,28},{14,30},{16,0},... | collective-permute-start | bytes 184328 | tf_op jit(solution)/shard_map/ppermute | solution.py:529
Sparse Core Ops, SparseCore 0:
  123.0 44.8 all-gather.3

commit v3 on v2

--- a/solution.py
+++ b/solution.py
@@ -29,7 +29,7 @@
 EPS_ADAM = 1e-08
 MASKED = -1e30
 SCALE = float(HEAD) ** (-0.5)
-VMEM_LIMIT = 56 * 1024 * 1024
+VMEM_LIMIT = 32 * 1024 * 1024
 HALF = 144
 CUT_ROWS = 72
 CUT_COLUMNS = 384
@@ -107,7 +107,7 @@
         full[rows, columns] = value
 
 
-def call(body, idx, arrays, weights, outs, scratch, flops, name):
+def call(body, idx, arrays, weights, outs, scratch, flops, name, after=()):
     counts = [len(w.arrays) for w in weights]
     flat = list(arrays) + [a for w in weights for a in w.arrays]
     weight_scratch = [w.scratch() for w in weights]
@@ -118,6 +118,7 @@
         take = lambda n: [refs.pop(0) for _ in range(n)]
         array_refs = take(len(arrays))
         weight_refs = [take(n) for n in counts]
+        take(len(after))
         out_refs = take(len(outs))
         own_scratch = take(len(scratch))
         scratch_refs = [take(len(s)) for s in weight_scratch]
@@ -133,13 +134,14 @@
         kernel,
         out_shape=tuple(outs),
         in_specs=[pl.BlockSpec(memory_space=pltpu.SMEM)]
-        + [pl.BlockSpec(memory_space=pltpu.VMEM)] * len(flat),
+        + [pl.BlockSpec(memory_space=pltpu.VMEM)] * len(flat)
+        + [pl.BlockSpec(memory_space=pl.ANY)] * len(after),
         out_specs=tuple([pl.BlockSpec(memory_space=pltpu.VMEM)] * len(outs)),
         scratch_shapes=list(scratch) + [s for group in weight_scratch for s in group],
         compiler_params=pltpu.CompilerParams(vmem_limit_bytes=VMEM_LIMIT),
         cost_estimate=pl.CostEstimate(flops=flops, bytes_accessed=moved, transcendentals=0),
         name=name,
-    )(idx, *flat)
+    )(idx, *flat, *after)
 
 
 def sds(shape, dtype):
@@ -207,7 +209,7 @@
     outs = (
         sds((HALF + 16, QKV + width), BF16),
         sds((HALF, FF), BF16),
-        sds((HALF, down_t.shape[1]), BF16),
+        sds((2 * HALF, down_t.shape[1]), BF16),
     )
     return pl.pallas_call(
         kernel,
@@ -218,7 +220,7 @@
                 pl.BlockSpec((HALF, QKV), lambda t, i: (i[1], 0)),
                 pl.BlockSpec((HALF, width), lambda t, i: (i[1], 0)),
                 pl.BlockSpec((HALF, FF), lambda t, i: (i[1], i[2])),
-                pl.BlockSpec((HALF, down_t.shape[1]), lambda t, i: (i[1] * 2 + i[2], 0)),
+                pl.BlockSpec((2 * HALF, down_t.shape[1]), lambda t, i: (i[1], 0)),
                 pl.BlockSpec(norm_gains.shape, lambda t, i: (0, 0)),
             ],
             out_specs=tuple(pl.BlockSpec(o.shape, lambda t, i: (0, 0)) for o in outs),
@@ -291,7 +293,7 @@
     )
 
 
-def feed_forward(idx, tokens_t, attended, gains, cotangent_t, w_out, w_gate_up, pieces):
+def feed_forward(idx, tokens_t, attended, gains, cotangent_t, w_out, w_gate_up, pieces, after):
     width, seq_length = tokens_t.shape
 
     def body(idx_ref, arrays, loads, outs, scratch):
@@ -330,6 +332,7 @@
         scratch,
         2 * 128 * 576 * 5200,
         "feed_forward",
+        after,
     )
 
 
@@ -368,26 +371,50 @@
     )
 
 
-def attention_back(
-    idx, tokens_t, cotangent_t, middle, gated, qkv, attended, tables, gains, weights, pieces
-):
-    width, seq_length = tokens_t.shape
+def middle_back(idx, cotangent_t, middle, gated, gains, w_gate_up, w_out, after):
+    width, seq_length = cotangent_t.shape
 
     def body(idx_ref, arrays, loads, outs, scratch):
-        x_ref, y_ref, u_ref, gg_ref, qkv_ref, o_ref = arrays[:6]
-        cos_ref, sin_ref, allowed_ref, gains_ref = arrays[6:]
-        grad_ref = outs[0]
-        grad_proj, gp_ref, gain_rows, *blocks = scratch
+        y_ref, u_ref, gg_ref, gains_ref = arrays
+        gu_ref, go_ref, gain_ref = outs
         u = u_ref[...]
         scale_two = norm_scale(u)
         normed = u * scale_two
         grad_normed = dot_right_t(gg_ref[...], loads[0]()[...])
-        grad_gain_two = jnp.sum(grad_normed * normed, axis=0, keepdims=True)
+        gain_ref[...] = jnp.sum(grad_normed * normed, axis=0, keepdims=True)
         gu = y_ref[...].astype(F32).T + norm_back(
             grad_normed * gains_ref[1:2, :], normed, scale_two
         )
+        gu_ref[...] = gu
+        go_ref[...] = dot_right_t(gu.astype(BF16), loads[1]()[...]).astype(BF16)
+
+    outs = [sds((seq_length, width), F32), sds((seq_length, width), BF16), sds((1, width), F32)]
+    return call(
+        body,
+        idx,
+        [cotangent_t, middle, gated, gains],
+        [w_gate_up, w_out],
+        outs,
+        [],
+        2 * 128 * 576 * 3700,
+        "middle_back",
+        after,
+    )
+
+
+def attention_back(
+    idx, tokens_t, grad_middle, grad_attended, gain_two, qkv, attended, tables, gains, w_qkv, pieces, after
+):
+    width, seq_length = tokens_t.shape
+
+    def body(idx_ref, arrays, loads, outs, scratch):
+        x_ref, gu_ref, go_ref, gain_two_ref, qkv_ref, o_ref = arrays[:6]
+        cos_ref, sin_ref, allowed_ref, gains_ref = arrays[6:]
+        grad_ref = outs[0]
+        grad_proj, gp_ref, gain_rows, *blocks = scratch
+        gu, go = gu_ref[...], go_ref[...]
         gu_low = gu.astype(BF16)
-        go = dot_right_t(gu_low, loads[1]()[...]).astype(BF16)
+        grad_gain_two = gain_two_ref[...]
         allowed = jnp.concatenate([allowed_ref[...]] * GROUP, axis=0) > 0.5
         qkv_values = qkv_ref[...]
         for kv in range(KV_HEADS):
@@ -420,7 +447,7 @@
         h1 = (normed * gains_ref[0:1, :]).astype(BF16)
         grad_qkv = dot_left_t(h1, gp_ref[...])
         grad_out = dot_left_t(o_ref[...], gu_low)
-        grad_normed = dot_right_t(gp_ref[...], loads[2]()[...])
+        grad_normed = dot_right_t(gp_ref[...], loads[0]()[...])
         grad_gain_one = jnp.sum(grad_normed * normed, axis=0, keepdims=True)
         if pieces is None:
             outs[1][:, :QKV] = grad_qkv
@@ -455,29 +482,74 @@
     return call(
         body,
         idx,
-        [tokens_t, cotangent_t, middle, gated, qkv, attended, *tables, gains],
-        weights,
+        [tokens_t, grad_middle, grad_attended, gain_two, qkv, attended, *tables, gains],
+        [w_qkv],
         outs,
         scratch,
-        2 * 128 * 576 * 8000,
+        2 * 128 * 576 * 4300,
         "attention_back",
-    )
-
-
-def update_state(summed, parts, blocks, puts, state, shape, name, gains=()):
+        after,
+    )
+
+
+def step(body, arrays, outs, name, after=()):
+    def kernel(*refs):
+        body(refs[: len(arrays)], refs[len(arrays) + len(after) :])
+
+    return pl.pallas_call(
+        kernel,
+        out_shape=tuple(outs),
+        in_specs=[pl.BlockSpec(memory_space=pltpu.VMEM)] * len(arrays)
+        + [pl.BlockSpec(memory_space=pl.ANY)] * len(after),
+        out_specs=tuple([pl.BlockSpec(memory_space=pltpu.VMEM)] * len(outs)),
+        compiler_params=pltpu.CompilerParams(vmem_limit_bytes=VMEM_LIMIT),
+        name=name,
+    )(*arrays, *after)
+
+
+def add_split(keep, arrived, axis, send_ref, keep_ref):
+    total = keep[...].astype(F32) + arrived[...].astype(F32)
+    low, high = lax.index_in_dim(total, 0, axis, False), lax.index_in_dim(total, 1, axis, False)
+    send_ref[...] = high.astype(BF16)
+    keep_ref[...] = low
+
+
+def add_step(jobs, name, after):
+    arrays, outs = [], []
+    for keep, arrived, axis in jobs:
+        arrays += [keep, arrived]
+        shape = keep.shape[:axis] + keep.shape[axis + 1 :]
+        outs += [sds(shape, BF16), sds(shape, F32)]
+
+    def body(ins, out_refs):
+        for i, (_, _, axis) in enumerate(jobs):
+            add_split(ins[2 * i], ins[2 * i + 1], axis, out_refs[2 * i], out_refs[2 * i + 1])
+
+    flat = step(body, arrays, outs, name, after)
+    return [(flat[2 * i], flat[2 * i + 1]) for i in range(len(jobs))]
+
+
+def update_state(idx, near, far, parts, blocks, puts, state, shape, name, gains=(), after=()):
     count = len(state) // 3
-    height, width = summed.shape[2:]
-    by_z = summed.reshape(4, 4, *summed.shape[1:])
-
-    def kernel(*refs):
-        part_refs, refs = refs[: len(parts)], refs[len(parts) :]
+    height, width = near.shape[3:]
+
+    def kernel(idx_ref, *refs):
+        part_refs, refs = refs[: 2 * len(parts)], refs[2 * len(parts) :]
         state_refs, refs = refs[: 3 * count], refs[3 * count :]
-        gain_refs, refs = refs[: len(gains)], refs[len(gains) :]
+        gain_refs, refs = refs[: len(gains)], refs[len(gains) + len(after) :]
         outs, refs = refs[: 3 * count], refs[3 * count :]
         gain_outs, full = refs[: len(gains)], refs[-1]
-        for ref, put in zip(part_refs, puts):
+        is_near = pl.program_id(0) % 2 == idx_ref[1]
+        for i, put in enumerate(puts):
             for z in range(4):
-                put(full, z, ref[z, 0, 0].astype(F32))
+                rel = z ^ idx_ref[3]
+                slot = (rel & 1) * 2 + (rel >> 1)
+                piece = jnp.where(
+                    is_near,
+                    part_refs[2 * i][0, 0, slot].astype(F32),
+                    part_refs[2 * i + 1][0, 0, slot].astype(F32),
+                )
+                put(full, z, piece)
         start = 0
         for i in range(count):
             columns = state_refs[i].shape[1]
@@ -506,22 +578,30 @@
                 gain_outs[2][...] = new
 
     state_specs = [pl.BlockSpec(*blocks[i]) for i in range(count)] * 3
-    gain_specs = [pl.BlockSpec(g.shape, lambda t: (0, 0)) for g in gains]
+    gain_specs = [pl.BlockSpec(g.shape, lambda t, _: (0, 0)) for g in gains]
     part_specs = [
-        pl.BlockSpec((4, 1, 1, height, width), lambda t, p=p: (0, t, p, 0, 0)) for p in parts
+        pl.BlockSpec((1, 1, 4, height, width), lambda t, i, p=p: (p, (t // 2) ^ i[2], 0, 0, 0))
+        for p in parts
+        for _ in range(2)
     ]
     moved = sum(a.size * 8 for a in state)
     return pl.pallas_call(
         kernel,
-        grid=(4,),
-        in_specs=part_specs + state_specs + gain_specs,
-        out_specs=tuple(state_specs + gain_specs),
-        scratch_shapes=[pltpu.VMEM(shape, F32)],
+        grid_spec=pltpu.PrefetchScalarGridSpec(
+            num_scalar_prefetch=1,
+            grid=(4,),
+            in_specs=part_specs
+            + state_specs
+            + gain_specs
+            + [pl.BlockSpec(memory_space=pl.ANY)] * len(after),
+            out_specs=tuple(state_specs + gain_specs),
+            scratch_shapes=[pltpu.VMEM(shape, F32)],
+        ),
         out_shape=tuple(sds(a.shape, F32) for a in [*state, *gains]),
         compiler_params=pltpu.CompilerParams(vmem_limit_bytes=VMEM_LIMIT),
         cost_estimate=pl.CostEstimate(flops=0, bytes_accessed=moved, transcendentals=0),
         name=name,
-    )(*[by_z] * len(parts), *state, *gains)
+    )(idx, *[near, far] * len(parts), *state, *gains, *after)
 
 
 def swap(values, axis, mask):
@@ -529,30 +609,11 @@
     return lax.ppermute(values, axis, [(i, i ^ mask) for i in range(size)])
 
 
-def sum_over_plane(keep, arrived, across_first):
-    total = keep.astype(F32) + arrived.astype(F32)
-    if across_first:
-        total = total[0] + swap(total[1].astype(BF16), "shard", 1).astype(F32)
-        return total[:4] + swap(total[4:].astype(BF16), "dp", 2).astype(F32)
-    total = total[:, :4] + swap(total[:, 4:].astype(BF16), "dp", 2).astype(F32)
-    return total[0] + swap(total[1].astype(BF16), "shard", 1).astype(F32)
-
-
-def sum_over_line(totals):
-    totals = totals[:, :2] + swap(totals[:, 2:].astype(BF16), "dp", 4).astype(F32)
-    piece = totals[:, 0] + swap(totals[:, 1].astype(BF16), "dp", 8).astype(F32)
-    return lax.all_gather(piece.astype(BF16), "dp", axis=0)
-
-
-def spread(mine):
-    near = swap(mine, "shard", 1)
-    near_x = swap(near, "dp", 2)
-    return [
-        (near, None, (0, 0)),
-        (near_x, None, (0, 1)),
-        (swap(near, "dp", 1), None, (1, 0)),
-        (swap(near_x, "dp", 1), None, (1, 1)),
-    ]
+over_y = functools.partial(swap, axis="shard", mask=1)
+over_core = functools.partial(swap, axis="dp", mask=1)
+over_x = functools.partial(swap, axis="dp", mask=2)
+over_z_low = functools.partial(swap, axis="dp", mask=4)
+over_z_high = functools.partial(swap, axis="dp", mask=8)
 
 
 def per_device(
@@ -590,10 +651,17 @@
     frequency = jnp.asarray(np.tile(frequency, 4)[None], F32)
     if fast:
         qo, gate_up, down = pack_weights(idx, w_qkv, w_out, w_gate_up, down_t, norm_gains)
-        gate_up_parts = spread(gate_up)
-        qo_near = swap(qo, "shard", 1)
-        qo_far = swap(qo_near, "dp", 1)
-        down_parts = spread(down)
+        gate_up_near = over_y(gate_up)
+        qo_near = over_y(qo)
+        down_near = over_y(down)
+        gate_up_near_x = over_x(gate_up_near)
+        gate_up_parts = [
+            (gate_up_near, None, (0, 0)),
+            (gate_up_near_x, None, (0, 1)),
+            (over_core(gate_up_near), None, (1, 0)),
+            (over_core(gate_up_near_x), None, (1, 1)),
+        ]
+        qo_far = over_core(qo_near)
         gains = (norm_gains, qo_near)
         by_rows = lambda o, c, x: (o * rows + c * HALF, 0)
         own_rows = lambda o: (o * rows, 0)
@@ -622,8 +690,8 @@
         mat_down = Weight(
             (width, FF),
             own=down_t,
-            parts=down_parts,
-            place=lambda o, c, x: ((c * 2 + x) * HALF, o * down_rows),
+            parts=(),
+            place=lambda o, c, x: (c * 2 * HALF, o * down_rows),
             own_place=lambda o: (0, o * down_rows),
         )
         cut_qkv_out = Pieces(lambda o, c, x, z, p: (o * 4 + c * 2 + x, z), extra=8)
@@ -643,24 +711,58 @@
         cut_qkv_out = cut_gate_up = cut_down = None
 
     qkv, attended, *tables, gains = attention_forward(idx, x_t, segments, frequency, gains, mat_qkv)
+    after = ()
+    if fast:
+
+        def pass_on(ins, outs):
+            outs[0][...] = ins[0][...]
+
+        (down_near,) = step(pass_on, [down_near], [sds(down_near.shape, BF16)], "pass_on", (attended,))
+        mat_down.parts = [(down_near, None, (0, 0)), (over_core(down_near), None, (1, 0))]
+        mat_down.arrays = [down_t] + [p[0] for p in mat_down.parts]
+        after = (down_near,)
     middle, normed_low, ab, hidden, *grad_down = feed_forward(
-        idx, x_t, attended, gains, y_t, mat_out, mat_gate_up, cut_down
-    )
+        idx, x_t, attended, gains, y_t, mat_out, mat_gate_up, cut_down, after
+    )
+    if fast:
+        arrived_down = over_core(grad_down[0])
     gated, output, *grad_gate_up = feed_back(
         idx, ab, normed_low, hidden, middle, y_t, mat_down, cut_gate_up
     )
+    if fast:
+        cut = lambda a, *lead: a.reshape(*lead, *a.shape[-2:])
+        arrived_gate_up = over_core(grad_gate_up[0])
+        ((send, keep_down),) = add_step(
+            [(grad_down[1][0], arrived_down[0], 0)], "down_core", (gated,)
+        )
+        arrived_down = over_y(send)
+        after = (keep_down,)
+    grad_middle, grad_attended, gain_two = middle_back(
+        idx, y_t, middle, gated, gains, mat_gate_up, mat_out, after
+    )
+    if fast:
+        halves = [
+            [cut(a[p], *lead) for a in (grad_gate_up[1], arrived_gate_up)]
+            for p, lead in ((0, (2, 2, 4)), (1, (4, 2, 2)))
+        ]
+        (send_up, keep_up), (send_low, keep_low) = add_step(
+            [(*halves[0], 1), (*halves[1], 1)], "gate_up_core", (grad_middle,)
+        )
+        arrived_up, arrived_low = over_x(send_up), over_z_low(send_low)
+        after = (keep_up,)
     token_grad, *grad_qkv_out = attention_back(
         idx,
         x_t,
-        y_t,
-        middle,
-        gated,
+        grad_middle,
+        grad_attended,
+        gain_two,
         qkv,
         attended,
         tables,
         gains,
-        [mat_gate_up, mat_out, mat_qkv],
+        mat_qkv,
         cut_qkv_out,
+        after,
     )
     if fast:
 
@@ -676,18 +778,128 @@
         def put_columns(full, z, piece):
             full[:, pl.ds(z * 384, 384)] = piece
 
-        arrived_down = swap(grad_down[0], "dp", 1)
-        plane_down = sum_over_plane(grad_down[1][0], arrived_down[0], True)
-        arrived_gate_up = swap(grad_gate_up[0], "dp", 1)
-        plane_upper = sum_over_plane(grad_gate_up[1][0], arrived_gate_up[0], False)
-        plane_lower = sum_over_plane(grad_gate_up[1][1], arrived_gate_up[1], True)
-        summed = sum_over_line(jnp.stack([plane_down, plane_upper, plane_lower]))
-        arrived_qkv_out = swap(grad_qkv_out[0], "dp", 1)
-        plane_qkv_out = sum_over_plane(grad_qkv_out[1][0], arrived_qkv_out[0], False)
-        summed_qkv_out = sum_over_line(plane_qkv_out[None])
-        by_row = lambda t: ((t % 2) * 2 + t // 2, 0)
+        arrived_qkv_out = over_core(grad_qkv_out[0])
+        ((send, keep_down),) = add_step(
+            [(cut(keep_down, 2, 4), cut(arrived_down, 2, 4), 0)], "down_y", (token_grad,)
+        )
+        arrived_down = over_x(send)
+        ((send, keep_qkv_out),) = add_step(
+            [(grad_qkv_out[1][0], arrived_qkv_out[0], 0)], "qkv_out_core", (keep_down,)
+        )
+        arrived_qkv_out = over_y(send)
+        (send_up, keep_up), (send_low, keep_low) = add_step(
+            [
+                (cut(keep_up, 2, 2, 2), cut(arrived_up, 2, 2, 2), 1),
+                (cut(keep_low, 2, 2, 2), cut(arrived_low, 2, 2, 2), 0),
+            ],
+            "up_x_low_z",
+            (keep_qkv_out,),
+        )
+        arrived_up, arrived_low = over_z_low(send_up), over_y(send_low)
+        (send, keep_down), (send_up, keep_up), (send_low, keep_low) = add_step(
+            [
+                (cut(keep_down, 2, 2), cut(arrived_down, 2, 2), 0),
+                (keep_up, arrived_up, 0),
+                (keep_low, arrived_low, 0),
+            ],
+            "down_x_up_z_low_y",
+            (keep_up,),
+        )
+        arrived_down, arrived_up, arrived_low = over_z_low(send), over_y(send_up), over_x(send_low)
+        ((send, keep_qkv_out),) = add_step(
+            [(cut(keep_qkv_out, 2, 4), cut(arrived_qkv_out, 2, 4), 0)], "qkv_out_y", (keep_down,)
+        )
+        arrived_qkv_out = over_x(send)
+
+        piece = (CUT_ROWS, CUT_COLUMNS)
+        taller = (CUT_ROWS + 8, CUT_COLUMNS)
+
+        def last_sums(ins, outs):
+            for i in range(3):
+                total = ins[2 * i][...] + ins[2 * i + 1][...].astype(F32)
+                outs[0][i] = total[1].astype(BF16)
+                outs[1][i] = total[0]
+
+        send, keep = step(
+            last_sums,
+            [keep_down, arrived_down, keep_up, arrived_up, keep_low, arrived_low],
+            [sds((3, *piece), BF16), sds((3, *piece), F32)],
+            "down_z_up_y_low_x",
+            (keep_qkv_out,),
+        )
+        arrived = over_z_high(send)
+        ((send, keep_qkv_out),) = add_step(
+            [(cut(keep_qkv_out, 2, 2), cut(arrived_qkv_out, 2, 2), 0)], "qkv_out_x", (keep,)
+        )
+        arrived_qkv_out = over_z_low(send)
+
+        def make_pieces(ins, outs):
+            outs[0][...] = (ins[0][...] + ins[1][...].astype(F32)).astype(BF16)
+            total = ins[2][...] + ins[3][...].astype(F32)
+            outs[1][...] = total[1].astype(BF16)
+            outs[2][...] = total[0]
+
+        pieces, send, keep_qkv_out = step(
+            make_pieces,
+            [keep, arrived, keep_qkv_out, arrived_qkv_out],
+            [sds((3, *piece), BF16), sds(taller, BF16), sds(taller, F32)],
+            "pieces_qkv_out_z",
+        )
+        pieces_high, arrived_qkv_out = over_z_high(pieces), over_z_high(send)
+
+        def share_high(ins, outs):
+            outs[0][0], outs[0][1] = ins[0][0], ins[1][0]
+            for part in range(2):
+                outs[1][part, 0], outs[1][part, 1] = ins[0][part + 1], ins[1][part + 1]
+            outs[2][...] = (ins[2][...] + ins[3][...].astype(F32)).astype(BF16)
+
+        near_down, near_gate_up, piece_qkv_out = step(
+            share_high,
+            [pieces, pieces_high, keep_qkv_out, arrived_qkv_out],
+            [sds((2, *piece), BF16), sds((2, 2, *piece), BF16), sds(taller, BF16)],
+            "share_z_high",
+        )
+        down_low, gate_up_x = over_z_low(near_down), over_x(near_gate_up)
+        qkv_out_high = over_z_high(piece_qkv_out)
+
+        def share_next(ins, outs):
+            outs[0][0], outs[0][1] = ins[0][...], ins[1][...]
+            for part in range(2):
+                outs[1][part, 0], outs[1][part, 1] = ins[2][part], ins[3][part]
+            outs[2][0], outs[2][1] = ins[4][...], ins[5][...]
+
+        near_down, near_gate_up, near_qkv_out = step(
+            share_next,
+            [near_down, down_low, near_gate_up, gate_up_x, piece_qkv_out, qkv_out_high],
+            [sds((2, 2, *piece), BF16), sds((2, 2, 2, *piece), BF16), sds((2, *taller), BF16)],
+            "share_next",
+        )
+        down_x, gate_up_low = over_x(near_down), over_z_low(near_gate_up)
+        qkv_out_x = over_x(near_qkv_out)
+
+        def share_last(ins, outs):
+            for x in range(2):
+                for low in range(2):
+                    for high in range(2):
+                        slot = low * 2 + high
+                        outs[0][0, x, slot] = ins[x][low, high]
+                        for part in range(2):
+                            outs[1][part, x, slot] = ins[2 + low][part, x, high]
+            outs[2][0], outs[2][1] = ins[4][...], ins[5][...]
+
+        near_down, near_gate_up, near_qkv_out = step(
+            share_last,
+            [near_down, down_x, near_gate_up, gate_up_low, near_qkv_out, qkv_out_x],
+            [sds((1, 2, 4, *piece), BF16), sds((2, 2, 4, *piece), BF16), sds((2, 2, *taller), BF16)],
+            "share_last",
+        )
+        far_down, far_gate_up = over_core(near_down), over_core(near_gate_up)
+        qkv_out_low = over_z_low(near_qkv_out)
+        by_row = lambda t, _: ((t % 2) * 2 + t // 2, 0)
         one_down, two_down, next_down = update_state(
-            summed,
+            idx,
+            near_down,
+            far_down,
             (0,),
             [((HALF, down_rows), by_row)],
             (put_down,),
@@ -695,17 +907,38 @@
             (HALF, down_rows),
             "update_down",
         )
+
+        def share_qkv_out(ins, outs):
+            for x in range(2):
+                for low in range(2):
+                    for high in range(2):
+                        outs[0][0, x, low * 2 + high] = ins[low][x, high]
+
+        (near_qkv_out,) = step(
+            share_qkv_out,
+            [near_qkv_out, qkv_out_low],
+            [sds((1, 2, 4, *taller), BF16)],
+            "share_qkv_out",
+            (one_down,),
+        )
+        far_qkv_out = over_core(near_qkv_out)
         one_gate_up, two_gate_up, next_gate_up = update_state(
-            summed,
-            (1, 2),
-            [((HALF, FF), lambda t: (t % 2, t // 2))],
+            idx,
+            near_gate_up,
+            far_gate_up,
+            (0, 1),
+            [((HALF, FF), lambda t, _: (t % 2, t // 2))],
             (put_upper, put_lower),
             [w_gate_up, first_gate_up, second_gate_up],
             (HALF, FF),
             "update_gate_up",
+            (),
+            (near_qkv_out,),
         )
         updated = update_state(
-            summed_qkv_out,
+            idx,
+            near_qkv_out,
+            far_qkv_out,
             (0,),
             [((CUT_ROWS, QKV), by_row), ((CUT_ROWS, width), by_row)],
             (put_columns,),
@@ -713,6 +946,7 @@
             (CUT_ROWS + 8, QKV + width),
             "update_qkv_out",
             (norm_gains, first_gains, second_gains),
+            (one_gate_up,),
         )
         one_qkv, one_out, two_qkv, two_out, next_qkv, next_out = updated[:6]
         one_gains, two_gains, next_gains = updated[6:]

time: 226 us -> 169 us (0.75)
  blocking collectives: 22.8 us -> 0 us
  Pallas kernels: 55 us -> 34.7 us
  between operations: 14.3 us -> 1.26 us
  waiting for transfers between devices: 98.1 us -> 85.7 us
  local copies, waits for them, and re-layouts: 2.76 us -> 12.3 us
  starting transfers between devices: 27.9 us -> 35.1 us
  other arithmetic: 4.17 us -> 0.08 us
    all_gather x1 -> x0, blocking collectives: 22.8 us -> none  [sum_over_line(): return lax.all_gather(piece.astype(BF16), 'dp', axis=0)]
    ppermute x25 -> x36, waiting for transfers between devices: 98.1 us -> 85.7 us  [swap(): return lax.ppermute(values, axis, [(i, i ^ mask) for i in range(size)])]
    pallas_call x4 -> x5, Pallas kernels: 29.4 us -> 17.2 us  [call(): pl.pallas_call(kernel, out_shape=tuple(outs), in_specs=[pl.BlockSpec(memo...]
    unnamed x24 -> x54, local copies, waits for them, and re-layouts: 2.35 us -> 11.9 us
    ppermute x25 -> x36, starting transfers between devices: 27.9 us -> 35.1 us  [swap(): return lax.ppermute(values, axis, [(i, i ^ mask) for i in range(size)])]
    pallas_call x3 -> x18, Pallas kernels: 22.2 us -> 16.8 us  [the longest x3 15 us: update_state(): pl.pallas_call(kernel, grid_spec=pltpu.PrefetchScalarGridSpec(num_scalar_...]
    pallas_call x1, Pallas kernels: 3.35 us -> 0.71 us  [pack_weights(): pl.pallas_call(kernel, grid_spec=pltpu.PrefetchScalarGridSpec(num_scalar_...]
    add x9 -> x0, other arithmetic: 2.5 us -> none  [the longest x3 1.96 us: sum_over_plane(): total = keep.astype(F32) + arrived.astype(F32)]
  transfers between devices with their start and end apart: 26 -> 36, of which waited for: 18 -> 19; matrix products, arithmetic and copies ran while one was open for 1% -> 0% of each run, Pallas kernels for 16% -> 12%
where the time goes in v3:
time: 169 us
  waiting for transfers between devices  85.7 us (51%)
  starting transfers between devices  35.1 us (21%)
  Pallas kernels  34.7 us (21%)
  local copies, waits for them, and re-layouts  12.3 us (7%)
    ppermute x36, waiting for transfers between devices, swap(): return lax.ppermute(values, axis, [(i, i ^ mask) for i in range(size)])  85.7 us
    ppermute x36, starting transfers between devices, swap(): return lax.ppermute(values, axis, [(i, i ^ mask) for i in range(size)])  35.1 us
    pallas_call x5, Pallas kernels, call(): pl.pallas_call(kernel, out_shape=tuple(outs), in_specs=[pl.BlockSpec(memo...  17.2 us
    pallas_call x3, Pallas kernels, update_state(): pl.pallas_call(kernel, grid_spec=pltpu.PrefetchScalarGridSpec(num_scalar_...  15 us
    unnamed x54, local copies, waits for them, and re-layouts  11.9 us
  transfers between devices with their start and end apart: 36, of which 19 were waited for; matrix products, arithmetic and copies ran while one was open for 0% of the time, Pallas kernels for 12%

profile of v3, /device:TPU:0, one launch (start us, length us, event | category | flops | bytes accessed | tf_op | source)
XLA Modules:
  0.0 169.1 jit_solution(8930485482805333119)
XLA Ops:
  0.7 2.0 %copy-done = f32[288,3072]{1,0:T(8,128)S(1)} copy-done((f32[288,3072]{1,0:T(8,128)S(1)}, f32[288,3072]{1,0:T(8,128)}, u32[]{:S(2)}) %copy-start) | copy-done | bytes 3538968
  2.7 1.3 copy-done.2
  4.0 1.5 copy-done.4
  5.5 1.1 copy-done.6
  8.0 3.0 %collective-permute-start = (bf16[160,1536]{1,0:T(8,128)(2,1)S(1)}, bf16[160,1536]{1,0:T(8,128)(2,1)S(1)}, u32[]{:S(2)}, u32[]{:S(2)}) collective-permute-start(bf16[160,1536]{1,0:T(8,128)(2,1)S(1)} %get-tuple-element.95), channel_id=1, source_target_pairs={{0,1},{1,0},{2,3},{3,2},{4,5},{5,4},{6,7},{7,6},{8,9},{9,8},{10,11... | collective-permute-start | bytes 1474568 | tf_op jit(solution)/shard_map/ppermute | solution.py:609
  11.1 20.6 %collective-permute-done.2.refs_9_.refs_6_ = bf16[144,1536]{1,0:T(8,128)(2,1)S(1)} collective-permute-done((bf16[144,1536]{1,0:T(8,128)(2,1)S(1)}, bf16[144,1536]{1,0:T(8,128)(2,1)S(1)}, u32[]{:S(2)}, u32[]{:S(2)}) %collective-permute-start.2) | collective-permute-done | bytes 442400 | tf_op jit(solution)/shard_map/ppermute | solution.py:609
  31.8 1.7 %collective-permute-start.3 = (bf16[144,1536]{1,0:T(8,128)(2,1)S(1)}, bf16[144,1536]{1,0:T(8,128)(2,1)S(1)}, u32[]{:S(2)}, u32[]{:S(2)}) collective-permute-start(bf16[144,1536]{1,0:T(8,128)(2,1)S(1)} %collective-permute-done.2.refs_9_.refs_6_), channel_id=1, source_target_pairs={{0,4},{2,6},{4,0},{6,2},{8,12},{10,14},{12,8},{14,10},{16,20},{18,... | collective-permute-start | bytes 1327112 | tf_op jit(solution)/shard_map/ppermute | solution.py:609
  33.5 1.5 collective-permute-start.6
  35.2 7.9 %collective-permute-done.3.refs_10_.refs_7_ = bf16[144,1536]{1,0:T(8,128)(2,1)S(1)} collective-permute-done((bf16[144,1536]{1,0:T(8,128)(2,1)S(1)}, bf16[144,1536]{1,0:T(8,128)(2,1)S(1)}, u32[]{:S(2)}, u32[]{:S(2)}) %collective-permute-start.3) | collective-permute-done | bytes 442400 | tf_op jit(solution)/shard_map/ppermute | solution.py:609
  43.2 2.3 %attention.1 = (bf16[128,960]{1,0:T(8,128)(2,1)S(1)}, bf16[128,576]{1,0:T(8,128)(2,1)S(1)}, f32[128,128]{1,0:T(8,128)S(1)}, f32[128,128]{1,0:T(8,128)S(1)}, f32[...) custom-call(s32[4]{0:T(128)S(1)} %pad_add_fusion.idx_ref.refs_0_, bf16[576,128]{1,0:T(8,128)(2,1)S(1)} %bitcast.57, ...), custom_call_target="tpu_custom_call" | custom-call | flops 141557760 | bytes 3325696 | tf_op jit(solution)/shard_map/attention/pallas_call | solution.py:133
  46.2 2.8 %feed_forward.1 = (f32[128,576]{1,0:T(8,128)S(1)}, bf16[128,576]{1,0:T(8,128)(2,1)S(1)}, f32[128,3072]{1,0:T(8,128)S(1)}, bf16[128,1536]{1,0:T(8,128)(2,1)S(1)},...) custom-call(s32[4]{0:T(128)S(1)} %pad_add_fusion.idx_ref.refs_0_, ...), custom_call_target="tpu_custom_call" | custom-call | flops 766771200 | bytes 11579904 | tf_op jit(solution)/shard_map/feed_forward/pallas_call | solution.py:133
  49.1 3.9 %feed_back.1 = (bf16[128,3072]{1,0:T(8,128)(2,1)S(1)}, bf16[576,128]{1,0:T(8,128)(2,1)}, bf16[2,2,8,72,384]{4,3,2,1,0:T(8,128)(2,1)S(1)}, bf16[2,2,8,72,384]{4,3,2,1,0:T(8,128)(2,1)S(1)}) custom-call(s32[4]{0:T(128)S(1)} %pad_add_fusion.idx_ref.refs_0_, f32[128,3072]{1,0:T(8,128)S(1)} %get-tuple-element.100.refs_1_, ...), custom_call_target="tpu_custom_call" | custom-call | flops 914227200 | bytes 9682944 | tf_op jit(solution)/shard_map/feed_back/pallas_call | solution.py:133
  53.6 4.4 %collective-permute-done.8 = bf16[1,2,8,72,384]{4,3,2,1,0:T(8,128)(2,1)S(1)} collective-permute-done((bf16[1,2,8,72,384]{4,3,2,1,0:T(8,128)(2,1)S(1)}, bf16[1,2,8,72,384]{4,3,2,1,0:T(8,128)(2,1)S(1)}, u32[]{:S(2)}, u32[]{:S(2)}) %collective-permute-start.8) | collective-permute-done | bytes 884768 | tf_op jit(solution)/shard_map/ppermute | solution.py:609
  58.2 3.1 %middle_back.1 = (f32[128,576]{1,0:T(8,128)S(1)}, bf16[128,576]{1,0:T(8,128)(2,1)S(1)}, f32[1,576]{1,0:T(1,128)S(1)}) custom-call(s32[4]{0:T(128)S(1)} %pad_add_fusion.idx_ref.refs_0_, bf16[576,128]{1,0:T(8,128)(2,1)S(1)} %bitcast.62, f32[128,576]{1,0:T(8,128)S(1)} %get-tuple-element.103.refs_4_.refs_2_, ...), custom_call_target="tpu_custom_call" | custom-call | flops 545587200 | bytes 8633088 | tf_op jit(solution)/shard_map/middle_back/pallas_call | solution.py:133
  62.8 5.1 %attention_back.1 = (bf16[576,128]{1,0:T(8,128)(2,1)}, bf16[1,2,8,80,384]{4,3,2,1,0:T(8,128)(2,1)S(1)}, bf16[1,2,8,80,384]{4,3,2,1,0:T(8,128)(2,1)S(1)}) custom-call(s32[4]{0:T(128)S(1)} %pad_add_fusion.idx_ref.refs_0_, bf16[576,128]{1,0:T(8,128)(2,1)S(1)} %bitcast.59, f32[128,576]{1,0:T(8,128)S(1)} %get-tuple-element.109.refs_4_.refs_2_, ...), custom_call_target="tpu_custom_call" | custom-call | flops 634060800 | bytes 5389056 | tf_op jit(solution)/shard_map/attention_back/pallas_call | solution.py:133
  68.3 1.5 collective-permute-start.10
  69.8 1.0 collective-permute-start.12
  70.8 1.6 collective-permute-start.13
  72.4 8.1 %collective-permute-done.10 = bf16[8,72,384]{2,1,0:T(8,128)(2,1)S(1)} collective-permute-done((bf16[8,72,384]{2,1,0:T(8,128)(2,1)S(1)}, bf16[8,72,384]{2,1,0:T(8,128)(2,1)S(1)}, u32[]{:S(2)}, u32[]{:S(2)}) %collective-permute-start.10) | collective-permute-done | bytes 442400 | tf_op jit(solution)/shard_map/ppermute | solution.py:609
  81.8 1.6 collective-permute-start.20
  83.3 1.2 collective-permute-start.11
  84.8 1.6 collective-permute-start.15
  86.9 2.8 %collective-permute-done.11 = bf16[4,72,384]{2,1,0:T(8,128)(2,1)S(1)} collective-permute-done((bf16[4,72,384]{2,1,0:T(8,128)(2,1)S(1)}, bf16[4,72,384]{2,1,0:T(8,128)(2,1)S(1)}, u32[]{:S(2)}, u32[]{:S(2)}) %collective-permute-start.11) | collective-permute-done | bytes 221216 | tf_op jit(solution)/shard_map/ppermute | solution.py:609
  89.7 1.5 collective-permute-done.15.refs_3_
  91.2 7.8 %collective-permute-done.16.refs_5_ = bf16[2,2,72,384]{3,2,1,0:T(8,128)(2,1)S(1)} collective-permute-done((bf16[2,2,72,384]{3,2,1,0:T(8,128)(2,1)S(1)}, bf16[2,2,72,384]{3,2,1,0:T(8,128)(2,1)S(1)}, u32[]{:S(2)}, u32[]{:S(2)}) %collective-permute-start.16) | collective-permute-done | bytes 221216 | tf_op jit(solution)/shard_map/ppermute | solution.py:609
  99.2 1.6 collective-permute-start.22
  100.8 1.6 collective-permute-start.17
  102.4 1.5 collective-permute-start.18
  104.4 1.1 collective-permute-done.17.refs_1_
  105.5 1.6 collective-permute-done.18.refs_3_
  107.1 1.5 collective-permute-done.19.refs_5_
  108.7 2.7 %collective-permute-start.21 = (bf16[3,72,384]{2,1,0:T(8,128)(2,1)S(1)}, bf16[3,72,384]{2,1,0:T(8,128)(2,1)S(1)}, u32[]{:S(2)}, u32[]{:S(2)}) collective-permute-start(bf16[3,72,384]{2,1,0:T(8,128)(2,1)S(1)} %get-tuple-element.142), channel_id=1, source_target_pairs={{0,16},{2,18},{4,20},{6,22},{8,24},{10,26},{12,28},{14,30},{16,0},... | collective-permute-start | bytes 497672 | tf_op jit(solution)/shard_map/ppermute | solution.py:609
  111.4 0.9 collective-permute-start.23
  112.3 5.2 %collective-permute-done.21.refs_1_ = bf16[3,72,384]{2,1,0:T(8,128)(2,1)S(1)} collective-permute-done((bf16[3,72,384]{2,1,0:T(8,128)(2,1)S(1)}, bf16[3,72,384]{2,1,0:T(8,128)(2,1)S(1)}, u32[]{:S(2)}, u32[]{:S(2)}) %collective-permute-start.21) | collective-permute-done | bytes 165920 | tf_op jit(solution)/shard_map/ppermute | solution.py:609
  118.5 2.9 %collective-permute-start.25 = (bf16[80,384]{1,0:T(8,128)(2,1)S(1)}, bf16[80,384]{1,0:T(8,128)(2,1)S(1)}, u32[]{:S(2)}, u32[]{:S(2)}) collective-permute-start(bf16[80,384]{1,0:T(8,128)(2,1)S(1)} %get-tuple-element.148), channel_id=1, source_target_pairs={{0,16},{2,18},{4,20},{6,22},{8,24},{10,26},{12,28},{14,30},{16,0},... | collective-permute-start | bytes 184328 | tf_op jit(solution)/shard_map/ppermute | solution.py:609
  121.4 7.1 %collective-permute-done.25.refs_3_ = bf16[80,384]{1,0:T(8,128)(2,1)S(1)} collective-permute-done((bf16[80,384]{1,0:T(8,128)(2,1)S(1)}, bf16[80,384]{1,0:T(8,128)(2,1)S(1)}, u32[]{:S(2)}, u32[]{:S(2)}) %collective-permute-start.25) | collective-permute-done | bytes 61472 | tf_op jit(solution)/shard_map/ppermute | solution.py:609
  128.6 1.6 collective-permute-start.26
  130.2 1.8 %collective-permute-start.28 = (bf16[80,384]{1,0:T(8,128)(2,1)S(1)}, bf16[80,384]{1,0:T(8,128)(2,1)S(1)}, u32[]{:S(2)}, u32[]{:S(2)}) collective-permute-start(bf16[80,384]{1,0:T(8,128)(2,1)S(1)} %get-tuple-element.151.refs_4_), channel_id=1, source_target_pairs={{0,16},{2,18},{4,20},{6,22},{8,24},{10,26},{12,28},{14,30},{16,0},... | collective-permute-start | bytes 184328 | tf_op jit(solution)/shard_map/ppermute | solution.py:609
  132.0 4.0 %collective-permute-done.28.refs_5_ = bf16[80,384]{1,0:T(8,128)(2,1)S(1)} collective-permute-done((bf16[80,384]{1,0:T(8,128)(2,1)S(1)}, bf16[80,384]{1,0:T(8,128)(2,1)S(1)}, u32[]{:S(2)}, u32[]{:S(2)}) %collective-permute-start.28) | collective-permute-done | bytes 61472 | tf_op jit(solution)/shard_map/ppermute | solution.py:609
  136.2 1.7 %collective-permute-start.29 = (bf16[2,2,72,384]{3,2,1,0:T(8,128)(2,1)S(1)}, bf16[2,2,72,384]{3,2,1,0:T(8,128)(2,1)S(1)}, u32[]{:S(2)}, u32[]{:S(2)}) collective-permute-start(bf16[2,2,72,384]{3,2,1,0:T(8,128)(2,1)S(1)} %get-tuple-element.152.refs_0_), channel_id=1, source_target_pairs={{0,4},{2,6},{4,0},{6,2},{8,12},{10,14},{12,8},{14,10},{16,20},{18,... | collective-permute-start | bytes 663560 | tf_op jit(solution)/shard_map/ppermute | solution.py:609
  138.3 5.2 %collective-permute-done.31.refs_5_ = bf16[2,80,384]{2,1,0:T(8,128)(2,1)S(1)} collective-permute-done((bf16[2,80,384]{2,1,0:T(8,128)(2,1)S(1)}, bf16[2,80,384]{2,1,0:T(8,128)(2,1)S(1)}, u32[]{:S(2)}, u32[]{:S(2)}) %collective-permute-start.31) | collective-permute-done | bytes 122912 | tf_op jit(solution)/shard_map/ppermute | solution.py:609
  143.5 1.8 %collective-permute-done.30.refs_3_ = bf16[2,2,2,72,384]{4,3,2,1,0:T(8,128)(2,1)S(1)} collective-permute-done((bf16[2,2,2,72,384]{4,3,2,1,0:T(8,128)(2,1)S(1)}, bf16[2,2,2,72,384]{4,3,2,1,0:T(8,128)(2,1)S(1)}, u32[]{:S(2)}, u32[]{:S(2)}) %collective-permute-start.30) | collective-permute-done | bytes 442400 | tf_op jit(solution)/shard_map/ppermute | solution.py:609
  147.3 3.8 %update_down.1 = (f32[576,768]{1,0:T(8,128)}, f32[576,768]{1,0:T(8,128)}, f32[576,768]{1,0:T(8,128)}) custom-call(s32[4]{0:T(128)S(1)} %pad_add_fusion.idx_ref.refs_0_, bf16[1,2,4,72,384]{4,3,2,1,0:T(8,128)(2,1)S(1)} %get-tuple-element.156.refs_0_, bf16[1,2,4,72,384]{4,3,2,1,0:T(8,128)(2,1)S(1)} %collective-permute-done.33.refs_1_, f32[576,768]{1,0:T(8,128)S(1)} %bitcast.44, ...), custom_call_target="tpu_custom_call" | custom-call | bytes 10616832 | tf_op jit(solution)/shard_map/update_down/pallas_call | solution.py:588
  151.2 2.8 %collective-permute-done.32.refs_1_ = bf16[2,2,80,384]{3,2,1,0:T(8,128)(2,1)S(1)} collective-permute-done((bf16[2,2,80,384]{3,2,1,0:T(8,128)(2,1)S(1)}, bf16[2,2,80,384]{3,2,1,0:T(8,128)(2,1)S(1)}, u32[]{:S(2)}, u32[]{:S(2)}) %collective-permute-start.32) | collective-permute-done | bytes 245792 | tf_op jit(solution)/shard_map/ppermute | solution.py:609
  154.0 1.5 copy-done.13
  155.7 6.5 %update_gate_up.1 = (f32[288,3072]{1,0:T(8,128)}, f32[288,3072]{1,0:T(8,128)}, f32[288,3072]{1,0:T(8,128)}) custom-call(s32[4]{0:T(128)S(1)} %pad_add_fusion.idx_ref.refs_0_, bf16[2,2,4,72,384]{4,3,2,1,0:T(8,128)(2,1)S(1)} %get-tuple-element.158.refs_0_.refs_2_, bf16[2,2,4,72,384]{4,3,2,1,0:T(8,128)(2,1)S(1)} %collective-permute-done.35.refs_1_.refs_3_, ...), custom_call_target="tpu_custom_call" | custom-call | bytes 21233664 | tf_op jit(solution)/shard_map/update_gate_up/pallas_call | solution.py:588
  162.2 2.0 %copy-done.10 = f32[288,3072]{1,0:T(8,128)S(1)} copy-done((f32[288,3072]{1,0:T(8,128)S(1)}, f32[288,3072]{1,0:T(8,128)}, u32[]{:S(2)}) %copy-start.10) | copy-done | bytes 3538968
  164.2 4.7 %update_qkv_out.1 = (f32[288,960]{1,0:T(8,128)}, f32[288,576]{1,0:T(8,128)}, f32[288,960]{1,0:T(8,128)}, f32[288,576]{1,0:T(8,128)}, f32[288,960]{1,0:T(8,128)},...) custom-call(s32[4]{0:T(128)S(1)} %pad_add_fusion.idx_ref.refs_0_, ...), custom_call_target="tpu_custom_call" | custom-call | bytes 10616832 | tf_op jit(solution)/shard_map/update_qkv_out/pallas_call | solution.py:588
  (105 shorter events, 11.8 us)
Async XLA Ops:
  7.3 35.8 %copy-start.14 = (bf16[1,128,576]{1,2,0:T(8,128)(2,1)S(1)}, bf16[1,128,576]{1,2,0:T(8,128)(2,1)}, u32[]{:S(2)}) copy-start(bf16[1,128,576]{1,2,0:T(8,128)(2,1)} %param.19) | copy-start | bytes 442372
  7.3 35.8 %copy-start.25 = (s32[1,128]{1,0:T(1,128)S(1)}, s32[1,128]{1,0:T(1,128)}, u32[]{:S(2)}) copy-start(s32[1,128]{1,0:T(1,128)} %refs_2_.2) | copy-start | bytes 1540
  7.3 35.8 %copy-start.26 = (f32[1,128]{1,0:T(1,128)S(1)}, f32[1,128]{1,0:T(1,128)}, u32[]{:S(2)}) copy-start(f32[1,128]{1,0:T(1,128)} %constant.14.clone.refs_3_) | copy-start | bytes 1540
  7.3 38.9 %copy-start.7 = (f32[288,576]{1,0:T(8,128)S(1)}, f32[288,576]{1,0:T(8,128)}, u32[]{:S(2)}) copy-start(f32[288,576]{1,0:T(8,128)} %refs_3_.2) | copy-start | bytes 1990660
  8.0 25.5 %collective-permute-start = (bf16[160,1536]{1,0:T(8,128)(2,1)S(1)}, bf16[160,1536]{1,0:T(8,128)(2,1)S(1)}, u32[]{:S(2)}, u32[]{:S(2)}) collective-permute-start(bf16[160,1536]{1,0:T(8,128)(2,1)S(1)} %get-tuple-element.95), channel_id=1, source_target_pairs={{0,1},{1,0},{2,3},{3,2},{4,5},{5,4},{6,7},{7,6},{8,9},{9,8},{10,11... | collective-permute-start | bytes 1474568 | tf_op jit(solution)/shard_map/ppermute | solution.py:609
  11.0 20.7 %collective-permute-start.2 = (bf16[144,1536]{1,0:T(8,128)(2,1)S(1)}, bf16[144,1536]{1,0:T(8,128)(2,1)S(1)}, u32[]{:S(2)}, u32[]{:S(2)}) collective-permute-start(bf16[144,1536]{1,0:T(8,128)(2,1)S(1)} %get-tuple-element.98), channel_id=1, source_target_pairs={{0,1},{1,0},{2,3},{3,2},{4,5},{5,4},{6,7},{7,6},{8,9},{9,8},{10,11... | collective-permute-start | bytes 1327112 | tf_op jit(solution)/shard_map/ppermute | solution.py:609
  31.8 11.4 %collective-permute-start.3 = (bf16[144,1536]{1,0:T(8,128)(2,1)S(1)}, bf16[144,1536]{1,0:T(8,128)(2,1)S(1)}, u32[]{:S(2)}, u32[]{:S(2)}) collective-permute-start(bf16[144,1536]{1,0:T(8,128)(2,1)S(1)} %collective-permute-done.2.refs_9_.refs_6_), channel_id=1, source_target_pairs={{0,4},{2,6},{4,0},{6,2},{8,12},{10,14},{12,8},{14,10},{16,20},{18,... | collective-permute-start | bytes 1327112 | tf_op jit(solution)/shard_map/ppermute | solution.py:609
  33.5 9.7 %collective-permute-start.1 = (bf16[160,1536]{1,0:T(8,128)(2,1)S(1)}, bf16[160,1536]{1,0:T(8,128)(2,1)S(1)}, u32[]{:S(2)}, u32[]{:S(2)}) collective-permute-start(bf16[160,1536]{1,0:T(8,128)(2,1)S(1)} %collective-permute-done.refs_5_.refs_7_.refs_6_.refs_11_.refs_12_), channel_id=1, source_target_pairs={{0,2},{2,0},{4,6},{6,4},{8,10},{10,8},{12,14},{14,12},{16,18},{18,... | collective-permute-start | bytes 1474568 | tf_op jit(solution)/shard_map/ppermute | solution.py:609
  33.5 12.6 %collective-permute-start.6 = (bf16[288,768]{1,0:T(8,128)(2,1)S(1)}, bf16[288,768]{1,0:T(8,128)(2,1)S(1)}, u32[]{:S(2)}, u32[]{:S(2)}) collective-permute-start(bf16[288,768]{1,0:T(8,128)(2,1)S(1)} %get-tuple-element.99), channel_id=1, source_target_pairs={{0,1},{1,0},{2,3},{3,2},{4,5},{5,4},{6,7},{7,6},{8,9},{9,8},{10,11... | collective-permute-start | bytes 1327112 | tf_op jit(solution)/shard_map/ppermute | solution.py:609
  35.0 11.2 %collective-permute-start.4 = (bf16[144,1536]{1,0:T(8,128)(2,1)S(1)}, bf16[144,1536]{1,0:T(8,128)(2,1)S(1)}, u32[]{:S(2)}, u32[]{:S(2)}) collective-permute-start(bf16[144,1536]{1,0:T(8,128)(2,1)S(1)} %collective-permute-done.2.refs_9_.refs_6_), channel_id=1, source_target_pairs={{0,2},{2,0},{4,6},{6,4},{8,10},{10,8},{12,14},{14,12},{16,18},{18,... | collective-permute-start | bytes 1327112 | tf_op jit(solution)/shard_map/ppermute | solution.py:609
  43.1 3.1 %collective-permute-start.5 = (bf16[144,1536]{1,0:T(8,128)(2,1)S(1)}, bf16[144,1536]{1,0:T(8,128)(2,1)S(1)}, u32[]{:S(2)}, u32[]{:S(2)}) collective-permute-start(bf16[144,1536]{1,0:T(8,128)(2,1)S(1)} %collective-permute-done.3.refs_10_.refs_7_), channel_id=1, source_target_pairs={{0,2},{2,0},{4,6},{6,4},{8,10},{10,8},{12,14},{14,12},{16,18},{18,... | collective-permute-start | bytes 1327112 | tf_op jit(solution)/shard_map/ppermute | solution.py:609
  46.1 3.0 %collective-permute-start.7 = (bf16[288,768]{1,0:T(8,128)(2,1)S(1)}, bf16[288,768]{1,0:T(8,128)(2,1)S(1)}, u32[]{:S(2)}, u32[]{:S(2)}) collective-permute-start(bf16[288,768]{1,0:T(8,128)(2,1)S(1)} %pass_on.1.refs_13_.refs_7_), channel_id=1, source_target_pairs={{0,2},{2,0},{4,6},{6,4},{8,10},{10,8},{12,14},{14,12},{16,18},{18,... | collective-permute-start | bytes 1327112 | tf_op jit(solution)/shard_map/ppermute | solution.py:609
  52.9 8.4 %collective-permute-start.9 = (bf16[2,2,8,72,384]{4,3,2,1,0:T(8,128)(2,1)S(1)}, bf16[2,2,8,72,384]{4,3,2,1,0:T(8,128)(2,1)S(1)}, u32[]{:S(2)}, u32[]{:S(2)}) collective-permute-start(bf16[2,2,8,72,384]{4,3,2,1,0:T(8,128)(2,1)S(1)} %get-tuple-element.117), channel_id=1, source_target_pairs={{0,2},{2,0},{4,6},{6,4},{8,10},{10,8},{12,14},{14,12},{16,18},{18,... | collective-permute-start | bytes 5308424 | tf_op jit(solution)/shard_map/ppermute | solution.py:609
  53.4 4.6 %collective-permute-start.8 = (bf16[1,2,8,72,384]{4,3,2,1,0:T(8,128)(2,1)S(1)}, bf16[1,2,8,72,384]{4,3,2,1,0:T(8,128)(2,1)S(1)}, u32[]{:S(2)}, u32[]{:S(2)}) collective-permute-start(bf16[1,2,8,72,384]{4,3,2,1,0:T(8,128)(2,1)S(1)} %get-tuple-element.107), channel_id=1, source_target_pairs={{0,2},{2,0},{4,6},{6,4},{8,10},{10,8},{12,14},{14,12},{16,18},{18,... | collective-permute-start | bytes 2654216 | tf_op jit(solution)/shard_map/ppermute | solution.py:609
  67.9 13.6 %collective-permute-start.14 = (bf16[1,2,8,80,384]{4,3,2,1,0:T(8,128)(2,1)S(1)}, bf16[1,2,8,80,384]{4,3,2,1,0:T(8,128)(2,1)S(1)}, u32[]{:S(2)}, u32[]{:S(2)}) collective-permute-start(bf16[1,2,8,80,384]{4,3,2,1,0:T(8,128)(2,1)S(1)} %get-tuple-element.127), channel_id=1, source_target_pairs={{0,2},{2,0},{4,6},{6,4},{8,10},{10,8},{12,14},{14,12},{16,18},{18,... | collective-permute-start | bytes 2949128 | tf_op jit(solution)/shard_map/ppermute | solution.py:609
  68.3 12.2 %collective-permute-start.10 = (bf16[8,72,384]{2,1,0:T(8,128)(2,1)S(1)}, bf16[8,72,384]{2,1,0:T(8,128)(2,1)S(1)}, u32[]{:S(2)}, u32[]{:S(2)}) collective-permute-start(bf16[8,72,384]{2,1,0:T(8,128)(2,1)S(1)} %get-tuple-element.120), channel_id=1, source_target_pairs={{0,1},{1,0},{2,3},{3,2},{4,5},{5,4},{6,7},{7,6},{8,9},{9,8},{10,11... | collective-permute-start | bytes 1327112 | tf_op jit(solution)/shard_map/ppermute | solution.py:609
  69.8 14.8 %collective-permute-start.12 = (bf16[2,4,72,384]{3,2,1,0:T(8,128)(2,1)S(1)}, bf16[2,4,72,384]{3,2,1,0:T(8,128)(2,1)S(1)}, u32[]{:S(2)}, u32[]{:S(2)}) collective-permute-start(bf16[2,4,72,384]{3,2,1,0:T(8,128)(2,1)S(1)} %get-tuple-element.123), channel_id=1, source_target_pairs={{0,4},{2,6},{4,0},{6,2},{8,12},{10,14},{12,8},{14,10},{16,20},{18,... | collective-permute-start | bytes 1327112 | tf_op jit(solution)/shard_map/ppermute | solution.py:609
  70.8 13.8 %collective-permute-start.13 = (bf16[4,2,72,384]{3,2,1,0:T(8,128)(2,1)S(1)}, bf16[4,2,72,384]{3,2,1,0:T(8,128)(2,1)S(1)}, u32[]{:S(2)}, u32[]{:S(2)}) collective-permute-start(bf16[4,2,72,384]{3,2,1,0:T(8,128)(2,1)S(1)} %get-tuple-element.125), channel_id=1, source_target_pairs={{0,8},{2,10},{4,12},{6,14},{8,0},{10,2},{12,4},{14,6},{16,24},{18,... | collective-permute-start | bytes 1327112 | tf_op jit(solution)/shard_map/ppermute | solution.py:609
  81.8 17.4 %collective-permute-start.20 = (bf16[8,80,384]{2,1,0:T(8,128)(2,1)S(1)}, bf16[8,80,384]{2,1,0:T(8,128)(2,1)S(1)}, u32[]{:S(2)}, u32[]{:S(2)}) collective-permute-start(bf16[8,80,384]{2,1,0:T(8,128)(2,1)S(1)} %get-tuple-element.139), channel_id=1, source_target_pairs={{0,1},{1,0},{2,3},{3,2},{4,5},{5,4},{6,7},{7,6},{8,9},{9,8},{10,11... | collective-permute-start | bytes 1474568 | tf_op jit(solution)/shard_map/ppermute | solution.py:609
  83.3 6.4 %collective-permute-start.11 = (bf16[4,72,384]{2,1,0:T(8,128)(2,1)S(1)}, bf16[4,72,384]{2,1,0:T(8,128)(2,1)S(1)}, u32[]{:S(2)}, u32[]{:S(2)}) collective-permute-start(bf16[4,72,384]{2,1,0:T(8,128)(2,1)S(1)} %get-tuple-element.122), channel_id=1, source_target_pairs={{0,4},{2,6},{4,0},{6,2},{8,12},{10,14},{12,8},{14,10},{16,20},{18,... | collective-permute-start | bytes 663560 | tf_op jit(solution)/shard_map/ppermute | solution.py:609
  84.8 6.4 %collective-permute-start.15 = (bf16[2,2,72,384]{3,2,1,0:T(8,128)(2,1)S(1)}, bf16[2,2,72,384]{3,2,1,0:T(8,128)(2,1)S(1)}, u32[]{:S(2)}, u32[]{:S(2)}) collective-permute-start(bf16[2,2,72,384]{3,2,1,0:T(8,128)(2,1)S(1)} %get-tuple-element.130), channel_id=1, source_target_pairs={{0,8},{2,10},{4,12},{6,14},{8,0},{10,2},{12,4},{14,6},{16,24},{18,... | collective-permute-start | bytes 663560 | tf_op jit(solution)/shard_map/ppermute | solution.py:609
  86.4 12.6 %collective-permute-start.16 = (bf16[2,2,72,384]{3,2,1,0:T(8,128)(2,1)S(1)}, bf16[2,2,72,384]{3,2,1,0:T(8,128)(2,1)S(1)}, u32[]{:S(2)}, u32[]{:S(2)}) collective-permute-start(bf16[2,2,72,384]{3,2,1,0:T(8,128)(2,1)S(1)} %get-tuple-element.132), channel_id=1, source_target_pairs={{0,1},{1,0},{2,3},{3,2},{4,5},{5,4},{6,7},{7,6},{8,9},{9,8},{10,11... | collective-permute-start | bytes 663560 | tf_op jit(solution)/shard_map/ppermute | solution.py:609
  99.2 12.1 %collective-permute-start.22 = (bf16[4,80,384]{2,1,0:T(8,128)(2,1)S(1)}, bf16[4,80,384]{2,1,0:T(8,128)(2,1)S(1)}, u32[]{:S(2)}, u32[]{:S(2)}) collective-permute-start(bf16[4,80,384]{2,1,0:T(8,128)(2,1)S(1)} %get-tuple-element.143), channel_id=1, source_target_pairs={{0,4},{2,6},{4,0},{6,2},{8,12},{10,14},{12,8},{14,10},{16,20},{18,... | collective-permute-start | bytes 737288 | tf_op jit(solution)/shard_map/ppermute | solution.py:609
  100.8 4.7 %collective-permute-start.17 = (bf16[2,72,384]{2,1,0:T(8,128)(2,1)S(1)}, bf16[2,72,384]{2,1,0:T(8,128)(2,1)S(1)}, u32[]{:S(2)}, u32[]{:S(2)}) collective-permute-start(bf16[2,72,384]{2,1,0:T(8,128)(2,1)S(1)} %get-tuple-element.134), channel_id=1, source_target_pairs={{0,8},{2,10},{4,12},{6,14},{8,0},{10,2},{12,4},{14,6},{16,24},{18,... | collective-permute-start | bytes 331784 | tf_op jit(solution)/shard_map/ppermute | solution.py:609
  102.4 4.7 %collective-permute-start.18 = (bf16[2,72,384]{2,1,0:T(8,128)(2,1)S(1)}, bf16[2,72,384]{2,1,0:T(8,128)(2,1)S(1)}, u32[]{:S(2)}, u32[]{:S(2)}) collective-permute-start(bf16[2,72,384]{2,1,0:T(8,128)(2,1)S(1)} %get-tuple-element.136), channel_id=1, source_target_pairs={{0,1},{1,0},{2,3},{3,2},{4,5},{5,4},{6,7},{7,6},{8,9},{9,8},{10,11... | collective-permute-start | bytes 331784 | tf_op jit(solution)/shard_map/ppermute | solution.py:609
  103.9 4.7 %collective-permute-start.19 = (bf16[2,72,384]{2,1,0:T(8,128)(2,1)S(1)}, bf16[2,72,384]{2,1,0:T(8,128)(2,1)S(1)}, u32[]{:S(2)}, u32[]{:S(2)}) collective-permute-start(bf16[2,72,384]{2,1,0:T(8,128)(2,1)S(1)} %get-tuple-element.138), channel_id=1, source_target_pairs={{0,4},{2,6},{4,0},{6,2},{8,12},{10,14},{12,8},{14,10},{16,20},{18,... | collective-permute-start | bytes 331784 | tf_op jit(solution)/shard_map/ppermute | solution.py:609
  108.7 8.8 %collective-permute-start.21 = (bf16[3,72,384]{2,1,0:T(8,128)(2,1)S(1)}, bf16[3,72,384]{2,1,0:T(8,128)(2,1)S(1)}, u32[]{:S(2)}, u32[]{:S(2)}) collective-permute-start(bf16[3,72,384]{2,1,0:T(8,128)(2,1)S(1)} %get-tuple-element.142), channel_id=1, source_target_pairs={{0,16},{2,18},{4,20},{6,22},{8,24},{10,26},{12,28},{14,30},{16,0},... | collective-permute-start | bytes 497672 | tf_op jit(solution)/shard_map/ppermute | solution.py:609
  111.4 7.0 %collective-permute-start.23 = (bf16[2,80,384]{2,1,0:T(8,128)(2,1)S(1)}, bf16[2,80,384]{2,1,0:T(8,128)(2,1)S(1)}, u32[]{:S(2)}, u32[]{:S(2)}) collective-permute-start(bf16[2,80,384]{2,1,0:T(8,128)(2,1)S(1)} %get-tuple-element.145), channel_id=1, source_target_pairs={{0,8},{2,10},{4,12},{6,14},{8,0},{10,2},{12,4},{14,6},{16,24},{18,... | collective-permute-start | bytes 368648 | tf_op jit(solution)/shard_map/ppermute | solution.py:609
  118.4 29.0 %copy-start.11 = (f32[768,576]{0,1:T(8,128)S(1)}, f32[768,576]{0,1:T(8,128)}, u32[]{:S(2)}) copy-start(f32[768,576]{0,1:T(8,128)} %param.30) | copy-start | bytes 5308420
  118.4 29.0 %copy-start.12 = (f32[768,576]{0,1:T(8,128)S(1)}, f32[768,576]{0,1:T(8,128)}, u32[]{:S(2)}) copy-start(f32[768,576]{0,1:T(8,128)} %param.35) | copy-start | bytes 5308420
  118.4 10.1 %collective-permute-start.24 = (bf16[3,72,384]{2,1,0:T(8,128)(2,1)S(1)}, bf16[3,72,384]{2,1,0:T(8,128)(2,1)S(1)}, u32[]{:S(2)}, u32[]{:S(2)}) collective-permute-start(bf16[3,72,384]{2,1,0:T(8,128)(2,1)S(1)} %get-tuple-element.146.refs_0_), channel_id=1, source_target_pairs={{0,16},{2,18},{4,20},{6,22},{8,24},{10,26},{12,28},{14,30},{16,0},... | collective-permute-start | bytes 497672 | tf_op jit(solution)/shard_map/ppermute | solution.py:609
  118.5 10.0 %collective-permute-start.25 = (bf16[80,384]{1,0:T(8,128)(2,1)S(1)}, bf16[80,384]{1,0:T(8,128)(2,1)S(1)}, u32[]{:S(2)}, u32[]{:S(2)}) collective-permute-start(bf16[80,384]{1,0:T(8,128)(2,1)S(1)} %get-tuple-element.148), channel_id=1, source_target_pairs={{0,16},{2,18},{4,20},{6,22},{8,24},{10,26},{12,28},{14,30},{16,0},... | collective-permute-start | bytes 184328 | tf_op jit(solution)/shard_map/ppermute | solution.py:609
  128.6 7.5 %collective-permute-start.27 = (bf16[2,2,72,384]{3,2,1,0:T(8,128)(2,1)S(1)}, bf16[2,2,72,384]{3,2,1,0:T(8,128)(2,1)S(1)}, u32[]{:S(2)}, u32[]{:S(2)}) collective-permute-start(bf16[2,2,72,384]{3,2,1,0:T(8,128)(2,1)S(1)} %get-tuple-element.150.refs_2_), channel_id=1, source_target_pairs={{0,4},{2,6},{4,0},{6,2},{8,12},{10,14},{12,8},{14,10},{16,20},{18,... | collective-permute-start | bytes 663560 | tf_op jit(solution)/shard_map/ppermute | solution.py:609
  128.6 7.4 %collective-permute-start.26 = (bf16[2,72,384]{2,1,0:T(8,128)(2,1)S(1)}, bf16[2,72,384]{2,1,0:T(8,128)(2,1)S(1)}, u32[]{:S(2)}, u32[]{:S(2)}) collective-permute-start(bf16[2,72,384]{2,1,0:T(8,128)(2,1)S(1)} %get-tuple-element.149.refs_0_), channel_id=1, source_target_pairs={{0,8},{2,10},{4,12},{6,14},{8,0},{10,2},{12,4},{14,6},{16,24},{18,... | collective-permute-start | bytes 331784 | tf_op jit(solution)/shard_map/ppermute | solution.py:609
  130.2 5.8 %collective-permute-start.28 = (bf16[80,384]{1,0:T(8,128)(2,1)S(1)}, bf16[80,384]{1,0:T(8,128)(2,1)S(1)}, u32[]{:S(2)}, u32[]{:S(2)}) collective-permute-start(bf16[80,384]{1,0:T(8,128)(2,1)S(1)} %get-tuple-element.151.refs_4_), channel_id=1, source_target_pairs={{0,16},{2,18},{4,20},{6,22},{8,24},{10,26},{12,28},{14,30},{16,0},... | collective-permute-start | bytes 184328 | tf_op jit(solution)/shard_map/ppermute | solution.py:609
  136.1 9.2 %collective-permute-start.30 = (bf16[2,2,2,72,384]{4,3,2,1,0:T(8,128)(2,1)S(1)}, bf16[2,2,2,72,384]{4,3,2,1,0:T(8,128)(2,1)S(1)}, u32[]{:S(2)}, u32[]{:S(2)}) collective-permute-start(bf16[2,2,2,72,384]{4,3,2,1,0:T(8,128)(2,1)S(1)} %get-tuple-element.153.refs_2_), channel_id=1, source_target_pairs={{0,8},{2,10},{4,12},{6,14},{8,0},{10,2},{12,4},{14,6},{16,24},{18,... | collective-permute-start | bytes 1327112 | tf_op jit(solution)/shard_map/ppermute | solution.py:609
  136.2 7.3 %collective-permute-start.29 = (bf16[2,2,72,384]{3,2,1,0:T(8,128)(2,1)S(1)}, bf16[2,2,72,384]{3,2,1,0:T(8,128)(2,1)S(1)}, u32[]{:S(2)}, u32[]{:S(2)}) collective-permute-start(bf16[2,2,72,384]{3,2,1,0:T(8,128)(2,1)S(1)} %get-tuple-element.152.refs_0_), channel_id=1, source_target_pairs={{0,4},{2,6},{4,0},{6,2},{8,12},{10,14},{12,8},{14,10},{16,20},{18,... | collective-permute-start | bytes 663560 | tf_op jit(solution)/shard_map/ppermute | solution.py:609
  137.9 5.6 %collective-permute-start.31 = (bf16[2,80,384]{2,1,0:T(8,128)(2,1)S(1)}, bf16[2,80,384]{2,1,0:T(8,128)(2,1)S(1)}, u32[]{:S(2)}, u32[]{:S(2)}) collective-permute-start(bf16[2,80,384]{2,1,0:T(8,128)(2,1)S(1)} %get-tuple-element.154.refs_4_), channel_id=1, source_target_pairs={{0,4},{2,6},{4,0},{6,2},{8,12},{10,14},{12,8},{14,10},{16,20},{18,... | collective-permute-start | bytes 368648 | tf_op jit(solution)/shard_map/ppermute | solution.py:609
  145.5 1.9 %collective-permute-start.33 = (bf16[1,2,4,72,384]{4,3,2,1,0:T(8,128)(2,1)S(1)}, bf16[1,2,4,72,384]{4,3,2,1,0:T(8,128)(2,1)S(1)}, u32[]{:S(2)}, u32[]{:S(2)}) collective-permute-start(bf16[1,2,4,72,384]{4,3,2,1,0:T(8,128)(2,1)S(1)} %get-tuple-element.156.refs_0_), channel_id=1, source_target_pairs={{0,2},{2,0},{4,6},{6,4},{8,10},{10,8},{12,14},{14,12},{16,18},{18,... | collective-permute-start | bytes 1327112 | tf_op jit(solution)/shard_map/ppermute | solution.py:609
  145.5 10.1 %collective-permute-start.35 = (bf16[2,2,4,72,384]{4,3,2,1,0:T(8,128)(2,1)S(1)}, bf16[2,2,4,72,384]{4,3,2,1,0:T(8,128)(2,1)S(1)}, u32[]{:S(2)}, u32[]{:S(2)}) collective-permute-start(bf16[2,2,4,72,384]{4,3,2,1,0:T(8,128)(2,1)S(1)} %get-tuple-element.158.refs_0_.refs_2_), channel_id=1, source_target_pairs={{0,2},{2,0},{4,6},{6,4},{8,10},{10,8},{12,14},{14,12},{16,18},{18,... | collective-permute-start | bytes 2654216 | tf_op jit(solution)/shard_map/ppermute | solution.py:609
  146.0 7.9 %collective-permute-start.32 = (bf16[2,2,80,384]{3,2,1,0:T(8,128)(2,1)S(1)}, bf16[2,2,80,384]{3,2,1,0:T(8,128)(2,1)S(1)}, u32[]{:S(2)}, u32[]{:S(2)}) collective-permute-start(bf16[2,2,80,384]{3,2,1,0:T(8,128)(2,1)S(1)} %get-tuple-element.155.refs_0_), channel_id=1, source_target_pairs={{0,8},{2,10},{4,12},{6,14},{8,0},{10,2},{12,4},{14,6},{16,24},{18,... | collective-permute-start | bytes 737288 | tf_op jit(solution)/shard_map/ppermute | solution.py:609
  147.3 8.4 %copy-start.8 = (f32[288,3072]{1,0:T(8,128)S(1)}, f32[288,3072]{1,0:T(8,128)}, u32[]{:S(2)}) copy-start(f32[288,3072]{1,0:T(8,128)} %refs_5_.6) | copy-start | bytes 10616836
  147.3 8.4 %copy-start.9 = (f32[288,3072]{1,0:T(8,128)S(1)}, f32[288,3072]{1,0:T(8,128)}, u32[]{:S(2)}) copy-start(f32[288,3072]{1,0:T(8,128)} %refs_6_.4) | copy-start | bytes 10616836
  155.5 6.7 %copy-start.16 = (f32[288,960]{1,0:T(8,128)S(1)}, f32[288,960]{1,0:T(8,128)}, u32[]{:S(2)}) copy-start(f32[288,960]{1,0:T(8,128)} %refs_4_.5) | copy-start | bytes 3317764
  155.5 6.7 %copy-start.17 = (f32[288,960]{1,0:T(8,128)S(1)}, f32[288,960]{1,0:T(8,128)}, u32[]{:S(2)}) copy-start(f32[288,960]{1,0:T(8,128)} %refs_6_.5) | copy-start | bytes 3317764
  155.5 6.7 %copy-start.18 = (f32[288,576]{1,0:T(8,128)S(1)}, f32[288,576]{1,0:T(8,128)}, u32[]{:S(2)}) copy-start(f32[288,576]{1,0:T(8,128)} %refs_5_.7) | copy-start | bytes 1990660
  155.5 6.7 %copy-start.19 = (f32[288,576]{1,0:T(8,128)S(1)}, f32[288,576]{1,0:T(8,128)}, u32[]{:S(2)}) copy-start(f32[288,576]{1,0:T(8,128)} %refs_7_.1) | copy-start | bytes 1990660
  155.6 6.6 %collective-permute-start.34 = (bf16[1,2,4,80,384]{4,3,2,1,0:T(8,128)(2,1)S(1)}, bf16[1,2,4,80,384]{4,3,2,1,0:T(8,128)(2,1)S(1)}, u32[]{:S(2)}, u32[]{:S(2)}) collective-permute-start(bf16[1,2,4,80,384]{4,3,2,1,0:T(8,128)(2,1)S(1)} %share_qkv_out.1.refs_7_.refs_0_), channel_id=1, source_target_pairs={{0,2},{2,0},{4,6},{6,4},{8,10},{10,8},{12,14},{14,12},{16,18},{18,... | collective-permute-start | bytes 1474568 | tf_op jit(solution)/shard_map/ppermute | solution.py:609
  (15 other events, 41.1 us)

commit v4 on v3

--- a/solution.py
+++ b/solution.py
@@ -79,38 +79,44 @@
 
 
 class Weight:
-    def __init__(self, shape, whole=None, own=None, parts=(), place=None, own_place=None):
-        self.shape, self.place, self.own_place = shape, place, own_place
-        self.parts = parts
-        self.arrays = [whole] if whole is not None else [own] + [p[0] for p in parts]
+    def __init__(self, shape, whole=None, own=(), parts=(), place=None):
+        self.shape, self.own, self.parts, self.place = shape, own, parts, place
+        self.arrays = [whole] if whole is not None else [a[0] for a in (*own, *parts)]
         self.split = whole is None
 
-    def scratch(self):
-        return [pltpu.VMEM(self.shape, BF16)] if self.split else []
-
-    def load(self, idx, refs, scratch):
+    def load(self, idx, refs, full):
         if not self.split:
             return refs[0]
-        full = scratch[0]
-        self.put(full, self.own_place(idx[0]), refs[0][...].astype(BF16))
-        for ref, (_, columns, (core, x)) in zip(refs[1:], self.parts):
-            value = ref[...] if columns is None else ref[:HALF, columns[0] : columns[1]]
-            self.put(full, self.place(1 - idx[0], idx[1] ^ core, idx[2] ^ x), value)
+        for ref, (_, place) in zip(refs, self.own):
+            self.put(full, place(idx[0]), ref[...].astype(BF16))
+        for ref, (_, (core, x, low)) in zip(refs[len(self.own) :], self.parts):
+            place = self.place(1 - idx[0], idx[1] ^ core, idx[2] ^ x, (idx[3] & 1) ^ low)
+            rows = ref.shape[0] // HALF * HALF
+            self.put(full, place, ref[:rows, :])
         return full
 
     def put(self, full, position, value):
-        rows, columns = slice(None), slice(None)
-        if value.shape[0] < self.shape[0]:
-            rows = pl.ds(pl.multiple_of(position[0], 16), value.shape[0])
-        if value.shape[1] < self.shape[1]:
-            columns = pl.ds(pl.multiple_of(position[1], LANES), value.shape[1])
-        full[rows, columns] = value
-
-
-def call(body, idx, arrays, weights, outs, scratch, flops, name, after=()):
+        where = []
+        for axis, tile in ((0, 16), (1, LANES)):
+            at, size = position[axis], value.shape[axis]
+            if size == self.shape[axis]:
+                where.append(slice(None))
+            elif isinstance(at, int):
+                where.append(slice(at, at + size))
+            else:
+                where.append(pl.ds(pl.multiple_of(at, tile), size))
+        full[tuple(where)] = value
+
+
+def call(body, idx, arrays, weights, outs, scratch, busy, name, after=(), hand_on=False):
     counts = [len(w.arrays) for w in weights]
     flat = list(arrays) + [a for w in weights for a in w.arrays]
-    weight_scratch = [w.scratch() for w in weights]
+    outs = list(outs)
+    split = [w for w in weights if w.split]
+    hand_on = hand_on and bool(split)
+    if hand_on:
+        outs += [sds(split[-1].shape, BF16)]
+    made = [pltpu.VMEM(w.shape, BF16) for w in (split[:-1] if hand_on else split)]
 
     def kernel(*refs):
         refs = list(refs)
@@ -121,15 +127,13 @@
         take(len(after))
         out_refs = take(len(outs))
         own_scratch = take(len(scratch))
-        scratch_refs = [take(len(s)) for s in weight_scratch]
+        fulls = take(len(made)) + ([out_refs.pop()] if hand_on else [])
         loads = [
-            functools.partial(w.load, idx_ref, r, s)
-            for w, r, s in zip(weights, weight_refs, scratch_refs)
+            functools.partial(w.load, idx_ref, r, fulls.pop(0) if w.split else None)
+            for w, r in zip(weights, weight_refs)
         ]
         body(idx_ref, array_refs, loads, out_refs, own_scratch)
 
-    moved = sum(a.size * a.dtype.itemsize for a in flat)
-    moved += sum(o.size * o.dtype.itemsize for o in outs)
     return pl.pallas_call(
         kernel,
         out_shape=tuple(outs),
@@ -137,11 +141,15 @@
         + [pl.BlockSpec(memory_space=pltpu.VMEM)] * len(flat)
         + [pl.BlockSpec(memory_space=pl.ANY)] * len(after),
         out_specs=tuple([pl.BlockSpec(memory_space=pltpu.VMEM)] * len(outs)),
-        scratch_shapes=list(scratch) + [s for group in weight_scratch for s in group],
+        scratch_shapes=list(scratch) + made,
         compiler_params=pltpu.CompilerParams(vmem_limit_bytes=VMEM_LIMIT),
-        cost_estimate=pl.CostEstimate(flops=flops, bytes_accessed=moved, transcendentals=0),
+        cost_estimate=busy_for(busy),
         name=name,
     )(idx, *flat, *after)
+
+
+def busy_for(microseconds):
+    return pl.CostEstimate(flops=int(microseconds * 1e9), bytes_accessed=0, transcendentals=0)
 
 
 def sds(shape, dtype):
@@ -195,43 +203,78 @@
     return exponent / jnp.sum(exponent, axis=-1, keepdims=True)
 
 
-def pack_weights(idx, w_qkv, w_out, w_gate_up, down_t, norm_gains):
-    width = w_out.shape[1]
-
-    def kernel(idx_ref, q_ref, o_ref, g_ref, d_ref, gains_ref, qo_out, g_out, d_out):
-        g_out[...] = g_ref[...].astype(BF16)
-        qo_out[:HALF, :QKV] = q_ref[...].astype(BF16)
-        qo_out[:HALF, QKV:] = o_ref[...].astype(BF16)
-        qo_out[HALF:, :] = jnp.zeros((16, QKV + width), BF16)
-        qo_out[HALF : HALF + 2, : gains_ref.shape[1]] = gains_ref[...].astype(BF16)
-        d_out[...] = d_ref[...].astype(BF16)
-
-    outs = (
-        sds((HALF + 16, QKV + width), BF16),
-        sds((HALF, FF), BF16),
-        sds((2 * HALF, down_t.shape[1]), BF16),
-    )
+def pack_kernel(body, idx, sources, places, outs, name, after=()):
+    windows = [shape for shape, _ in places]
+
+    def kernel(idx_ref, *refs):
+        sources_in, refs = refs[: len(sources)], refs[len(sources) + len(after) :]
+        out_refs, buffers, sem = refs[: len(outs)], refs[len(outs) : -1], refs[-1]
+        copies = []
+        for i, (source, (shape, place)) in enumerate(zip(sources_in, places)):
+            where = []
+            for axis, tile in ((0, 8), (1, LANES)):
+                if shape[axis] == source.shape[axis]:
+                    where.append(slice(None))
+                else:
+                    where.append(pl.ds(pl.multiple_of(place(idx_ref)[axis], tile), shape[axis]))
+            copies.append(pltpu.make_async_copy(source.at[tuple(where)], buffers[i], sem.at[i]))
+        for copy in copies:
+            copy.start()
+        for copy in copies:
+            copy.wait()
+        body(idx_ref, buffers, out_refs)
+
     return pl.pallas_call(
         kernel,
-        grid_spec=pltpu.PrefetchScalarGridSpec(
-            num_scalar_prefetch=1,
-            grid=(1,),
-            in_specs=[
-                pl.BlockSpec((HALF, QKV), lambda t, i: (i[1], 0)),
-                pl.BlockSpec((HALF, width), lambda t, i: (i[1], 0)),
-                pl.BlockSpec((HALF, FF), lambda t, i: (i[1], i[2])),
-                pl.BlockSpec((2 * HALF, down_t.shape[1]), lambda t, i: (i[1], 0)),
-                pl.BlockSpec(norm_gains.shape, lambda t, i: (0, 0)),
-            ],
-            out_specs=tuple(pl.BlockSpec(o.shape, lambda t, i: (0, 0)) for o in outs),
-        ),
-        out_shape=outs,
+        out_shape=tuple(outs),
+        in_specs=[pl.BlockSpec(memory_space=pltpu.SMEM)]
+        + [pl.BlockSpec(memory_space=pltpu.HBM)] * len(sources)
+        + [pl.BlockSpec(memory_space=pl.ANY)] * len(after),
+        out_specs=tuple([pl.BlockSpec(memory_space=pltpu.VMEM)] * len(outs)),
+        scratch_shapes=[pltpu.VMEM(w, F32) for w in windows]
+        + [pltpu.SemaphoreType.DMA((len(sources),))],
         compiler_params=pltpu.CompilerParams(vmem_limit_bytes=VMEM_LIMIT),
-        name="pack_weights",
-    )(idx, w_qkv, w_out, w_gate_up, down_t, norm_gains)
-
-
-def attention_forward(idx, tokens_t, segments, frequency, gains, w_qkv):
+        cost_estimate=busy_for(10),
+        name=name,
+    )(idx, *sources, *after)
+
+
+def cast_out(idx_ref, buffers, outs):
+    outs[0][...] = buffers[0][...].astype(BF16)
+
+
+def pack_gate_up(idx, w_gate_up):
+    window = ((HALF, FF), lambda i: (i[1] * HALF, i[2] * FF))
+    return pack_kernel(
+        cast_out, idx, [w_gate_up], [window], [sds((HALF, FF), BF16)], "pack_gate_up"
+    )[0]
+
+
+def pack_down(idx, down_t, after):
+    shape = (HALF, down_t.shape[1])
+    window = (shape, lambda i: ((i[1] * 2 + (i[3] & 1)) * HALF, 0))
+    return pack_kernel(cast_out, idx, [down_t], [window], [sds(shape, BF16)], "pack_down", after)[0]
+
+
+def pack_qkv_out(idx, w_qkv, w_out, norm_gains, after):
+    columns = (QKV + w_out.shape[1]) // 2
+    windows = [((HALF, m.shape[1]), lambda i: (i[1] * HALF, 0)) for m in (w_qkv, w_out)]
+    windows.append((norm_gains.shape, lambda i: (0, 0)))
+
+    def body(idx_ref, buffers, outs):
+        q_ref, o_ref, gains_ref = buffers
+        both = jnp.concatenate([q_ref[:, columns:], o_ref[...]], axis=1)
+        outs[0][:HALF, :] = jnp.where((idx_ref[3] & 1) == 0, q_ref[:, :columns], both).astype(BF16)
+        outs[0][HALF:, :] = jnp.zeros((16, columns), BF16)
+        outs[0][HALF : HALF + 2, : gains_ref.shape[1]] = gains_ref[...].astype(BF16)
+
+    outs = [sds((HALF + 16, columns), BF16)]
+    return pack_kernel(
+        body, idx, [w_qkv, w_out, norm_gains], windows, outs, "pack_qkv_out", after
+    )[0]
+
+
+def attention_forward(idx, tokens_t, segments, frequency, gains, w_qkv_out):
     width, seq_length = tokens_t.shape
     split_gains = len(gains) > 1
 
@@ -263,7 +306,7 @@
         allowed = jnp.concatenate([allowed] * GROUP, axis=0) > 0.5
         x = x_ref[...].astype(F32).T
         h1 = (x * norm_scale(x) * gains_ref[0:1, :]).astype(BF16)
-        projected = dot(h1, loads[0]()[...])
+        projected = dot(h1, loads[0]()[:, :QKV])
         for start in range(0, ROPED, LANES):
             block = projected[:, start : start + LANES]
             qkv_ref[:, start : start + LANES] = rotate_block(block, cosine, sine).astype(BF16)
@@ -285,21 +328,22 @@
         body,
         idx,
         [tokens_t, segments, frequency, *gains],
-        [w_qkv],
+        [w_qkv_out],
         outs,
         [],
-        2 * 128 * 576 * 960,
+        10,
         "attention",
-    )
-
-
-def feed_forward(idx, tokens_t, attended, gains, cotangent_t, w_out, w_gate_up, pieces, after):
+        hand_on=True,
+    )
+
+
+def feed_forward(idx, tokens_t, attended, gains, cotangent_t, w_qkv_out, w_gate_up, pieces, after):
     width, seq_length = tokens_t.shape
 
     def body(idx_ref, arrays, loads, outs, scratch):
         x_ref, o_ref, gains_ref, y_ref = arrays
         u_ref, h2_ref, ab_ref, z_ref = outs[:4]
-        u = x_ref[...].astype(F32).T + dot(o_ref[...], loads[0]()[...])
+        u = x_ref[...].astype(F32).T + dot(o_ref[...], loads[0]()[:, QKV:])
         u_ref[...] = u
         h2 = (u * norm_scale(u) * gains_ref[1:2, :]).astype(BF16)
         h2_ref[...] = h2
@@ -327,12 +371,13 @@
         body,
         idx,
         [tokens_t, attended, gains, cotangent_t],
-        [w_out, w_gate_up],
+        [w_qkv_out, w_gate_up],
         outs,
         scratch,
-        2 * 128 * 576 * 5200,
+        20,
         "feed_forward",
         after,
+        True,
     )
 
 
@@ -366,12 +411,12 @@
         [down_t],
         outs,
         scratch,
-        2 * 128 * 576 * 6200,
+        20,
         "feed_back",
     )
 
 
-def middle_back(idx, cotangent_t, middle, gated, gains, w_gate_up, w_out, after):
+def middle_back(idx, cotangent_t, middle, gated, gains, w_gate_up, w_qkv_out, after):
     width, seq_length = cotangent_t.shape
 
     def body(idx_ref, arrays, loads, outs, scratch):
@@ -386,17 +431,17 @@
             grad_normed * gains_ref[1:2, :], normed, scale_two
         )
         gu_ref[...] = gu
-        go_ref[...] = dot_right_t(gu.astype(BF16), loads[1]()[...]).astype(BF16)
+        go_ref[...] = dot_right_t(gu.astype(BF16), loads[1]()[:, QKV:]).astype(BF16)
 
     outs = [sds((seq_length, width), F32), sds((seq_length, width), BF16), sds((1, width), F32)]
     return call(
         body,
         idx,
         [cotangent_t, middle, gated, gains],
-        [w_gate_up, w_out],
+        [w_gate_up, w_qkv_out],
         outs,
         [],
-        2 * 128 * 576 * 3700,
+        20,
         "middle_back",
         after,
     )
@@ -447,7 +492,7 @@
         h1 = (normed * gains_ref[0:1, :]).astype(BF16)
         grad_qkv = dot_left_t(h1, gp_ref[...])
         grad_out = dot_left_t(o_ref[...], gu_low)
-        grad_normed = dot_right_t(gp_ref[...], loads[0]()[...])
+        grad_normed = dot_right_t(gp_ref[...], loads[0]()[:, :QKV])
         grad_gain_one = jnp.sum(grad_normed * normed, axis=0, keepdims=True)
         if pieces is None:
             outs[1][:, :QKV] = grad_qkv
@@ -486,7 +531,7 @@
         [w_qkv],
         outs,
         scratch,
-        2 * 128 * 576 * 4300,
+        20,
         "attention_back",
         after,
     )
@@ -503,6 +548,7 @@
         + [pl.BlockSpec(memory_space=pl.ANY)] * len(after),
         out_specs=tuple([pl.BlockSpec(memory_space=pltpu.VMEM)] * len(outs)),
         compiler_params=pltpu.CompilerParams(vmem_limit_bytes=VMEM_LIMIT),
+        cost_estimate=busy_for(4),
         name=name,
     )(*arrays, *after)
 
@@ -650,49 +696,38 @@
     frequency = ROPE_BASE ** (-(np.arange(half_size) * 2.0 / HEAD))
     frequency = jnp.asarray(np.tile(frequency, 4)[None], F32)
     if fast:
-        qo, gate_up, down = pack_weights(idx, w_qkv, w_out, w_gate_up, down_t, norm_gains)
+        gate_up = pack_gate_up(idx, w_gate_up)
         gate_up_near = over_y(gate_up)
-        qo_near = over_y(qo)
-        down_near = over_y(down)
+        qo_near = over_y(pack_qkv_out(idx, w_qkv, w_out, norm_gains, (gate_up,)))
+        down_near = over_y(pack_down(idx, down_t, (gate_up_near,)))
         gate_up_near_x = over_x(gate_up_near)
-        gate_up_parts = [
-            (gate_up_near, None, (0, 0)),
-            (gate_up_near_x, None, (0, 1)),
-            (over_core(gate_up_near), None, (1, 0)),
-            (over_core(gate_up_near_x), None, (1, 1)),
-        ]
-        qo_far = over_core(qo_near)
+        gate_up_far, gate_up_far_x = over_core(gate_up_near), over_core(gate_up_near_x)
+        qo_near_low = over_z_low(qo_near)
+        qo_far, qo_far_low = over_core(qo_near), over_core(qo_near_low)
         gains = (norm_gains, qo_near)
-        by_rows = lambda o, c, x: (o * rows + c * HALF, 0)
         own_rows = lambda o: (o * rows, 0)
-        rels = ((0, 0), (1, 0))
-        mat_qkv = Weight(
-            (width, QKV),
-            own=w_qkv,
-            parts=[(a, (0, QKV), r) for a, r in zip((qo_near, qo_far), rels)],
-            place=by_rows,
-            own_place=own_rows,
-        )
-        mat_out = Weight(
-            (width, width),
-            own=w_out,
-            parts=[(a, (QKV, QKV + width), r) for a, r in zip((qo_near, qo_far), rels)],
-            place=by_rows,
-            own_place=own_rows,
+        own_rows_out = lambda o: (o * rows, QKV)
+        mat_qkv_out = Weight(
+            (width, QKV + width),
+            own=[(w_qkv, own_rows), (w_out, own_rows_out)],
+            parts=[
+                (qo_near, (0, 0, 0)),
+                (qo_near_low, (0, 0, 1)),
+                (qo_far, (1, 0, 0)),
+                (qo_far_low, (1, 0, 1)),
+            ],
+            place=lambda o, c, x, low: (o * rows + c * HALF, low * ((QKV + width) // 2)),
         )
         mat_gate_up = Weight(
             (width, 2 * FF),
-            own=w_gate_up,
-            parts=gate_up_parts,
-            place=lambda o, c, x: (o * rows + c * HALF, x * FF),
-            own_place=own_rows,
-        )
-        mat_down = Weight(
-            (width, FF),
-            own=down_t,
-            parts=(),
-            place=lambda o, c, x: (c * 2 * HALF, o * down_rows),
-            own_place=lambda o: (0, o * down_rows),
+            own=[(w_gate_up, own_rows)],
+            parts=[
+                (gate_up_near, (0, 0, 0)),
+                (gate_up_near_x, (0, 1, 0)),
+                (gate_up_far, (1, 0, 0)),
+                (gate_up_far_x, (1, 1, 0)),
+            ],
+            place=lambda o, c, x, low: (o * rows + c * HALF, x * FF),
         )
         cut_qkv_out = Pieces(lambda o, c, x, z, p: (o * 4 + c * 2 + x, z), extra=8)
         cut_gate_up = Pieces(lambda o, c, x, z, p: (o * 4 + c * 2 + p, x * 4 + z), parts=2)
@@ -705,25 +740,44 @@
             lax.all_gather(m.astype(BF16), "shard", axis=0, tiled=True)
             for m in (w_qkv, w_out, w_gate_up, w_down)
         ]
-        mat_qkv, mat_out, mat_gate_up, mat_down = [
-            Weight(m.shape, whole=m) for m in (mat_qkv, mat_out, mat_gate_up, mat_down.T)
+        mat_qkv_out, mat_gate_up, mat_down = [
+            Weight(m.shape, whole=m)
+            for m in (jnp.concatenate([mat_qkv, mat_out], axis=1), mat_gate_up, mat_down.T)
         ]
         cut_qkv_out = cut_gate_up = cut_down = None
 
-    qkv, attended, *tables, gains = attention_forward(idx, x_t, segments, frequency, gains, mat_qkv)
+    qkv, attended, *tables, gains, whole = attention_forward(
+        idx, x_t, segments, frequency, gains, mat_qkv_out
+    ) + (() if fast else (None,))
     after = ()
     if fast:
+        mat_qkv_out = Weight(whole.shape, whole=whole)
 
         def pass_on(ins, outs):
             outs[0][...] = ins[0][...]
 
-        (down_near,) = step(pass_on, [down_near], [sds(down_near.shape, BF16)], "pass_on", (attended,))
-        mat_down.parts = [(down_near, None, (0, 0)), (over_core(down_near), None, (1, 0))]
-        mat_down.arrays = [down_t] + [p[0] for p in mat_down.parts]
+        (down_near,) = step(
+            pass_on, [down_near], [sds(down_near.shape, BF16)], "pass_on", (attended,)
+        )
+        down_near_low = over_z_low(down_near)
         after = (down_near,)
     middle, normed_low, ab, hidden, *grad_down = feed_forward(
-        idx, x_t, attended, gains, y_t, mat_out, mat_gate_up, cut_down, after
-    )
+        idx, x_t, attended, gains, y_t, mat_qkv_out, mat_gate_up, cut_down, after
+    )
+    if fast:
+        whole = grad_down.pop()
+        mat_gate_up = Weight(whole.shape, whole=whole)
+        mat_down = Weight(
+            (width, FF),
+            own=[(down_t, lambda o: (0, o * down_rows))],
+            parts=[
+                (down_near, (0, 0, 0)),
+                (down_near_low, (0, 0, 1)),
+                (over_core(down_near), (1, 0, 0)),
+                (over_core(down_near_low), (1, 0, 1)),
+            ],
+            place=lambda o, c, x, low: ((c * 2 + low) * HALF, o * down_rows),
+        )
     if fast:
         arrived_down = over_core(grad_down[0])
     gated, output, *grad_gate_up = feed_back(
@@ -738,7 +792,7 @@
         arrived_down = over_y(send)
         after = (keep_down,)
     grad_middle, grad_attended, gain_two = middle_back(
-        idx, y_t, middle, gated, gains, mat_gate_up, mat_out, after
+        idx, y_t, middle, gated, gains, mat_gate_up, mat_qkv_out, after
     )
     if fast:
         halves = [
@@ -760,7 +814,7 @@
         attended,
         tables,
         gains,
-        mat_qkv,
+        mat_qkv_out,
         cut_qkv_out,
         after,
     )
@@ -790,22 +844,22 @@
         (send_up, keep_up), (send_low, keep_low) = add_step(
             [
                 (cut(keep_up, 2, 2, 2), cut(arrived_up, 2, 2, 2), 1),
-                (cut(keep_low, 2, 2, 2), cut(arrived_low, 2, 2, 2), 0),
+                (cut(keep_low, 2, 2, 2), cut(arrived_low, 2, 2, 2), 1),
             ],
             "up_x_low_z",
             (keep_qkv_out,),
         )
-        arrived_up, arrived_low = over_z_low(send_up), over_y(send_low)
+        arrived_up, arrived_low = over_z_low(send_up), over_x(send_low)
         (send, keep_down), (send_up, keep_up), (send_low, keep_low) = add_step(
             [
                 (cut(keep_down, 2, 2), cut(arrived_down, 2, 2), 0),
                 (keep_up, arrived_up, 0),
                 (keep_low, arrived_low, 0),
             ],
-            "down_x_up_z_low_y",
+            "down_x_up_z_low_x",
             (keep_up,),
         )
-        arrived_down, arrived_up, arrived_low = over_z_low(send), over_y(send_up), over_x(send_low)
+        arrived_down, arrived_up, arrived_low = over_z_low(send), over_y(send_up), over_y(send_low)
         ((send, keep_qkv_out),) = add_step(
             [(cut(keep_qkv_out, 2, 4), cut(arrived_qkv_out, 2, 4), 0)], "qkv_out_y", (keep_down,)
         )
@@ -824,7 +878,7 @@
             last_sums,
             [keep_down, arrived_down, keep_up, arrived_up, keep_low, arrived_low],
             [sds((3, *piece), BF16), sds((3, *piece), F32)],
-            "down_z_up_y_low_x",
+            "down_z_up_y_low_y",
             (keep_qkv_out,),
         )
         arrived = over_z_high(send)

time: 169 us -> 162 us (0.959)
  waiting for transfers between devices: 85.7 us -> 73.1 us
  starting transfers between devices: 35.1 us -> 40.8 us
  local copies, waits for them, and re-layouts: 12.3 us -> 10.5 us
    ppermute x36 -> x40, waiting for transfers between devices: 85.7 us -> 73.1 us  [swap(): return lax.ppermute(values, axis, [(i, i ^ mask) for i in range(size)])]
    ppermute x36 -> x40, starting transfers between devices: 35.1 us -> 40.8 us  [swap(): return lax.ppermute(values, axis, [(i, i ^ mask) for i in range(size)])]
    unnamed x54 -> x52, local copies, waits for them, and re-layouts: 11.9 us -> 10.1 us
    pallas_call x1 -> x3, Pallas kernels: 0.71 us -> 2.47 us  [pack_kernel(): pl.pallas_call(kernel, out_shape=tuple(outs), in_specs=[pl.BlockSpec(memo...]
  transfers between devices with their start and end apart: 36 -> 40, of which waited for: 19 -> 21; matrix products, arithmetic and copies ran while one was open for 0% -> 0% of each run, Pallas kernels for 12% -> 15%
where the time goes in v4:
time: 162 us
  waiting for transfers between devices  73.1 us (45%)
  starting transfers between devices  40.8 us (25%)
  Pallas kernels  36.1 us (22%)
  local copies, waits for them, and re-layouts  10.5 us (6%)
    ppermute x40, waiting for transfers between devices, swap(): return lax.ppermute(values, axis, [(i, i ^ mask) for i in range(size)])  73.1 us
    ppermute x40, starting transfers between devices, swap(): return lax.ppermute(values, axis, [(i, i ^ mask) for i in range(size)])  40.8 us
    pallas_call x5, Pallas kernels, call(): pl.pallas_call(kernel, out_shape=tuple(outs), in_specs=[pl.BlockSpec(memo...  16.9 us
    pallas_call x3, Pallas kernels, update_state(): pl.pallas_call(kernel, grid_spec=pltpu.PrefetchScalarGridSpec(num_scalar_...  15 us
    unnamed x52, local copies, waits for them, and re-layouts  10.1 us
  transfers between devices with their start and end apart: 40, of which 21 were waited for; matrix products, arithmetic and copies ran while one was open for 0% of the time, Pallas kernels for 15%

profile of v4, /device:TPU:0, one launch (start us, length us, event | category | flops | bytes accessed | tf_op | source)
XLA Modules:
  0.0 161.9 jit_solution(18070891715887292212)
XLA Ops:
  0.7 2.0 %copy-done = f32[288,3072]{1,0:T(8,128)S(1)} copy-done((f32[288,3072]{1,0:T(8,128)S(1)}, f32[288,3072]{1,0:T(8,128)}, u32[]{:S(2)}) %copy-start) | copy-done | bytes 3538968
  4.2 1.0 pack_qkv_out.1
  5.2 3.0 %collective-permute-start = (bf16[160,768]{1,0:T(8,128)(2,1)S(1)}, bf16[160,768]{1,0:T(8,128)(2,1)S(1)}, u32[]{:S(2)}, u32[]{:S(2)}) collective-permute-start(bf16[160,768]{1,0:T(8,128)(2,1)S(1)} %pack_qkv_out.1), channel_id=1, source_target_pairs={{0,1},{1,0},{2,3},{3,2},{4,5},{5,4},{6,7},{7,6},{8,9},{9,8},{10,11... | collective-permute-start | bytes 737288 | tf_op jit(solution)/shard_map/ppermute | solution.py:655
  8.3 6.7 %collective-permute-done.refs_5_.refs_8_ = bf16[160,768]{1,0:T(8,128)(2,1)S(1)} collective-permute-done((bf16[160,768]{1,0:T(8,128)(2,1)S(1)}, bf16[160,768]{1,0:T(8,128)(2,1)S(1)}, u32[]{:S(2)}, u32[]{:S(2)}) %collective-permute-start) | collective-permute-done | bytes 245792 | tf_op jit(solution)/shard_map/ppermute | solution.py:655
  15.0 2.1 %collective-permute-start.1 = (bf16[160,768]{1,0:T(8,128)(2,1)S(1)}, bf16[160,768]{1,0:T(8,128)(2,1)S(1)}, u32[]{:S(2)}, u32[]{:S(2)}) collective-permute-start(bf16[160,768]{1,0:T(8,128)(2,1)S(1)} %collective-permute-done.refs_5_.refs_8_), channel_id=1, source_target_pairs={{0,8},{2,10},{4,12},{6,14},{8,0},{10,2},{12,4},{14,6},{16,24},{18,... | collective-permute-start | bytes 737288 | tf_op jit(solution)/shard_map/ppermute | solution.py:655
  17.1 4.2 %collective-permute-done.1.refs_9_ = bf16[160,768]{1,0:T(8,128)(2,1)S(1)} collective-permute-done((bf16[160,768]{1,0:T(8,128)(2,1)S(1)}, bf16[160,768]{1,0:T(8,128)(2,1)S(1)}, u32[]{:S(2)}, u32[]{:S(2)}) %collective-permute-start.1) | collective-permute-done | bytes 245792 | tf_op jit(solution)/shard_map/ppermute | solution.py:655
  21.3 2.3 %collective-permute-done.4.refs_1_.refs_7_ = bf16[144,1536]{1,0:T(8,128)(2,1)S(1)} collective-permute-done((bf16[144,1536]{1,0:T(8,128)(2,1)S(1)}, bf16[144,1536]{1,0:T(8,128)(2,1)S(1)}, u32[]{:S(2)}, u32[]{:S(2)}) %collective-permute-start.4) | collective-permute-done | bytes 442400 | tf_op jit(solution)/shard_map/ppermute | solution.py:655
  24.5 1.8 %collective-permute-start.8 = (bf16[144,768]{1,0:T(8,128)(2,1)S(1)}, bf16[144,768]{1,0:T(8,128)(2,1)S(1)}, u32[]{:S(2)}, u32[]{:S(2)}) collective-permute-start(bf16[144,768]{1,0:T(8,128)(2,1)S(1)} %pack_down.1), channel_id=1, source_target_pairs={{0,1},{1,0},{2,3},{3,2},{4,5},{5,4},{6,7},{7,6},{8,9},{9,8},{10,11... | collective-permute-start | bytes 663560 | tf_op jit(solution)/shard_map/ppermute | solution.py:655
  26.3 1.5 collective-permute-start.5
  27.9 2.5 %attention.1 = (bf16[128,960]{1,0:T(8,128)(2,1)S(1)}, bf16[128,576]{1,0:T(8,128)(2,1)S(1)}, f32[128,128]{1,0:T(8,128)S(1)}, f32[128,128]{1,0:T(8,128)S(1)}, f32[...) custom-call(s32[4]{0:T(128)S(1)} %pad_add_fusion.idx_ref.refs_0_, ...), custom_call_target="tpu_custom_call" | custom-call | flops 10000000000 | tf_op jit(solution)/shard_map/attention/pallas_call | solution.py:137
  30.4 8.5 %collective-permute-done.5.refs_8_ = bf16[144,1536]{1,0:T(8,128)(2,1)S(1)} collective-permute-done((bf16[144,1536]{1,0:T(8,128)(2,1)S(1)}, bf16[144,1536]{1,0:T(8,128)(2,1)S(1)}, u32[]{:S(2)}, u32[]{:S(2)}) %collective-permute-start.5) | collective-permute-done | bytes 442400 | tf_op jit(solution)/shard_map/ppermute | solution.py:655
  39.0 1.6 %collective-permute-start.9 = (bf16[144,768]{1,0:T(8,128)(2,1)S(1)}, bf16[144,768]{1,0:T(8,128)(2,1)S(1)}, u32[]{:S(2)}, u32[]{:S(2)}) collective-permute-start(bf16[144,768]{1,0:T(8,128)(2,1)S(1)} %pass_on.1.refs_11_.refs_7_), channel_id=1, source_target_pairs={{0,8},{2,10},{4,12},{6,14},{8,0},{10,2},{12,4},{14,6},{16,24},{18,... | collective-permute-start | bytes 663560 | tf_op jit(solution)/shard_map/ppermute | solution.py:655
  40.8 6.0 %collective-permute-done.9.refs_8_ = bf16[144,768]{1,0:T(8,128)(2,1)S(1)} collective-permute-done((bf16[144,768]{1,0:T(8,128)(2,1)S(1)}, bf16[144,768]{1,0:T(8,128)(2,1)S(1)}, u32[]{:S(2)}, u32[]{:S(2)}) %collective-permute-start.9) | collective-permute-done | bytes 221216 | tf_op jit(solution)/shard_map/ppermute | solution.py:655
  46.9 2.8 %feed_forward.1 = (f32[128,576]{1,0:T(8,128)S(1)}, bf16[128,576]{1,0:T(8,128)(2,1)S(1)}, f32[128,3072]{1,0:T(8,128)S(1)}, bf16[128,1536]{1,0:T(8,128)(2,1)S(1)},...) custom-call(s32[4]{0:T(128)S(1)} %pad_add_fusion.idx_ref.refs_0_, ...), custom_call_target="tpu_custom_call" | custom-call | flops 20000000000 | tf_op jit(solution)/shard_map/feed_forward/pallas_call | solution.py:137
  50.3 3.8 %feed_back.1 = (bf16[128,3072]{1,0:T(8,128)(2,1)S(1)}, bf16[576,128]{1,0:T(8,128)(2,1)}, bf16[2,2,8,72,384]{4,3,2,1,0:T(8,128)(2,1)S(1)}, bf16[2,2,8,72,384]{4,3,2,1,0:T(8,128)(2,1)S(1)}) custom-call(s32[4]{0:T(128)S(1)} %pad_add_fusion.idx_ref.refs_0_, f32[128,3072]{1,0:T(8,128)S(1)} %get-tuple-element.97.refs_1_, ...), custom_call_target="tpu_custom_call" | custom-call | flops 20000000000 | tf_op jit(solution)/shard_map/feed_back/pallas_call | solution.py:137
  54.5 2.7 %middle_back.1 = (f32[128,576]{1,0:T(8,128)S(1)}, bf16[128,576]{1,0:T(8,128)(2,1)S(1)}, f32[1,576]{1,0:T(1,128)S(1)}) custom-call(s32[4]{0:T(128)S(1)} %pad_add_fusion.idx_ref.refs_0_, bf16[576,128]{1,0:T(8,128)(2,1)S(1)} %bitcast.62, f32[128,576]{1,0:T(8,128)S(1)} %get-tuple-element.100.refs_4_.refs_2_, ...), custom_call_target="tpu_custom_call" | custom-call | flops 20000000000 | tf_op jit(solution)/shard_map/middle_back/pallas_call | solution.py:137
  58.3 5.1 %attention_back.1 = (bf16[576,128]{1,0:T(8,128)(2,1)}, bf16[1,2,8,80,384]{4,3,2,1,0:T(8,128)(2,1)S(1)}, bf16[1,2,8,80,384]{4,3,2,1,0:T(8,128)(2,1)S(1)}) custom-call(s32[4]{0:T(128)S(1)} %pad_add_fusion.idx_ref.refs_0_, bf16[576,128]{1,0:T(8,128)(2,1)S(1)} %bitcast.65, f32[128,576]{1,0:T(8,128)S(1)} %get-tuple-element.107.refs_4_.refs_2_, ...), custom_call_target="tpu_custom_call" | custom-call | flops 20000000000 | tf_op jit(solution)/shard_map/attention_back/pallas_call | solution.py:137
  63.9 1.7 %collective-permute-start.16 = (bf16[2,4,72,384]{3,2,1,0:T(8,128)(2,1)S(1)}, bf16[2,4,72,384]{3,2,1,0:T(8,128)(2,1)S(1)}, u32[]{:S(2)}, u32[]{:S(2)}) collective-permute-start(bf16[2,4,72,384]{3,2,1,0:T(8,128)(2,1)S(1)} %get-tuple-element.121), channel_id=1, source_target_pairs={{0,4},{2,6},{4,0},{6,2},{8,12},{10,14},{12,8},{14,10},{16,20},{18,... | collective-permute-start | bytes 1327112 | tf_op jit(solution)/shard_map/ppermute | solution.py:655
  65.6 1.6 collective-permute-start.17
  67.1 8.9 %collective-permute-done.14 = bf16[8,72,384]{2,1,0:T(8,128)(2,1)S(1)} collective-permute-done((bf16[8,72,384]{2,1,0:T(8,128)(2,1)S(1)}, bf16[8,72,384]{2,1,0:T(8,128)(2,1)S(1)}, u32[]{:S(2)}, u32[]{:S(2)}) %collective-permute-start.14) | collective-permute-done | bytes 442400 | tf_op jit(solution)/shard_map/ppermute | solution.py:655
  77.0 1.6 collective-permute-start.15
  79.0 1.6 %collective-permute-start.19 = (bf16[2,2,72,384]{3,2,1,0:T(8,128)(2,1)S(1)}, bf16[2,2,72,384]{3,2,1,0:T(8,128)(2,1)S(1)}, u32[]{:S(2)}, u32[]{:S(2)}) collective-permute-start(bf16[2,2,72,384]{3,2,1,0:T(8,128)(2,1)S(1)} %get-tuple-element.128), channel_id=1, source_target_pairs={{0,8},{2,10},{4,12},{6,14},{8,0},{10,2},{12,4},{14,6},{16,24},{18,... | collective-permute-start | bytes 663560 | tf_op jit(solution)/shard_map/ppermute | solution.py:655
  81.7 3.7 %collective-permute-done.15 = bf16[4,72,384]{2,1,0:T(8,128)(2,1)S(1)} collective-permute-done((bf16[4,72,384]{2,1,0:T(8,128)(2,1)S(1)}, bf16[4,72,384]{2,1,0:T(8,128)(2,1)S(1)}, u32[]{:S(2)}, u32[]{:S(2)}) %collective-permute-start.15) | collective-permute-done | bytes 221216 | tf_op jit(solution)/shard_map/ppermute | solution.py:655
  85.7 3.0 %collective-permute-done.20.refs_5_ = bf16[2,2,72,384]{3,2,1,0:T(8,128)(2,1)S(1)} collective-permute-done((bf16[2,2,72,384]{3,2,1,0:T(8,128)(2,1)S(1)}, bf16[2,2,72,384]{3,2,1,0:T(8,128)(2,1)S(1)}, u32[]{:S(2)}, u32[]{:S(2)}) %collective-permute-start.20) | collective-permute-done | bytes 221216 | tf_op jit(solution)/shard_map/ppermute | solution.py:655
  88.8 1.6 %collective-permute-start.21 = (bf16[2,72,384]{2,1,0:T(8,128)(2,1)S(1)}, bf16[2,72,384]{2,1,0:T(8,128)(2,1)S(1)}, u32[]{:S(2)}, u32[]{:S(2)}) collective-permute-start(bf16[2,72,384]{2,1,0:T(8,128)(2,1)S(1)} %get-tuple-element.132), channel_id=1, source_target_pairs={{0,8},{2,10},{4,12},{6,14},{8,0},{10,2},{12,4},{14,6},{16,24},{18,... | collective-permute-start | bytes 331784 | tf_op jit(solution)/shard_map/ppermute | solution.py:655
  91.0 1.5 collective-permute-start.23
  92.5 2.0 %collective-permute-done.24 = bf16[8,80,384]{2,1,0:T(8,128)(2,1)S(1)} collective-permute-done((bf16[8,80,384]{2,1,0:T(8,128)(2,1)S(1)}, bf16[8,80,384]{2,1,0:T(8,128)(2,1)S(1)}, u32[]{:S(2)}, u32[]{:S(2)}) %collective-permute-start.24) | collective-permute-done | bytes 491552 | tf_op jit(solution)/shard_map/ppermute | solution.py:655
  94.6 1.5 collective-permute-start.26
  96.6 1.2 collective-permute-done.23.refs_5_
  97.8 2.7 %collective-permute-start.25 = (bf16[3,72,384]{2,1,0:T(8,128)(2,1)S(1)}, bf16[3,72,384]{2,1,0:T(8,128)(2,1)S(1)}, u32[]{:S(2)}, u32[]{:S(2)}) collective-permute-start(bf16[3,72,384]{2,1,0:T(8,128)(2,1)S(1)} %get-tuple-element.140), channel_id=1, source_target_pairs={{0,16},{2,18},{4,20},{6,22},{8,24},{10,26},{12,28},{14,30},{16,0},... | collective-permute-start | bytes 497672 | tf_op jit(solution)/shard_map/ppermute | solution.py:655
  101.4 5.6 %collective-permute-done.25.refs_1_ = bf16[3,72,384]{2,1,0:T(8,128)(2,1)S(1)} collective-permute-done((bf16[3,72,384]{2,1,0:T(8,128)(2,1)S(1)}, bf16[3,72,384]{2,1,0:T(8,128)(2,1)S(1)}, u32[]{:S(2)}, u32[]{:S(2)}) %collective-permute-start.25) | collective-permute-done | bytes 165920 | tf_op jit(solution)/shard_map/ppermute | solution.py:655
  108.6 2.5 %collective-permute-start.29 = (bf16[80,384]{1,0:T(8,128)(2,1)S(1)}, bf16[80,384]{1,0:T(8,128)(2,1)S(1)}, u32[]{:S(2)}, u32[]{:S(2)}) collective-permute-start(bf16[80,384]{1,0:T(8,128)(2,1)S(1)} %get-tuple-element.146), channel_id=1, source_target_pairs={{0,16},{2,18},{4,20},{6,22},{8,24},{10,26},{12,28},{14,30},{16,0},... | collective-permute-start | bytes 184328 | tf_op jit(solution)/shard_map/ppermute | solution.py:655
  111.1 7.2 %collective-permute-done.29.refs_3_ = bf16[80,384]{1,0:T(8,128)(2,1)S(1)} collective-permute-done((bf16[80,384]{1,0:T(8,128)(2,1)S(1)}, bf16[80,384]{1,0:T(8,128)(2,1)S(1)}, u32[]{:S(2)}, u32[]{:S(2)}) %collective-permute-start.29) | collective-permute-done | bytes 61472 | tf_op jit(solution)/shard_map/ppermute | solution.py:655
  118.3 1.6 collective-permute-start.31
  119.9 3.2 %collective-permute-start.32 = (bf16[80,384]{1,0:T(8,128)(2,1)S(1)}, bf16[80,384]{1,0:T(8,128)(2,1)S(1)}, u32[]{:S(2)}, u32[]{:S(2)}) collective-permute-start(bf16[80,384]{1,0:T(8,128)(2,1)S(1)} %get-tuple-element.149.refs_4_), channel_id=1, source_target_pairs={{0,16},{2,18},{4,20},{6,22},{8,24},{10,26},{12,28},{14,30},{16,0},... | collective-permute-start | bytes 184328 | tf_op jit(solution)/shard_map/ppermute | solution.py:655
  123.1 2.2 %collective-permute-done.32.refs_5_ = bf16[80,384]{1,0:T(8,128)(2,1)S(1)} collective-permute-done((bf16[80,384]{1,0:T(8,128)(2,1)S(1)}, bf16[80,384]{1,0:T(8,128)(2,1)S(1)}, u32[]{:S(2)}, u32[]{:S(2)}) %collective-permute-start.32) | collective-permute-done | bytes 61472 | tf_op jit(solution)/shard_map/ppermute | solution.py:655
  125.4 1.8 %collective-permute-start.34 = (bf16[2,2,2,72,384]{4,3,2,1,0:T(8,128)(2,1)S(1)}, bf16[2,2,2,72,384]{4,3,2,1,0:T(8,128)(2,1)S(1)}, u32[]{:S(2)}, u32[]{:S(2)}) collective-permute-start(bf16[2,2,2,72,384]{4,3,2,1,0:T(8,128)(2,1)S(1)} %get-tuple-element.151.refs_2_), channel_id=1, source_target_pairs={{0,8},{2,10},{4,12},{6,14},{8,0},{10,2},{12,4},{14,6},{16,24},{18,... | collective-permute-start | bytes 1327112 | tf_op jit(solution)/shard_map/ppermute | solution.py:655
  127.7 1.5 collective-permute-start.35
  129.2 5.3 %collective-permute-done.35.refs_5_ = bf16[2,80,384]{2,1,0:T(8,128)(2,1)S(1)} collective-permute-done((bf16[2,80,384]{2,1,0:T(8,128)(2,1)S(1)}, bf16[2,80,384]{2,1,0:T(8,128)(2,1)S(1)}, u32[]{:S(2)}, u32[]{:S(2)}) %collective-permute-start.35) | collective-permute-done | bytes 122912 | tf_op jit(solution)/shard_map/ppermute | solution.py:655
  135.6 1.6 collective-permute-start.36
  137.4 3.8 %update_down.1 = (f32[576,768]{1,0:T(8,128)}, f32[576,768]{1,0:T(8,128)}, f32[576,768]{1,0:T(8,128)}) custom-call(s32[4]{0:T(128)S(1)} %pad_add_fusion.idx_ref.refs_0_, bf16[1,2,4,72,384]{4,3,2,1,0:T(8,128)(2,1)S(1)} %get-tuple-element.154.refs_0_, bf16[1,2,4,72,384]{4,3,2,1,0:T(8,128)(2,1)S(1)} %collective-permute-done.37.refs_1_, f32[576,768]{1,0:T(8,128)S(1)} %bitcast.44, ...), custom_call_target="tpu_custom_call" | custom-call | bytes 10616832 | tf_op jit(solution)/shard_map/update_down/pallas_call | solution.py:634
  141.2 2.7 %collective-permute-done.36.refs_1_ = bf16[2,2,80,384]{3,2,1,0:T(8,128)(2,1)S(1)} collective-permute-done((bf16[2,2,80,384]{3,2,1,0:T(8,128)(2,1)S(1)}, bf16[2,2,80,384]{3,2,1,0:T(8,128)(2,1)S(1)}, u32[]{:S(2)}, u32[]{:S(2)}) %collective-permute-start.36) | collective-permute-done | bytes 245792 | tf_op jit(solution)/shard_map/ppermute | solution.py:655
  143.9 1.5 copy-done.20
  145.7 1.8 %copy-done.2 = f32[288,3072]{1,0:T(8,128)S(1)} copy-done((f32[288,3072]{1,0:T(8,128)S(1)}, f32[288,3072]{1,0:T(8,128)}, u32[]{:S(2)}) %copy-start.2) | copy-done | bytes 3538968
  147.4 1.1 copy-done.3
  148.5 6.5 %update_gate_up.1 = (f32[288,3072]{1,0:T(8,128)}, f32[288,3072]{1,0:T(8,128)}, f32[288,3072]{1,0:T(8,128)}) custom-call(s32[4]{0:T(128)S(1)} %pad_add_fusion.idx_ref.refs_0_, bf16[2,2,4,72,384]{4,3,2,1,0:T(8,128)(2,1)S(1)} %get-tuple-element.156.refs_0_.refs_2_, bf16[2,2,4,72,384]{4,3,2,1,0:T(8,128)(2,1)S(1)} %collective-permute-done.39.refs_1_.refs_3_, ...), custom_call_target="tpu_custom_call" | custom-call | bytes 21233664 | tf_op jit(solution)/shard_map/update_gate_up/pallas_call | solution.py:634
  155.0 2.0 %copy-done.4 = f32[288,3072]{1,0:T(8,128)S(1)} copy-done((f32[288,3072]{1,0:T(8,128)S(1)}, f32[288,3072]{1,0:T(8,128)}, u32[]{:S(2)}) %copy-start.4) | copy-done | bytes 3538968
  157.0 4.7 %update_qkv_out.1 = (f32[288,960]{1,0:T(8,128)}, f32[288,576]{1,0:T(8,128)}, f32[288,960]{1,0:T(8,128)}, f32[288,576]{1,0:T(8,128)}, f32[288,960]{1,0:T(8,128)},...) custom-call(s32[4]{0:T(128)S(1)} %pad_add_fusion.idx_ref.refs_0_, ...), custom_call_target="tpu_custom_call" | custom-call | bytes 10616832 | tf_op jit(solution)/shard_map/update_qkv_out/pallas_call | solution.py:634
  (113 shorter events, 13.7 us)
Async XLA Ops:
  4.2 19.5 %copy-start.5 = (f32[768,576]{0,1:T(8,128)S(1)}, f32[768,576]{0,1:T(8,128)}, u32[]{:S(2)}) copy-start(f32[768,576]{0,1:T(8,128)} %param.25) | copy-start | bytes 5308420
  5.2 9.8 %collective-permute-start = (bf16[160,768]{1,0:T(8,128)(2,1)S(1)}, bf16[160,768]{1,0:T(8,128)(2,1)S(1)}, u32[]{:S(2)}, u32[]{:S(2)}) collective-permute-start(bf16[160,768]{1,0:T(8,128)(2,1)S(1)} %pack_qkv_out.1), channel_id=1, source_target_pairs={{0,1},{1,0},{2,3},{3,2},{4,5},{5,4},{6,7},{7,6},{8,9},{9,8},{10,11... | collective-permute-start | bytes 737288 | tf_op jit(solution)/shard_map/ppermute | solution.py:655
  8.2 15.4 %collective-permute-start.4 = (bf16[144,1536]{1,0:T(8,128)(2,1)S(1)}, bf16[144,1536]{1,0:T(8,128)(2,1)S(1)}, u32[]{:S(2)}, u32[]{:S(2)}) collective-permute-start(bf16[144,1536]{1,0:T(8,128)(2,1)S(1)} %pack_gate_up.1.refs_3_), channel_id=1, source_target_pairs={{0,1},{1,0},{2,3},{3,2},{4,5},{5,4},{6,7},{7,6},{8,9},{9,8},{10,11... | collective-permute-start | bytes 1327112 | tf_op jit(solution)/shard_map/ppermute | solution.py:655
  15.0 6.3 %collective-permute-start.1 = (bf16[160,768]{1,0:T(8,128)(2,1)S(1)}, bf16[160,768]{1,0:T(8,128)(2,1)S(1)}, u32[]{:S(2)}, u32[]{:S(2)}) collective-permute-start(bf16[160,768]{1,0:T(8,128)(2,1)S(1)} %collective-permute-done.refs_5_.refs_8_), channel_id=1, source_target_pairs={{0,8},{2,10},{4,12},{6,14},{8,0},{10,2},{12,4},{14,6},{16,24},{18,... | collective-permute-start | bytes 737288 | tf_op jit(solution)/shard_map/ppermute | solution.py:655
  17.1 10.7 %collective-permute-start.2 = (bf16[160,768]{1,0:T(8,128)(2,1)S(1)}, bf16[160,768]{1,0:T(8,128)(2,1)S(1)}, u32[]{:S(2)}, u32[]{:S(2)}) collective-permute-start(bf16[160,768]{1,0:T(8,128)(2,1)S(1)} %collective-permute-done.refs_5_.refs_8_), channel_id=1, source_target_pairs={{0,2},{2,0},{4,6},{6,4},{8,10},{10,8},{12,14},{14,12},{16,18},{18,... | collective-permute-start | bytes 737288 | tf_op jit(solution)/shard_map/ppermute | solution.py:655
  21.3 6.5 %collective-permute-start.3 = (bf16[160,768]{1,0:T(8,128)(2,1)S(1)}, bf16[160,768]{1,0:T(8,128)(2,1)S(1)}, u32[]{:S(2)}, u32[]{:S(2)}) collective-permute-start(bf16[160,768]{1,0:T(8,128)(2,1)S(1)} %collective-permute-done.1.refs_9_), channel_id=1, source_target_pairs={{0,2},{2,0},{4,6},{6,4},{8,10},{10,8},{12,14},{14,12},{16,18},{18,... | collective-permute-start | bytes 737288 | tf_op jit(solution)/shard_map/ppermute | solution.py:655
  24.5 14.4 %collective-permute-start.8 = (bf16[144,768]{1,0:T(8,128)(2,1)S(1)}, bf16[144,768]{1,0:T(8,128)(2,1)S(1)}, u32[]{:S(2)}, u32[]{:S(2)}) collective-permute-start(bf16[144,768]{1,0:T(8,128)(2,1)S(1)} %pack_down.1), channel_id=1, source_target_pairs={{0,1},{1,0},{2,3},{3,2},{4,5},{5,4},{6,7},{7,6},{8,9},{9,8},{10,11... | collective-permute-start | bytes 663560 | tf_op jit(solution)/shard_map/ppermute | solution.py:655
  26.3 20.5 %collective-permute-start.6 = (bf16[144,1536]{1,0:T(8,128)(2,1)S(1)}, bf16[144,1536]{1,0:T(8,128)(2,1)S(1)}, u32[]{:S(2)}, u32[]{:S(2)}) collective-permute-start(bf16[144,1536]{1,0:T(8,128)(2,1)S(1)} %collective-permute-done.4.refs_1_.refs_7_), channel_id=1, source_target_pairs={{0,2},{2,0},{4,6},{6,4},{8,10},{10,8},{12,14},{14,12},{16,18},{18,... | collective-permute-start | bytes 1327112 | tf_op jit(solution)/shard_map/ppermute | solution.py:655
  26.3 12.6 %collective-permute-start.5 = (bf16[144,1536]{1,0:T(8,128)(2,1)S(1)}, bf16[144,1536]{1,0:T(8,128)(2,1)S(1)}, u32[]{:S(2)}, u32[]{:S(2)}) collective-permute-start(bf16[144,1536]{1,0:T(8,128)(2,1)S(1)} %collective-permute-done.4.refs_1_.refs_7_), channel_id=1, source_target_pairs={{0,4},{2,6},{4,0},{6,2},{8,12},{10,14},{12,8},{14,10},{16,20},{18,... | collective-permute-start | bytes 1327112 | tf_op jit(solution)/shard_map/ppermute | solution.py:655
  38.9 7.9 %collective-permute-start.7 = (bf16[144,1536]{1,0:T(8,128)(2,1)S(1)}, bf16[144,1536]{1,0:T(8,128)(2,1)S(1)}, u32[]{:S(2)}, u32[]{:S(2)}) collective-permute-start(bf16[144,1536]{1,0:T(8,128)(2,1)S(1)} %collective-permute-done.5.refs_8_), channel_id=1, source_target_pairs={{0,2},{2,0},{4,6},{6,4},{8,10},{10,8},{12,14},{14,12},{16,18},{18,... | collective-permute-start | bytes 1327112 | tf_op jit(solution)/shard_map/ppermute | solution.py:655
  39.0 7.9 %collective-permute-start.9 = (bf16[144,768]{1,0:T(8,128)(2,1)S(1)}, bf16[144,768]{1,0:T(8,128)(2,1)S(1)}, u32[]{:S(2)}, u32[]{:S(2)}) collective-permute-start(bf16[144,768]{1,0:T(8,128)(2,1)S(1)} %pass_on.1.refs_11_.refs_7_), channel_id=1, source_target_pairs={{0,8},{2,10},{4,12},{6,14},{8,0},{10,2},{12,4},{14,6},{16,24},{18,... | collective-permute-start | bytes 663560 | tf_op jit(solution)/shard_map/ppermute | solution.py:655
  40.6 9.7 %collective-permute-start.10 = (bf16[144,768]{1,0:T(8,128)(2,1)S(1)}, bf16[144,768]{1,0:T(8,128)(2,1)S(1)}, u32[]{:S(2)}, u32[]{:S(2)}) collective-permute-start(bf16[144,768]{1,0:T(8,128)(2,1)S(1)} %pass_on.1.refs_11_.refs_7_), channel_id=1, source_target_pairs={{0,2},{2,0},{4,6},{6,4},{8,10},{10,8},{12,14},{14,12},{16,18},{18,... | collective-permute-start | bytes 663560 | tf_op jit(solution)/shard_map/ppermute | solution.py:655
  46.8 3.4 %collective-permute-start.11 = (bf16[144,768]{1,0:T(8,128)(2,1)S(1)}, bf16[144,768]{1,0:T(8,128)(2,1)S(1)}, u32[]{:S(2)}, u32[]{:S(2)}) collective-permute-start(bf16[144,768]{1,0:T(8,128)(2,1)S(1)} %collective-permute-done.9.refs_8_), channel_id=1, source_target_pairs={{0,2},{2,0},{4,6},{6,4},{8,10},{10,8},{12,14},{14,12},{16,18},{18,... | collective-permute-start | bytes 663560 | tf_op jit(solution)/shard_map/ppermute | solution.py:655
  49.7 4.6 %collective-permute-start.12 = (bf16[1,2,8,72,384]{4,3,2,1,0:T(8,128)(2,1)S(1)}, bf16[1,2,8,72,384]{4,3,2,1,0:T(8,128)(2,1)S(1)}, u32[]{:S(2)}, u32[]{:S(2)}) collective-permute-start(bf16[1,2,8,72,384]{4,3,2,1,0:T(8,128)(2,1)S(1)} %get-tuple-element.105), channel_id=1, source_target_pairs={{0,2},{2,0},{4,6},{6,4},{8,10},{10,8},{12,14},{14,12},{16,18},{18,... | collective-permute-start | bytes 2654216 | tf_op jit(solution)/shard_map/ppermute | solution.py:655
  54.1 3.7 %collective-permute-start.13 = (bf16[2,2,8,72,384]{4,3,2,1,0:T(8,128)(2,1)S(1)}, bf16[2,2,8,72,384]{4,3,2,1,0:T(8,128)(2,1)S(1)}, u32[]{:S(2)}, u32[]{:S(2)}) collective-permute-start(bf16[2,2,8,72,384]{4,3,2,1,0:T(8,128)(2,1)S(1)} %get-tuple-element.115), channel_id=1, source_target_pairs={{0,2},{2,0},{4,6},{6,4},{8,10},{10,8},{12,14},{14,12},{16,18},{18,... | collective-permute-start | bytes 5308424 | tf_op jit(solution)/shard_map/ppermute | solution.py:655
  63.4 15.1 %collective-permute-start.18 = (bf16[1,2,8,80,384]{4,3,2,1,0:T(8,128)(2,1)S(1)}, bf16[1,2,8,80,384]{4,3,2,1,0:T(8,128)(2,1)S(1)}, u32[]{:S(2)}, u32[]{:S(2)}) collective-permute-start(bf16[1,2,8,80,384]{4,3,2,1,0:T(8,128)(2,1)S(1)} %get-tuple-element.125), channel_id=1, source_target_pairs={{0,2},{2,0},{4,6},{6,4},{8,10},{10,8},{12,14},{14,12},{16,18},{18,... | collective-permute-start | bytes 2949128 | tf_op jit(solution)/shard_map/ppermute | solution.py:655
  63.6 12.5 %collective-permute-start.14 = (bf16[8,72,384]{2,1,0:T(8,128)(2,1)S(1)}, bf16[8,72,384]{2,1,0:T(8,128)(2,1)S(1)}, u32[]{:S(2)}, u32[]{:S(2)}) collective-permute-start(bf16[8,72,384]{2,1,0:T(8,128)(2,1)S(1)} %get-tuple-element.118), channel_id=1, source_target_pairs={{0,1},{1,0},{2,3},{3,2},{4,5},{5,4},{6,7},{7,6},{8,9},{9,8},{10,11... | collective-permute-start | bytes 1327112 | tf_op jit(solution)/shard_map/ppermute | solution.py:655
  63.9 14.9 %collective-permute-start.16 = (bf16[2,4,72,384]{3,2,1,0:T(8,128)(2,1)S(1)}, bf16[2,4,72,384]{3,2,1,0:T(8,128)(2,1)S(1)}, u32[]{:S(2)}, u32[]{:S(2)}) collective-permute-start(bf16[2,4,72,384]{3,2,1,0:T(8,128)(2,1)S(1)} %get-tuple-element.121), channel_id=1, source_target_pairs={{0,4},{2,6},{4,0},{6,2},{8,12},{10,14},{12,8},{14,10},{16,20},{18,... | collective-permute-start | bytes 1327112 | tf_op jit(solution)/shard_map/ppermute | solution.py:655
  65.6 13.3 %collective-permute-start.17 = (bf16[4,2,72,384]{3,2,1,0:T(8,128)(2,1)S(1)}, bf16[4,2,72,384]{3,2,1,0:T(8,128)(2,1)S(1)}, u32[]{:S(2)}, u32[]{:S(2)}) collective-permute-start(bf16[4,2,72,384]{3,2,1,0:T(8,128)(2,1)S(1)} %get-tuple-element.123), channel_id=1, source_target_pairs={{0,8},{2,10},{4,12},{6,14},{8,0},{10,2},{12,4},{14,6},{16,24},{18,... | collective-permute-start | bytes 1327112 | tf_op jit(solution)/shard_map/ppermute | solution.py:655
  77.0 8.4 %collective-permute-start.15 = (bf16[4,72,384]{2,1,0:T(8,128)(2,1)S(1)}, bf16[4,72,384]{2,1,0:T(8,128)(2,1)S(1)}, u32[]{:S(2)}, u32[]{:S(2)}) collective-permute-start(bf16[4,72,384]{2,1,0:T(8,128)(2,1)S(1)} %get-tuple-element.120), channel_id=1, source_target_pairs={{0,4},{2,6},{4,0},{6,2},{8,12},{10,14},{12,8},{14,10},{16,20},{18,... | collective-permute-start | bytes 663560 | tf_op jit(solution)/shard_map/ppermute | solution.py:655
  79.0 6.7 %collective-permute-start.19 = (bf16[2,2,72,384]{3,2,1,0:T(8,128)(2,1)S(1)}, bf16[2,2,72,384]{3,2,1,0:T(8,128)(2,1)S(1)}, u32[]{:S(2)}, u32[]{:S(2)}) collective-permute-start(bf16[2,2,72,384]{3,2,1,0:T(8,128)(2,1)S(1)} %get-tuple-element.128), channel_id=1, source_target_pairs={{0,8},{2,10},{4,12},{6,14},{8,0},{10,2},{12,4},{14,6},{16,24},{18,... | collective-permute-start | bytes 663560 | tf_op jit(solution)/shard_map/ppermute | solution.py:655
  80.6 8.1 %collective-permute-start.20 = (bf16[2,2,72,384]{3,2,1,0:T(8,128)(2,1)S(1)}, bf16[2,2,72,384]{3,2,1,0:T(8,128)(2,1)S(1)}, u32[]{:S(2)}, u32[]{:S(2)}) collective-permute-start(bf16[2,2,72,384]{3,2,1,0:T(8,128)(2,1)S(1)} %get-tuple-element.130), channel_id=1, source_target_pairs={{0,4},{2,6},{4,0},{6,2},{8,12},{10,14},{12,8},{14,10},{16,20},{18,... | collective-permute-start | bytes 663560 | tf_op jit(solution)/shard_map/ppermute | solution.py:655
  81.2 13.4 %collective-permute-start.24 = (bf16[8,80,384]{2,1,0:T(8,128)(2,1)S(1)}, bf16[8,80,384]{2,1,0:T(8,128)(2,1)S(1)}, u32[]{:S(2)}, u32[]{:S(2)}) collective-permute-start(bf16[8,80,384]{2,1,0:T(8,128)(2,1)S(1)} %get-tuple-element.137), channel_id=1, source_target_pairs={{0,1},{1,0},{2,3},{3,2},{4,5},{5,4},{6,7},{7,6},{8,9},{9,8},{10,11... | collective-permute-start | bytes 1474568 | tf_op jit(solution)/shard_map/ppermute | solution.py:655
  88.8 7.3 %collective-permute-start.21 = (bf16[2,72,384]{2,1,0:T(8,128)(2,1)S(1)}, bf16[2,72,384]{2,1,0:T(8,128)(2,1)S(1)}, u32[]{:S(2)}, u32[]{:S(2)}) collective-permute-start(bf16[2,72,384]{2,1,0:T(8,128)(2,1)S(1)} %get-tuple-element.132), channel_id=1, source_target_pairs={{0,8},{2,10},{4,12},{6,14},{8,0},{10,2},{12,4},{14,6},{16,24},{18,... | collective-permute-start | bytes 331784 | tf_op jit(solution)/shard_map/ppermute | solution.py:655
  90.5 6.1 %collective-permute-start.22 = (bf16[2,72,384]{2,1,0:T(8,128)(2,1)S(1)}, bf16[2,72,384]{2,1,0:T(8,128)(2,1)S(1)}, u32[]{:S(2)}, u32[]{:S(2)}) collective-permute-start(bf16[2,72,384]{2,1,0:T(8,128)(2,1)S(1)} %get-tuple-element.134), channel_id=1, source_target_pairs={{0,1},{1,0},{2,3},{3,2},{4,5},{5,4},{6,7},{7,6},{8,9},{9,8},{10,11... | collective-permute-start | bytes 331784 | tf_op jit(solution)/shard_map/ppermute | solution.py:655
  91.0 6.8 %collective-permute-start.23 = (bf16[2,72,384]{2,1,0:T(8,128)(2,1)S(1)}, bf16[2,72,384]{2,1,0:T(8,128)(2,1)S(1)}, u32[]{:S(2)}, u32[]{:S(2)}) collective-permute-start(bf16[2,72,384]{2,1,0:T(8,128)(2,1)S(1)} %get-tuple-element.136), channel_id=1, source_target_pairs={{0,1},{1,0},{2,3},{3,2},{4,5},{5,4},{6,7},{7,6},{8,9},{9,8},{10,11... | collective-permute-start | bytes 331784 | tf_op jit(solution)/shard_map/ppermute | solution.py:655
  94.6 6.3 %collective-permute-start.26 = (bf16[4,80,384]{2,1,0:T(8,128)(2,1)S(1)}, bf16[4,80,384]{2,1,0:T(8,128)(2,1)S(1)}, u32[]{:S(2)}, u32[]{:S(2)}) collective-permute-start(bf16[4,80,384]{2,1,0:T(8,128)(2,1)S(1)} %get-tuple-element.141), channel_id=1, source_target_pairs={{0,4},{2,6},{4,0},{6,2},{8,12},{10,14},{12,8},{14,10},{16,20},{18,... | collective-permute-start | bytes 737288 | tf_op jit(solution)/shard_map/ppermute | solution.py:655
  97.8 9.3 %collective-permute-start.25 = (bf16[3,72,384]{2,1,0:T(8,128)(2,1)S(1)}, bf16[3,72,384]{2,1,0:T(8,128)(2,1)S(1)}, u32[]{:S(2)}, u32[]{:S(2)}) collective-permute-start(bf16[3,72,384]{2,1,0:T(8,128)(2,1)S(1)} %get-tuple-element.140), channel_id=1, source_target_pairs={{0,16},{2,18},{4,20},{6,22},{8,24},{10,26},{12,28},{14,30},{16,0},... | collective-permute-start | bytes 497672 | tf_op jit(solution)/shard_map/ppermute | solution.py:655
  100.9 7.1 %collective-permute-start.27 = (bf16[2,80,384]{2,1,0:T(8,128)(2,1)S(1)}, bf16[2,80,384]{2,1,0:T(8,128)(2,1)S(1)}, u32[]{:S(2)}, u32[]{:S(2)}) collective-permute-start(bf16[2,80,384]{2,1,0:T(8,128)(2,1)S(1)} %get-tuple-element.143), channel_id=1, source_target_pairs={{0,8},{2,10},{4,12},{6,14},{8,0},{10,2},{12,4},{14,6},{16,24},{18,... | collective-permute-start | bytes 368648 | tf_op jit(solution)/shard_map/ppermute | solution.py:655
  108.1 10.2 %collective-permute-start.28 = (bf16[3,72,384]{2,1,0:T(8,128)(2,1)S(1)}, bf16[3,72,384]{2,1,0:T(8,128)(2,1)S(1)}, u32[]{:S(2)}, u32[]{:S(2)}) collective-permute-start(bf16[3,72,384]{2,1,0:T(8,128)(2,1)S(1)} %get-tuple-element.144.refs_0_), channel_id=1, source_target_pairs={{0,16},{2,18},{4,20},{6,22},{8,24},{10,26},{12,28},{14,30},{16,0},... | collective-permute-start | bytes 497672 | tf_op jit(solution)/shard_map/ppermute | solution.py:655
  108.6 9.7 %collective-permute-start.29 = (bf16[80,384]{1,0:T(8,128)(2,1)S(1)}, bf16[80,384]{1,0:T(8,128)(2,1)S(1)}, u32[]{:S(2)}, u32[]{:S(2)}) collective-permute-start(bf16[80,384]{1,0:T(8,128)(2,1)S(1)} %get-tuple-element.146), channel_id=1, source_target_pairs={{0,16},{2,18},{4,20},{6,22},{8,24},{10,26},{12,28},{14,30},{16,0},... | collective-permute-start | bytes 184328 | tf_op jit(solution)/shard_map/ppermute | solution.py:655
  118.3 7.0 %collective-permute-start.31 = (bf16[2,2,72,384]{3,2,1,0:T(8,128)(2,1)S(1)}, bf16[2,2,72,384]{3,2,1,0:T(8,128)(2,1)S(1)}, u32[]{:S(2)}, u32[]{:S(2)}) collective-permute-start(bf16[2,2,72,384]{3,2,1,0:T(8,128)(2,1)S(1)} %get-tuple-element.148.refs_2_), channel_id=1, source_target_pairs={{0,4},{2,6},{4,0},{6,2},{8,12},{10,14},{12,8},{14,10},{16,20},{18,... | collective-permute-start | bytes 663560 | tf_op jit(solution)/shard_map/ppermute | solution.py:655
  119.9 5.4 %collective-permute-start.30 = (bf16[2,72,384]{2,1,0:T(8,128)(2,1)S(1)}, bf16[2,72,384]{2,1,0:T(8,128)(2,1)S(1)}, u32[]{:S(2)}, u32[]{:S(2)}) collective-permute-start(bf16[2,72,384]{2,1,0:T(8,128)(2,1)S(1)} %get-tuple-element.147.refs_0_), channel_id=1, source_target_pairs={{0,8},{2,10},{4,12},{6,14},{8,0},{10,2},{12,4},{14,6},{16,24},{18,... | collective-permute-start | bytes 331784 | tf_op jit(solution)/shard_map/ppermute | solution.py:655
  119.9 5.4 %collective-permute-start.32 = (bf16[80,384]{1,0:T(8,128)(2,1)S(1)}, bf16[80,384]{1,0:T(8,128)(2,1)S(1)}, u32[]{:S(2)}, u32[]{:S(2)}) collective-permute-start(bf16[80,384]{1,0:T(8,128)(2,1)S(1)} %get-tuple-element.149.refs_4_), channel_id=1, source_target_pairs={{0,16},{2,18},{4,20},{6,22},{8,24},{10,26},{12,28},{14,30},{16,0},... | collective-permute-start | bytes 184328 | tf_op jit(solution)/shard_map/ppermute | solution.py:655
  125.4 9.9 %collective-permute-start.34 = (bf16[2,2,2,72,384]{4,3,2,1,0:T(8,128)(2,1)S(1)}, bf16[2,2,2,72,384]{4,3,2,1,0:T(8,128)(2,1)S(1)}, u32[]{:S(2)}, u32[]{:S(2)}) collective-permute-start(bf16[2,2,2,72,384]{4,3,2,1,0:T(8,128)(2,1)S(1)} %get-tuple-element.151.refs_2_), channel_id=1, source_target_pairs={{0,8},{2,10},{4,12},{6,14},{8,0},{10,2},{12,4},{14,6},{16,24},{18,... | collective-permute-start | bytes 1327112 | tf_op jit(solution)/shard_map/ppermute | solution.py:655
  127.2 7.3 %collective-permute-start.33 = (bf16[2,2,72,384]{3,2,1,0:T(8,128)(2,1)S(1)}, bf16[2,2,72,384]{3,2,1,0:T(8,128)(2,1)S(1)}, u32[]{:S(2)}, u32[]{:S(2)}) collective-permute-start(bf16[2,2,72,384]{3,2,1,0:T(8,128)(2,1)S(1)} %get-tuple-element.150.refs_0_), channel_id=1, source_target_pairs={{0,4},{2,6},{4,0},{6,2},{8,12},{10,14},{12,8},{14,10},{16,20},{18,... | collective-permute-start | bytes 663560 | tf_op jit(solution)/shard_map/ppermute | solution.py:655
  127.7 9.6 %copy-start.6 = (f32[768,576]{0,1:T(8,128)S(1)}, f32[768,576]{0,1:T(8,128)}, u32[]{:S(2)}) copy-start(f32[768,576]{0,1:T(8,128)} %param.30) | copy-start | bytes 5308420
  127.7 9.6 %copy-start.7 = (f32[768,576]{0,1:T(8,128)S(1)}, f32[768,576]{0,1:T(8,128)}, u32[]{:S(2)}) copy-start(f32[768,576]{0,1:T(8,128)} %param.35) | copy-start | bytes 5308420
  127.7 6.8 %collective-permute-start.35 = (bf16[2,80,384]{2,1,0:T(8,128)(2,1)S(1)}, bf16[2,80,384]{2,1,0:T(8,128)(2,1)S(1)}, u32[]{:S(2)}, u32[]{:S(2)}) collective-permute-start(bf16[2,80,384]{2,1,0:T(8,128)(2,1)S(1)} %get-tuple-element.152.refs_4_), channel_id=1, source_target_pairs={{0,4},{2,6},{4,0},{6,2},{8,12},{10,14},{12,8},{14,10},{16,20},{18,... | collective-permute-start | bytes 368648 | tf_op jit(solution)/shard_map/ppermute | solution.py:655
  135.5 1.9 %collective-permute-start.37 = (bf16[1,2,4,72,384]{4,3,2,1,0:T(8,128)(2,1)S(1)}, bf16[1,2,4,72,384]{4,3,2,1,0:T(8,128)(2,1)S(1)}, u32[]{:S(2)}, u32[]{:S(2)}) collective-permute-start(bf16[1,2,4,72,384]{4,3,2,1,0:T(8,128)(2,1)S(1)} %get-tuple-element.154.refs_0_), channel_id=1, source_target_pairs={{0,2},{2,0},{4,6},{6,4},{8,10},{10,8},{12,14},{14,12},{16,18},{18,... | collective-permute-start | bytes 1327112 | tf_op jit(solution)/shard_map/ppermute | solution.py:655
  135.6 8.4 %collective-permute-start.36 = (bf16[2,2,80,384]{3,2,1,0:T(8,128)(2,1)S(1)}, bf16[2,2,80,384]{3,2,1,0:T(8,128)(2,1)S(1)}, u32[]{:S(2)}, u32[]{:S(2)}) collective-permute-start(bf16[2,2,80,384]{3,2,1,0:T(8,128)(2,1)S(1)} %get-tuple-element.153.refs_0_), channel_id=1, source_target_pairs={{0,8},{2,10},{4,12},{6,14},{8,0},{10,2},{12,4},{14,6},{16,24},{18,... | collective-permute-start | bytes 737288 | tf_op jit(solution)/shard_map/ppermute | solution.py:655
  137.2 8.5 %collective-permute-start.39 = (bf16[2,2,4,72,384]{4,3,2,1,0:T(8,128)(2,1)S(1)}, bf16[2,2,4,72,384]{4,3,2,1,0:T(8,128)(2,1)S(1)}, u32[]{:S(2)}, u32[]{:S(2)}) collective-permute-start(bf16[2,2,4,72,384]{4,3,2,1,0:T(8,128)(2,1)S(1)} %get-tuple-element.156.refs_0_.refs_2_), channel_id=1, source_target_pairs={{0,2},{2,0},{4,6},{6,4},{8,10},{10,8},{12,14},{14,12},{16,18},{18,... | collective-permute-start | bytes 2654216 | tf_op jit(solution)/shard_map/ppermute | solution.py:655
  145.5 9.5 %copy-start.9 = (f32[288,960]{1,0:T(8,128)S(1)}, f32[288,960]{1,0:T(8,128)}, u32[]{:S(2)}) copy-start(f32[288,960]{1,0:T(8,128)} %refs_2_.5) | copy-start | bytes 3317764
  145.5 9.5 %copy-start.10 = (f32[288,960]{1,0:T(8,128)S(1)}, f32[288,960]{1,0:T(8,128)}, u32[]{:S(2)}) copy-start(f32[288,960]{1,0:T(8,128)} %refs_4_.5) | copy-start | bytes 3317764
  145.5 9.5 %copy-start.11 = (f32[288,960]{1,0:T(8,128)S(1)}, f32[288,960]{1,0:T(8,128)}, u32[]{:S(2)}) copy-start(f32[288,960]{1,0:T(8,128)} %refs_6_.7) | copy-start | bytes 3317764
  145.5 9.5 %copy-start.13 = (f32[288,576]{1,0:T(8,128)S(1)}, f32[288,576]{1,0:T(8,128)}, u32[]{:S(2)}) copy-start(f32[288,576]{1,0:T(8,128)} %refs_3_.2) | copy-start | bytes 1990660
  145.5 9.5 %copy-start.14 = (f32[288,576]{1,0:T(8,128)S(1)}, f32[288,576]{1,0:T(8,128)}, u32[]{:S(2)}) copy-start(f32[288,576]{1,0:T(8,128)} %refs_5_.3) | copy-start | bytes 1990660
  145.6 9.4 %collective-permute-start.38 = (bf16[1,2,4,80,384]{4,3,2,1,0:T(8,128)(2,1)S(1)}, bf16[1,2,4,80,384]{4,3,2,1,0:T(8,128)(2,1)S(1)}, u32[]{:S(2)}, u32[]{:S(2)}) collective-permute-start(bf16[1,2,4,80,384]{4,3,2,1,0:T(8,128)(2,1)S(1)} %share_qkv_out.1.refs_7_.refs_0_), channel_id=1, source_target_pairs={{0,2},{2,0},{4,6},{6,4},{8,10},{10,8},{12,14},{14,12},{16,18},{18,... | collective-permute-start | bytes 1474568 | tf_op jit(solution)/shard_map/ppermute | solution.py:655
  (18 other events, 82.0 us)

commit v5 on v4

--- a/solution.py
+++ b/solution.py
@@ -30,8 +30,10 @@
 MASKED = -1e30
 SCALE = float(HEAD) ** (-0.5)
 VMEM_LIMIT = 32 * 1024 * 1024
+PACK_LIMIT = 60 * 1024 * 1024
 HALF = 144
 CUT_ROWS = 72
+MARK = (8, 128)
 CUT_COLUMNS = 384
 F32 = jnp.float32
 BF16 = jnp.bfloat16
@@ -79,8 +81,8 @@
 
 
 class Weight:
-    def __init__(self, shape, whole=None, own=(), parts=(), place=None):
-        self.shape, self.own, self.parts, self.place = shape, own, parts, place
+    def __init__(self, shape, whole=None, own=(), parts=()):
+        self.shape, self.own, self.parts = shape, own, parts
         self.arrays = [whole] if whole is not None else [a[0] for a in (*own, *parts)]
         self.split = whole is None
 
@@ -89,8 +91,8 @@
             return refs[0]
         for ref, (_, place) in zip(refs, self.own):
             self.put(full, place(idx[0]), ref[...].astype(BF16))
-        for ref, (_, (core, x, low)) in zip(refs[len(self.own) :], self.parts):
-            place = self.place(1 - idx[0], idx[1] ^ core, idx[2] ^ x, (idx[3] & 1) ^ low)
+        for ref, (_, (core, x, low), place) in zip(refs[len(self.own) :], self.parts):
+            place = place(1 - idx[0], idx[1] ^ core, idx[2] ^ x, (idx[3] & 1) ^ low)
             rows = ref.shape[0] // HALF * HALF
             self.put(full, place, ref[:rows, :])
         return full
@@ -203,7 +205,7 @@
     return exponent / jnp.sum(exponent, axis=-1, keepdims=True)
 
 
-def pack_kernel(body, idx, sources, places, outs, name, after=()):
+def pack_kernel(body, idx, sources, places, outs, name, after=(), limit=PACK_LIMIT):
     windows = [shape for shape, _ in places]
 
     def kernel(idx_ref, *refs):
@@ -233,27 +235,35 @@
         out_specs=tuple([pl.BlockSpec(memory_space=pltpu.VMEM)] * len(outs)),
         scratch_shapes=[pltpu.VMEM(w, F32) for w in windows]
         + [pltpu.SemaphoreType.DMA((len(sources),))],
-        compiler_params=pltpu.CompilerParams(vmem_limit_bytes=VMEM_LIMIT),
+        compiler_params=pltpu.CompilerParams(vmem_limit_bytes=limit),
         cost_estimate=busy_for(10),
         name=name,
     )(idx, *sources, *after)
 
 
 def cast_out(idx_ref, buffers, outs):
-    outs[0][...] = buffers[0][...].astype(BF16)
+    for buffer, out in zip(buffers, outs):
+        out[...] = buffer[...].astype(BF16)
 
 
 def pack_gate_up(idx, w_gate_up):
-    window = ((HALF, FF), lambda i: (i[1] * HALF, i[2] * FF))
+    shape = (HALF, FF // 2)
+    windows = [
+        (shape, lambda i: (i[1] * HALF, i[2] * (FF // 2))),
+        (shape, lambda i: (i[1] * HALF, FF + (i[3] & 1) * (FF // 2))),
+    ]
     return pack_kernel(
-        cast_out, idx, [w_gate_up], [window], [sds((HALF, FF), BF16)], "pack_gate_up"
+        cast_out, idx, [w_gate_up] * 2, windows, [sds(shape, BF16)] * 2, "pack_gate_up"
+    )
+
+
+def pack_down(idx, down_t, after):
+    shape = (2 * HALF, down_t.shape[1])
+    window = (shape, lambda i: (i[1] * 2 * HALF, 0))
+    outs = [sds(shape, BF16)]
+    return pack_kernel(
+        cast_out, idx, [down_t], [window], outs, "pack_down", after, VMEM_LIMIT
     )[0]
-
-
-def pack_down(idx, down_t, after):
-    shape = (HALF, down_t.shape[1])
-    window = (shape, lambda i: ((i[1] * 2 + (i[3] & 1)) * HALF, 0))
-    return pack_kernel(cast_out, idx, [down_t], [window], [sds(shape, BF16)], "pack_down", after)[0]
 
 
 def pack_qkv_out(idx, w_qkv, w_out, norm_gains, after):
@@ -508,7 +518,8 @@
                 columns = slice(owner * half, (owner + 1) * half)
                 gain_rows[owner, 0:1, :half] = grad_gain_one[:, columns]
                 gain_rows[owner, 1:2, :half] = grad_gain_two[:, columns]
-            pieces.emit(idx_ref, blocks[0], outs[1:], gain_rows)
+            pieces.emit(idx_ref, blocks[0], outs[1:3], gain_rows)
+            outs[3][...] = jnp.zeros_like(outs[3])
         grad_ref[...] = (
             (gu + norm_back(grad_normed * gains_ref[0:1, :], normed, scale_one)).T
         ).astype(BF16)
@@ -522,7 +533,7 @@
     if pieces is None:
         outs += [sds((width, QKV + width), F32), sds((2, width), F32)]
     else:
-        outs += pieces.outs()
+        outs += pieces.outs() + [sds(MARK, F32)]
         scratch += [pieces.scratch(QKV + width)]
     return call(
         body,
@@ -548,7 +559,7 @@
         + [pl.BlockSpec(memory_space=pl.ANY)] * len(after),
         out_specs=tuple([pl.BlockSpec(memory_space=pltpu.VMEM)] * len(outs)),
         compiler_params=pltpu.CompilerParams(vmem_limit_bytes=VMEM_LIMIT),
-        cost_estimate=busy_for(4),
+        cost_estimate=busy_for(20),
         name=name,
     )(*arrays, *after)
 
@@ -584,7 +595,8 @@
         state_refs, refs = refs[: 3 * count], refs[3 * count :]
         gain_refs, refs = refs[: len(gains)], refs[len(gains) + len(after) :]
         outs, refs = refs[: 3 * count], refs[3 * count :]
-        gain_outs, full = refs[: len(gains)], refs[-1]
+        gain_outs, mark, full = refs[: len(gains)], refs[-2], refs[-1]
+        mark[...] = jnp.zeros_like(mark)
         is_near = pl.program_id(0) % 2 == idx_ref[1]
         for i, put in enumerate(puts):
             for z in range(4):
@@ -630,7 +642,6 @@
         for p in parts
         for _ in range(2)
     ]
-    moved = sum(a.size * 8 for a in state)
     return pl.pallas_call(
         kernel,
         grid_spec=pltpu.PrefetchScalarGridSpec(
@@ -640,12 +651,12 @@
             + state_specs
             + gain_specs
             + [pl.BlockSpec(memory_space=pl.ANY)] * len(after),
-            out_specs=tuple(state_specs + gain_specs),
+            out_specs=tuple(state_specs + gain_specs + [pl.BlockSpec(MARK, lambda t, _: (0, 0))]),
             scratch_shapes=[pltpu.VMEM(shape, F32)],
         ),
-        out_shape=tuple(sds(a.shape, F32) for a in [*state, *gains]),
+        out_shape=tuple(sds(a.shape, F32) for a in [*state, *gains]) + (sds(MARK, F32),),
         compiler_params=pltpu.CompilerParams(vmem_limit_bytes=VMEM_LIMIT),
-        cost_estimate=pl.CostEstimate(flops=0, bytes_accessed=moved, transcendentals=0),
+        cost_estimate=busy_for(20),
         name=name,
     )(idx, *[near, far] * len(parts), *state, *gains, *after)
 
@@ -696,38 +707,41 @@
     frequency = ROPE_BASE ** (-(np.arange(half_size) * 2.0 / HEAD))
     frequency = jnp.asarray(np.tile(frequency, 4)[None], F32)
     if fast:
-        gate_up = pack_gate_up(idx, w_gate_up)
-        gate_up_near = over_y(gate_up)
-        qo_near = over_y(pack_qkv_out(idx, w_qkv, w_out, norm_gains, (gate_up,)))
-        down_near = over_y(pack_down(idx, down_t, (gate_up_near,)))
-        gate_up_near_x = over_x(gate_up_near)
-        gate_up_far, gate_up_far_x = over_core(gate_up_near), over_core(gate_up_near_x)
+        by_x, by_low = pack_gate_up(idx, w_gate_up)
+        by_x, by_low = over_y(by_x), over_y(by_low)
+        qo_near = over_y(pack_qkv_out(idx, w_qkv, w_out, norm_gains, ()))
+        down_near = over_y(pack_down(idx, down_t, (by_low,)))
+        by_x_next, by_low_next = over_x(by_x), over_z_low(by_low)
         qo_near_low = over_z_low(qo_near)
-        qo_far, qo_far_low = over_core(qo_near), over_core(qo_near_low)
         gains = (norm_gains, qo_near)
         own_rows = lambda o: (o * rows, 0)
         own_rows_out = lambda o: (o * rows, QKV)
+        qo_place = lambda o, c, x, low: (o * rows + c * HALF, low * ((QKV + width) // 2))
+        x_place = lambda o, c, x, low: (o * rows + c * HALF, x * (FF // 2))
+        low_place = lambda o, c, x, low: (o * rows + c * HALF, FF + low * (FF // 2))
         mat_qkv_out = Weight(
             (width, QKV + width),
             own=[(w_qkv, own_rows), (w_out, own_rows_out)],
             parts=[
-                (qo_near, (0, 0, 0)),
-                (qo_near_low, (0, 0, 1)),
-                (qo_far, (1, 0, 0)),
-                (qo_far_low, (1, 0, 1)),
+                (qo_near, (0, 0, 0), qo_place),
+                (qo_near_low, (0, 0, 1), qo_place),
+                (over_core(qo_near), (1, 0, 0), qo_place),
+                (over_core(qo_near_low), (1, 0, 1), qo_place),
             ],
-            place=lambda o, c, x, low: (o * rows + c * HALF, low * ((QKV + width) // 2)),
         )
         mat_gate_up = Weight(
             (width, 2 * FF),
             own=[(w_gate_up, own_rows)],
             parts=[
-                (gate_up_near, (0, 0, 0)),
-                (gate_up_near_x, (0, 1, 0)),
-                (gate_up_far, (1, 0, 0)),
-                (gate_up_far_x, (1, 1, 0)),
+                (by_x, (0, 0, 0), x_place),
+                (by_x_next, (0, 1, 0), x_place),
+                (over_core(by_x), (1, 0, 0), x_place),
+                (over_core(by_x_next), (1, 1, 0), x_place),
+                (by_low, (0, 0, 0), low_place),
+                (by_low_next, (0, 0, 1), low_place),
+                (over_core(by_low), (1, 0, 0), low_place),
+                (over_core(by_low_next), (1, 0, 1), low_place),
             ],
-            place=lambda o, c, x, low: (o * rows + c * HALF, x * FF),
         )
         cut_qkv_out = Pieces(lambda o, c, x, z, p: (o * 4 + c * 2 + x, z), extra=8)
         cut_gate_up = Pieces(lambda o, c, x, z, p: (o * 4 + c * 2 + p, x * 4 + z), parts=2)
@@ -749,34 +763,30 @@
     qkv, attended, *tables, gains, whole = attention_forward(
         idx, x_t, segments, frequency, gains, mat_qkv_out
     ) + (() if fast else (None,))
-    after = ()
     if fast:
         mat_qkv_out = Weight(whole.shape, whole=whole)
-
-        def pass_on(ins, outs):
-            outs[0][...] = ins[0][...]
-
-        (down_near,) = step(
-            pass_on, [down_near], [sds(down_near.shape, BF16)], "pass_on", (attended,)
-        )
-        down_near_low = over_z_low(down_near)
-        after = (down_near,)
     middle, normed_low, ab, hidden, *grad_down = feed_forward(
-        idx, x_t, attended, gains, y_t, mat_qkv_out, mat_gate_up, cut_down, after
-    )
+        idx, x_t, attended, gains, y_t, mat_qkv_out, mat_gate_up, cut_down, ()
+    )
+    after = ()
     if fast:
         whole = grad_down.pop()
         mat_gate_up = Weight(whole.shape, whole=whole)
+
+        def pass_on(ins, outs):
+            outs[0][...] = ins[0][...]
+
+        (down_near,) = step(
+            pass_on, [down_near], [sds(down_near.shape, BF16)], "pass_on", (normed_low,)
+        )
+        down_place = lambda o, c, x, low: (c * 2 * HALF, o * down_rows)
         mat_down = Weight(
             (width, FF),
             own=[(down_t, lambda o: (0, o * down_rows))],
             parts=[
-                (down_near, (0, 0, 0)),
-                (down_near_low, (0, 0, 1)),
-                (over_core(down_near), (1, 0, 0)),
-                (over_core(down_near_low), (1, 0, 1)),
+                (down_near, (0, 0, 0), down_place),
+                (over_core(down_near), (1, 0, 0), down_place),
             ],
-            place=lambda o, c, x, low: ((c * 2 + low) * HALF, o * down_rows),
         )
     if fast:
         arrived_down = over_core(grad_down[0])
@@ -833,124 +843,148 @@
             full[:, pl.ds(z * 384, 384)] = piece
 
         arrived_qkv_out = over_core(grad_qkv_out[0])
+        piece = (CUT_ROWS, CUT_COLUMNS)
+        taller = (CUT_ROWS + 8, CUT_COLUMNS)
         ((send, keep_down),) = add_step(
-            [(cut(keep_down, 2, 4), cut(arrived_down, 2, 4), 0)], "down_y", (token_grad,)
+            [(cut(keep_down, 2, 4), cut(arrived_down, 2, 4), 0)], "down_y", (grad_qkv_out[2],)
         )
         arrived_down = over_x(send)
-        ((send, keep_qkv_out),) = add_step(
-            [(grad_qkv_out[1][0], arrived_qkv_out[0], 0)], "qkv_out_core", (keep_down,)
-        )
-        arrived_qkv_out = over_y(send)
         (send_up, keep_up), (send_low, keep_low) = add_step(
             [
                 (cut(keep_up, 2, 2, 2), cut(arrived_up, 2, 2, 2), 1),
-                (cut(keep_low, 2, 2, 2), cut(arrived_low, 2, 2, 2), 1),
+                (cut(keep_low, 2, 2, 2), cut(arrived_low, 2, 2, 2), 0),
             ],
             "up_x_low_z",
-            (keep_qkv_out,),
-        )
-        arrived_up, arrived_low = over_z_low(send_up), over_x(send_low)
-        (send, keep_down), (send_up, keep_up), (send_low, keep_low) = add_step(
+            (keep_down,),
+        )
+        arrived_up, arrived_low = over_z_low(send_up), over_y(send_low)
+
+        def qkv_out_core(ins, outs):
+            total = ins[0][...].astype(F32) + ins[1][...].astype(F32)
+            outs[0][...] = total[1, :, 0].astype(BF16)
+            outs[1][...] = total[0, :, 0]
+            outs[2][...] = total[:, 1, 1].astype(BF16)
+            outs[3][...] = total[:, 0, 1]
+
+        send_a, keep_a, send_b, keep_b = step(
+            qkv_out_core,
+            [cut(a, 2, 2, 2, 2) for a in (grad_qkv_out[1], arrived_qkv_out)],
+            [sds((2, 2, *taller), t) for t in (BF16, F32, BF16, F32)],
+            "qkv_out_core",
+            (keep_up,),
+        )
+        arrived_a, arrived_b = over_y(send_a), over_x(send_b)
+        ((send, keep_down),) = add_step(
+            [(cut(keep_down, 2, 2), cut(arrived_down, 2, 2), 0)], "down_x", (keep_a,)
+        )
+        arrived_down = over_z_low(send)
+        (send_up, keep_up), (send_low, keep_low), (send_a, keep_a), (send_b, keep_b) = add_step(
             [
-                (cut(keep_down, 2, 2), cut(arrived_down, 2, 2), 0),
                 (keep_up, arrived_up, 0),
                 (keep_low, arrived_low, 0),
+                (keep_a, arrived_a, 0),
+                (keep_b, arrived_b, 0),
             ],
-            "down_x_up_z_low_x",
-            (keep_up,),
-        )
-        arrived_down, arrived_up, arrived_low = over_z_low(send), over_y(send_up), over_y(send_low)
-        ((send, keep_qkv_out),) = add_step(
-            [(cut(keep_qkv_out, 2, 4), cut(arrived_qkv_out, 2, 4), 0)], "qkv_out_y", (keep_down,)
-        )
-        arrived_qkv_out = over_x(send)
-
-        piece = (CUT_ROWS, CUT_COLUMNS)
-        taller = (CUT_ROWS + 8, CUT_COLUMNS)
-
-        def last_sums(ins, outs):
-            for i in range(3):
+            "up_z_low_y_qkv_out_xy",
+            (keep_down,),
+        )
+        arrived_up, arrived_low = over_y(send_up), over_x(send_low)
+        arrived_a, arrived_b = over_x(send_a), over_y(send_b)
+        ((send, keep_down),) = add_step([(keep_down, arrived_down, 0)], "down_z_low", (keep_up,))
+        arrived_down = over_z_high(send)
+
+        def planes(ins, outs):
+            for i in range(2):
                 total = ins[2 * i][...] + ins[2 * i + 1][...].astype(F32)
                 outs[0][i] = total[1].astype(BF16)
                 outs[1][i] = total[0]
-
-        send, keep = step(
-            last_sums,
-            [keep_down, arrived_down, keep_up, arrived_up, keep_low, arrived_low],
-            [sds((3, *piece), BF16), sds((3, *piece), F32)],
-            "down_z_up_y_low_y",
-            (keep_qkv_out,),
+            outs[2][...] = (ins[6][...] + ins[7][...].astype(F32)).astype(BF16)
+            outs[3][...] = ins[4][...] + ins[5][...].astype(F32)
+            outs[4][...] = (ins[8][...] + ins[9][...].astype(F32)).astype(BF16)
+
+        send, keep, send_qkv_out, keep_qkv_out, piece_down = step(
+            planes,
+            [
+                *(keep_up, arrived_up, keep_low, arrived_low),
+                *(keep_a, arrived_a, keep_b, arrived_b),
+                *(keep_down, arrived_down),
+            ],
+            [
+                *(sds((2, *piece), BF16), sds((2, *piece), F32)),
+                *(sds((2, *taller), BF16), sds((2, *taller), F32)),
+                sds(piece, BF16),
+            ],
+            "planes",
         )
         arrived = over_z_high(send)
-        ((send, keep_qkv_out),) = add_step(
-            [(cut(keep_qkv_out, 2, 2), cut(arrived_qkv_out, 2, 2), 0)], "qkv_out_x", (keep,)
-        )
-        arrived_qkv_out = over_z_low(send)
-
-        def make_pieces(ins, outs):
+        arrived_qkv_out = over_z_low(send_qkv_out)
+        down_high = over_z_high(piece_down)
+
+        def lines(ins, outs):
             outs[0][...] = (ins[0][...] + ins[1][...].astype(F32)).astype(BF16)
             total = ins[2][...] + ins[3][...].astype(F32)
             outs[1][...] = total[1].astype(BF16)
             outs[2][...] = total[0]
-
-        pieces, send, keep_qkv_out = step(
-            make_pieces,
-            [keep, arrived, keep_qkv_out, arrived_qkv_out],
-            [sds((3, *piece), BF16), sds(taller, BF16), sds(taller, F32)],
-            "pieces_qkv_out_z",
-        )
-        pieces_high, arrived_qkv_out = over_z_high(pieces), over_z_high(send)
+            outs[3][0], outs[3][1] = ins[4][...], ins[5][...]
+
+        pieces, send_qkv_out, keep_qkv_out, near_down = step(
+            lines,
+            [keep, arrived, keep_qkv_out, arrived_qkv_out, piece_down, down_high],
+            [
+                sds((2, *piece), BF16),
+                *(sds(taller, BF16), sds(taller, F32)),
+                sds((2, *piece), BF16),
+            ],
+            "lines",
+        )
+        pieces_high = over_z_high(pieces)
+        arrived_qkv_out = over_z_high(send_qkv_out)
+        down_low = over_z_low(near_down)
 
         def share_high(ins, outs):
-            outs[0][0], outs[0][1] = ins[0][0], ins[1][0]
             for part in range(2):
-                outs[1][part, 0], outs[1][part, 1] = ins[0][part + 1], ins[1][part + 1]
+                outs[part][0], outs[part][1] = ins[0][part], ins[1][part]
             outs[2][...] = (ins[2][...] + ins[3][...].astype(F32)).astype(BF16)
-
-        near_down, near_gate_up, piece_qkv_out = step(
+            outs[3][0], outs[3][1] = ins[4][...], ins[5][...]
+
+        near_up, near_low, piece_qkv_out, near_down = step(
             share_high,
-            [pieces, pieces_high, keep_qkv_out, arrived_qkv_out],
-            [sds((2, *piece), BF16), sds((2, 2, *piece), BF16), sds(taller, BF16)],
-            "share_z_high",
-        )
-        down_low, gate_up_x = over_z_low(near_down), over_x(near_gate_up)
+            [pieces, pieces_high, keep_qkv_out, arrived_qkv_out, near_down, down_low],
+            [
+                *(sds((2, *piece), BF16), sds((2, *piece), BF16)),
+                sds(taller, BF16),
+                sds((2, 2, *piece), BF16),
+            ],
+            "share_high",
+        )
+        up_x, low_low = over_x(near_up), over_z_low(near_low)
         qkv_out_high = over_z_high(piece_qkv_out)
+        down_x = over_x(near_down)
 
         def share_next(ins, outs):
-            outs[0][0], outs[0][1] = ins[0][...], ins[1][...]
-            for part in range(2):
-                outs[1][part, 0], outs[1][part, 1] = ins[2][part], ins[3][part]
-            outs[2][0], outs[2][1] = ins[4][...], ins[5][...]
-
-        near_down, near_gate_up, near_qkv_out = step(
-            share_next,
-            [near_down, down_low, near_gate_up, gate_up_x, piece_qkv_out, qkv_out_high],
-            [sds((2, 2, *piece), BF16), sds((2, 2, 2, *piece), BF16), sds((2, *taller), BF16)],
-            "share_next",
-        )
-        down_x, gate_up_low = over_x(near_down), over_z_low(near_gate_up)
-        qkv_out_x = over_x(near_qkv_out)
-
-        def share_last(ins, outs):
+            for i in (0, 1, 2):
+                outs[i][0], outs[i][1] = ins[2 * i][...], ins[2 * i + 1][...]
             for x in range(2):
                 for low in range(2):
                     for high in range(2):
-                        slot = low * 2 + high
-                        outs[0][0, x, slot] = ins[x][low, high]
-                        for part in range(2):
-                            outs[1][part, x, slot] = ins[2 + low][part, x, high]
-            outs[2][0], outs[2][1] = ins[4][...], ins[5][...]
-
-        near_down, near_gate_up, near_qkv_out = step(
-            share_last,
-            [near_down, down_x, near_gate_up, gate_up_low, near_qkv_out, qkv_out_x],
-            [sds((1, 2, 4, *piece), BF16), sds((2, 2, 4, *piece), BF16), sds((2, 2, *taller), BF16)],
-            "share_last",
-        )
-        far_down, far_gate_up = over_core(near_down), over_core(near_gate_up)
-        qkv_out_low = over_z_low(near_qkv_out)
+                        outs[3][0, x, low * 2 + high] = ins[6 + x][low, high]
+
+        near_up, near_low, near_qkv_out, near_down = step(
+            share_next,
+            [near_up, up_x, near_low, low_low, piece_qkv_out, qkv_out_high, near_down, down_x],
+            [
+                *(sds((2, 2, *piece), BF16), sds((2, 2, *piece), BF16)),
+                sds((2, *taller), BF16),
+                sds((1, 2, 4, *piece), BF16),
+            ],
+            "share_next",
+        )
+        far_down = over_core(near_down)
+        up_low, low_x = over_z_low(near_up), over_x(near_low)
+        qkv_out_x, qkv_out_low = over_x(near_qkv_out), over_z_low(near_qkv_out)
+        qkv_out_both = swap(near_qkv_out, "dp", 6)
         by_row = lambda t, _: ((t % 2) * 2 + t // 2, 0)
-        one_down, two_down, next_down = update_state(
+        one_down, two_down, next_down, mark = update_state(
             idx,
             near_down,
             far_down,
@@ -962,21 +996,37 @@
             "update_down",
         )
 
+        def share_gate_up(ins, outs):
+            for near in range(2):
+                for far in range(2):
+                    for high in range(2):
+                        outs[0][0, near, far * 2 + high] = ins[far][near, high]
+                        outs[0][1, far, near * 2 + high] = ins[2 + far][near, high]
+
+        (near_gate_up,) = step(
+            share_gate_up,
+            [near_up, up_low, near_low, low_x],
+            [sds((2, 2, 4, *piece), BF16)],
+            "share_gate_up",
+            (mark,),
+        )
+        far_gate_up = over_core(near_gate_up)
+
         def share_qkv_out(ins, outs):
             for x in range(2):
                 for low in range(2):
                     for high in range(2):
-                        outs[0][0, x, low * 2 + high] = ins[low][x, high]
+                        outs[0][0, x, low * 2 + high] = ins[low * 2 + x][high]
 
         (near_qkv_out,) = step(
             share_qkv_out,
-            [near_qkv_out, qkv_out_low],
+            [near_qkv_out, qkv_out_x, qkv_out_low, qkv_out_both],
             [sds((1, 2, 4, *taller), BF16)],
             "share_qkv_out",
-            (one_down,),
+            (near_gate_up,),
         )
         far_qkv_out = over_core(near_qkv_out)
-        one_gate_up, two_gate_up, next_gate_up = update_state(
+        one_gate_up, two_gate_up, next_gate_up, mark = update_state(
             idx,
             near_gate_up,
             far_gate_up,
@@ -1000,10 +1050,10 @@
             (CUT_ROWS + 8, QKV + width),
             "update_qkv_out",
             (norm_gains, first_gains, second_gains),
-            (one_gate_up,),
+            (mark,),
         )
         one_qkv, one_out, two_qkv, two_out, next_qkv, next_out = updated[:6]
-        one_gains, two_gains, next_gains = updated[6:]
+        one_gains, two_gains, next_gains = updated[6:9]
     else:
         sums = lax.psum((*grad_qkv_out, grad_gate_up[0], grad_down[0].T), ("dp", "shard"))
         grad_qkv_out, grad_gains, grad_gate_up, grad_down = sums

time: 162 us -> 149 us (0.920)
  waiting for transfers between devices: 73.1 us -> 58.1 us
  local copies, waits for them, and re-layouts: 10.5 us -> 1.06 us
  starting transfers between devices: 40.8 us -> 47.9 us
  Pallas kernels: 36.1 us -> 40 us
    ppermute x40 -> x49, waiting for transfers between devices: 73.1 us -> 58.1 us  [swap(): return lax.ppermute(values, axis, [(i, i ^ mask) for i in range(size)])]
    unnamed x52 -> x46, local copies, waits for them, and re-layouts: 10.1 us -> 0.7 us
    ppermute x40 -> x49, starting transfers between devices: 40.8 us -> 47.9 us  [swap(): return lax.ppermute(values, axis, [(i, i ^ mask) for i in range(size)])]
    pallas_call x3, Pallas kernels: 2.47 us -> 6.07 us  [pack_kernel(): pl.pallas_call(kernel, out_shape=tuple(outs), in_specs=[pl.BlockSpec(memo...]
  transfers between devices with their start and end apart: 40 -> 49, of which waited for: 21 -> 19; matrix products, arithmetic and copies ran while one was open for 0% -> 0% of each run, Pallas kernels for 15% -> 22%
where the time goes in v5:
time: 149 us
  waiting for transfers between devices  58.1 us (39%)
  starting transfers between devices  47.9 us (32%)
  Pallas kernels  40 us (27%)
    ppermute x49, waiting for transfers between devices, swap(): return lax.ppermute(values, axis, [(i, i ^ mask) for i in range(size)])  58.1 us
    ppermute x49, starting transfers between devices, swap(): return lax.ppermute(values, axis, [(i, i ^ mask) for i in range(size)])  47.9 us
    pallas_call x5, Pallas kernels, call(): pl.pallas_call(kernel, out_shape=tuple(outs), in_specs=[pl.BlockSpec(memo...  17 us
    pallas_call x3, Pallas kernels, update_state(): pl.pallas_call(kernel, grid_spec=pltpu.PrefetchScalarGridSpec(num_scalar_...  15 us
    pallas_call x3, Pallas kernels, pack_kernel(): pl.pallas_call(kernel, out_shape=tuple(outs), in_specs=[pl.BlockSpec(memo...  6.07 us
  transfers between devices with their start and end apart: 49, of which 19 were waited for; matrix products, arithmetic and copies ran while one was open for 0% of the time, Pallas kernels for 22%

profile of v5, /device:TPU:0, one launch (start us, length us, event | category | flops | bytes accessed | tf_op | source)
XLA Modules:
  0.0 149.0 jit_solution(2452340208601410098)
XLA Ops:
  1.2 2.7 %pack_qkv_out.1 = bf16[160,768]{1,0:T(8,128)(2,1)} custom-call(s32[4]{0:T(128)} %pad_add_fusion.idx_ref.refs_0_, f32[288,960]{1,0:T(8,128)} %refs_2_.5, f32[288,576]{1,0:T(8,128)} %refs_3_.2, f32[2,288]{1,0:T(2,128)} %refs_8_.1), custom_call_target="tpu_custom_call" | custom-call | flops 10000000000 | tf_op jit(solution)/shard_map/pack_qkv_out/pallas_call | solution.py:229
  4.0 3.0 %collective-permute-start = (bf16[160,768]{1,0:T(8,128)(2,1)}, bf16[160,768]{1,0:T(8,128)(2,1)S(1)}, u32[]{:S(2)}, u32[]{:S(2)}) collective-permute-start(bf16[160,768]{1,0:T(8,128)(2,1)} %pack_qkv_out.1), channel_id=1, source_target_pairs={{0,1},{1,0},{2,3},{3,2},{4,5},{5,4},{6,7},{7,6},{8,9},{9,8},{10,11... | collective-permute-start | bytes 737288 | tf_op jit(solution)/shard_map/ppermute | solution.py:666
  7.0 6.2 %collective-permute-done.refs_5_.refs_8_ = bf16[160,768]{1,0:T(8,128)(2,1)S(1)} collective-permute-done((bf16[160,768]{1,0:T(8,128)(2,1)}, bf16[160,768]{1,0:T(8,128)(2,1)S(1)}, u32[]{:S(2)}, u32[]{:S(2)}) %collective-permute-start) | collective-permute-done | bytes 245792 | tf_op jit(solution)/shard_map/ppermute | solution.py:666
  13.2 1.8 %collective-permute-start.1 = (bf16[160,768]{1,0:T(8,128)(2,1)S(1)}, bf16[160,768]{1,0:T(8,128)(2,1)S(1)}, u32[]{:S(2)}, u32[]{:S(2)}) collective-permute-start(bf16[160,768]{1,0:T(8,128)(2,1)S(1)} %collective-permute-done.refs_5_.refs_8_), channel_id=1, source_target_pairs={{0,8},{2,10},{4,12},{6,14},{8,0},{10,2},{12,4},{14,6},{16,24},{18,... | collective-permute-start | bytes 737288 | tf_op jit(solution)/shard_map/ppermute | solution.py:666
  14.9 2.6 %pack_gate_up.1 = (bf16[144,768]{1,0:T(8,128)(2,1)}, bf16[144,768]{1,0:T(8,128)(2,1)}) custom-call(s32[4]{0:T(128)} %pad_add_fusion.idx_ref.refs_0_, f32[288,3072]{1,0:T(8,128)} %refs_4_.4, f32[288,3072]{1,0:T(8,128)} %refs_4_.4), custom_call_target="tpu_custom_call" | custom-call | flops 10000000000 | tf_op jit(solution)/shard_map/pack_gate_up/pallas_call | solution.py:229
  17.6 1.6 %collective-permute-start.4 = (bf16[144,768]{1,0:T(8,128)(2,1)}, bf16[144,768]{1,0:T(8,128)(2,1)S(1)}, u32[]{:S(2)}, u32[]{:S(2)}) collective-permute-start(bf16[144,768]{1,0:T(8,128)(2,1)} %get-tuple-element.109), channel_id=1, source_target_pairs={{0,1},{1,0},{2,3},{3,2},{4,5},{5,4},{6,7},{7,6},{8,9},{9,8},{10,11... | collective-permute-start | bytes 663560 | tf_op jit(solution)/shard_map/ppermute | solution.py:666
  19.7 6.5 %collective-permute-done.4.refs_7_ = bf16[144,768]{1,0:T(8,128)(2,1)S(1)} collective-permute-done((bf16[144,768]{1,0:T(8,128)(2,1)}, bf16[144,768]{1,0:T(8,128)(2,1)S(1)}, u32[]{:S(2)}, u32[]{:S(2)}) %collective-permute-start.4) | collective-permute-done | bytes 221216 | tf_op jit(solution)/shard_map/ppermute | solution.py:666
  26.2 1.5 %collective-permute-start.5 = (bf16[144,768]{1,0:T(8,128)(2,1)S(1)}, bf16[144,768]{1,0:T(8,128)(2,1)S(1)}, u32[]{:S(2)}, u32[]{:S(2)}) collective-permute-start(bf16[144,768]{1,0:T(8,128)(2,1)S(1)} %collective-permute-done.4.refs_7_), channel_id=1, source_target_pairs={{0,4},{2,6},{4,0},{6,2},{8,12},{10,14},{12,8},{14,10},{16,20},{18,... | collective-permute-start | bytes 663560 | tf_op jit(solution)/shard_map/ppermute | solution.py:666
  27.7 0.9 collective-permute-done.8.refs_11_.refs_1_
  30.5 1.5 collective-permute-start.12
  32.1 2.4 %collective-permute-done.9.refs_12_ = bf16[144,768]{1,0:T(8,128)(2,1)S(1)} collective-permute-done((bf16[144,768]{1,0:T(8,128)(2,1)S(1)}, bf16[144,768]{1,0:T(8,128)(2,1)S(1)}, u32[]{:S(2)}, u32[]{:S(2)}) %collective-permute-start.9) | collective-permute-done | bytes 221216 | tf_op jit(solution)/shard_map/ppermute | solution.py:666
  35.2 2.5 %attention.1 = (bf16[128,960]{1,0:T(8,128)(2,1)S(1)}, bf16[128,576]{1,0:T(8,128)(2,1)S(1)}, f32[128,128]{1,0:T(8,128)S(1)}, f32[128,128]{1,0:T(8,128)S(1)}, f32[...) custom-call(s32[4]{0:T(128)S(1)} %copy-done, bf16[576,128]{1,0:T(8,128)(2,1)S(1)} %bitcast.56, ...), custom_call_target="tpu_custom_call" | custom-call | flops 10000000000 | tf_op jit(solution)/shard_map/attention/pallas_call | solution.py:139
  37.8 2.8 %feed_forward.1 = (f32[128,576]{1,0:T(8,128)S(1)}, bf16[128,576]{1,0:T(8,128)(2,1)S(1)}, f32[128,3072]{1,0:T(8,128)S(1)}, bf16[128,1536]{1,0:T(8,128)(2,1)S(1)},...) custom-call(s32[4]{0:T(128)S(1)} %copy-done, ...), custom_call_target="tpu_custom_call" | custom-call | flops 20000000000 | tf_op jit(solution)/shard_map/feed_forward/pallas_call | solution.py:139
  40.6 2.1 %collective-permute-done.12.refs_0_ = bf16[288,768]{1,0:T(8,128)(2,1)S(1)} collective-permute-done((bf16[288,768]{1,0:T(8,128)(2,1)S(1)}, bf16[288,768]{1,0:T(8,128)(2,1)S(1)}, u32[]{:S(2)}, u32[]{:S(2)}) %collective-permute-start.12) | collective-permute-done | bytes 442400 | tf_op jit(solution)/shard_map/ppermute | solution.py:666
  43.3 1.3 collective-permute-done.13.refs_8_
  44.6 3.9 %feed_back.1 = (bf16[128,3072]{1,0:T(8,128)(2,1)S(1)}, bf16[576,128]{1,0:T(8,128)(2,1)}, bf16[2,2,8,72,384]{4,3,2,1,0:T(8,128)(2,1)S(1)}, bf16[2,2,8,72,384]{4,3,2,1,0:T(8,128)(2,1)S(1)}) custom-call(s32[4]{0:T(128)S(1)} %copy-done, f32[128,3072]{1,0:T(8,128)S(1)} %get-tuple-element.111.refs_1_, bf16[128,576]{1,0:T(8,128)(2,1)S(1)} %get-tuple-element.112.refs_1_.refs_2_, ...), custom_call_target="tpu_custom_call" | custom-call | flops 20000000000 | tf_op jit(solution)/shard_map/feed_back/pallas_call | solution.py:139
  49.0 1.5 %collective-permute-start.18 = (bf16[8,72,384]{2,1,0:T(8,128)(2,1)S(1)}, bf16[8,72,384]{2,1,0:T(8,128)(2,1)S(1)}, u32[]{:S(2)}, u32[]{:S(2)}) collective-permute-start(bf16[8,72,384]{2,1,0:T(8,128)(2,1)S(1)} %get-tuple-element.135), channel_id=1, source_target_pairs={{0,1},{1,0},{2,3},{3,2},{4,5},{5,4},{6,7},{7,6},{8,9},{9,8},{10,11... | collective-permute-start | bytes 1327112 | tf_op jit(solution)/shard_map/ppermute | solution.py:666
  50.5 2.7 %middle_back.1 = (f32[128,576]{1,0:T(8,128)S(1)}, bf16[128,576]{1,0:T(8,128)(2,1)S(1)}, f32[1,576]{1,0:T(1,128)S(1)}) custom-call(s32[4]{0:T(128)S(1)} %copy-done, bf16[576,128]{1,0:T(8,128)(2,1)S(1)} %bitcast.55, f32[128,576]{1,0:T(8,128)S(1)} %get-tuple-element.114.refs_4_.refs_2_, bf16[128,3072]{1,0:T(8,128)(2,1)S(1)} %get-tuple-element.116.refs_2_.refs_3_, ...), custom_call_target="tpu_custom_call" | custom-call | flops 20000000000 | tf_op jit(solution)/shard_map/middle_back/pallas_call | solution.py:139
  53.9 1.6 %collective-permute-start.16 = (bf16[2,4,72,384]{3,2,1,0:T(8,128)(2,1)S(1)}, bf16[2,4,72,384]{3,2,1,0:T(8,128)(2,1)S(1)}, u32[]{:S(2)}, u32[]{:S(2)}) collective-permute-start(bf16[2,4,72,384]{3,2,1,0:T(8,128)(2,1)S(1)} %get-tuple-element.132), channel_id=1, source_target_pairs={{0,4},{2,6},{4,0},{6,2},{8,12},{10,14},{12,8},{14,10},{16,20},{18,... | collective-permute-start | bytes 1327112 | tf_op jit(solution)/shard_map/ppermute | solution.py:666
  55.4 1.6 %collective-permute-start.17 = (bf16[4,2,72,384]{3,2,1,0:T(8,128)(2,1)S(1)}, bf16[4,2,72,384]{3,2,1,0:T(8,128)(2,1)S(1)}, u32[]{:S(2)}, u32[]{:S(2)}) collective-permute-start(bf16[4,2,72,384]{3,2,1,0:T(8,128)(2,1)S(1)} %get-tuple-element.134), channel_id=1, source_target_pairs={{0,8},{2,10},{4,12},{6,14},{8,0},{10,2},{12,4},{14,6},{16,24},{18,... | collective-permute-start | bytes 1327112 | tf_op jit(solution)/shard_map/ppermute | solution.py:666
  57.0 5.1 %attention_back.1 = (bf16[576,128]{1,0:T(8,128)(2,1)}, bf16[1,2,8,80,384]{4,3,2,1,0:T(8,128)(2,1)S(1)}, bf16[1,2,8,80,384]{4,3,2,1,0:T(8,128)(2,1)S(1)}, f32[8,128]{1,0:T(8,128)S(1)}) custom-call(s32[4]{0:T(128)S(1)} %copy-done, bf16[576,128]{1,0:T(8,128)(2,1)S(1)} %bitcast.58, f32[128,576]{1,0:T(8,128)S(1)} %get-tuple-element.121.refs_4_.refs_2_, ...), custom_call_target="tpu_custom_call" | custom-call | flops 20000000000 | tf_op jit(solution)/shard_map/attention_back/pallas_call | solution.py:139
  63.1 3.9 %collective-permute-done.16 = bf16[2,4,72,384]{3,2,1,0:T(8,128)(2,1)S(1)} collective-permute-done((bf16[2,4,72,384]{3,2,1,0:T(8,128)(2,1)S(1)}, bf16[2,4,72,384]{3,2,1,0:T(8,128)(2,1)S(1)}, u32[]{:S(2)}, u32[]{:S(2)}) %collective-permute-start.16) | collective-permute-done | bytes 442400 | tf_op jit(solution)/shard_map/ppermute | solution.py:666
  67.4 1.6 %collective-permute-start.19 = (bf16[2,2,72,384]{3,2,1,0:T(8,128)(2,1)S(1)}, bf16[2,2,72,384]{3,2,1,0:T(8,128)(2,1)S(1)}, u32[]{:S(2)}, u32[]{:S(2)}) collective-permute-start(bf16[2,2,72,384]{3,2,1,0:T(8,128)(2,1)S(1)} %get-tuple-element.139), channel_id=1, source_target_pairs={{0,8},{2,10},{4,12},{6,14},{8,0},{10,2},{12,4},{14,6},{16,24},{18,... | collective-permute-start | bytes 663560 | tf_op jit(solution)/shard_map/ppermute | solution.py:666
  69.8 1.6 %collective-permute-start.22 = (bf16[2,2,80,384]{3,2,1,0:T(8,128)(2,1)S(1)}, bf16[2,2,80,384]{3,2,1,0:T(8,128)(2,1)S(1)}, u32[]{:S(2)}, u32[]{:S(2)}) collective-permute-start(bf16[2,2,80,384]{3,2,1,0:T(8,128)(2,1)S(1)} %get-tuple-element.145), channel_id=1, source_target_pairs={{0,1},{1,0},{2,3},{3,2},{4,5},{5,4},{6,7},{7,6},{8,9},{9,8},{10,11... | collective-permute-start | bytes 737288 | tf_op jit(solution)/shard_map/ppermute | solution.py:666
  71.4 1.2 collective-permute-start.23
  73.2 1.5 %collective-permute-done.19.refs_1_ = bf16[2,2,72,384]{3,2,1,0:T(8,128)(2,1)S(1)} collective-permute-done((bf16[2,2,72,384]{3,2,1,0:T(8,128)(2,1)S(1)}, bf16[2,2,72,384]{3,2,1,0:T(8,128)(2,1)S(1)}, u32[]{:S(2)}, u32[]{:S(2)}) %collective-permute-start.19) | collective-permute-done | bytes 221216 | tf_op jit(solution)/shard_map/ppermute | solution.py:666
  74.7 2.8 %collective-permute-done.20.refs_3_ = bf16[2,2,72,384]{3,2,1,0:T(8,128)(2,1)S(1)} collective-permute-done((bf16[2,2,72,384]{3,2,1,0:T(8,128)(2,1)S(1)}, bf16[2,2,72,384]{3,2,1,0:T(8,128)(2,1)S(1)}, u32[]{:S(2)}, u32[]{:S(2)}) %collective-permute-start.20) | collective-permute-done | bytes 221216 | tf_op jit(solution)/shard_map/ppermute | solution.py:666
  77.4 2.9 %collective-permute-done.22.refs_5_ = bf16[2,2,80,384]{3,2,1,0:T(8,128)(2,1)S(1)} collective-permute-done((bf16[2,2,80,384]{3,2,1,0:T(8,128)(2,1)S(1)}, bf16[2,2,80,384]{3,2,1,0:T(8,128)(2,1)S(1)}, u32[]{:S(2)}, u32[]{:S(2)}) %collective-permute-start.22) | collective-permute-done | bytes 245792 | tf_op jit(solution)/shard_map/ppermute | solution.py:666
  81.7 1.4 collective-permute-start.27
  83.1 1.5 %collective-permute-start.28 = (bf16[2,80,384]{2,1,0:T(8,128)(2,1)S(1)}, bf16[2,80,384]{2,1,0:T(8,128)(2,1)S(1)}, u32[]{:S(2)}, u32[]{:S(2)}) collective-permute-start(bf16[2,80,384]{2,1,0:T(8,128)(2,1)S(1)} %get-tuple-element.157), channel_id=1, source_target_pairs={{0,1},{1,0},{2,3},{3,2},{4,5},{5,4},{6,7},{7,6},{8,9},{9,8},{10,11... | collective-permute-start | bytes 368648 | tf_op jit(solution)/shard_map/ppermute | solution.py:666
  84.7 2.7 %collective-permute-start.30 = (bf16[72,384]{1,0:T(8,128)(2,1)S(1)}, bf16[72,384]{1,0:T(8,128)(2,1)S(1)}, u32[]{:S(2)}, u32[]{:S(2)}) collective-permute-start(bf16[72,384]{1,0:T(8,128)(2,1)S(1)} %get-tuple-element.160), channel_id=1, source_target_pairs={{0,16},{2,18},{4,20},{6,22},{8,24},{10,26},{12,28},{14,30},{16,0},... | collective-permute-start | bytes 165896 | tf_op jit(solution)/shard_map/ppermute | solution.py:666
  87.3 3.6 %collective-permute-done.30.refs_9_ = bf16[72,384]{1,0:T(8,128)(2,1)S(1)} collective-permute-done((bf16[72,384]{1,0:T(8,128)(2,1)S(1)}, bf16[72,384]{1,0:T(8,128)(2,1)S(1)}, u32[]{:S(2)}, u32[]{:S(2)}) %collective-permute-start.30) | collective-permute-done | bytes 55328 | tf_op jit(solution)/shard_map/ppermute | solution.py:666
  91.2 2.2 %collective-permute-start.31 = (bf16[2,72,384]{2,1,0:T(8,128)(2,1)S(1)}, bf16[2,72,384]{2,1,0:T(8,128)(2,1)S(1)}, u32[]{:S(2)}, u32[]{:S(2)}) collective-permute-start(bf16[2,72,384]{2,1,0:T(8,128)(2,1)S(1)} %get-tuple-element.162), channel_id=1, source_target_pairs={{0,16},{2,18},{4,20},{6,22},{8,24},{10,26},{12,28},{14,30},{16,0},... | collective-permute-start | bytes 331784 | tf_op jit(solution)/shard_map/ppermute | solution.py:666
  94.1 7.6 %collective-permute-done.33.refs_5_ = bf16[72,384]{1,0:T(8,128)(2,1)S(1)} collective-permute-done((bf16[72,384]{1,0:T(8,128)(2,1)S(1)}, bf16[72,384]{1,0:T(8,128)(2,1)S(1)}, u32[]{:S(2)}, u32[]{:S(2)}) %collective-permute-start.33) | collective-permute-done | bytes 55328 | tf_op jit(solution)/shard_map/ppermute | solution.py:666
  101.9 4.4 %collective-permute-start.36 = (bf16[2,72,384]{2,1,0:T(8,128)(2,1)S(1)}, bf16[2,72,384]{2,1,0:T(8,128)(2,1)S(1)}, u32[]{:S(2)}, u32[]{:S(2)}) collective-permute-start(bf16[2,72,384]{2,1,0:T(8,128)(2,1)S(1)} %get-tuple-element.169.refs_4_), channel_id=1, source_target_pairs={{0,8},{2,10},{4,12},{6,14},{8,0},{10,2},{12,4},{14,6},{16,24},{18,... | collective-permute-start | bytes 331784 | tf_op jit(solution)/shard_map/ppermute | solution.py:666
  106.4 6.2 %collective-permute-done.35.refs_3_ = bf16[80,384]{1,0:T(8,128)(2,1)S(1)} collective-permute-done((bf16[80,384]{1,0:T(8,128)(2,1)S(1)}, bf16[80,384]{1,0:T(8,128)(2,1)S(1)}, u32[]{:S(2)}, u32[]{:S(2)}) %collective-permute-start.35) | collective-permute-done | bytes 61472 | tf_op jit(solution)/shard_map/ppermute | solution.py:666
  113.3 1.5 collective-permute-start.37
  115.0 1.5 %collective-permute-start.39 = (bf16[80,384]{1,0:T(8,128)(2,1)S(1)}, bf16[80,384]{1,0:T(8,128)(2,1)S(1)}, u32[]{:S(2)}, u32[]{:S(2)}) collective-permute-start(bf16[80,384]{1,0:T(8,128)(2,1)S(1)} %get-tuple-element.172.refs_4_), channel_id=1, source_target_pairs={{0,16},{2,18},{4,20},{6,22},{8,24},{10,26},{12,28},{14,30},{16,0},... | collective-permute-start | bytes 184328 | tf_op jit(solution)/shard_map/ppermute | solution.py:666
  116.5 3.7 %collective-permute-done.39.refs_5_ = bf16[80,384]{1,0:T(8,128)(2,1)S(1)} collective-permute-done((bf16[80,384]{1,0:T(8,128)(2,1)S(1)}, bf16[80,384]{1,0:T(8,128)(2,1)S(1)}, u32[]{:S(2)}, u32[]{:S(2)}) %collective-permute-start.39) | collective-permute-done | bytes 61472 | tf_op jit(solution)/shard_map/ppermute | solution.py:666
  120.4 1.8 %collective-permute-start.43 = (bf16[2,80,384]{2,1,0:T(8,128)(2,1)S(1)}, bf16[2,80,384]{2,1,0:T(8,128)(2,1)S(1)}, u32[]{:S(2)}, u32[]{:S(2)}) collective-permute-start(bf16[2,80,384]{2,1,0:T(8,128)(2,1)S(1)} %get-tuple-element.174.refs_0_), channel_id=1, source_target_pairs={{0,12},{2,14},{4,8},{6,10},{8,4},{10,6},{12,0},{14,2},{16,28},{18,... | collective-permute-start | bytes 368648 | tf_op jit(solution)/shard_map/ppermute | solution.py:666
  122.5 1.5 collective-permute-start.41
  123.9 1.7 %collective-permute-start.44 = (bf16[2,2,72,384]{3,2,1,0:T(8,128)(2,1)S(1)}, bf16[2,2,72,384]{3,2,1,0:T(8,128)(2,1)S(1)}, u32[]{:S(2)}, u32[]{:S(2)}) collective-permute-start(bf16[2,2,72,384]{3,2,1,0:T(8,128)(2,1)S(1)} %get-tuple-element.175.refs_0_), channel_id=1, source_target_pairs={{0,8},{2,10},{4,12},{6,14},{8,0},{10,2},{12,4},{14,6},{16,24},{18,... | collective-permute-start | bytes 663560 | tf_op jit(solution)/shard_map/ppermute | solution.py:666
  126.2 3.8 %update_down.1 = (f32[576,768]{1,0:T(8,128)}, f32[576,768]{1,0:T(8,128)}, f32[576,768]{1,0:T(8,128)}, f32[8,128]{1,0:T(8,128)S(1)}) custom-call(s32[4]{0:T(128)S(1)} %copy-done, bf16[1,2,4,72,384]{4,3,2,1,0:T(8,128)(2,1)S(1)} %get-tuple-element.177.refs_0_, bf16[1,2,4,72,384]{4,3,2,1,0:T(8,128)(2,1)S(1)} %collective-permute-done.46.refs_1_, ...), custom_call_target="tpu_custom_call" | custom-call | flops 20000000000 | tf_op jit(solution)/shard_map/update_down/pallas_call | solution.py:645
  130.1 3.4 %collective-permute-done.44.refs_1_ = bf16[2,2,72,384]{3,2,1,0:T(8,128)(2,1)S(1)} collective-permute-done((bf16[2,2,72,384]{3,2,1,0:T(8,128)(2,1)S(1)}, bf16[2,2,72,384]{3,2,1,0:T(8,128)(2,1)S(1)}, u32[]{:S(2)}, u32[]{:S(2)}) %collective-permute-start.44) | collective-permute-done | bytes 221216 | tf_op jit(solution)/shard_map/ppermute | solution.py:666
  133.5 0.9 collective-permute-done.45.refs_3_
  135.3 1.7 %collective-permute-done.48.refs_1_.refs_3_ = bf16[2,2,4,72,384]{4,3,2,1,0:T(8,128)(2,1)S(1)} collective-permute-done((bf16[2,2,4,72,384]{4,3,2,1,0:T(8,128)(2,1)S(1)}, bf16[2,2,4,72,384]{4,3,2,1,0:T(8,128)(2,1)S(1)}, u32[]{:S(2)}, u32[]{:S(2)}) %collective-permute-start.48) | collective-permute-done | bytes 884768 | tf_op jit(solution)/shard_map/ppermute | solution.py:666
  137.6 6.5 %update_gate_up.1 = (f32[288,3072]{1,0:T(8,128)}, f32[288,3072]{1,0:T(8,128)}, f32[288,3072]{1,0:T(8,128)}, f32[8,128]{1,0:T(8,128)S(1)}) custom-call(s32[4]{0:T(128)S(1)} %copy-done, bf16[2,2,4,72,384]{4,3,2,1,0:T(8,128)(2,1)S(1)} %share_gate_up.1.refs_4_.refs_0_.refs_2_, bf16[2,2,4,72,384]{4,3,2,1,0:T(8,128)(2,1)S(1)} %collective-permute-done.48.refs_1_.refs_3_, ...), custom_call_target="tpu_custom_call" | custom-call | flops 20000000000 | tf_op jit(solution)/shard_map/update_gate_up/pallas_call | solution.py:645
  144.1 4.7 %update_qkv_out.1 = (f32[288,960]{1,0:T(8,128)}, f32[288,576]{1,0:T(8,128)}, f32[288,960]{1,0:T(8,128)}, f32[288,576]{1,0:T(8,128)}, f32[288,960]{1,0:T(8,128)},...) custom-call(s32[4]{0:T(128)S(1)} %copy-done, ...), custom_call_target="tpu_custom_call" | custom-call | flops 20000000000 | tf_op jit(solution)/shard_map/update_qkv_out/pallas_call | solution.py:645
  (125 shorter events, 14.1 us)
Async XLA Ops:
  4.0 9.2 %collective-permute-start = (bf16[160,768]{1,0:T(8,128)(2,1)}, bf16[160,768]{1,0:T(8,128)(2,1)S(1)}, u32[]{:S(2)}, u32[]{:S(2)}) collective-permute-start(bf16[160,768]{1,0:T(8,128)(2,1)} %pack_qkv_out.1), channel_id=1, source_target_pairs={{0,1},{1,0},{2,3},{3,2},{4,5},{5,4},{6,7},{7,6},{8,9},{9,8},{10,11... | collective-permute-start | bytes 737288 | tf_op jit(solution)/shard_map/ppermute | solution.py:666
  13.2 16.0 %collective-permute-start.1 = (bf16[160,768]{1,0:T(8,128)(2,1)S(1)}, bf16[160,768]{1,0:T(8,128)(2,1)S(1)}, u32[]{:S(2)}, u32[]{:S(2)}) collective-permute-start(bf16[160,768]{1,0:T(8,128)(2,1)S(1)} %collective-permute-done.refs_5_.refs_8_), channel_id=1, source_target_pairs={{0,8},{2,10},{4,12},{6,14},{8,0},{10,2},{12,4},{14,6},{16,24},{18,... | collective-permute-start | bytes 737288 | tf_op jit(solution)/shard_map/ppermute | solution.py:666
  17.6 8.6 %collective-permute-start.4 = (bf16[144,768]{1,0:T(8,128)(2,1)}, bf16[144,768]{1,0:T(8,128)(2,1)S(1)}, u32[]{:S(2)}, u32[]{:S(2)}) collective-permute-start(bf16[144,768]{1,0:T(8,128)(2,1)} %get-tuple-element.109), channel_id=1, source_target_pairs={{0,1},{1,0},{2,3},{3,2},{4,5},{5,4},{6,7},{7,6},{8,9},{9,8},{10,11... | collective-permute-start | bytes 663560 | tf_op jit(solution)/shard_map/ppermute | solution.py:666
  19.2 9.4 %collective-permute-start.8 = (bf16[144,768]{1,0:T(8,128)(2,1)}, bf16[144,768]{1,0:T(8,128)(2,1)S(1)}, u32[]{:S(2)}, u32[]{:S(2)}) collective-permute-start(bf16[144,768]{1,0:T(8,128)(2,1)} %get-tuple-element.110), channel_id=1, source_target_pairs={{0,1},{1,0},{2,3},{3,2},{4,5},{5,4},{6,7},{7,6},{8,9},{9,8},{10,11... | collective-permute-start | bytes 663560 | tf_op jit(solution)/shard_map/ppermute | solution.py:666
  26.2 5.9 %collective-permute-start.5 = (bf16[144,768]{1,0:T(8,128)(2,1)S(1)}, bf16[144,768]{1,0:T(8,128)(2,1)S(1)}, u32[]{:S(2)}, u32[]{:S(2)}) collective-permute-start(bf16[144,768]{1,0:T(8,128)(2,1)S(1)} %collective-permute-done.4.refs_7_), channel_id=1, source_target_pairs={{0,4},{2,6},{4,0},{6,2},{8,12},{10,14},{12,8},{14,10},{16,20},{18,... | collective-permute-start | bytes 663560 | tf_op jit(solution)/shard_map/ppermute | solution.py:666
  28.6 5.9 %collective-permute-start.9 = (bf16[144,768]{1,0:T(8,128)(2,1)S(1)}, bf16[144,768]{1,0:T(8,128)(2,1)S(1)}, u32[]{:S(2)}, u32[]{:S(2)}) collective-permute-start(bf16[144,768]{1,0:T(8,128)(2,1)S(1)} %collective-permute-done.8.refs_11_.refs_1_), channel_id=1, source_target_pairs={{0,8},{2,10},{4,12},{6,14},{8,0},{10,2},{12,4},{14,6},{16,24},{18,... | collective-permute-start | bytes 663560 | tf_op jit(solution)/shard_map/ppermute | solution.py:666
  29.1 5.4 %collective-permute-start.2 = (bf16[160,768]{1,0:T(8,128)(2,1)S(1)}, bf16[160,768]{1,0:T(8,128)(2,1)S(1)}, u32[]{:S(2)}, u32[]{:S(2)}) collective-permute-start(bf16[160,768]{1,0:T(8,128)(2,1)S(1)} %collective-permute-done.refs_5_.refs_8_), channel_id=1, source_target_pairs={{0,2},{2,0},{4,6},{6,4},{8,10},{10,8},{12,14},{14,12},{16,18},{18,... | collective-permute-start | bytes 737288 | tf_op jit(solution)/shard_map/ppermute | solution.py:666
  29.2 5.9 %collective-permute-start.3 = (bf16[160,768]{1,0:T(8,128)(2,1)S(1)}, bf16[160,768]{1,0:T(8,128)(2,1)S(1)}, u32[]{:S(2)}, u32[]{:S(2)}) collective-permute-start(bf16[160,768]{1,0:T(8,128)(2,1)S(1)} %collective-permute-done.1.refs_9_), channel_id=1, source_target_pairs={{0,2},{2,0},{4,6},{6,4},{8,10},{10,8},{12,14},{14,12},{16,18},{18,... | collective-permute-start | bytes 737288 | tf_op jit(solution)/shard_map/ppermute | solution.py:666
  30.5 12.2 %collective-permute-start.12 = (bf16[288,768]{1,0:T(8,128)(2,1)S(1)}, bf16[288,768]{1,0:T(8,128)(2,1)S(1)}, u32[]{:S(2)}, u32[]{:S(2)}) collective-permute-start(bf16[288,768]{1,0:T(8,128)(2,1)S(1)} %pack_down.1), channel_id=1, source_target_pairs={{0,1},{1,0},{2,3},{3,2},{4,5},{5,4},{6,7},{7,6},{8,9},{9,8},{10,11... | collective-permute-start | bytes 1327112 | tf_op jit(solution)/shard_map/ppermute | solution.py:666
  32.1 5.6 %collective-permute-start.6 = (bf16[144,768]{1,0:T(8,128)(2,1)S(1)}, bf16[144,768]{1,0:T(8,128)(2,1)S(1)}, u32[]{:S(2)}, u32[]{:S(2)}) collective-permute-start(bf16[144,768]{1,0:T(8,128)(2,1)S(1)} %collective-permute-done.4.refs_7_), channel_id=1, source_target_pairs={{0,2},{2,0},{4,6},{6,4},{8,10},{10,8},{12,14},{14,12},{16,18},{18,... | collective-permute-start | bytes 663560 | tf_op jit(solution)/shard_map/ppermute | solution.py:666
  34.5 3.2 %collective-permute-start.10 = (bf16[144,768]{1,0:T(8,128)(2,1)S(1)}, bf16[144,768]{1,0:T(8,128)(2,1)S(1)}, u32[]{:S(2)}, u32[]{:S(2)}) collective-permute-start(bf16[144,768]{1,0:T(8,128)(2,1)S(1)} %collective-permute-done.8.refs_11_.refs_1_), channel_id=1, source_target_pairs={{0,2},{2,0},{4,6},{6,4},{8,10},{10,8},{12,14},{14,12},{16,18},{18,... | collective-permute-start | bytes 663560 | tf_op jit(solution)/shard_map/ppermute | solution.py:666
  34.5 3.2 %collective-permute-start.7 = (bf16[144,768]{1,0:T(8,128)(2,1)S(1)}, bf16[144,768]{1,0:T(8,128)(2,1)S(1)}, u32[]{:S(2)}, u32[]{:S(2)}) collective-permute-start(bf16[144,768]{1,0:T(8,128)(2,1)S(1)} %collective-permute-done.5.refs_8_), channel_id=1, source_target_pairs={{0,2},{2,0},{4,6},{6,4},{8,10},{10,8},{12,14},{14,12},{16,18},{18,... | collective-permute-start | bytes 663560 | tf_op jit(solution)/shard_map/ppermute | solution.py:666
  35.1 2.7 %collective-permute-start.11 = (bf16[144,768]{1,0:T(8,128)(2,1)S(1)}, bf16[144,768]{1,0:T(8,128)(2,1)S(1)}, u32[]{:S(2)}, u32[]{:S(2)}) collective-permute-start(bf16[144,768]{1,0:T(8,128)(2,1)S(1)} %collective-permute-done.9.refs_12_), channel_id=1, source_target_pairs={{0,2},{2,0},{4,6},{6,4},{8,10},{10,8},{12,14},{14,12},{16,18},{18,... | collective-permute-start | bytes 663560 | tf_op jit(solution)/shard_map/ppermute | solution.py:666
  42.8 6.0 %collective-permute-start.14 = (bf16[1,2,8,72,384]{4,3,2,1,0:T(8,128)(2,1)S(1)}, bf16[1,2,8,72,384]{4,3,2,1,0:T(8,128)(2,1)S(1)}, u32[]{:S(2)}, u32[]{:S(2)}) collective-permute-start(bf16[1,2,8,72,384]{4,3,2,1,0:T(8,128)(2,1)S(1)} %get-tuple-element.119), channel_id=1, source_target_pairs={{0,2},{2,0},{4,6},{6,4},{8,10},{10,8},{12,14},{14,12},{16,18},{18,... | collective-permute-start | bytes 2654216 | tf_op jit(solution)/shard_map/ppermute | solution.py:666
  48.5 4.8 %collective-permute-start.15 = (bf16[2,2,8,72,384]{4,3,2,1,0:T(8,128)(2,1)S(1)}, bf16[2,2,8,72,384]{4,3,2,1,0:T(8,128)(2,1)S(1)}, u32[]{:S(2)}, u32[]{:S(2)}) collective-permute-start(bf16[2,2,8,72,384]{4,3,2,1,0:T(8,128)(2,1)S(1)} %get-tuple-element.129), channel_id=1, source_target_pairs={{0,2},{2,0},{4,6},{6,4},{8,10},{10,8},{12,14},{14,12},{16,18},{18,... | collective-permute-start | bytes 5308424 | tf_op jit(solution)/shard_map/ppermute | solution.py:666
  49.0 13.1 %collective-permute-start.18 = (bf16[8,72,384]{2,1,0:T(8,128)(2,1)S(1)}, bf16[8,72,384]{2,1,0:T(8,128)(2,1)S(1)}, u32[]{:S(2)}, u32[]{:S(2)}) collective-permute-start(bf16[8,72,384]{2,1,0:T(8,128)(2,1)S(1)} %get-tuple-element.135), channel_id=1, source_target_pairs={{0,1},{1,0},{2,3},{3,2},{4,5},{5,4},{6,7},{7,6},{8,9},{9,8},{10,11... | collective-permute-start | bytes 1327112 | tf_op jit(solution)/shard_map/ppermute | solution.py:666
  53.9 13.1 %collective-permute-start.16 = (bf16[2,4,72,384]{3,2,1,0:T(8,128)(2,1)S(1)}, bf16[2,4,72,384]{3,2,1,0:T(8,128)(2,1)S(1)}, u32[]{:S(2)}, u32[]{:S(2)}) collective-permute-start(bf16[2,4,72,384]{3,2,1,0:T(8,128)(2,1)S(1)} %get-tuple-element.132), channel_id=1, source_target_pairs={{0,4},{2,6},{4,0},{6,2},{8,12},{10,14},{12,8},{14,10},{16,20},{18,... | collective-permute-start | bytes 1327112 | tf_op jit(solution)/shard_map/ppermute | solution.py:666
  55.4 11.9 %collective-permute-start.17 = (bf16[4,2,72,384]{3,2,1,0:T(8,128)(2,1)S(1)}, bf16[4,2,72,384]{3,2,1,0:T(8,128)(2,1)S(1)}, u32[]{:S(2)}, u32[]{:S(2)}) collective-permute-start(bf16[4,2,72,384]{3,2,1,0:T(8,128)(2,1)S(1)} %get-tuple-element.134), channel_id=1, source_target_pairs={{0,8},{2,10},{4,12},{6,14},{8,0},{10,2},{12,4},{14,6},{16,24},{18,... | collective-permute-start | bytes 1327112 | tf_op jit(solution)/shard_map/ppermute | solution.py:666
  62.2 10.4 %collective-permute-start.24 = (bf16[4,72,384]{2,1,0:T(8,128)(2,1)S(1)}, bf16[4,72,384]{2,1,0:T(8,128)(2,1)S(1)}, u32[]{:S(2)}, u32[]{:S(2)}) collective-permute-start(bf16[4,72,384]{2,1,0:T(8,128)(2,1)S(1)} %get-tuple-element.148), channel_id=1, source_target_pairs={{0,4},{2,6},{4,0},{6,2},{8,12},{10,14},{12,8},{14,10},{16,20},{18,... | collective-permute-start | bytes 663560 | tf_op jit(solution)/shard_map/ppermute | solution.py:666
  63.1 6.5 %collective-permute-start.21 = (bf16[1,2,8,80,384]{4,3,2,1,0:T(8,128)(2,1)S(1)}, bf16[1,2,8,80,384]{4,3,2,1,0:T(8,128)(2,1)S(1)}, u32[]{:S(2)}, u32[]{:S(2)}) collective-permute-start(bf16[1,2,8,80,384]{4,3,2,1,0:T(8,128)(2,1)S(1)} %get-tuple-element.143), channel_id=1, source_target_pairs={{0,2},{2,0},{4,6},{6,4},{8,10},{10,8},{12,14},{14,12},{16,18},{18,... | collective-permute-start | bytes 2949128 | tf_op jit(solution)/shard_map/ppermute | solution.py:666
  67.4 7.3 %collective-permute-start.19 = (bf16[2,2,72,384]{3,2,1,0:T(8,128)(2,1)S(1)}, bf16[2,2,72,384]{3,2,1,0:T(8,128)(2,1)S(1)}, u32[]{:S(2)}, u32[]{:S(2)}) collective-permute-start(bf16[2,2,72,384]{3,2,1,0:T(8,128)(2,1)S(1)} %get-tuple-element.139), channel_id=1, source_target_pairs={{0,8},{2,10},{4,12},{6,14},{8,0},{10,2},{12,4},{14,6},{16,24},{18,... | collective-permute-start | bytes 663560 | tf_op jit(solution)/shard_map/ppermute | solution.py:666
  69.1 8.4 %collective-permute-start.20 = (bf16[2,2,72,384]{3,2,1,0:T(8,128)(2,1)S(1)}, bf16[2,2,72,384]{3,2,1,0:T(8,128)(2,1)S(1)}, u32[]{:S(2)}, u32[]{:S(2)}) collective-permute-start(bf16[2,2,72,384]{3,2,1,0:T(8,128)(2,1)S(1)} %get-tuple-element.141), channel_id=1, source_target_pairs={{0,1},{1,0},{2,3},{3,2},{4,5},{5,4},{6,7},{7,6},{8,9},{9,8},{10,11... | collective-permute-start | bytes 663560 | tf_op jit(solution)/shard_map/ppermute | solution.py:666
  69.8 10.5 %collective-permute-start.22 = (bf16[2,2,80,384]{3,2,1,0:T(8,128)(2,1)S(1)}, bf16[2,2,80,384]{3,2,1,0:T(8,128)(2,1)S(1)}, u32[]{:S(2)}, u32[]{:S(2)}) collective-permute-start(bf16[2,2,80,384]{3,2,1,0:T(8,128)(2,1)S(1)} %get-tuple-element.145), channel_id=1, source_target_pairs={{0,1},{1,0},{2,3},{3,2},{4,5},{5,4},{6,7},{7,6},{8,9},{9,8},{10,11... | collective-permute-start | bytes 737288 | tf_op jit(solution)/shard_map/ppermute | solution.py:666
  71.4 8.9 %collective-permute-start.23 = (bf16[2,2,80,384]{3,2,1,0:T(8,128)(2,1)S(1)}, bf16[2,2,80,384]{3,2,1,0:T(8,128)(2,1)S(1)}, u32[]{:S(2)}, u32[]{:S(2)}) collective-permute-start(bf16[2,2,80,384]{3,2,1,0:T(8,128)(2,1)S(1)} %get-tuple-element.147), channel_id=1, source_target_pairs={{0,4},{2,6},{4,0},{6,2},{8,12},{10,14},{12,8},{14,10},{16,20},{18,... | collective-permute-start | bytes 737288 | tf_op jit(solution)/shard_map/ppermute | solution.py:666
  72.6 12.0 %collective-permute-start.29 = (bf16[2,72,384]{2,1,0:T(8,128)(2,1)S(1)}, bf16[2,72,384]{2,1,0:T(8,128)(2,1)S(1)}, u32[]{:S(2)}, u32[]{:S(2)}) collective-permute-start(bf16[2,72,384]{2,1,0:T(8,128)(2,1)S(1)} %get-tuple-element.158), channel_id=1, source_target_pairs={{0,8},{2,10},{4,12},{6,14},{8,0},{10,2},{12,4},{14,6},{16,24},{18,... | collective-permute-start | bytes 331784 | tf_op jit(solution)/shard_map/ppermute | solution.py:666
  80.5 10.4 %collective-permute-start.25 = (bf16[2,72,384]{2,1,0:T(8,128)(2,1)S(1)}, bf16[2,72,384]{2,1,0:T(8,128)(2,1)S(1)}, u32[]{:S(2)}, u32[]{:S(2)}) collective-permute-start(bf16[2,72,384]{2,1,0:T(8,128)(2,1)S(1)} %get-tuple-element.151), channel_id=1, source_target_pairs={{0,1},{1,0},{2,3},{3,2},{4,5},{5,4},{6,7},{7,6},{8,9},{9,8},{10,11... | collective-permute-start | bytes 331784 | tf_op jit(solution)/shard_map/ppermute | solution.py:666
  81.1 9.8 %collective-permute-start.26 = (bf16[2,72,384]{2,1,0:T(8,128)(2,1)S(1)}, bf16[2,72,384]{2,1,0:T(8,128)(2,1)S(1)}, u32[]{:S(2)}, u32[]{:S(2)}) collective-permute-start(bf16[2,72,384]{2,1,0:T(8,128)(2,1)S(1)} %get-tuple-element.153), channel_id=1, source_target_pairs={{0,4},{2,6},{4,0},{6,2},{8,12},{10,14},{12,8},{14,10},{16,20},{18,... | collective-permute-start | bytes 331784 | tf_op jit(solution)/shard_map/ppermute | solution.py:666
  81.7 9.2 %collective-permute-start.27 = (bf16[2,80,384]{2,1,0:T(8,128)(2,1)S(1)}, bf16[2,80,384]{2,1,0:T(8,128)(2,1)S(1)}, u32[]{:S(2)}, u32[]{:S(2)}) collective-permute-start(bf16[2,80,384]{2,1,0:T(8,128)(2,1)S(1)} %get-tuple-element.155), channel_id=1, source_target_pairs={{0,4},{2,6},{4,0},{6,2},{8,12},{10,14},{12,8},{14,10},{16,20},{18,... | collective-permute-start | bytes 368648 | tf_op jit(solution)/shard_map/ppermute | solution.py:666
  83.1 7.8 %collective-permute-start.28 = (bf16[2,80,384]{2,1,0:T(8,128)(2,1)S(1)}, bf16[2,80,384]{2,1,0:T(8,128)(2,1)S(1)}, u32[]{:S(2)}, u32[]{:S(2)}) collective-permute-start(bf16[2,80,384]{2,1,0:T(8,128)(2,1)S(1)} %get-tuple-element.157), channel_id=1, source_target_pairs={{0,1},{1,0},{2,3},{3,2},{4,5},{5,4},{6,7},{7,6},{8,9},{9,8},{10,11... | collective-permute-start | bytes 368648 | tf_op jit(solution)/shard_map/ppermute | solution.py:666
  84.7 6.3 %collective-permute-start.30 = (bf16[72,384]{1,0:T(8,128)(2,1)S(1)}, bf16[72,384]{1,0:T(8,128)(2,1)S(1)}, u32[]{:S(2)}, u32[]{:S(2)}) collective-permute-start(bf16[72,384]{1,0:T(8,128)(2,1)S(1)} %get-tuple-element.160), channel_id=1, source_target_pairs={{0,16},{2,18},{4,20},{6,22},{8,24},{10,26},{12,28},{14,30},{16,0},... | collective-permute-start | bytes 165896 | tf_op jit(solution)/shard_map/ppermute | solution.py:666
  91.1 10.7 %collective-permute-start.32 = (bf16[2,80,384]{2,1,0:T(8,128)(2,1)S(1)}, bf16[2,80,384]{2,1,0:T(8,128)(2,1)S(1)}, u32[]{:S(2)}, u32[]{:S(2)}) collective-permute-start(bf16[2,80,384]{2,1,0:T(8,128)(2,1)S(1)} %get-tuple-element.164), channel_id=1, source_target_pairs={{0,8},{2,10},{4,12},{6,14},{8,0},{10,2},{12,4},{14,6},{16,24},{18,... | collective-permute-start | bytes 368648 | tf_op jit(solution)/shard_map/ppermute | solution.py:666
  91.2 10.6 %collective-permute-start.31 = (bf16[2,72,384]{2,1,0:T(8,128)(2,1)S(1)}, bf16[2,72,384]{2,1,0:T(8,128)(2,1)S(1)}, u32[]{:S(2)}, u32[]{:S(2)}) collective-permute-start(bf16[2,72,384]{2,1,0:T(8,128)(2,1)S(1)} %get-tuple-element.162), channel_id=1, source_target_pairs={{0,16},{2,18},{4,20},{6,22},{8,24},{10,26},{12,28},{14,30},{16,0},... | collective-permute-start | bytes 331784 | tf_op jit(solution)/shard_map/ppermute | solution.py:666
  93.4 8.4 %collective-permute-start.33 = (bf16[72,384]{1,0:T(8,128)(2,1)S(1)}, bf16[72,384]{1,0:T(8,128)(2,1)S(1)}, u32[]{:S(2)}, u32[]{:S(2)}) collective-permute-start(bf16[72,384]{1,0:T(8,128)(2,1)S(1)} %get-tuple-element.165.refs_4_), channel_id=1, source_target_pairs={{0,16},{2,18},{4,20},{6,22},{8,24},{10,26},{12,28},{14,30},{16,0},... | collective-permute-start | bytes 165896 | tf_op jit(solution)/shard_map/ppermute | solution.py:666
  101.8 10.8 %collective-permute-start.34 = (bf16[2,72,384]{2,1,0:T(8,128)(2,1)S(1)}, bf16[2,72,384]{2,1,0:T(8,128)(2,1)S(1)}, u32[]{:S(2)}, u32[]{:S(2)}) collective-permute-start(bf16[2,72,384]{2,1,0:T(8,128)(2,1)S(1)} %get-tuple-element.166.refs_0_), channel_id=1, source_target_pairs={{0,16},{2,18},{4,20},{6,22},{8,24},{10,26},{12,28},{14,30},{16,0},... | collective-permute-start | bytes 331784 | tf_op jit(solution)/shard_map/ppermute | solution.py:666
  101.9 10.7 %collective-permute-start.36 = (bf16[2,72,384]{2,1,0:T(8,128)(2,1)S(1)}, bf16[2,72,384]{2,1,0:T(8,128)(2,1)S(1)}, u32[]{:S(2)}, u32[]{:S(2)}) collective-permute-start(bf16[2,72,384]{2,1,0:T(8,128)(2,1)S(1)} %get-tuple-element.169.refs_4_), channel_id=1, source_target_pairs={{0,8},{2,10},{4,12},{6,14},{8,0},{10,2},{12,4},{14,6},{16,24},{18,... | collective-permute-start | bytes 331784 | tf_op jit(solution)/shard_map/ppermute | solution.py:666
  106.3 6.3 %collective-permute-start.35 = (bf16[80,384]{1,0:T(8,128)(2,1)S(1)}, bf16[80,384]{1,0:T(8,128)(2,1)S(1)}, u32[]{:S(2)}, u32[]{:S(2)}) collective-permute-start(bf16[80,384]{1,0:T(8,128)(2,1)S(1)} %get-tuple-element.168), channel_id=1, source_target_pairs={{0,16},{2,18},{4,20},{6,22},{8,24},{10,26},{12,28},{14,30},{16,0},... | collective-permute-start | bytes 184328 | tf_op jit(solution)/shard_map/ppermute | solution.py:666
  112.7 7.5 %collective-permute-start.40 = (bf16[2,2,72,384]{3,2,1,0:T(8,128)(2,1)S(1)}, bf16[2,2,72,384]{3,2,1,0:T(8,128)(2,1)S(1)}, u32[]{:S(2)}, u32[]{:S(2)}) collective-permute-start(bf16[2,2,72,384]{3,2,1,0:T(8,128)(2,1)S(1)} %get-tuple-element.173.refs_6_), channel_id=1, source_target_pairs={{0,4},{2,6},{4,0},{6,2},{8,12},{10,14},{12,8},{14,10},{16,20},{18,... | collective-permute-start | bytes 663560 | tf_op jit(solution)/shard_map/ppermute | solution.py:666
  113.3 6.9 %collective-permute-start.37 = (bf16[2,72,384]{2,1,0:T(8,128)(2,1)S(1)}, bf16[2,72,384]{2,1,0:T(8,128)(2,1)S(1)}, u32[]{:S(2)}, u32[]{:S(2)}) collective-permute-start(bf16[2,72,384]{2,1,0:T(8,128)(2,1)S(1)} %get-tuple-element.170.refs_0_), channel_id=1, source_target_pairs={{0,4},{2,6},{4,0},{6,2},{8,12},{10,14},{12,8},{14,10},{16,20},{18,... | collective-permute-start | bytes 331784 | tf_op jit(solution)/shard_map/ppermute | solution.py:666
  114.8 5.4 %collective-permute-start.38 = (bf16[2,72,384]{2,1,0:T(8,128)(2,1)S(1)}, bf16[2,72,384]{2,1,0:T(8,128)(2,1)S(1)}, u32[]{:S(2)}, u32[]{:S(2)}) collective-permute-start(bf16[2,72,384]{2,1,0:T(8,128)(2,1)S(1)} %get-tuple-element.171.refs_2_), channel_id=1, source_target_pairs={{0,8},{2,10},{4,12},{6,14},{8,0},{10,2},{12,4},{14,6},{16,24},{18,... | collective-permute-start | bytes 331784 | tf_op jit(solution)/shard_map/ppermute | solution.py:666
  115.0 5.2 %collective-permute-start.39 = (bf16[80,384]{1,0:T(8,128)(2,1)S(1)}, bf16[80,384]{1,0:T(8,128)(2,1)S(1)}, u32[]{:S(2)}, u32[]{:S(2)}) collective-permute-start(bf16[80,384]{1,0:T(8,128)(2,1)S(1)} %get-tuple-element.172.refs_4_), channel_id=1, source_target_pairs={{0,16},{2,18},{4,20},{6,22},{8,24},{10,26},{12,28},{14,30},{16,0},... | collective-permute-start | bytes 184328 | tf_op jit(solution)/shard_map/ppermute | solution.py:666
  120.3 5.4 %collective-permute-start.46 = (bf16[1,2,4,72,384]{4,3,2,1,0:T(8,128)(2,1)S(1)}, bf16[1,2,4,72,384]{4,3,2,1,0:T(8,128)(2,1)S(1)}, u32[]{:S(2)}, u32[]{:S(2)}) collective-permute-start(bf16[1,2,4,72,384]{4,3,2,1,0:T(8,128)(2,1)S(1)} %get-tuple-element.177.refs_0_), channel_id=1, source_target_pairs={{0,2},{2,0},{4,6},{6,4},{8,10},{10,8},{12,14},{14,12},{16,18},{18,... | collective-permute-start | bytes 1327112 | tf_op jit(solution)/shard_map/ppermute | solution.py:666
  120.4 14.2 %collective-permute-start.43 = (bf16[2,80,384]{2,1,0:T(8,128)(2,1)S(1)}, bf16[2,80,384]{2,1,0:T(8,128)(2,1)S(1)}, u32[]{:S(2)}, u32[]{:S(2)}) collective-permute-start(bf16[2,80,384]{2,1,0:T(8,128)(2,1)S(1)} %get-tuple-element.174.refs_0_), channel_id=1, source_target_pairs={{0,12},{2,14},{4,8},{6,10},{8,4},{10,6},{12,0},{14,2},{16,28},{18,... | collective-permute-start | bytes 368648 | tf_op jit(solution)/shard_map/ppermute | solution.py:666
  122.2 12.4 %collective-permute-start.42 = (bf16[2,80,384]{2,1,0:T(8,128)(2,1)S(1)}, bf16[2,80,384]{2,1,0:T(8,128)(2,1)S(1)}, u32[]{:S(2)}, u32[]{:S(2)}) collective-permute-start(bf16[2,80,384]{2,1,0:T(8,128)(2,1)S(1)} %get-tuple-element.174.refs_0_), channel_id=1, source_target_pairs={{0,8},{2,10},{4,12},{6,14},{8,0},{10,2},{12,4},{14,6},{16,24},{18,... | collective-permute-start | bytes 368648 | tf_op jit(solution)/shard_map/ppermute | solution.py:666
  122.5 12.1 %collective-permute-start.41 = (bf16[2,80,384]{2,1,0:T(8,128)(2,1)S(1)}, bf16[2,80,384]{2,1,0:T(8,128)(2,1)S(1)}, u32[]{:S(2)}, u32[]{:S(2)}) collective-permute-start(bf16[2,80,384]{2,1,0:T(8,128)(2,1)S(1)} %get-tuple-element.174.refs_0_), channel_id=1, source_target_pairs={{0,4},{2,6},{4,0},{6,2},{8,12},{10,14},{12,8},{14,10},{16,20},{18,... | collective-permute-start | bytes 368648 | tf_op jit(solution)/shard_map/ppermute | solution.py:666
  123.9 9.5 %collective-permute-start.44 = (bf16[2,2,72,384]{3,2,1,0:T(8,128)(2,1)S(1)}, bf16[2,2,72,384]{3,2,1,0:T(8,128)(2,1)S(1)}, u32[]{:S(2)}, u32[]{:S(2)}) collective-permute-start(bf16[2,2,72,384]{3,2,1,0:T(8,128)(2,1)S(1)} %get-tuple-element.175.refs_0_), channel_id=1, source_target_pairs={{0,8},{2,10},{4,12},{6,14},{8,0},{10,2},{12,4},{14,6},{16,24},{18,... | collective-permute-start | bytes 663560 | tf_op jit(solution)/shard_map/ppermute | solution.py:666
  125.7 8.7 %collective-permute-start.45 = (bf16[2,2,72,384]{3,2,1,0:T(8,128)(2,1)S(1)}, bf16[2,2,72,384]{3,2,1,0:T(8,128)(2,1)S(1)}, u32[]{:S(2)}, u32[]{:S(2)}) collective-permute-start(bf16[2,2,72,384]{3,2,1,0:T(8,128)(2,1)S(1)} %get-tuple-element.176.refs_2_), channel_id=1, source_target_pairs={{0,4},{2,6},{4,0},{6,2},{8,12},{10,14},{12,8},{14,10},{16,20},{18,... | collective-permute-start | bytes 663560 | tf_op jit(solution)/shard_map/ppermute | solution.py:666
  134.5 2.5 %collective-permute-start.48 = (bf16[2,2,4,72,384]{4,3,2,1,0:T(8,128)(2,1)S(1)}, bf16[2,2,4,72,384]{4,3,2,1,0:T(8,128)(2,1)S(1)}, u32[]{:S(2)}, u32[]{:S(2)}) collective-permute-start(bf16[2,2,4,72,384]{4,3,2,1,0:T(8,128)(2,1)S(1)} %share_gate_up.1.refs_4_.refs_0_.refs_2_), channel_id=1, source_target_pairs={{0,2},{2,0},{4,6},{6,4},{8,10},{10,8},{12,14},{14,12},{16,18},{18,... | collective-permute-start | bytes 2654216 | tf_op jit(solution)/shard_map/ppermute | solution.py:666
  134.8 9.3 %collective-permute-start.47 = (bf16[1,2,4,80,384]{4,3,2,1,0:T(8,128)(2,1)S(1)}, bf16[1,2,4,80,384]{4,3,2,1,0:T(8,128)(2,1)S(1)}, u32[]{:S(2)}, u32[]{:S(2)}) collective-permute-start(bf16[1,2,4,80,384]{4,3,2,1,0:T(8,128)(2,1)S(1)} %share_qkv_out.1.refs_7_.refs_0_), channel_id=1, source_target_pairs={{0,2},{2,0},{4,6},{6,4},{8,10},{10,8},{12,14},{14,12},{16,18},{18,... | collective-permute-start | bytes 1474568 | tf_op jit(solution)/shard_map/ppermute | solution.py:666
  (24 other events, 203.5 us)

commit v6 on v5

--- a/solution.py
+++ b/solution.py
@@ -52,9 +52,9 @@
 def adamw(weight, first_moment, second_moment, gradient, step_rate, weight_decay):
     first_new = BETA_ONE * first_moment + (1.0 - BETA_ONE) * gradient
     second_new = BETA_TWO * second_moment + (1.0 - BETA_TWO) * gradient * gradient
-    fix_one = 1.0 - BETA_ONE**STEP
-    fix_two = 1.0 - BETA_TWO**STEP
-    update = first_new / fix_one / (jnp.sqrt(second_new / fix_two) + EPS_ADAM)
+    fix_one = 1.0 / (1.0 - BETA_ONE**STEP)
+    fix_two = 1.0 / (1.0 - BETA_TWO**STEP)
+    update = first_new * fix_one / (jnp.sqrt(second_new * fix_two) + EPS_ADAM)
     return (first_new, second_new, weight - step_rate * (update + weight_decay * weight))
 
 
@@ -246,17 +246,6 @@
         out[...] = buffer[...].astype(BF16)
 
 
-def pack_gate_up(idx, w_gate_up):
-    shape = (HALF, FF // 2)
-    windows = [
-        (shape, lambda i: (i[1] * HALF, i[2] * (FF // 2))),
-        (shape, lambda i: (i[1] * HALF, FF + (i[3] & 1) * (FF // 2))),
-    ]
-    return pack_kernel(
-        cast_out, idx, [w_gate_up] * 2, windows, [sds(shape, BF16)] * 2, "pack_gate_up"
-    )
-
-
 def pack_down(idx, down_t, after):
     shape = (2 * HALF, down_t.shape[1])
     window = (shape, lambda i: (i[1] * 2 * HALF, 0))
@@ -266,22 +255,25 @@
     )[0]
 
 
-def pack_qkv_out(idx, w_qkv, w_out, norm_gains, after):
+def pack_first(idx, w_qkv, w_out, norm_gains, w_gate_up):
     columns = (QKV + w_out.shape[1]) // 2
+    quarter = FF // 2
     windows = [((HALF, m.shape[1]), lambda i: (i[1] * HALF, 0)) for m in (w_qkv, w_out)]
     windows.append((norm_gains.shape, lambda i: (0, 0)))
+    windows.append(((HALF, quarter), lambda i: (i[1] * HALF, i[2] * quarter)))
+    windows.append(((HALF, quarter), lambda i: (i[1] * HALF, FF + (i[3] & 1) * quarter)))
 
     def body(idx_ref, buffers, outs):
-        q_ref, o_ref, gains_ref = buffers
+        q_ref, o_ref, gains_ref = buffers[:3]
         both = jnp.concatenate([q_ref[:, columns:], o_ref[...]], axis=1)
         outs[0][:HALF, :] = jnp.where((idx_ref[3] & 1) == 0, q_ref[:, :columns], both).astype(BF16)
         outs[0][HALF:, :] = jnp.zeros((16, columns), BF16)
         outs[0][HALF : HALF + 2, : gains_ref.shape[1]] = gains_ref[...].astype(BF16)
-
-    outs = [sds((HALF + 16, columns), BF16)]
-    return pack_kernel(
-        body, idx, [w_qkv, w_out, norm_gains], windows, outs, "pack_qkv_out", after
-    )[0]
+        cast_out(idx_ref, buffers[3:], outs[1:])
+
+    outs = [sds((HALF + 16, columns), BF16)] + [sds((HALF, quarter), BF16)] * 2
+    sources = [w_qkv, w_out, norm_gains, w_gate_up, w_gate_up]
+    return pack_kernel(body, idx, sources, windows, outs, "pack_first")
 
 
 def attention_forward(idx, tokens_t, segments, frequency, gains, w_qkv_out):
@@ -341,7 +333,7 @@
         [w_qkv_out],
         outs,
         [],
-        10,
+        1,
         "attention",
         hand_on=True,
     )
@@ -384,7 +376,7 @@
         [w_qkv_out, w_gate_up],
         outs,
         scratch,
-        20,
+        2,
         "feed_forward",
         after,
         True,
@@ -707,9 +699,8 @@
     frequency = ROPE_BASE ** (-(np.arange(half_size) * 2.0 / HEAD))
     frequency = jnp.asarray(np.tile(frequency, 4)[None], F32)
     if fast:
-        by_x, by_low = pack_gate_up(idx, w_gate_up)
-        by_x, by_low = over_y(by_x), over_y(by_low)
-        qo_near = over_y(pack_qkv_out(idx, w_qkv, w_out, norm_gains, ()))
+        qo_near, by_x, by_low = pack_first(idx, w_qkv, w_out, norm_gains, w_gate_up)
+        qo_near, by_x, by_low = over_y(qo_near), over_y(by_x), over_y(by_low)
         down_near = over_y(pack_down(idx, down_t, (by_low,)))
         by_x_next, by_low_next = over_x(by_x), over_z_low(by_low)
         qo_near_low = over_z_low(qo_near)
@@ -878,19 +869,21 @@
             [(cut(keep_down, 2, 2), cut(arrived_down, 2, 2), 0)], "down_x", (keep_a,)
         )
         arrived_down = over_z_low(send)
-        (send_up, keep_up), (send_low, keep_low), (send_a, keep_a), (send_b, keep_b) = add_step(
+        sums = add_step(
             [
                 (keep_up, arrived_up, 0),
                 (keep_low, arrived_low, 0),
                 (keep_a, arrived_a, 0),
                 (keep_b, arrived_b, 0),
+                (keep_down, arrived_down, 0),
             ],
             "up_z_low_y_qkv_out_xy",
             (keep_down,),
         )
+        (send_up, keep_up), (send_low, keep_low), (send_a, keep_a), (send_b, keep_b) = sums[:4]
+        ((send, keep_down),) = sums[4:]
         arrived_up, arrived_low = over_y(send_up), over_x(send_low)
         arrived_a, arrived_b = over_x(send_a), over_y(send_b)
-        ((send, keep_down),) = add_step([(keep_down, arrived_down, 0)], "down_z_low", (keep_up,))
         arrived_down = over_z_high(send)
 
         def planes(ins, outs):

time: 149 us -> 147 us (0.987)
  Pallas kernels: 40 us -> 37.8 us
    pallas_call x3 -> x2, Pallas kernels: 6.07 us -> 3.97 us  [pack_kernel(): pl.pallas_call(kernel, out_shape=tuple(outs), in_specs=[pl.BlockSpec(memo...]
  transfers between devices with their start and end apart: 49 -> 49, of which waited for: 19 -> 19; matrix products, arithmetic and copies ran while one was open for 0% -> 0% of each run, Pallas kernels for 22% -> 20%
where the time goes in v6:
time: 147 us
  waiting for transfers between devices  58.1 us (40%)
  starting transfers between devices  47.8 us (33%)
  Pallas kernels  37.8 us (26%)
    ppermute x49, waiting for transfers between devices, swap(): return lax.ppermute(values, axis, [(i, i ^ mask) for i in range(size)])  58.1 us
    ppermute x49, starting transfers between devices, swap(): return lax.ppermute(values, axis, [(i, i ^ mask) for i in range(size)])  47.8 us
    pallas_call x5, Pallas kernels, call(): pl.pallas_call(kernel, out_shape=tuple(outs), in_specs=[pl.BlockSpec(memo...  17 us
    pallas_call x3, Pallas kernels, update_state(): pl.pallas_call(kernel, grid_spec=pltpu.PrefetchScalarGridSpec(num_scalar_...  15 us
    pallas_call x2, Pallas kernels, pack_kernel(): pl.pallas_call(kernel, out_shape=tuple(outs), in_specs=[pl.BlockSpec(memo...  3.97 us
  transfers between devices with their start and end apart: 49, of which 19 were waited for; matrix products, arithmetic and copies ran while one was open for 0% of the time, Pallas kernels for 20%

profile of v6, /device:TPU:0, one launch (start us, length us, event | category | flops | bytes accessed | tf_op | source)
XLA Modules:
  0.0 146.7 jit_solution(10069930799496566161)
XLA Ops:
  1.3 3.2 %pack_first.1 = (bf16[160,768]{1,0:T(8,128)(2,1)}, bf16[144,768]{1,0:T(8,128)(2,1)}, bf16[144,768]{1,0:T(8,128)(2,1)}) custom-call(s32[4]{0:T(128)} %pad_add_fusion.idx_ref.refs_0_, f32[288,960]{1,0:T(8,128)} %refs_2_.5, f32[288,576]{1,0:T(8,128)} %refs_3_.4, f32[2,288]{1,0:T(2,128)} %refs_8_.1, f32[288,3072]{1,0:T(8,128)} %refs_4_.6, f32[288,3072]{1,0:T(8,128)} %refs_4_.6), custom_call_target="tpu_custom_call" | custom-call | flops 10000000000 | tf_op jit(solution)/shard_map/pack_first/pallas_call | solution.py:229
  4.4 3.0 %collective-permute-start = (bf16[160,768]{1,0:T(8,128)(2,1)}, bf16[160,768]{1,0:T(8,128)(2,1)S(1)}, u32[]{:S(2)}, u32[]{:S(2)}) collective-permute-start(bf16[160,768]{1,0:T(8,128)(2,1)} %get-tuple-element.107), channel_id=1, source_target_pairs={{0,1},{1,0},{2,3},{3,2},{4,5},{5,4},{6,7},{7,6},{8,9},{9,8},{10,11... | collective-permute-start | bytes 737288 | tf_op jit(solution)/shard_map/ppermute | solution.py:658
  7.5 6.2 %collective-permute-done.refs_5_.refs_8_ = bf16[160,768]{1,0:T(8,128)(2,1)S(1)} collective-permute-done((bf16[160,768]{1,0:T(8,128)(2,1)}, bf16[160,768]{1,0:T(8,128)(2,1)S(1)}, u32[]{:S(2)}, u32[]{:S(2)}) %collective-permute-start) | collective-permute-done | bytes 245792 | tf_op jit(solution)/shard_map/ppermute | solution.py:658
  13.6 1.8 %collective-permute-start.1 = (bf16[160,768]{1,0:T(8,128)(2,1)S(1)}, bf16[160,768]{1,0:T(8,128)(2,1)S(1)}, u32[]{:S(2)}, u32[]{:S(2)}) collective-permute-start(bf16[160,768]{1,0:T(8,128)(2,1)S(1)} %collective-permute-done.refs_5_.refs_8_), channel_id=1, source_target_pairs={{0,8},{2,10},{4,12},{6,14},{8,0},{10,2},{12,4},{14,6},{16,24},{18,... | collective-permute-start | bytes 737288 | tf_op jit(solution)/shard_map/ppermute | solution.py:658
  15.4 1.5 %collective-permute-start.4 = (bf16[144,768]{1,0:T(8,128)(2,1)}, bf16[144,768]{1,0:T(8,128)(2,1)S(1)}, u32[]{:S(2)}, u32[]{:S(2)}) collective-permute-start(bf16[144,768]{1,0:T(8,128)(2,1)} %get-tuple-element.111), channel_id=1, source_target_pairs={{0,1},{1,0},{2,3},{3,2},{4,5},{5,4},{6,7},{7,6},{8,9},{9,8},{10,11... | collective-permute-start | bytes 663560 | tf_op jit(solution)/shard_map/ppermute | solution.py:658
  17.5 6.5 %collective-permute-done.4.refs_7_ = bf16[144,768]{1,0:T(8,128)(2,1)S(1)} collective-permute-done((bf16[144,768]{1,0:T(8,128)(2,1)}, bf16[144,768]{1,0:T(8,128)(2,1)S(1)}, u32[]{:S(2)}, u32[]{:S(2)}) %collective-permute-start.4) | collective-permute-done | bytes 221216 | tf_op jit(solution)/shard_map/ppermute | solution.py:658
  24.0 1.5 %collective-permute-start.5 = (bf16[144,768]{1,0:T(8,128)(2,1)S(1)}, bf16[144,768]{1,0:T(8,128)(2,1)S(1)}, u32[]{:S(2)}, u32[]{:S(2)}) collective-permute-start(bf16[144,768]{1,0:T(8,128)(2,1)S(1)} %collective-permute-done.4.refs_7_), channel_id=1, source_target_pairs={{0,4},{2,6},{4,0},{6,2},{8,12},{10,14},{12,8},{14,10},{16,20},{18,... | collective-permute-start | bytes 663560 | tf_op jit(solution)/shard_map/ppermute | solution.py:658
  25.5 0.9 collective-permute-done.8.refs_11_.refs_1_
  28.3 1.5 %collective-permute-start.12 = (bf16[288,768]{1,0:T(8,128)(2,1)S(1)}, bf16[288,768]{1,0:T(8,128)(2,1)S(1)}, u32[]{:S(2)}, u32[]{:S(2)}) collective-permute-start(bf16[288,768]{1,0:T(8,128)(2,1)S(1)} %pack_down.1), channel_id=1, source_target_pairs={{0,1},{1,0},{2,3},{3,2},{4,5},{5,4},{6,7},{7,6},{8,9},{9,8},{10,11... | collective-permute-start | bytes 1327112 | tf_op jit(solution)/shard_map/ppermute | solution.py:658
  30.0 2.4 %collective-permute-done.9.refs_12_ = bf16[144,768]{1,0:T(8,128)(2,1)S(1)} collective-permute-done((bf16[144,768]{1,0:T(8,128)(2,1)S(1)}, bf16[144,768]{1,0:T(8,128)(2,1)S(1)}, u32[]{:S(2)}, u32[]{:S(2)}) %collective-permute-start.9) | collective-permute-done | bytes 221216 | tf_op jit(solution)/shard_map/ppermute | solution.py:658
  33.0 2.5 %attention.1 = (bf16[128,960]{1,0:T(8,128)(2,1)S(1)}, bf16[128,576]{1,0:T(8,128)(2,1)S(1)}, f32[128,128]{1,0:T(8,128)S(1)}, f32[128,128]{1,0:T(8,128)S(1)}, f32[...) custom-call(s32[4]{0:T(128)S(1)} %copy-done.3, bf16[576,128]{1,0:T(8,128)(2,1)S(1)} %bitcast.45, ...), custom_call_target="tpu_custom_call" | custom-call | flops 1000000000 | tf_op jit(solution)/shard_map/attention/pallas_call | solution.py:139
  35.6 2.8 %feed_forward.1 = (f32[128,576]{1,0:T(8,128)S(1)}, bf16[128,576]{1,0:T(8,128)(2,1)S(1)}, f32[128,3072]{1,0:T(8,128)S(1)}, bf16[128,1536]{1,0:T(8,128)(2,1)S(1)},...) custom-call(s32[4]{0:T(128)S(1)} %copy-done.3, ...), custom_call_target="tpu_custom_call" | custom-call | flops 2000000000 | tf_op jit(solution)/shard_map/feed_forward/pallas_call | solution.py:139
  38.4 2.1 %collective-permute-done.12.refs_0_ = bf16[288,768]{1,0:T(8,128)(2,1)S(1)} collective-permute-done((bf16[288,768]{1,0:T(8,128)(2,1)S(1)}, bf16[288,768]{1,0:T(8,128)(2,1)S(1)}, u32[]{:S(2)}, u32[]{:S(2)}) %collective-permute-start.12) | collective-permute-done | bytes 442400 | tf_op jit(solution)/shard_map/ppermute | solution.py:658
  41.1 1.3 collective-permute-done.13.refs_8_
  42.4 3.9 %feed_back.1 = (bf16[128,3072]{1,0:T(8,128)(2,1)S(1)}, bf16[576,128]{1,0:T(8,128)(2,1)}, bf16[2,2,8,72,384]{4,3,2,1,0:T(8,128)(2,1)S(1)}, bf16[2,2,8,72,384]{4,3,2,1,0:T(8,128)(2,1)S(1)}) custom-call(s32[4]{0:T(128)S(1)} %copy-done.3, f32[128,3072]{1,0:T(8,128)S(1)} %get-tuple-element.113.refs_1_, bf16[128,576]{1,0:T(8,128)(2,1)S(1)} %get-tuple-element.114.refs_1_.refs_2_, ...), custom_call_target="tpu_custom_call" | custom-call | flops 20000000000 | tf_op jit(solution)/shard_map/feed_back/pallas_call | solution.py:139
  46.8 1.5 %collective-permute-start.18 = (bf16[8,72,384]{2,1,0:T(8,128)(2,1)S(1)}, bf16[8,72,384]{2,1,0:T(8,128)(2,1)S(1)}, u32[]{:S(2)}, u32[]{:S(2)}) collective-permute-start(bf16[8,72,384]{2,1,0:T(8,128)(2,1)S(1)} %get-tuple-element.137), channel_id=1, source_target_pairs={{0,1},{1,0},{2,3},{3,2},{4,5},{5,4},{6,7},{7,6},{8,9},{9,8},{10,11... | collective-permute-start | bytes 1327112 | tf_op jit(solution)/shard_map/ppermute | solution.py:658
  48.3 2.7 %middle_back.1 = (f32[128,576]{1,0:T(8,128)S(1)}, bf16[128,576]{1,0:T(8,128)(2,1)S(1)}, f32[1,576]{1,0:T(1,128)S(1)}) custom-call(s32[4]{0:T(128)S(1)} %copy-done.3, bf16[576,128]{1,0:T(8,128)(2,1)S(1)} %bitcast.44, f32[128,576]{1,0:T(8,128)S(1)} %get-tuple-element.116.refs_4_.refs_2_, bf16[128,3072]{1,0:T(8,128)(2,1)S(1)} %get-tuple-element.118.refs_2_.refs_3_, ...), custom_call_target="tpu_custom_call" | custom-call | flops 20000000000 | tf_op jit(solution)/shard_map/middle_back/pallas_call | solution.py:139
  51.7 1.6 %collective-permute-start.16 = (bf16[2,4,72,384]{3,2,1,0:T(8,128)(2,1)S(1)}, bf16[2,4,72,384]{3,2,1,0:T(8,128)(2,1)S(1)}, u32[]{:S(2)}, u32[]{:S(2)}) collective-permute-start(bf16[2,4,72,384]{3,2,1,0:T(8,128)(2,1)S(1)} %get-tuple-element.134), channel_id=1, source_target_pairs={{0,4},{2,6},{4,0},{6,2},{8,12},{10,14},{12,8},{14,10},{16,20},{18,... | collective-permute-start | bytes 1327112 | tf_op jit(solution)/shard_map/ppermute | solution.py:658
  53.2 1.6 %collective-permute-start.17 = (bf16[4,2,72,384]{3,2,1,0:T(8,128)(2,1)S(1)}, bf16[4,2,72,384]{3,2,1,0:T(8,128)(2,1)S(1)}, u32[]{:S(2)}, u32[]{:S(2)}) collective-permute-start(bf16[4,2,72,384]{3,2,1,0:T(8,128)(2,1)S(1)} %get-tuple-element.136), channel_id=1, source_target_pairs={{0,8},{2,10},{4,12},{6,14},{8,0},{10,2},{12,4},{14,6},{16,24},{18,... | collective-permute-start | bytes 1327112 | tf_op jit(solution)/shard_map/ppermute | solution.py:658
  54.8 5.1 %attention_back.1 = (bf16[576,128]{1,0:T(8,128)(2,1)}, bf16[1,2,8,80,384]{4,3,2,1,0:T(8,128)(2,1)S(1)}, bf16[1,2,8,80,384]{4,3,2,1,0:T(8,128)(2,1)S(1)}, f32[8,128]{1,0:T(8,128)S(1)}) custom-call(s32[4]{0:T(128)S(1)} %copy-done.3, bf16[576,128]{1,0:T(8,128)(2,1)S(1)} %bitcast.47, f32[128,576]{1,0:T(8,128)S(1)} %get-tuple-element.123.refs_4_.refs_2_, ...), custom_call_target="tpu_custom_call" | custom-call | flops 20000000000 | tf_op jit(solution)/shard_map/attention_back/pallas_call | solution.py:139
  60.0 0.9 collective-permute-start.24
  60.9 3.9 %collective-permute-done.16 = bf16[2,4,72,384]{3,2,1,0:T(8,128)(2,1)S(1)} collective-permute-done((bf16[2,4,72,384]{3,2,1,0:T(8,128)(2,1)S(1)}, bf16[2,4,72,384]{3,2,1,0:T(8,128)(2,1)S(1)}, u32[]{:S(2)}, u32[]{:S(2)}) %collective-permute-start.16) | collective-permute-done | bytes 442400 | tf_op jit(solution)/shard_map/ppermute | solution.py:658
  65.3 1.6 %collective-permute-start.19 = (bf16[2,2,72,384]{3,2,1,0:T(8,128)(2,1)S(1)}, bf16[2,2,72,384]{3,2,1,0:T(8,128)(2,1)S(1)}, u32[]{:S(2)}, u32[]{:S(2)}) collective-permute-start(bf16[2,2,72,384]{3,2,1,0:T(8,128)(2,1)S(1)} %get-tuple-element.141), channel_id=1, source_target_pairs={{0,8},{2,10},{4,12},{6,14},{8,0},{10,2},{12,4},{14,6},{16,24},{18,... | collective-permute-start | bytes 663560 | tf_op jit(solution)/shard_map/ppermute | solution.py:658
  67.7 1.6 %collective-permute-start.22 = (bf16[2,2,80,384]{3,2,1,0:T(8,128)(2,1)S(1)}, bf16[2,2,80,384]{3,2,1,0:T(8,128)(2,1)S(1)}, u32[]{:S(2)}, u32[]{:S(2)}) collective-permute-start(bf16[2,2,80,384]{3,2,1,0:T(8,128)(2,1)S(1)} %get-tuple-element.147), channel_id=1, source_target_pairs={{0,1},{1,0},{2,3},{3,2},{4,5},{5,4},{6,7},{7,6},{8,9},{9,8},{10,11... | collective-permute-start | bytes 737288 | tf_op jit(solution)/shard_map/ppermute | solution.py:658
  69.2 1.2 collective-permute-start.23
  71.0 1.5 %collective-permute-done.19.refs_1_ = bf16[2,2,72,384]{3,2,1,0:T(8,128)(2,1)S(1)} collective-permute-done((bf16[2,2,72,384]{3,2,1,0:T(8,128)(2,1)S(1)}, bf16[2,2,72,384]{3,2,1,0:T(8,128)(2,1)S(1)}, u32[]{:S(2)}, u32[]{:S(2)}) %collective-permute-start.19) | collective-permute-done | bytes 221216 | tf_op jit(solution)/shard_map/ppermute | solution.py:658
  72.5 2.8 %collective-permute-done.20.refs_3_ = bf16[2,2,72,384]{3,2,1,0:T(8,128)(2,1)S(1)} collective-permute-done((bf16[2,2,72,384]{3,2,1,0:T(8,128)(2,1)S(1)}, bf16[2,2,72,384]{3,2,1,0:T(8,128)(2,1)S(1)}, u32[]{:S(2)}, u32[]{:S(2)}) %collective-permute-start.20) | collective-permute-done | bytes 221216 | tf_op jit(solution)/shard_map/ppermute | solution.py:658
  75.3 2.9 %collective-permute-done.22.refs_5_ = bf16[2,2,80,384]{3,2,1,0:T(8,128)(2,1)S(1)} collective-permute-done((bf16[2,2,80,384]{3,2,1,0:T(8,128)(2,1)S(1)}, bf16[2,2,80,384]{3,2,1,0:T(8,128)(2,1)S(1)}, u32[]{:S(2)}, u32[]{:S(2)}) %collective-permute-start.22) | collective-permute-done | bytes 245792 | tf_op jit(solution)/shard_map/ppermute | solution.py:658
  79.5 1.5 %collective-permute-start.26 = (bf16[2,72,384]{2,1,0:T(8,128)(2,1)S(1)}, bf16[2,72,384]{2,1,0:T(8,128)(2,1)S(1)}, u32[]{:S(2)}, u32[]{:S(2)}) collective-permute-start(bf16[2,72,384]{2,1,0:T(8,128)(2,1)S(1)} %get-tuple-element.154), channel_id=1, source_target_pairs={{0,1},{1,0},{2,3},{3,2},{4,5},{5,4},{6,7},{7,6},{8,9},{9,8},{10,11... | collective-permute-start | bytes 331784 | tf_op jit(solution)/shard_map/ppermute | solution.py:658
  81.1 1.4 collective-permute-start.27
  82.5 2.6 %collective-permute-start.30 = (bf16[72,384]{1,0:T(8,128)(2,1)S(1)}, bf16[72,384]{1,0:T(8,128)(2,1)S(1)}, u32[]{:S(2)}, u32[]{:S(2)}) collective-permute-start(bf16[72,384]{1,0:T(8,128)(2,1)S(1)} %get-tuple-element.162), channel_id=1, source_target_pairs={{0,16},{2,18},{4,20},{6,22},{8,24},{10,26},{12,28},{14,30},{16,0},... | collective-permute-start | bytes 165896 | tf_op jit(solution)/shard_map/ppermute | solution.py:658
  85.0 3.6 %collective-permute-done.30.refs_9_ = bf16[72,384]{1,0:T(8,128)(2,1)S(1)} collective-permute-done((bf16[72,384]{1,0:T(8,128)(2,1)S(1)}, bf16[72,384]{1,0:T(8,128)(2,1)S(1)}, u32[]{:S(2)}, u32[]{:S(2)}) %collective-permute-start.30) | collective-permute-done | bytes 55328 | tf_op jit(solution)/shard_map/ppermute | solution.py:658
  88.9 2.2 %collective-permute-start.31 = (bf16[2,72,384]{2,1,0:T(8,128)(2,1)S(1)}, bf16[2,72,384]{2,1,0:T(8,128)(2,1)S(1)}, u32[]{:S(2)}, u32[]{:S(2)}) collective-permute-start(bf16[2,72,384]{2,1,0:T(8,128)(2,1)S(1)} %get-tuple-element.164), channel_id=1, source_target_pairs={{0,16},{2,18},{4,20},{6,22},{8,24},{10,26},{12,28},{14,30},{16,0},... | collective-permute-start | bytes 331784 | tf_op jit(solution)/shard_map/ppermute | solution.py:658
  91.9 7.6 %collective-permute-done.33.refs_5_ = bf16[72,384]{1,0:T(8,128)(2,1)S(1)} collective-permute-done((bf16[72,384]{1,0:T(8,128)(2,1)S(1)}, bf16[72,384]{1,0:T(8,128)(2,1)S(1)}, u32[]{:S(2)}, u32[]{:S(2)}) %collective-permute-start.33) | collective-permute-done | bytes 55328 | tf_op jit(solution)/shard_map/ppermute | solution.py:658
  99.6 4.4 %collective-permute-start.36 = (bf16[2,72,384]{2,1,0:T(8,128)(2,1)S(1)}, bf16[2,72,384]{2,1,0:T(8,128)(2,1)S(1)}, u32[]{:S(2)}, u32[]{:S(2)}) collective-permute-start(bf16[2,72,384]{2,1,0:T(8,128)(2,1)S(1)} %get-tuple-element.171.refs_4_), channel_id=1, source_target_pairs={{0,8},{2,10},{4,12},{6,14},{8,0},{10,2},{12,4},{14,6},{16,24},{18,... | collective-permute-start | bytes 331784 | tf_op jit(solution)/shard_map/ppermute | solution.py:658
  104.1 6.2 %collective-permute-done.35.refs_3_ = bf16[80,384]{1,0:T(8,128)(2,1)S(1)} collective-permute-done((bf16[80,384]{1,0:T(8,128)(2,1)S(1)}, bf16[80,384]{1,0:T(8,128)(2,1)S(1)}, u32[]{:S(2)}, u32[]{:S(2)}) %collective-permute-start.35) | collective-permute-done | bytes 61472 | tf_op jit(solution)/shard_map/ppermute | solution.py:658
  111.1 1.4 collective-permute-start.37
  112.7 1.5 %collective-permute-start.39 = (bf16[80,384]{1,0:T(8,128)(2,1)S(1)}, bf16[80,384]{1,0:T(8,128)(2,1)S(1)}, u32[]{:S(2)}, u32[]{:S(2)}) collective-permute-start(bf16[80,384]{1,0:T(8,128)(2,1)S(1)} %get-tuple-element.174.refs_4_), channel_id=1, source_target_pairs={{0,16},{2,18},{4,20},{6,22},{8,24},{10,26},{12,28},{14,30},{16,0},... | collective-permute-start | bytes 184328 | tf_op jit(solution)/shard_map/ppermute | solution.py:658
  114.2 3.7 %collective-permute-done.39.refs_5_ = bf16[80,384]{1,0:T(8,128)(2,1)S(1)} collective-permute-done((bf16[80,384]{1,0:T(8,128)(2,1)S(1)}, bf16[80,384]{1,0:T(8,128)(2,1)S(1)}, u32[]{:S(2)}, u32[]{:S(2)}) %collective-permute-start.39) | collective-permute-done | bytes 61472 | tf_op jit(solution)/shard_map/ppermute | solution.py:658
  118.1 1.9 %collective-permute-start.43 = (bf16[2,80,384]{2,1,0:T(8,128)(2,1)S(1)}, bf16[2,80,384]{2,1,0:T(8,128)(2,1)S(1)}, u32[]{:S(2)}, u32[]{:S(2)}) collective-permute-start(bf16[2,80,384]{2,1,0:T(8,128)(2,1)S(1)} %get-tuple-element.176.refs_0_), channel_id=1, source_target_pairs={{0,12},{2,14},{4,8},{6,10},{8,4},{10,6},{12,0},{14,2},{16,28},{18,... | collective-permute-start | bytes 368648 | tf_op jit(solution)/shard_map/ppermute | solution.py:658
  120.2 1.4 collective-permute-start.41
  121.7 1.7 %collective-permute-start.44 = (bf16[2,2,72,384]{3,2,1,0:T(8,128)(2,1)S(1)}, bf16[2,2,72,384]{3,2,1,0:T(8,128)(2,1)S(1)}, u32[]{:S(2)}, u32[]{:S(2)}) collective-permute-start(bf16[2,2,72,384]{3,2,1,0:T(8,128)(2,1)S(1)} %get-tuple-element.177.refs_0_), channel_id=1, source_target_pairs={{0,8},{2,10},{4,12},{6,14},{8,0},{10,2},{12,4},{14,6},{16,24},{18,... | collective-permute-start | bytes 663560 | tf_op jit(solution)/shard_map/ppermute | solution.py:658
  124.0 3.8 %update_down.1 = (f32[576,768]{1,0:T(8,128)}, f32[576,768]{1,0:T(8,128)}, f32[576,768]{1,0:T(8,128)}, f32[8,128]{1,0:T(8,128)S(1)}) custom-call(s32[4]{0:T(128)S(1)} %copy-done.3, bf16[1,2,4,72,384]{4,3,2,1,0:T(8,128)(2,1)S(1)} %get-tuple-element.179.refs_0_, bf16[1,2,4,72,384]{4,3,2,1,0:T(8,128)(2,1)S(1)} %collective-permute-done.46.refs_1_, ...), custom_call_target="tpu_custom_call" | custom-call | flops 20000000000 | tf_op jit(solution)/shard_map/update_down/pallas_call | solution.py:637
  127.9 3.4 %collective-permute-done.44.refs_1_ = bf16[2,2,72,384]{3,2,1,0:T(8,128)(2,1)S(1)} collective-permute-done((bf16[2,2,72,384]{3,2,1,0:T(8,128)(2,1)S(1)}, bf16[2,2,72,384]{3,2,1,0:T(8,128)(2,1)S(1)}, u32[]{:S(2)}, u32[]{:S(2)}) %collective-permute-start.44) | collective-permute-done | bytes 221216 | tf_op jit(solution)/shard_map/ppermute | solution.py:658
  131.3 0.8 collective-permute-done.45.refs_3_
  133.0 1.7 %collective-permute-done.48.refs_1_.refs_3_ = bf16[2,2,4,72,384]{4,3,2,1,0:T(8,128)(2,1)S(1)} collective-permute-done((bf16[2,2,4,72,384]{4,3,2,1,0:T(8,128)(2,1)S(1)}, bf16[2,2,4,72,384]{4,3,2,1,0:T(8,128)(2,1)S(1)}, u32[]{:S(2)}, u32[]{:S(2)}) %collective-permute-start.48) | collective-permute-done | bytes 884768 | tf_op jit(solution)/shard_map/ppermute | solution.py:658
  135.3 6.5 %update_gate_up.1 = (f32[288,3072]{1,0:T(8,128)}, f32[288,3072]{1,0:T(8,128)}, f32[288,3072]{1,0:T(8,128)}, f32[8,128]{1,0:T(8,128)S(1)}) custom-call(s32[4]{0:T(128)S(1)} %copy-done.3, bf16[2,2,4,72,384]{4,3,2,1,0:T(8,128)(2,1)S(1)} %share_gate_up.1.refs_4_.refs_0_.refs_2_, bf16[2,2,4,72,384]{4,3,2,1,0:T(8,128)(2,1)S(1)} %collective-permute-done.48.refs_1_.refs_3_, ...), custom_call_target="tpu_custom_call" | custom-call | flops 20000000000 | tf_op jit(solution)/shard_map/update_gate_up/pallas_call | solution.py:637
  141.8 4.7 %update_qkv_out.1 = (f32[288,960]{1,0:T(8,128)}, f32[288,576]{1,0:T(8,128)}, f32[288,960]{1,0:T(8,128)}, f32[288,576]{1,0:T(8,128)}, f32[288,960]{1,0:T(8,128)},...) custom-call(s32[4]{0:T(128)S(1)} %copy-done.3, ...), custom_call_target="tpu_custom_call" | custom-call | flops 20000000000 | tf_op jit(solution)/shard_map/update_qkv_out/pallas_call | solution.py:637
  (123 shorter events, 13.4 us)
Async XLA Ops:
  4.4 9.2 %collective-permute-start = (bf16[160,768]{1,0:T(8,128)(2,1)}, bf16[160,768]{1,0:T(8,128)(2,1)S(1)}, u32[]{:S(2)}, u32[]{:S(2)}) collective-permute-start(bf16[160,768]{1,0:T(8,128)(2,1)} %get-tuple-element.107), channel_id=1, source_target_pairs={{0,1},{1,0},{2,3},{3,2},{4,5},{5,4},{6,7},{7,6},{8,9},{9,8},{10,11... | collective-permute-start | bytes 737288 | tf_op jit(solution)/shard_map/ppermute | solution.py:658
  13.6 13.3 %collective-permute-start.1 = (bf16[160,768]{1,0:T(8,128)(2,1)S(1)}, bf16[160,768]{1,0:T(8,128)(2,1)S(1)}, u32[]{:S(2)}, u32[]{:S(2)}) collective-permute-start(bf16[160,768]{1,0:T(8,128)(2,1)S(1)} %collective-permute-done.refs_5_.refs_8_), channel_id=1, source_target_pairs={{0,8},{2,10},{4,12},{6,14},{8,0},{10,2},{12,4},{14,6},{16,24},{18,... | collective-permute-start | bytes 737288 | tf_op jit(solution)/shard_map/ppermute | solution.py:658
  15.4 8.6 %collective-permute-start.4 = (bf16[144,768]{1,0:T(8,128)(2,1)}, bf16[144,768]{1,0:T(8,128)(2,1)S(1)}, u32[]{:S(2)}, u32[]{:S(2)}) collective-permute-start(bf16[144,768]{1,0:T(8,128)(2,1)} %get-tuple-element.111), channel_id=1, source_target_pairs={{0,1},{1,0},{2,3},{3,2},{4,5},{5,4},{6,7},{7,6},{8,9},{9,8},{10,11... | collective-permute-start | bytes 663560 | tf_op jit(solution)/shard_map/ppermute | solution.py:658
  17.0 9.4 %collective-permute-start.8 = (bf16[144,768]{1,0:T(8,128)(2,1)}, bf16[144,768]{1,0:T(8,128)(2,1)S(1)}, u32[]{:S(2)}, u32[]{:S(2)}) collective-permute-start(bf16[144,768]{1,0:T(8,128)(2,1)} %get-tuple-element.112), channel_id=1, source_target_pairs={{0,1},{1,0},{2,3},{3,2},{4,5},{5,4},{6,7},{7,6},{8,9},{9,8},{10,11... | collective-permute-start | bytes 663560 | tf_op jit(solution)/shard_map/ppermute | solution.py:658
  24.0 5.9 %collective-permute-start.5 = (bf16[144,768]{1,0:T(8,128)(2,1)S(1)}, bf16[144,768]{1,0:T(8,128)(2,1)S(1)}, u32[]{:S(2)}, u32[]{:S(2)}) collective-permute-start(bf16[144,768]{1,0:T(8,128)(2,1)S(1)} %collective-permute-done.4.refs_7_), channel_id=1, source_target_pairs={{0,4},{2,6},{4,0},{6,2},{8,12},{10,14},{12,8},{14,10},{16,20},{18,... | collective-permute-start | bytes 663560 | tf_op jit(solution)/shard_map/ppermute | solution.py:658
  26.4 5.9 %collective-permute-start.9 = (bf16[144,768]{1,0:T(8,128)(2,1)S(1)}, bf16[144,768]{1,0:T(8,128)(2,1)S(1)}, u32[]{:S(2)}, u32[]{:S(2)}) collective-permute-start(bf16[144,768]{1,0:T(8,128)(2,1)S(1)} %collective-permute-done.8.refs_11_.refs_1_), channel_id=1, source_target_pairs={{0,8},{2,10},{4,12},{6,14},{8,0},{10,2},{12,4},{14,6},{16,24},{18,... | collective-permute-start | bytes 663560 | tf_op jit(solution)/shard_map/ppermute | solution.py:658
  27.0 5.4 %collective-permute-start.2 = (bf16[160,768]{1,0:T(8,128)(2,1)S(1)}, bf16[160,768]{1,0:T(8,128)(2,1)S(1)}, u32[]{:S(2)}, u32[]{:S(2)}) collective-permute-start(bf16[160,768]{1,0:T(8,128)(2,1)S(1)} %collective-permute-done.refs_5_.refs_8_), channel_id=1, source_target_pairs={{0,2},{2,0},{4,6},{6,4},{8,10},{10,8},{12,14},{14,12},{16,18},{18,... | collective-permute-start | bytes 737288 | tf_op jit(solution)/shard_map/ppermute | solution.py:658
  27.0 5.9 %collective-permute-start.3 = (bf16[160,768]{1,0:T(8,128)(2,1)S(1)}, bf16[160,768]{1,0:T(8,128)(2,1)S(1)}, u32[]{:S(2)}, u32[]{:S(2)}) collective-permute-start(bf16[160,768]{1,0:T(8,128)(2,1)S(1)} %collective-permute-done.1.refs_9_), channel_id=1, source_target_pairs={{0,2},{2,0},{4,6},{6,4},{8,10},{10,8},{12,14},{14,12},{16,18},{18,... | collective-permute-start | bytes 737288 | tf_op jit(solution)/shard_map/ppermute | solution.py:658
  28.3 12.2 %collective-permute-start.12 = (bf16[288,768]{1,0:T(8,128)(2,1)S(1)}, bf16[288,768]{1,0:T(8,128)(2,1)S(1)}, u32[]{:S(2)}, u32[]{:S(2)}) collective-permute-start(bf16[288,768]{1,0:T(8,128)(2,1)S(1)} %pack_down.1), channel_id=1, source_target_pairs={{0,1},{1,0},{2,3},{3,2},{4,5},{5,4},{6,7},{7,6},{8,9},{9,8},{10,11... | collective-permute-start | bytes 1327112 | tf_op jit(solution)/shard_map/ppermute | solution.py:658
  30.0 5.6 %collective-permute-start.6 = (bf16[144,768]{1,0:T(8,128)(2,1)S(1)}, bf16[144,768]{1,0:T(8,128)(2,1)S(1)}, u32[]{:S(2)}, u32[]{:S(2)}) collective-permute-start(bf16[144,768]{1,0:T(8,128)(2,1)S(1)} %collective-permute-done.4.refs_7_), channel_id=1, source_target_pairs={{0,2},{2,0},{4,6},{6,4},{8,10},{10,8},{12,14},{14,12},{16,18},{18,... | collective-permute-start | bytes 663560 | tf_op jit(solution)/shard_map/ppermute | solution.py:658
  32.3 3.2 %collective-permute-start.10 = (bf16[144,768]{1,0:T(8,128)(2,1)S(1)}, bf16[144,768]{1,0:T(8,128)(2,1)S(1)}, u32[]{:S(2)}, u32[]{:S(2)}) collective-permute-start(bf16[144,768]{1,0:T(8,128)(2,1)S(1)} %collective-permute-done.8.refs_11_.refs_1_), channel_id=1, source_target_pairs={{0,2},{2,0},{4,6},{6,4},{8,10},{10,8},{12,14},{14,12},{16,18},{18,... | collective-permute-start | bytes 663560 | tf_op jit(solution)/shard_map/ppermute | solution.py:658
  32.4 3.2 %collective-permute-start.7 = (bf16[144,768]{1,0:T(8,128)(2,1)S(1)}, bf16[144,768]{1,0:T(8,128)(2,1)S(1)}, u32[]{:S(2)}, u32[]{:S(2)}) collective-permute-start(bf16[144,768]{1,0:T(8,128)(2,1)S(1)} %collective-permute-done.5.refs_8_), channel_id=1, source_target_pairs={{0,2},{2,0},{4,6},{6,4},{8,10},{10,8},{12,14},{14,12},{16,18},{18,... | collective-permute-start | bytes 663560 | tf_op jit(solution)/shard_map/ppermute | solution.py:658
  32.9 2.7 %collective-permute-start.11 = (bf16[144,768]{1,0:T(8,128)(2,1)S(1)}, bf16[144,768]{1,0:T(8,128)(2,1)S(1)}, u32[]{:S(2)}, u32[]{:S(2)}) collective-permute-start(bf16[144,768]{1,0:T(8,128)(2,1)S(1)} %collective-permute-done.9.refs_12_), channel_id=1, source_target_pairs={{0,2},{2,0},{4,6},{6,4},{8,10},{10,8},{12,14},{14,12},{16,18},{18,... | collective-permute-start | bytes 663560 | tf_op jit(solution)/shard_map/ppermute | solution.py:658
  40.6 6.0 %collective-permute-start.14 = (bf16[1,2,8,72,384]{4,3,2,1,0:T(8,128)(2,1)S(1)}, bf16[1,2,8,72,384]{4,3,2,1,0:T(8,128)(2,1)S(1)}, u32[]{:S(2)}, u32[]{:S(2)}) collective-permute-start(bf16[1,2,8,72,384]{4,3,2,1,0:T(8,128)(2,1)S(1)} %get-tuple-element.121), channel_id=1, source_target_pairs={{0,2},{2,0},{4,6},{6,4},{8,10},{10,8},{12,14},{14,12},{16,18},{18,... | collective-permute-start | bytes 2654216 | tf_op jit(solution)/shard_map/ppermute | solution.py:658
  46.3 4.8 %collective-permute-start.15 = (bf16[2,2,8,72,384]{4,3,2,1,0:T(8,128)(2,1)S(1)}, bf16[2,2,8,72,384]{4,3,2,1,0:T(8,128)(2,1)S(1)}, u32[]{:S(2)}, u32[]{:S(2)}) collective-permute-start(bf16[2,2,8,72,384]{4,3,2,1,0:T(8,128)(2,1)S(1)} %get-tuple-element.131), channel_id=1, source_target_pairs={{0,2},{2,0},{4,6},{6,4},{8,10},{10,8},{12,14},{14,12},{16,18},{18,... | collective-permute-start | bytes 5308424 | tf_op jit(solution)/shard_map/ppermute | solution.py:658
  46.8 13.1 %collective-permute-start.18 = (bf16[8,72,384]{2,1,0:T(8,128)(2,1)S(1)}, bf16[8,72,384]{2,1,0:T(8,128)(2,1)S(1)}, u32[]{:S(2)}, u32[]{:S(2)}) collective-permute-start(bf16[8,72,384]{2,1,0:T(8,128)(2,1)S(1)} %get-tuple-element.137), channel_id=1, source_target_pairs={{0,1},{1,0},{2,3},{3,2},{4,5},{5,4},{6,7},{7,6},{8,9},{9,8},{10,11... | collective-permute-start | bytes 1327112 | tf_op jit(solution)/shard_map/ppermute | solution.py:658
  51.7 13.1 %collective-permute-start.16 = (bf16[2,4,72,384]{3,2,1,0:T(8,128)(2,1)S(1)}, bf16[2,4,72,384]{3,2,1,0:T(8,128)(2,1)S(1)}, u32[]{:S(2)}, u32[]{:S(2)}) collective-permute-start(bf16[2,4,72,384]{3,2,1,0:T(8,128)(2,1)S(1)} %get-tuple-element.134), channel_id=1, source_target_pairs={{0,4},{2,6},{4,0},{6,2},{8,12},{10,14},{12,8},{14,10},{16,20},{18,... | collective-permute-start | bytes 1327112 | tf_op jit(solution)/shard_map/ppermute | solution.py:658
  53.2 11.9 %collective-permute-start.17 = (bf16[4,2,72,384]{3,2,1,0:T(8,128)(2,1)S(1)}, bf16[4,2,72,384]{3,2,1,0:T(8,128)(2,1)S(1)}, u32[]{:S(2)}, u32[]{:S(2)}) collective-permute-start(bf16[4,2,72,384]{3,2,1,0:T(8,128)(2,1)S(1)} %get-tuple-element.136), channel_id=1, source_target_pairs={{0,8},{2,10},{4,12},{6,14},{8,0},{10,2},{12,4},{14,6},{16,24},{18,... | collective-permute-start | bytes 1327112 | tf_op jit(solution)/shard_map/ppermute | solution.py:658
  60.0 10.4 %collective-permute-start.24 = (bf16[4,72,384]{2,1,0:T(8,128)(2,1)S(1)}, bf16[4,72,384]{2,1,0:T(8,128)(2,1)S(1)}, u32[]{:S(2)}, u32[]{:S(2)}) collective-permute-start(bf16[4,72,384]{2,1,0:T(8,128)(2,1)S(1)} %get-tuple-element.150), channel_id=1, source_target_pairs={{0,4},{2,6},{4,0},{6,2},{8,12},{10,14},{12,8},{14,10},{16,20},{18,... | collective-permute-start | bytes 663560 | tf_op jit(solution)/shard_map/ppermute | solution.py:658
  60.9 6.5 %collective-permute-start.21 = (bf16[1,2,8,80,384]{4,3,2,1,0:T(8,128)(2,1)S(1)}, bf16[1,2,8,80,384]{4,3,2,1,0:T(8,128)(2,1)S(1)}, u32[]{:S(2)}, u32[]{:S(2)}) collective-permute-start(bf16[1,2,8,80,384]{4,3,2,1,0:T(8,128)(2,1)S(1)} %get-tuple-element.145), channel_id=1, source_target_pairs={{0,2},{2,0},{4,6},{6,4},{8,10},{10,8},{12,14},{14,12},{16,18},{18,... | collective-permute-start | bytes 2949128 | tf_op jit(solution)/shard_map/ppermute | solution.py:658
  65.3 7.2 %collective-permute-start.19 = (bf16[2,2,72,384]{3,2,1,0:T(8,128)(2,1)S(1)}, bf16[2,2,72,384]{3,2,1,0:T(8,128)(2,1)S(1)}, u32[]{:S(2)}, u32[]{:S(2)}) collective-permute-start(bf16[2,2,72,384]{3,2,1,0:T(8,128)(2,1)S(1)} %get-tuple-element.141), channel_id=1, source_target_pairs={{0,8},{2,10},{4,12},{6,14},{8,0},{10,2},{12,4},{14,6},{16,24},{18,... | collective-permute-start | bytes 663560 | tf_op jit(solution)/shard_map/ppermute | solution.py:658
  66.9 8.4 %collective-permute-start.20 = (bf16[2,2,72,384]{3,2,1,0:T(8,128)(2,1)S(1)}, bf16[2,2,72,384]{3,2,1,0:T(8,128)(2,1)S(1)}, u32[]{:S(2)}, u32[]{:S(2)}) collective-permute-start(bf16[2,2,72,384]{3,2,1,0:T(8,128)(2,1)S(1)} %get-tuple-element.143), channel_id=1, source_target_pairs={{0,1},{1,0},{2,3},{3,2},{4,5},{5,4},{6,7},{7,6},{8,9},{9,8},{10,11... | collective-permute-start | bytes 663560 | tf_op jit(solution)/shard_map/ppermute | solution.py:658
  67.7 10.5 %collective-permute-start.22 = (bf16[2,2,80,384]{3,2,1,0:T(8,128)(2,1)S(1)}, bf16[2,2,80,384]{3,2,1,0:T(8,128)(2,1)S(1)}, u32[]{:S(2)}, u32[]{:S(2)}) collective-permute-start(bf16[2,2,80,384]{3,2,1,0:T(8,128)(2,1)S(1)} %get-tuple-element.147), channel_id=1, source_target_pairs={{0,1},{1,0},{2,3},{3,2},{4,5},{5,4},{6,7},{7,6},{8,9},{9,8},{10,11... | collective-permute-start | bytes 737288 | tf_op jit(solution)/shard_map/ppermute | solution.py:658
  69.2 8.9 %collective-permute-start.23 = (bf16[2,2,80,384]{3,2,1,0:T(8,128)(2,1)S(1)}, bf16[2,2,80,384]{3,2,1,0:T(8,128)(2,1)S(1)}, u32[]{:S(2)}, u32[]{:S(2)}) collective-permute-start(bf16[2,2,80,384]{3,2,1,0:T(8,128)(2,1)S(1)} %get-tuple-element.149), channel_id=1, source_target_pairs={{0,4},{2,6},{4,0},{6,2},{8,12},{10,14},{12,8},{14,10},{16,20},{18,... | collective-permute-start | bytes 737288 | tf_op jit(solution)/shard_map/ppermute | solution.py:658
  70.5 4.8 %collective-permute-start.25 = (bf16[2,72,384]{2,1,0:T(8,128)(2,1)S(1)}, bf16[2,72,384]{2,1,0:T(8,128)(2,1)S(1)}, u32[]{:S(2)}, u32[]{:S(2)}) collective-permute-start(bf16[2,72,384]{2,1,0:T(8,128)(2,1)S(1)} %get-tuple-element.152), channel_id=1, source_target_pairs={{0,8},{2,10},{4,12},{6,14},{8,0},{10,2},{12,4},{14,6},{16,24},{18,... | collective-permute-start | bytes 331784 | tf_op jit(solution)/shard_map/ppermute | solution.py:658
  78.4 10.3 %collective-permute-start.28 = (bf16[2,80,384]{2,1,0:T(8,128)(2,1)S(1)}, bf16[2,80,384]{2,1,0:T(8,128)(2,1)S(1)}, u32[]{:S(2)}, u32[]{:S(2)}) collective-permute-start(bf16[2,80,384]{2,1,0:T(8,128)(2,1)S(1)} %get-tuple-element.158), channel_id=1, source_target_pairs={{0,4},{2,6},{4,0},{6,2},{8,12},{10,14},{12,8},{14,10},{16,20},{18,... | collective-permute-start | bytes 368648 | tf_op jit(solution)/shard_map/ppermute | solution.py:658
  79.0 9.7 %collective-permute-start.29 = (bf16[2,80,384]{2,1,0:T(8,128)(2,1)S(1)}, bf16[2,80,384]{2,1,0:T(8,128)(2,1)S(1)}, u32[]{:S(2)}, u32[]{:S(2)}) collective-permute-start(bf16[2,80,384]{2,1,0:T(8,128)(2,1)S(1)} %get-tuple-element.160), channel_id=1, source_target_pairs={{0,1},{1,0},{2,3},{3,2},{4,5},{5,4},{6,7},{7,6},{8,9},{9,8},{10,11... | collective-permute-start | bytes 368648 | tf_op jit(solution)/shard_map/ppermute | solution.py:658
  79.5 9.1 %collective-permute-start.26 = (bf16[2,72,384]{2,1,0:T(8,128)(2,1)S(1)}, bf16[2,72,384]{2,1,0:T(8,128)(2,1)S(1)}, u32[]{:S(2)}, u32[]{:S(2)}) collective-permute-start(bf16[2,72,384]{2,1,0:T(8,128)(2,1)S(1)} %get-tuple-element.154), channel_id=1, source_target_pairs={{0,1},{1,0},{2,3},{3,2},{4,5},{5,4},{6,7},{7,6},{8,9},{9,8},{10,11... | collective-permute-start | bytes 331784 | tf_op jit(solution)/shard_map/ppermute | solution.py:658
  81.1 7.6 %collective-permute-start.27 = (bf16[2,72,384]{2,1,0:T(8,128)(2,1)S(1)}, bf16[2,72,384]{2,1,0:T(8,128)(2,1)S(1)}, u32[]{:S(2)}, u32[]{:S(2)}) collective-permute-start(bf16[2,72,384]{2,1,0:T(8,128)(2,1)S(1)} %get-tuple-element.156), channel_id=1, source_target_pairs={{0,4},{2,6},{4,0},{6,2},{8,12},{10,14},{12,8},{14,10},{16,20},{18,... | collective-permute-start | bytes 331784 | tf_op jit(solution)/shard_map/ppermute | solution.py:658
  82.5 6.2 %collective-permute-start.30 = (bf16[72,384]{1,0:T(8,128)(2,1)S(1)}, bf16[72,384]{1,0:T(8,128)(2,1)S(1)}, u32[]{:S(2)}, u32[]{:S(2)}) collective-permute-start(bf16[72,384]{1,0:T(8,128)(2,1)S(1)} %get-tuple-element.162), channel_id=1, source_target_pairs={{0,16},{2,18},{4,20},{6,22},{8,24},{10,26},{12,28},{14,30},{16,0},... | collective-permute-start | bytes 165896 | tf_op jit(solution)/shard_map/ppermute | solution.py:658
  88.8 10.7 %collective-permute-start.32 = (bf16[2,80,384]{2,1,0:T(8,128)(2,1)S(1)}, bf16[2,80,384]{2,1,0:T(8,128)(2,1)S(1)}, u32[]{:S(2)}, u32[]{:S(2)}) collective-permute-start(bf16[2,80,384]{2,1,0:T(8,128)(2,1)S(1)} %get-tuple-element.166), channel_id=1, source_target_pairs={{0,8},{2,10},{4,12},{6,14},{8,0},{10,2},{12,4},{14,6},{16,24},{18,... | collective-permute-start | bytes 368648 | tf_op jit(solution)/shard_map/ppermute | solution.py:658
  88.9 10.6 %collective-permute-start.31 = (bf16[2,72,384]{2,1,0:T(8,128)(2,1)S(1)}, bf16[2,72,384]{2,1,0:T(8,128)(2,1)S(1)}, u32[]{:S(2)}, u32[]{:S(2)}) collective-permute-start(bf16[2,72,384]{2,1,0:T(8,128)(2,1)S(1)} %get-tuple-element.164), channel_id=1, source_target_pairs={{0,16},{2,18},{4,20},{6,22},{8,24},{10,26},{12,28},{14,30},{16,0},... | collective-permute-start | bytes 331784 | tf_op jit(solution)/shard_map/ppermute | solution.py:658
  91.1 8.4 %collective-permute-start.33 = (bf16[72,384]{1,0:T(8,128)(2,1)S(1)}, bf16[72,384]{1,0:T(8,128)(2,1)S(1)}, u32[]{:S(2)}, u32[]{:S(2)}) collective-permute-start(bf16[72,384]{1,0:T(8,128)(2,1)S(1)} %get-tuple-element.167.refs_4_), channel_id=1, source_target_pairs={{0,16},{2,18},{4,20},{6,22},{8,24},{10,26},{12,28},{14,30},{16,0},... | collective-permute-start | bytes 165896 | tf_op jit(solution)/shard_map/ppermute | solution.py:658
  99.5 10.8 %collective-permute-start.34 = (bf16[2,72,384]{2,1,0:T(8,128)(2,1)S(1)}, bf16[2,72,384]{2,1,0:T(8,128)(2,1)S(1)}, u32[]{:S(2)}, u32[]{:S(2)}) collective-permute-start(bf16[2,72,384]{2,1,0:T(8,128)(2,1)S(1)} %get-tuple-element.168.refs_0_), channel_id=1, source_target_pairs={{0,16},{2,18},{4,20},{6,22},{8,24},{10,26},{12,28},{14,30},{16,0},... | collective-permute-start | bytes 331784 | tf_op jit(solution)/shard_map/ppermute | solution.py:658
  99.6 10.7 %collective-permute-start.36 = (bf16[2,72,384]{2,1,0:T(8,128)(2,1)S(1)}, bf16[2,72,384]{2,1,0:T(8,128)(2,1)S(1)}, u32[]{:S(2)}, u32[]{:S(2)}) collective-permute-start(bf16[2,72,384]{2,1,0:T(8,128)(2,1)S(1)} %get-tuple-element.171.refs_4_), channel_id=1, source_target_pairs={{0,8},{2,10},{4,12},{6,14},{8,0},{10,2},{12,4},{14,6},{16,24},{18,... | collective-permute-start | bytes 331784 | tf_op jit(solution)/shard_map/ppermute | solution.py:658
  104.0 6.3 %collective-permute-start.35 = (bf16[80,384]{1,0:T(8,128)(2,1)S(1)}, bf16[80,384]{1,0:T(8,128)(2,1)S(1)}, u32[]{:S(2)}, u32[]{:S(2)}) collective-permute-start(bf16[80,384]{1,0:T(8,128)(2,1)S(1)} %get-tuple-element.170), channel_id=1, source_target_pairs={{0,16},{2,18},{4,20},{6,22},{8,24},{10,26},{12,28},{14,30},{16,0},... | collective-permute-start | bytes 184328 | tf_op jit(solution)/shard_map/ppermute | solution.py:658
  110.4 7.5 %collective-permute-start.40 = (bf16[2,2,72,384]{3,2,1,0:T(8,128)(2,1)S(1)}, bf16[2,2,72,384]{3,2,1,0:T(8,128)(2,1)S(1)}, u32[]{:S(2)}, u32[]{:S(2)}) collective-permute-start(bf16[2,2,72,384]{3,2,1,0:T(8,128)(2,1)S(1)} %get-tuple-element.175.refs_6_), channel_id=1, source_target_pairs={{0,4},{2,6},{4,0},{6,2},{8,12},{10,14},{12,8},{14,10},{16,20},{18,... | collective-permute-start | bytes 663560 | tf_op jit(solution)/shard_map/ppermute | solution.py:658
  111.1 6.8 %collective-permute-start.37 = (bf16[2,72,384]{2,1,0:T(8,128)(2,1)S(1)}, bf16[2,72,384]{2,1,0:T(8,128)(2,1)S(1)}, u32[]{:S(2)}, u32[]{:S(2)}) collective-permute-start(bf16[2,72,384]{2,1,0:T(8,128)(2,1)S(1)} %get-tuple-element.172.refs_0_), channel_id=1, source_target_pairs={{0,4},{2,6},{4,0},{6,2},{8,12},{10,14},{12,8},{14,10},{16,20},{18,... | collective-permute-start | bytes 331784 | tf_op jit(solution)/shard_map/ppermute | solution.py:658
  112.5 5.4 %collective-permute-start.38 = (bf16[2,72,384]{2,1,0:T(8,128)(2,1)S(1)}, bf16[2,72,384]{2,1,0:T(8,128)(2,1)S(1)}, u32[]{:S(2)}, u32[]{:S(2)}) collective-permute-start(bf16[2,72,384]{2,1,0:T(8,128)(2,1)S(1)} %get-tuple-element.173.refs_2_), channel_id=1, source_target_pairs={{0,8},{2,10},{4,12},{6,14},{8,0},{10,2},{12,4},{14,6},{16,24},{18,... | collective-permute-start | bytes 331784 | tf_op jit(solution)/shard_map/ppermute | solution.py:658
  112.7 5.2 %collective-permute-start.39 = (bf16[80,384]{1,0:T(8,128)(2,1)S(1)}, bf16[80,384]{1,0:T(8,128)(2,1)S(1)}, u32[]{:S(2)}, u32[]{:S(2)}) collective-permute-start(bf16[80,384]{1,0:T(8,128)(2,1)S(1)} %get-tuple-element.174.refs_4_), channel_id=1, source_target_pairs={{0,16},{2,18},{4,20},{6,22},{8,24},{10,26},{12,28},{14,30},{16,0},... | collective-permute-start | bytes 184328 | tf_op jit(solution)/shard_map/ppermute | solution.py:658
  118.0 5.4 %collective-permute-start.46 = (bf16[1,2,4,72,384]{4,3,2,1,0:T(8,128)(2,1)S(1)}, bf16[1,2,4,72,384]{4,3,2,1,0:T(8,128)(2,1)S(1)}, u32[]{:S(2)}, u32[]{:S(2)}) collective-permute-start(bf16[1,2,4,72,384]{4,3,2,1,0:T(8,128)(2,1)S(1)} %get-tuple-element.179.refs_0_), channel_id=1, source_target_pairs={{0,2},{2,0},{4,6},{6,4},{8,10},{10,8},{12,14},{14,12},{16,18},{18,... | collective-permute-start | bytes 1327112 | tf_op jit(solution)/shard_map/ppermute | solution.py:658
  118.1 14.2 %collective-permute-start.43 = (bf16[2,80,384]{2,1,0:T(8,128)(2,1)S(1)}, bf16[2,80,384]{2,1,0:T(8,128)(2,1)S(1)}, u32[]{:S(2)}, u32[]{:S(2)}) collective-permute-start(bf16[2,80,384]{2,1,0:T(8,128)(2,1)S(1)} %get-tuple-element.176.refs_0_), channel_id=1, source_target_pairs={{0,12},{2,14},{4,8},{6,10},{8,4},{10,6},{12,0},{14,2},{16,28},{18,... | collective-permute-start | bytes 368648 | tf_op jit(solution)/shard_map/ppermute | solution.py:658
  120.0 12.3 %collective-permute-start.42 = (bf16[2,80,384]{2,1,0:T(8,128)(2,1)S(1)}, bf16[2,80,384]{2,1,0:T(8,128)(2,1)S(1)}, u32[]{:S(2)}, u32[]{:S(2)}) collective-permute-start(bf16[2,80,384]{2,1,0:T(8,128)(2,1)S(1)} %get-tuple-element.176.refs_0_), channel_id=1, source_target_pairs={{0,8},{2,10},{4,12},{6,14},{8,0},{10,2},{12,4},{14,6},{16,24},{18,... | collective-permute-start | bytes 368648 | tf_op jit(solution)/shard_map/ppermute | solution.py:658
  120.2 12.1 %collective-permute-start.41 = (bf16[2,80,384]{2,1,0:T(8,128)(2,1)S(1)}, bf16[2,80,384]{2,1,0:T(8,128)(2,1)S(1)}, u32[]{:S(2)}, u32[]{:S(2)}) collective-permute-start(bf16[2,80,384]{2,1,0:T(8,128)(2,1)S(1)} %get-tuple-element.176.refs_0_), channel_id=1, source_target_pairs={{0,4},{2,6},{4,0},{6,2},{8,12},{10,14},{12,8},{14,10},{16,20},{18,... | collective-permute-start | bytes 368648 | tf_op jit(solution)/shard_map/ppermute | solution.py:658
  121.7 9.6 %collective-permute-start.44 = (bf16[2,2,72,384]{3,2,1,0:T(8,128)(2,1)S(1)}, bf16[2,2,72,384]{3,2,1,0:T(8,128)(2,1)S(1)}, u32[]{:S(2)}, u32[]{:S(2)}) collective-permute-start(bf16[2,2,72,384]{3,2,1,0:T(8,128)(2,1)S(1)} %get-tuple-element.177.refs_0_), channel_id=1, source_target_pairs={{0,8},{2,10},{4,12},{6,14},{8,0},{10,2},{12,4},{14,6},{16,24},{18,... | collective-permute-start | bytes 663560 | tf_op jit(solution)/shard_map/ppermute | solution.py:658
  123.4 8.7 %collective-permute-start.45 = (bf16[2,2,72,384]{3,2,1,0:T(8,128)(2,1)S(1)}, bf16[2,2,72,384]{3,2,1,0:T(8,128)(2,1)S(1)}, u32[]{:S(2)}, u32[]{:S(2)}) collective-permute-start(bf16[2,2,72,384]{3,2,1,0:T(8,128)(2,1)S(1)} %get-tuple-element.178.refs_2_), channel_id=1, source_target_pairs={{0,4},{2,6},{4,0},{6,2},{8,12},{10,14},{12,8},{14,10},{16,20},{18,... | collective-permute-start | bytes 663560 | tf_op jit(solution)/shard_map/ppermute | solution.py:658
  132.2 2.5 %collective-permute-start.48 = (bf16[2,2,4,72,384]{4,3,2,1,0:T(8,128)(2,1)S(1)}, bf16[2,2,4,72,384]{4,3,2,1,0:T(8,128)(2,1)S(1)}, u32[]{:S(2)}, u32[]{:S(2)}) collective-permute-start(bf16[2,2,4,72,384]{4,3,2,1,0:T(8,128)(2,1)S(1)} %share_gate_up.1.refs_4_.refs_0_.refs_2_), channel_id=1, source_target_pairs={{0,2},{2,0},{4,6},{6,4},{8,10},{10,8},{12,14},{14,12},{16,18},{18,... | collective-permute-start | bytes 2654216 | tf_op jit(solution)/shard_map/ppermute | solution.py:658
  132.5 9.3 %collective-permute-start.47 = (bf16[1,2,4,80,384]{4,3,2,1,0:T(8,128)(2,1)S(1)}, bf16[1,2,4,80,384]{4,3,2,1,0:T(8,128)(2,1)S(1)}, u32[]{:S(2)}, u32[]{:S(2)}) collective-permute-start(bf16[1,2,4,80,384]{4,3,2,1,0:T(8,128)(2,1)S(1)} %share_qkv_out.1.refs_7_.refs_0_), channel_id=1, source_target_pairs={{0,2},{2,0},{4,6},{6,4},{8,10},{10,8},{12,14},{14,12},{16,18},{18,... | collective-permute-start | bytes 1474568 | tf_op jit(solution)/shard_map/ppermute | solution.py:658
  (24 other events, 204.5 us)

commit v7 on v6

--- a/solution.py
+++ b/solution.py
@@ -383,39 +383,49 @@
     )
 
 
-def feed_back(idx, ab, normed_low, hidden, middle, cotangent_t, down_t, pieces):
+def feed_back(idx, ab, normed_low, cotangent_t, down_t, pieces):
     width, seq_length = cotangent_t.shape
 
     def body(idx_ref, arrays, loads, outs, scratch):
-        ab_ref, h2_ref, z_ref, u_ref, y_ref = arrays
-        gg_ref, out_ref = outs[:2]
-        down = loads[0]()
+        ab_ref, h2_ref, y_ref = arrays
+        gg_ref = outs[0]
         gate, up = ab_ref[:, :FF], ab_ref[:, FF:]
         sig = jax.nn.sigmoid(gate)
-        grad_hidden = dot_left_t(y_ref[...], down[...])
+        grad_hidden = dot_left_t(y_ref[...], loads[0]()[...])
         gg_ref[:, :FF] = (grad_hidden * up * sig * (1.0 + gate * (1.0 - sig))).astype(BF16)
         gg_ref[:, FF:] = (grad_hidden * gate * sig).astype(BF16)
         grad = dot_left_t(h2_ref[...], gg_ref[...])
         if pieces is None:
-            outs[2][...] = grad
+            outs[1][...] = grad
         else:
             pieces.store(scratch[0], grad)
-            pieces.emit(idx_ref, scratch[0], outs[2:])
-        out_ref[...] = (u_ref[...] + dot_right_t(z_ref[...], down[...])).T.astype(BF16)
-
-    outs = [sds((seq_length, 2 * FF), BF16), sds((width, seq_length), BF16)]
+            pieces.emit(idx_ref, scratch[0], outs[1:])
+
+    outs = [sds((seq_length, 2 * FF), BF16)]
     outs += [sds((width, 2 * FF), F32)] if pieces is None else pieces.outs()
     scratch = [] if pieces is None else [pieces.scratch(2 * FF)]
     return call(
         body,
         idx,
-        [ab, normed_low, hidden, middle, cotangent_t],
+        [ab, normed_low, cotangent_t],
         [down_t],
         outs,
         scratch,
         20,
         "feed_back",
-    )
+        hand_on=True,
+    )
+
+
+def layer_output(middle, hidden, down_t, after):
+    seq_length, width = middle.shape
+
+    def body(ins, outs):
+        outs[0][...] = (ins[0][...] + dot_right_t(ins[1][...], ins[2][...])).T.astype(BF16)
+
+    return step(
+        body, [middle, hidden, down_t], [sds((width, seq_length), BF16)], "layer_output", after, 2
+    )[0]
 
 
 def middle_back(idx, cotangent_t, middle, gated, gains, w_gate_up, w_qkv_out, after):
@@ -540,7 +550,7 @@
     )
 
 
-def step(body, arrays, outs, name, after=()):
+def step(body, arrays, outs, name, after=(), busy=20):
     def kernel(*refs):
         body(refs[: len(arrays)], refs[len(arrays) + len(after) :])
 
@@ -551,9 +561,13 @@
         + [pl.BlockSpec(memory_space=pl.ANY)] * len(after),
         out_specs=tuple([pl.BlockSpec(memory_space=pltpu.VMEM)] * len(outs)),
         compiler_params=pltpu.CompilerParams(vmem_limit_bytes=VMEM_LIMIT),
-        cost_estimate=busy_for(20),
+        cost_estimate=busy_for(busy),
         name=name,
     )(*arrays, *after)
+
+
+def pass_on(ins, outs):
+    outs[0][...] = ins[0][...]
 
 
 def add_split(keep, arrived, axis, send_ref, keep_ref):
@@ -578,79 +592,85 @@
     return [(flat[2 * i], flat[2 * i + 1]) for i in range(len(jobs))]
 
 
-def update_state(idx, near, far, parts, blocks, puts, state, shape, name, gains=(), after=()):
+def update_half(idx, far, pieces, place, height, state, earlier, gains, name, after):
     count = len(state) // 3
-    height, width = near.shape[3:]
+    columns = [a.shape[1] for a in state[:count]]
+    chunks = height // CUT_ROWS
+    order = [(k, count + k, 2 * count + k) for k in range(count)]
 
     def kernel(idx_ref, *refs):
-        part_refs, refs = refs[: 2 * len(parts)], refs[2 * len(parts) :]
-        state_refs, refs = refs[: 3 * count], refs[3 * count :]
-        gain_refs, refs = refs[: len(gains)], refs[len(gains) + len(after) :]
-        outs, refs = refs[: 3 * count], refs[3 * count :]
-        gain_outs, mark, full = refs[: len(gains)], refs[-2], refs[-1]
+        refs = list(refs)
+        take = lambda n: [refs.pop(0) for _ in range(n)]
+        (piece_ref,) = take(1)
+        state_refs, gain_refs = take(3 * count), take(len(gains))
+        take(len(earlier) + len(after))
+        outs, gain_outs, (mark,) = take(3 * count), take(len(gains)), take(1)
+        buffers, (full, sem) = take(3 * count), refs
         mark[...] = jnp.zeros_like(mark)
-        is_near = pl.program_id(0) % 2 == idx_ref[1]
-        for i, put in enumerate(puts):
-            for z in range(4):
-                rel = z ^ idx_ref[3]
-                slot = (rel & 1) * 2 + (rel >> 1)
-                piece = jnp.where(
-                    is_near,
-                    part_refs[2 * i][0, 0, slot].astype(F32),
-                    part_refs[2 * i + 1][0, 0, slot].astype(F32),
+        for part in range(pieces.shape[0]):
+            for x in range(2):
+                for slot in range(4):
+                    z = (slot >> 1) | ((slot & 1) << 1)
+                    row, column = place(part, idx_ref[2] ^ x, idx_ref[3] ^ z)
+                    rows = pl.ds(pl.multiple_of(row, 8), CUT_ROWS)
+                    where = pl.ds(pl.multiple_of(column, LANES), CUT_COLUMNS)
+                    full[rows, where] = piece_ref[part, x, slot, :CUT_ROWS, :].astype(F32)
+        base = (idx_ref[1] ^ far) * height
+        copies = []
+        for chunk in range(chunks):
+
+            def eight_rows(i, carry, chunk=chunk):
+                near_rows = pl.ds(pl.multiple_of(chunk * CUT_ROWS + i * 8, 8), 8)
+                rows = pl.ds(pl.multiple_of(base + chunk * CUT_ROWS + i * 8, 8), 8)
+                start = 0
+                for k in range(count):
+                    for at in range(0, columns[k], 768):
+                        size = min(768, columns[k] - at)
+                        where = slice(at, at + size)
+                        results = adamw(
+                            *[state_refs[j][rows, where] for j in order[k]],
+                            full[near_rows, start + at : start + at + size],
+                            RATE_MATRIX,
+                            DECAY_MATRIX,
+                        )
+                        for j, result in zip(order[k], results):
+                            buffers[j][near_rows, where] = result
+                    start += columns[k]
+                return carry
+
+            lax.fori_loop(0, CUT_ROWS // 8, eight_rows, 0)
+            near_rows = pl.ds(chunk * CUT_ROWS, CUT_ROWS)
+            rows = pl.ds(pl.multiple_of(base + chunk * CUT_ROWS, 8), CUT_ROWS)
+            for j in range(3 * count):
+                copy = pltpu.make_async_copy(
+                    buffers[j].at[near_rows], outs[j].at[rows], sem.at[chunk, j]
                 )
-                put(full, z, piece)
-        start = 0
-        for i in range(count):
-            columns = state_refs[i].shape[1]
-            first, second, new = adamw(
-                state_refs[i][...],
-                state_refs[count + i][...],
-                state_refs[2 * count + i][...],
-                full[: state_refs[i].shape[0], start : start + columns],
-                RATE_MATRIX,
-                DECAY_MATRIX,
-            )
-            start += columns
-            outs[i][...] = first
-            outs[count + i][...] = second
-            outs[2 * count + i][...] = new
+                copy.start()
+                copies.append(copy)
         if gains:
-
-            @pl.when(pl.program_id(0) == 0)
-            def _():
-                gradient = full[CUT_ROWS : CUT_ROWS + 2, : gain_refs[0].shape[1]]
-                first, second, new = adamw(
-                    gain_refs[0][...], gain_refs[1][...], gain_refs[2][...], gradient, RATE_GAIN, 0.0
-                )
-                gain_outs[0][...] = first
-                gain_outs[1][...] = second
-                gain_outs[2][...] = new
-
-    state_specs = [pl.BlockSpec(*blocks[i]) for i in range(count)] * 3
-    gain_specs = [pl.BlockSpec(g.shape, lambda t, _: (0, 0)) for g in gains]
-    part_specs = [
-        pl.BlockSpec((1, 1, 4, height, width), lambda t, i, p=p: (p, (t // 2) ^ i[2], 0, 0, 0))
-        for p in parts
-        for _ in range(2)
-    ]
+            gradient = piece_ref[0, 0, 0, CUT_ROWS:, :].astype(F32)[:2, : gains[0].shape[1]]
+            results = adamw(*[g[...] for g in gain_refs], gradient, RATE_GAIN, 0.0)
+            for out, result in zip(gain_outs, results):
+                out[...] = result
+        for copy in copies:
+            copy.wait()
+
+    vmem, anywhere = pl.BlockSpec(memory_space=pltpu.VMEM), pl.BlockSpec(memory_space=pl.ANY)
+    first_earlier = 2 + 3 * count + len(gains)
     return pl.pallas_call(
         kernel,
-        grid_spec=pltpu.PrefetchScalarGridSpec(
-            num_scalar_prefetch=1,
-            grid=(4,),
-            in_specs=part_specs
-            + state_specs
-            + gain_specs
-            + [pl.BlockSpec(memory_space=pl.ANY)] * len(after),
-            out_specs=tuple(state_specs + gain_specs + [pl.BlockSpec(MARK, lambda t, _: (0, 0))]),
-            scratch_shapes=[pltpu.VMEM(shape, F32)],
-        ),
         out_shape=tuple(sds(a.shape, F32) for a in [*state, *gains]) + (sds(MARK, F32),),
+        in_specs=[pl.BlockSpec(memory_space=pltpu.SMEM)]
+        + [vmem] * (1 + 3 * count + len(gains))
+        + [anywhere] * (len(earlier) + len(after)),
+        out_specs=tuple([anywhere] * (3 * count) + [vmem] * (len(gains) + 1)),
+        scratch_shapes=[pltpu.VMEM((height, a.shape[1]), F32) for a in state]
+        + [pltpu.VMEM((height, sum(columns)), F32), pltpu.SemaphoreType.DMA((chunks, 3 * count))],
+        input_output_aliases={first_earlier + i: i for i in range(len(earlier))},
         compiler_params=pltpu.CompilerParams(vmem_limit_bytes=VMEM_LIMIT),
         cost_estimate=busy_for(20),
         name=name,
-    )(idx, *[near, far] * len(parts), *state, *gains, *after)
+    )(idx, pieces, *state, *gains, *earlier, *after)
 
 
 def swap(values, axis, mask):
@@ -705,6 +725,9 @@
         by_x_next, by_low_next = over_x(by_x), over_z_low(by_low)
         qo_near_low = over_z_low(qo_near)
         gains = (norm_gains, qo_near)
+        (low_far,) = step(
+            pass_on, [over_core(by_low_next)], [sds(by_low.shape, BF16)], "pass_on_low", (), 1
+        )
         own_rows = lambda o: (o * rows, 0)
         own_rows_out = lambda o: (o * rows, QKV)
         qo_place = lambda o, c, x, low: (o * rows + c * HALF, low * ((QKV + width) // 2))
@@ -731,7 +754,7 @@
                 (by_low, (0, 0, 0), low_place),
                 (by_low_next, (0, 0, 1), low_place),
                 (over_core(by_low), (1, 0, 0), low_place),
-                (over_core(by_low_next), (1, 0, 1), low_place),
+                (low_far, (1, 0, 1), low_place),
             ],
         )
         cut_qkv_out = Pieces(lambda o, c, x, z, p: (o * 4 + c * 2 + x, z), extra=8)
@@ -764,9 +787,6 @@
         whole = grad_down.pop()
         mat_gate_up = Weight(whole.shape, whole=whole)
 
-        def pass_on(ins, outs):
-            outs[0][...] = ins[0][...]
-
         (down_near,) = step(
             pass_on, [down_near], [sds(down_near.shape, BF16)], "pass_on", (normed_low,)
         )
@@ -781,10 +801,11 @@
         )
     if fast:
         arrived_down = over_core(grad_down[0])
-    gated, output, *grad_gate_up = feed_back(
-        idx, ab, normed_low, hidden, middle, y_t, mat_down, cut_gate_up
-    )
+    gated, *grad_gate_up = feed_back(idx, ab, normed_low, y_t, mat_down, cut_gate_up)
+    if not fast:
+        output = layer_output(middle, hidden, mat_down.arrays[0], ())
     if fast:
+        down_whole = grad_gate_up.pop()
         cut = lambda a, *lead: a.reshape(*lead, *a.shape[-2:])
         arrived_gate_up = over_core(grad_gate_up[0])
         ((send, keep_down),) = add_step(
@@ -821,18 +842,6 @@
     )
     if fast:
 
-        def put_down(full, z, piece):
-            full[(z >> 1) * CUT_ROWS : ((z >> 1) + 1) * CUT_ROWS, pl.ds((z & 1) * 384, 384)] = piece
-
-        def put_upper(full, z, piece):
-            full[:CUT_ROWS, pl.ds(z * 384, 384)] = piece
-
-        def put_lower(full, z, piece):
-            full[CUT_ROWS:, pl.ds(z * 384, 384)] = piece
-
-        def put_columns(full, z, piece):
-            full[:, pl.ds(z * 384, 384)] = piece
-
         arrived_qkv_out = over_core(grad_qkv_out[0])
         piece = (CUT_ROWS, CUT_COLUMNS)
         taller = (CUT_ROWS + 8, CUT_COLUMNS)
@@ -843,12 +852,12 @@
         (send_up, keep_up), (send_low, keep_low) = add_step(
             [
                 (cut(keep_up, 2, 2, 2), cut(arrived_up, 2, 2, 2), 1),
-                (cut(keep_low, 2, 2, 2), cut(arrived_low, 2, 2, 2), 0),
+                (cut(keep_low, 2, 2, 2), cut(arrived_low, 2, 2, 2), 2),
             ],
             "up_x_low_z",
             (keep_down,),
         )
-        arrived_up, arrived_low = over_z_low(send_up), over_y(send_low)
+        arrived_up, arrived_low = over_z_low(send_up), over_z_high(send_low)
 
         def qkv_out_core(ins, outs):
             total = ins[0][...].astype(F32) + ins[1][...].astype(F32)
@@ -869,10 +878,11 @@
             [(cut(keep_down, 2, 2), cut(arrived_down, 2, 2), 0)], "down_x", (keep_a,)
         )
         arrived_down = over_z_low(send)
+        output = layer_output(middle, hidden, down_whole, (keep_down,))
         sums = add_step(
             [
                 (keep_up, arrived_up, 0),
-                (keep_low, arrived_low, 0),
+                (keep_low, arrived_low, 1),
                 (keep_a, arrived_a, 0),
                 (keep_b, arrived_b, 0),
                 (keep_down, arrived_down, 0),
@@ -889,13 +899,13 @@
         def planes(ins, outs):
             for i in range(2):
                 total = ins[2 * i][...] + ins[2 * i + 1][...].astype(F32)
-                outs[0][i] = total[1].astype(BF16)
-                outs[1][i] = total[0]
-            outs[2][...] = (ins[6][...] + ins[7][...].astype(F32)).astype(BF16)
-            outs[3][...] = ins[4][...] + ins[5][...].astype(F32)
-            outs[4][...] = (ins[8][...] + ins[9][...].astype(F32)).astype(BF16)
-
-        send, keep, send_qkv_out, keep_qkv_out, piece_down = step(
+                outs[i][...] = total[1].astype(BF16)
+                outs[2][i] = total[0]
+            outs[3][...] = (ins[6][...] + ins[7][...].astype(F32)).astype(BF16)
+            outs[4][...] = ins[4][...] + ins[5][...].astype(F32)
+            outs[5][...] = (ins[8][...] + ins[9][...].astype(F32)).astype(BF16)
+
+        send_up, send_low, keep, send_qkv_out, keep_qkv_out, piece_down = step(
             planes,
             [
                 *(keep_up, arrived_up, keep_low, arrived_low),
@@ -903,26 +913,28 @@
                 *(keep_down, arrived_down),
             ],
             [
-                *(sds((2, *piece), BF16), sds((2, *piece), F32)),
+                *(sds(piece, BF16), sds(piece, BF16), sds((2, *piece), F32)),
                 *(sds((2, *taller), BF16), sds((2, *taller), F32)),
                 sds(piece, BF16),
             ],
             "planes",
         )
-        arrived = over_z_high(send)
+        arrived_up, arrived_low = over_z_high(send_up), over_y(send_low)
         arrived_qkv_out = over_z_low(send_qkv_out)
         down_high = over_z_high(piece_down)
 
         def lines(ins, outs):
-            outs[0][...] = (ins[0][...] + ins[1][...].astype(F32)).astype(BF16)
-            total = ins[2][...] + ins[3][...].astype(F32)
+            for part in range(2):
+                total = ins[0][part] + ins[1 + part][...].astype(F32)
+                outs[0][part] = total.astype(BF16)
+            total = ins[3][...] + ins[4][...].astype(F32)
             outs[1][...] = total[1].astype(BF16)
             outs[2][...] = total[0]
-            outs[3][0], outs[3][1] = ins[4][...], ins[5][...]
+            outs[3][0], outs[3][1] = ins[5][...], ins[6][...]
 
         pieces, send_qkv_out, keep_qkv_out, near_down = step(
             lines,
-            [keep, arrived, keep_qkv_out, arrived_qkv_out, piece_down, down_high],
+            [keep, arrived_up, arrived_low, keep_qkv_out, arrived_qkv_out, piece_down, down_high],
             [
                 sds((2, *piece), BF16),
                 *(sds(taller, BF16), sds(taller, F32)),
@@ -955,39 +967,60 @@
         down_x = over_x(near_down)
 
         def share_next(ins, outs):
-            for i in (0, 1, 2):
+            for i in range(2):
                 outs[i][0], outs[i][1] = ins[2 * i][...], ins[2 * i + 1][...]
             for x in range(2):
                 for low in range(2):
                     for high in range(2):
-                        outs[3][0, x, low * 2 + high] = ins[6 + x][low, high]
-
-        near_up, near_low, near_qkv_out, near_down = step(
+                        outs[2][0, x, low * 2 + high] = ins[4 + x][low, high]
+
+        near_up, near_low, near_down = step(
             share_next,
-            [near_up, up_x, near_low, low_low, piece_qkv_out, qkv_out_high, near_down, down_x],
+            [near_up, up_x, near_low, low_low, near_down, down_x],
             [
                 *(sds((2, 2, *piece), BF16), sds((2, 2, *piece), BF16)),
-                sds((2, *taller), BF16),
                 sds((1, 2, 4, *piece), BF16),
             ],
             "share_next",
+            (qkv_out_high,),
         )
         far_down = over_core(near_down)
         up_low, low_x = over_z_low(near_up), over_x(near_low)
+
+        def update(near, far, place, height, state, gains, name, after):
+            near_out = update_half(
+                idx, 0, near, place, height, state, (), gains, name + "_near", after
+            )
+            count = len(state)
+            mark = near_out[-1]
+            far_out = update_half(
+                idx, 1, far, place, height, state, near_out[:count], (), name + "_far", (mark,)
+            )
+            return (*far_out[:count], *near_out[count:-1], far_out[-1])
+
+        one_down, two_down, next_down, mark = update(
+            near_down,
+            far_down,
+            lambda p, x, z: ((x * 2 + (z >> 1)) * CUT_ROWS, (z & 1) * CUT_COLUMNS),
+            2 * HALF,
+            [down_t, first_down_t, second_down_t],
+            (),
+            "update_down",
+            (near_up,),
+        )
+
+        def share_qkv_out_high(ins, outs):
+            outs[0][0], outs[0][1] = ins[0][...], ins[1][...]
+
+        (near_qkv_out,) = step(
+            share_qkv_out_high,
+            [piece_qkv_out, qkv_out_high],
+            [sds((2, *taller), BF16)],
+            "share_qkv_out_high",
+            (mark,),
+        )
         qkv_out_x, qkv_out_low = over_x(near_qkv_out), over_z_low(near_qkv_out)
         qkv_out_both = swap(near_qkv_out, "dp", 6)
-        by_row = lambda t, _: ((t % 2) * 2 + t // 2, 0)
-        one_down, two_down, next_down, mark = update_state(
-            idx,
-            near_down,
-            far_down,
-            (0,),
-            [((HALF, down_rows), by_row)],
-            (put_down,),
-            [down_t, first_down_t, second_down_t],
-            (HALF, down_rows),
-            "update_down",
-        )
 
         def share_gate_up(ins, outs):
             for near in range(2):
@@ -1001,9 +1034,19 @@
             [near_up, up_low, near_low, low_x],
             [sds((2, 2, 4, *piece), BF16)],
             "share_gate_up",
-            (mark,),
+            (near_qkv_out,),
         )
         far_gate_up = over_core(near_gate_up)
+        one_gate_up, two_gate_up, next_gate_up, mark = update(
+            near_gate_up,
+            far_gate_up,
+            lambda p, x, z: (p * CUT_ROWS, (x * 4 + z) * CUT_COLUMNS),
+            HALF,
+            [w_gate_up, first_gate_up, second_gate_up],
+            (),
+            "update_gate_up",
+            (),
+        )
 
         def share_qkv_out(ins, outs):
             for x in range(2):
@@ -1016,34 +1059,18 @@
             [near_qkv_out, qkv_out_x, qkv_out_low, qkv_out_both],
             [sds((1, 2, 4, *taller), BF16)],
             "share_qkv_out",
-            (near_gate_up,),
+            (mark,),
         )
         far_qkv_out = over_core(near_qkv_out)
-        one_gate_up, two_gate_up, next_gate_up, mark = update_state(
-            idx,
-            near_gate_up,
-            far_gate_up,
-            (0, 1),
-            [((HALF, FF), lambda t, _: (t % 2, t // 2))],
-            (put_upper, put_lower),
-            [w_gate_up, first_gate_up, second_gate_up],
-            (HALF, FF),
-            "update_gate_up",
-            (),
-            (near_qkv_out,),
-        )
-        updated = update_state(
-            idx,
+        updated = update(
             near_qkv_out,
             far_qkv_out,
-            (0,),
-            [((CUT_ROWS, QKV), by_row), ((CUT_ROWS, width), by_row)],
-            (put_columns,),
+            lambda p, x, z: (x * CUT_ROWS, z * CUT_COLUMNS),
+            HALF,
             [w_qkv, w_out, first_qkv, first_out, second_qkv, second_out],
-            (CUT_ROWS + 8, QKV + width),
+            (norm_gains, first_gains, second_gains),
             "update_qkv_out",
-            (norm_gains, first_gains, second_gains),
-            (mark,),
+            (),
         )
         one_qkv, one_out, two_qkv, two_out, next_qkv, next_out = updated[:6]
         one_gains, two_gains, next_gains = updated[6:9]

time: 147 us -> 145 us (0.986)
  waiting for transfers between devices: 58.1 us -> 43.8 us
  Pallas kernels: 37.8 us -> 44.2 us
  starting transfers between devices: 47.8 us -> 52.1 us
    ppermute x49 -> x50, waiting for transfers between devices: 58.1 us -> 43.8 us  [swap(): return lax.ppermute(values, axis, [(i, i ^ mask) for i in range(size)])]
    pallas_call x3 -> x6, Pallas kernels: 15 us -> 21.1 us  [update_half(): pl.pallas_call(kernel, out_shape=tuple((sds(a.shape, F32) for a in [*stat...]
    ppermute x49 -> x50, starting transfers between devices: 47.8 us -> 52.1 us  [swap(): return lax.ppermute(values, axis, [(i, i ^ mask) for i in range(size)])]
    pallas_call x14 -> x17, Pallas kernels: 1.84 us -> 3.37 us  [step(): pl.pallas_call(kernel, out_shape=tuple(outs), in_specs=[pl.BlockSpec(memo...]
  transfers between devices with their start and end apart: 49 -> 50, of which waited for: 19 -> 17; matrix products, arithmetic and copies ran while one was open for 0% -> 0% of each run, Pallas kernels for 20% -> 25%
where the time goes in v7:
time: 145 us
  starting transfers between devices  52.1 us (36%)
  Pallas kernels  44.2 us (30%)
  waiting for transfers between devices  43.8 us (30%)
  local copies, waits for them, and re-layouts  2.42 us (2%)
    ppermute x50, starting transfers between devices, swap(): return lax.ppermute(values, axis, [(i, i ^ mask) for i in range(size)])  52.1 us
    ppermute x50, waiting for transfers between devices, swap(): return lax.ppermute(values, axis, [(i, i ^ mask) for i in range(size)])  43.8 us
    pallas_call x6, Pallas kernels, update_half(): pl.pallas_call(kernel, out_shape=tuple((sds(a.shape, F32) for a in [*stat...  21.1 us
    pallas_call x5, Pallas kernels, call(): pl.pallas_call(kernel, out_shape=tuple(outs), in_specs=[pl.BlockSpec(memo...  15.7 us
    pallas_call x2, Pallas kernels, pack_kernel(): pl.pallas_call(kernel, out_shape=tuple(outs), in_specs=[pl.BlockSpec(memo...  3.97 us
    pallas_call x17, Pallas kernels, step(): pl.pallas_call(kernel, out_shape=tuple(outs), in_specs=[pl.BlockSpec(memo...  3.37 us
  transfers between devices with their start and end apart: 50, of which 17 were waited for; matrix products, arithmetic and copies ran while one was open for 0% of the time, Pallas kernels for 25%

profile of v7, /device:TPU:0, one launch (start us, length us, event | category | flops | bytes accessed | tf_op | source)
XLA Modules:
  0.0 144.6 jit_solution(17845204495090515189)
XLA Ops:
  1.3 3.2 %pack_first.1 = (bf16[160,768]{1,0:T(8,128)(2,1)}, bf16[144,768]{1,0:T(8,128)(2,1)}, bf16[144,768]{1,0:T(8,128)(2,1)}) custom-call(s32[4]{0:T(128)} %pad_add_fusion.idx_ref.refs_0_, f32[288,960]{1,0:T(8,128)} %refs_1_.9, f32[288,576]{1,0:T(8,128)} %refs_2_.11, f32[2,288]{1,0:T(2,128)} %refs_7_.3, f32[288,3072]{1,0:T(8,128)} %refs_1_.7, f32[288,3072]{1,0:T(8,128)} %refs_1_.7), custom_call_target="tpu_custom_call" | custom-call | flops 10000000000 | tf_op jit(solution)/shard_map/pack_first/pallas_call | solution.py:229
  4.4 3.0 %collective-permute-start = (bf16[160,768]{1,0:T(8,128)(2,1)}, bf16[160,768]{1,0:T(8,128)(2,1)S(1)}, u32[]{:S(2)}, u32[]{:S(2)}) collective-permute-start(bf16[160,768]{1,0:T(8,128)(2,1)} %get-tuple-element.122), channel_id=1, source_target_pairs={{0,1},{1,0},{2,3},{3,2},{4,5},{5,4},{6,7},{7,6},{8,9},{9,8},{10,11... | collective-permute-start | bytes 737288 | tf_op jit(solution)/shard_map/ppermute | solution.py:678
  7.6 6.9 %collective-permute-done.refs_5_.refs_8_ = bf16[160,768]{1,0:T(8,128)(2,1)S(1)} collective-permute-done((bf16[160,768]{1,0:T(8,128)(2,1)}, bf16[160,768]{1,0:T(8,128)(2,1)S(1)}, u32[]{:S(2)}, u32[]{:S(2)}) %collective-permute-start) | collective-permute-done | bytes 245792 | tf_op jit(solution)/shard_map/ppermute | solution.py:678
  14.5 2.1 %collective-permute-start.1 = (bf16[160,768]{1,0:T(8,128)(2,1)S(1)}, bf16[160,768]{1,0:T(8,128)(2,1)S(1)}, u32[]{:S(2)}, u32[]{:S(2)}) collective-permute-start(bf16[160,768]{1,0:T(8,128)(2,1)S(1)} %collective-permute-done.refs_5_.refs_8_), channel_id=1, source_target_pairs={{0,8},{2,10},{4,12},{6,14},{8,0},{10,2},{12,4},{14,6},{16,24},{18,... | collective-permute-start | bytes 737288 | tf_op jit(solution)/shard_map/ppermute | solution.py:678
  16.6 1.5 %collective-permute-start.4 = (bf16[144,768]{1,0:T(8,128)(2,1)}, bf16[144,768]{1,0:T(8,128)(2,1)S(1)}, u32[]{:S(2)}, u32[]{:S(2)}) collective-permute-start(bf16[144,768]{1,0:T(8,128)(2,1)} %get-tuple-element.126), channel_id=1, source_target_pairs={{0,1},{1,0},{2,3},{3,2},{4,5},{5,4},{6,7},{7,6},{8,9},{9,8},{10,11... | collective-permute-start | bytes 663560 | tf_op jit(solution)/shard_map/ppermute | solution.py:678
  19.2 2.1 %collective-permute-start.9 = (bf16[144,768]{1,0:T(8,128)(2,1)S(1)}, bf16[144,768]{1,0:T(8,128)(2,1)S(1)}, u32[]{:S(2)}, u32[]{:S(2)}) collective-permute-start(bf16[144,768]{1,0:T(8,128)(2,1)S(1)} %collective-permute-done.8.refs_11_.refs_1_), channel_id=1, source_target_pairs={{0,8},{2,10},{4,12},{6,14},{8,0},{10,2},{12,4},{14,6},{16,24},{18,... | collective-permute-start | bytes 663560 | tf_op jit(solution)/shard_map/ppermute | solution.py:678
  21.3 1.8 %collective-permute-done.4.refs_7_ = bf16[144,768]{1,0:T(8,128)(2,1)S(1)} collective-permute-done((bf16[144,768]{1,0:T(8,128)(2,1)}, bf16[144,768]{1,0:T(8,128)(2,1)S(1)}, u32[]{:S(2)}, u32[]{:S(2)}) %collective-permute-start.4) | collective-permute-done | bytes 221216 | tf_op jit(solution)/shard_map/ppermute | solution.py:678
  23.1 1.7 %collective-permute-start.5 = (bf16[144,768]{1,0:T(8,128)(2,1)S(1)}, bf16[144,768]{1,0:T(8,128)(2,1)S(1)}, u32[]{:S(2)}, u32[]{:S(2)}) collective-permute-start(bf16[144,768]{1,0:T(8,128)(2,1)S(1)} %collective-permute-done.4.refs_7_), channel_id=1, source_target_pairs={{0,4},{2,6},{4,0},{6,2},{8,12},{10,14},{12,8},{14,10},{16,20},{18,... | collective-permute-start | bytes 663560 | tf_op jit(solution)/shard_map/ppermute | solution.py:678
  26.9 2.0 %collective-permute-start.12 = (bf16[288,768]{1,0:T(8,128)(2,1)S(1)}, bf16[288,768]{1,0:T(8,128)(2,1)S(1)}, u32[]{:S(2)}, u32[]{:S(2)}) collective-permute-start(bf16[288,768]{1,0:T(8,128)(2,1)S(1)} %pack_down.1), channel_id=1, source_target_pairs={{0,1},{1,0},{2,3},{3,2},{4,5},{5,4},{6,7},{7,6},{8,9},{9,8},{10,11... | collective-permute-start | bytes 1327112 | tf_op jit(solution)/shard_map/ppermute | solution.py:678
  29.8 2.5 %attention.1 = (bf16[128,960]{1,0:T(8,128)(2,1)S(1)}, bf16[128,576]{1,0:T(8,128)(2,1)S(1)}, f32[128,128]{1,0:T(8,128)S(1)}, f32[128,128]{1,0:T(8,128)S(1)}, f32[...) custom-call(s32[4]{0:T(128)S(1)} %copy-done.3, bf16[576,128]{1,0:T(8,128)(2,1)S(1)} %bitcast.45, ...), custom_call_target="tpu_custom_call" | custom-call | flops 1000000000 | tf_op jit(solution)/shard_map/attention/pallas_call | solution.py:139
  32.3 2.8 %feed_forward.1 = (f32[128,576]{1,0:T(8,128)S(1)}, bf16[128,576]{1,0:T(8,128)(2,1)S(1)}, f32[128,3072]{1,0:T(8,128)S(1)}, bf16[128,1536]{1,0:T(8,128)(2,1)S(1)},...) custom-call(s32[4]{0:T(128)S(1)} %copy-done.3, ...), custom_call_target="tpu_custom_call" | custom-call | flops 2000000000 | tf_op jit(solution)/shard_map/feed_forward/pallas_call | solution.py:139
  35.2 4.1 %collective-permute-done.12.refs_0_ = bf16[288,768]{1,0:T(8,128)(2,1)S(1)} collective-permute-done((bf16[288,768]{1,0:T(8,128)(2,1)S(1)}, bf16[288,768]{1,0:T(8,128)(2,1)S(1)}, u32[]{:S(2)}, u32[]{:S(2)}) %collective-permute-start.12) | collective-permute-done | bytes 442400 | tf_op jit(solution)/shard_map/ppermute | solution.py:678
  39.9 1.3 collective-permute-done.13.refs_6_
  41.2 2.6 %feed_back.1 = (bf16[128,3072]{1,0:T(8,128)(2,1)S(1)}, bf16[2,2,8,72,384]{4,3,2,1,0:T(8,128)(2,1)S(1)}, bf16[2,2,8,72,384]{4,3,2,1,0:T(8,128)(2,1)S(1)}, bf16[576,1536]{1,0:T(8,128)(2,1)S(1)}) custom-call(s32[4]{0:T(128)S(1)} %copy-done.3, f32[128,3072]{1,0:T(8,128)S(1)} %get-tuple-element.130.refs_1_, ...), custom_call_target="tpu_custom_call" | custom-call | flops 20000000000 | tf_op jit(solution)/shard_map/feed_back/pallas_call | solution.py:139
  44.4 1.8 %collective-permute-start.15 = (bf16[8,72,384]{2,1,0:T(8,128)(2,1)S(1)}, bf16[8,72,384]{2,1,0:T(8,128)(2,1)S(1)}, u32[]{:S(2)}, u32[]{:S(2)}) collective-permute-start(bf16[8,72,384]{2,1,0:T(8,128)(2,1)S(1)} %get-tuple-element.137), channel_id=1, source_target_pairs={{0,1},{1,0},{2,3},{3,2},{4,5},{5,4},{6,7},{7,6},{8,9},{9,8},{10,11... | collective-permute-start | bytes 1327112 | tf_op jit(solution)/shard_map/ppermute | solution.py:678
  46.2 2.7 %middle_back.1 = (f32[128,576]{1,0:T(8,128)S(1)}, bf16[128,576]{1,0:T(8,128)(2,1)S(1)}, f32[1,576]{1,0:T(1,128)S(1)}) custom-call(s32[4]{0:T(128)S(1)} %copy-done.3, bf16[576,128]{1,0:T(8,128)(2,1)S(1)} %bitcast.44, f32[128,576]{1,0:T(8,128)S(1)} %get-tuple-element.128.refs_2_.refs_0_, bf16[128,3072]{1,0:T(8,128)(2,1)S(1)} %get-tuple-element.135.refs_2_.refs_3_, ...), custom_call_target="tpu_custom_call" | custom-call | flops 20000000000 | tf_op jit(solution)/shard_map/middle_back/pallas_call | solution.py:139
  49.6 1.6 %collective-permute-start.19 = (bf16[2,4,72,384]{3,2,1,0:T(8,128)(2,1)S(1)}, bf16[2,4,72,384]{3,2,1,0:T(8,128)(2,1)S(1)}, u32[]{:S(2)}, u32[]{:S(2)}) collective-permute-start(bf16[2,4,72,384]{3,2,1,0:T(8,128)(2,1)S(1)} %get-tuple-element.154), channel_id=1, source_target_pairs={{0,4},{2,6},{4,0},{6,2},{8,12},{10,14},{12,8},{14,10},{16,20},{18,... | collective-permute-start | bytes 1327112 | tf_op jit(solution)/shard_map/ppermute | solution.py:678
  51.1 1.6 %collective-permute-start.20 = (bf16[4,2,72,384]{3,2,1,0:T(8,128)(2,1)S(1)}, bf16[4,2,72,384]{3,2,1,0:T(8,128)(2,1)S(1)}, u32[]{:S(2)}, u32[]{:S(2)}) collective-permute-start(bf16[4,2,72,384]{3,2,1,0:T(8,128)(2,1)S(1)} %get-tuple-element.156), channel_id=1, source_target_pairs={{0,8},{2,10},{4,12},{6,14},{8,0},{10,2},{12,4},{14,6},{16,24},{18,... | collective-permute-start | bytes 1327112 | tf_op jit(solution)/shard_map/ppermute | solution.py:678
  52.7 5.1 %attention_back.1 = (bf16[576,128]{1,0:T(8,128)(2,1)}, bf16[1,2,8,80,384]{4,3,2,1,0:T(8,128)(2,1)S(1)}, bf16[1,2,8,80,384]{4,3,2,1,0:T(8,128)(2,1)S(1)}, f32[8,128]{1,0:T(8,128)S(1)}) custom-call(s32[4]{0:T(128)S(1)} %copy-done.3, bf16[576,128]{1,0:T(8,128)(2,1)S(1)} %bitcast.47, f32[128,576]{1,0:T(8,128)S(1)} %get-tuple-element.139.refs_4_.refs_2_, ...), custom_call_target="tpu_custom_call" | custom-call | flops 20000000000 | tf_op jit(solution)/shard_map/attention_back/pallas_call | solution.py:139
  58.8 3.9 %collective-permute-done.19 = bf16[2,4,72,384]{3,2,1,0:T(8,128)(2,1)S(1)} collective-permute-done((bf16[2,4,72,384]{3,2,1,0:T(8,128)(2,1)S(1)}, bf16[2,4,72,384]{3,2,1,0:T(8,128)(2,1)S(1)}, u32[]{:S(2)}, u32[]{:S(2)}) %collective-permute-start.19) | collective-permute-done | bytes 442400 | tf_op jit(solution)/shard_map/ppermute | solution.py:678
  63.2 1.6 %collective-permute-start.21 = (bf16[2,2,72,384]{3,2,1,0:T(8,128)(2,1)S(1)}, bf16[2,2,72,384]{3,2,1,0:T(8,128)(2,1)S(1)}, u32[]{:S(2)}, u32[]{:S(2)}) collective-permute-start(bf16[2,2,72,384]{3,2,1,0:T(8,128)(2,1)S(1)} %get-tuple-element.161), channel_id=1, source_target_pairs={{0,8},{2,10},{4,12},{6,14},{8,0},{10,2},{12,4},{14,6},{16,24},{18,... | collective-permute-start | bytes 663560 | tf_op jit(solution)/shard_map/ppermute | solution.py:678
  64.8 2.6 %collective-permute-start.22 = (bf16[2,2,72,384]{3,2,1,0:T(8,128)(2,1)S(1)}, bf16[2,2,72,384]{3,2,1,0:T(8,128)(2,1)S(1)}, u32[]{:S(2)}, u32[]{:S(2)}) collective-permute-start(bf16[2,2,72,384]{3,2,1,0:T(8,128)(2,1)S(1)} %get-tuple-element.163), channel_id=1, source_target_pairs={{0,16},{2,18},{4,20},{6,22},{8,24},{10,26},{12,28},{14,30},{16,0},... | collective-permute-start | bytes 663560 | tf_op jit(solution)/shard_map/ppermute | solution.py:678
  68.2 1.2 collective-permute-start.24
  69.9 5.5 %collective-permute-done.21.refs_1_ = bf16[2,2,72,384]{3,2,1,0:T(8,128)(2,1)S(1)} collective-permute-done((bf16[2,2,72,384]{3,2,1,0:T(8,128)(2,1)S(1)}, bf16[2,2,72,384]{3,2,1,0:T(8,128)(2,1)S(1)}, u32[]{:S(2)}, u32[]{:S(2)}) %collective-permute-start.21) | collective-permute-done | bytes 221216 | tf_op jit(solution)/shard_map/ppermute | solution.py:678
  75.4 1.2 collective-permute-done.25.refs_9_
  78.0 1.5 %collective-permute-start.26 = (bf16[2,72,384]{2,1,0:T(8,128)(2,1)S(1)}, bf16[2,72,384]{2,1,0:T(8,128)(2,1)S(1)}, u32[]{:S(2)}, u32[]{:S(2)}) collective-permute-start(bf16[2,72,384]{2,1,0:T(8,128)(2,1)S(1)} %get-tuple-element.169), channel_id=1, source_target_pairs={{0,1},{1,0},{2,3},{3,2},{4,5},{5,4},{6,7},{7,6},{8,9},{9,8},{10,11... | collective-permute-start | bytes 331784 | tf_op jit(solution)/shard_map/ppermute | solution.py:678
  79.5 1.4 collective-permute-start.27
  80.9 2.6 %collective-permute-start.30 = (bf16[72,384]{1,0:T(8,128)(2,1)S(1)}, bf16[72,384]{1,0:T(8,128)(2,1)S(1)}, u32[]{:S(2)}, u32[]{:S(2)}) collective-permute-start(bf16[72,384]{1,0:T(8,128)(2,1)S(1)} %get-tuple-element.177), channel_id=1, source_target_pairs={{0,16},{2,18},{4,20},{6,22},{8,24},{10,26},{12,28},{14,30},{16,0},... | collective-permute-start | bytes 165896 | tf_op jit(solution)/shard_map/ppermute | solution.py:678
  83.5 2.6 %collective-permute-done.30.refs_9_ = bf16[72,384]{1,0:T(8,128)(2,1)S(1)} collective-permute-done((bf16[72,384]{1,0:T(8,128)(2,1)S(1)}, bf16[72,384]{1,0:T(8,128)(2,1)S(1)}, u32[]{:S(2)}, u32[]{:S(2)}) %collective-permute-start.30) | collective-permute-done | bytes 55328 | tf_op jit(solution)/shard_map/ppermute | solution.py:678
  86.2 1.5 %collective-permute-start.33 = (bf16[2,80,384]{2,1,0:T(8,128)(2,1)S(1)}, bf16[2,80,384]{2,1,0:T(8,128)(2,1)S(1)}, u32[]{:S(2)}, u32[]{:S(2)}) collective-permute-start(bf16[2,80,384]{2,1,0:T(8,128)(2,1)S(1)} %get-tuple-element.182), channel_id=1, source_target_pairs={{0,8},{2,10},{4,12},{6,14},{8,0},{10,2},{12,4},{14,6},{16,24},{18,... | collective-permute-start | bytes 368648 | tf_op jit(solution)/shard_map/ppermute | solution.py:678
  87.8 3.4 %collective-permute-start.31 = (bf16[72,384]{1,0:T(8,128)(2,1)S(1)}, bf16[72,384]{1,0:T(8,128)(2,1)S(1)}, u32[]{:S(2)}, u32[]{:S(2)}) collective-permute-start(bf16[72,384]{1,0:T(8,128)(2,1)S(1)} %get-tuple-element.179), channel_id=1, source_target_pairs={{0,16},{2,18},{4,20},{6,22},{8,24},{10,26},{12,28},{14,30},{16,0},... | collective-permute-start | bytes 165896 | tf_op jit(solution)/shard_map/ppermute | solution.py:678
  91.7 1.8 %collective-permute-done.31.refs_1_ = bf16[72,384]{1,0:T(8,128)(2,1)S(1)} collective-permute-done((bf16[72,384]{1,0:T(8,128)(2,1)S(1)}, bf16[72,384]{1,0:T(8,128)(2,1)S(1)}, u32[]{:S(2)}, u32[]{:S(2)}) %collective-permute-start.31) | collective-permute-done | bytes 55328 | tf_op jit(solution)/shard_map/ppermute | solution.py:678
  93.5 1.9 %collective-permute-done.32.refs_2_ = bf16[72,384]{1,0:T(8,128)(2,1)S(1)} collective-permute-done((bf16[72,384]{1,0:T(8,128)(2,1)S(1)}, bf16[72,384]{1,0:T(8,128)(2,1)S(1)}, u32[]{:S(2)}, u32[]{:S(2)}) %collective-permute-start.32) | collective-permute-done | bytes 55328 | tf_op jit(solution)/shard_map/ppermute | solution.py:678
  95.3 3.1 %collective-permute-done.34.refs_6_ = bf16[72,384]{1,0:T(8,128)(2,1)S(1)} collective-permute-done((bf16[72,384]{1,0:T(8,128)(2,1)S(1)}, bf16[72,384]{1,0:T(8,128)(2,1)S(1)}, u32[]{:S(2)}, u32[]{:S(2)}) %collective-permute-start.34) | collective-permute-done | bytes 55328 | tf_op jit(solution)/shard_map/ppermute | solution.py:678
  98.6 2.3 %collective-permute-start.37 = (bf16[2,72,384]{2,1,0:T(8,128)(2,1)S(1)}, bf16[2,72,384]{2,1,0:T(8,128)(2,1)S(1)}, u32[]{:S(2)}, u32[]{:S(2)}) collective-permute-start(bf16[2,72,384]{2,1,0:T(8,128)(2,1)S(1)} %get-tuple-element.187.refs_4_), channel_id=1, source_target_pairs={{0,8},{2,10},{4,12},{6,14},{8,0},{10,2},{12,4},{14,6},{16,24},{18,... | collective-permute-start | bytes 331784 | tf_op jit(solution)/shard_map/ppermute | solution.py:678
  101.5 4.8 %collective-permute-done.36.refs_3_ = bf16[80,384]{1,0:T(8,128)(2,1)S(1)} collective-permute-done((bf16[80,384]{1,0:T(8,128)(2,1)S(1)}, bf16[80,384]{1,0:T(8,128)(2,1)S(1)}, u32[]{:S(2)}, u32[]{:S(2)}) %collective-permute-start.36) | collective-permute-done | bytes 61472 | tf_op jit(solution)/shard_map/ppermute | solution.py:678
  106.9 1.1 collective-permute-start.38
  108.0 1.9 %collective-permute-start.39 = (bf16[2,72,384]{2,1,0:T(8,128)(2,1)S(1)}, bf16[2,72,384]{2,1,0:T(8,128)(2,1)S(1)}, u32[]{:S(2)}, u32[]{:S(2)}) collective-permute-start(bf16[2,72,384]{2,1,0:T(8,128)(2,1)S(1)} %get-tuple-element.189.refs_0_), channel_id=1, source_target_pairs={{0,4},{2,6},{4,0},{6,2},{8,12},{10,14},{12,8},{14,10},{16,20},{18,... | collective-permute-start | bytes 331784 | tf_op jit(solution)/shard_map/ppermute | solution.py:678
  110.0 1.8 %collective-permute-start.40 = (bf16[2,72,384]{2,1,0:T(8,128)(2,1)S(1)}, bf16[2,72,384]{2,1,0:T(8,128)(2,1)S(1)}, u32[]{:S(2)}, u32[]{:S(2)}) collective-permute-start(bf16[2,72,384]{2,1,0:T(8,128)(2,1)S(1)} %get-tuple-element.190.refs_2_), channel_id=1, source_target_pairs={{0,8},{2,10},{4,12},{6,14},{8,0},{10,2},{12,4},{14,6},{16,24},{18,... | collective-permute-start | bytes 331784 | tf_op jit(solution)/shard_map/ppermute | solution.py:678
  111.8 1.5 %layer_output.1 = bf16[576,128]{1,0:T(8,128)(2,1)} custom-call(f32[128,576]{1,0:T(8,128)S(1)} %copy-done.18, bf16[128,1536]{1,0:T(8,128)(2,1)S(1)} %get-tuple-element.129.refs_1_, bf16[576,1536]{1,0:T(8,128)(2,1)S(1)} %get-tuple-element.132.refs_2_, f32[2,72,384]{2,1,0:T(8,128)S(1)} %get-tuple-element.159.refs_3_.refs_8_.refs_10_), custom_call_target="tpu_custom_call" | custom-call | flops 2000000000 | tf_op jit(solution)/shard_map/layer_output/pallas_call | solution.py:557
  113.2 2.7 %collective-permute-done.39.refs_1_ = bf16[2,72,384]{2,1,0:T(8,128)(2,1)S(1)} collective-permute-done((bf16[2,72,384]{2,1,0:T(8,128)(2,1)S(1)}, bf16[2,72,384]{2,1,0:T(8,128)(2,1)S(1)}, u32[]{:S(2)}, u32[]{:S(2)}) %collective-permute-start.39) | collective-permute-done | bytes 110624 | tf_op jit(solution)/shard_map/ppermute | solution.py:678
  116.8 2.6 %update_down_near.1 = (f32[576,768]{1,0:T(8,128)}, f32[576,768]{1,0:T(8,128)}, f32[576,768]{1,0:T(8,128)}, f32[8,128]{1,0:T(8,128)S(1)}) custom-call(s32[4]{0:T(128)S(1)} %copy-done.3, bf16[1,2,4,72,384]{4,3,2,1,0:T(8,128)(2,1)S(1)} %get-tuple-element.192.refs_0_, f32[576,768]{1,0:T(8,128)S(1)} %bitcast.50, f32[576,768]{1,0:T(8,128)S(1)} %bitcast.52, ...), custom_call_target="tpu_custom_call" | custom-call | flops 20000000000 | tf_op jit(solution)/shard_map/update_down_near/pallas_call | solution.py:660
  119.4 2.6 %update_down_far.1 = (f32[576,768]{1,0:T(8,128)}, f32[576,768]{1,0:T(8,128)}, f32[576,768]{1,0:T(8,128)}, f32[8,128]{1,0:T(8,128)S(1)}) custom-call(s32[4]{0:T(128)S(1)} %copy-done.3, bf16[1,2,4,72,384]{4,3,2,1,0:T(8,128)(2,1)S(1)} %collective-permute-done.42.refs_0_, ...), custom_call_target="tpu_custom_call", output_to_operand_aliasing={{0}: (5, {}), {1}: (6, {}), {2}: (7, {})} | custom-call | flops 20000000000 | tf_op jit(solution)/shard_map/update_down_far/pallas_call | solution.py:660
  122.1 2.9 %collective-permute-start.45 = (bf16[2,80,384]{2,1,0:T(8,128)(2,1)S(1)}, bf16[2,80,384]{2,1,0:T(8,128)(2,1)S(1)}, u32[]{:S(2)}, u32[]{:S(2)}) collective-permute-start(bf16[2,80,384]{2,1,0:T(8,128)(2,1)S(1)} %share_qkv_out_high.1.refs_4_.refs_0_), channel_id=1, source_target_pairs={{0,12},{2,14},{4,8},{6,10},{8,4},{10,6},{12,0},{14,2},{16,28},{18,... | collective-permute-start | bytes 368648 | tf_op jit(solution)/shard_map/ppermute | solution.py:678
  125.8 3.9 %update_gate_up_near.1 = (f32[288,3072]{1,0:T(8,128)}, f32[288,3072]{1,0:T(8,128)}, f32[288,3072]{1,0:T(8,128)}, f32[8,128]{1,0:T(8,128)S(1)}) custom-call(s32[4]{0:T(128)S(1)} %copy-done.3, bf16[2,2,4,72,384]{4,3,2,1,0:T(8,128)(2,1)S(1)} %share_gate_up.1.refs_0_, f32[288,3072]{1,0:T(8,128)S(1)} %copy-done, f32[288,3072]{1,0:T(8,128)S(1)} %copy-done.4, ...), custom_call_target="tpu_custom_call" | custom-call | flops 20000000000 | tf_op jit(solution)/shard_map/update_gate_up_near/pallas_call | solution.py:660
  129.7 3.9 %update_gate_up_far.1 = (f32[288,3072]{1,0:T(8,128)}, f32[288,3072]{1,0:T(8,128)}, f32[288,3072]{1,0:T(8,128)}, f32[8,128]{1,0:T(8,128)S(1)}) custom-call(s32[4]{0:T(128)S(1)} %copy-done.3, bf16[2,2,4,72,384]{4,3,2,1,0:T(8,128)(2,1)S(1)} %collective-permute-done.48.refs_0_, ...), custom_call_target="tpu_custom_call", output_to_operand_aliasing={{0}: (5, {}), {1}: (6, {}), {2}: (7, {})} | custom-call | flops 20000000000 | tf_op jit(solution)/shard_map/update_gate_up_far/pallas_call | solution.py:660
  136.3 4.1 %update_qkv_out_near.1 = (f32[288,960]{1,0:T(8,128)}, f32[288,576]{1,0:T(8,128)}, f32[288,960]{1,0:T(8,128)}, f32[288,576]{1,0:T(8,128)}, f32[288,960]{1,0:T(8,1...) custom-call(s32[4]{0:T(128)S(1)} %copy-done.3, ...), custom_call_target="tpu_custom_call" | custom-call | flops 20000000000 | tf_op jit(solution)/shard_map/update_qkv_out_near/pallas_call | solution.py:660
  140.4 4.1 %update_qkv_out_far.1 = (f32[288,960]{1,0:T(8,128)}, f32[288,576]{1,0:T(8,128)}, f32[288,960]{1,0:T(8,128)}, f32[288,576]{1,0:T(8,128)}, f32[288,960]{1,0:T(8,12...) custom-call(s32[4]{0:T(128)S(1)} %copy-done.3, ...), custom_call_target="tpu_custom_call", output_to_operand_aliasing={{0}: (8, {}), {1}: (9, {}), {2}: (10, {}), {3}: (11, {}), {... | custom-call | flops 20000000000 | tf_op jit(solution)/shard_map/update_qkv_out_far/pallas_call | solution.py:660
  (135 shorter events, 16.9 us)
Async XLA Ops:
  4.4 10.0 %collective-permute-start = (bf16[160,768]{1,0:T(8,128)(2,1)}, bf16[160,768]{1,0:T(8,128)(2,1)S(1)}, u32[]{:S(2)}, u32[]{:S(2)}) collective-permute-start(bf16[160,768]{1,0:T(8,128)(2,1)} %get-tuple-element.122), channel_id=1, source_target_pairs={{0,1},{1,0},{2,3},{3,2},{4,5},{5,4},{6,7},{7,6},{8,9},{9,8},{10,11... | collective-permute-start | bytes 737288 | tf_op jit(solution)/shard_map/ppermute | solution.py:678
  7.5 11.7 %collective-permute-start.8 = (bf16[144,768]{1,0:T(8,128)(2,1)}, bf16[144,768]{1,0:T(8,128)(2,1)S(1)}, u32[]{:S(2)}, u32[]{:S(2)}) collective-permute-start(bf16[144,768]{1,0:T(8,128)(2,1)} %get-tuple-element.127), channel_id=1, source_target_pairs={{0,1},{1,0},{2,3},{3,2},{4,5},{5,4},{6,7},{7,6},{8,9},{9,8},{10,11... | collective-permute-start | bytes 663560 | tf_op jit(solution)/shard_map/ppermute | solution.py:678
  14.5 11.1 %collective-permute-start.1 = (bf16[160,768]{1,0:T(8,128)(2,1)S(1)}, bf16[160,768]{1,0:T(8,128)(2,1)S(1)}, u32[]{:S(2)}, u32[]{:S(2)}) collective-permute-start(bf16[160,768]{1,0:T(8,128)(2,1)S(1)} %collective-permute-done.refs_5_.refs_8_), channel_id=1, source_target_pairs={{0,8},{2,10},{4,12},{6,14},{8,0},{10,2},{12,4},{14,6},{16,24},{18,... | collective-permute-start | bytes 737288 | tf_op jit(solution)/shard_map/ppermute | solution.py:678
  16.6 6.5 %collective-permute-start.4 = (bf16[144,768]{1,0:T(8,128)(2,1)}, bf16[144,768]{1,0:T(8,128)(2,1)S(1)}, u32[]{:S(2)}, u32[]{:S(2)}) collective-permute-start(bf16[144,768]{1,0:T(8,128)(2,1)} %get-tuple-element.126), channel_id=1, source_target_pairs={{0,1},{1,0},{2,3},{3,2},{4,5},{5,4},{6,7},{7,6},{8,9},{9,8},{10,11... | collective-permute-start | bytes 663560 | tf_op jit(solution)/shard_map/ppermute | solution.py:678
  19.2 6.3 %collective-permute-start.9 = (bf16[144,768]{1,0:T(8,128)(2,1)S(1)}, bf16[144,768]{1,0:T(8,128)(2,1)S(1)}, u32[]{:S(2)}, u32[]{:S(2)}) collective-permute-start(bf16[144,768]{1,0:T(8,128)(2,1)S(1)} %collective-permute-done.8.refs_11_.refs_1_), channel_id=1, source_target_pairs={{0,8},{2,10},{4,12},{6,14},{8,0},{10,2},{12,4},{14,6},{16,24},{18,... | collective-permute-start | bytes 663560 | tf_op jit(solution)/shard_map/ppermute | solution.py:678
  23.1 5.9 %collective-permute-start.5 = (bf16[144,768]{1,0:T(8,128)(2,1)S(1)}, bf16[144,768]{1,0:T(8,128)(2,1)S(1)}, u32[]{:S(2)}, u32[]{:S(2)}) collective-permute-start(bf16[144,768]{1,0:T(8,128)(2,1)S(1)} %collective-permute-done.4.refs_7_), channel_id=1, source_target_pairs={{0,4},{2,6},{4,0},{6,2},{8,12},{10,14},{12,8},{14,10},{16,20},{18,... | collective-permute-start | bytes 663560 | tf_op jit(solution)/shard_map/ppermute | solution.py:678
  24.8 4.2 %collective-permute-start.2 = (bf16[160,768]{1,0:T(8,128)(2,1)S(1)}, bf16[160,768]{1,0:T(8,128)(2,1)S(1)}, u32[]{:S(2)}, u32[]{:S(2)}) collective-permute-start(bf16[160,768]{1,0:T(8,128)(2,1)S(1)} %collective-permute-done.refs_5_.refs_8_), channel_id=1, source_target_pairs={{0,2},{2,0},{4,6},{6,4},{8,10},{10,8},{12,14},{14,12},{16,18},{18,... | collective-permute-start | bytes 737288 | tf_op jit(solution)/shard_map/ppermute | solution.py:678
  25.5 4.0 %collective-permute-start.11 = (bf16[144,768]{1,0:T(8,128)(2,1)S(1)}, bf16[144,768]{1,0:T(8,128)(2,1)S(1)}, u32[]{:S(2)}, u32[]{:S(2)}) collective-permute-start(bf16[144,768]{1,0:T(8,128)(2,1)S(1)} %collective-permute-done.9.refs_12_), channel_id=1, source_target_pairs={{0,2},{2,0},{4,6},{6,4},{8,10},{10,8},{12,14},{14,12},{16,18},{18,... | collective-permute-start | bytes 663560 | tf_op jit(solution)/shard_map/ppermute | solution.py:678
  25.5 4.1 %collective-permute-start.3 = (bf16[160,768]{1,0:T(8,128)(2,1)S(1)}, bf16[160,768]{1,0:T(8,128)(2,1)S(1)}, u32[]{:S(2)}, u32[]{:S(2)}) collective-permute-start(bf16[160,768]{1,0:T(8,128)(2,1)S(1)} %collective-permute-done.1.refs_9_), channel_id=1, source_target_pairs={{0,2},{2,0},{4,6},{6,4},{8,10},{10,8},{12,14},{14,12},{16,18},{18,... | collective-permute-start | bytes 737288 | tf_op jit(solution)/shard_map/ppermute | solution.py:678
  26.9 12.4 %collective-permute-start.12 = (bf16[288,768]{1,0:T(8,128)(2,1)S(1)}, bf16[288,768]{1,0:T(8,128)(2,1)S(1)}, u32[]{:S(2)}, u32[]{:S(2)}) collective-permute-start(bf16[288,768]{1,0:T(8,128)(2,1)S(1)} %pack_down.1), channel_id=1, source_target_pairs={{0,1},{1,0},{2,3},{3,2},{4,5},{5,4},{6,7},{7,6},{8,9},{9,8},{10,11... | collective-permute-start | bytes 1327112 | tf_op jit(solution)/shard_map/ppermute | solution.py:678
  29.1 3.2 %collective-permute-start.6 = (bf16[144,768]{1,0:T(8,128)(2,1)S(1)}, bf16[144,768]{1,0:T(8,128)(2,1)S(1)}, u32[]{:S(2)}, u32[]{:S(2)}) collective-permute-start(bf16[144,768]{1,0:T(8,128)(2,1)S(1)} %collective-permute-done.4.refs_7_), channel_id=1, source_target_pairs={{0,2},{2,0},{4,6},{6,4},{8,10},{10,8},{12,14},{14,12},{16,18},{18,... | collective-permute-start | bytes 663560 | tf_op jit(solution)/shard_map/ppermute | solution.py:678
  29.1 3.2 %collective-permute-start.10 = (bf16[144,768]{1,0:T(8,128)(2,1)S(1)}, bf16[144,768]{1,0:T(8,128)(2,1)S(1)}, u32[]{:S(2)}, u32[]{:S(2)}) collective-permute-start(bf16[144,768]{1,0:T(8,128)(2,1)S(1)} %collective-permute-done.8.refs_11_.refs_1_), channel_id=1, source_target_pairs={{0,2},{2,0},{4,6},{6,4},{8,10},{10,8},{12,14},{14,12},{16,18},{18,... | collective-permute-start | bytes 663560 | tf_op jit(solution)/shard_map/ppermute | solution.py:678
  29.6 2.7 %collective-permute-start.7 = (bf16[144,768]{1,0:T(8,128)(2,1)S(1)}, bf16[144,768]{1,0:T(8,128)(2,1)S(1)}, u32[]{:S(2)}, u32[]{:S(2)}) collective-permute-start(bf16[144,768]{1,0:T(8,128)(2,1)S(1)} %collective-permute-done.5.refs_8_), channel_id=1, source_target_pairs={{0,2},{2,0},{4,6},{6,4},{8,10},{10,8},{12,14},{14,12},{16,18},{18,... | collective-permute-start | bytes 663560 | tf_op jit(solution)/shard_map/ppermute | solution.py:678
  39.4 4.8 %collective-permute-start.14 = (bf16[1,2,8,72,384]{4,3,2,1,0:T(8,128)(2,1)S(1)}, bf16[1,2,8,72,384]{4,3,2,1,0:T(8,128)(2,1)S(1)}, u32[]{:S(2)}, u32[]{:S(2)}) collective-permute-start(bf16[1,2,8,72,384]{4,3,2,1,0:T(8,128)(2,1)S(1)} %get-tuple-element.134), channel_id=1, source_target_pairs={{0,2},{2,0},{4,6},{6,4},{8,10},{10,8},{12,14},{14,12},{16,18},{18,... | collective-permute-start | bytes 2654216 | tf_op jit(solution)/shard_map/ppermute | solution.py:678
  43.8 5.2 %collective-permute-start.16 = (bf16[2,2,8,72,384]{4,3,2,1,0:T(8,128)(2,1)S(1)}, bf16[2,2,8,72,384]{4,3,2,1,0:T(8,128)(2,1)S(1)}, u32[]{:S(2)}, u32[]{:S(2)}) collective-permute-start(bf16[2,2,8,72,384]{4,3,2,1,0:T(8,128)(2,1)S(1)} %get-tuple-element.147), channel_id=1, source_target_pairs={{0,2},{2,0},{4,6},{6,4},{8,10},{10,8},{12,14},{14,12},{16,18},{18,... | collective-permute-start | bytes 5308424 | tf_op jit(solution)/shard_map/ppermute | solution.py:678
  44.4 13.4 %collective-permute-start.15 = (bf16[8,72,384]{2,1,0:T(8,128)(2,1)S(1)}, bf16[8,72,384]{2,1,0:T(8,128)(2,1)S(1)}, u32[]{:S(2)}, u32[]{:S(2)}) collective-permute-start(bf16[8,72,384]{2,1,0:T(8,128)(2,1)S(1)} %get-tuple-element.137), channel_id=1, source_target_pairs={{0,1},{1,0},{2,3},{3,2},{4,5},{5,4},{6,7},{7,6},{8,9},{9,8},{10,11... | collective-permute-start | bytes 1327112 | tf_op jit(solution)/shard_map/ppermute | solution.py:678
  49.6 13.1 %collective-permute-start.19 = (bf16[2,4,72,384]{3,2,1,0:T(8,128)(2,1)S(1)}, bf16[2,4,72,384]{3,2,1,0:T(8,128)(2,1)S(1)}, u32[]{:S(2)}, u32[]{:S(2)}) collective-permute-start(bf16[2,4,72,384]{3,2,1,0:T(8,128)(2,1)S(1)} %get-tuple-element.154), channel_id=1, source_target_pairs={{0,4},{2,6},{4,0},{6,2},{8,12},{10,14},{12,8},{14,10},{16,20},{18,... | collective-permute-start | bytes 1327112 | tf_op jit(solution)/shard_map/ppermute | solution.py:678
  51.1 11.9 %collective-permute-start.20 = (bf16[4,2,72,384]{3,2,1,0:T(8,128)(2,1)S(1)}, bf16[4,2,72,384]{3,2,1,0:T(8,128)(2,1)S(1)}, u32[]{:S(2)}, u32[]{:S(2)}) collective-permute-start(bf16[4,2,72,384]{3,2,1,0:T(8,128)(2,1)S(1)} %get-tuple-element.156), channel_id=1, source_target_pairs={{0,8},{2,10},{4,12},{6,14},{8,0},{10,2},{12,4},{14,6},{16,24},{18,... | collective-permute-start | bytes 1327112 | tf_op jit(solution)/shard_map/ppermute | solution.py:678
  57.9 11.5 %collective-permute-start.17 = (bf16[4,72,384]{2,1,0:T(8,128)(2,1)S(1)}, bf16[4,72,384]{2,1,0:T(8,128)(2,1)S(1)}, u32[]{:S(2)}, u32[]{:S(2)}) collective-permute-start(bf16[4,72,384]{2,1,0:T(8,128)(2,1)S(1)} %get-tuple-element.151), channel_id=1, source_target_pairs={{0,4},{2,6},{4,0},{6,2},{8,12},{10,14},{12,8},{14,10},{16,20},{18,... | collective-permute-start | bytes 663560 | tf_op jit(solution)/shard_map/ppermute | solution.py:678
  58.8 8.6 %collective-permute-start.18 = (bf16[1,2,8,80,384]{4,3,2,1,0:T(8,128)(2,1)S(1)}, bf16[1,2,8,80,384]{4,3,2,1,0:T(8,128)(2,1)S(1)}, u32[]{:S(2)}, u32[]{:S(2)}) collective-permute-start(bf16[1,2,8,80,384]{4,3,2,1,0:T(8,128)(2,1)S(1)} %get-tuple-element.153), channel_id=1, source_target_pairs={{0,2},{2,0},{4,6},{6,4},{8,10},{10,8},{12,14},{14,12},{16,18},{18,... | collective-permute-start | bytes 2949128 | tf_op jit(solution)/shard_map/ppermute | solution.py:678
  63.2 12.2 %collective-permute-start.21 = (bf16[2,2,72,384]{3,2,1,0:T(8,128)(2,1)S(1)}, bf16[2,2,72,384]{3,2,1,0:T(8,128)(2,1)S(1)}, u32[]{:S(2)}, u32[]{:S(2)}) collective-permute-start(bf16[2,2,72,384]{3,2,1,0:T(8,128)(2,1)S(1)} %get-tuple-element.161), channel_id=1, source_target_pairs={{0,8},{2,10},{4,12},{6,14},{8,0},{10,2},{12,4},{14,6},{16,24},{18,... | collective-permute-start | bytes 663560 | tf_op jit(solution)/shard_map/ppermute | solution.py:678
  64.8 10.6 %collective-permute-start.22 = (bf16[2,2,72,384]{3,2,1,0:T(8,128)(2,1)S(1)}, bf16[2,2,72,384]{3,2,1,0:T(8,128)(2,1)S(1)}, u32[]{:S(2)}, u32[]{:S(2)}) collective-permute-start(bf16[2,2,72,384]{3,2,1,0:T(8,128)(2,1)S(1)} %get-tuple-element.163), channel_id=1, source_target_pairs={{0,16},{2,18},{4,20},{6,22},{8,24},{10,26},{12,28},{14,30},{16,0},... | collective-permute-start | bytes 663560 | tf_op jit(solution)/shard_map/ppermute | solution.py:678
  67.6 9.0 %collective-permute-start.23 = (bf16[2,2,80,384]{3,2,1,0:T(8,128)(2,1)S(1)}, bf16[2,2,80,384]{3,2,1,0:T(8,128)(2,1)S(1)}, u32[]{:S(2)}, u32[]{:S(2)}) collective-permute-start(bf16[2,2,80,384]{3,2,1,0:T(8,128)(2,1)S(1)} %get-tuple-element.164), channel_id=1, source_target_pairs={{0,1},{1,0},{2,3},{3,2},{4,5},{5,4},{6,7},{7,6},{8,9},{9,8},{10,11... | collective-permute-start | bytes 737288 | tf_op jit(solution)/shard_map/ppermute | solution.py:678
  68.2 8.4 %collective-permute-start.24 = (bf16[2,2,80,384]{3,2,1,0:T(8,128)(2,1)S(1)}, bf16[2,2,80,384]{3,2,1,0:T(8,128)(2,1)S(1)}, u32[]{:S(2)}, u32[]{:S(2)}) collective-permute-start(bf16[2,2,80,384]{3,2,1,0:T(8,128)(2,1)S(1)} %get-tuple-element.166), channel_id=1, source_target_pairs={{0,4},{2,6},{4,0},{6,2},{8,12},{10,14},{12,8},{14,10},{16,20},{18,... | collective-permute-start | bytes 737288 | tf_op jit(solution)/shard_map/ppermute | solution.py:678
  69.4 7.2 %collective-permute-start.25 = (bf16[2,72,384]{2,1,0:T(8,128)(2,1)S(1)}, bf16[2,72,384]{2,1,0:T(8,128)(2,1)S(1)}, u32[]{:S(2)}, u32[]{:S(2)}) collective-permute-start(bf16[2,72,384]{2,1,0:T(8,128)(2,1)S(1)} %get-tuple-element.167), channel_id=1, source_target_pairs={{0,8},{2,10},{4,12},{6,14},{8,0},{10,2},{12,4},{14,6},{16,24},{18,... | collective-permute-start | bytes 331784 | tf_op jit(solution)/shard_map/ppermute | solution.py:678
  76.8 9.3 %collective-permute-start.28 = (bf16[2,80,384]{2,1,0:T(8,128)(2,1)S(1)}, bf16[2,80,384]{2,1,0:T(8,128)(2,1)S(1)}, u32[]{:S(2)}, u32[]{:S(2)}) collective-permute-start(bf16[2,80,384]{2,1,0:T(8,128)(2,1)S(1)} %get-tuple-element.173), channel_id=1, source_target_pairs={{0,4},{2,6},{4,0},{6,2},{8,12},{10,14},{12,8},{14,10},{16,20},{18,... | collective-permute-start | bytes 368648 | tf_op jit(solution)/shard_map/ppermute | solution.py:678
  77.5 8.6 %collective-permute-start.29 = (bf16[2,80,384]{2,1,0:T(8,128)(2,1)S(1)}, bf16[2,80,384]{2,1,0:T(8,128)(2,1)S(1)}, u32[]{:S(2)}, u32[]{:S(2)}) collective-permute-start(bf16[2,80,384]{2,1,0:T(8,128)(2,1)S(1)} %get-tuple-element.175), channel_id=1, source_target_pairs={{0,1},{1,0},{2,3},{3,2},{4,5},{5,4},{6,7},{7,6},{8,9},{9,8},{10,11... | collective-permute-start | bytes 368648 | tf_op jit(solution)/shard_map/ppermute | solution.py:678
  78.0 8.1 %collective-permute-start.26 = (bf16[2,72,384]{2,1,0:T(8,128)(2,1)S(1)}, bf16[2,72,384]{2,1,0:T(8,128)(2,1)S(1)}, u32[]{:S(2)}, u32[]{:S(2)}) collective-permute-start(bf16[2,72,384]{2,1,0:T(8,128)(2,1)S(1)} %get-tuple-element.169), channel_id=1, source_target_pairs={{0,1},{1,0},{2,3},{3,2},{4,5},{5,4},{6,7},{7,6},{8,9},{9,8},{10,11... | collective-permute-start | bytes 331784 | tf_op jit(solution)/shard_map/ppermute | solution.py:678
  79.5 6.6 %collective-permute-start.27 = (bf16[2,72,384]{2,1,0:T(8,128)(2,1)S(1)}, bf16[2,72,384]{2,1,0:T(8,128)(2,1)S(1)}, u32[]{:S(2)}, u32[]{:S(2)}) collective-permute-start(bf16[2,72,384]{2,1,0:T(8,128)(2,1)S(1)} %get-tuple-element.171), channel_id=1, source_target_pairs={{0,4},{2,6},{4,0},{6,2},{8,12},{10,14},{12,8},{14,10},{16,20},{18,... | collective-permute-start | bytes 331784 | tf_op jit(solution)/shard_map/ppermute | solution.py:678
  80.9 5.2 %collective-permute-start.30 = (bf16[72,384]{1,0:T(8,128)(2,1)S(1)}, bf16[72,384]{1,0:T(8,128)(2,1)S(1)}, u32[]{:S(2)}, u32[]{:S(2)}) collective-permute-start(bf16[72,384]{1,0:T(8,128)(2,1)S(1)} %get-tuple-element.177), channel_id=1, source_target_pairs={{0,16},{2,18},{4,20},{6,22},{8,24},{10,26},{12,28},{14,30},{16,0},... | collective-permute-start | bytes 165896 | tf_op jit(solution)/shard_map/ppermute | solution.py:678
  86.2 12.2 %collective-permute-start.33 = (bf16[2,80,384]{2,1,0:T(8,128)(2,1)S(1)}, bf16[2,80,384]{2,1,0:T(8,128)(2,1)S(1)}, u32[]{:S(2)}, u32[]{:S(2)}) collective-permute-start(bf16[2,80,384]{2,1,0:T(8,128)(2,1)S(1)} %get-tuple-element.182), channel_id=1, source_target_pairs={{0,8},{2,10},{4,12},{6,14},{8,0},{10,2},{12,4},{14,6},{16,24},{18,... | collective-permute-start | bytes 368648 | tf_op jit(solution)/shard_map/ppermute | solution.py:678
  87.8 5.7 %collective-permute-start.31 = (bf16[72,384]{1,0:T(8,128)(2,1)S(1)}, bf16[72,384]{1,0:T(8,128)(2,1)S(1)}, u32[]{:S(2)}, u32[]{:S(2)}) collective-permute-start(bf16[72,384]{1,0:T(8,128)(2,1)S(1)} %get-tuple-element.179), channel_id=1, source_target_pairs={{0,16},{2,18},{4,20},{6,22},{8,24},{10,26},{12,28},{14,30},{16,0},... | collective-permute-start | bytes 165896 | tf_op jit(solution)/shard_map/ppermute | solution.py:678
  91.2 4.2 %collective-permute-start.32 = (bf16[72,384]{1,0:T(8,128)(2,1)S(1)}, bf16[72,384]{1,0:T(8,128)(2,1)S(1)}, u32[]{:S(2)}, u32[]{:S(2)}) collective-permute-start(bf16[72,384]{1,0:T(8,128)(2,1)S(1)} %get-tuple-element.180), channel_id=1, source_target_pairs={{0,1},{1,0},{2,3},{3,2},{4,5},{5,4},{6,7},{7,6},{8,9},{9,8},{10,11... | collective-permute-start | bytes 165896 | tf_op jit(solution)/shard_map/ppermute | solution.py:678
  91.7 6.8 %collective-permute-start.34 = (bf16[72,384]{1,0:T(8,128)(2,1)S(1)}, bf16[72,384]{1,0:T(8,128)(2,1)S(1)}, u32[]{:S(2)}, u32[]{:S(2)}) collective-permute-start(bf16[72,384]{1,0:T(8,128)(2,1)S(1)} %get-tuple-element.183.refs_5_), channel_id=1, source_target_pairs={{0,16},{2,18},{4,20},{6,22},{8,24},{10,26},{12,28},{14,30},{16,0},... | collective-permute-start | bytes 165896 | tf_op jit(solution)/shard_map/ppermute | solution.py:678
  98.5 7.8 %collective-permute-start.35 = (bf16[2,72,384]{2,1,0:T(8,128)(2,1)S(1)}, bf16[2,72,384]{2,1,0:T(8,128)(2,1)S(1)}, u32[]{:S(2)}, u32[]{:S(2)}) collective-permute-start(bf16[2,72,384]{2,1,0:T(8,128)(2,1)S(1)} %get-tuple-element.184.refs_0_), channel_id=1, source_target_pairs={{0,16},{2,18},{4,20},{6,22},{8,24},{10,26},{12,28},{14,30},{16,0},... | collective-permute-start | bytes 331784 | tf_op jit(solution)/shard_map/ppermute | solution.py:678
  98.6 7.7 %collective-permute-start.37 = (bf16[2,72,384]{2,1,0:T(8,128)(2,1)S(1)}, bf16[2,72,384]{2,1,0:T(8,128)(2,1)S(1)}, u32[]{:S(2)}, u32[]{:S(2)}) collective-permute-start(bf16[2,72,384]{2,1,0:T(8,128)(2,1)S(1)} %get-tuple-element.187.refs_4_), channel_id=1, source_target_pairs={{0,8},{2,10},{4,12},{6,14},{8,0},{10,2},{12,4},{14,6},{16,24},{18,... | collective-permute-start | bytes 331784 | tf_op jit(solution)/shard_map/ppermute | solution.py:678
  100.9 5.4 %collective-permute-start.36 = (bf16[80,384]{1,0:T(8,128)(2,1)S(1)}, bf16[80,384]{1,0:T(8,128)(2,1)S(1)}, u32[]{:S(2)}, u32[]{:S(2)}) collective-permute-start(bf16[80,384]{1,0:T(8,128)(2,1)S(1)} %get-tuple-element.186), channel_id=1, source_target_pairs={{0,16},{2,18},{4,20},{6,22},{8,24},{10,26},{12,28},{14,30},{16,0},... | collective-permute-start | bytes 184328 | tf_op jit(solution)/shard_map/ppermute | solution.py:678
  106.4 9.5 %collective-permute-start.41 = (bf16[2,2,72,384]{3,2,1,0:T(8,128)(2,1)S(1)}, bf16[2,2,72,384]{3,2,1,0:T(8,128)(2,1)S(1)}, u32[]{:S(2)}, u32[]{:S(2)}) collective-permute-start(bf16[2,2,72,384]{3,2,1,0:T(8,128)(2,1)S(1)} %get-tuple-element.191.refs_4_), channel_id=1, source_target_pairs={{0,4},{2,6},{4,0},{6,2},{8,12},{10,14},{12,8},{14,10},{16,20},{18,... | collective-permute-start | bytes 663560 | tf_op jit(solution)/shard_map/ppermute | solution.py:678
  106.9 6.3 %collective-permute-start.38 = (bf16[80,384]{1,0:T(8,128)(2,1)S(1)}, bf16[80,384]{1,0:T(8,128)(2,1)S(1)}, u32[]{:S(2)}, u32[]{:S(2)}) collective-permute-start(bf16[80,384]{1,0:T(8,128)(2,1)S(1)} %get-tuple-element.188.refs_0_), channel_id=1, source_target_pairs={{0,16},{2,18},{4,20},{6,22},{8,24},{10,26},{12,28},{14,30},{16,0},... | collective-permute-start | bytes 184328 | tf_op jit(solution)/shard_map/ppermute | solution.py:678
  108.0 7.9 %collective-permute-start.39 = (bf16[2,72,384]{2,1,0:T(8,128)(2,1)S(1)}, bf16[2,72,384]{2,1,0:T(8,128)(2,1)S(1)}, u32[]{:S(2)}, u32[]{:S(2)}) collective-permute-start(bf16[2,72,384]{2,1,0:T(8,128)(2,1)S(1)} %get-tuple-element.189.refs_0_), channel_id=1, source_target_pairs={{0,4},{2,6},{4,0},{6,2},{8,12},{10,14},{12,8},{14,10},{16,20},{18,... | collective-permute-start | bytes 331784 | tf_op jit(solution)/shard_map/ppermute | solution.py:678
  110.0 5.9 %collective-permute-start.40 = (bf16[2,72,384]{2,1,0:T(8,128)(2,1)S(1)}, bf16[2,72,384]{2,1,0:T(8,128)(2,1)S(1)}, u32[]{:S(2)}, u32[]{:S(2)}) collective-permute-start(bf16[2,72,384]{2,1,0:T(8,128)(2,1)S(1)} %get-tuple-element.190.refs_2_), channel_id=1, source_target_pairs={{0,8},{2,10},{4,12},{6,14},{8,0},{10,2},{12,4},{14,6},{16,24},{18,... | collective-permute-start | bytes 331784 | tf_op jit(solution)/shard_map/ppermute | solution.py:678
  116.0 9.7 %collective-permute-start.47 = (bf16[2,2,72,384]{3,2,1,0:T(8,128)(2,1)S(1)}, bf16[2,2,72,384]{3,2,1,0:T(8,128)(2,1)S(1)}, u32[]{:S(2)}, u32[]{:S(2)}) collective-permute-start(bf16[2,2,72,384]{3,2,1,0:T(8,128)(2,1)S(1)} %get-tuple-element.199.refs_2_), channel_id=1, source_target_pairs={{0,4},{2,6},{4,0},{6,2},{8,12},{10,14},{12,8},{14,10},{16,20},{18,... | collective-permute-start | bytes 663560 | tf_op jit(solution)/shard_map/ppermute | solution.py:678
  116.3 9.3 %collective-permute-start.46 = (bf16[2,2,72,384]{3,2,1,0:T(8,128)(2,1)S(1)}, bf16[2,2,72,384]{3,2,1,0:T(8,128)(2,1)S(1)}, u32[]{:S(2)}, u32[]{:S(2)}) collective-permute-start(bf16[2,2,72,384]{3,2,1,0:T(8,128)(2,1)S(1)} %get-tuple-element.193.refs_4_.refs_0_), channel_id=1, source_target_pairs={{0,8},{2,10},{4,12},{6,14},{8,0},{10,2},{12,4},{14,6},{16,24},{18,... | collective-permute-start | bytes 663560 | tf_op jit(solution)/shard_map/ppermute | solution.py:678
  122.1 11.5 %collective-permute-start.45 = (bf16[2,80,384]{2,1,0:T(8,128)(2,1)S(1)}, bf16[2,80,384]{2,1,0:T(8,128)(2,1)S(1)}, u32[]{:S(2)}, u32[]{:S(2)}) collective-permute-start(bf16[2,80,384]{2,1,0:T(8,128)(2,1)S(1)} %share_qkv_out_high.1.refs_4_.refs_0_), channel_id=1, source_target_pairs={{0,12},{2,14},{4,8},{6,10},{8,4},{10,6},{12,0},{14,2},{16,28},{18,... | collective-permute-start | bytes 368648 | tf_op jit(solution)/shard_map/ppermute | solution.py:678
  125.0 8.6 %collective-permute-start.44 = (bf16[2,80,384]{2,1,0:T(8,128)(2,1)S(1)}, bf16[2,80,384]{2,1,0:T(8,128)(2,1)S(1)}, u32[]{:S(2)}, u32[]{:S(2)}) collective-permute-start(bf16[2,80,384]{2,1,0:T(8,128)(2,1)S(1)} %share_qkv_out_high.1.refs_4_.refs_0_), channel_id=1, source_target_pairs={{0,8},{2,10},{4,12},{6,14},{8,0},{10,2},{12,4},{14,6},{16,24},{18,... | collective-permute-start | bytes 368648 | tf_op jit(solution)/shard_map/ppermute | solution.py:678
  125.6 8.0 %collective-permute-start.43 = (bf16[2,80,384]{2,1,0:T(8,128)(2,1)S(1)}, bf16[2,80,384]{2,1,0:T(8,128)(2,1)S(1)}, u32[]{:S(2)}, u32[]{:S(2)}) collective-permute-start(bf16[2,80,384]{2,1,0:T(8,128)(2,1)S(1)} %share_qkv_out_high.1.refs_4_.refs_0_), channel_id=1, source_target_pairs={{0,4},{2,6},{4,0},{6,2},{8,12},{10,14},{12,8},{14,10},{16,20},{18,... | collective-permute-start | bytes 368648 | tf_op jit(solution)/shard_map/ppermute | solution.py:678
  125.7 4.0 %collective-permute-start.48 = (bf16[2,2,4,72,384]{4,3,2,1,0:T(8,128)(2,1)S(1)}, bf16[2,2,4,72,384]{4,3,2,1,0:T(8,128)(2,1)S(1)}, u32[]{:S(2)}, u32[]{:S(2)}) collective-permute-start(bf16[2,2,4,72,384]{4,3,2,1,0:T(8,128)(2,1)S(1)} %share_gate_up.1.refs_0_), channel_id=1, source_target_pairs={{0,2},{2,0},{4,6},{6,4},{8,10},{10,8},{12,14},{14,12},{16,18},{18,... | collective-permute-start | bytes 2654216 | tf_op jit(solution)/shard_map/ppermute | solution.py:678
  133.8 6.6 %collective-permute-start.49 = (bf16[1,2,4,80,384]{4,3,2,1,0:T(8,128)(2,1)S(1)}, bf16[1,2,4,80,384]{4,3,2,1,0:T(8,128)(2,1)S(1)}, u32[]{:S(2)}, u32[]{:S(2)}) collective-permute-start(bf16[1,2,4,80,384]{4,3,2,1,0:T(8,128)(2,1)S(1)} %share_qkv_out.1.refs_0_), channel_id=1, source_target_pairs={{0,2},{2,0},{4,6},{6,4},{8,10},{10,8},{12,14},{14,12},{16,18},{18,... | collective-permute-start | bytes 1474568 | tf_op jit(solution)/shard_map/ppermute | solution.py:678
  (27 other events, 126.9 us)

commit v8 on v7

--- a/solution.py
+++ b/solution.py
@@ -56,6 +56,17 @@
     fix_two = 1.0 / (1.0 - BETA_TWO**STEP)
     update = first_new * fix_one / (jnp.sqrt(second_new * fix_two) + EPS_ADAM)
     return (first_new, second_new, weight - step_rate * (update + weight_decay * weight))
+
+
+def adamw_rows(weight, first_moment, second_moment, gradient, step_rate, weight_decay):
+    first_new = BETA_ONE * first_moment + (1.0 - BETA_ONE) * gradient
+    second_new = BETA_TWO * second_moment + (1.0 - BETA_TWO) * gradient * gradient
+    value = second_new * (1.0 / (1.0 - BETA_TWO**STEP))
+    guess = lax.rsqrt(value)
+    divisor = value * guess + EPS_ADAM
+    inverse = guess * (2.0 - divisor * guess)
+    update = first_new * (step_rate / (1.0 - BETA_ONE**STEP)) * inverse
+    return (first_new, second_new, weight * (1.0 - step_rate * weight_decay) - update)
 
 
 def dot(left, right):
@@ -376,7 +387,7 @@
         [w_qkv_out, w_gate_up],
         outs,
         scratch,
-        2,
+        5,
         "feed_forward",
         after,
         True,
@@ -595,6 +606,7 @@
 def update_half(idx, far, pieces, place, height, state, earlier, gains, name, after):
     count = len(state) // 3
     columns = [a.shape[1] for a in state[:count]]
+    starts = [sum(-(-c // LANES) * LANES for c in columns[:k]) for k in range(count + 1)]
     chunks = height // CUT_ROWS
     order = [(k, count + k, 2 * count + k) for k in range(count)]
 
@@ -609,12 +621,18 @@
         mark[...] = jnp.zeros_like(mark)
         for part in range(pieces.shape[0]):
             for x in range(2):
-                for slot in range(4):
-                    z = (slot >> 1) | ((slot & 1) << 1)
-                    row, column = place(part, idx_ref[2] ^ x, idx_ref[3] ^ z)
+                for z in range(4):
+                    rel = z ^ idx_ref[3]
+                    slot = ((rel & 1) << 1) | (rel >> 1)
+                    piece = piece_ref[part, x, slot].astype(F32)[:CUT_ROWS]
+                    row, cuts = place(part, idx_ref[2] ^ x, z)
                     rows = pl.ds(pl.multiple_of(row, 8), CUT_ROWS)
-                    where = pl.ds(pl.multiple_of(column, LANES), CUT_COLUMNS)
-                    full[rows, where] = piece_ref[part, x, slot, :CUT_ROWS, :].astype(F32)
+                    for begin, size, to in cuts:
+                        if isinstance(to, int):
+                            where = slice(to, to + size)
+                        else:
+                            where = pl.ds(pl.multiple_of(to, LANES), size)
+                        full[rows, where] = piece[:, begin : begin + size]
         base = (idx_ref[1] ^ far) * height
         copies = []
         for chunk in range(chunks):
@@ -622,20 +640,18 @@
             def eight_rows(i, carry, chunk=chunk):
                 near_rows = pl.ds(pl.multiple_of(chunk * CUT_ROWS + i * 8, 8), 8)
                 rows = pl.ds(pl.multiple_of(base + chunk * CUT_ROWS + i * 8, 8), 8)
-                start = 0
                 for k in range(count):
                     for at in range(0, columns[k], 768):
                         size = min(768, columns[k] - at)
                         where = slice(at, at + size)
-                        results = adamw(
+                        results = adamw_rows(
                             *[state_refs[j][rows, where] for j in order[k]],
-                            full[near_rows, start + at : start + at + size],
+                            full[near_rows, starts[k] + at : starts[k] + at + size],
                             RATE_MATRIX,
                             DECAY_MATRIX,
                         )
                         for j, result in zip(order[k], results):
                             buffers[j][near_rows, where] = result
-                    start += columns[k]
                 return carry
 
             lax.fori_loop(0, CUT_ROWS // 8, eight_rows, 0)
@@ -649,7 +665,7 @@
                 copies.append(copy)
         if gains:
             gradient = piece_ref[0, 0, 0, CUT_ROWS:, :].astype(F32)[:2, : gains[0].shape[1]]
-            results = adamw(*[g[...] for g in gain_refs], gradient, RATE_GAIN, 0.0)
+            results = adamw_rows(*[g[...] for g in gain_refs], gradient, RATE_GAIN, 0.0)
             for out, result in zip(gain_outs, results):
                 out[...] = result
         for copy in copies:
@@ -665,7 +681,7 @@
         + [anywhere] * (len(earlier) + len(after)),
         out_specs=tuple([anywhere] * (3 * count) + [vmem] * (len(gains) + 1)),
         scratch_shapes=[pltpu.VMEM((height, a.shape[1]), F32) for a in state]
-        + [pltpu.VMEM((height, sum(columns)), F32), pltpu.SemaphoreType.DMA((chunks, 3 * count))],
+        + [pltpu.VMEM((height, starts[-1]), F32), pltpu.SemaphoreType.DMA((chunks, 3 * count))],
         input_output_aliases={first_earlier + i: i for i in range(len(earlier))},
         compiler_params=pltpu.CompilerParams(vmem_limit_bytes=VMEM_LIMIT),
         cost_estimate=busy_for(20),
@@ -788,7 +804,7 @@
         mat_gate_up = Weight(whole.shape, whole=whole)
 
         (down_near,) = step(
-            pass_on, [down_near], [sds(down_near.shape, BF16)], "pass_on", (normed_low,)
+            pass_on, [down_near], [sds(down_near.shape, BF16)], "pass_on", (attended,), 0.1
         )
         down_place = lambda o, c, x, low: (c * 2 * HALF, o * down_rows)
         mat_down = Weight(
@@ -852,131 +868,122 @@
         (send_up, keep_up), (send_low, keep_low) = add_step(
             [
                 (cut(keep_up, 2, 2, 2), cut(arrived_up, 2, 2, 2), 1),
-                (cut(keep_low, 2, 2, 2), cut(arrived_low, 2, 2, 2), 2),
+                (cut(keep_low, 2, 2, 2), cut(arrived_low, 2, 2, 2), 1),
             ],
             "up_x_low_z",
             (keep_down,),
         )
-        arrived_up, arrived_low = over_z_low(send_up), over_z_high(send_low)
-
-        def qkv_out_core(ins, outs):
-            total = ins[0][...].astype(F32) + ins[1][...].astype(F32)
-            outs[0][...] = total[1, :, 0].astype(BF16)
-            outs[1][...] = total[0, :, 0]
-            outs[2][...] = total[:, 1, 1].astype(BF16)
-            outs[3][...] = total[:, 0, 1]
-
-        send_a, keep_a, send_b, keep_b = step(
-            qkv_out_core,
-            [cut(a, 2, 2, 2, 2) for a in (grad_qkv_out[1], arrived_qkv_out)],
-            [sds((2, 2, *taller), t) for t in (BF16, F32, BF16, F32)],
-            "qkv_out_core",
-            (keep_up,),
-        )
-        arrived_a, arrived_b = over_y(send_a), over_x(send_b)
+        arrived_up, arrived_low = over_z_low(send_up), over_x(send_low)
+        ((send, keep_qkv_out),) = add_step(
+            [(grad_qkv_out[1][0], arrived_qkv_out[0], 0)], "qkv_out_core", (keep_up,)
+        )
+        arrived_qkv_out = over_y(send)
         ((send, keep_down),) = add_step(
-            [(cut(keep_down, 2, 2), cut(arrived_down, 2, 2), 0)], "down_x", (keep_a,)
+            [(cut(keep_down, 2, 2), cut(arrived_down, 2, 2), 0)], "down_x", (keep_qkv_out,)
         )
         arrived_down = over_z_low(send)
-        output = layer_output(middle, hidden, down_whole, (keep_down,))
-        sums = add_step(
-            [
-                (keep_up, arrived_up, 0),
-                (keep_low, arrived_low, 1),
-                (keep_a, arrived_a, 0),
-                (keep_b, arrived_b, 0),
-                (keep_down, arrived_down, 0),
-            ],
-            "up_z_low_y_qkv_out_xy",
-            (keep_down,),
-        )
-        (send_up, keep_up), (send_low, keep_low), (send_a, keep_a), (send_b, keep_b) = sums[:4]
-        ((send, keep_down),) = sums[4:]
-        arrived_up, arrived_low = over_y(send_up), over_x(send_low)
-        arrived_a, arrived_b = over_x(send_a), over_y(send_b)
-        arrived_down = over_z_high(send)
-
-        def planes(ins, outs):
-            for i in range(2):
-                total = ins[2 * i][...] + ins[2 * i + 1][...].astype(F32)
-                outs[i][...] = total[1].astype(BF16)
-                outs[2][i] = total[0]
-            outs[3][...] = (ins[6][...] + ins[7][...].astype(F32)).astype(BF16)
-            outs[4][...] = ins[4][...] + ins[5][...].astype(F32)
-            outs[5][...] = (ins[8][...] + ins[9][...].astype(F32)).astype(BF16)
-
-        send_up, send_low, keep, send_qkv_out, keep_qkv_out, piece_down = step(
-            planes,
+
+        def columns(ins, outs):
+            for part in range(2):
+                total = ins[2 * part][...] + ins[2 * part + 1][...].astype(F32)
+                outs[0][part] = total[1].astype(BF16)
+                outs[1][part] = total[0]
+            for i in (1, 2):
+                total = ins[2 * i + 2][...] + ins[2 * i + 3][...].astype(F32)
+                outs[2 * i][...] = total[1].astype(BF16)
+                outs[2 * i + 1][...] = total[0]
+
+        send, keep, send_qkv_out, keep_qkv_out, send_down, keep_down = step(
+            columns,
             [
                 *(keep_up, arrived_up, keep_low, arrived_low),
-                *(keep_a, arrived_a, keep_b, arrived_b),
+                *(cut(keep_qkv_out, 2, 4), cut(arrived_qkv_out, 2, 4)),
                 *(keep_down, arrived_down),
             ],
             [
-                *(sds(piece, BF16), sds(piece, BF16), sds((2, *piece), F32)),
+                *(sds((2, 2, *piece), BF16), sds((2, 2, *piece), F32)),
+                *(sds((4, *taller), BF16), sds((4, *taller), F32)),
+                *(sds(piece, BF16), sds(piece, F32)),
+            ],
+            "columns",
+        )
+        arrived, arrived_qkv_out = over_y(send), over_x(send_qkv_out)
+        arrived_down = over_z_high(send_down)
+
+        def planes(ins, outs):
+            for part in range(2):
+                total = ins[0][part] + ins[1][part].astype(F32)
+                outs[0][part] = total[1].astype(BF16)
+                outs[1][part] = total[0]
+            outs[0][2] = (ins[4][...] + ins[5][...].astype(F32)).astype(BF16)
+            total = ins[2][...] + ins[3][...].astype(F32)
+            outs[2][...] = total[1].astype(BF16)
+            outs[3][...] = total[0]
+
+        send, keep, send_qkv_out, keep_qkv_out = step(
+            planes,
+            [
+                *(keep, arrived),
+                *(cut(keep_qkv_out, 2, 2), cut(arrived_qkv_out, 2, 2)),
+                *(keep_down, arrived_down),
+            ],
+            [
+                *(sds((3, *piece), BF16), sds((2, *piece), F32)),
                 *(sds((2, *taller), BF16), sds((2, *taller), F32)),
-                sds(piece, BF16),
             ],
             "planes",
         )
-        arrived_up, arrived_low = over_z_high(send_up), over_y(send_low)
-        arrived_qkv_out = over_z_low(send_qkv_out)
-        down_high = over_z_high(piece_down)
+        arrived, arrived_qkv_out = over_z_high(send), over_z_low(send_qkv_out)
 
         def lines(ins, outs):
+            send, keep, arrived, keep_qkv_out, arrived_qkv_out = ins
+            total = keep_qkv_out[...] + arrived_qkv_out[...].astype(F32)
+            outs[0][0] = total[1].astype(BF16)
+            outs[1][...] = total[0]
             for part in range(2):
-                total = ins[0][part] + ins[1 + part][...].astype(F32)
-                outs[0][part] = total.astype(BF16)
-            total = ins[3][...] + ins[4][...].astype(F32)
-            outs[1][...] = total[1].astype(BF16)
-            outs[2][...] = total[0]
-            outs[3][0], outs[3][1] = ins[5][...], ins[6][...]
-
-        pieces, send_qkv_out, keep_qkv_out, near_down = step(
+                total = keep[part] + arrived[part].astype(F32)
+                total = jnp.concatenate([total, jnp.zeros((8, CUT_COLUMNS), F32)], axis=0)
+                outs[0][part + 1] = total.astype(BF16)
+            outs[2][0], outs[2][1] = send[2], arrived[2]
+
+        pieces, keep_qkv_out, near_down = step(
             lines,
-            [keep, arrived_up, arrived_low, keep_qkv_out, arrived_qkv_out, piece_down, down_high],
-            [
-                sds((2, *piece), BF16),
-                *(sds(taller, BF16), sds(taller, F32)),
-                sds((2, *piece), BF16),
-            ],
+            [send, keep, arrived, keep_qkv_out, arrived_qkv_out],
+            [sds((3, *taller), BF16), sds(taller, F32), sds((2, *piece), BF16)],
             "lines",
         )
-        pieces_high = over_z_high(pieces)
-        arrived_qkv_out = over_z_high(send_qkv_out)
-        down_low = over_z_low(near_down)
+        arrived, down_low = over_z_high(pieces), over_z_low(near_down)
 
         def share_high(ins, outs):
-            for part in range(2):
-                outs[part][0], outs[part][1] = ins[0][part], ins[1][part]
-            outs[2][...] = (ins[2][...] + ins[3][...].astype(F32)).astype(BF16)
-            outs[3][0], outs[3][1] = ins[4][...], ins[5][...]
-
-        near_up, near_low, piece_qkv_out, near_down = step(
+            pieces, arrived, keep_qkv_out, near_down, down_low = ins
+            for high in range(2):
+                outs[0][0, high], outs[0][1, high] = near_down[high], down_low[high]
+            outs[0][2, 0], outs[0][2, 1] = pieces[1, :CUT_ROWS], arrived[1, :CUT_ROWS]
+            outs[1][0], outs[1][1] = pieces[2, :CUT_ROWS], arrived[2, :CUT_ROWS]
+            outs[2][...] = (keep_qkv_out[...] + arrived[0].astype(F32)).astype(BF16)
+
+        near_x, near_low, piece_qkv_out = step(
             share_high,
-            [pieces, pieces_high, keep_qkv_out, arrived_qkv_out, near_down, down_low],
-            [
-                *(sds((2, *piece), BF16), sds((2, *piece), BF16)),
-                sds(taller, BF16),
-                sds((2, 2, *piece), BF16),
-            ],
+            [pieces, arrived, keep_qkv_out, near_down, down_low],
+            [sds((3, 2, *piece), BF16), sds((2, *piece), BF16), sds(taller, BF16)],
             "share_high",
         )
-        up_x, low_low = over_x(near_up), over_z_low(near_low)
+        arrived_x, low_low = over_x(near_x), over_z_low(near_low)
         qkv_out_high = over_z_high(piece_qkv_out)
-        down_x = over_x(near_down)
+        output = layer_output(middle, hidden, down_whole, (near_x,))
 
         def share_next(ins, outs):
-            for i in range(2):
-                outs[i][0], outs[i][1] = ins[2 * i][...], ins[2 * i + 1][...]
-            for x in range(2):
-                for low in range(2):
-                    for high in range(2):
-                        outs[2][0, x, low * 2 + high] = ins[4 + x][low, high]
+            near_x, arrived_x, near_low, low_low = ins
+            outs[0][0], outs[0][1] = near_x[2], arrived_x[2]
+            outs[1][0], outs[1][1] = near_low[...], low_low[...]
+            for low in range(2):
+                for high in range(2):
+                    outs[2][0, 0, low * 2 + high] = near_x[low, high]
+                    outs[2][0, 1, low * 2 + high] = arrived_x[low, high]
 
         near_up, near_low, near_down = step(
             share_next,
-            [near_up, up_x, near_low, low_low, near_down, down_x],
+            [near_x, arrived_x, near_low, low_low],
             [
                 *(sds((2, 2, *piece), BF16), sds((2, 2, *piece), BF16)),
                 sds((1, 2, 4, *piece), BF16),
@@ -1001,7 +1008,10 @@
         one_down, two_down, next_down, mark = update(
             near_down,
             far_down,
-            lambda p, x, z: ((x * 2 + (z >> 1)) * CUT_ROWS, (z & 1) * CUT_COLUMNS),
+            lambda p, x, z: (
+                (x * 2 + (z >> 1)) * CUT_ROWS,
+                [(0, CUT_COLUMNS, (z & 1) * CUT_COLUMNS)],
+            ),
             2 * HALF,
             [down_t, first_down_t, second_down_t],
             (),
@@ -1040,7 +1050,7 @@
         one_gate_up, two_gate_up, next_gate_up, mark = update(
             near_gate_up,
             far_gate_up,
-            lambda p, x, z: (p * CUT_ROWS, (x * 4 + z) * CUT_COLUMNS),
+            lambda p, x, z: (p * CUT_ROWS, [(0, CUT_COLUMNS, (x * 4 + z) * CUT_COLUMNS)]),
             HALF,
             [w_gate_up, first_gate_up, second_gate_up],
             (),
@@ -1062,10 +1072,11 @@
             (mark,),
         )
         far_qkv_out = over_core(near_qkv_out)
+        cuts = [[(0, 384, 0)], [(0, 384, 384)], [(0, 192, 768), (192, 192, 1024)], [(0, 384, 1216)]]
         updated = update(
             near_qkv_out,
             far_qkv_out,
-            lambda p, x, z: (x * CUT_ROWS, z * CUT_COLUMNS),
+            lambda p, x, z: (x * CUT_ROWS, cuts[z]),
             HALF,
             [w_qkv, w_out, first_qkv, first_out, second_qkv, second_out],
             (norm_gains, first_gains, second_gains),

time: 145 us -> 140 us (0.966)
  starting transfers between devices: 52.1 us -> 38.6 us
  waiting for transfers between devices: 43.8 us -> 53.5 us
  Pallas kernels: 44.2 us -> 42.3 us
    ppermute x50 -> x43, starting transfers between devices: 52.1 us -> 38.6 us  [swap(): return lax.ppermute(values, axis, [(i, i ^ mask) for i in range(size)])]
    ppermute x50 -> x43, waiting for transfers between devices: 43.8 us -> 53.5 us  [swap(): return lax.ppermute(values, axis, [(i, i ^ mask) for i in range(size)])]
    pallas_call x6, Pallas kernels: 21.1 us -> 19.2 us  [update_half(): pl.pallas_call(kernel, out_shape=tuple((sds(a.shape, F32) for a in [*stat...]
  transfers between devices with their start and end apart: 50 -> 43, of which waited for: 17 -> 19; matrix products, arithmetic and copies ran while one was open for 0% -> 0% of each run, Pallas kernels for 25% -> 25%
where the time goes in v8:
time: 140 us; the launch traced here: 139 us
  waiting for transfers between devices  53.5 us (38%)
  Pallas kernels  42.3 us (30%)
  starting transfers between devices  38.6 us (28%)
  local copies, waits for them, and re-layouts  2.42 us (2%)
    ppermute x43, waiting for transfers between devices, swap(): return lax.ppermute(values, axis, [(i, i ^ mask) for i in range(size)])  53.5 us
    ppermute x43, starting transfers between devices, swap(): return lax.ppermute(values, axis, [(i, i ^ mask) for i in range(size)])  38.6 us
    pallas_call x6, Pallas kernels, update_half(): pl.pallas_call(kernel, out_shape=tuple((sds(a.shape, F32) for a in [*stat...  19.2 us
    pallas_call x5, Pallas kernels, call(): pl.pallas_call(kernel, out_shape=tuple(outs), in_specs=[pl.BlockSpec(memo...  15.8 us
    pallas_call x2, Pallas kernels, pack_kernel(): pl.pallas_call(kernel, out_shape=tuple(outs), in_specs=[pl.BlockSpec(memo...  3.97 us
    pallas_call x17, Pallas kernels, step(): pl.pallas_call(kernel, out_shape=tuple(outs), in_specs=[pl.BlockSpec(memo...  3.31 us
  transfers between devices with their start and end apart: 43, of which 19 were waited for; matrix products, arithmetic and copies ran while one was open for 0% of the time, Pallas kernels for 25%

profile of v8, /device:TPU:0, one launch (start us, length us, event | category | flops | bytes accessed | tf_op | source)
XLA Modules:
  0.0 138.8 jit_solution(10073425405588115546)
XLA Ops:
  1.3 3.2 %pack_first.1 = (bf16[160,768]{1,0:T(8,128)(2,1)}, bf16[144,768]{1,0:T(8,128)(2,1)}, bf16[144,768]{1,0:T(8,128)(2,1)}) custom-call(s32[4]{0:T(128)} %pad_add_fusion.idx_ref.refs_0_, f32[288,960]{1,0:T(8,128)} %refs_1_.9, f32[288,576]{1,0:T(8,128)} %refs_2_.11, f32[2,288]{1,0:T(2,128)} %refs_7_.3, f32[288,3072]{1,0:T(8,128)} %refs_1_.7, f32[288,3072]{1,0:T(8,128)} %refs_1_.7), custom_call_target="tpu_custom_call" | custom-call | flops 10000000000 | tf_op jit(solution)/shard_map/pack_first/pallas_call | solution.py:240
  4.4 3.0 %collective-permute-start = (bf16[160,768]{1,0:T(8,128)(2,1)}, bf16[160,768]{1,0:T(8,128)(2,1)S(1)}, u32[]{:S(2)}, u32[]{:S(2)}) collective-permute-start(bf16[160,768]{1,0:T(8,128)(2,1)} %get-tuple-element.112), channel_id=1, source_target_pairs={{0,1},{1,0},{2,3},{3,2},{4,5},{5,4},{6,7},{7,6},{8,9},{9,8},{10,11... | collective-permute-start | bytes 737288 | tf_op jit(solution)/shard_map/ppermute | solution.py:694
  7.6 1.9 %collective-permute-start.4 = (bf16[144,768]{1,0:T(8,128)(2,1)}, bf16[144,768]{1,0:T(8,128)(2,1)S(1)}, u32[]{:S(2)}, u32[]{:S(2)}) collective-permute-start(bf16[144,768]{1,0:T(8,128)(2,1)} %get-tuple-element.116), channel_id=1, source_target_pairs={{0,1},{1,0},{2,3},{3,2},{4,5},{5,4},{6,7},{7,6},{8,9},{9,8},{10,11... | collective-permute-start | bytes 663560 | tf_op jit(solution)/shard_map/ppermute | solution.py:694
  9.5 9.7 %collective-permute-done.8.refs_11_.refs_1_ = bf16[144,768]{1,0:T(8,128)(2,1)S(1)} collective-permute-done((bf16[144,768]{1,0:T(8,128)(2,1)}, bf16[144,768]{1,0:T(8,128)(2,1)S(1)}, u32[]{:S(2)}, u32[]{:S(2)}) %collective-permute-start.8) | collective-permute-done | bytes 221216 | tf_op jit(solution)/shard_map/ppermute | solution.py:694
  19.2 2.1 %collective-permute-start.9 = (bf16[144,768]{1,0:T(8,128)(2,1)S(1)}, bf16[144,768]{1,0:T(8,128)(2,1)S(1)}, u32[]{:S(2)}, u32[]{:S(2)}) collective-permute-start(bf16[144,768]{1,0:T(8,128)(2,1)S(1)} %collective-permute-done.8.refs_11_.refs_1_), channel_id=1, source_target_pairs={{0,8},{2,10},{4,12},{6,14},{8,0},{10,2},{12,4},{14,6},{16,24},{18,... | collective-permute-start | bytes 663560 | tf_op jit(solution)/shard_map/ppermute | solution.py:694
  21.4 0.8 pack_down.1
  22.3 2.0 %collective-permute-start.12 = (bf16[288,768]{1,0:T(8,128)(2,1)S(1)}, bf16[288,768]{1,0:T(8,128)(2,1)S(1)}, u32[]{:S(2)}, u32[]{:S(2)}) collective-permute-start(bf16[288,768]{1,0:T(8,128)(2,1)S(1)} %pack_down.1), channel_id=1, source_target_pairs={{0,1},{1,0},{2,3},{3,2},{4,5},{5,4},{6,7},{7,6},{8,9},{9,8},{10,11... | collective-permute-start | bytes 1327112 | tf_op jit(solution)/shard_map/ppermute | solution.py:694
  24.2 1.5 %collective-permute-start.5 = (bf16[144,768]{1,0:T(8,128)(2,1)S(1)}, bf16[144,768]{1,0:T(8,128)(2,1)S(1)}, u32[]{:S(2)}, u32[]{:S(2)}) collective-permute-start(bf16[144,768]{1,0:T(8,128)(2,1)S(1)} %collective-permute-done.4.refs_7_), channel_id=1, source_target_pairs={{0,4},{2,6},{4,0},{6,2},{8,12},{10,14},{12,8},{14,10},{16,20},{18,... | collective-permute-start | bytes 663560 | tf_op jit(solution)/shard_map/ppermute | solution.py:694
  25.7 1.4 %collective-permute-done.9.refs_12_ = bf16[144,768]{1,0:T(8,128)(2,1)S(1)} collective-permute-done((bf16[144,768]{1,0:T(8,128)(2,1)S(1)}, bf16[144,768]{1,0:T(8,128)(2,1)S(1)}, u32[]{:S(2)}, u32[]{:S(2)}) %collective-permute-start.9) | collective-permute-done | bytes 221216 | tf_op jit(solution)/shard_map/ppermute | solution.py:694
  27.2 3.4 %collective-permute-done.1.refs_9_ = bf16[160,768]{1,0:T(8,128)(2,1)S(1)} collective-permute-done((bf16[160,768]{1,0:T(8,128)(2,1)S(1)}, bf16[160,768]{1,0:T(8,128)(2,1)S(1)}, u32[]{:S(2)}, u32[]{:S(2)}) %collective-permute-start.1) | collective-permute-done | bytes 245792 | tf_op jit(solution)/shard_map/ppermute | solution.py:694
  30.5 1.0 collective-permute-done.5.refs_8_
  32.2 2.5 %attention.1 = (bf16[128,960]{1,0:T(8,128)(2,1)S(1)}, bf16[128,576]{1,0:T(8,128)(2,1)S(1)}, f32[128,128]{1,0:T(8,128)S(1)}, f32[128,128]{1,0:T(8,128)S(1)}, f32[...) custom-call(s32[4]{0:T(128)S(1)} %copy-done, bf16[576,128]{1,0:T(8,128)(2,1)S(1)} %bitcast.65, ...), custom_call_target="tpu_custom_call" | custom-call | flops 1000000000 | tf_op jit(solution)/shard_map/attention/pallas_call | solution.py:150
  35.4 2.8 %feed_forward.1 = (f32[128,576]{1,0:T(8,128)S(1)}, bf16[128,576]{1,0:T(8,128)(2,1)S(1)}, f32[128,3072]{1,0:T(8,128)S(1)}, bf16[128,1536]{1,0:T(8,128)(2,1)S(1)},...) custom-call(s32[4]{0:T(128)S(1)} %copy-done, ...), custom_call_target="tpu_custom_call" | custom-call | flops 5000000000 | tf_op jit(solution)/shard_map/feed_forward/pallas_call | solution.py:150
  38.4 2.6 %feed_back.1 = (bf16[128,3072]{1,0:T(8,128)(2,1)S(1)}, bf16[2,2,8,72,384]{4,3,2,1,0:T(8,128)(2,1)S(1)}, bf16[2,2,8,72,384]{4,3,2,1,0:T(8,128)(2,1)S(1)}, bf16[576,1536]{1,0:T(8,128)(2,1)S(1)}) custom-call(s32[4]{0:T(128)S(1)} %copy-done, f32[128,3072]{1,0:T(8,128)S(1)} %get-tuple-element.120.refs_1_, bf16[128,576]{1,0:T(8,128)(2,1)S(1)} %get-tuple-element.121.refs_2_, ...), custom_call_target="tpu_custom_call" | custom-call | flops 20000000000 | tf_op jit(solution)/shard_map/feed_back/pallas_call | solution.py:150
  41.9 1.6 %collective-permute-start.18 = (bf16[8,72,384]{2,1,0:T(8,128)(2,1)S(1)}, bf16[8,72,384]{2,1,0:T(8,128)(2,1)S(1)}, u32[]{:S(2)}, u32[]{:S(2)}) collective-permute-start(bf16[8,72,384]{2,1,0:T(8,128)(2,1)S(1)} %get-tuple-element.135), channel_id=1, source_target_pairs={{0,1},{1,0},{2,3},{3,2},{4,5},{5,4},{6,7},{7,6},{8,9},{9,8},{10,11... | collective-permute-start | bytes 1327112 | tf_op jit(solution)/shard_map/ppermute | solution.py:694
  43.5 2.7 %middle_back.1 = (f32[128,576]{1,0:T(8,128)S(1)}, bf16[128,576]{1,0:T(8,128)(2,1)S(1)}, f32[1,576]{1,0:T(1,128)S(1)}) custom-call(s32[4]{0:T(128)S(1)} %copy-done, bf16[576,128]{1,0:T(8,128)(2,1)S(1)} %bitcast.64, f32[128,576]{1,0:T(8,128)S(1)} %get-tuple-element.118.refs_2_.refs_0_, bf16[128,3072]{1,0:T(8,128)(2,1)S(1)} %get-tuple-element.125.refs_2_.refs_3_, ...), custom_call_target="tpu_custom_call" | custom-call | flops 20000000000 | tf_op jit(solution)/shard_map/middle_back/pallas_call | solution.py:150
  46.8 1.5 %collective-permute-start.16 = (bf16[2,4,72,384]{3,2,1,0:T(8,128)(2,1)S(1)}, bf16[2,4,72,384]{3,2,1,0:T(8,128)(2,1)S(1)}, u32[]{:S(2)}, u32[]{:S(2)}) collective-permute-start(bf16[2,4,72,384]{3,2,1,0:T(8,128)(2,1)S(1)} %get-tuple-element.132), channel_id=1, source_target_pairs={{0,4},{2,6},{4,0},{6,2},{8,12},{10,14},{12,8},{14,10},{16,20},{18,... | collective-permute-start | bytes 1327112 | tf_op jit(solution)/shard_map/ppermute | solution.py:694
  48.4 1.6 %collective-permute-start.17 = (bf16[4,2,72,384]{3,2,1,0:T(8,128)(2,1)S(1)}, bf16[4,2,72,384]{3,2,1,0:T(8,128)(2,1)S(1)}, u32[]{:S(2)}, u32[]{:S(2)}) collective-permute-start(bf16[4,2,72,384]{3,2,1,0:T(8,128)(2,1)S(1)} %get-tuple-element.134), channel_id=1, source_target_pairs={{0,8},{2,10},{4,12},{6,14},{8,0},{10,2},{12,4},{14,6},{16,24},{18,... | collective-permute-start | bytes 1327112 | tf_op jit(solution)/shard_map/ppermute | solution.py:694
  50.0 5.1 %attention_back.1 = (bf16[576,128]{1,0:T(8,128)(2,1)}, bf16[1,2,8,80,384]{4,3,2,1,0:T(8,128)(2,1)S(1)}, bf16[1,2,8,80,384]{4,3,2,1,0:T(8,128)(2,1)S(1)}, f32[8,128]{1,0:T(8,128)S(1)}) custom-call(s32[4]{0:T(128)S(1)} %copy-done, bf16[576,128]{1,0:T(8,128)(2,1)S(1)} %bitcast.67, f32[128,576]{1,0:T(8,128)S(1)} %get-tuple-element.130.refs_4_.refs_2_, ...), custom_call_target="tpu_custom_call" | custom-call | flops 20000000000 | tf_op jit(solution)/shard_map/attention_back/pallas_call | solution.py:150
  55.1 0.9 collective-permute-start.23
  56.0 3.9 %collective-permute-done.16 = bf16[2,4,72,384]{3,2,1,0:T(8,128)(2,1)S(1)} collective-permute-done((bf16[2,4,72,384]{3,2,1,0:T(8,128)(2,1)S(1)}, bf16[2,4,72,384]{3,2,1,0:T(8,128)(2,1)S(1)}, u32[]{:S(2)}, u32[]{:S(2)}) %collective-permute-start.16) | collective-permute-done | bytes 442400 | tf_op jit(solution)/shard_map/ppermute | solution.py:694
  60.4 1.6 %collective-permute-start.19 = (bf16[2,2,72,384]{3,2,1,0:T(8,128)(2,1)S(1)}, bf16[2,2,72,384]{3,2,1,0:T(8,128)(2,1)S(1)}, u32[]{:S(2)}, u32[]{:S(2)}) collective-permute-start(bf16[2,2,72,384]{3,2,1,0:T(8,128)(2,1)S(1)} %get-tuple-element.145), channel_id=1, source_target_pairs={{0,8},{2,10},{4,12},{6,14},{8,0},{10,2},{12,4},{14,6},{16,24},{18,... | collective-permute-start | bytes 663560 | tf_op jit(solution)/shard_map/ppermute | solution.py:694
  62.1 1.1 collective-permute-start.20
  64.2 2.1 %collective-permute-start.24 = (bf16[2,72,384]{2,1,0:T(8,128)(2,1)S(1)}, bf16[2,72,384]{2,1,0:T(8,128)(2,1)S(1)}, u32[]{:S(2)}, u32[]{:S(2)}) collective-permute-start(bf16[2,72,384]{2,1,0:T(8,128)(2,1)S(1)} %get-tuple-element.154), channel_id=1, source_target_pairs={{0,8},{2,10},{4,12},{6,14},{8,0},{10,2},{12,4},{14,6},{16,24},{18,... | collective-permute-start | bytes 331784 | tf_op jit(solution)/shard_map/ppermute | solution.py:694
  66.3 1.4 collective-permute-done.19.refs_1_
  67.7 0.8 collective-permute-done.20.refs_3_
  69.1 5.3 %collective-permute-done.22 = bf16[8,80,384]{2,1,0:T(8,128)(2,1)S(1)} collective-permute-done((bf16[8,80,384]{2,1,0:T(8,128)(2,1)S(1)}, bf16[8,80,384]{2,1,0:T(8,128)(2,1)S(1)}, u32[]{:S(2)}, u32[]{:S(2)}) %collective-permute-start.22) | collective-permute-done | bytes 491552 | tf_op jit(solution)/shard_map/ppermute | solution.py:694
  74.7 1.5 %collective-permute-start.26 = (bf16[4,80,384]{2,1,0:T(8,128)(2,1)S(1)}, bf16[4,80,384]{2,1,0:T(8,128)(2,1)S(1)}, u32[]{:S(2)}, u32[]{:S(2)}) collective-permute-start(bf16[4,80,384]{2,1,0:T(8,128)(2,1)S(1)} %get-tuple-element.158), channel_id=1, source_target_pairs={{0,4},{2,6},{4,0},{6,2},{8,12},{10,14},{12,8},{14,10},{16,20},{18,... | collective-permute-start | bytes 737288 | tf_op jit(solution)/shard_map/ppermute | solution.py:694
  76.7 2.6 %collective-permute-start.27 = (bf16[72,384]{1,0:T(8,128)(2,1)S(1)}, bf16[72,384]{1,0:T(8,128)(2,1)S(1)}, u32[]{:S(2)}, u32[]{:S(2)}) collective-permute-start(bf16[72,384]{1,0:T(8,128)(2,1)S(1)} %get-tuple-element.160), channel_id=1, source_target_pairs={{0,16},{2,18},{4,20},{6,22},{8,24},{10,26},{12,28},{14,30},{16,0},... | collective-permute-start | bytes 165896 | tf_op jit(solution)/shard_map/ppermute | solution.py:694
  79.3 5.3 %collective-permute-done.27.refs_5_ = bf16[72,384]{1,0:T(8,128)(2,1)S(1)} collective-permute-done((bf16[72,384]{1,0:T(8,128)(2,1)S(1)}, bf16[72,384]{1,0:T(8,128)(2,1)S(1)}, u32[]{:S(2)}, u32[]{:S(2)}) %collective-permute-start.27) | collective-permute-done | bytes 55328 | tf_op jit(solution)/shard_map/ppermute | solution.py:694
  85.3 5.7 %collective-permute-done.29.refs_4_ = bf16[2,80,384]{2,1,0:T(8,128)(2,1)S(1)} collective-permute-done((bf16[2,80,384]{2,1,0:T(8,128)(2,1)S(1)}, bf16[2,80,384]{2,1,0:T(8,128)(2,1)S(1)}, u32[]{:S(2)}, u32[]{:S(2)}) %collective-permute-start.29) | collective-permute-done | bytes 122912 | tf_op jit(solution)/shard_map/ppermute | solution.py:694
  91.0 3.4 %collective-permute-done.28.refs_2_ = bf16[3,72,384]{2,1,0:T(8,128)(2,1)S(1)} collective-permute-done((bf16[3,72,384]{2,1,0:T(8,128)(2,1)S(1)}, bf16[3,72,384]{2,1,0:T(8,128)(2,1)S(1)}, u32[]{:S(2)}, u32[]{:S(2)}) %collective-permute-start.28) | collective-permute-done | bytes 165920 | tf_op jit(solution)/shard_map/ppermute | solution.py:694
  94.5 1.5 %collective-permute-start.31 = (bf16[2,72,384]{2,1,0:T(8,128)(2,1)S(1)}, bf16[2,72,384]{2,1,0:T(8,128)(2,1)S(1)}, u32[]{:S(2)}, u32[]{:S(2)}) collective-permute-start(bf16[2,72,384]{2,1,0:T(8,128)(2,1)S(1)} %get-tuple-element.167.refs_3_), channel_id=1, source_target_pairs={{0,8},{2,10},{4,12},{6,14},{8,0},{10,2},{12,4},{14,6},{16,24},{18,... | collective-permute-start | bytes 331784 | tf_op jit(solution)/shard_map/ppermute | solution.py:694
  96.0 7.1 %collective-permute-done.31.refs_4_ = bf16[2,72,384]{2,1,0:T(8,128)(2,1)S(1)} collective-permute-done((bf16[2,72,384]{2,1,0:T(8,128)(2,1)S(1)}, bf16[2,72,384]{2,1,0:T(8,128)(2,1)S(1)}, u32[]{:S(2)}, u32[]{:S(2)}) %collective-permute-start.31) | collective-permute-done | bytes 110624 | tf_op jit(solution)/shard_map/ppermute | solution.py:694
  104.1 2.5 %collective-permute-start.34 = (bf16[2,72,384]{2,1,0:T(8,128)(2,1)S(1)}, bf16[2,72,384]{2,1,0:T(8,128)(2,1)S(1)}, u32[]{:S(2)}, u32[]{:S(2)}) collective-permute-start(bf16[2,72,384]{2,1,0:T(8,128)(2,1)S(1)} %get-tuple-element.171.refs_2_), channel_id=1, source_target_pairs={{0,8},{2,10},{4,12},{6,14},{8,0},{10,2},{12,4},{14,6},{16,24},{18,... | collective-permute-start | bytes 331784 | tf_op jit(solution)/shard_map/ppermute | solution.py:694
  106.6 1.5 %layer_output.1 = bf16[576,128]{1,0:T(8,128)(2,1)} custom-call(f32[128,576]{1,0:T(8,128)S(1)} %copy-done.24, bf16[128,1536]{1,0:T(8,128)(2,1)S(1)} %get-tuple-element.119.refs_1_, bf16[576,1536]{1,0:T(8,128)(2,1)S(1)} %get-tuple-element.122.refs_2_, bf16[3,2,72,384]{3,2,1,0:T(8,128)(2,1)S(1)} %get-tuple-element.168.refs_3_.refs_0_), custom_call_target="tpu_custom_call" | custom-call | flops 2000000000 | tf_op jit(solution)/shard_map/layer_output/pallas_call | solution.py:568
  108.1 1.4 %collective-permute-done.32.refs_4_.refs_1_ = bf16[80,384]{1,0:T(8,128)(2,1)S(1)} collective-permute-done((bf16[80,384]{1,0:T(8,128)(2,1)S(1)}, bf16[80,384]{1,0:T(8,128)(2,1)S(1)}, u32[]{:S(2)}, u32[]{:S(2)}) %collective-permute-start.32) | collective-permute-done | bytes 61472 | tf_op jit(solution)/shard_map/ppermute | solution.py:694
  109.5 0.9 collective-permute-done.34.refs_3_
  110.4 1.4 %collective-permute-done.33.refs_1_ = bf16[3,2,72,384]{3,2,1,0:T(8,128)(2,1)S(1)} collective-permute-done((bf16[3,2,72,384]{3,2,1,0:T(8,128)(2,1)S(1)}, bf16[3,2,72,384]{3,2,1,0:T(8,128)(2,1)S(1)}, u32[]{:S(2)}, u32[]{:S(2)}) %collective-permute-start.33) | collective-permute-done | bytes 331808 | tf_op jit(solution)/shard_map/ppermute | solution.py:694
  112.0 0.6 collective-permute-start.40
  112.8 2.5 %update_down_near.1 = (f32[576,768]{1,0:T(8,128)}, f32[576,768]{1,0:T(8,128)}, f32[576,768]{1,0:T(8,128)}, f32[8,128]{1,0:T(8,128)S(1)}) custom-call(s32[4]{0:T(128)S(1)} %copy-done, bf16[1,2,4,72,384]{4,3,2,1,0:T(8,128)(2,1)S(1)} %get-tuple-element.172.refs_0_, f32[576,768]{1,0:T(8,128)S(1)} %bitcast.48, f32[576,768]{1,0:T(8,128)S(1)} %bitcast.50, ...), custom_call_target="tpu_custom_call" | custom-call | flops 20000000000 | tf_op jit(solution)/shard_map/update_down_near/pallas_call | solution.py:676
  115.4 2.5 %update_down_far.1 = (f32[576,768]{1,0:T(8,128)}, f32[576,768]{1,0:T(8,128)}, f32[576,768]{1,0:T(8,128)}, f32[8,128]{1,0:T(8,128)S(1)}) custom-call(s32[4]{0:T(128)S(1)} %copy-done, bf16[1,2,4,72,384]{4,3,2,1,0:T(8,128)(2,1)S(1)} %collective-permute-done.35.refs_0_, ...), custom_call_target="tpu_custom_call", output_to_operand_aliasing={{0}: (5, {}), {1}: (6, {}), {2}: (7, {})} | custom-call | flops 20000000000 | tf_op jit(solution)/shard_map/update_down_far/pallas_call | solution.py:676
  117.9 2.8 %collective-permute-start.38 = (bf16[2,80,384]{2,1,0:T(8,128)(2,1)S(1)}, bf16[2,80,384]{2,1,0:T(8,128)(2,1)S(1)}, u32[]{:S(2)}, u32[]{:S(2)}) collective-permute-start(bf16[2,80,384]{2,1,0:T(8,128)(2,1)S(1)} %share_qkv_out_high.1.refs_4_.refs_0_), channel_id=1, source_target_pairs={{0,12},{2,14},{4,8},{6,10},{8,4},{10,6},{12,0},{14,2},{16,28},{18,... | collective-permute-start | bytes 368648 | tf_op jit(solution)/shard_map/ppermute | solution.py:694
  120.7 0.8 collective-permute-start.36
  121.7 3.7 %update_gate_up_near.1 = (f32[288,3072]{1,0:T(8,128)}, f32[288,3072]{1,0:T(8,128)}, f32[288,3072]{1,0:T(8,128)}, f32[8,128]{1,0:T(8,128)S(1)}) custom-call(s32[4]{0:T(128)S(1)} %copy-done, bf16[2,2,4,72,384]{4,3,2,1,0:T(8,128)(2,1)S(1)} %share_gate_up.1.refs_0_, f32[288,3072]{1,0:T(8,128)S(1)} %copy-done.1, f32[288,3072]{1,0:T(8,128)S(1)} %copy-done.2, ...), custom_call_target="tpu_custom_call" | custom-call | flops 20000000000 | tf_op jit(solution)/shard_map/update_gate_up_near/pallas_call | solution.py:676
  125.4 3.7 %update_gate_up_far.1 = (f32[288,3072]{1,0:T(8,128)}, f32[288,3072]{1,0:T(8,128)}, f32[288,3072]{1,0:T(8,128)}, f32[8,128]{1,0:T(8,128)S(1)}) custom-call(s32[4]{0:T(128)S(1)} %copy-done, bf16[2,2,4,72,384]{4,3,2,1,0:T(8,128)(2,1)S(1)} %collective-permute-done.41.refs_0_, ...), custom_call_target="tpu_custom_call", output_to_operand_aliasing={{0}: (5, {}), {1}: (6, {}), {2}: (7, {})} | custom-call | flops 20000000000 | tf_op jit(solution)/shard_map/update_gate_up_far/pallas_call | solution.py:676
  131.9 3.3 %update_qkv_out_near.1 = (f32[288,960]{1,0:T(8,128)}, f32[288,576]{1,0:T(8,128)}, f32[288,960]{1,0:T(8,128)}, f32[288,576]{1,0:T(8,128)}, f32[288,960]{1,0:T(8,1...) custom-call(s32[4]{0:T(128)S(1)} %copy-done, ...), custom_call_target="tpu_custom_call" | custom-call | flops 20000000000 | tf_op jit(solution)/shard_map/update_qkv_out_near/pallas_call | solution.py:676
  135.2 3.4 %update_qkv_out_far.1 = (f32[288,960]{1,0:T(8,128)}, f32[288,576]{1,0:T(8,128)}, f32[288,960]{1,0:T(8,128)}, f32[288,576]{1,0:T(8,128)}, f32[288,960]{1,0:T(8,12...) custom-call(s32[4]{0:T(128)S(1)} %copy-done, ...), custom_call_target="tpu_custom_call", output_to_operand_aliasing={{0}: (8, {}), {1}: (9, {}), {2}: (10, {}), {3}: (11, {}), {... | custom-call | flops 20000000000 | tf_op jit(solution)/shard_map/update_qkv_out_far/pallas_call | solution.py:676
  (121 shorter events, 11.5 us)
Async XLA Ops:
  1.2 20.2 %copy-start = (s32[4]{0:T(128)S(1)}, s32[4]{0:T(128)}, u32[]{:S(2)}) copy-start(s32[4]{0:T(128)} %pad_add_fusion.idx_ref.refs_0_) | copy-start | bytes 52
  1.3 20.2 %copy-start.4 = (f32[768,576]{0,1:T(8,128)S(1)}, f32[768,576]{0,1:T(8,128)}, u32[]{:S(2)}) copy-start(f32[768,576]{0,1:T(8,128)} %param.25) | copy-start | bytes 5308420
  4.4 16.9 %collective-permute-start = (bf16[160,768]{1,0:T(8,128)(2,1)}, bf16[160,768]{1,0:T(8,128)(2,1)S(1)}, u32[]{:S(2)}, u32[]{:S(2)}) collective-permute-start(bf16[160,768]{1,0:T(8,128)(2,1)} %get-tuple-element.112), channel_id=1, source_target_pairs={{0,1},{1,0},{2,3},{3,2},{4,5},{5,4},{6,7},{7,6},{8,9},{9,8},{10,11... | collective-permute-start | bytes 737288 | tf_op jit(solution)/shard_map/ppermute | solution.py:694
  7.5 11.7 %collective-permute-start.8 = (bf16[144,768]{1,0:T(8,128)(2,1)}, bf16[144,768]{1,0:T(8,128)(2,1)S(1)}, u32[]{:S(2)}, u32[]{:S(2)}) collective-permute-start(bf16[144,768]{1,0:T(8,128)(2,1)} %get-tuple-element.117), channel_id=1, source_target_pairs={{0,1},{1,0},{2,3},{3,2},{4,5},{5,4},{6,7},{7,6},{8,9},{9,8},{10,11... | collective-permute-start | bytes 663560 | tf_op jit(solution)/shard_map/ppermute | solution.py:694
  7.6 16.7 %collective-permute-start.4 = (bf16[144,768]{1,0:T(8,128)(2,1)}, bf16[144,768]{1,0:T(8,128)(2,1)S(1)}, u32[]{:S(2)}, u32[]{:S(2)}) collective-permute-start(bf16[144,768]{1,0:T(8,128)(2,1)} %get-tuple-element.116), channel_id=1, source_target_pairs={{0,1},{1,0},{2,3},{3,2},{4,5},{5,4},{6,7},{7,6},{8,9},{9,8},{10,11... | collective-permute-start | bytes 663560 | tf_op jit(solution)/shard_map/ppermute | solution.py:694
  19.2 7.9 %collective-permute-start.9 = (bf16[144,768]{1,0:T(8,128)(2,1)S(1)}, bf16[144,768]{1,0:T(8,128)(2,1)S(1)}, u32[]{:S(2)}, u32[]{:S(2)}) collective-permute-start(bf16[144,768]{1,0:T(8,128)(2,1)S(1)} %collective-permute-done.8.refs_11_.refs_1_), channel_id=1, source_target_pairs={{0,8},{2,10},{4,12},{6,14},{8,0},{10,2},{12,4},{14,6},{16,24},{18,... | collective-permute-start | bytes 663560 | tf_op jit(solution)/shard_map/ppermute | solution.py:694
  21.3 10.2 %collective-permute-start.2 = (bf16[160,768]{1,0:T(8,128)(2,1)S(1)}, bf16[160,768]{1,0:T(8,128)(2,1)S(1)}, u32[]{:S(2)}, u32[]{:S(2)}) collective-permute-start(bf16[160,768]{1,0:T(8,128)(2,1)S(1)} %collective-permute-done.refs_5_.refs_8_), channel_id=1, source_target_pairs={{0,2},{2,0},{4,6},{6,4},{8,10},{10,8},{12,14},{14,12},{16,18},{18,... | collective-permute-start | bytes 737288 | tf_op jit(solution)/shard_map/ppermute | solution.py:694
  21.3 9.2 %collective-permute-start.1 = (bf16[160,768]{1,0:T(8,128)(2,1)S(1)}, bf16[160,768]{1,0:T(8,128)(2,1)S(1)}, u32[]{:S(2)}, u32[]{:S(2)}) collective-permute-start(bf16[160,768]{1,0:T(8,128)(2,1)S(1)} %collective-permute-done.refs_5_.refs_8_), channel_id=1, source_target_pairs={{0,8},{2,10},{4,12},{6,14},{8,0},{10,2},{12,4},{14,6},{16,24},{18,... | collective-permute-start | bytes 737288 | tf_op jit(solution)/shard_map/ppermute | solution.py:694
  22.2 9.9 %copy-start.7 = (f32[288,960]{1,0:T(8,128)S(1)}, f32[288,960]{1,0:T(8,128)}, u32[]{:S(2)}) copy-start(f32[288,960]{1,0:T(8,128)} %refs_1_.9) | copy-start | bytes 3317764
  22.2 9.9 %copy-start.11 = (f32[288,576]{1,0:T(8,128)S(1)}, f32[288,576]{1,0:T(8,128)}, u32[]{:S(2)}) copy-start(f32[288,576]{1,0:T(8,128)} %refs_2_.11) | copy-start | bytes 1990660
  22.2 9.9 %copy-start.16 = (bf16[1,128,576]{1,2,0:T(8,128)(2,1)S(1)}, bf16[1,128,576]{1,2,0:T(8,128)(2,1)}, u32[]{:S(2)}) copy-start(bf16[1,128,576]{1,2,0:T(8,128)(2,1)} %param.19) | copy-start | bytes 442372
  22.3 12.6 %collective-permute-start.12 = (bf16[288,768]{1,0:T(8,128)(2,1)S(1)}, bf16[288,768]{1,0:T(8,128)(2,1)S(1)}, u32[]{:S(2)}, u32[]{:S(2)}) collective-permute-start(bf16[288,768]{1,0:T(8,128)(2,1)S(1)} %pack_down.1), channel_id=1, source_target_pairs={{0,1},{1,0},{2,3},{3,2},{4,5},{5,4},{6,7},{7,6},{8,9},{9,8},{10,11... | collective-permute-start | bytes 1327112 | tf_op jit(solution)/shard_map/ppermute | solution.py:694
  24.2 7.3 %collective-permute-start.5 = (bf16[144,768]{1,0:T(8,128)(2,1)S(1)}, bf16[144,768]{1,0:T(8,128)(2,1)S(1)}, u32[]{:S(2)}, u32[]{:S(2)}) collective-permute-start(bf16[144,768]{1,0:T(8,128)(2,1)S(1)} %collective-permute-done.4.refs_7_), channel_id=1, source_target_pairs={{0,4},{2,6},{4,0},{6,2},{8,12},{10,14},{12,8},{14,10},{16,20},{18,... | collective-permute-start | bytes 663560 | tf_op jit(solution)/shard_map/ppermute | solution.py:694
  27.2 4.9 %collective-permute-start.11 = (bf16[144,768]{1,0:T(8,128)(2,1)S(1)}, bf16[144,768]{1,0:T(8,128)(2,1)S(1)}, u32[]{:S(2)}, u32[]{:S(2)}) collective-permute-start(bf16[144,768]{1,0:T(8,128)(2,1)S(1)} %collective-permute-done.9.refs_12_), channel_id=1, source_target_pairs={{0,2},{2,0},{4,6},{6,4},{8,10},{10,8},{12,14},{14,12},{16,18},{18,... | collective-permute-start | bytes 663560 | tf_op jit(solution)/shard_map/ppermute | solution.py:694
  30.5 1.6 %collective-permute-start.3 = (bf16[160,768]{1,0:T(8,128)(2,1)S(1)}, bf16[160,768]{1,0:T(8,128)(2,1)S(1)}, u32[]{:S(2)}, u32[]{:S(2)}) collective-permute-start(bf16[160,768]{1,0:T(8,128)(2,1)S(1)} %collective-permute-done.1.refs_9_), channel_id=1, source_target_pairs={{0,2},{2,0},{4,6},{6,4},{8,10},{10,8},{12,14},{14,12},{16,18},{18,... | collective-permute-start | bytes 737288 | tf_op jit(solution)/shard_map/ppermute | solution.py:694
  31.5 3.8 %collective-permute-start.6 = (bf16[144,768]{1,0:T(8,128)(2,1)S(1)}, bf16[144,768]{1,0:T(8,128)(2,1)S(1)}, u32[]{:S(2)}, u32[]{:S(2)}) collective-permute-start(bf16[144,768]{1,0:T(8,128)(2,1)S(1)} %collective-permute-done.4.refs_7_), channel_id=1, source_target_pairs={{0,2},{2,0},{4,6},{6,4},{8,10},{10,8},{12,14},{14,12},{16,18},{18,... | collective-permute-start | bytes 663560 | tf_op jit(solution)/shard_map/ppermute | solution.py:694
  31.5 3.8 %collective-permute-start.10 = (bf16[144,768]{1,0:T(8,128)(2,1)S(1)}, bf16[144,768]{1,0:T(8,128)(2,1)S(1)}, u32[]{:S(2)}, u32[]{:S(2)}) collective-permute-start(bf16[144,768]{1,0:T(8,128)(2,1)S(1)} %collective-permute-done.8.refs_11_.refs_1_), channel_id=1, source_target_pairs={{0,2},{2,0},{4,6},{6,4},{8,10},{10,8},{12,14},{14,12},{16,18},{18,... | collective-permute-start | bytes 663560 | tf_op jit(solution)/shard_map/ppermute | solution.py:694
  32.0 3.3 %collective-permute-start.7 = (bf16[144,768]{1,0:T(8,128)(2,1)S(1)}, bf16[144,768]{1,0:T(8,128)(2,1)S(1)}, u32[]{:S(2)}, u32[]{:S(2)}) collective-permute-start(bf16[144,768]{1,0:T(8,128)(2,1)S(1)} %collective-permute-done.5.refs_8_), channel_id=1, source_target_pairs={{0,2},{2,0},{4,6},{6,4},{8,10},{10,8},{12,14},{14,12},{16,18},{18,... | collective-permute-start | bytes 663560 | tf_op jit(solution)/shard_map/ppermute | solution.py:694
  34.9 3.5 %collective-permute-start.13 = (bf16[288,768]{1,0:T(8,128)(2,1)S(1)}, bf16[288,768]{1,0:T(8,128)(2,1)S(1)}, u32[]{:S(2)}, u32[]{:S(2)}) collective-permute-start(bf16[288,768]{1,0:T(8,128)(2,1)S(1)} %pass_on.1.refs_5_), channel_id=1, source_target_pairs={{0,2},{2,0},{4,6},{6,4},{8,10},{10,8},{12,14},{14,12},{16,18},{18,... | collective-permute-start | bytes 1327112 | tf_op jit(solution)/shard_map/ppermute | solution.py:694
  38.2 3.5 %collective-permute-start.15 = (bf16[1,2,8,72,384]{4,3,2,1,0:T(8,128)(2,1)S(1)}, bf16[1,2,8,72,384]{4,3,2,1,0:T(8,128)(2,1)S(1)}, u32[]{:S(2)}, u32[]{:S(2)}) collective-permute-start(bf16[1,2,8,72,384]{4,3,2,1,0:T(8,128)(2,1)S(1)} %get-tuple-element.128), channel_id=1, source_target_pairs={{0,2},{2,0},{4,6},{6,4},{8,10},{10,8},{12,14},{14,12},{16,18},{18,... | collective-permute-start | bytes 2654216 | tf_op jit(solution)/shard_map/ppermute | solution.py:694
  41.0 5.2 %collective-permute-start.14 = (bf16[2,2,8,72,384]{4,3,2,1,0:T(8,128)(2,1)S(1)}, bf16[2,2,8,72,384]{4,3,2,1,0:T(8,128)(2,1)S(1)}, u32[]{:S(2)}, u32[]{:S(2)}) collective-permute-start(bf16[2,2,8,72,384]{4,3,2,1,0:T(8,128)(2,1)S(1)} %get-tuple-element.124), channel_id=1, source_target_pairs={{0,2},{2,0},{4,6},{6,4},{8,10},{10,8},{12,14},{14,12},{16,18},{18,... | collective-permute-start | bytes 5308424 | tf_op jit(solution)/shard_map/ppermute | solution.py:694
  41.9 13.2 %collective-permute-start.18 = (bf16[8,72,384]{2,1,0:T(8,128)(2,1)S(1)}, bf16[8,72,384]{2,1,0:T(8,128)(2,1)S(1)}, u32[]{:S(2)}, u32[]{:S(2)}) collective-permute-start(bf16[8,72,384]{2,1,0:T(8,128)(2,1)S(1)} %get-tuple-element.135), channel_id=1, source_target_pairs={{0,1},{1,0},{2,3},{3,2},{4,5},{5,4},{6,7},{7,6},{8,9},{9,8},{10,11... | collective-permute-start | bytes 1327112 | tf_op jit(solution)/shard_map/ppermute | solution.py:694
  46.8 13.1 %collective-permute-start.16 = (bf16[2,4,72,384]{3,2,1,0:T(8,128)(2,1)S(1)}, bf16[2,4,72,384]{3,2,1,0:T(8,128)(2,1)S(1)}, u32[]{:S(2)}, u32[]{:S(2)}) collective-permute-start(bf16[2,4,72,384]{3,2,1,0:T(8,128)(2,1)S(1)} %get-tuple-element.132), channel_id=1, source_target_pairs={{0,4},{2,6},{4,0},{6,2},{8,12},{10,14},{12,8},{14,10},{16,20},{18,... | collective-permute-start | bytes 1327112 | tf_op jit(solution)/shard_map/ppermute | solution.py:694
  48.4 11.9 %collective-permute-start.17 = (bf16[4,2,72,384]{3,2,1,0:T(8,128)(2,1)S(1)}, bf16[4,2,72,384]{3,2,1,0:T(8,128)(2,1)S(1)}, u32[]{:S(2)}, u32[]{:S(2)}) collective-permute-start(bf16[4,2,72,384]{3,2,1,0:T(8,128)(2,1)S(1)} %get-tuple-element.134), channel_id=1, source_target_pairs={{0,8},{2,10},{4,12},{6,14},{8,0},{10,2},{12,4},{14,6},{16,24},{18,... | collective-permute-start | bytes 1327112 | tf_op jit(solution)/shard_map/ppermute | solution.py:694
  55.1 9.1 %collective-permute-start.23 = (bf16[4,72,384]{2,1,0:T(8,128)(2,1)S(1)}, bf16[4,72,384]{2,1,0:T(8,128)(2,1)S(1)}, u32[]{:S(2)}, u32[]{:S(2)}) collective-permute-start(bf16[4,72,384]{2,1,0:T(8,128)(2,1)S(1)} %get-tuple-element.152), channel_id=1, source_target_pairs={{0,4},{2,6},{4,0},{6,2},{8,12},{10,14},{12,8},{14,10},{16,20},{18,... | collective-permute-start | bytes 663560 | tf_op jit(solution)/shard_map/ppermute | solution.py:694
  56.0 7.2 %collective-permute-start.21 = (bf16[1,2,8,80,384]{4,3,2,1,0:T(8,128)(2,1)S(1)}, bf16[1,2,8,80,384]{4,3,2,1,0:T(8,128)(2,1)S(1)}, u32[]{:S(2)}, u32[]{:S(2)}) collective-permute-start(bf16[1,2,8,80,384]{4,3,2,1,0:T(8,128)(2,1)S(1)} %get-tuple-element.149), channel_id=1, source_target_pairs={{0,2},{2,0},{4,6},{6,4},{8,10},{10,8},{12,14},{14,12},{16,18},{18,... | collective-permute-start | bytes 2949128 | tf_op jit(solution)/shard_map/ppermute | solution.py:694
  60.4 7.3 %collective-permute-start.19 = (bf16[2,2,72,384]{3,2,1,0:T(8,128)(2,1)S(1)}, bf16[2,2,72,384]{3,2,1,0:T(8,128)(2,1)S(1)}, u32[]{:S(2)}, u32[]{:S(2)}) collective-permute-start(bf16[2,2,72,384]{3,2,1,0:T(8,128)(2,1)S(1)} %get-tuple-element.145), channel_id=1, source_target_pairs={{0,8},{2,10},{4,12},{6,14},{8,0},{10,2},{12,4},{14,6},{16,24},{18,... | collective-permute-start | bytes 663560 | tf_op jit(solution)/shard_map/ppermute | solution.py:694
  62.1 6.5 %collective-permute-start.20 = (bf16[2,2,72,384]{3,2,1,0:T(8,128)(2,1)S(1)}, bf16[2,2,72,384]{3,2,1,0:T(8,128)(2,1)S(1)}, u32[]{:S(2)}, u32[]{:S(2)}) collective-permute-start(bf16[2,2,72,384]{3,2,1,0:T(8,128)(2,1)S(1)} %get-tuple-element.147), channel_id=1, source_target_pairs={{0,4},{2,6},{4,0},{6,2},{8,12},{10,14},{12,8},{14,10},{16,20},{18,... | collective-permute-start | bytes 663560 | tf_op jit(solution)/shard_map/ppermute | solution.py:694
  63.4 11.0 %collective-permute-start.22 = (bf16[8,80,384]{2,1,0:T(8,128)(2,1)S(1)}, bf16[8,80,384]{2,1,0:T(8,128)(2,1)S(1)}, u32[]{:S(2)}, u32[]{:S(2)}) collective-permute-start(bf16[8,80,384]{2,1,0:T(8,128)(2,1)S(1)} %get-tuple-element.151), channel_id=1, source_target_pairs={{0,1},{1,0},{2,3},{3,2},{4,5},{5,4},{6,7},{7,6},{8,9},{9,8},{10,11... | collective-permute-start | bytes 1474568 | tf_op jit(solution)/shard_map/ppermute | solution.py:694
  64.2 4.9 %collective-permute-start.24 = (bf16[2,72,384]{2,1,0:T(8,128)(2,1)S(1)}, bf16[2,72,384]{2,1,0:T(8,128)(2,1)S(1)}, u32[]{:S(2)}, u32[]{:S(2)}) collective-permute-start(bf16[2,72,384]{2,1,0:T(8,128)(2,1)S(1)} %get-tuple-element.154), channel_id=1, source_target_pairs={{0,8},{2,10},{4,12},{6,14},{8,0},{10,2},{12,4},{14,6},{16,24},{18,... | collective-permute-start | bytes 331784 | tf_op jit(solution)/shard_map/ppermute | solution.py:694
  74.7 9.9 %collective-permute-start.26 = (bf16[4,80,384]{2,1,0:T(8,128)(2,1)S(1)}, bf16[4,80,384]{2,1,0:T(8,128)(2,1)S(1)}, u32[]{:S(2)}, u32[]{:S(2)}) collective-permute-start(bf16[4,80,384]{2,1,0:T(8,128)(2,1)S(1)} %get-tuple-element.158), channel_id=1, source_target_pairs={{0,4},{2,6},{4,0},{6,2},{8,12},{10,14},{12,8},{14,10},{16,20},{18,... | collective-permute-start | bytes 737288 | tf_op jit(solution)/shard_map/ppermute | solution.py:694
  76.2 8.4 %collective-permute-start.25 = (bf16[2,2,72,384]{3,2,1,0:T(8,128)(2,1)S(1)}, bf16[2,2,72,384]{3,2,1,0:T(8,128)(2,1)S(1)}, u32[]{:S(2)}, u32[]{:S(2)}) collective-permute-start(bf16[2,2,72,384]{3,2,1,0:T(8,128)(2,1)S(1)} %get-tuple-element.156), channel_id=1, source_target_pairs={{0,1},{1,0},{2,3},{3,2},{4,5},{5,4},{6,7},{7,6},{8,9},{9,8},{10,11... | collective-permute-start | bytes 663560 | tf_op jit(solution)/shard_map/ppermute | solution.py:694
  76.7 7.9 %collective-permute-start.27 = (bf16[72,384]{1,0:T(8,128)(2,1)S(1)}, bf16[72,384]{1,0:T(8,128)(2,1)S(1)}, u32[]{:S(2)}, u32[]{:S(2)}) collective-permute-start(bf16[72,384]{1,0:T(8,128)(2,1)S(1)} %get-tuple-element.160), channel_id=1, source_target_pairs={{0,16},{2,18},{4,20},{6,22},{8,24},{10,26},{12,28},{14,30},{16,0},... | collective-permute-start | bytes 165896 | tf_op jit(solution)/shard_map/ppermute | solution.py:694
  84.7 9.7 %collective-permute-start.28 = (bf16[3,72,384]{2,1,0:T(8,128)(2,1)S(1)}, bf16[3,72,384]{2,1,0:T(8,128)(2,1)S(1)}, u32[]{:S(2)}, u32[]{:S(2)}) collective-permute-start(bf16[3,72,384]{2,1,0:T(8,128)(2,1)S(1)} %get-tuple-element.161.refs_0_), channel_id=1, source_target_pairs={{0,16},{2,18},{4,20},{6,22},{8,24},{10,26},{12,28},{14,30},{16,0},... | collective-permute-start | bytes 497672 | tf_op jit(solution)/shard_map/ppermute | solution.py:694
  84.9 6.2 %collective-permute-start.29 = (bf16[2,80,384]{2,1,0:T(8,128)(2,1)S(1)}, bf16[2,80,384]{2,1,0:T(8,128)(2,1)S(1)}, u32[]{:S(2)}, u32[]{:S(2)}) collective-permute-start(bf16[2,80,384]{2,1,0:T(8,128)(2,1)S(1)} %get-tuple-element.164), channel_id=1, source_target_pairs={{0,8},{2,10},{4,12},{6,14},{8,0},{10,2},{12,4},{14,6},{16,24},{18,... | collective-permute-start | bytes 368648 | tf_op jit(solution)/shard_map/ppermute | solution.py:694
  94.5 8.7 %collective-permute-start.30 = (bf16[3,80,384]{2,1,0:T(8,128)(2,1)S(1)}, bf16[3,80,384]{2,1,0:T(8,128)(2,1)S(1)}, u32[]{:S(2)}, u32[]{:S(2)}) collective-permute-start(bf16[3,80,384]{2,1,0:T(8,128)(2,1)S(1)} %get-tuple-element.165.refs_0_), channel_id=1, source_target_pairs={{0,16},{2,18},{4,20},{6,22},{8,24},{10,26},{12,28},{14,30},{16,0},... | collective-permute-start | bytes 552968 | tf_op jit(solution)/shard_map/ppermute | solution.py:694
  94.5 8.6 %collective-permute-start.31 = (bf16[2,72,384]{2,1,0:T(8,128)(2,1)S(1)}, bf16[2,72,384]{2,1,0:T(8,128)(2,1)S(1)}, u32[]{:S(2)}, u32[]{:S(2)}) collective-permute-start(bf16[2,72,384]{2,1,0:T(8,128)(2,1)S(1)} %get-tuple-element.167.refs_3_), channel_id=1, source_target_pairs={{0,8},{2,10},{4,12},{6,14},{8,0},{10,2},{12,4},{14,6},{16,24},{18,... | collective-permute-start | bytes 331784 | tf_op jit(solution)/shard_map/ppermute | solution.py:694
  103.2 8.7 %collective-permute-start.33 = (bf16[3,2,72,384]{3,2,1,0:T(8,128)(2,1)S(1)}, bf16[3,2,72,384]{3,2,1,0:T(8,128)(2,1)S(1)}, u32[]{:S(2)}, u32[]{:S(2)}) collective-permute-start(bf16[3,2,72,384]{3,2,1,0:T(8,128)(2,1)S(1)} %get-tuple-element.168.refs_3_.refs_0_), channel_id=1, source_target_pairs={{0,4},{2,6},{4,0},{6,2},{8,12},{10,14},{12,8},{14,10},{16,20},{18,... | collective-permute-start | bytes 995336 | tf_op jit(solution)/shard_map/ppermute | solution.py:694
  103.7 5.8 %collective-permute-start.32 = (bf16[80,384]{1,0:T(8,128)(2,1)S(1)}, bf16[80,384]{1,0:T(8,128)(2,1)S(1)}, u32[]{:S(2)}, u32[]{:S(2)}) collective-permute-start(bf16[80,384]{1,0:T(8,128)(2,1)S(1)} %get-tuple-element.170.refs_0_), channel_id=1, source_target_pairs={{0,16},{2,18},{4,20},{6,22},{8,24},{10,26},{12,28},{14,30},{16,0},... | collective-permute-start | bytes 184328 | tf_op jit(solution)/shard_map/ppermute | solution.py:694
  104.1 6.3 %collective-permute-start.34 = (bf16[2,72,384]{2,1,0:T(8,128)(2,1)S(1)}, bf16[2,72,384]{2,1,0:T(8,128)(2,1)S(1)}, u32[]{:S(2)}, u32[]{:S(2)}) collective-permute-start(bf16[2,72,384]{2,1,0:T(8,128)(2,1)S(1)} %get-tuple-element.171.refs_2_), channel_id=1, source_target_pairs={{0,8},{2,10},{4,12},{6,14},{8,0},{10,2},{12,4},{14,6},{16,24},{18,... | collective-permute-start | bytes 331784 | tf_op jit(solution)/shard_map/ppermute | solution.py:694
  112.0 9.6 %collective-permute-start.40 = (bf16[2,2,72,384]{3,2,1,0:T(8,128)(2,1)S(1)}, bf16[2,2,72,384]{3,2,1,0:T(8,128)(2,1)S(1)}, u32[]{:S(2)}, u32[]{:S(2)}) collective-permute-start(bf16[2,2,72,384]{3,2,1,0:T(8,128)(2,1)S(1)} %get-tuple-element.179.refs_2_), channel_id=1, source_target_pairs={{0,4},{2,6},{4,0},{6,2},{8,12},{10,14},{12,8},{14,10},{16,20},{18,... | collective-permute-start | bytes 663560 | tf_op jit(solution)/shard_map/ppermute | solution.py:694
  112.6 8.9 %collective-permute-start.39 = (bf16[2,2,72,384]{3,2,1,0:T(8,128)(2,1)S(1)}, bf16[2,2,72,384]{3,2,1,0:T(8,128)(2,1)S(1)}, u32[]{:S(2)}, u32[]{:S(2)}) collective-permute-start(bf16[2,2,72,384]{3,2,1,0:T(8,128)(2,1)S(1)} %get-tuple-element.173.refs_4_.refs_0_), channel_id=1, source_target_pairs={{0,8},{2,10},{4,12},{6,14},{8,0},{10,2},{12,4},{14,6},{16,24},{18,... | collective-permute-start | bytes 663560 | tf_op jit(solution)/shard_map/ppermute | solution.py:694
  112.8 2.5 %collective-permute-start.35 = (bf16[1,2,4,72,384]{4,3,2,1,0:T(8,128)(2,1)S(1)}, bf16[1,2,4,72,384]{4,3,2,1,0:T(8,128)(2,1)S(1)}, u32[]{:S(2)}, u32[]{:S(2)}) collective-permute-start(bf16[1,2,4,72,384]{4,3,2,1,0:T(8,128)(2,1)S(1)} %get-tuple-element.172.refs_0_), channel_id=1, source_target_pairs={{0,2},{2,0},{4,6},{6,4},{8,10},{10,8},{12,14},{14,12},{16,18},{18,... | collective-permute-start | bytes 1327112 | tf_op jit(solution)/shard_map/ppermute | solution.py:694
  117.9 11.3 %collective-permute-start.38 = (bf16[2,80,384]{2,1,0:T(8,128)(2,1)S(1)}, bf16[2,80,384]{2,1,0:T(8,128)(2,1)S(1)}, u32[]{:S(2)}, u32[]{:S(2)}) collective-permute-start(bf16[2,80,384]{2,1,0:T(8,128)(2,1)S(1)} %share_qkv_out_high.1.refs_4_.refs_0_), channel_id=1, source_target_pairs={{0,12},{2,14},{4,8},{6,10},{8,4},{10,6},{12,0},{14,2},{16,28},{18,... | collective-permute-start | bytes 368648 | tf_op jit(solution)/shard_map/ppermute | solution.py:694
  120.7 8.5 %collective-permute-start.37 = (bf16[2,80,384]{2,1,0:T(8,128)(2,1)S(1)}, bf16[2,80,384]{2,1,0:T(8,128)(2,1)S(1)}, u32[]{:S(2)}, u32[]{:S(2)}) collective-permute-start(bf16[2,80,384]{2,1,0:T(8,128)(2,1)S(1)} %share_qkv_out_high.1.refs_4_.refs_0_), channel_id=1, source_target_pairs={{0,8},{2,10},{4,12},{6,14},{8,0},{10,2},{12,4},{14,6},{16,24},{18,... | collective-permute-start | bytes 368648 | tf_op jit(solution)/shard_map/ppermute | solution.py:694
  120.7 8.5 %collective-permute-start.36 = (bf16[2,80,384]{2,1,0:T(8,128)(2,1)S(1)}, bf16[2,80,384]{2,1,0:T(8,128)(2,1)S(1)}, u32[]{:S(2)}, u32[]{:S(2)}) collective-permute-start(bf16[2,80,384]{2,1,0:T(8,128)(2,1)S(1)} %share_qkv_out_high.1.refs_4_.refs_0_), channel_id=1, source_target_pairs={{0,4},{2,6},{4,0},{6,2},{8,12},{10,14},{12,8},{14,10},{16,20},{18,... | collective-permute-start | bytes 368648 | tf_op jit(solution)/shard_map/ppermute | solution.py:694
  121.6 3.8 %collective-permute-start.41 = (bf16[2,2,4,72,384]{4,3,2,1,0:T(8,128)(2,1)S(1)}, bf16[2,2,4,72,384]{4,3,2,1,0:T(8,128)(2,1)S(1)}, u32[]{:S(2)}, u32[]{:S(2)}) collective-permute-start(bf16[2,2,4,72,384]{4,3,2,1,0:T(8,128)(2,1)S(1)} %share_gate_up.1.refs_0_), channel_id=1, source_target_pairs={{0,2},{2,0},{4,6},{6,4},{8,10},{10,8},{12,14},{14,12},{16,18},{18,... | collective-permute-start | bytes 2654216 | tf_op jit(solution)/shard_map/ppermute | solution.py:694
  129.4 5.8 %collective-permute-start.42 = (bf16[1,2,4,80,384]{4,3,2,1,0:T(8,128)(2,1)S(1)}, bf16[1,2,4,80,384]{4,3,2,1,0:T(8,128)(2,1)S(1)}, u32[]{:S(2)}, u32[]{:S(2)}) collective-permute-start(bf16[1,2,4,80,384]{4,3,2,1,0:T(8,128)(2,1)S(1)} %share_qkv_out.1.refs_0_), channel_id=1, source_target_pairs={{0,2},{2,0},{4,6},{6,4},{8,10},{10,8},{12,14},{14,12},{16,18},{18,... | collective-permute-start | bytes 1474568 | tf_op jit(solution)/shard_map/ppermute | solution.py:694
  (20 other events, 81.5 us)

commit v9 on v8

--- a/solution.py
+++ b/solution.py
@@ -30,7 +30,7 @@
 MASKED = -1e30
 SCALE = float(HEAD) ** (-0.5)
 VMEM_LIMIT = 32 * 1024 * 1024
-PACK_LIMIT = 60 * 1024 * 1024
+PACK_LIMIT = 53 * 1024 * 1024
 HALF = 144
 CUT_ROWS = 72
 MARK = (8, 128)
@@ -603,68 +603,73 @@
     return [(flat[2 * i], flat[2 * i + 1]) for i in range(len(jobs))]
 
 
-def update_half(idx, far, pieces, place, height, state, earlier, gains, name, after):
+def update_rows(idx, shares, place, height, chunk, state, earlier, gains, name, after, busy=20):
     count = len(state) // 3
     columns = [a.shape[1] for a in state[:count]]
     starts = [sum(-(-c // LANES) * LANES for c in columns[:k]) for k in range(count + 1)]
-    chunks = height // CUT_ROWS
+    chunks = height // chunk
     order = [(k, count + k, 2 * count + k) for k in range(count)]
 
     def kernel(idx_ref, *refs):
         refs = list(refs)
         take = lambda n: [refs.pop(0) for _ in range(n)]
-        (piece_ref,) = take(1)
+        share_refs = take(len(shares))
         state_refs, gain_refs = take(3 * count), take(len(gains))
         take(len(earlier) + len(after))
         outs, gain_outs, (mark,) = take(3 * count), take(len(gains)), take(1)
         buffers, (full, sem) = take(3 * count), refs
         mark[...] = jnp.zeros_like(mark)
-        for part in range(pieces.shape[0]):
-            for x in range(2):
-                for z in range(4):
-                    rel = z ^ idx_ref[3]
-                    slot = ((rel & 1) << 1) | (rel >> 1)
-                    piece = piece_ref[part, x, slot].astype(F32)[:CUT_ROWS]
-                    row, cuts = place(part, idx_ref[2] ^ x, z)
-                    rows = pl.ds(pl.multiple_of(row, 8), CUT_ROWS)
-                    for begin, size, to in cuts:
-                        if isinstance(to, int):
-                            where = slice(to, to + size)
-                        else:
-                            where = pl.ds(pl.multiple_of(to, LANES), size)
-                        full[rows, where] = piece[:, begin : begin + size]
-        base = (idx_ref[1] ^ far) * height
         copies = []
-        for chunk in range(chunks):
-
-            def eight_rows(i, carry, chunk=chunk):
-                near_rows = pl.ds(pl.multiple_of(chunk * CUT_ROWS + i * 8, 8), 8)
-                rows = pl.ds(pl.multiple_of(base + chunk * CUT_ROWS + i * 8, 8), 8)
-                for k in range(count):
-                    for at in range(0, columns[k], 768):
-                        size = min(768, columns[k] - at)
-                        where = slice(at, at + size)
-                        results = adamw_rows(
-                            *[state_refs[j][rows, where] for j in order[k]],
-                            full[near_rows, starts[k] + at : starts[k] + at + size],
-                            RATE_MATRIX,
-                            DECAY_MATRIX,
-                        )
-                        for j, result in zip(order[k], results):
-                            buffers[j][near_rows, where] = result
-                return carry
-
-            lax.fori_loop(0, CUT_ROWS // 8, eight_rows, 0)
-            near_rows = pl.ds(chunk * CUT_ROWS, CUT_ROWS)
-            rows = pl.ds(pl.multiple_of(base + chunk * CUT_ROWS, 8), CUT_ROWS)
-            for j in range(3 * count):
-                copy = pltpu.make_async_copy(
-                    buffers[j].at[near_rows], outs[j].at[rows], sem.at[chunk, j]
-                )
-                copy.start()
-                copies.append(copy)
+        for share, (far, _) in enumerate(shares):
+            piece_ref = share_refs[share]
+            for part in range(piece_ref.shape[0]):
+                for x in range(2):
+                    for z in range(4):
+                        rel = z ^ idx_ref[3]
+                        slot = ((rel & 1) << 1) | (rel >> 1)
+                        piece = piece_ref[part, x, slot].astype(F32)[:CUT_ROWS]
+                        row, cuts = place(part, idx_ref[2] ^ x, z)
+                        rows = pl.ds(pl.multiple_of(share * height + row, 8), CUT_ROWS)
+                        for begin, size, to in cuts:
+                            if isinstance(to, int):
+                                where = slice(to, to + size)
+                            else:
+                                where = pl.ds(pl.multiple_of(to, LANES), size)
+                            full[rows, where] = piece[:, begin : begin + size]
+            base = (idx_ref[1] ^ far) * height
+            for at_chunk in range(chunks):
+
+                def eight_rows(i, carry, at_chunk=at_chunk, share=share, base=base):
+                    at_row = at_chunk * chunk + i * 8
+                    near_rows = pl.ds(pl.multiple_of(share * height + at_row, 8), 8)
+                    rows = pl.ds(pl.multiple_of(base + at_row, 8), 8)
+                    for k in range(count):
+                        for at in range(0, columns[k], 768):
+                            size = min(768, columns[k] - at)
+                            where = slice(at, at + size)
+                            results = adamw_rows(
+                                *[state_refs[j][rows, where] for j in order[k]],
+                                full[near_rows, starts[k] + at : starts[k] + at + size],
+                                RATE_MATRIX,
+                                DECAY_MATRIX,
+                            )
+                            for j, result in zip(order[k], results):
+                                buffers[j][near_rows, where] = result
+                    return carry
+
+                lax.fori_loop(0, chunk // 8, eight_rows, 0, unroll=3)
+                near_rows = pl.ds(share * height + at_chunk * chunk, chunk)
+                rows = pl.ds(pl.multiple_of(base + at_chunk * chunk, 8), chunk)
+                for j in range(3 * count):
+                    copy = pltpu.make_async_copy(
+                        buffers[j].at[near_rows],
+                        outs[j].at[rows],
+                        sem.at[share * chunks + at_chunk, j],
+                    )
+                    copy.start()
+                    copies.append(copy)
         if gains:
-            gradient = piece_ref[0, 0, 0, CUT_ROWS:, :].astype(F32)[:2, : gains[0].shape[1]]
+            gradient = share_refs[0][0, 0, 0, CUT_ROWS:, :].astype(F32)[:2, : gains[0].shape[1]]
             results = adamw_rows(*[g[...] for g in gain_refs], gradient, RATE_GAIN, 0.0)
             for out, result in zip(gain_outs, results):
                 out[...] = result
@@ -672,21 +677,23 @@
             copy.wait()
 
     vmem, anywhere = pl.BlockSpec(memory_space=pltpu.VMEM), pl.BlockSpec(memory_space=pl.ANY)
-    first_earlier = 2 + 3 * count + len(gains)
+    first_earlier = 1 + len(shares) + 3 * count + len(gains)
+    total = len(shares) * height
     return pl.pallas_call(
         kernel,
         out_shape=tuple(sds(a.shape, F32) for a in [*state, *gains]) + (sds(MARK, F32),),
         in_specs=[pl.BlockSpec(memory_space=pltpu.SMEM)]
-        + [vmem] * (1 + 3 * count + len(gains))
+        + [vmem] * (len(shares) + 3 * count + len(gains))
         + [anywhere] * (len(earlier) + len(after)),
         out_specs=tuple([anywhere] * (3 * count) + [vmem] * (len(gains) + 1)),
-        scratch_shapes=[pltpu.VMEM((height, a.shape[1]), F32) for a in state]
-        + [pltpu.VMEM((height, starts[-1]), F32), pltpu.SemaphoreType.DMA((chunks, 3 * count))],
+        scratch_shapes=[pltpu.VMEM((total, a.shape[1]), F32) for a in state]
+        + [pltpu.VMEM((total, starts[-1]), F32)]
+        + [pltpu.SemaphoreType.DMA((len(shares) * chunks, 3 * count))],
         input_output_aliases={first_earlier + i: i for i in range(len(earlier))},
         compiler_params=pltpu.CompilerParams(vmem_limit_bytes=VMEM_LIMIT),
-        cost_estimate=busy_for(20),
+        cost_estimate=busy_for(busy),
         name=name,
-    )(idx, pieces, *state, *gains, *earlier, *after)
+    )(idx, *[p for _, p in shares], *state, *gains, *earlier, *after)
 
 
 def swap(values, axis, mask):
@@ -884,16 +891,20 @@
         arrived_down = over_z_low(send)
 
         def columns(ins, outs):
-            for part in range(2):
-                total = ins[2 * part][...] + ins[2 * part + 1][...].astype(F32)
-                outs[0][part] = total[1].astype(BF16)
-                outs[1][part] = total[0]
-            for i in (1, 2):
-                total = ins[2 * i + 2][...] + ins[2 * i + 3][...].astype(F32)
-                outs[2 * i][...] = total[1].astype(BF16)
-                outs[2 * i + 1][...] = total[0]
-
-        send, keep, send_qkv_out, keep_qkv_out, send_down, keep_down = step(
+            total = ins[0][...] + ins[1][...].astype(F32)
+            outs[0][...] = total[1].astype(BF16)
+            outs[1][...] = total[0]
+            total = ins[2][...] + ins[3][...].astype(F32)
+            outs[2][0], outs[2][1] = total[0, 1].astype(BF16), total[1, 1].astype(BF16)
+            outs[3][...] = total[:, 0]
+            total = ins[4][...] + ins[5][...].astype(F32)
+            outs[4][...] = total[1].astype(BF16)
+            outs[5][...] = total[0]
+            total = ins[6][...] + ins[7][...].astype(F32)
+            outs[2][2] = total[1].astype(BF16)
+            outs[6][...] = total[0]
+
+        send_up, keep_up, send, keep_low, send_qkv_out, keep_qkv_out, keep_down = step(
             columns,
             [
                 *(keep_up, arrived_up, keep_low, arrived_low),
@@ -901,54 +912,57 @@
                 *(keep_down, arrived_down),
             ],
             [
-                *(sds((2, 2, *piece), BF16), sds((2, 2, *piece), F32)),
+                *(sds((2, *piece), BF16), sds((2, *piece), F32)),
+                *(sds((3, *piece), BF16), sds((2, *piece), F32)),
                 *(sds((4, *taller), BF16), sds((4, *taller), F32)),
-                *(sds(piece, BF16), sds(piece, F32)),
+                sds(piece, F32),
             ],
             "columns",
         )
-        arrived, arrived_qkv_out = over_y(send), over_x(send_qkv_out)
-        arrived_down = over_z_high(send_down)
+        arrived_up, arrived_qkv_out = over_y(send_up), over_x(send_qkv_out)
+        arrived = over_z_high(send)
 
         def planes(ins, outs):
-            for part in range(2):
-                total = ins[0][part] + ins[1][part].astype(F32)
-                outs[0][part] = total[1].astype(BF16)
-                outs[1][part] = total[0]
-            outs[0][2] = (ins[4][...] + ins[5][...].astype(F32)).astype(BF16)
-            total = ins[2][...] + ins[3][...].astype(F32)
-            outs[2][...] = total[1].astype(BF16)
-            outs[3][...] = total[0]
-
-        send, keep, send_qkv_out, keep_qkv_out = step(
+            keep_up, arrived_up, keep_low, arrived, keep_down, keep_qkv_out, arrived_qkv_out = ins
+            total = keep_up[...] + arrived_up[...].astype(F32)
+            outs[0][0] = total[1].astype(BF16)
+            outs[1][0] = total[0]
+            outs[0][1] = (keep_down[...] + arrived[2].astype(F32)).astype(BF16)
+            outs[2][...] = (keep_low[1] + arrived[1].astype(F32)).astype(BF16)
+            outs[1][1] = keep_low[0] + arrived[0].astype(F32)
+            total = keep_qkv_out[...] + arrived_qkv_out[...].astype(F32)
+            outs[3][...] = total[1].astype(BF16)
+            outs[4][...] = total[0]
+
+        send, keep, send_low, send_qkv_out, keep_qkv_out = step(
             planes,
             [
-                *(keep, arrived),
+                *(keep_up, arrived_up, keep_low, arrived, keep_down),
                 *(cut(keep_qkv_out, 2, 2), cut(arrived_qkv_out, 2, 2)),
-                *(keep_down, arrived_down),
             ],
             [
-                *(sds((3, *piece), BF16), sds((2, *piece), F32)),
+                *(sds((2, *piece), BF16), sds((2, *piece), F32), sds(piece, BF16)),
                 *(sds((2, *taller), BF16), sds((2, *taller), F32)),
             ],
             "planes",
         )
-        arrived, arrived_qkv_out = over_z_high(send), over_z_low(send_qkv_out)
+        arrived, arrived_low = over_z_high(send), over_y(send_low)
+        arrived_qkv_out = over_z_low(send_qkv_out)
 
         def lines(ins, outs):
-            send, keep, arrived, keep_qkv_out, arrived_qkv_out = ins
+            send, keep, arrived, arrived_low, keep_qkv_out, arrived_qkv_out = ins
             total = keep_qkv_out[...] + arrived_qkv_out[...].astype(F32)
             outs[0][0] = total[1].astype(BF16)
             outs[1][...] = total[0]
-            for part in range(2):
-                total = keep[part] + arrived[part].astype(F32)
+            for part, came in enumerate((arrived[0], arrived_low[...])):
+                total = keep[part] + came.astype(F32)
                 total = jnp.concatenate([total, jnp.zeros((8, CUT_COLUMNS), F32)], axis=0)
                 outs[0][part + 1] = total.astype(BF16)
-            outs[2][0], outs[2][1] = send[2], arrived[2]
+            outs[2][0], outs[2][1] = send[1], arrived[1]
 
         pieces, keep_qkv_out, near_down = step(
             lines,
-            [send, keep, arrived, keep_qkv_out, arrived_qkv_out],
+            [send, keep, arrived, arrived_low, keep_qkv_out, arrived_qkv_out],
             [sds((3, *taller), BF16), sds(taller, F32), sds((2, *piece), BF16)],
             "lines",
         )
@@ -994,43 +1008,34 @@
         far_down = over_core(near_down)
         up_low, low_x = over_z_low(near_up), over_x(near_low)
 
-        def update(near, far, place, height, state, gains, name, after):
-            near_out = update_half(
-                idx, 0, near, place, height, state, (), gains, name + "_near", after
-            )
-            count = len(state)
-            mark = near_out[-1]
-            far_out = update_half(
-                idx, 1, far, place, height, state, near_out[:count], (), name + "_far", (mark,)
-            )
-            return (*far_out[:count], *near_out[count:-1], far_out[-1])
-
-        one_down, two_down, next_down, mark = update(
-            near_down,
-            far_down,
+        def share_qkv_out_high(ins, outs):
+            outs[0][0], outs[0][1] = ins[0][...], ins[1][...]
+
+        (near_qkv_out,) = step(
+            share_qkv_out_high,
+            [piece_qkv_out, qkv_out_high],
+            [sds((2, *taller), BF16)],
+            "share_qkv_out_high",
+            (near_up,),
+        )
+        qkv_out_x, qkv_out_low = over_x(near_qkv_out), over_z_low(near_qkv_out)
+        qkv_out_both = swap(near_qkv_out, "dp", 6)
+        one_down, two_down, next_down, mark = update_rows(
+            idx,
+            [(0, near_down), (1, far_down)],
             lambda p, x, z: (
                 (x * 2 + (z >> 1)) * CUT_ROWS,
                 [(0, CUT_COLUMNS, (z & 1) * CUT_COLUMNS)],
             ),
             2 * HALF,
+            96,
             [down_t, first_down_t, second_down_t],
             (),
+            (),
             "update_down",
-            (near_up,),
-        )
-
-        def share_qkv_out_high(ins, outs):
-            outs[0][0], outs[0][1] = ins[0][...], ins[1][...]
-
-        (near_qkv_out,) = step(
-            share_qkv_out_high,
-            [piece_qkv_out, qkv_out_high],
-            [sds((2, *taller), BF16)],
-            "share_qkv_out_high",
-            (mark,),
-        )
-        qkv_out_x, qkv_out_low = over_x(near_qkv_out), over_z_low(near_qkv_out)
-        qkv_out_both = swap(near_qkv_out, "dp", 6)
+            (near_qkv_out,),
+            0.1,
+        )
 
         def share_gate_up(ins, outs):
             for near in range(2):
@@ -1044,17 +1049,21 @@
             [near_up, up_low, near_low, low_x],
             [sds((2, 2, 4, *piece), BF16)],
             "share_gate_up",
-            (near_qkv_out,),
+            (mark,),
         )
         far_gate_up = over_core(near_gate_up)
-        one_gate_up, two_gate_up, next_gate_up, mark = update(
-            near_gate_up,
-            far_gate_up,
-            lambda p, x, z: (p * CUT_ROWS, [(0, CUT_COLUMNS, (x * 4 + z) * CUT_COLUMNS)]),
+        place_gate_up = lambda p, x, z: (p * CUT_ROWS, [(0, CUT_COLUMNS, (x * 4 + z) * CUT_COLUMNS)])
+        state_gate_up = [w_gate_up, first_gate_up, second_gate_up]
+        *near_state, mark = update_rows(
+            idx,
+            [(0, near_gate_up)],
+            place_gate_up,
             HALF,
-            [w_gate_up, first_gate_up, second_gate_up],
+            24,
+            state_gate_up,
             (),
-            "update_gate_up",
+            (),
+            "update_gate_up_near",
             (),
         )
 
@@ -1072,16 +1081,30 @@
             (mark,),
         )
         far_qkv_out = over_core(near_qkv_out)
+        one_gate_up, two_gate_up, next_gate_up, mark = update_rows(
+            idx,
+            [(1, far_gate_up)],
+            place_gate_up,
+            HALF,
+            24,
+            state_gate_up,
+            near_state,
+            (),
+            "update_gate_up_far",
+            (near_qkv_out,),
+        )
         cuts = [[(0, 384, 0)], [(0, 384, 384)], [(0, 192, 768), (192, 192, 1024)], [(0, 384, 1216)]]
-        updated = update(
-            near_qkv_out,
-            far_qkv_out,
+        updated = update_rows(
+            idx,
+            [(0, near_qkv_out), (1, far_qkv_out)],
             lambda p, x, z: (x * CUT_ROWS, cuts[z]),
             HALF,
+            48,
             [w_qkv, w_out, first_qkv, first_out, second_qkv, second_out],
+            (),
             (norm_gains, first_gains, second_gains),
             "update_qkv_out",
-            (),
+            (mark,),
         )
         one_qkv, one_out, two_qkv, two_out, next_qkv, next_out = updated[:6]
         one_gains, two_gains, next_gains = updated[6:9]

time: 140 us -> 136 us (0.971)
  starting transfers between devices: 38.6 us -> 48.3 us
  waiting for transfers between devices: 53.5 us -> 44.6 us
  Pallas kernels: 42.3 us -> 36.7 us
  local copies, waits for them, and re-layouts: 2.42 us -> 4.68 us
    ppermute x43 -> x44, starting transfers between devices: 38.6 us -> 48.3 us  [swap(): return lax.ppermute(values, axis, [(i, i ^ mask) for i in range(size)])]
    ppermute x43 -> x44, waiting for transfers between devices: 53.5 us -> 44.6 us  [swap(): return lax.ppermute(values, axis, [(i, i ^ mask) for i in range(size)])]
    pallas_call x6 -> x4, Pallas kernels: 19.2 us -> 14.7 us  [update_rows(): pl.pallas_call(kernel, out_shape=tuple((sds(a.shape, F32) for a in [*stat...]
    unnamed x50 -> x48, local copies, waits for them, and re-layouts: 2.06 us -> 4.33 us
  transfers between devices with their start and end apart: 43 -> 44, of which waited for: 19 -> 20; matrix products, arithmetic and copies ran while one was open for 0% -> 0% of each run, Pallas kernels for 25% -> 22%
where the time goes in v9:
time: 136 us
  starting transfers between devices  48.3 us (36%)
  waiting for transfers between devices  44.6 us (33%)
  Pallas kernels  36.7 us (27%)
  local copies, waits for them, and re-layouts  4.68 us (3%)
    ppermute x44, starting transfers between devices, swap(): return lax.ppermute(values, axis, [(i, i ^ mask) for i in range(size)])  48.3 us
    ppermute x44, waiting for transfers between devices, swap(): return lax.ppermute(values, axis, [(i, i ^ mask) for i in range(size)])  44.6 us
    pallas_call x5, Pallas kernels, call(): pl.pallas_call(kernel, out_shape=tuple(outs), in_specs=[pl.BlockSpec(memo...  15.7 us
    pallas_call x4, Pallas kernels, update_rows(): pl.pallas_call(kernel, out_shape=tuple((sds(a.shape, F32) for a in [*stat...  14.7 us
    unnamed x48, local copies, waits for them, and re-layouts  4.33 us
    pallas_call x17, Pallas kernels, step(): pl.pallas_call(kernel, out_shape=tuple(outs), in_specs=[pl.BlockSpec(memo...  3.34 us
    pallas_call x2, Pallas kernels, pack_kernel(): pl.pallas_call(kernel, out_shape=tuple(outs), in_specs=[pl.BlockSpec(memo...  2.97 us
  transfers between devices with their start and end apart: 44, of which 20 were waited for; matrix products, arithmetic and copies ran while one was open for 0% of the time, Pallas kernels for 22%

profile of v9, /device:TPU:0, one launch (start us, length us, event | category | flops | bytes accessed | tf_op | source)
XLA Modules:
  0.0 135.7 jit_solution(11785710369239854371)
XLA Ops:
  1.4 2.2 %pack_first.1 = (bf16[160,768]{1,0:T(8,128)(2,1)S(1)}, bf16[144,768]{1,0:T(8,128)(2,1)S(1)}, bf16[144,768]{1,0:T(8,128)(2,1)S(1)}) custom-call(s32[4]{0:T(128)S(1)} %pad_add_fusion.idx_ref.refs_0_, f32[288,960]{1,0:T(8,128)} %refs_2_.9, f32[288,576]{1,0:T(8,128)} %refs_3_.8, f32[2,288]{1,0:T(2,128)S(1)} %copy-done.16, f32[288,3072]{1,0:T(8,128)} %refs_1_.5, ...), custom_call_target="tpu_custom_call" | custom-call | flops 10000000000 | tf_op jit(solution)/shard_map/pack_first/pallas_call | solution.py:240
  3.6 3.0 %collective-permute-start = (bf16[160,768]{1,0:T(8,128)(2,1)S(1)}, bf16[160,768]{1,0:T(8,128)(2,1)S(1)}, u32[]{:S(2)}, u32[]{:S(2)}) collective-permute-start(bf16[160,768]{1,0:T(8,128)(2,1)S(1)} %get-tuple-element.103), channel_id=1, source_target_pairs={{0,1},{1,0},{2,3},{3,2},{4,5},{5,4},{6,7},{7,6},{8,9},{9,8},{10,11... | collective-permute-start | bytes 737288 | tf_op jit(solution)/shard_map/ppermute | solution.py:701
  6.7 1.9 %collective-permute-start.4 = (bf16[144,768]{1,0:T(8,128)(2,1)S(1)}, bf16[144,768]{1,0:T(8,128)(2,1)S(1)}, u32[]{:S(2)}, u32[]{:S(2)}) collective-permute-start(bf16[144,768]{1,0:T(8,128)(2,1)S(1)} %get-tuple-element.107), channel_id=1, source_target_pairs={{0,1},{1,0},{2,3},{3,2},{4,5},{5,4},{6,7},{7,6},{8,9},{9,8},{10,11... | collective-permute-start | bytes 663560 | tf_op jit(solution)/shard_map/ppermute | solution.py:701
  8.7 9.5 %collective-permute-done.8.refs_11_.refs_1_ = bf16[144,768]{1,0:T(8,128)(2,1)S(1)} collective-permute-done((bf16[144,768]{1,0:T(8,128)(2,1)S(1)}, bf16[144,768]{1,0:T(8,128)(2,1)S(1)}, u32[]{:S(2)}, u32[]{:S(2)}) %collective-permute-start.8) | collective-permute-done | bytes 221216 | tf_op jit(solution)/shard_map/ppermute | solution.py:701
  18.2 2.1 %collective-permute-start.9 = (bf16[144,768]{1,0:T(8,128)(2,1)S(1)}, bf16[144,768]{1,0:T(8,128)(2,1)S(1)}, u32[]{:S(2)}, u32[]{:S(2)}) collective-permute-start(bf16[144,768]{1,0:T(8,128)(2,1)S(1)} %collective-permute-done.8.refs_11_.refs_1_), channel_id=1, source_target_pairs={{0,8},{2,10},{4,12},{6,14},{8,0},{10,2},{12,4},{14,6},{16,24},{18,... | collective-permute-start | bytes 663560 | tf_op jit(solution)/shard_map/ppermute | solution.py:701
  21.2 2.0 %collective-permute-start.12 = (bf16[288,768]{1,0:T(8,128)(2,1)S(1)}, bf16[288,768]{1,0:T(8,128)(2,1)S(1)}, u32[]{:S(2)}, u32[]{:S(2)}) collective-permute-start(bf16[288,768]{1,0:T(8,128)(2,1)S(1)} %pack_down.1), channel_id=1, source_target_pairs={{0,1},{1,0},{2,3},{3,2},{4,5},{5,4},{6,7},{7,6},{8,9},{9,8},{10,11... | collective-permute-start | bytes 1327112 | tf_op jit(solution)/shard_map/ppermute | solution.py:701
  23.2 1.5 %collective-permute-start.5 = (bf16[144,768]{1,0:T(8,128)(2,1)S(1)}, bf16[144,768]{1,0:T(8,128)(2,1)S(1)}, u32[]{:S(2)}, u32[]{:S(2)}) collective-permute-start(bf16[144,768]{1,0:T(8,128)(2,1)S(1)} %collective-permute-done.4.refs_7_), channel_id=1, source_target_pairs={{0,4},{2,6},{4,0},{6,2},{8,12},{10,14},{12,8},{14,10},{16,20},{18,... | collective-permute-start | bytes 663560 | tf_op jit(solution)/shard_map/ppermute | solution.py:701
  24.7 1.4 %collective-permute-done.9.refs_12_ = bf16[144,768]{1,0:T(8,128)(2,1)S(1)} collective-permute-done((bf16[144,768]{1,0:T(8,128)(2,1)S(1)}, bf16[144,768]{1,0:T(8,128)(2,1)S(1)}, u32[]{:S(2)}, u32[]{:S(2)}) %collective-permute-start.9) | collective-permute-done | bytes 221216 | tf_op jit(solution)/shard_map/ppermute | solution.py:701
  26.1 3.4 %collective-permute-done.1.refs_9_ = bf16[160,768]{1,0:T(8,128)(2,1)S(1)} collective-permute-done((bf16[160,768]{1,0:T(8,128)(2,1)S(1)}, bf16[160,768]{1,0:T(8,128)(2,1)S(1)}, u32[]{:S(2)}, u32[]{:S(2)}) %collective-permute-start.1) | collective-permute-done | bytes 245792 | tf_op jit(solution)/shard_map/ppermute | solution.py:701
  29.5 1.0 collective-permute-done.5.refs_8_
  31.2 2.5 %attention.1 = (bf16[128,960]{1,0:T(8,128)(2,1)S(1)}, bf16[128,576]{1,0:T(8,128)(2,1)S(1)}, f32[128,128]{1,0:T(8,128)S(1)}, f32[128,128]{1,0:T(8,128)S(1)}, f32[...) custom-call(s32[4]{0:T(128)S(1)} %pad_add_fusion.idx_ref.refs_0_, ...), custom_call_target="tpu_custom_call" | custom-call | flops 1000000000 | tf_op jit(solution)/shard_map/attention/pallas_call | solution.py:150
  34.3 2.8 %feed_forward.1 = (f32[128,576]{1,0:T(8,128)S(1)}, bf16[128,576]{1,0:T(8,128)(2,1)S(1)}, f32[128,3072]{1,0:T(8,128)S(1)}, bf16[128,1536]{1,0:T(8,128)(2,1)S(1)},...) custom-call(s32[4]{0:T(128)S(1)} %pad_add_fusion.idx_ref.refs_0_, ...), custom_call_target="tpu_custom_call" | custom-call | flops 5000000000 | tf_op jit(solution)/shard_map/feed_forward/pallas_call | solution.py:150
  37.3 2.6 %feed_back.1 = (bf16[128,3072]{1,0:T(8,128)(2,1)S(1)}, bf16[2,2,8,72,384]{4,3,2,1,0:T(8,128)(2,1)S(1)}, bf16[2,2,8,72,384]{4,3,2,1,0:T(8,128)(2,1)S(1)}, bf16[576,1536]{1,0:T(8,128)(2,1)S(1)}) custom-call(s32[4]{0:T(128)S(1)} %pad_add_fusion.idx_ref.refs_0_, f32[128,3072]{1,0:T(8,128)S(1)} %get-tuple-element.111.refs_1_, ...), custom_call_target="tpu_custom_call" | custom-call | flops 20000000000 | tf_op jit(solution)/shard_map/feed_back/pallas_call | solution.py:150
  40.8 1.6 %collective-permute-start.18 = (bf16[8,72,384]{2,1,0:T(8,128)(2,1)S(1)}, bf16[8,72,384]{2,1,0:T(8,128)(2,1)S(1)}, u32[]{:S(2)}, u32[]{:S(2)}) collective-permute-start(bf16[8,72,384]{2,1,0:T(8,128)(2,1)S(1)} %get-tuple-element.126), channel_id=1, source_target_pairs={{0,1},{1,0},{2,3},{3,2},{4,5},{5,4},{6,7},{7,6},{8,9},{9,8},{10,11... | collective-permute-start | bytes 1327112 | tf_op jit(solution)/shard_map/ppermute | solution.py:701
  42.4 2.7 %middle_back.1 = (f32[128,576]{1,0:T(8,128)S(1)}, bf16[128,576]{1,0:T(8,128)(2,1)S(1)}, f32[1,576]{1,0:T(1,128)S(1)}) custom-call(s32[4]{0:T(128)S(1)} %pad_add_fusion.idx_ref.refs_0_, bf16[576,128]{1,0:T(8,128)(2,1)S(1)} %bitcast.61, f32[128,576]{1,0:T(8,128)S(1)} %get-tuple-element.109.refs_2_.refs_0_, ...), custom_call_target="tpu_custom_call" | custom-call | flops 20000000000 | tf_op jit(solution)/shard_map/middle_back/pallas_call | solution.py:150
  45.7 1.6 %collective-permute-start.16 = (bf16[2,4,72,384]{3,2,1,0:T(8,128)(2,1)S(1)}, bf16[2,4,72,384]{3,2,1,0:T(8,128)(2,1)S(1)}, u32[]{:S(2)}, u32[]{:S(2)}) collective-permute-start(bf16[2,4,72,384]{3,2,1,0:T(8,128)(2,1)S(1)} %get-tuple-element.123), channel_id=1, source_target_pairs={{0,4},{2,6},{4,0},{6,2},{8,12},{10,14},{12,8},{14,10},{16,20},{18,... | collective-permute-start | bytes 1327112 | tf_op jit(solution)/shard_map/ppermute | solution.py:701
  47.3 1.6 %collective-permute-start.17 = (bf16[4,2,72,384]{3,2,1,0:T(8,128)(2,1)S(1)}, bf16[4,2,72,384]{3,2,1,0:T(8,128)(2,1)S(1)}, u32[]{:S(2)}, u32[]{:S(2)}) collective-permute-start(bf16[4,2,72,384]{3,2,1,0:T(8,128)(2,1)S(1)} %get-tuple-element.125), channel_id=1, source_target_pairs={{0,8},{2,10},{4,12},{6,14},{8,0},{10,2},{12,4},{14,6},{16,24},{18,... | collective-permute-start | bytes 1327112 | tf_op jit(solution)/shard_map/ppermute | solution.py:701
  48.8 5.1 %attention_back.1 = (bf16[576,128]{1,0:T(8,128)(2,1)}, bf16[1,2,8,80,384]{4,3,2,1,0:T(8,128)(2,1)S(1)}, bf16[1,2,8,80,384]{4,3,2,1,0:T(8,128)(2,1)S(1)}, f32[8,128]{1,0:T(8,128)S(1)}) custom-call(s32[4]{0:T(128)S(1)} %pad_add_fusion.idx_ref.refs_0_, bf16[576,128]{1,0:T(8,128)(2,1)S(1)} %bitcast.64, f32[128,576]{1,0:T(8,128)S(1)} %get-tuple-element.121.refs_4_.refs_2_, ...), custom_call_target="tpu_custom_call" | custom-call | flops 20000000000 | tf_op jit(solution)/shard_map/attention_back/pallas_call | solution.py:150
  54.0 1.0 collective-permute-start.23
  55.0 3.8 %collective-permute-done.16 = bf16[2,4,72,384]{3,2,1,0:T(8,128)(2,1)S(1)} collective-permute-done((bf16[2,4,72,384]{3,2,1,0:T(8,128)(2,1)S(1)}, bf16[2,4,72,384]{3,2,1,0:T(8,128)(2,1)S(1)}, u32[]{:S(2)}, u32[]{:S(2)}) %collective-permute-start.16) | collective-permute-done | bytes 442400 | tf_op jit(solution)/shard_map/ppermute | solution.py:701
  59.3 1.6 %collective-permute-start.19 = (bf16[2,2,72,384]{3,2,1,0:T(8,128)(2,1)S(1)}, bf16[2,2,72,384]{3,2,1,0:T(8,128)(2,1)S(1)}, u32[]{:S(2)}, u32[]{:S(2)}) collective-permute-start(bf16[2,2,72,384]{3,2,1,0:T(8,128)(2,1)S(1)} %get-tuple-element.136), channel_id=1, source_target_pairs={{0,8},{2,10},{4,12},{6,14},{8,0},{10,2},{12,4},{14,6},{16,24},{18,... | collective-permute-start | bytes 663560 | tf_op jit(solution)/shard_map/ppermute | solution.py:701
  60.9 1.2 collective-permute-start.20
  63.1 2.1 %collective-permute-start.24 = (bf16[2,72,384]{2,1,0:T(8,128)(2,1)S(1)}, bf16[2,72,384]{2,1,0:T(8,128)(2,1)S(1)}, u32[]{:S(2)}, u32[]{:S(2)}) collective-permute-start(bf16[2,72,384]{2,1,0:T(8,128)(2,1)S(1)} %get-tuple-element.145), channel_id=1, source_target_pairs={{0,8},{2,10},{4,12},{6,14},{8,0},{10,2},{12,4},{14,6},{16,24},{18,... | collective-permute-start | bytes 331784 | tf_op jit(solution)/shard_map/ppermute | solution.py:701
  65.2 1.3 collective-permute-done.19.refs_1_
  68.0 5.3 %collective-permute-done.22 = bf16[8,80,384]{2,1,0:T(8,128)(2,1)S(1)} collective-permute-done((bf16[8,80,384]{2,1,0:T(8,128)(2,1)S(1)}, bf16[8,80,384]{2,1,0:T(8,128)(2,1)S(1)}, u32[]{:S(2)}, u32[]{:S(2)}) %collective-permute-start.22) | collective-permute-done | bytes 491552 | tf_op jit(solution)/shard_map/ppermute | solution.py:701
  73.6 1.5 %collective-permute-start.27 = (bf16[4,80,384]{2,1,0:T(8,128)(2,1)S(1)}, bf16[4,80,384]{2,1,0:T(8,128)(2,1)S(1)}, u32[]{:S(2)}, u32[]{:S(2)}) collective-permute-start(bf16[4,80,384]{2,1,0:T(8,128)(2,1)S(1)} %get-tuple-element.152), channel_id=1, source_target_pairs={{0,4},{2,6},{4,0},{6,2},{8,12},{10,14},{12,8},{14,10},{16,20},{18,... | collective-permute-start | bytes 737288 | tf_op jit(solution)/shard_map/ppermute | solution.py:701
  75.1 2.6 %collective-permute-start.26 = (bf16[3,72,384]{2,1,0:T(8,128)(2,1)S(1)}, bf16[3,72,384]{2,1,0:T(8,128)(2,1)S(1)}, u32[]{:S(2)}, u32[]{:S(2)}) collective-permute-start(bf16[3,72,384]{2,1,0:T(8,128)(2,1)S(1)} %get-tuple-element.149), channel_id=1, source_target_pairs={{0,16},{2,18},{4,20},{6,22},{8,24},{10,26},{12,28},{14,30},{16,0},... | collective-permute-start | bytes 497672 | tf_op jit(solution)/shard_map/ppermute | solution.py:701
  78.2 4.2 %collective-permute-done.25.refs_1_ = bf16[2,72,384]{2,1,0:T(8,128)(2,1)S(1)} collective-permute-done((bf16[2,72,384]{2,1,0:T(8,128)(2,1)S(1)}, bf16[2,72,384]{2,1,0:T(8,128)(2,1)S(1)}, u32[]{:S(2)}, u32[]{:S(2)}) %collective-permute-start.25) | collective-permute-done | bytes 110624 | tf_op jit(solution)/shard_map/ppermute | solution.py:701
  83.3 2.8 %collective-permute-start.28 = (bf16[2,72,384]{2,1,0:T(8,128)(2,1)S(1)}, bf16[2,72,384]{2,1,0:T(8,128)(2,1)S(1)}, u32[]{:S(2)}, u32[]{:S(2)}) collective-permute-start(bf16[2,72,384]{2,1,0:T(8,128)(2,1)S(1)} %get-tuple-element.153.refs_0_), channel_id=1, source_target_pairs={{0,16},{2,18},{4,20},{6,22},{8,24},{10,26},{12,28},{14,30},{16,0},... | collective-permute-start | bytes 331784 | tf_op jit(solution)/shard_map/ppermute | solution.py:701
  86.6 3.6 %collective-permute-done.29.refs_3_ = bf16[72,384]{1,0:T(8,128)(2,1)S(1)} collective-permute-done((bf16[72,384]{1,0:T(8,128)(2,1)S(1)}, bf16[72,384]{1,0:T(8,128)(2,1)S(1)}, u32[]{:S(2)}, u32[]{:S(2)}) %collective-permute-start.29) | collective-permute-done | bytes 55328 | tf_op jit(solution)/shard_map/ppermute | solution.py:701
  90.3 2.8 %collective-permute-start.31 = (bf16[3,80,384]{2,1,0:T(8,128)(2,1)S(1)}, bf16[3,80,384]{2,1,0:T(8,128)(2,1)S(1)}, u32[]{:S(2)}, u32[]{:S(2)}) collective-permute-start(bf16[3,80,384]{2,1,0:T(8,128)(2,1)S(1)} %get-tuple-element.158.refs_0_), channel_id=1, source_target_pairs={{0,16},{2,18},{4,20},{6,22},{8,24},{10,26},{12,28},{14,30},{16,0},... | collective-permute-start | bytes 552968 | tf_op jit(solution)/shard_map/ppermute | solution.py:701
  93.2 3.8 %collective-permute-start.32 = (bf16[2,72,384]{2,1,0:T(8,128)(2,1)S(1)}, bf16[2,72,384]{2,1,0:T(8,128)(2,1)S(1)}, u32[]{:S(2)}, u32[]{:S(2)}) collective-permute-start(bf16[2,72,384]{2,1,0:T(8,128)(2,1)S(1)} %get-tuple-element.160.refs_3_), channel_id=1, source_target_pairs={{0,8},{2,10},{4,12},{6,14},{8,0},{10,2},{12,4},{14,6},{16,24},{18,... | collective-permute-start | bytes 331784 | tf_op jit(solution)/shard_map/ppermute | solution.py:701
  97.0 4.5 %collective-permute-done.32.refs_4_ = bf16[2,72,384]{2,1,0:T(8,128)(2,1)S(1)} collective-permute-done((bf16[2,72,384]{2,1,0:T(8,128)(2,1)S(1)}, bf16[2,72,384]{2,1,0:T(8,128)(2,1)S(1)}, u32[]{:S(2)}, u32[]{:S(2)}) %collective-permute-start.32) | collective-permute-done | bytes 110624 | tf_op jit(solution)/shard_map/ppermute | solution.py:701
  101.5 1.9 %collective-permute-start.34 = (bf16[3,2,72,384]{3,2,1,0:T(8,128)(2,1)S(1)}, bf16[3,2,72,384]{3,2,1,0:T(8,128)(2,1)S(1)}, u32[]{:S(2)}, u32[]{:S(2)}) collective-permute-start(bf16[3,2,72,384]{3,2,1,0:T(8,128)(2,1)S(1)} %get-tuple-element.161.refs_3_.refs_0_), channel_id=1, source_target_pairs={{0,4},{2,6},{4,0},{6,2},{8,12},{10,14},{12,8},{14,10},{16,20},{18,... | collective-permute-start | bytes 995336 | tf_op jit(solution)/shard_map/ppermute | solution.py:701
  103.4 1.0 collective-permute-start.33
  104.4 1.4 %collective-permute-start.35 = (bf16[2,72,384]{2,1,0:T(8,128)(2,1)S(1)}, bf16[2,72,384]{2,1,0:T(8,128)(2,1)S(1)}, u32[]{:S(2)}, u32[]{:S(2)}) collective-permute-start(bf16[2,72,384]{2,1,0:T(8,128)(2,1)S(1)} %get-tuple-element.164.refs_2_), channel_id=1, source_target_pairs={{0,8},{2,10},{4,12},{6,14},{8,0},{10,2},{12,4},{14,6},{16,24},{18,... | collective-permute-start | bytes 331784 | tf_op jit(solution)/shard_map/ppermute | solution.py:701
  105.8 1.5 %layer_output.1 = bf16[576,128]{1,0:T(8,128)(2,1)} custom-call(f32[128,576]{1,0:T(8,128)S(1)} %copy-done.23, bf16[128,1536]{1,0:T(8,128)(2,1)S(1)} %get-tuple-element.110.refs_1_, bf16[576,1536]{1,0:T(8,128)(2,1)S(1)} %get-tuple-element.113.refs_2_, bf16[3,2,72,384]{3,2,1,0:T(8,128)(2,1)S(1)} %get-tuple-element.161.refs_3_.refs_0_), custom_call_target="tpu_custom_call" | custom-call | flops 2000000000 | tf_op jit(solution)/shard_map/layer_output/pallas_call | solution.py:568
  107.3 1.6 %collective-permute-done.33.refs_4_.refs_1_ = bf16[80,384]{1,0:T(8,128)(2,1)S(1)} collective-permute-done((bf16[80,384]{1,0:T(8,128)(2,1)S(1)}, bf16[80,384]{1,0:T(8,128)(2,1)S(1)}, u32[]{:S(2)}, u32[]{:S(2)}) %collective-permute-start.33) | collective-permute-done | bytes 61472 | tf_op jit(solution)/shard_map/ppermute | solution.py:701
  108.8 1.2 collective-permute-done.35.refs_3_
  110.4 1.8 %collective-permute-start.40 = (bf16[2,2,72,384]{3,2,1,0:T(8,128)(2,1)S(1)}, bf16[2,2,72,384]{3,2,1,0:T(8,128)(2,1)S(1)}, u32[]{:S(2)}, u32[]{:S(2)}) collective-permute-start(bf16[2,2,72,384]{3,2,1,0:T(8,128)(2,1)S(1)} %get-tuple-element.166.refs_2_), channel_id=1, source_target_pairs={{0,4},{2,6},{4,0},{6,2},{8,12},{10,14},{12,8},{14,10},{16,20},{18,... | collective-permute-start | bytes 663560 | tf_op jit(solution)/shard_map/ppermute | solution.py:701
  112.7 1.3 collective-permute-start.38
  114.9 1.3 collective-permute-start.36
  116.2 3.3 %update_down.1 = (f32[576,768]{1,0:T(8,128)}, f32[576,768]{1,0:T(8,128)}, f32[576,768]{1,0:T(8,128)}, f32[8,128]{1,0:T(8,128)S(1)}) custom-call(s32[4]{0:T(128)S(1)} %pad_add_fusion.idx_ref.refs_0_, bf16[1,2,4,72,384]{4,3,2,1,0:T(8,128)(2,1)S(1)} %get-tuple-element.167.refs_0_, bf16[1,2,4,72,384]{4,3,2,1,0:T(8,128)(2,1)S(1)} %collective-permute-done.41.refs_1_, ...), custom_call_target="tpu_custom_call" | custom-call | flops 100000000 | tf_op jit(solution)/shard_map/update_down/pallas_call | solution.py:682
  120.3 1.8 %copy-done.4 = f32[288,3072]{1,0:T(8,128)S(1)} copy-done((f32[288,3072]{1,0:T(8,128)S(1)}, f32[288,3072]{1,0:T(8,128)}, u32[]{:S(2)}) %copy-start.4) | copy-done | bytes 3538968
  122.2 1.1 copy-done.5
  123.2 3.4 %update_gate_up_near.1 = (f32[288,3072]{1,0:T(8,128)}, f32[288,3072]{1,0:T(8,128)}, f32[288,3072]{1,0:T(8,128)}, f32[8,128]{1,0:T(8,128)S(1)}) custom-call(s32[4]{0:T(128)S(1)} %pad_add_fusion.idx_ref.refs_0_, bf16[2,2,4,72,384]{4,3,2,1,0:T(8,128)(2,1)S(1)} %share_gate_up.1.refs_0_, f32[288,3072]{1,0:T(8,128)S(1)} %copy-done.3, f32[288,3072]{1,0:T(8,128)S(1)} %copy-done.4, ...), custom_call_target="tpu_custom_call" | custom-call | flops 20000000000 | tf_op jit(solution)/shard_map/update_gate_up_near/pallas_call | solution.py:682
  126.9 3.7 %update_gate_up_far.1 = (f32[288,3072]{1,0:T(8,128)}, f32[288,3072]{1,0:T(8,128)}, f32[288,3072]{1,0:T(8,128)}, f32[8,128]{1,0:T(8,128)S(1)}) custom-call(s32[4]{0:T(128)S(1)} %pad_add_fusion.idx_ref.refs_0_, bf16[2,2,4,72,384]{4,3,2,1,0:T(8,128)(2,1)S(1)} %collective-permute-done.43.refs_0_, ...), custom_call_target="tpu_custom_call", output_to_operand_aliasing={{0}: (5, {}), {1}: (6, {}), {2}: (7, {})} | custom-call | flops 20000000000 | tf_op jit(solution)/shard_map/update_gate_up_far/pallas_call | solution.py:682
  131.3 4.3 %update_qkv_out.1 = (f32[288,960]{1,0:T(8,128)}, f32[288,576]{1,0:T(8,128)}, f32[288,960]{1,0:T(8,128)}, f32[288,576]{1,0:T(8,128)}, f32[288,960]{1,0:T(8,128)},...) custom-call(s32[4]{0:T(128)S(1)} %pad_add_fusion.idx_ref.refs_0_, ...), custom_call_target="tpu_custom_call" | custom-call | flops 20000000000 | tf_op jit(solution)/shard_map/update_qkv_out/pallas_call | solution.py:682
  (119 shorter events, 13.2 us)
Async XLA Ops:
  1.4 19.0 %copy-start = (f32[768,576]{0,1:T(8,128)S(1)}, f32[768,576]{0,1:T(8,128)}, u32[]{:S(2)}) copy-start(f32[768,576]{0,1:T(8,128)} %param.25) | copy-start | bytes 5308420
  3.6 16.7 %collective-permute-start = (bf16[160,768]{1,0:T(8,128)(2,1)S(1)}, bf16[160,768]{1,0:T(8,128)(2,1)S(1)}, u32[]{:S(2)}, u32[]{:S(2)}) collective-permute-start(bf16[160,768]{1,0:T(8,128)(2,1)S(1)} %get-tuple-element.103), channel_id=1, source_target_pairs={{0,1},{1,0},{2,3},{3,2},{4,5},{5,4},{6,7},{7,6},{8,9},{9,8},{10,11... | collective-permute-start | bytes 737288 | tf_op jit(solution)/shard_map/ppermute | solution.py:701
  6.7 11.5 %collective-permute-start.8 = (bf16[144,768]{1,0:T(8,128)(2,1)S(1)}, bf16[144,768]{1,0:T(8,128)(2,1)S(1)}, u32[]{:S(2)}, u32[]{:S(2)}) collective-permute-start(bf16[144,768]{1,0:T(8,128)(2,1)S(1)} %get-tuple-element.108), channel_id=1, source_target_pairs={{0,1},{1,0},{2,3},{3,2},{4,5},{5,4},{6,7},{7,6},{8,9},{9,8},{10,11... | collective-permute-start | bytes 663560 | tf_op jit(solution)/shard_map/ppermute | solution.py:701
  6.7 16.5 %collective-permute-start.4 = (bf16[144,768]{1,0:T(8,128)(2,1)S(1)}, bf16[144,768]{1,0:T(8,128)(2,1)S(1)}, u32[]{:S(2)}, u32[]{:S(2)}) collective-permute-start(bf16[144,768]{1,0:T(8,128)(2,1)S(1)} %get-tuple-element.107), channel_id=1, source_target_pairs={{0,1},{1,0},{2,3},{3,2},{4,5},{5,4},{6,7},{7,6},{8,9},{9,8},{10,11... | collective-permute-start | bytes 663560 | tf_op jit(solution)/shard_map/ppermute | solution.py:701
  18.2 7.9 %collective-permute-start.9 = (bf16[144,768]{1,0:T(8,128)(2,1)S(1)}, bf16[144,768]{1,0:T(8,128)(2,1)S(1)}, u32[]{:S(2)}, u32[]{:S(2)}) collective-permute-start(bf16[144,768]{1,0:T(8,128)(2,1)S(1)} %collective-permute-done.8.refs_11_.refs_1_), channel_id=1, source_target_pairs={{0,8},{2,10},{4,12},{6,14},{8,0},{10,2},{12,4},{14,6},{16,24},{18,... | collective-permute-start | bytes 663560 | tf_op jit(solution)/shard_map/ppermute | solution.py:701
  20.3 10.2 %collective-permute-start.2 = (bf16[160,768]{1,0:T(8,128)(2,1)S(1)}, bf16[160,768]{1,0:T(8,128)(2,1)S(1)}, u32[]{:S(2)}, u32[]{:S(2)}) collective-permute-start(bf16[160,768]{1,0:T(8,128)(2,1)S(1)} %collective-permute-done.refs_5_.refs_8_), channel_id=1, source_target_pairs={{0,2},{2,0},{4,6},{6,4},{8,10},{10,8},{12,14},{14,12},{16,18},{18,... | collective-permute-start | bytes 737288 | tf_op jit(solution)/shard_map/ppermute | solution.py:701
  20.3 9.2 %collective-permute-start.1 = (bf16[160,768]{1,0:T(8,128)(2,1)S(1)}, bf16[160,768]{1,0:T(8,128)(2,1)S(1)}, u32[]{:S(2)}, u32[]{:S(2)}) collective-permute-start(bf16[160,768]{1,0:T(8,128)(2,1)S(1)} %collective-permute-done.refs_5_.refs_8_), channel_id=1, source_target_pairs={{0,8},{2,10},{4,12},{6,14},{8,0},{10,2},{12,4},{14,6},{16,24},{18,... | collective-permute-start | bytes 737288 | tf_op jit(solution)/shard_map/ppermute | solution.py:701
  21.2 9.9 %copy-start.6 = (f32[288,960]{1,0:T(8,128)S(1)}, f32[288,960]{1,0:T(8,128)}, u32[]{:S(2)}) copy-start(f32[288,960]{1,0:T(8,128)} %refs_2_.9) | copy-start | bytes 3317764
  21.2 9.9 %copy-start.10 = (f32[288,576]{1,0:T(8,128)S(1)}, f32[288,576]{1,0:T(8,128)}, u32[]{:S(2)}) copy-start(f32[288,576]{1,0:T(8,128)} %refs_3_.8) | copy-start | bytes 1990660
  21.2 9.9 %copy-start.15 = (bf16[1,128,576]{1,2,0:T(8,128)(2,1)S(1)}, bf16[1,128,576]{1,2,0:T(8,128)(2,1)}, u32[]{:S(2)}) copy-start(bf16[1,128,576]{1,2,0:T(8,128)(2,1)} %param.19) | copy-start | bytes 442372
  21.2 12.6 %collective-permute-start.12 = (bf16[288,768]{1,0:T(8,128)(2,1)S(1)}, bf16[288,768]{1,0:T(8,128)(2,1)S(1)}, u32[]{:S(2)}, u32[]{:S(2)}) collective-permute-start(bf16[288,768]{1,0:T(8,128)(2,1)S(1)} %pack_down.1), channel_id=1, source_target_pairs={{0,1},{1,0},{2,3},{3,2},{4,5},{5,4},{6,7},{7,6},{8,9},{9,8},{10,11... | collective-permute-start | bytes 1327112 | tf_op jit(solution)/shard_map/ppermute | solution.py:701
  23.2 7.3 %collective-permute-start.5 = (bf16[144,768]{1,0:T(8,128)(2,1)S(1)}, bf16[144,768]{1,0:T(8,128)(2,1)S(1)}, u32[]{:S(2)}, u32[]{:S(2)}) collective-permute-start(bf16[144,768]{1,0:T(8,128)(2,1)S(1)} %collective-permute-done.4.refs_7_), channel_id=1, source_target_pairs={{0,4},{2,6},{4,0},{6,2},{8,12},{10,14},{12,8},{14,10},{16,20},{18,... | collective-permute-start | bytes 663560 | tf_op jit(solution)/shard_map/ppermute | solution.py:701
  26.1 4.9 %collective-permute-start.11 = (bf16[144,768]{1,0:T(8,128)(2,1)S(1)}, bf16[144,768]{1,0:T(8,128)(2,1)S(1)}, u32[]{:S(2)}, u32[]{:S(2)}) collective-permute-start(bf16[144,768]{1,0:T(8,128)(2,1)S(1)} %collective-permute-done.9.refs_12_), channel_id=1, source_target_pairs={{0,2},{2,0},{4,6},{6,4},{8,10},{10,8},{12,14},{14,12},{16,18},{18,... | collective-permute-start | bytes 663560 | tf_op jit(solution)/shard_map/ppermute | solution.py:701
  29.5 1.6 %collective-permute-start.3 = (bf16[160,768]{1,0:T(8,128)(2,1)S(1)}, bf16[160,768]{1,0:T(8,128)(2,1)S(1)}, u32[]{:S(2)}, u32[]{:S(2)}) collective-permute-start(bf16[160,768]{1,0:T(8,128)(2,1)S(1)} %collective-permute-done.1.refs_9_), channel_id=1, source_target_pairs={{0,2},{2,0},{4,6},{6,4},{8,10},{10,8},{12,14},{14,12},{16,18},{18,... | collective-permute-start | bytes 737288 | tf_op jit(solution)/shard_map/ppermute | solution.py:701
  30.5 3.8 %collective-permute-start.6 = (bf16[144,768]{1,0:T(8,128)(2,1)S(1)}, bf16[144,768]{1,0:T(8,128)(2,1)S(1)}, u32[]{:S(2)}, u32[]{:S(2)}) collective-permute-start(bf16[144,768]{1,0:T(8,128)(2,1)S(1)} %collective-permute-done.4.refs_7_), channel_id=1, source_target_pairs={{0,2},{2,0},{4,6},{6,4},{8,10},{10,8},{12,14},{14,12},{16,18},{18,... | collective-permute-start | bytes 663560 | tf_op jit(solution)/shard_map/ppermute | solution.py:701
  30.5 3.8 %collective-permute-start.10 = (bf16[144,768]{1,0:T(8,128)(2,1)S(1)}, bf16[144,768]{1,0:T(8,128)(2,1)S(1)}, u32[]{:S(2)}, u32[]{:S(2)}) collective-permute-start(bf16[144,768]{1,0:T(8,128)(2,1)S(1)} %collective-permute-done.8.refs_11_.refs_1_), channel_id=1, source_target_pairs={{0,2},{2,0},{4,6},{6,4},{8,10},{10,8},{12,14},{14,12},{16,18},{18,... | collective-permute-start | bytes 663560 | tf_op jit(solution)/shard_map/ppermute | solution.py:701
  31.0 3.3 %collective-permute-start.7 = (bf16[144,768]{1,0:T(8,128)(2,1)S(1)}, bf16[144,768]{1,0:T(8,128)(2,1)S(1)}, u32[]{:S(2)}, u32[]{:S(2)}) collective-permute-start(bf16[144,768]{1,0:T(8,128)(2,1)S(1)} %collective-permute-done.5.refs_8_), channel_id=1, source_target_pairs={{0,2},{2,0},{4,6},{6,4},{8,10},{10,8},{12,14},{14,12},{16,18},{18,... | collective-permute-start | bytes 663560 | tf_op jit(solution)/shard_map/ppermute | solution.py:701
  33.8 3.5 %collective-permute-start.13 = (bf16[288,768]{1,0:T(8,128)(2,1)S(1)}, bf16[288,768]{1,0:T(8,128)(2,1)S(1)}, u32[]{:S(2)}, u32[]{:S(2)}) collective-permute-start(bf16[288,768]{1,0:T(8,128)(2,1)S(1)} %pass_on.1.refs_5_), channel_id=1, source_target_pairs={{0,2},{2,0},{4,6},{6,4},{8,10},{10,8},{12,14},{14,12},{16,18},{18,... | collective-permute-start | bytes 1327112 | tf_op jit(solution)/shard_map/ppermute | solution.py:701
  37.1 3.5 %collective-permute-start.15 = (bf16[1,2,8,72,384]{4,3,2,1,0:T(8,128)(2,1)S(1)}, bf16[1,2,8,72,384]{4,3,2,1,0:T(8,128)(2,1)S(1)}, u32[]{:S(2)}, u32[]{:S(2)}) collective-permute-start(bf16[1,2,8,72,384]{4,3,2,1,0:T(8,128)(2,1)S(1)} %get-tuple-element.119), channel_id=1, source_target_pairs={{0,2},{2,0},{4,6},{6,4},{8,10},{10,8},{12,14},{14,12},{16,18},{18,... | collective-permute-start | bytes 2654216 | tf_op jit(solution)/shard_map/ppermute | solution.py:701
  40.0 5.1 %collective-permute-start.14 = (bf16[2,2,8,72,384]{4,3,2,1,0:T(8,128)(2,1)S(1)}, bf16[2,2,8,72,384]{4,3,2,1,0:T(8,128)(2,1)S(1)}, u32[]{:S(2)}, u32[]{:S(2)}) collective-permute-start(bf16[2,2,8,72,384]{4,3,2,1,0:T(8,128)(2,1)S(1)} %get-tuple-element.115), channel_id=1, source_target_pairs={{0,2},{2,0},{4,6},{6,4},{8,10},{10,8},{12,14},{14,12},{16,18},{18,... | collective-permute-start | bytes 5308424 | tf_op jit(solution)/shard_map/ppermute | solution.py:701
  40.8 13.1 %collective-permute-start.18 = (bf16[8,72,384]{2,1,0:T(8,128)(2,1)S(1)}, bf16[8,72,384]{2,1,0:T(8,128)(2,1)S(1)}, u32[]{:S(2)}, u32[]{:S(2)}) collective-permute-start(bf16[8,72,384]{2,1,0:T(8,128)(2,1)S(1)} %get-tuple-element.126), channel_id=1, source_target_pairs={{0,1},{1,0},{2,3},{3,2},{4,5},{5,4},{6,7},{7,6},{8,9},{9,8},{10,11... | collective-permute-start | bytes 1327112 | tf_op jit(solution)/shard_map/ppermute | solution.py:701
  45.7 13.1 %collective-permute-start.16 = (bf16[2,4,72,384]{3,2,1,0:T(8,128)(2,1)S(1)}, bf16[2,4,72,384]{3,2,1,0:T(8,128)(2,1)S(1)}, u32[]{:S(2)}, u32[]{:S(2)}) collective-permute-start(bf16[2,4,72,384]{3,2,1,0:T(8,128)(2,1)S(1)} %get-tuple-element.123), channel_id=1, source_target_pairs={{0,4},{2,6},{4,0},{6,2},{8,12},{10,14},{12,8},{14,10},{16,20},{18,... | collective-permute-start | bytes 1327112 | tf_op jit(solution)/shard_map/ppermute | solution.py:701
  47.3 11.9 %collective-permute-start.17 = (bf16[4,2,72,384]{3,2,1,0:T(8,128)(2,1)S(1)}, bf16[4,2,72,384]{3,2,1,0:T(8,128)(2,1)S(1)}, u32[]{:S(2)}, u32[]{:S(2)}) collective-permute-start(bf16[4,2,72,384]{3,2,1,0:T(8,128)(2,1)S(1)} %get-tuple-element.125), channel_id=1, source_target_pairs={{0,8},{2,10},{4,12},{6,14},{8,0},{10,2},{12,4},{14,6},{16,24},{18,... | collective-permute-start | bytes 1327112 | tf_op jit(solution)/shard_map/ppermute | solution.py:701
  54.0 9.1 %collective-permute-start.23 = (bf16[4,72,384]{2,1,0:T(8,128)(2,1)S(1)}, bf16[4,72,384]{2,1,0:T(8,128)(2,1)S(1)}, u32[]{:S(2)}, u32[]{:S(2)}) collective-permute-start(bf16[4,72,384]{2,1,0:T(8,128)(2,1)S(1)} %get-tuple-element.143), channel_id=1, source_target_pairs={{0,4},{2,6},{4,0},{6,2},{8,12},{10,14},{12,8},{14,10},{16,20},{18,... | collective-permute-start | bytes 663560 | tf_op jit(solution)/shard_map/ppermute | solution.py:701
  55.0 7.1 %collective-permute-start.21 = (bf16[1,2,8,80,384]{4,3,2,1,0:T(8,128)(2,1)S(1)}, bf16[1,2,8,80,384]{4,3,2,1,0:T(8,128)(2,1)S(1)}, u32[]{:S(2)}, u32[]{:S(2)}) collective-permute-start(bf16[1,2,8,80,384]{4,3,2,1,0:T(8,128)(2,1)S(1)} %get-tuple-element.140), channel_id=1, source_target_pairs={{0,2},{2,0},{4,6},{6,4},{8,10},{10,8},{12,14},{14,12},{16,18},{18,... | collective-permute-start | bytes 2949128 | tf_op jit(solution)/shard_map/ppermute | solution.py:701
  59.3 7.3 %collective-permute-start.19 = (bf16[2,2,72,384]{3,2,1,0:T(8,128)(2,1)S(1)}, bf16[2,2,72,384]{3,2,1,0:T(8,128)(2,1)S(1)}, u32[]{:S(2)}, u32[]{:S(2)}) collective-permute-start(bf16[2,2,72,384]{3,2,1,0:T(8,128)(2,1)S(1)} %get-tuple-element.136), channel_id=1, source_target_pairs={{0,8},{2,10},{4,12},{6,14},{8,0},{10,2},{12,4},{14,6},{16,24},{18,... | collective-permute-start | bytes 663560 | tf_op jit(solution)/shard_map/ppermute | solution.py:701
  60.9 6.5 %collective-permute-start.20 = (bf16[2,2,72,384]{3,2,1,0:T(8,128)(2,1)S(1)}, bf16[2,2,72,384]{3,2,1,0:T(8,128)(2,1)S(1)}, u32[]{:S(2)}, u32[]{:S(2)}) collective-permute-start(bf16[2,2,72,384]{3,2,1,0:T(8,128)(2,1)S(1)} %get-tuple-element.138), channel_id=1, source_target_pairs={{0,4},{2,6},{4,0},{6,2},{8,12},{10,14},{12,8},{14,10},{16,20},{18,... | collective-permute-start | bytes 663560 | tf_op jit(solution)/shard_map/ppermute | solution.py:701
  62.4 11.0 %collective-permute-start.22 = (bf16[8,80,384]{2,1,0:T(8,128)(2,1)S(1)}, bf16[8,80,384]{2,1,0:T(8,128)(2,1)S(1)}, u32[]{:S(2)}, u32[]{:S(2)}) collective-permute-start(bf16[8,80,384]{2,1,0:T(8,128)(2,1)S(1)} %get-tuple-element.142), channel_id=1, source_target_pairs={{0,1},{1,0},{2,3},{3,2},{4,5},{5,4},{6,7},{7,6},{8,9},{9,8},{10,11... | collective-permute-start | bytes 1474568 | tf_op jit(solution)/shard_map/ppermute | solution.py:701
  63.1 4.9 %collective-permute-start.24 = (bf16[2,72,384]{2,1,0:T(8,128)(2,1)S(1)}, bf16[2,72,384]{2,1,0:T(8,128)(2,1)S(1)}, u32[]{:S(2)}, u32[]{:S(2)}) collective-permute-start(bf16[2,72,384]{2,1,0:T(8,128)(2,1)S(1)} %get-tuple-element.145), channel_id=1, source_target_pairs={{0,8},{2,10},{4,12},{6,14},{8,0},{10,2},{12,4},{14,6},{16,24},{18,... | collective-permute-start | bytes 331784 | tf_op jit(solution)/shard_map/ppermute | solution.py:701
  73.6 9.5 %collective-permute-start.27 = (bf16[4,80,384]{2,1,0:T(8,128)(2,1)S(1)}, bf16[4,80,384]{2,1,0:T(8,128)(2,1)S(1)}, u32[]{:S(2)}, u32[]{:S(2)}) collective-permute-start(bf16[4,80,384]{2,1,0:T(8,128)(2,1)S(1)} %get-tuple-element.152), channel_id=1, source_target_pairs={{0,4},{2,6},{4,0},{6,2},{8,12},{10,14},{12,8},{14,10},{16,20},{18,... | collective-permute-start | bytes 737288 | tf_op jit(solution)/shard_map/ppermute | solution.py:701
  75.1 8.0 %collective-permute-start.26 = (bf16[3,72,384]{2,1,0:T(8,128)(2,1)S(1)}, bf16[3,72,384]{2,1,0:T(8,128)(2,1)S(1)}, u32[]{:S(2)}, u32[]{:S(2)}) collective-permute-start(bf16[3,72,384]{2,1,0:T(8,128)(2,1)S(1)} %get-tuple-element.149), channel_id=1, source_target_pairs={{0,16},{2,18},{4,20},{6,22},{8,24},{10,26},{12,28},{14,30},{16,0},... | collective-permute-start | bytes 497672 | tf_op jit(solution)/shard_map/ppermute | solution.py:701
  77.7 4.7 %collective-permute-start.25 = (bf16[2,72,384]{2,1,0:T(8,128)(2,1)S(1)}, bf16[2,72,384]{2,1,0:T(8,128)(2,1)S(1)}, u32[]{:S(2)}, u32[]{:S(2)}) collective-permute-start(bf16[2,72,384]{2,1,0:T(8,128)(2,1)S(1)} %get-tuple-element.147), channel_id=1, source_target_pairs={{0,1},{1,0},{2,3},{3,2},{4,5},{5,4},{6,7},{7,6},{8,9},{9,8},{10,11... | collective-permute-start | bytes 331784 | tf_op jit(solution)/shard_map/ppermute | solution.py:701
  83.2 7.0 %collective-permute-start.30 = (bf16[2,80,384]{2,1,0:T(8,128)(2,1)S(1)}, bf16[2,80,384]{2,1,0:T(8,128)(2,1)S(1)}, u32[]{:S(2)}, u32[]{:S(2)}) collective-permute-start(bf16[2,80,384]{2,1,0:T(8,128)(2,1)S(1)} %get-tuple-element.157), channel_id=1, source_target_pairs={{0,8},{2,10},{4,12},{6,14},{8,0},{10,2},{12,4},{14,6},{16,24},{18,... | collective-permute-start | bytes 368648 | tf_op jit(solution)/shard_map/ppermute | solution.py:701
  83.3 6.9 %collective-permute-start.28 = (bf16[2,72,384]{2,1,0:T(8,128)(2,1)S(1)}, bf16[2,72,384]{2,1,0:T(8,128)(2,1)S(1)}, u32[]{:S(2)}, u32[]{:S(2)}) collective-permute-start(bf16[2,72,384]{2,1,0:T(8,128)(2,1)S(1)} %get-tuple-element.153.refs_0_), channel_id=1, source_target_pairs={{0,16},{2,18},{4,20},{6,22},{8,24},{10,26},{12,28},{14,30},{16,0},... | collective-permute-start | bytes 331784 | tf_op jit(solution)/shard_map/ppermute | solution.py:701
  86.1 4.2 %collective-permute-start.29 = (bf16[72,384]{1,0:T(8,128)(2,1)S(1)}, bf16[72,384]{1,0:T(8,128)(2,1)S(1)}, u32[]{:S(2)}, u32[]{:S(2)}) collective-permute-start(bf16[72,384]{1,0:T(8,128)(2,1)S(1)} %get-tuple-element.155), channel_id=1, source_target_pairs={{0,1},{1,0},{2,3},{3,2},{4,5},{5,4},{6,7},{7,6},{8,9},{9,8},{10,11... | collective-permute-start | bytes 165896 | tf_op jit(solution)/shard_map/ppermute | solution.py:701
  90.3 11.2 %collective-permute-start.31 = (bf16[3,80,384]{2,1,0:T(8,128)(2,1)S(1)}, bf16[3,80,384]{2,1,0:T(8,128)(2,1)S(1)}, u32[]{:S(2)}, u32[]{:S(2)}) collective-permute-start(bf16[3,80,384]{2,1,0:T(8,128)(2,1)S(1)} %get-tuple-element.158.refs_0_), channel_id=1, source_target_pairs={{0,16},{2,18},{4,20},{6,22},{8,24},{10,26},{12,28},{14,30},{16,0},... | collective-permute-start | bytes 552968 | tf_op jit(solution)/shard_map/ppermute | solution.py:701
  93.2 8.3 %collective-permute-start.32 = (bf16[2,72,384]{2,1,0:T(8,128)(2,1)S(1)}, bf16[2,72,384]{2,1,0:T(8,128)(2,1)S(1)}, u32[]{:S(2)}, u32[]{:S(2)}) collective-permute-start(bf16[2,72,384]{2,1,0:T(8,128)(2,1)S(1)} %get-tuple-element.160.refs_3_), channel_id=1, source_target_pairs={{0,8},{2,10},{4,12},{6,14},{8,0},{10,2},{12,4},{14,6},{16,24},{18,... | collective-permute-start | bytes 331784 | tf_op jit(solution)/shard_map/ppermute | solution.py:701
  101.5 8.7 %collective-permute-start.34 = (bf16[3,2,72,384]{3,2,1,0:T(8,128)(2,1)S(1)}, bf16[3,2,72,384]{3,2,1,0:T(8,128)(2,1)S(1)}, u32[]{:S(2)}, u32[]{:S(2)}) collective-permute-start(bf16[3,2,72,384]{3,2,1,0:T(8,128)(2,1)S(1)} %get-tuple-element.161.refs_3_.refs_0_), channel_id=1, source_target_pairs={{0,4},{2,6},{4,0},{6,2},{8,12},{10,14},{12,8},{14,10},{16,20},{18,... | collective-permute-start | bytes 995336 | tf_op jit(solution)/shard_map/ppermute | solution.py:701
  103.4 5.4 %collective-permute-start.33 = (bf16[80,384]{1,0:T(8,128)(2,1)S(1)}, bf16[80,384]{1,0:T(8,128)(2,1)S(1)}, u32[]{:S(2)}, u32[]{:S(2)}) collective-permute-start(bf16[80,384]{1,0:T(8,128)(2,1)S(1)} %get-tuple-element.163.refs_0_), channel_id=1, source_target_pairs={{0,16},{2,18},{4,20},{6,22},{8,24},{10,26},{12,28},{14,30},{16,0},... | collective-permute-start | bytes 184328 | tf_op jit(solution)/shard_map/ppermute | solution.py:701
  104.4 5.6 %collective-permute-start.35 = (bf16[2,72,384]{2,1,0:T(8,128)(2,1)S(1)}, bf16[2,72,384]{2,1,0:T(8,128)(2,1)S(1)}, u32[]{:S(2)}, u32[]{:S(2)}) collective-permute-start(bf16[2,72,384]{2,1,0:T(8,128)(2,1)S(1)} %get-tuple-element.164.refs_2_), channel_id=1, source_target_pairs={{0,8},{2,10},{4,12},{6,14},{8,0},{10,2},{12,4},{14,6},{16,24},{18,... | collective-permute-start | bytes 331784 | tf_op jit(solution)/shard_map/ppermute | solution.py:701
  110.4 9.2 %collective-permute-start.40 = (bf16[2,2,72,384]{3,2,1,0:T(8,128)(2,1)S(1)}, bf16[2,2,72,384]{3,2,1,0:T(8,128)(2,1)S(1)}, u32[]{:S(2)}, u32[]{:S(2)}) collective-permute-start(bf16[2,2,72,384]{3,2,1,0:T(8,128)(2,1)S(1)} %get-tuple-element.166.refs_2_), channel_id=1, source_target_pairs={{0,4},{2,6},{4,0},{6,2},{8,12},{10,14},{12,8},{14,10},{16,20},{18,... | collective-permute-start | bytes 663560 | tf_op jit(solution)/shard_map/ppermute | solution.py:701
  112.2 8.0 %collective-permute-start.39 = (bf16[2,2,72,384]{3,2,1,0:T(8,128)(2,1)S(1)}, bf16[2,2,72,384]{3,2,1,0:T(8,128)(2,1)S(1)}, u32[]{:S(2)}, u32[]{:S(2)}) collective-permute-start(bf16[2,2,72,384]{3,2,1,0:T(8,128)(2,1)S(1)} %get-tuple-element.165.refs_2_.refs_0_), channel_id=1, source_target_pairs={{0,8},{2,10},{4,12},{6,14},{8,0},{10,2},{12,4},{14,6},{16,24},{18,... | collective-permute-start | bytes 663560 | tf_op jit(solution)/shard_map/ppermute | solution.py:701
  112.7 2.3 %collective-permute-start.41 = (bf16[1,2,4,72,384]{4,3,2,1,0:T(8,128)(2,1)S(1)}, bf16[1,2,4,72,384]{4,3,2,1,0:T(8,128)(2,1)S(1)}, u32[]{:S(2)}, u32[]{:S(2)}) collective-permute-start(bf16[1,2,4,72,384]{4,3,2,1,0:T(8,128)(2,1)S(1)} %get-tuple-element.167.refs_0_), channel_id=1, source_target_pairs={{0,2},{2,0},{4,6},{6,4},{8,10},{10,8},{12,14},{14,12},{16,18},{18,... | collective-permute-start | bytes 1327112 | tf_op jit(solution)/shard_map/ppermute | solution.py:701
  112.7 13.9 %collective-permute-start.38 = (bf16[2,80,384]{2,1,0:T(8,128)(2,1)S(1)}, bf16[2,80,384]{2,1,0:T(8,128)(2,1)S(1)}, u32[]{:S(2)}, u32[]{:S(2)}) collective-permute-start(bf16[2,80,384]{2,1,0:T(8,128)(2,1)S(1)} %share_qkv_out_high.1.refs_5_.refs_0_), channel_id=1, source_target_pairs={{0,12},{2,14},{4,8},{6,10},{8,4},{10,6},{12,0},{14,2},{16,28},{18,... | collective-permute-start | bytes 368648 | tf_op jit(solution)/shard_map/ppermute | solution.py:701
  114.0 12.6 %collective-permute-start.37 = (bf16[2,80,384]{2,1,0:T(8,128)(2,1)S(1)}, bf16[2,80,384]{2,1,0:T(8,128)(2,1)S(1)}, u32[]{:S(2)}, u32[]{:S(2)}) collective-permute-start(bf16[2,80,384]{2,1,0:T(8,128)(2,1)S(1)} %share_qkv_out_high.1.refs_5_.refs_0_), channel_id=1, source_target_pairs={{0,8},{2,10},{4,12},{6,14},{8,0},{10,2},{12,4},{14,6},{16,24},{18,... | collective-permute-start | bytes 368648 | tf_op jit(solution)/shard_map/ppermute | solution.py:701
  114.9 11.7 %collective-permute-start.36 = (bf16[2,80,384]{2,1,0:T(8,128)(2,1)S(1)}, bf16[2,80,384]{2,1,0:T(8,128)(2,1)S(1)}, u32[]{:S(2)}, u32[]{:S(2)}) collective-permute-start(bf16[2,80,384]{2,1,0:T(8,128)(2,1)S(1)} %share_qkv_out_high.1.refs_5_.refs_0_), channel_id=1, source_target_pairs={{0,4},{2,6},{4,0},{6,2},{8,12},{10,14},{12,8},{14,10},{16,20},{18,... | collective-permute-start | bytes 368648 | tf_op jit(solution)/shard_map/ppermute | solution.py:701
  120.3 6.5 %collective-permute-start.43 = (bf16[2,2,4,72,384]{4,3,2,1,0:T(8,128)(2,1)S(1)}, bf16[2,2,4,72,384]{4,3,2,1,0:T(8,128)(2,1)S(1)}, u32[]{:S(2)}, u32[]{:S(2)}) collective-permute-start(bf16[2,2,4,72,384]{4,3,2,1,0:T(8,128)(2,1)S(1)} %share_gate_up.1.refs_0_), channel_id=1, source_target_pairs={{0,2},{2,0},{4,6},{6,4},{8,10},{10,8},{12,14},{14,12},{16,18},{18,... | collective-permute-start | bytes 2654216 | tf_op jit(solution)/shard_map/ppermute | solution.py:701
  126.7 3.9 %collective-permute-start.42 = (bf16[1,2,4,80,384]{4,3,2,1,0:T(8,128)(2,1)S(1)}, bf16[1,2,4,80,384]{4,3,2,1,0:T(8,128)(2,1)S(1)}, u32[]{:S(2)}, u32[]{:S(2)}) collective-permute-start(bf16[1,2,4,80,384]{4,3,2,1,0:T(8,128)(2,1)S(1)} %share_qkv_out.1.refs_7_.refs_0_), channel_id=1, source_target_pairs={{0,2},{2,0},{4,6},{6,4},{8,10},{10,8},{12,14},{14,12},{16,18},{18,... | collective-permute-start | bytes 1474568 | tf_op jit(solution)/shard_map/ppermute | solution.py:701
  (20 other events, 85.3 us)

commit v10 on v9

--- a/solution.py
+++ b/solution.py
@@ -31,6 +31,8 @@
 SCALE = float(HEAD) ** (-0.5)
 VMEM_LIMIT = 32 * 1024 * 1024
 PACK_LIMIT = 53 * 1024 * 1024
+STEP_LIMIT = 14 * 1024 * 1024
+UPDATE_LIMIT = 27 * 1024 * 1024
 HALF = 144
 CUT_ROWS = 72
 MARK = (8, 128)
@@ -262,7 +264,7 @@
     window = (shape, lambda i: (i[1] * 2 * HALF, 0))
     outs = [sds(shape, BF16)]
     return pack_kernel(
-        cast_out, idx, [down_t], [window], outs, "pack_down", after, VMEM_LIMIT
+        cast_out, idx, [down_t], [window], outs, "pack_down", after, STEP_LIMIT
     )[0]
 
 
@@ -571,7 +573,7 @@
         in_specs=[pl.BlockSpec(memory_space=pltpu.VMEM)] * len(arrays)
         + [pl.BlockSpec(memory_space=pl.ANY)] * len(after),
         out_specs=tuple([pl.BlockSpec(memory_space=pltpu.VMEM)] * len(outs)),
-        compiler_params=pltpu.CompilerParams(vmem_limit_bytes=VMEM_LIMIT),
+        compiler_params=pltpu.CompilerParams(vmem_limit_bytes=STEP_LIMIT),
         cost_estimate=busy_for(busy),
         name=name,
     )(*arrays, *after)
@@ -588,7 +590,7 @@
     keep_ref[...] = low
 
 
-def add_step(jobs, name, after):
+def add_step(jobs, name, after, busy=20):
     arrays, outs = [], []
     for keep, arrived, axis in jobs:
         arrays += [keep, arrived]
@@ -599,7 +601,7 @@
         for i, (_, _, axis) in enumerate(jobs):
             add_split(ins[2 * i], ins[2 * i + 1], axis, out_refs[2 * i], out_refs[2 * i + 1])
 
-    flat = step(body, arrays, outs, name, after)
+    flat = step(body, arrays, outs, name, after, busy)
     return [(flat[2 * i], flat[2 * i + 1]) for i in range(len(jobs))]
 
 
@@ -690,7 +692,7 @@
         + [pltpu.VMEM((total, starts[-1]), F32)]
         + [pltpu.SemaphoreType.DMA((len(shares) * chunks, 3 * count))],
         input_output_aliases={first_earlier + i: i for i in range(len(earlier))},
-        compiler_params=pltpu.CompilerParams(vmem_limit_bytes=VMEM_LIMIT),
+        compiler_params=pltpu.CompilerParams(vmem_limit_bytes=UPDATE_LIMIT),
         cost_estimate=busy_for(busy),
         name=name,
     )(idx, *[p for _, p in shares], *state, *gains, *earlier, *after)
@@ -872,21 +874,21 @@
             [(cut(keep_down, 2, 4), cut(arrived_down, 2, 4), 0)], "down_y", (grad_qkv_out[2],)
         )
         arrived_down = over_x(send)
+        ((send, keep_qkv_out),) = add_step(
+            [(grad_qkv_out[1][0], arrived_qkv_out[0], 0)], "qkv_out_core", (keep_down,), 0.1
+        )
+        arrived_qkv_out = over_y(send)
         (send_up, keep_up), (send_low, keep_low) = add_step(
             [
                 (cut(keep_up, 2, 2, 2), cut(arrived_up, 2, 2, 2), 1),
                 (cut(keep_low, 2, 2, 2), cut(arrived_low, 2, 2, 2), 1),
             ],
             "up_x_low_z",
-            (keep_down,),
+            (keep_qkv_out,),
         )
         arrived_up, arrived_low = over_z_low(send_up), over_x(send_low)
-        ((send, keep_qkv_out),) = add_step(
-            [(grad_qkv_out[1][0], arrived_qkv_out[0], 0)], "qkv_out_core", (keep_up,)
-        )
-        arrived_qkv_out = over_y(send)
         ((send, keep_down),) = add_step(
-            [(cut(keep_down, 2, 2), cut(arrived_down, 2, 2), 0)], "down_x", (keep_qkv_out,)
+            [(cut(keep_down, 2, 2), cut(arrived_down, 2, 2), 0)], "down_x", (keep_up,)
         )
         arrived_down = over_z_low(send)
 
@@ -970,43 +972,54 @@
 
         def share_high(ins, outs):
             pieces, arrived, keep_qkv_out, near_down, down_low = ins
-            for high in range(2):
-                outs[0][0, high], outs[0][1, high] = near_down[high], down_low[high]
-            outs[0][2, 0], outs[0][2, 1] = pieces[1, :CUT_ROWS], arrived[1, :CUT_ROWS]
-            outs[1][0], outs[1][1] = pieces[2, :CUT_ROWS], arrived[2, :CUT_ROWS]
-            outs[2][...] = (keep_qkv_out[...] + arrived[0].astype(F32)).astype(BF16)
-
-        near_x, near_low, piece_qkv_out = step(
+            outs[0][0], outs[0][1] = near_down[...], down_low[...]
+            for part in range(2):
+                outs[1 + part][0] = pieces[1 + part, :CUT_ROWS]
+                outs[1 + part][1] = arrived[1 + part, :CUT_ROWS]
+            outs[3][...] = (keep_qkv_out[...] + arrived[0].astype(F32)).astype(BF16)
+
+        near_down, near_up, near_low, piece_qkv_out = step(
             share_high,
             [pieces, arrived, keep_qkv_out, near_down, down_low],
-            [sds((3, 2, *piece), BF16), sds((2, *piece), BF16), sds(taller, BF16)],
+            [
+                *(sds((2, 2, *piece), BF16), sds((2, *piece), BF16), sds((2, *piece), BF16)),
+                sds(taller, BF16),
+            ],
             "share_high",
         )
-        arrived_x, low_low = over_x(near_x), over_z_low(near_low)
+        up_x, low_low = over_x(near_up), over_z_low(near_low)
         qkv_out_high = over_z_high(piece_qkv_out)
-        output = layer_output(middle, hidden, down_whole, (near_x,))
+        (near_down,) = step(pass_on, [near_down], [sds(near_down.shape, BF16)], "pass_down", (near_low,))
+        down_x = over_x(near_down)
+        output = layer_output(middle, hidden, down_whole, (near_down,))
 
         def share_next(ins, outs):
-            near_x, arrived_x, near_low, low_low = ins
-            outs[0][0], outs[0][1] = near_x[2], arrived_x[2]
-            outs[1][0], outs[1][1] = near_low[...], low_low[...]
-            for low in range(2):
-                for high in range(2):
-                    outs[2][0, 0, low * 2 + high] = near_x[low, high]
-                    outs[2][0, 1, low * 2 + high] = arrived_x[low, high]
-
-        near_up, near_low, near_down = step(
+            for i in range(2):
+                outs[i][0], outs[i][1] = ins[2 * i][...], ins[2 * i + 1][...]
+
+        near_up, near_low = step(
             share_next,
-            [near_x, arrived_x, near_low, low_low],
-            [
-                *(sds((2, 2, *piece), BF16), sds((2, 2, *piece), BF16)),
-                sds((1, 2, 4, *piece), BF16),
-            ],
+            [near_up, up_x, near_low, low_low],
+            [sds((2, 2, *piece), BF16), sds((2, 2, *piece), BF16)],
             "share_next",
-            (qkv_out_high,),
+            (output,),
+        )
+        up_low, low_x = over_z_low(near_up), over_x(near_low)
+
+        def share_down(ins, outs):
+            for x in range(2):
+                for low in range(2):
+                    for high in range(2):
+                        outs[0][0, x, low * 2 + high] = ins[x][low, high]
+
+        (near_down,) = step(
+            share_down,
+            [near_down, down_x],
+            [sds((1, 2, 4, *piece), BF16)],
+            "share_down",
+            (near_up,),
         )
         far_down = over_core(near_down)
-        up_low, low_x = over_z_low(near_up), over_x(near_low)
 
         def share_qkv_out_high(ins, outs):
             outs[0][0], outs[0][1] = ins[0][...], ins[1][...]
@@ -1016,10 +1029,26 @@
             [piece_qkv_out, qkv_out_high],
             [sds((2, *taller), BF16)],
             "share_qkv_out_high",
-            (near_up,),
+            (near_down,),
         )
         qkv_out_x, qkv_out_low = over_x(near_qkv_out), over_z_low(near_qkv_out)
         qkv_out_both = swap(near_qkv_out, "dp", 6)
+
+        def share_gate_up(ins, outs):
+            for near in range(2):
+                for far in range(2):
+                    for high in range(2):
+                        outs[0][0, near, far * 2 + high] = ins[far][near, high]
+                        outs[0][1, far, near * 2 + high] = ins[2 + far][near, high]
+
+        (near_gate_up,) = step(
+            share_gate_up,
+            [near_up, up_low, near_low, low_x],
+            [sds((2, 2, 4, *piece), BF16)],
+            "share_gate_up",
+            (near_qkv_out,),
+        )
+        far_gate_up = over_core(near_gate_up)
         one_down, two_down, next_down, mark = update_rows(
             idx,
             [(0, near_down), (1, far_down)],
@@ -1033,38 +1062,7 @@
             (),
             (),
             "update_down",
-            (near_qkv_out,),
-            0.1,
-        )
-
-        def share_gate_up(ins, outs):
-            for near in range(2):
-                for far in range(2):
-                    for high in range(2):
-                        outs[0][0, near, far * 2 + high] = ins[far][near, high]
-                        outs[0][1, far, near * 2 + high] = ins[2 + far][near, high]
-
-        (near_gate_up,) = step(
-            share_gate_up,
-            [near_up, up_low, near_low, low_x],
-            [sds((2, 2, 4, *piece), BF16)],
-            "share_gate_up",
-            (mark,),
-        )
-        far_gate_up = over_core(near_gate_up)
-        place_gate_up = lambda p, x, z: (p * CUT_ROWS, [(0, CUT_COLUMNS, (x * 4 + z) * CUT_COLUMNS)])
-        state_gate_up = [w_gate_up, first_gate_up, second_gate_up]
-        *near_state, mark = update_rows(
-            idx,
-            [(0, near_gate_up)],
-            place_gate_up,
-            HALF,
-            24,
-            state_gate_up,
-            (),
-            (),
-            "update_gate_up_near",
-            (),
+            (near_gate_up,),
         )
 
         def share_qkv_out(ins, outs):
@@ -1083,14 +1081,14 @@
         far_qkv_out = over_core(near_qkv_out)
         one_gate_up, two_gate_up, next_gate_up, mark = update_rows(
             idx,
-            [(1, far_gate_up)],
-            place_gate_up,
+            [(0, near_gate_up), (1, far_gate_up)],
+            lambda p, x, z: (p * CUT_ROWS, [(0, CUT_COLUMNS, (x * 4 + z) * CUT_COLUMNS)]),
             HALF,
             24,
-            state_gate_up,
-            near_state,
+            [w_gate_up, first_gate_up, second_gate_up],
             (),
-            "update_gate_up_far",
+            (),
+            "update_gate_up",
             (near_qkv_out,),
         )
         cuts = [[(0, 384, 0)], [(0, 384, 384)], [(0, 192, 768), (192, 192, 1024)], [(0, 384, 1216)]]

time: 136 us -> 136 us (level)
  starting transfers between devices: 48.3 us -> 51 us
  Pallas kernels: 36.7 us -> 34.7 us
    ppermute x44 -> x45, starting transfers between devices: 48.3 us -> 51 us  [swap(): return lax.ppermute(values, axis, [(i, i ^ mask) for i in range(size)])]
    pallas_call x4 -> x3, Pallas kernels: 14.7 us -> 12.7 us  [update_rows(): pl.pallas_call(kernel, out_shape=tuple((sds(a.shape, F32) for a in [*stat...]
    ppermute x44 -> x45, waiting for transfers between devices: 44.6 us -> 44.2 us  [swap(): return lax.ppermute(values, axis, [(i, i ^ mask) for i in range(size)])]
    unnamed x48 -> x50, local copies, waits for them, and re-layouts: 4.33 us -> 4.44 us
    pallas_call x17 -> x19, Pallas kernels: 3.34 us -> 3.3 us  [step(): pl.pallas_call(kernel, out_shape=tuple(outs), in_specs=[pl.BlockSpec(memo...]
  transfers between devices with their start and end apart: 44 -> 45, of which waited for: 20 -> 19; matrix products, arithmetic and copies ran while one was open for 0% -> 0% of each run, Pallas kernels for 22% -> 20%
where the time goes in v10:
time: 136 us
  starting transfers between devices  51 us (38%)
  waiting for transfers between devices  44.2 us (32%)
  Pallas kernels  34.7 us (26%)
  local copies, waits for them, and re-layouts  4.8 us (4%)
  between operations  1.4 us (1%)
    ppermute x45, starting transfers between devices, swap(): return lax.ppermute(values, axis, [(i, i ^ mask) for i in range(size)])  51 us
    ppermute x45, waiting for transfers between devices, swap(): return lax.ppermute(values, axis, [(i, i ^ mask) for i in range(size)])  44.2 us
    pallas_call x5, Pallas kernels, call(): pl.pallas_call(kernel, out_shape=tuple(outs), in_specs=[pl.BlockSpec(memo...  15.7 us
    pallas_call x3, Pallas kernels, update_rows(): pl.pallas_call(kernel, out_shape=tuple((sds(a.shape, F32) for a in [*stat...  12.7 us
    unnamed x50, local copies, waits for them, and re-layouts  4.44 us
    pallas_call x19, Pallas kernels, step(): pl.pallas_call(kernel, out_shape=tuple(outs), in_specs=[pl.BlockSpec(memo...  3.3 us
    pallas_call x2, Pallas kernels, pack_kernel(): pl.pallas_call(kernel, out_shape=tuple(outs), in_specs=[pl.BlockSpec(memo...  2.97 us
  transfers between devices with their start and end apart: 45, of which 19 were waited for; matrix products, arithmetic and copies ran while one was open for 0% of the time, Pallas kernels for 20%

profile of v10, /device:TPU:0, one launch (start us, length us, event | category | flops | bytes accessed | tf_op | source)
XLA Modules:
  0.0 136.3 jit_solution(5860745549151352281)
XLA Ops:
  1.4 2.2 %pack_first.1 = (bf16[160,768]{1,0:T(8,128)(2,1)S(1)}, bf16[144,768]{1,0:T(8,128)(2,1)S(1)}, bf16[144,768]{1,0:T(8,128)(2,1)S(1)}) custom-call(s32[4]{0:T(128)S(1)} %pad_add_fusion.idx_ref.refs_0_, f32[288,960]{1,0:T(8,128)} %refs_2_.7, f32[288,576]{1,0:T(8,128)} %refs_3_.6, f32[2,288]{1,0:T(2,128)S(1)} %copy-done.16, f32[288,3072]{1,0:T(8,128)} %refs_2_.6, ...), custom_call_target="tpu_custom_call" | custom-call | flops 10000000000 | tf_op jit(solution)/shard_map/pack_first/pallas_call | solution.py:242
  3.6 3.0 %collective-permute-start = (bf16[160,768]{1,0:T(8,128)(2,1)S(1)}, bf16[160,768]{1,0:T(8,128)(2,1)S(1)}, u32[]{:S(2)}, u32[]{:S(2)}) collective-permute-start(bf16[160,768]{1,0:T(8,128)(2,1)S(1)} %get-tuple-element.99), channel_id=1, source_target_pairs={{0,1},{1,0},{2,3},{3,2},{4,5},{5,4},{6,7},{7,6},{8,9},{9,8},{10,11... | collective-permute-start | bytes 737288 | tf_op jit(solution)/shard_map/ppermute | solution.py:703
  6.7 1.9 %collective-permute-start.4 = (bf16[144,768]{1,0:T(8,128)(2,1)S(1)}, bf16[144,768]{1,0:T(8,128)(2,1)S(1)}, u32[]{:S(2)}, u32[]{:S(2)}) collective-permute-start(bf16[144,768]{1,0:T(8,128)(2,1)S(1)} %get-tuple-element.103), channel_id=1, source_target_pairs={{0,1},{1,0},{2,3},{3,2},{4,5},{5,4},{6,7},{7,6},{8,9},{9,8},{10,11... | collective-permute-start | bytes 663560 | tf_op jit(solution)/shard_map/ppermute | solution.py:703
  8.7 9.5 %collective-permute-done.8.refs_11_.refs_1_ = bf16[144,768]{1,0:T(8,128)(2,1)S(1)} collective-permute-done((bf16[144,768]{1,0:T(8,128)(2,1)S(1)}, bf16[144,768]{1,0:T(8,128)(2,1)S(1)}, u32[]{:S(2)}, u32[]{:S(2)}) %collective-permute-start.8) | collective-permute-done | bytes 221216 | tf_op jit(solution)/shard_map/ppermute | solution.py:703
  18.2 2.1 %collective-permute-start.9 = (bf16[144,768]{1,0:T(8,128)(2,1)S(1)}, bf16[144,768]{1,0:T(8,128)(2,1)S(1)}, u32[]{:S(2)}, u32[]{:S(2)}) collective-permute-start(bf16[144,768]{1,0:T(8,128)(2,1)S(1)} %collective-permute-done.8.refs_11_.refs_1_), channel_id=1, source_target_pairs={{0,8},{2,10},{4,12},{6,14},{8,0},{10,2},{12,4},{14,6},{16,24},{18,... | collective-permute-start | bytes 663560 | tf_op jit(solution)/shard_map/ppermute | solution.py:703
  21.2 2.0 %collective-permute-start.12 = (bf16[288,768]{1,0:T(8,128)(2,1)S(1)}, bf16[288,768]{1,0:T(8,128)(2,1)S(1)}, u32[]{:S(2)}, u32[]{:S(2)}) collective-permute-start(bf16[288,768]{1,0:T(8,128)(2,1)S(1)} %pack_down.1), channel_id=1, source_target_pairs={{0,1},{1,0},{2,3},{3,2},{4,5},{5,4},{6,7},{7,6},{8,9},{9,8},{10,11... | collective-permute-start | bytes 1327112 | tf_op jit(solution)/shard_map/ppermute | solution.py:703
  23.2 1.5 %collective-permute-start.5 = (bf16[144,768]{1,0:T(8,128)(2,1)S(1)}, bf16[144,768]{1,0:T(8,128)(2,1)S(1)}, u32[]{:S(2)}, u32[]{:S(2)}) collective-permute-start(bf16[144,768]{1,0:T(8,128)(2,1)S(1)} %collective-permute-done.4.refs_7_), channel_id=1, source_target_pairs={{0,4},{2,6},{4,0},{6,2},{8,12},{10,14},{12,8},{14,10},{16,20},{18,... | collective-permute-start | bytes 663560 | tf_op jit(solution)/shard_map/ppermute | solution.py:703
  24.7 1.4 %collective-permute-done.9.refs_12_ = bf16[144,768]{1,0:T(8,128)(2,1)S(1)} collective-permute-done((bf16[144,768]{1,0:T(8,128)(2,1)S(1)}, bf16[144,768]{1,0:T(8,128)(2,1)S(1)}, u32[]{:S(2)}, u32[]{:S(2)}) %collective-permute-start.9) | collective-permute-done | bytes 221216 | tf_op jit(solution)/shard_map/ppermute | solution.py:703
  26.1 3.4 %collective-permute-done.1.refs_9_ = bf16[160,768]{1,0:T(8,128)(2,1)S(1)} collective-permute-done((bf16[160,768]{1,0:T(8,128)(2,1)S(1)}, bf16[160,768]{1,0:T(8,128)(2,1)S(1)}, u32[]{:S(2)}, u32[]{:S(2)}) %collective-permute-start.1) | collective-permute-done | bytes 245792 | tf_op jit(solution)/shard_map/ppermute | solution.py:703
  29.5 1.0 collective-permute-done.5.refs_8_
  31.2 2.5 %attention.1 = (bf16[128,960]{1,0:T(8,128)(2,1)S(1)}, bf16[128,576]{1,0:T(8,128)(2,1)S(1)}, f32[128,128]{1,0:T(8,128)S(1)}, f32[128,128]{1,0:T(8,128)S(1)}, f32[...) custom-call(s32[4]{0:T(128)S(1)} %pad_add_fusion.idx_ref.refs_0_, ...), custom_call_target="tpu_custom_call" | custom-call | flops 1000000000 | tf_op jit(solution)/shard_map/attention/pallas_call | solution.py:152
  34.3 2.8 %feed_forward.1 = (f32[128,576]{1,0:T(8,128)S(1)}, bf16[128,576]{1,0:T(8,128)(2,1)S(1)}, f32[128,3072]{1,0:T(8,128)S(1)}, bf16[128,1536]{1,0:T(8,128)(2,1)S(1)},...) custom-call(s32[4]{0:T(128)S(1)} %pad_add_fusion.idx_ref.refs_0_, ...), custom_call_target="tpu_custom_call" | custom-call | flops 5000000000 | tf_op jit(solution)/shard_map/feed_forward/pallas_call | solution.py:152
  37.4 2.6 %feed_back.1 = (bf16[128,3072]{1,0:T(8,128)(2,1)S(1)}, bf16[2,2,8,72,384]{4,3,2,1,0:T(8,128)(2,1)S(1)}, bf16[2,2,8,72,384]{4,3,2,1,0:T(8,128)(2,1)S(1)}, bf16[576,1536]{1,0:T(8,128)(2,1)S(1)}) custom-call(s32[4]{0:T(128)S(1)} %pad_add_fusion.idx_ref.refs_0_, f32[128,3072]{1,0:T(8,128)S(1)} %get-tuple-element.107.refs_1_, ...), custom_call_target="tpu_custom_call" | custom-call | flops 20000000000 | tf_op jit(solution)/shard_map/feed_back/pallas_call | solution.py:152
  40.8 1.6 %collective-permute-start.19 = (bf16[8,72,384]{2,1,0:T(8,128)(2,1)S(1)}, bf16[8,72,384]{2,1,0:T(8,128)(2,1)S(1)}, u32[]{:S(2)}, u32[]{:S(2)}) collective-permute-start(bf16[8,72,384]{2,1,0:T(8,128)(2,1)S(1)} %get-tuple-element.130), channel_id=1, source_target_pairs={{0,1},{1,0},{2,3},{3,2},{4,5},{5,4},{6,7},{7,6},{8,9},{9,8},{10,11... | collective-permute-start | bytes 1327112 | tf_op jit(solution)/shard_map/ppermute | solution.py:703
  42.4 2.7 %middle_back.1 = (f32[128,576]{1,0:T(8,128)S(1)}, bf16[128,576]{1,0:T(8,128)(2,1)S(1)}, f32[1,576]{1,0:T(1,128)S(1)}) custom-call(s32[4]{0:T(128)S(1)} %pad_add_fusion.idx_ref.refs_0_, bf16[576,128]{1,0:T(8,128)(2,1)S(1)} %bitcast.64, f32[128,576]{1,0:T(8,128)S(1)} %get-tuple-element.105.refs_2_.refs_0_, ...), custom_call_target="tpu_custom_call" | custom-call | flops 20000000000 | tf_op jit(solution)/shard_map/middle_back/pallas_call | solution.py:152
  45.8 1.6 %collective-permute-start.16 = (bf16[2,4,72,384]{3,2,1,0:T(8,128)(2,1)S(1)}, bf16[2,4,72,384]{3,2,1,0:T(8,128)(2,1)S(1)}, u32[]{:S(2)}, u32[]{:S(2)}) collective-permute-start(bf16[2,4,72,384]{3,2,1,0:T(8,128)(2,1)S(1)} %get-tuple-element.119), channel_id=1, source_target_pairs={{0,4},{2,6},{4,0},{6,2},{8,12},{10,14},{12,8},{14,10},{16,20},{18,... | collective-permute-start | bytes 1327112 | tf_op jit(solution)/shard_map/ppermute | solution.py:703
  47.3 1.6 %collective-permute-start.17 = (bf16[4,2,72,384]{3,2,1,0:T(8,128)(2,1)S(1)}, bf16[4,2,72,384]{3,2,1,0:T(8,128)(2,1)S(1)}, u32[]{:S(2)}, u32[]{:S(2)}) collective-permute-start(bf16[4,2,72,384]{3,2,1,0:T(8,128)(2,1)S(1)} %get-tuple-element.121), channel_id=1, source_target_pairs={{0,8},{2,10},{4,12},{6,14},{8,0},{10,2},{12,4},{14,6},{16,24},{18,... | collective-permute-start | bytes 1327112 | tf_op jit(solution)/shard_map/ppermute | solution.py:703
  48.9 5.1 %attention_back.1 = (bf16[576,128]{1,0:T(8,128)(2,1)}, bf16[1,2,8,80,384]{4,3,2,1,0:T(8,128)(2,1)S(1)}, bf16[1,2,8,80,384]{4,3,2,1,0:T(8,128)(2,1)S(1)}, f32[8,128]{1,0:T(8,128)S(1)}) custom-call(s32[4]{0:T(128)S(1)} %pad_add_fusion.idx_ref.refs_0_, bf16[576,128]{1,0:T(8,128)(2,1)S(1)} %bitcast.67, f32[128,576]{1,0:T(8,128)S(1)} %get-tuple-element.117.refs_4_.refs_2_, ...), custom_call_target="tpu_custom_call" | custom-call | flops 20000000000 | tf_op jit(solution)/shard_map/attention_back/pallas_call | solution.py:152
  55.0 1.6 %collective-permute-done.18 = bf16[1,2,8,80,384]{4,3,2,1,0:T(8,128)(2,1)S(1)} collective-permute-done((bf16[1,2,8,80,384]{4,3,2,1,0:T(8,128)(2,1)S(1)}, bf16[1,2,8,80,384]{4,3,2,1,0:T(8,128)(2,1)S(1)}, u32[]{:S(2)}, u32[]{:S(2)}) %collective-permute-start.18) | collective-permute-done | bytes 983072 | tf_op jit(solution)/shard_map/ppermute | solution.py:703
  56.7 1.9 %collective-permute-done.16 = bf16[2,4,72,384]{3,2,1,0:T(8,128)(2,1)S(1)} collective-permute-done((bf16[2,4,72,384]{3,2,1,0:T(8,128)(2,1)S(1)}, bf16[2,4,72,384]{3,2,1,0:T(8,128)(2,1)S(1)}, u32[]{:S(2)}, u32[]{:S(2)}) %collective-permute-start.16) | collective-permute-done | bytes 442400 | tf_op jit(solution)/shard_map/ppermute | solution.py:703
  59.4 1.6 %collective-permute-start.20 = (bf16[2,2,72,384]{3,2,1,0:T(8,128)(2,1)S(1)}, bf16[2,2,72,384]{3,2,1,0:T(8,128)(2,1)S(1)}, u32[]{:S(2)}, u32[]{:S(2)}) collective-permute-start(bf16[2,2,72,384]{3,2,1,0:T(8,128)(2,1)S(1)} %get-tuple-element.135), channel_id=1, source_target_pairs={{0,8},{2,10},{4,12},{6,14},{8,0},{10,2},{12,4},{14,6},{16,24},{18,... | collective-permute-start | bytes 663560 | tf_op jit(solution)/shard_map/ppermute | solution.py:703
  61.0 1.2 collective-permute-start.21
  63.2 2.1 %collective-permute-start.24 = (bf16[2,72,384]{2,1,0:T(8,128)(2,1)S(1)}, bf16[2,72,384]{2,1,0:T(8,128)(2,1)S(1)}, u32[]{:S(2)}, u32[]{:S(2)}) collective-permute-start(bf16[2,72,384]{2,1,0:T(8,128)(2,1)S(1)} %get-tuple-element.141), channel_id=1, source_target_pairs={{0,8},{2,10},{4,12},{6,14},{8,0},{10,2},{12,4},{14,6},{16,24},{18,... | collective-permute-start | bytes 331784 | tf_op jit(solution)/shard_map/ppermute | solution.py:703
  65.3 2.8 %collective-permute-done.24.refs_7_ = bf16[2,72,384]{2,1,0:T(8,128)(2,1)S(1)} collective-permute-done((bf16[2,72,384]{2,1,0:T(8,128)(2,1)S(1)}, bf16[2,72,384]{2,1,0:T(8,128)(2,1)S(1)}, u32[]{:S(2)}, u32[]{:S(2)}) %collective-permute-start.24) | collective-permute-done | bytes 110624 | tf_op jit(solution)/shard_map/ppermute | solution.py:703
  68.1 5.0 %collective-permute-done.22 = bf16[8,80,384]{2,1,0:T(8,128)(2,1)S(1)} collective-permute-done((bf16[8,80,384]{2,1,0:T(8,128)(2,1)S(1)}, bf16[8,80,384]{2,1,0:T(8,128)(2,1)S(1)}, u32[]{:S(2)}, u32[]{:S(2)}) %collective-permute-start.22) | collective-permute-done | bytes 491552 | tf_op jit(solution)/shard_map/ppermute | solution.py:703
  73.3 1.5 %collective-permute-start.27 = (bf16[4,80,384]{2,1,0:T(8,128)(2,1)S(1)}, bf16[4,80,384]{2,1,0:T(8,128)(2,1)S(1)}, u32[]{:S(2)}, u32[]{:S(2)}) collective-permute-start(bf16[4,80,384]{2,1,0:T(8,128)(2,1)S(1)} %get-tuple-element.148), channel_id=1, source_target_pairs={{0,4},{2,6},{4,0},{6,2},{8,12},{10,14},{12,8},{14,10},{16,20},{18,... | collective-permute-start | bytes 737288 | tf_op jit(solution)/shard_map/ppermute | solution.py:703
  74.8 2.6 %collective-permute-start.26 = (bf16[3,72,384]{2,1,0:T(8,128)(2,1)S(1)}, bf16[3,72,384]{2,1,0:T(8,128)(2,1)S(1)}, u32[]{:S(2)}, u32[]{:S(2)}) collective-permute-start(bf16[3,72,384]{2,1,0:T(8,128)(2,1)S(1)} %get-tuple-element.145), channel_id=1, source_target_pairs={{0,16},{2,18},{4,20},{6,22},{8,24},{10,26},{12,28},{14,30},{16,0},... | collective-permute-start | bytes 497672 | tf_op jit(solution)/shard_map/ppermute | solution.py:703
  77.9 4.3 %collective-permute-done.25.refs_1_ = bf16[2,72,384]{2,1,0:T(8,128)(2,1)S(1)} collective-permute-done((bf16[2,72,384]{2,1,0:T(8,128)(2,1)S(1)}, bf16[2,72,384]{2,1,0:T(8,128)(2,1)S(1)}, u32[]{:S(2)}, u32[]{:S(2)}) %collective-permute-start.25) | collective-permute-done | bytes 110624 | tf_op jit(solution)/shard_map/ppermute | solution.py:703
  83.0 2.8 %collective-permute-start.28 = (bf16[2,72,384]{2,1,0:T(8,128)(2,1)S(1)}, bf16[2,72,384]{2,1,0:T(8,128)(2,1)S(1)}, u32[]{:S(2)}, u32[]{:S(2)}) collective-permute-start(bf16[2,72,384]{2,1,0:T(8,128)(2,1)S(1)} %get-tuple-element.149.refs_0_), channel_id=1, source_target_pairs={{0,16},{2,18},{4,20},{6,22},{8,24},{10,26},{12,28},{14,30},{16,0},... | collective-permute-start | bytes 331784 | tf_op jit(solution)/shard_map/ppermute | solution.py:703
  86.3 3.6 %collective-permute-done.29.refs_3_ = bf16[72,384]{1,0:T(8,128)(2,1)S(1)} collective-permute-done((bf16[72,384]{1,0:T(8,128)(2,1)S(1)}, bf16[72,384]{1,0:T(8,128)(2,1)S(1)}, u32[]{:S(2)}, u32[]{:S(2)}) %collective-permute-start.29) | collective-permute-done | bytes 55328 | tf_op jit(solution)/shard_map/ppermute | solution.py:703
  90.0 2.8 %collective-permute-start.31 = (bf16[3,80,384]{2,1,0:T(8,128)(2,1)S(1)}, bf16[3,80,384]{2,1,0:T(8,128)(2,1)S(1)}, u32[]{:S(2)}, u32[]{:S(2)}) collective-permute-start(bf16[3,80,384]{2,1,0:T(8,128)(2,1)S(1)} %get-tuple-element.154.refs_0_), channel_id=1, source_target_pairs={{0,16},{2,18},{4,20},{6,22},{8,24},{10,26},{12,28},{14,30},{16,0},... | collective-permute-start | bytes 552968 | tf_op jit(solution)/shard_map/ppermute | solution.py:703
  92.9 3.8 %collective-permute-start.32 = (bf16[2,72,384]{2,1,0:T(8,128)(2,1)S(1)}, bf16[2,72,384]{2,1,0:T(8,128)(2,1)S(1)}, u32[]{:S(2)}, u32[]{:S(2)}) collective-permute-start(bf16[2,72,384]{2,1,0:T(8,128)(2,1)S(1)} %get-tuple-element.156.refs_3_), channel_id=1, source_target_pairs={{0,8},{2,10},{4,12},{6,14},{8,0},{10,2},{12,4},{14,6},{16,24},{18,... | collective-permute-start | bytes 331784 | tf_op jit(solution)/shard_map/ppermute | solution.py:703
  96.6 3.4 %collective-permute-done.32.refs_4_ = bf16[2,72,384]{2,1,0:T(8,128)(2,1)S(1)} collective-permute-done((bf16[2,72,384]{2,1,0:T(8,128)(2,1)S(1)}, bf16[2,72,384]{2,1,0:T(8,128)(2,1)S(1)}, u32[]{:S(2)}, u32[]{:S(2)}) %collective-permute-start.32) | collective-permute-done | bytes 110624 | tf_op jit(solution)/shard_map/ppermute | solution.py:703
  100.1 2.0 %collective-permute-start.36 = (bf16[2,72,384]{2,1,0:T(8,128)(2,1)S(1)}, bf16[2,72,384]{2,1,0:T(8,128)(2,1)S(1)}, u32[]{:S(2)}, u32[]{:S(2)}) collective-permute-start(bf16[2,72,384]{2,1,0:T(8,128)(2,1)S(1)} %get-tuple-element.158.refs_1_.refs_2_), channel_id=1, source_target_pairs={{0,8},{2,10},{4,12},{6,14},{8,0},{10,2},{12,4},{14,6},{16,24},{18,... | collective-permute-start | bytes 331784 | tf_op jit(solution)/shard_map/ppermute | solution.py:703
  102.1 3.2 %collective-permute-start.33 = (bf16[80,384]{1,0:T(8,128)(2,1)S(1)}, bf16[80,384]{1,0:T(8,128)(2,1)S(1)}, u32[]{:S(2)}, u32[]{:S(2)}) collective-permute-start(bf16[80,384]{1,0:T(8,128)(2,1)S(1)} %get-tuple-element.160.refs_0_), channel_id=1, source_target_pairs={{0,16},{2,18},{4,20},{6,22},{8,24},{10,26},{12,28},{14,30},{16,0},... | collective-permute-start | bytes 184328 | tf_op jit(solution)/shard_map/ppermute | solution.py:703
  105.8 1.6 %collective-permute-start.34 = (bf16[2,2,72,384]{3,2,1,0:T(8,128)(2,1)S(1)}, bf16[2,2,72,384]{3,2,1,0:T(8,128)(2,1)S(1)}, u32[]{:S(2)}, u32[]{:S(2)}) collective-permute-start(bf16[2,2,72,384]{3,2,1,0:T(8,128)(2,1)S(1)} %pass_down.1.refs_3_.refs_0_), channel_id=1, source_target_pairs={{0,4},{2,6},{4,0},{6,2},{8,12},{10,14},{12,8},{14,10},{16,20},{18,... | collective-permute-start | bytes 663560 | tf_op jit(solution)/shard_map/ppermute | solution.py:703
  107.4 1.5 %layer_output.1.refs_4_ = bf16[576,128]{1,0:T(8,128)(2,1)} custom-call(f32[128,576]{1,0:T(8,128)S(1)} %copy-done.24, bf16[128,1536]{1,0:T(8,128)(2,1)S(1)} %get-tuple-element.106.refs_1_, bf16[576,1536]{1,0:T(8,128)(2,1)S(1)} %get-tuple-element.109.refs_2_, bf16[2,2,72,384]{3,2,1,0:T(8,128)(2,1)S(1)} %pass_down.1.refs_3_.refs_0_), custom_call_target="tpu_custom_call" | custom-call | flops 2000000000 | tf_op jit(solution)/shard_map/layer_output/pallas_call | solution.py:570
  108.8 2.6 %collective-permute-done.35.refs_1_ = bf16[2,72,384]{2,1,0:T(8,128)(2,1)S(1)} collective-permute-done((bf16[2,72,384]{2,1,0:T(8,128)(2,1)S(1)}, bf16[2,72,384]{2,1,0:T(8,128)(2,1)S(1)}, u32[]{:S(2)}, u32[]{:S(2)}) %collective-permute-start.35) | collective-permute-done | bytes 110624 | tf_op jit(solution)/shard_map/ppermute | solution.py:703
  111.4 0.9 copy-done.21
  112.3 1.2 collective-permute-start.42
  114.5 1.6 %collective-permute-start.39 = (bf16[2,80,384]{2,1,0:T(8,128)(2,1)S(1)}, bf16[2,80,384]{2,1,0:T(8,128)(2,1)S(1)}, u32[]{:S(2)}, u32[]{:S(2)}) collective-permute-start(bf16[2,80,384]{2,1,0:T(8,128)(2,1)S(1)} %share_qkv_out_high.1.refs_4_.refs_0_), channel_id=1, source_target_pairs={{0,12},{2,14},{4,8},{6,10},{8,4},{10,6},{12,0},{14,2},{16,28},{18,... | collective-permute-start | bytes 368648 | tf_op jit(solution)/shard_map/ppermute | solution.py:703
  116.1 1.2 collective-permute-start.38
  118.3 1.1 collective-permute-done.41.refs_1_
  120.1 3.3 %update_down.1 = (f32[576,768]{1,0:T(8,128)}, f32[576,768]{1,0:T(8,128)}, f32[576,768]{1,0:T(8,128)}, f32[8,128]{1,0:T(8,128)S(1)}) custom-call(s32[4]{0:T(128)S(1)} %pad_add_fusion.idx_ref.refs_0_, bf16[1,2,4,72,384]{4,3,2,1,0:T(8,128)(2,1)S(1)} %share_down.1.refs_2_.refs_0_, bf16[1,2,4,72,384]{4,3,2,1,0:T(8,128)(2,1)S(1)} %collective-permute-done.40.refs_1_, ...), custom_call_target="tpu_custom_call" | custom-call | flops 20000000000 | tf_op jit(solution)/shard_map/update_down/pallas_call | solution.py:684
  123.9 1.6 %copy-done.1 = f32[288,3072]{1,0:T(8,128)S(1)} copy-done((f32[288,3072]{1,0:T(8,128)S(1)}, f32[288,3072]{1,0:T(8,128)}, u32[]{:S(2)}) %copy-start.1) | copy-done | bytes 3538968
  125.5 1.1 copy-done.2
  126.6 5.1 %update_gate_up.1 = (f32[288,3072]{1,0:T(8,128)}, f32[288,3072]{1,0:T(8,128)}, f32[288,3072]{1,0:T(8,128)}, f32[8,128]{1,0:T(8,128)S(1)}) custom-call(s32[4]{0:T(128)S(1)} %pad_add_fusion.idx_ref.refs_0_, bf16[2,2,4,72,384]{4,3,2,1,0:T(8,128)(2,1)S(1)} %share_gate_up.1.refs_5_.refs_0_, bf16[2,2,4,72,384]{4,3,2,1,0:T(8,128)(2,1)S(1)} %collective-permute-done.44.refs_1_, ...), custom_call_target="tpu_custom_call" | custom-call | flops 20000000000 | tf_op jit(solution)/shard_map/update_gate_up/pallas_call | solution.py:684
  131.8 4.3 %update_qkv_out.1 = (f32[288,960]{1,0:T(8,128)}, f32[288,576]{1,0:T(8,128)}, f32[288,960]{1,0:T(8,128)}, f32[288,576]{1,0:T(8,128)}, f32[288,960]{1,0:T(8,128)},...) custom-call(s32[4]{0:T(128)S(1)} %pad_add_fusion.idx_ref.refs_0_, ...), custom_call_target="tpu_custom_call" | custom-call | flops 20000000000 | tf_op jit(solution)/shard_map/update_qkv_out/pallas_call | solution.py:684
  (124 shorter events, 13.1 us)
Async XLA Ops:
  1.4 19.0 %copy-start.3 = (f32[768,576]{0,1:T(8,128)S(1)}, f32[768,576]{0,1:T(8,128)}, u32[]{:S(2)}) copy-start(f32[768,576]{0,1:T(8,128)} %param.25) | copy-start | bytes 5308420
  3.6 16.7 %collective-permute-start = (bf16[160,768]{1,0:T(8,128)(2,1)S(1)}, bf16[160,768]{1,0:T(8,128)(2,1)S(1)}, u32[]{:S(2)}, u32[]{:S(2)}) collective-permute-start(bf16[160,768]{1,0:T(8,128)(2,1)S(1)} %get-tuple-element.99), channel_id=1, source_target_pairs={{0,1},{1,0},{2,3},{3,2},{4,5},{5,4},{6,7},{7,6},{8,9},{9,8},{10,11... | collective-permute-start | bytes 737288 | tf_op jit(solution)/shard_map/ppermute | solution.py:703
  6.7 11.5 %collective-permute-start.8 = (bf16[144,768]{1,0:T(8,128)(2,1)S(1)}, bf16[144,768]{1,0:T(8,128)(2,1)S(1)}, u32[]{:S(2)}, u32[]{:S(2)}) collective-permute-start(bf16[144,768]{1,0:T(8,128)(2,1)S(1)} %get-tuple-element.104), channel_id=1, source_target_pairs={{0,1},{1,0},{2,3},{3,2},{4,5},{5,4},{6,7},{7,6},{8,9},{9,8},{10,11... | collective-permute-start | bytes 663560 | tf_op jit(solution)/shard_map/ppermute | solution.py:703
  6.7 16.5 %collective-permute-start.4 = (bf16[144,768]{1,0:T(8,128)(2,1)S(1)}, bf16[144,768]{1,0:T(8,128)(2,1)S(1)}, u32[]{:S(2)}, u32[]{:S(2)}) collective-permute-start(bf16[144,768]{1,0:T(8,128)(2,1)S(1)} %get-tuple-element.103), channel_id=1, source_target_pairs={{0,1},{1,0},{2,3},{3,2},{4,5},{5,4},{6,7},{7,6},{8,9},{9,8},{10,11... | collective-permute-start | bytes 663560 | tf_op jit(solution)/shard_map/ppermute | solution.py:703
  18.2 7.9 %collective-permute-start.9 = (bf16[144,768]{1,0:T(8,128)(2,1)S(1)}, bf16[144,768]{1,0:T(8,128)(2,1)S(1)}, u32[]{:S(2)}, u32[]{:S(2)}) collective-permute-start(bf16[144,768]{1,0:T(8,128)(2,1)S(1)} %collective-permute-done.8.refs_11_.refs_1_), channel_id=1, source_target_pairs={{0,8},{2,10},{4,12},{6,14},{8,0},{10,2},{12,4},{14,6},{16,24},{18,... | collective-permute-start | bytes 663560 | tf_op jit(solution)/shard_map/ppermute | solution.py:703
  20.3 10.2 %collective-permute-start.2 = (bf16[160,768]{1,0:T(8,128)(2,1)S(1)}, bf16[160,768]{1,0:T(8,128)(2,1)S(1)}, u32[]{:S(2)}, u32[]{:S(2)}) collective-permute-start(bf16[160,768]{1,0:T(8,128)(2,1)S(1)} %collective-permute-done.refs_5_.refs_8_), channel_id=1, source_target_pairs={{0,2},{2,0},{4,6},{6,4},{8,10},{10,8},{12,14},{14,12},{16,18},{18,... | collective-permute-start | bytes 737288 | tf_op jit(solution)/shard_map/ppermute | solution.py:703
  20.3 9.2 %collective-permute-start.1 = (bf16[160,768]{1,0:T(8,128)(2,1)S(1)}, bf16[160,768]{1,0:T(8,128)(2,1)S(1)}, u32[]{:S(2)}, u32[]{:S(2)}) collective-permute-start(bf16[160,768]{1,0:T(8,128)(2,1)S(1)} %collective-permute-done.refs_5_.refs_8_), channel_id=1, source_target_pairs={{0,8},{2,10},{4,12},{6,14},{8,0},{10,2},{12,4},{14,6},{16,24},{18,... | collective-permute-start | bytes 737288 | tf_op jit(solution)/shard_map/ppermute | solution.py:703
  21.2 9.9 %copy-start.6 = (f32[288,960]{1,0:T(8,128)S(1)}, f32[288,960]{1,0:T(8,128)}, u32[]{:S(2)}) copy-start(f32[288,960]{1,0:T(8,128)} %refs_2_.7) | copy-start | bytes 3317764
  21.2 9.9 %copy-start.10 = (f32[288,576]{1,0:T(8,128)S(1)}, f32[288,576]{1,0:T(8,128)}, u32[]{:S(2)}) copy-start(f32[288,576]{1,0:T(8,128)} %refs_3_.6) | copy-start | bytes 1990660
  21.2 12.6 %collective-permute-start.12 = (bf16[288,768]{1,0:T(8,128)(2,1)S(1)}, bf16[288,768]{1,0:T(8,128)(2,1)S(1)}, u32[]{:S(2)}, u32[]{:S(2)}) collective-permute-start(bf16[288,768]{1,0:T(8,128)(2,1)S(1)} %pack_down.1), channel_id=1, source_target_pairs={{0,1},{1,0},{2,3},{3,2},{4,5},{5,4},{6,7},{7,6},{8,9},{9,8},{10,11... | collective-permute-start | bytes 1327112 | tf_op jit(solution)/shard_map/ppermute | solution.py:703
  23.2 7.3 %collective-permute-start.5 = (bf16[144,768]{1,0:T(8,128)(2,1)S(1)}, bf16[144,768]{1,0:T(8,128)(2,1)S(1)}, u32[]{:S(2)}, u32[]{:S(2)}) collective-permute-start(bf16[144,768]{1,0:T(8,128)(2,1)S(1)} %collective-permute-done.4.refs_7_), channel_id=1, source_target_pairs={{0,4},{2,6},{4,0},{6,2},{8,12},{10,14},{12,8},{14,10},{16,20},{18,... | collective-permute-start | bytes 663560 | tf_op jit(solution)/shard_map/ppermute | solution.py:703
  26.1 4.9 %collective-permute-start.11 = (bf16[144,768]{1,0:T(8,128)(2,1)S(1)}, bf16[144,768]{1,0:T(8,128)(2,1)S(1)}, u32[]{:S(2)}, u32[]{:S(2)}) collective-permute-start(bf16[144,768]{1,0:T(8,128)(2,1)S(1)} %collective-permute-done.9.refs_12_), channel_id=1, source_target_pairs={{0,2},{2,0},{4,6},{6,4},{8,10},{10,8},{12,14},{14,12},{16,18},{18,... | collective-permute-start | bytes 663560 | tf_op jit(solution)/shard_map/ppermute | solution.py:703
  29.5 1.6 %collective-permute-start.3 = (bf16[160,768]{1,0:T(8,128)(2,1)S(1)}, bf16[160,768]{1,0:T(8,128)(2,1)S(1)}, u32[]{:S(2)}, u32[]{:S(2)}) collective-permute-start(bf16[160,768]{1,0:T(8,128)(2,1)S(1)} %collective-permute-done.1.refs_9_), channel_id=1, source_target_pairs={{0,2},{2,0},{4,6},{6,4},{8,10},{10,8},{12,14},{14,12},{16,18},{18,... | collective-permute-start | bytes 737288 | tf_op jit(solution)/shard_map/ppermute | solution.py:703
  30.5 3.8 %collective-permute-start.6 = (bf16[144,768]{1,0:T(8,128)(2,1)S(1)}, bf16[144,768]{1,0:T(8,128)(2,1)S(1)}, u32[]{:S(2)}, u32[]{:S(2)}) collective-permute-start(bf16[144,768]{1,0:T(8,128)(2,1)S(1)} %collective-permute-done.4.refs_7_), channel_id=1, source_target_pairs={{0,2},{2,0},{4,6},{6,4},{8,10},{10,8},{12,14},{14,12},{16,18},{18,... | collective-permute-start | bytes 663560 | tf_op jit(solution)/shard_map/ppermute | solution.py:703
  30.5 3.8 %collective-permute-start.10 = (bf16[144,768]{1,0:T(8,128)(2,1)S(1)}, bf16[144,768]{1,0:T(8,128)(2,1)S(1)}, u32[]{:S(2)}, u32[]{:S(2)}) collective-permute-start(bf16[144,768]{1,0:T(8,128)(2,1)S(1)} %collective-permute-done.8.refs_11_.refs_1_), channel_id=1, source_target_pairs={{0,2},{2,0},{4,6},{6,4},{8,10},{10,8},{12,14},{14,12},{16,18},{18,... | collective-permute-start | bytes 663560 | tf_op jit(solution)/shard_map/ppermute | solution.py:703
  31.0 3.3 %collective-permute-start.7 = (bf16[144,768]{1,0:T(8,128)(2,1)S(1)}, bf16[144,768]{1,0:T(8,128)(2,1)S(1)}, u32[]{:S(2)}, u32[]{:S(2)}) collective-permute-start(bf16[144,768]{1,0:T(8,128)(2,1)S(1)} %collective-permute-done.5.refs_8_), channel_id=1, source_target_pairs={{0,2},{2,0},{4,6},{6,4},{8,10},{10,8},{12,14},{14,12},{16,18},{18,... | collective-permute-start | bytes 663560 | tf_op jit(solution)/shard_map/ppermute | solution.py:703
  33.8 3.5 %collective-permute-start.13 = (bf16[288,768]{1,0:T(8,128)(2,1)S(1)}, bf16[288,768]{1,0:T(8,128)(2,1)S(1)}, u32[]{:S(2)}, u32[]{:S(2)}) collective-permute-start(bf16[288,768]{1,0:T(8,128)(2,1)S(1)} %pass_on.1.refs_5_), channel_id=1, source_target_pairs={{0,2},{2,0},{4,6},{6,4},{8,10},{10,8},{12,14},{14,12},{16,18},{18,... | collective-permute-start | bytes 1327112 | tf_op jit(solution)/shard_map/ppermute | solution.py:703
  37.1 3.5 %collective-permute-start.15 = (bf16[1,2,8,72,384]{4,3,2,1,0:T(8,128)(2,1)S(1)}, bf16[1,2,8,72,384]{4,3,2,1,0:T(8,128)(2,1)S(1)}, u32[]{:S(2)}, u32[]{:S(2)}) collective-permute-start(bf16[1,2,8,72,384]{4,3,2,1,0:T(8,128)(2,1)S(1)} %get-tuple-element.115), channel_id=1, source_target_pairs={{0,2},{2,0},{4,6},{6,4},{8,10},{10,8},{12,14},{14,12},{16,18},{18,... | collective-permute-start | bytes 2654216 | tf_op jit(solution)/shard_map/ppermute | solution.py:703
  40.0 5.1 %collective-permute-start.14 = (bf16[2,2,8,72,384]{4,3,2,1,0:T(8,128)(2,1)S(1)}, bf16[2,2,8,72,384]{4,3,2,1,0:T(8,128)(2,1)S(1)}, u32[]{:S(2)}, u32[]{:S(2)}) collective-permute-start(bf16[2,2,8,72,384]{4,3,2,1,0:T(8,128)(2,1)S(1)} %get-tuple-element.111), channel_id=1, source_target_pairs={{0,2},{2,0},{4,6},{6,4},{8,10},{10,8},{12,14},{14,12},{16,18},{18,... | collective-permute-start | bytes 5308424 | tf_op jit(solution)/shard_map/ppermute | solution.py:703
  40.8 13.2 %collective-permute-start.19 = (bf16[8,72,384]{2,1,0:T(8,128)(2,1)S(1)}, bf16[8,72,384]{2,1,0:T(8,128)(2,1)S(1)}, u32[]{:S(2)}, u32[]{:S(2)}) collective-permute-start(bf16[8,72,384]{2,1,0:T(8,128)(2,1)S(1)} %get-tuple-element.130), channel_id=1, source_target_pairs={{0,1},{1,0},{2,3},{3,2},{4,5},{5,4},{6,7},{7,6},{8,9},{9,8},{10,11... | collective-permute-start | bytes 1327112 | tf_op jit(solution)/shard_map/ppermute | solution.py:703
  45.8 12.9 %collective-permute-start.16 = (bf16[2,4,72,384]{3,2,1,0:T(8,128)(2,1)S(1)}, bf16[2,4,72,384]{3,2,1,0:T(8,128)(2,1)S(1)}, u32[]{:S(2)}, u32[]{:S(2)}) collective-permute-start(bf16[2,4,72,384]{3,2,1,0:T(8,128)(2,1)S(1)} %get-tuple-element.119), channel_id=1, source_target_pairs={{0,4},{2,6},{4,0},{6,2},{8,12},{10,14},{12,8},{14,10},{16,20},{18,... | collective-permute-start | bytes 1327112 | tf_op jit(solution)/shard_map/ppermute | solution.py:703
  47.3 11.9 %collective-permute-start.17 = (bf16[4,2,72,384]{3,2,1,0:T(8,128)(2,1)S(1)}, bf16[4,2,72,384]{3,2,1,0:T(8,128)(2,1)S(1)}, u32[]{:S(2)}, u32[]{:S(2)}) collective-permute-start(bf16[4,2,72,384]{3,2,1,0:T(8,128)(2,1)S(1)} %get-tuple-element.121), channel_id=1, source_target_pairs={{0,8},{2,10},{4,12},{6,14},{8,0},{10,2},{12,4},{14,6},{16,24},{18,... | collective-permute-start | bytes 1327112 | tf_op jit(solution)/shard_map/ppermute | solution.py:703
  54.0 2.6 %collective-permute-start.18 = (bf16[1,2,8,80,384]{4,3,2,1,0:T(8,128)(2,1)S(1)}, bf16[1,2,8,80,384]{4,3,2,1,0:T(8,128)(2,1)S(1)}, u32[]{:S(2)}, u32[]{:S(2)}) collective-permute-start(bf16[1,2,8,80,384]{4,3,2,1,0:T(8,128)(2,1)S(1)} %get-tuple-element.129), channel_id=1, source_target_pairs={{0,2},{2,0},{4,6},{6,4},{8,10},{10,8},{12,14},{14,12},{16,18},{18,... | collective-permute-start | bytes 2949128 | tf_op jit(solution)/shard_map/ppermute | solution.py:703
  54.1 9.1 %collective-permute-start.23 = (bf16[4,72,384]{2,1,0:T(8,128)(2,1)S(1)}, bf16[4,72,384]{2,1,0:T(8,128)(2,1)S(1)}, u32[]{:S(2)}, u32[]{:S(2)}) collective-permute-start(bf16[4,72,384]{2,1,0:T(8,128)(2,1)S(1)} %get-tuple-element.139), channel_id=1, source_target_pairs={{0,4},{2,6},{4,0},{6,2},{8,12},{10,14},{12,8},{14,10},{16,20},{18,... | collective-permute-start | bytes 663560 | tf_op jit(solution)/shard_map/ppermute | solution.py:703
  59.4 8.7 %collective-permute-start.20 = (bf16[2,2,72,384]{3,2,1,0:T(8,128)(2,1)S(1)}, bf16[2,2,72,384]{3,2,1,0:T(8,128)(2,1)S(1)}, u32[]{:S(2)}, u32[]{:S(2)}) collective-permute-start(bf16[2,2,72,384]{3,2,1,0:T(8,128)(2,1)S(1)} %get-tuple-element.135), channel_id=1, source_target_pairs={{0,8},{2,10},{4,12},{6,14},{8,0},{10,2},{12,4},{14,6},{16,24},{18,... | collective-permute-start | bytes 663560 | tf_op jit(solution)/shard_map/ppermute | solution.py:703
  61.0 7.1 %collective-permute-start.21 = (bf16[2,2,72,384]{3,2,1,0:T(8,128)(2,1)S(1)}, bf16[2,2,72,384]{3,2,1,0:T(8,128)(2,1)S(1)}, u32[]{:S(2)}, u32[]{:S(2)}) collective-permute-start(bf16[2,2,72,384]{3,2,1,0:T(8,128)(2,1)S(1)} %get-tuple-element.137), channel_id=1, source_target_pairs={{0,4},{2,6},{4,0},{6,2},{8,12},{10,14},{12,8},{14,10},{16,20},{18,... | collective-permute-start | bytes 663560 | tf_op jit(solution)/shard_map/ppermute | solution.py:703
  62.2 10.9 %collective-permute-start.22 = (bf16[8,80,384]{2,1,0:T(8,128)(2,1)S(1)}, bf16[8,80,384]{2,1,0:T(8,128)(2,1)S(1)}, u32[]{:S(2)}, u32[]{:S(2)}) collective-permute-start(bf16[8,80,384]{2,1,0:T(8,128)(2,1)S(1)} %get-tuple-element.138), channel_id=1, source_target_pairs={{0,1},{1,0},{2,3},{3,2},{4,5},{5,4},{6,7},{7,6},{8,9},{9,8},{10,11... | collective-permute-start | bytes 1474568 | tf_op jit(solution)/shard_map/ppermute | solution.py:703
  63.2 4.9 %collective-permute-start.24 = (bf16[2,72,384]{2,1,0:T(8,128)(2,1)S(1)}, bf16[2,72,384]{2,1,0:T(8,128)(2,1)S(1)}, u32[]{:S(2)}, u32[]{:S(2)}) collective-permute-start(bf16[2,72,384]{2,1,0:T(8,128)(2,1)S(1)} %get-tuple-element.141), channel_id=1, source_target_pairs={{0,8},{2,10},{4,12},{6,14},{8,0},{10,2},{12,4},{14,6},{16,24},{18,... | collective-permute-start | bytes 331784 | tf_op jit(solution)/shard_map/ppermute | solution.py:703
  73.3 9.5 %collective-permute-start.27 = (bf16[4,80,384]{2,1,0:T(8,128)(2,1)S(1)}, bf16[4,80,384]{2,1,0:T(8,128)(2,1)S(1)}, u32[]{:S(2)}, u32[]{:S(2)}) collective-permute-start(bf16[4,80,384]{2,1,0:T(8,128)(2,1)S(1)} %get-tuple-element.148), channel_id=1, source_target_pairs={{0,4},{2,6},{4,0},{6,2},{8,12},{10,14},{12,8},{14,10},{16,20},{18,... | collective-permute-start | bytes 737288 | tf_op jit(solution)/shard_map/ppermute | solution.py:703
  74.8 8.0 %collective-permute-start.26 = (bf16[3,72,384]{2,1,0:T(8,128)(2,1)S(1)}, bf16[3,72,384]{2,1,0:T(8,128)(2,1)S(1)}, u32[]{:S(2)}, u32[]{:S(2)}) collective-permute-start(bf16[3,72,384]{2,1,0:T(8,128)(2,1)S(1)} %get-tuple-element.145), channel_id=1, source_target_pairs={{0,16},{2,18},{4,20},{6,22},{8,24},{10,26},{12,28},{14,30},{16,0},... | collective-permute-start | bytes 497672 | tf_op jit(solution)/shard_map/ppermute | solution.py:703
  77.4 4.7 %collective-permute-start.25 = (bf16[2,72,384]{2,1,0:T(8,128)(2,1)S(1)}, bf16[2,72,384]{2,1,0:T(8,128)(2,1)S(1)}, u32[]{:S(2)}, u32[]{:S(2)}) collective-permute-start(bf16[2,72,384]{2,1,0:T(8,128)(2,1)S(1)} %get-tuple-element.143), channel_id=1, source_target_pairs={{0,1},{1,0},{2,3},{3,2},{4,5},{5,4},{6,7},{7,6},{8,9},{9,8},{10,11... | collective-permute-start | bytes 331784 | tf_op jit(solution)/shard_map/ppermute | solution.py:703
  82.9 7.0 %collective-permute-start.30 = (bf16[2,80,384]{2,1,0:T(8,128)(2,1)S(1)}, bf16[2,80,384]{2,1,0:T(8,128)(2,1)S(1)}, u32[]{:S(2)}, u32[]{:S(2)}) collective-permute-start(bf16[2,80,384]{2,1,0:T(8,128)(2,1)S(1)} %get-tuple-element.153), channel_id=1, source_target_pairs={{0,8},{2,10},{4,12},{6,14},{8,0},{10,2},{12,4},{14,6},{16,24},{18,... | collective-permute-start | bytes 368648 | tf_op jit(solution)/shard_map/ppermute | solution.py:703
  83.0 7.0 %collective-permute-start.28 = (bf16[2,72,384]{2,1,0:T(8,128)(2,1)S(1)}, bf16[2,72,384]{2,1,0:T(8,128)(2,1)S(1)}, u32[]{:S(2)}, u32[]{:S(2)}) collective-permute-start(bf16[2,72,384]{2,1,0:T(8,128)(2,1)S(1)} %get-tuple-element.149.refs_0_), channel_id=1, source_target_pairs={{0,16},{2,18},{4,20},{6,22},{8,24},{10,26},{12,28},{14,30},{16,0},... | collective-permute-start | bytes 331784 | tf_op jit(solution)/shard_map/ppermute | solution.py:703
  85.8 4.2 %collective-permute-start.29 = (bf16[72,384]{1,0:T(8,128)(2,1)S(1)}, bf16[72,384]{1,0:T(8,128)(2,1)S(1)}, u32[]{:S(2)}, u32[]{:S(2)}) collective-permute-start(bf16[72,384]{1,0:T(8,128)(2,1)S(1)} %get-tuple-element.151), channel_id=1, source_target_pairs={{0,1},{1,0},{2,3},{3,2},{4,5},{5,4},{6,7},{7,6},{8,9},{9,8},{10,11... | collective-permute-start | bytes 165896 | tf_op jit(solution)/shard_map/ppermute | solution.py:703
  90.0 10.0 %collective-permute-start.31 = (bf16[3,80,384]{2,1,0:T(8,128)(2,1)S(1)}, bf16[3,80,384]{2,1,0:T(8,128)(2,1)S(1)}, u32[]{:S(2)}, u32[]{:S(2)}) collective-permute-start(bf16[3,80,384]{2,1,0:T(8,128)(2,1)S(1)} %get-tuple-element.154.refs_0_), channel_id=1, source_target_pairs={{0,16},{2,18},{4,20},{6,22},{8,24},{10,26},{12,28},{14,30},{16,0},... | collective-permute-start | bytes 552968 | tf_op jit(solution)/shard_map/ppermute | solution.py:703
  92.9 7.2 %collective-permute-start.32 = (bf16[2,72,384]{2,1,0:T(8,128)(2,1)S(1)}, bf16[2,72,384]{2,1,0:T(8,128)(2,1)S(1)}, u32[]{:S(2)}, u32[]{:S(2)}) collective-permute-start(bf16[2,72,384]{2,1,0:T(8,128)(2,1)S(1)} %get-tuple-element.156.refs_3_), channel_id=1, source_target_pairs={{0,8},{2,10},{4,12},{6,14},{8,0},{10,2},{12,4},{14,6},{16,24},{18,... | collective-permute-start | bytes 331784 | tf_op jit(solution)/shard_map/ppermute | solution.py:703
  100.1 11.3 %collective-permute-start.36 = (bf16[2,72,384]{2,1,0:T(8,128)(2,1)S(1)}, bf16[2,72,384]{2,1,0:T(8,128)(2,1)S(1)}, u32[]{:S(2)}, u32[]{:S(2)}) collective-permute-start(bf16[2,72,384]{2,1,0:T(8,128)(2,1)S(1)} %get-tuple-element.158.refs_1_.refs_2_), channel_id=1, source_target_pairs={{0,8},{2,10},{4,12},{6,14},{8,0},{10,2},{12,4},{14,6},{16,24},{18,... | collective-permute-start | bytes 331784 | tf_op jit(solution)/shard_map/ppermute | solution.py:703
  102.1 12.3 %collective-permute-start.33 = (bf16[80,384]{1,0:T(8,128)(2,1)S(1)}, bf16[80,384]{1,0:T(8,128)(2,1)S(1)}, u32[]{:S(2)}, u32[]{:S(2)}) collective-permute-start(bf16[80,384]{1,0:T(8,128)(2,1)S(1)} %get-tuple-element.160.refs_0_), channel_id=1, source_target_pairs={{0,16},{2,18},{4,20},{6,22},{8,24},{10,26},{12,28},{14,30},{16,0},... | collective-permute-start | bytes 184328 | tf_op jit(solution)/shard_map/ppermute | solution.py:703
  105.3 6.1 %collective-permute-start.35 = (bf16[2,72,384]{2,1,0:T(8,128)(2,1)S(1)}, bf16[2,72,384]{2,1,0:T(8,128)(2,1)S(1)}, u32[]{:S(2)}, u32[]{:S(2)}) collective-permute-start(bf16[2,72,384]{2,1,0:T(8,128)(2,1)S(1)} %get-tuple-element.161.refs_0_), channel_id=1, source_target_pairs={{0,4},{2,6},{4,0},{6,2},{8,12},{10,14},{12,8},{14,10},{16,20},{18,... | collective-permute-start | bytes 331784 | tf_op jit(solution)/shard_map/ppermute | solution.py:703
  105.8 8.6 %collective-permute-start.34 = (bf16[2,2,72,384]{3,2,1,0:T(8,128)(2,1)S(1)}, bf16[2,2,72,384]{3,2,1,0:T(8,128)(2,1)S(1)}, u32[]{:S(2)}, u32[]{:S(2)}) collective-permute-start(bf16[2,2,72,384]{3,2,1,0:T(8,128)(2,1)S(1)} %pass_down.1.refs_3_.refs_0_), channel_id=1, source_target_pairs={{0,4},{2,6},{4,0},{6,2},{8,12},{10,14},{12,8},{14,10},{16,20},{18,... | collective-permute-start | bytes 663560 | tf_op jit(solution)/shard_map/ppermute | solution.py:703
  112.3 6.0 %collective-permute-start.42 = (bf16[2,2,72,384]{3,2,1,0:T(8,128)(2,1)S(1)}, bf16[2,2,72,384]{3,2,1,0:T(8,128)(2,1)S(1)}, u32[]{:S(2)}, u32[]{:S(2)}) collective-permute-start(bf16[2,2,72,384]{3,2,1,0:T(8,128)(2,1)S(1)} %get-tuple-element.163.refs_2_), channel_id=1, source_target_pairs={{0,4},{2,6},{4,0},{6,2},{8,12},{10,14},{12,8},{14,10},{16,20},{18,... | collective-permute-start | bytes 663560 | tf_op jit(solution)/shard_map/ppermute | solution.py:703
  113.5 5.9 %collective-permute-start.41 = (bf16[2,2,72,384]{3,2,1,0:T(8,128)(2,1)S(1)}, bf16[2,2,72,384]{3,2,1,0:T(8,128)(2,1)S(1)}, u32[]{:S(2)}, u32[]{:S(2)}) collective-permute-start(bf16[2,2,72,384]{3,2,1,0:T(8,128)(2,1)S(1)} %get-tuple-element.162.refs_2_.refs_0_), channel_id=1, source_target_pairs={{0,8},{2,10},{4,12},{6,14},{8,0},{10,2},{12,4},{14,6},{16,24},{18,... | collective-permute-start | bytes 663560 | tf_op jit(solution)/shard_map/ppermute | solution.py:703
  114.5 9.0 %collective-permute-start.39 = (bf16[2,80,384]{2,1,0:T(8,128)(2,1)S(1)}, bf16[2,80,384]{2,1,0:T(8,128)(2,1)S(1)}, u32[]{:S(2)}, u32[]{:S(2)}) collective-permute-start(bf16[2,80,384]{2,1,0:T(8,128)(2,1)S(1)} %share_qkv_out_high.1.refs_4_.refs_0_), channel_id=1, source_target_pairs={{0,12},{2,14},{4,8},{6,10},{8,4},{10,6},{12,0},{14,2},{16,28},{18,... | collective-permute-start | bytes 368648 | tf_op jit(solution)/shard_map/ppermute | solution.py:703
  116.1 7.4 %collective-permute-start.38 = (bf16[2,80,384]{2,1,0:T(8,128)(2,1)S(1)}, bf16[2,80,384]{2,1,0:T(8,128)(2,1)S(1)}, u32[]{:S(2)}, u32[]{:S(2)}) collective-permute-start(bf16[2,80,384]{2,1,0:T(8,128)(2,1)S(1)} %share_qkv_out_high.1.refs_4_.refs_0_), channel_id=1, source_target_pairs={{0,8},{2,10},{4,12},{6,14},{8,0},{10,2},{12,4},{14,6},{16,24},{18,... | collective-permute-start | bytes 368648 | tf_op jit(solution)/shard_map/ppermute | solution.py:703
  117.3 6.2 %collective-permute-start.37 = (bf16[2,80,384]{2,1,0:T(8,128)(2,1)S(1)}, bf16[2,80,384]{2,1,0:T(8,128)(2,1)S(1)}, u32[]{:S(2)}, u32[]{:S(2)}) collective-permute-start(bf16[2,80,384]{2,1,0:T(8,128)(2,1)S(1)} %share_qkv_out_high.1.refs_4_.refs_0_), channel_id=1, source_target_pairs={{0,4},{2,6},{4,0},{6,2},{8,12},{10,14},{12,8},{14,10},{16,20},{18,... | collective-permute-start | bytes 368648 | tf_op jit(solution)/shard_map/ppermute | solution.py:703
  118.3 1.8 %collective-permute-start.40 = (bf16[1,2,4,72,384]{4,3,2,1,0:T(8,128)(2,1)S(1)}, bf16[1,2,4,72,384]{4,3,2,1,0:T(8,128)(2,1)S(1)}, u32[]{:S(2)}, u32[]{:S(2)}) collective-permute-start(bf16[1,2,4,72,384]{4,3,2,1,0:T(8,128)(2,1)S(1)} %share_down.1.refs_2_.refs_0_), channel_id=1, source_target_pairs={{0,2},{2,0},{4,6},{6,4},{8,10},{10,8},{12,14},{14,12},{16,18},{18,... | collective-permute-start | bytes 1327112 | tf_op jit(solution)/shard_map/ppermute | solution.py:703
  119.6 4.3 %collective-permute-start.44 = (bf16[2,2,4,72,384]{4,3,2,1,0:T(8,128)(2,1)S(1)}, bf16[2,2,4,72,384]{4,3,2,1,0:T(8,128)(2,1)S(1)}, u32[]{:S(2)}, u32[]{:S(2)}) collective-permute-start(bf16[2,2,4,72,384]{4,3,2,1,0:T(8,128)(2,1)S(1)} %share_gate_up.1.refs_5_.refs_0_), channel_id=1, source_target_pairs={{0,2},{2,0},{4,6},{6,4},{8,10},{10,8},{12,14},{14,12},{16,18},{18,... | collective-permute-start | bytes 2654216 | tf_op jit(solution)/shard_map/ppermute | solution.py:703
  123.7 8.0 %collective-permute-start.43 = (bf16[1,2,4,80,384]{4,3,2,1,0:T(8,128)(2,1)S(1)}, bf16[1,2,4,80,384]{4,3,2,1,0:T(8,128)(2,1)S(1)}, u32[]{:S(2)}, u32[]{:S(2)}) collective-permute-start(bf16[1,2,4,80,384]{4,3,2,1,0:T(8,128)(2,1)S(1)} %share_qkv_out.1.refs_5_.refs_0_), channel_id=1, source_target_pairs={{0,2},{2,0},{4,6},{6,4},{8,10},{10,8},{12,14},{14,12},{16,18},{18,... | collective-permute-start | bytes 1474568 | tf_op jit(solution)/shard_map/ppermute | solution.py:703
  (22 other events, 139.6 us)

commit v11 on v9

--- a/solution.py
+++ b/solution.py
@@ -31,6 +31,8 @@
 SCALE = float(HEAD) ** (-0.5)
 VMEM_LIMIT = 32 * 1024 * 1024
 PACK_LIMIT = 53 * 1024 * 1024
+STEP_LIMIT = 14 * 1024 * 1024
+UPDATE_LIMIT = 20 * 1024 * 1024
 HALF = 144
 CUT_ROWS = 72
 MARK = (8, 128)
@@ -262,7 +264,7 @@
     window = (shape, lambda i: (i[1] * 2 * HALF, 0))
     outs = [sds(shape, BF16)]
     return pack_kernel(
-        cast_out, idx, [down_t], [window], outs, "pack_down", after, VMEM_LIMIT
+        cast_out, idx, [down_t], [window], outs, "pack_down", after, STEP_LIMIT
     )[0]
 
 
@@ -571,7 +573,7 @@
         in_specs=[pl.BlockSpec(memory_space=pltpu.VMEM)] * len(arrays)
         + [pl.BlockSpec(memory_space=pl.ANY)] * len(after),
         out_specs=tuple([pl.BlockSpec(memory_space=pltpu.VMEM)] * len(outs)),
-        compiler_params=pltpu.CompilerParams(vmem_limit_bytes=VMEM_LIMIT),
+        compiler_params=pltpu.CompilerParams(vmem_limit_bytes=STEP_LIMIT),
         cost_estimate=busy_for(busy),
         name=name,
     )(*arrays, *after)
@@ -690,7 +692,7 @@
         + [pltpu.VMEM((total, starts[-1]), F32)]
         + [pltpu.SemaphoreType.DMA((len(shares) * chunks, 3 * count))],
         input_output_aliases={first_earlier + i: i for i in range(len(earlier))},
-        compiler_params=pltpu.CompilerParams(vmem_limit_bytes=VMEM_LIMIT),
+        compiler_params=pltpu.CompilerParams(vmem_limit_bytes=UPDATE_LIMIT),
         cost_estimate=busy_for(busy),
         name=name,
     )(idx, *[p for _, p in shares], *state, *gains, *earlier, *after)
@@ -965,6 +967,7 @@
             [send, keep, arrived, arrived_low, keep_qkv_out, arrived_qkv_out],
             [sds((3, *taller), BF16), sds(taller, F32), sds((2, *piece), BF16)],
             "lines",
+            (w_gate_up, first_gate_up, second_gate_up),
         )
         arrived, down_low = over_z_high(pieces), over_z_low(near_down)
 
@@ -981,6 +984,10 @@
             [pieces, arrived, keep_qkv_out, near_down, down_low],
             [sds((3, 2, *piece), BF16), sds((2, *piece), BF16), sds(taller, BF16)],
             "share_high",
+            (
+                *(w_qkv, w_out, first_qkv, first_out, second_qkv, second_out),
+                *(down_t, first_down_t, second_down_t, first_gains, second_gains),
+            ),
         )
         arrived_x, low_low = over_x(near_x), over_z_low(near_low)
         qkv_out_high = over_z_high(piece_qkv_out)

time: 136 us -> 132 us (0.971)
  local copies, waits for them, and re-layouts: 4.68 us -> 1.18 us
    unnamed x48, local copies, waits for them, and re-layouts: 4.33 us -> 0.82 us
where the time goes in v11:
time: 132 us
  starting transfers between devices  48.7 us (37%)
  waiting for transfers between devices  44.6 us (34%)
  Pallas kernels  36.3 us (27%)
  between operations  1.39 us (1%)
    ppermute x44, starting transfers between devices, swap(): return lax.ppermute(values, axis, [(i, i ^ mask) for i in range(size)])  48.7 us
    ppermute x44, waiting for transfers between devices, swap(): return lax.ppermute(values, axis, [(i, i ^ mask) for i in range(size)])  44.6 us
    pallas_call x5, Pallas kernels, call(): pl.pallas_call(kernel, out_shape=tuple(outs), in_specs=[pl.BlockSpec(memo...  15.7 us
    pallas_call x4, Pallas kernels, update_rows(): pl.pallas_call(kernel, out_shape=tuple((sds(a.shape, F32) for a in [*stat...  14.3 us
    pallas_call x17, Pallas kernels, step(): pl.pallas_call(kernel, out_shape=tuple(outs), in_specs=[pl.BlockSpec(memo...  3.32 us
    pallas_call x2, Pallas kernels, pack_kernel(): pl.pallas_call(kernel, out_shape=tuple(outs), in_specs=[pl.BlockSpec(memo...  2.97 us
  transfers between devices with their start and end apart: 44, of which 20 were waited for; matrix products, arithmetic and copies ran while one was open for 0% of the time, Pallas kernels for 22%

profile of v11, /device:TPU:0, one launch (start us, length us, event | category | flops | bytes accessed | tf_op | source)
XLA Modules:
  0.0 132.3 jit_solution(17655477683234741035)
XLA Ops:
  1.4 2.2 %pack_first.1 = (bf16[160,768]{1,0:T(8,128)(2,1)S(1)}, bf16[144,768]{1,0:T(8,128)(2,1)S(1)}, bf16[144,768]{1,0:T(8,128)(2,1)S(1)}) custom-call(s32[4]{0:T(128)S(1)} %pad_add_fusion.idx_ref.refs_0_, f32[288,960]{1,0:T(8,128)} %refs_2_.9, f32[288,576]{1,0:T(8,128)} %refs_3_.8, f32[2,288]{1,0:T(2,128)S(1)} %copy-done.16, f32[288,3072]{1,0:T(8,128)} %refs_1_.5, ...), custom_call_target="tpu_custom_call" | custom-call | flops 10000000000 | tf_op jit(solution)/shard_map/pack_first/pallas_call | solution.py:242
  3.6 3.0 %collective-permute-start = (bf16[160,768]{1,0:T(8,128)(2,1)S(1)}, bf16[160,768]{1,0:T(8,128)(2,1)S(1)}, u32[]{:S(2)}, u32[]{:S(2)}) collective-permute-start(bf16[160,768]{1,0:T(8,128)(2,1)S(1)} %get-tuple-element.103), channel_id=1, source_target_pairs={{0,1},{1,0},{2,3},{3,2},{4,5},{5,4},{6,7},{7,6},{8,9},{9,8},{10,11... | collective-permute-start | bytes 737288 | tf_op jit(solution)/shard_map/ppermute | solution.py:703
  6.7 1.9 %collective-permute-start.4 = (bf16[144,768]{1,0:T(8,128)(2,1)S(1)}, bf16[144,768]{1,0:T(8,128)(2,1)S(1)}, u32[]{:S(2)}, u32[]{:S(2)}) collective-permute-start(bf16[144,768]{1,0:T(8,128)(2,1)S(1)} %get-tuple-element.107), channel_id=1, source_target_pairs={{0,1},{1,0},{2,3},{3,2},{4,5},{5,4},{6,7},{7,6},{8,9},{9,8},{10,11... | collective-permute-start | bytes 663560 | tf_op jit(solution)/shard_map/ppermute | solution.py:703
  8.7 9.5 %collective-permute-done.8.refs_11_.refs_1_ = bf16[144,768]{1,0:T(8,128)(2,1)S(1)} collective-permute-done((bf16[144,768]{1,0:T(8,128)(2,1)S(1)}, bf16[144,768]{1,0:T(8,128)(2,1)S(1)}, u32[]{:S(2)}, u32[]{:S(2)}) %collective-permute-start.8) | collective-permute-done | bytes 221216 | tf_op jit(solution)/shard_map/ppermute | solution.py:703
  18.2 2.1 %collective-permute-start.9 = (bf16[144,768]{1,0:T(8,128)(2,1)S(1)}, bf16[144,768]{1,0:T(8,128)(2,1)S(1)}, u32[]{:S(2)}, u32[]{:S(2)}) collective-permute-start(bf16[144,768]{1,0:T(8,128)(2,1)S(1)} %collective-permute-done.8.refs_11_.refs_1_), channel_id=1, source_target_pairs={{0,8},{2,10},{4,12},{6,14},{8,0},{10,2},{12,4},{14,6},{16,24},{18,... | collective-permute-start | bytes 663560 | tf_op jit(solution)/shard_map/ppermute | solution.py:703
  20.4 0.8 pack_down.1
  21.2 2.0 %collective-permute-start.12 = (bf16[288,768]{1,0:T(8,128)(2,1)S(1)}, bf16[288,768]{1,0:T(8,128)(2,1)S(1)}, u32[]{:S(2)}, u32[]{:S(2)}) collective-permute-start(bf16[288,768]{1,0:T(8,128)(2,1)S(1)} %pack_down.1), channel_id=1, source_target_pairs={{0,1},{1,0},{2,3},{3,2},{4,5},{5,4},{6,7},{7,6},{8,9},{9,8},{10,11... | collective-permute-start | bytes 1327112 | tf_op jit(solution)/shard_map/ppermute | solution.py:703
  23.2 1.5 %collective-permute-start.5 = (bf16[144,768]{1,0:T(8,128)(2,1)S(1)}, bf16[144,768]{1,0:T(8,128)(2,1)S(1)}, u32[]{:S(2)}, u32[]{:S(2)}) collective-permute-start(bf16[144,768]{1,0:T(8,128)(2,1)S(1)} %collective-permute-done.4.refs_7_), channel_id=1, source_target_pairs={{0,4},{2,6},{4,0},{6,2},{8,12},{10,14},{12,8},{14,10},{16,20},{18,... | collective-permute-start | bytes 663560 | tf_op jit(solution)/shard_map/ppermute | solution.py:703
  24.7 1.4 %collective-permute-done.9.refs_12_ = bf16[144,768]{1,0:T(8,128)(2,1)S(1)} collective-permute-done((bf16[144,768]{1,0:T(8,128)(2,1)S(1)}, bf16[144,768]{1,0:T(8,128)(2,1)S(1)}, u32[]{:S(2)}, u32[]{:S(2)}) %collective-permute-start.9) | collective-permute-done | bytes 221216 | tf_op jit(solution)/shard_map/ppermute | solution.py:703
  26.1 3.4 %collective-permute-done.1.refs_9_ = bf16[160,768]{1,0:T(8,128)(2,1)S(1)} collective-permute-done((bf16[160,768]{1,0:T(8,128)(2,1)S(1)}, bf16[160,768]{1,0:T(8,128)(2,1)S(1)}, u32[]{:S(2)}, u32[]{:S(2)}) %collective-permute-start.1) | collective-permute-done | bytes 245792 | tf_op jit(solution)/shard_map/ppermute | solution.py:703
  29.5 1.0 collective-permute-done.5.refs_8_
  31.2 2.5 %attention.1 = (bf16[128,960]{1,0:T(8,128)(2,1)S(1)}, bf16[128,576]{1,0:T(8,128)(2,1)S(1)}, f32[128,128]{1,0:T(8,128)S(1)}, f32[128,128]{1,0:T(8,128)S(1)}, f32[...) custom-call(s32[4]{0:T(128)S(1)} %pad_add_fusion.idx_ref.refs_0_, ...), custom_call_target="tpu_custom_call" | custom-call | flops 1000000000 | tf_op jit(solution)/shard_map/attention/pallas_call | solution.py:152
  34.3 2.8 %feed_forward.1 = (f32[128,576]{1,0:T(8,128)S(1)}, bf16[128,576]{1,0:T(8,128)(2,1)S(1)}, f32[128,3072]{1,0:T(8,128)S(1)}, bf16[128,1536]{1,0:T(8,128)(2,1)S(1)},...) custom-call(s32[4]{0:T(128)S(1)} %pad_add_fusion.idx_ref.refs_0_, ...), custom_call_target="tpu_custom_call" | custom-call | flops 5000000000 | tf_op jit(solution)/shard_map/feed_forward/pallas_call | solution.py:152
  37.4 2.6 %feed_back.1 = (bf16[128,3072]{1,0:T(8,128)(2,1)S(1)}, bf16[2,2,8,72,384]{4,3,2,1,0:T(8,128)(2,1)S(1)}, bf16[2,2,8,72,384]{4,3,2,1,0:T(8,128)(2,1)S(1)}, bf16[576,1536]{1,0:T(8,128)(2,1)S(1)}) custom-call(s32[4]{0:T(128)S(1)} %pad_add_fusion.idx_ref.refs_0_, f32[128,3072]{1,0:T(8,128)S(1)} %get-tuple-element.111.refs_1_, ...), custom_call_target="tpu_custom_call" | custom-call | flops 20000000000 | tf_op jit(solution)/shard_map/feed_back/pallas_call | solution.py:152
  40.8 1.6 %collective-permute-start.18 = (bf16[8,72,384]{2,1,0:T(8,128)(2,1)S(1)}, bf16[8,72,384]{2,1,0:T(8,128)(2,1)S(1)}, u32[]{:S(2)}, u32[]{:S(2)}) collective-permute-start(bf16[8,72,384]{2,1,0:T(8,128)(2,1)S(1)} %get-tuple-element.126), channel_id=1, source_target_pairs={{0,1},{1,0},{2,3},{3,2},{4,5},{5,4},{6,7},{7,6},{8,9},{9,8},{10,11... | collective-permute-start | bytes 1327112 | tf_op jit(solution)/shard_map/ppermute | solution.py:703
  42.4 2.7 %middle_back.1 = (f32[128,576]{1,0:T(8,128)S(1)}, bf16[128,576]{1,0:T(8,128)(2,1)S(1)}, f32[1,576]{1,0:T(1,128)S(1)}) custom-call(s32[4]{0:T(128)S(1)} %pad_add_fusion.idx_ref.refs_0_, bf16[576,128]{1,0:T(8,128)(2,1)S(1)} %bitcast.64, f32[128,576]{1,0:T(8,128)S(1)} %get-tuple-element.109.refs_2_.refs_0_, ...), custom_call_target="tpu_custom_call" | custom-call | flops 20000000000 | tf_op jit(solution)/shard_map/middle_back/pallas_call | solution.py:152
  45.7 1.6 %collective-permute-start.16 = (bf16[2,4,72,384]{3,2,1,0:T(8,128)(2,1)S(1)}, bf16[2,4,72,384]{3,2,1,0:T(8,128)(2,1)S(1)}, u32[]{:S(2)}, u32[]{:S(2)}) collective-permute-start(bf16[2,4,72,384]{3,2,1,0:T(8,128)(2,1)S(1)} %get-tuple-element.123), channel_id=1, source_target_pairs={{0,4},{2,6},{4,0},{6,2},{8,12},{10,14},{12,8},{14,10},{16,20},{18,... | collective-permute-start | bytes 1327112 | tf_op jit(solution)/shard_map/ppermute | solution.py:703
  47.3 1.6 %collective-permute-start.17 = (bf16[4,2,72,384]{3,2,1,0:T(8,128)(2,1)S(1)}, bf16[4,2,72,384]{3,2,1,0:T(8,128)(2,1)S(1)}, u32[]{:S(2)}, u32[]{:S(2)}) collective-permute-start(bf16[4,2,72,384]{3,2,1,0:T(8,128)(2,1)S(1)} %get-tuple-element.125), channel_id=1, source_target_pairs={{0,8},{2,10},{4,12},{6,14},{8,0},{10,2},{12,4},{14,6},{16,24},{18,... | collective-permute-start | bytes 1327112 | tf_op jit(solution)/shard_map/ppermute | solution.py:703
  48.9 5.1 %attention_back.1 = (bf16[576,128]{1,0:T(8,128)(2,1)}, bf16[1,2,8,80,384]{4,3,2,1,0:T(8,128)(2,1)S(1)}, bf16[1,2,8,80,384]{4,3,2,1,0:T(8,128)(2,1)S(1)}, f32[8,128]{1,0:T(8,128)S(1)}) custom-call(s32[4]{0:T(128)S(1)} %pad_add_fusion.idx_ref.refs_0_, bf16[576,128]{1,0:T(8,128)(2,1)S(1)} %bitcast.67, f32[128,576]{1,0:T(8,128)S(1)} %get-tuple-element.121.refs_4_.refs_2_, ...), custom_call_target="tpu_custom_call" | custom-call | flops 20000000000 | tf_op jit(solution)/shard_map/attention_back/pallas_call | solution.py:152
  54.0 1.0 collective-permute-start.23
  55.0 3.8 %collective-permute-done.16 = bf16[2,4,72,384]{3,2,1,0:T(8,128)(2,1)S(1)} collective-permute-done((bf16[2,4,72,384]{3,2,1,0:T(8,128)(2,1)S(1)}, bf16[2,4,72,384]{3,2,1,0:T(8,128)(2,1)S(1)}, u32[]{:S(2)}, u32[]{:S(2)}) %collective-permute-start.16) | collective-permute-done | bytes 442400 | tf_op jit(solution)/shard_map/ppermute | solution.py:703
  59.4 1.6 %collective-permute-start.19 = (bf16[2,2,72,384]{3,2,1,0:T(8,128)(2,1)S(1)}, bf16[2,2,72,384]{3,2,1,0:T(8,128)(2,1)S(1)}, u32[]{:S(2)}, u32[]{:S(2)}) collective-permute-start(bf16[2,2,72,384]{3,2,1,0:T(8,128)(2,1)S(1)} %get-tuple-element.136), channel_id=1, source_target_pairs={{0,8},{2,10},{4,12},{6,14},{8,0},{10,2},{12,4},{14,6},{16,24},{18,... | collective-permute-start | bytes 663560 | tf_op jit(solution)/shard_map/ppermute | solution.py:703
  61.0 1.1 collective-permute-start.20
  63.1 2.1 %collective-permute-start.24 = (bf16[2,72,384]{2,1,0:T(8,128)(2,1)S(1)}, bf16[2,72,384]{2,1,0:T(8,128)(2,1)S(1)}, u32[]{:S(2)}, u32[]{:S(2)}) collective-permute-start(bf16[2,72,384]{2,1,0:T(8,128)(2,1)S(1)} %get-tuple-element.145), channel_id=1, source_target_pairs={{0,8},{2,10},{4,12},{6,14},{8,0},{10,2},{12,4},{14,6},{16,24},{18,... | collective-permute-start | bytes 331784 | tf_op jit(solution)/shard_map/ppermute | solution.py:703
  65.2 1.4 %collective-permute-done.19.refs_1_ = bf16[2,2,72,384]{3,2,1,0:T(8,128)(2,1)S(1)} collective-permute-done((bf16[2,2,72,384]{3,2,1,0:T(8,128)(2,1)S(1)}, bf16[2,2,72,384]{3,2,1,0:T(8,128)(2,1)S(1)}, u32[]{:S(2)}, u32[]{:S(2)}) %collective-permute-start.19) | collective-permute-done | bytes 221216 | tf_op jit(solution)/shard_map/ppermute | solution.py:703
  68.1 5.3 %collective-permute-done.22 = bf16[8,80,384]{2,1,0:T(8,128)(2,1)S(1)} collective-permute-done((bf16[8,80,384]{2,1,0:T(8,128)(2,1)S(1)}, bf16[8,80,384]{2,1,0:T(8,128)(2,1)S(1)}, u32[]{:S(2)}, u32[]{:S(2)}) %collective-permute-start.22) | collective-permute-done | bytes 491552 | tf_op jit(solution)/shard_map/ppermute | solution.py:703
  73.6 1.5 %collective-permute-start.27 = (bf16[4,80,384]{2,1,0:T(8,128)(2,1)S(1)}, bf16[4,80,384]{2,1,0:T(8,128)(2,1)S(1)}, u32[]{:S(2)}, u32[]{:S(2)}) collective-permute-start(bf16[4,80,384]{2,1,0:T(8,128)(2,1)S(1)} %get-tuple-element.152), channel_id=1, source_target_pairs={{0,4},{2,6},{4,0},{6,2},{8,12},{10,14},{12,8},{14,10},{16,20},{18,... | collective-permute-start | bytes 737288 | tf_op jit(solution)/shard_map/ppermute | solution.py:703
  75.1 2.6 %collective-permute-start.26 = (bf16[3,72,384]{2,1,0:T(8,128)(2,1)S(1)}, bf16[3,72,384]{2,1,0:T(8,128)(2,1)S(1)}, u32[]{:S(2)}, u32[]{:S(2)}) collective-permute-start(bf16[3,72,384]{2,1,0:T(8,128)(2,1)S(1)} %get-tuple-element.149), channel_id=1, source_target_pairs={{0,16},{2,18},{4,20},{6,22},{8,24},{10,26},{12,28},{14,30},{16,0},... | collective-permute-start | bytes 497672 | tf_op jit(solution)/shard_map/ppermute | solution.py:703
  78.2 4.2 %collective-permute-done.25.refs_1_ = bf16[2,72,384]{2,1,0:T(8,128)(2,1)S(1)} collective-permute-done((bf16[2,72,384]{2,1,0:T(8,128)(2,1)S(1)}, bf16[2,72,384]{2,1,0:T(8,128)(2,1)S(1)}, u32[]{:S(2)}, u32[]{:S(2)}) %collective-permute-start.25) | collective-permute-done | bytes 110624 | tf_op jit(solution)/shard_map/ppermute | solution.py:703
  83.3 2.8 %collective-permute-start.28 = (bf16[2,72,384]{2,1,0:T(8,128)(2,1)S(1)}, bf16[2,72,384]{2,1,0:T(8,128)(2,1)S(1)}, u32[]{:S(2)}, u32[]{:S(2)}) collective-permute-start(bf16[2,72,384]{2,1,0:T(8,128)(2,1)S(1)} %get-tuple-element.153.refs_0_), channel_id=1, source_target_pairs={{0,16},{2,18},{4,20},{6,22},{8,24},{10,26},{12,28},{14,30},{16,0},... | collective-permute-start | bytes 331784 | tf_op jit(solution)/shard_map/ppermute | solution.py:703
  86.6 3.6 %collective-permute-done.29.refs_3_ = bf16[72,384]{1,0:T(8,128)(2,1)S(1)} collective-permute-done((bf16[72,384]{1,0:T(8,128)(2,1)S(1)}, bf16[72,384]{1,0:T(8,128)(2,1)S(1)}, u32[]{:S(2)}, u32[]{:S(2)}) %collective-permute-start.29) | collective-permute-done | bytes 55328 | tf_op jit(solution)/shard_map/ppermute | solution.py:703
  90.5 2.8 %collective-permute-start.31 = (bf16[3,80,384]{2,1,0:T(8,128)(2,1)S(1)}, bf16[3,80,384]{2,1,0:T(8,128)(2,1)S(1)}, u32[]{:S(2)}, u32[]{:S(2)}) collective-permute-start(bf16[3,80,384]{2,1,0:T(8,128)(2,1)S(1)} %get-tuple-element.158.refs_0_), channel_id=1, source_target_pairs={{0,16},{2,18},{4,20},{6,22},{8,24},{10,26},{12,28},{14,30},{16,0},... | collective-permute-start | bytes 552968 | tf_op jit(solution)/shard_map/ppermute | solution.py:703
  93.3 3.6 %collective-permute-start.32 = (bf16[2,72,384]{2,1,0:T(8,128)(2,1)S(1)}, bf16[2,72,384]{2,1,0:T(8,128)(2,1)S(1)}, u32[]{:S(2)}, u32[]{:S(2)}) collective-permute-start(bf16[2,72,384]{2,1,0:T(8,128)(2,1)S(1)} %get-tuple-element.160.refs_3_), channel_id=1, source_target_pairs={{0,8},{2,10},{4,12},{6,14},{8,0},{10,2},{12,4},{14,6},{16,24},{18,... | collective-permute-start | bytes 331784 | tf_op jit(solution)/shard_map/ppermute | solution.py:703
  96.9 4.3 %collective-permute-done.32.refs_4_ = bf16[2,72,384]{2,1,0:T(8,128)(2,1)S(1)} collective-permute-done((bf16[2,72,384]{2,1,0:T(8,128)(2,1)S(1)}, bf16[2,72,384]{2,1,0:T(8,128)(2,1)S(1)}, u32[]{:S(2)}, u32[]{:S(2)}) %collective-permute-start.32) | collective-permute-done | bytes 110624 | tf_op jit(solution)/shard_map/ppermute | solution.py:703
  101.4 2.3 %collective-permute-start.34 = (bf16[3,2,72,384]{3,2,1,0:T(8,128)(2,1)S(1)}, bf16[3,2,72,384]{3,2,1,0:T(8,128)(2,1)S(1)}, u32[]{:S(2)}, u32[]{:S(2)}) collective-permute-start(bf16[3,2,72,384]{3,2,1,0:T(8,128)(2,1)S(1)} %get-tuple-element.161.refs_3_.refs_0_), channel_id=1, source_target_pairs={{0,4},{2,6},{4,0},{6,2},{8,12},{10,14},{12,8},{14,10},{16,20},{18,... | collective-permute-start | bytes 995336 | tf_op jit(solution)/shard_map/ppermute | solution.py:703
  103.7 1.0 collective-permute-start.33
  104.7 1.4 %collective-permute-start.35 = (bf16[2,72,384]{2,1,0:T(8,128)(2,1)S(1)}, bf16[2,72,384]{2,1,0:T(8,128)(2,1)S(1)}, u32[]{:S(2)}, u32[]{:S(2)}) collective-permute-start(bf16[2,72,384]{2,1,0:T(8,128)(2,1)S(1)} %get-tuple-element.164.refs_2_), channel_id=1, source_target_pairs={{0,8},{2,10},{4,12},{6,14},{8,0},{10,2},{12,4},{14,6},{16,24},{18,... | collective-permute-start | bytes 331784 | tf_op jit(solution)/shard_map/ppermute | solution.py:703
  106.1 1.5 %layer_output.1 = bf16[576,128]{1,0:T(8,128)(2,1)} custom-call(f32[128,576]{1,0:T(8,128)S(1)} %copy-done.23, bf16[128,1536]{1,0:T(8,128)(2,1)S(1)} %get-tuple-element.110.refs_1_, bf16[576,1536]{1,0:T(8,128)(2,1)S(1)} %get-tuple-element.113.refs_2_, bf16[3,2,72,384]{3,2,1,0:T(8,128)(2,1)S(1)} %get-tuple-element.161.refs_3_.refs_0_), custom_call_target="tpu_custom_call" | custom-call | flops 2000000000 | tf_op jit(solution)/shard_map/layer_output/pallas_call | solution.py:570
  107.6 1.7 %collective-permute-done.33.refs_4_.refs_1_ = bf16[80,384]{1,0:T(8,128)(2,1)S(1)} collective-permute-done((bf16[80,384]{1,0:T(8,128)(2,1)S(1)}, bf16[80,384]{1,0:T(8,128)(2,1)S(1)}, u32[]{:S(2)}, u32[]{:S(2)}) %collective-permute-start.33) | collective-permute-done | bytes 61472 | tf_op jit(solution)/shard_map/ppermute | solution.py:703
  109.3 1.0 collective-permute-done.35.refs_3_
  110.6 1.8 %collective-permute-start.40 = (bf16[2,2,72,384]{3,2,1,0:T(8,128)(2,1)S(1)}, bf16[2,2,72,384]{3,2,1,0:T(8,128)(2,1)S(1)}, u32[]{:S(2)}, u32[]{:S(2)}) collective-permute-start(bf16[2,2,72,384]{3,2,1,0:T(8,128)(2,1)S(1)} %get-tuple-element.166.refs_2_), channel_id=1, source_target_pairs={{0,4},{2,6},{4,0},{6,2},{8,12},{10,14},{12,8},{14,10},{16,20},{18,... | collective-permute-start | bytes 663560 | tf_op jit(solution)/shard_map/ppermute | solution.py:703
  112.5 1.7 %collective-permute-start.38 = (bf16[2,80,384]{2,1,0:T(8,128)(2,1)S(1)}, bf16[2,80,384]{2,1,0:T(8,128)(2,1)S(1)}, u32[]{:S(2)}, u32[]{:S(2)}) collective-permute-start(bf16[2,80,384]{2,1,0:T(8,128)(2,1)S(1)} %share_qkv_out_high.1.refs_5_.refs_0_), channel_id=1, source_target_pairs={{0,12},{2,14},{4,8},{6,10},{8,4},{10,6},{12,0},{14,2},{16,28},{18,... | collective-permute-start | bytes 368648 | tf_op jit(solution)/shard_map/ppermute | solution.py:703
  114.2 1.2 collective-permute-start.37
  116.1 3.3 %update_down.1 = (f32[576,768]{1,0:T(8,128)}, f32[576,768]{1,0:T(8,128)}, f32[576,768]{1,0:T(8,128)}, f32[8,128]{1,0:T(8,128)S(1)}) custom-call(s32[4]{0:T(128)S(1)} %pad_add_fusion.idx_ref.refs_0_, bf16[1,2,4,72,384]{4,3,2,1,0:T(8,128)(2,1)S(1)} %get-tuple-element.167.refs_0_, bf16[1,2,4,72,384]{4,3,2,1,0:T(8,128)(2,1)S(1)} %collective-permute-done.41.refs_1_, ...), custom_call_target="tpu_custom_call" | custom-call | flops 100000000 | tf_op jit(solution)/shard_map/update_down/pallas_call | solution.py:684
  119.4 0.8 collective-permute-done.39.refs_1_
  120.4 3.4 %update_gate_up_near.1 = (f32[288,3072]{1,0:T(8,128)}, f32[288,3072]{1,0:T(8,128)}, f32[288,3072]{1,0:T(8,128)}, f32[8,128]{1,0:T(8,128)S(1)}) custom-call(s32[4]{0:T(128)S(1)} %pad_add_fusion.idx_ref.refs_0_, bf16[2,2,4,72,384]{4,3,2,1,0:T(8,128)(2,1)S(1)} %share_gate_up.1.refs_0_, f32[288,3072]{1,0:T(8,128)S(1)} %copy-done.3, f32[288,3072]{1,0:T(8,128)S(1)} %copy-done.4, ...), custom_call_target="tpu_custom_call" | custom-call | flops 20000000000 | tf_op jit(solution)/shard_map/update_gate_up_near/pallas_call | solution.py:684
  124.4 3.3 %update_gate_up_far.1 = (f32[288,3072]{1,0:T(8,128)}, f32[288,3072]{1,0:T(8,128)}, f32[288,3072]{1,0:T(8,128)}, f32[8,128]{1,0:T(8,128)S(1)}) custom-call(s32[4]{0:T(128)S(1)} %pad_add_fusion.idx_ref.refs_0_, bf16[2,2,4,72,384]{4,3,2,1,0:T(8,128)(2,1)S(1)} %collective-permute-done.43.refs_0_, ...), custom_call_target="tpu_custom_call", output_to_operand_aliasing={{0}: (5, {}), {1}: (6, {}), {2}: (7, {})} | custom-call | flops 20000000000 | tf_op jit(solution)/shard_map/update_gate_up_far/pallas_call | solution.py:684
  127.8 4.3 %update_qkv_out.1 = (f32[288,960]{1,0:T(8,128)}, f32[288,576]{1,0:T(8,128)}, f32[288,960]{1,0:T(8,128)}, f32[288,576]{1,0:T(8,128)}, f32[288,960]{1,0:T(8,128)},...) custom-call(s32[4]{0:T(128)S(1)} %pad_add_fusion.idx_ref.refs_0_, ...), custom_call_target="tpu_custom_call" | custom-call | flops 20000000000 | tf_op jit(solution)/shard_map/update_qkv_out/pallas_call | solution.py:684
  (119 shorter events, 11.1 us)
Async XLA Ops:
  1.4 19.0 %copy-start = (f32[768,576]{0,1:T(8,128)S(1)}, f32[768,576]{0,1:T(8,128)}, u32[]{:S(2)}) copy-start(f32[768,576]{0,1:T(8,128)} %param.25) | copy-start | bytes 5308420
  3.6 16.7 %collective-permute-start = (bf16[160,768]{1,0:T(8,128)(2,1)S(1)}, bf16[160,768]{1,0:T(8,128)(2,1)S(1)}, u32[]{:S(2)}, u32[]{:S(2)}) collective-permute-start(bf16[160,768]{1,0:T(8,128)(2,1)S(1)} %get-tuple-element.103), channel_id=1, source_target_pairs={{0,1},{1,0},{2,3},{3,2},{4,5},{5,4},{6,7},{7,6},{8,9},{9,8},{10,11... | collective-permute-start | bytes 737288 | tf_op jit(solution)/shard_map/ppermute | solution.py:703
  6.7 11.5 %collective-permute-start.8 = (bf16[144,768]{1,0:T(8,128)(2,1)S(1)}, bf16[144,768]{1,0:T(8,128)(2,1)S(1)}, u32[]{:S(2)}, u32[]{:S(2)}) collective-permute-start(bf16[144,768]{1,0:T(8,128)(2,1)S(1)} %get-tuple-element.108), channel_id=1, source_target_pairs={{0,1},{1,0},{2,3},{3,2},{4,5},{5,4},{6,7},{7,6},{8,9},{9,8},{10,11... | collective-permute-start | bytes 663560 | tf_op jit(solution)/shard_map/ppermute | solution.py:703
  6.7 16.5 %collective-permute-start.4 = (bf16[144,768]{1,0:T(8,128)(2,1)S(1)}, bf16[144,768]{1,0:T(8,128)(2,1)S(1)}, u32[]{:S(2)}, u32[]{:S(2)}) collective-permute-start(bf16[144,768]{1,0:T(8,128)(2,1)S(1)} %get-tuple-element.107), channel_id=1, source_target_pairs={{0,1},{1,0},{2,3},{3,2},{4,5},{5,4},{6,7},{7,6},{8,9},{9,8},{10,11... | collective-permute-start | bytes 663560 | tf_op jit(solution)/shard_map/ppermute | solution.py:703
  18.2 7.9 %collective-permute-start.9 = (bf16[144,768]{1,0:T(8,128)(2,1)S(1)}, bf16[144,768]{1,0:T(8,128)(2,1)S(1)}, u32[]{:S(2)}, u32[]{:S(2)}) collective-permute-start(bf16[144,768]{1,0:T(8,128)(2,1)S(1)} %collective-permute-done.8.refs_11_.refs_1_), channel_id=1, source_target_pairs={{0,8},{2,10},{4,12},{6,14},{8,0},{10,2},{12,4},{14,6},{16,24},{18,... | collective-permute-start | bytes 663560 | tf_op jit(solution)/shard_map/ppermute | solution.py:703
  20.3 10.2 %collective-permute-start.2 = (bf16[160,768]{1,0:T(8,128)(2,1)S(1)}, bf16[160,768]{1,0:T(8,128)(2,1)S(1)}, u32[]{:S(2)}, u32[]{:S(2)}) collective-permute-start(bf16[160,768]{1,0:T(8,128)(2,1)S(1)} %collective-permute-done.refs_5_.refs_8_), channel_id=1, source_target_pairs={{0,2},{2,0},{4,6},{6,4},{8,10},{10,8},{12,14},{14,12},{16,18},{18,... | collective-permute-start | bytes 737288 | tf_op jit(solution)/shard_map/ppermute | solution.py:703
  20.3 9.2 %collective-permute-start.1 = (bf16[160,768]{1,0:T(8,128)(2,1)S(1)}, bf16[160,768]{1,0:T(8,128)(2,1)S(1)}, u32[]{:S(2)}, u32[]{:S(2)}) collective-permute-start(bf16[160,768]{1,0:T(8,128)(2,1)S(1)} %collective-permute-done.refs_5_.refs_8_), channel_id=1, source_target_pairs={{0,8},{2,10},{4,12},{6,14},{8,0},{10,2},{12,4},{14,6},{16,24},{18,... | collective-permute-start | bytes 737288 | tf_op jit(solution)/shard_map/ppermute | solution.py:703
  21.2 12.6 %collective-permute-start.12 = (bf16[288,768]{1,0:T(8,128)(2,1)S(1)}, bf16[288,768]{1,0:T(8,128)(2,1)S(1)}, u32[]{:S(2)}, u32[]{:S(2)}) collective-permute-start(bf16[288,768]{1,0:T(8,128)(2,1)S(1)} %pack_down.1), channel_id=1, source_target_pairs={{0,1},{1,0},{2,3},{3,2},{4,5},{5,4},{6,7},{7,6},{8,9},{9,8},{10,11... | collective-permute-start | bytes 1327112 | tf_op jit(solution)/shard_map/ppermute | solution.py:703
  23.2 7.3 %collective-permute-start.5 = (bf16[144,768]{1,0:T(8,128)(2,1)S(1)}, bf16[144,768]{1,0:T(8,128)(2,1)S(1)}, u32[]{:S(2)}, u32[]{:S(2)}) collective-permute-start(bf16[144,768]{1,0:T(8,128)(2,1)S(1)} %collective-permute-done.4.refs_7_), channel_id=1, source_target_pairs={{0,4},{2,6},{4,0},{6,2},{8,12},{10,14},{12,8},{14,10},{16,20},{18,... | collective-permute-start | bytes 663560 | tf_op jit(solution)/shard_map/ppermute | solution.py:703
  26.1 4.9 %collective-permute-start.11 = (bf16[144,768]{1,0:T(8,128)(2,1)S(1)}, bf16[144,768]{1,0:T(8,128)(2,1)S(1)}, u32[]{:S(2)}, u32[]{:S(2)}) collective-permute-start(bf16[144,768]{1,0:T(8,128)(2,1)S(1)} %collective-permute-done.9.refs_12_), channel_id=1, source_target_pairs={{0,2},{2,0},{4,6},{6,4},{8,10},{10,8},{12,14},{14,12},{16,18},{18,... | collective-permute-start | bytes 663560 | tf_op jit(solution)/shard_map/ppermute | solution.py:703
  29.5 1.6 %collective-permute-start.3 = (bf16[160,768]{1,0:T(8,128)(2,1)S(1)}, bf16[160,768]{1,0:T(8,128)(2,1)S(1)}, u32[]{:S(2)}, u32[]{:S(2)}) collective-permute-start(bf16[160,768]{1,0:T(8,128)(2,1)S(1)} %collective-permute-done.1.refs_9_), channel_id=1, source_target_pairs={{0,2},{2,0},{4,6},{6,4},{8,10},{10,8},{12,14},{14,12},{16,18},{18,... | collective-permute-start | bytes 737288 | tf_op jit(solution)/shard_map/ppermute | solution.py:703
  30.5 3.8 %collective-permute-start.6 = (bf16[144,768]{1,0:T(8,128)(2,1)S(1)}, bf16[144,768]{1,0:T(8,128)(2,1)S(1)}, u32[]{:S(2)}, u32[]{:S(2)}) collective-permute-start(bf16[144,768]{1,0:T(8,128)(2,1)S(1)} %collective-permute-done.4.refs_7_), channel_id=1, source_target_pairs={{0,2},{2,0},{4,6},{6,4},{8,10},{10,8},{12,14},{14,12},{16,18},{18,... | collective-permute-start | bytes 663560 | tf_op jit(solution)/shard_map/ppermute | solution.py:703
  30.5 3.8 %collective-permute-start.10 = (bf16[144,768]{1,0:T(8,128)(2,1)S(1)}, bf16[144,768]{1,0:T(8,128)(2,1)S(1)}, u32[]{:S(2)}, u32[]{:S(2)}) collective-permute-start(bf16[144,768]{1,0:T(8,128)(2,1)S(1)} %collective-permute-done.8.refs_11_.refs_1_), channel_id=1, source_target_pairs={{0,2},{2,0},{4,6},{6,4},{8,10},{10,8},{12,14},{14,12},{16,18},{18,... | collective-permute-start | bytes 663560 | tf_op jit(solution)/shard_map/ppermute | solution.py:703
  31.0 3.3 %collective-permute-start.7 = (bf16[144,768]{1,0:T(8,128)(2,1)S(1)}, bf16[144,768]{1,0:T(8,128)(2,1)S(1)}, u32[]{:S(2)}, u32[]{:S(2)}) collective-permute-start(bf16[144,768]{1,0:T(8,128)(2,1)S(1)} %collective-permute-done.5.refs_8_), channel_id=1, source_target_pairs={{0,2},{2,0},{4,6},{6,4},{8,10},{10,8},{12,14},{14,12},{16,18},{18,... | collective-permute-start | bytes 663560 | tf_op jit(solution)/shard_map/ppermute | solution.py:703
  33.8 3.5 %collective-permute-start.13 = (bf16[288,768]{1,0:T(8,128)(2,1)S(1)}, bf16[288,768]{1,0:T(8,128)(2,1)S(1)}, u32[]{:S(2)}, u32[]{:S(2)}) collective-permute-start(bf16[288,768]{1,0:T(8,128)(2,1)S(1)} %pass_on.1.refs_5_), channel_id=1, source_target_pairs={{0,2},{2,0},{4,6},{6,4},{8,10},{10,8},{12,14},{14,12},{16,18},{18,... | collective-permute-start | bytes 1327112 | tf_op jit(solution)/shard_map/ppermute | solution.py:703
  37.1 3.5 %collective-permute-start.15 = (bf16[1,2,8,72,384]{4,3,2,1,0:T(8,128)(2,1)S(1)}, bf16[1,2,8,72,384]{4,3,2,1,0:T(8,128)(2,1)S(1)}, u32[]{:S(2)}, u32[]{:S(2)}) collective-permute-start(bf16[1,2,8,72,384]{4,3,2,1,0:T(8,128)(2,1)S(1)} %get-tuple-element.119), channel_id=1, source_target_pairs={{0,2},{2,0},{4,6},{6,4},{8,10},{10,8},{12,14},{14,12},{16,18},{18,... | collective-permute-start | bytes 2654216 | tf_op jit(solution)/shard_map/ppermute | solution.py:703
  40.0 5.1 %collective-permute-start.14 = (bf16[2,2,8,72,384]{4,3,2,1,0:T(8,128)(2,1)S(1)}, bf16[2,2,8,72,384]{4,3,2,1,0:T(8,128)(2,1)S(1)}, u32[]{:S(2)}, u32[]{:S(2)}) collective-permute-start(bf16[2,2,8,72,384]{4,3,2,1,0:T(8,128)(2,1)S(1)} %get-tuple-element.115), channel_id=1, source_target_pairs={{0,2},{2,0},{4,6},{6,4},{8,10},{10,8},{12,14},{14,12},{16,18},{18,... | collective-permute-start | bytes 5308424 | tf_op jit(solution)/shard_map/ppermute | solution.py:703
  40.8 13.1 %collective-permute-start.18 = (bf16[8,72,384]{2,1,0:T(8,128)(2,1)S(1)}, bf16[8,72,384]{2,1,0:T(8,128)(2,1)S(1)}, u32[]{:S(2)}, u32[]{:S(2)}) collective-permute-start(bf16[8,72,384]{2,1,0:T(8,128)(2,1)S(1)} %get-tuple-element.126), channel_id=1, source_target_pairs={{0,1},{1,0},{2,3},{3,2},{4,5},{5,4},{6,7},{7,6},{8,9},{9,8},{10,11... | collective-permute-start | bytes 1327112 | tf_op jit(solution)/shard_map/ppermute | solution.py:703
  45.7 13.1 %collective-permute-start.16 = (bf16[2,4,72,384]{3,2,1,0:T(8,128)(2,1)S(1)}, bf16[2,4,72,384]{3,2,1,0:T(8,128)(2,1)S(1)}, u32[]{:S(2)}, u32[]{:S(2)}) collective-permute-start(bf16[2,4,72,384]{3,2,1,0:T(8,128)(2,1)S(1)} %get-tuple-element.123), channel_id=1, source_target_pairs={{0,4},{2,6},{4,0},{6,2},{8,12},{10,14},{12,8},{14,10},{16,20},{18,... | collective-permute-start | bytes 1327112 | tf_op jit(solution)/shard_map/ppermute | solution.py:703
  47.3 11.9 %collective-permute-start.17 = (bf16[4,2,72,384]{3,2,1,0:T(8,128)(2,1)S(1)}, bf16[4,2,72,384]{3,2,1,0:T(8,128)(2,1)S(1)}, u32[]{:S(2)}, u32[]{:S(2)}) collective-permute-start(bf16[4,2,72,384]{3,2,1,0:T(8,128)(2,1)S(1)} %get-tuple-element.125), channel_id=1, source_target_pairs={{0,8},{2,10},{4,12},{6,14},{8,0},{10,2},{12,4},{14,6},{16,24},{18,... | collective-permute-start | bytes 1327112 | tf_op jit(solution)/shard_map/ppermute | solution.py:703
  54.0 9.1 %collective-permute-start.23 = (bf16[4,72,384]{2,1,0:T(8,128)(2,1)S(1)}, bf16[4,72,384]{2,1,0:T(8,128)(2,1)S(1)}, u32[]{:S(2)}, u32[]{:S(2)}) collective-permute-start(bf16[4,72,384]{2,1,0:T(8,128)(2,1)S(1)} %get-tuple-element.143), channel_id=1, source_target_pairs={{0,4},{2,6},{4,0},{6,2},{8,12},{10,14},{12,8},{14,10},{16,20},{18,... | collective-permute-start | bytes 663560 | tf_op jit(solution)/shard_map/ppermute | solution.py:703
  55.0 7.2 %collective-permute-start.21 = (bf16[1,2,8,80,384]{4,3,2,1,0:T(8,128)(2,1)S(1)}, bf16[1,2,8,80,384]{4,3,2,1,0:T(8,128)(2,1)S(1)}, u32[]{:S(2)}, u32[]{:S(2)}) collective-permute-start(bf16[1,2,8,80,384]{4,3,2,1,0:T(8,128)(2,1)S(1)} %get-tuple-element.140), channel_id=1, source_target_pairs={{0,2},{2,0},{4,6},{6,4},{8,10},{10,8},{12,14},{14,12},{16,18},{18,... | collective-permute-start | bytes 2949128 | tf_op jit(solution)/shard_map/ppermute | solution.py:703
  59.4 7.3 %collective-permute-start.19 = (bf16[2,2,72,384]{3,2,1,0:T(8,128)(2,1)S(1)}, bf16[2,2,72,384]{3,2,1,0:T(8,128)(2,1)S(1)}, u32[]{:S(2)}, u32[]{:S(2)}) collective-permute-start(bf16[2,2,72,384]{3,2,1,0:T(8,128)(2,1)S(1)} %get-tuple-element.136), channel_id=1, source_target_pairs={{0,8},{2,10},{4,12},{6,14},{8,0},{10,2},{12,4},{14,6},{16,24},{18,... | collective-permute-start | bytes 663560 | tf_op jit(solution)/shard_map/ppermute | solution.py:703
  61.0 6.4 %collective-permute-start.20 = (bf16[2,2,72,384]{3,2,1,0:T(8,128)(2,1)S(1)}, bf16[2,2,72,384]{3,2,1,0:T(8,128)(2,1)S(1)}, u32[]{:S(2)}, u32[]{:S(2)}) collective-permute-start(bf16[2,2,72,384]{3,2,1,0:T(8,128)(2,1)S(1)} %get-tuple-element.138), channel_id=1, source_target_pairs={{0,4},{2,6},{4,0},{6,2},{8,12},{10,14},{12,8},{14,10},{16,20},{18,... | collective-permute-start | bytes 663560 | tf_op jit(solution)/shard_map/ppermute | solution.py:703
  62.4 11.0 %collective-permute-start.22 = (bf16[8,80,384]{2,1,0:T(8,128)(2,1)S(1)}, bf16[8,80,384]{2,1,0:T(8,128)(2,1)S(1)}, u32[]{:S(2)}, u32[]{:S(2)}) collective-permute-start(bf16[8,80,384]{2,1,0:T(8,128)(2,1)S(1)} %get-tuple-element.142), channel_id=1, source_target_pairs={{0,1},{1,0},{2,3},{3,2},{4,5},{5,4},{6,7},{7,6},{8,9},{9,8},{10,11... | collective-permute-start | bytes 1474568 | tf_op jit(solution)/shard_map/ppermute | solution.py:703
  63.1 4.9 %collective-permute-start.24 = (bf16[2,72,384]{2,1,0:T(8,128)(2,1)S(1)}, bf16[2,72,384]{2,1,0:T(8,128)(2,1)S(1)}, u32[]{:S(2)}, u32[]{:S(2)}) collective-permute-start(bf16[2,72,384]{2,1,0:T(8,128)(2,1)S(1)} %get-tuple-element.145), channel_id=1, source_target_pairs={{0,8},{2,10},{4,12},{6,14},{8,0},{10,2},{12,4},{14,6},{16,24},{18,... | collective-permute-start | bytes 331784 | tf_op jit(solution)/shard_map/ppermute | solution.py:703
  73.6 9.6 %collective-permute-start.27 = (bf16[4,80,384]{2,1,0:T(8,128)(2,1)S(1)}, bf16[4,80,384]{2,1,0:T(8,128)(2,1)S(1)}, u32[]{:S(2)}, u32[]{:S(2)}) collective-permute-start(bf16[4,80,384]{2,1,0:T(8,128)(2,1)S(1)} %get-tuple-element.152), channel_id=1, source_target_pairs={{0,4},{2,6},{4,0},{6,2},{8,12},{10,14},{12,8},{14,10},{16,20},{18,... | collective-permute-start | bytes 737288 | tf_op jit(solution)/shard_map/ppermute | solution.py:703
  75.1 8.1 %collective-permute-start.26 = (bf16[3,72,384]{2,1,0:T(8,128)(2,1)S(1)}, bf16[3,72,384]{2,1,0:T(8,128)(2,1)S(1)}, u32[]{:S(2)}, u32[]{:S(2)}) collective-permute-start(bf16[3,72,384]{2,1,0:T(8,128)(2,1)S(1)} %get-tuple-element.149), channel_id=1, source_target_pairs={{0,16},{2,18},{4,20},{6,22},{8,24},{10,26},{12,28},{14,30},{16,0},... | collective-permute-start | bytes 497672 | tf_op jit(solution)/shard_map/ppermute | solution.py:703
  77.7 4.7 %collective-permute-start.25 = (bf16[2,72,384]{2,1,0:T(8,128)(2,1)S(1)}, bf16[2,72,384]{2,1,0:T(8,128)(2,1)S(1)}, u32[]{:S(2)}, u32[]{:S(2)}) collective-permute-start(bf16[2,72,384]{2,1,0:T(8,128)(2,1)S(1)} %get-tuple-element.147), channel_id=1, source_target_pairs={{0,1},{1,0},{2,3},{3,2},{4,5},{5,4},{6,7},{7,6},{8,9},{9,8},{10,11... | collective-permute-start | bytes 331784 | tf_op jit(solution)/shard_map/ppermute | solution.py:703
  83.3 7.0 %collective-permute-start.30 = (bf16[2,80,384]{2,1,0:T(8,128)(2,1)S(1)}, bf16[2,80,384]{2,1,0:T(8,128)(2,1)S(1)}, u32[]{:S(2)}, u32[]{:S(2)}) collective-permute-start(bf16[2,80,384]{2,1,0:T(8,128)(2,1)S(1)} %get-tuple-element.157), channel_id=1, source_target_pairs={{0,8},{2,10},{4,12},{6,14},{8,0},{10,2},{12,4},{14,6},{16,24},{18,... | collective-permute-start | bytes 368648 | tf_op jit(solution)/shard_map/ppermute | solution.py:703
  83.3 6.9 %collective-permute-start.28 = (bf16[2,72,384]{2,1,0:T(8,128)(2,1)S(1)}, bf16[2,72,384]{2,1,0:T(8,128)(2,1)S(1)}, u32[]{:S(2)}, u32[]{:S(2)}) collective-permute-start(bf16[2,72,384]{2,1,0:T(8,128)(2,1)S(1)} %get-tuple-element.153.refs_0_), channel_id=1, source_target_pairs={{0,16},{2,18},{4,20},{6,22},{8,24},{10,26},{12,28},{14,30},{16,0},... | collective-permute-start | bytes 331784 | tf_op jit(solution)/shard_map/ppermute | solution.py:703
  86.1 4.2 %collective-permute-start.29 = (bf16[72,384]{1,0:T(8,128)(2,1)S(1)}, bf16[72,384]{1,0:T(8,128)(2,1)S(1)}, u32[]{:S(2)}, u32[]{:S(2)}) collective-permute-start(bf16[72,384]{1,0:T(8,128)(2,1)S(1)} %get-tuple-element.155), channel_id=1, source_target_pairs={{0,1},{1,0},{2,3},{3,2},{4,5},{5,4},{6,7},{7,6},{8,9},{9,8},{10,11... | collective-permute-start | bytes 165896 | tf_op jit(solution)/shard_map/ppermute | solution.py:703
  90.3 10.9 %copy-start.1 = (f32[768,576]{0,1:T(8,128)S(1)}, f32[768,576]{0,1:T(8,128)}, u32[]{:S(2)}) copy-start(f32[768,576]{0,1:T(8,128)} %param.30) | copy-start | bytes 5308420
  90.3 10.9 %copy-start.2 = (f32[768,576]{0,1:T(8,128)S(1)}, f32[768,576]{0,1:T(8,128)}, u32[]{:S(2)}) copy-start(f32[768,576]{0,1:T(8,128)} %param.35) | copy-start | bytes 5308420
  90.3 10.9 %copy-start.7 = (f32[288,960]{1,0:T(8,128)S(1)}, f32[288,960]{1,0:T(8,128)}, u32[]{:S(2)}) copy-start(f32[288,960]{1,0:T(8,128)} %refs_2_.9) | copy-start | bytes 3317764
  90.5 10.7 %collective-permute-start.31 = (bf16[3,80,384]{2,1,0:T(8,128)(2,1)S(1)}, bf16[3,80,384]{2,1,0:T(8,128)(2,1)S(1)}, u32[]{:S(2)}, u32[]{:S(2)}) collective-permute-start(bf16[3,80,384]{2,1,0:T(8,128)(2,1)S(1)} %get-tuple-element.158.refs_0_), channel_id=1, source_target_pairs={{0,16},{2,18},{4,20},{6,22},{8,24},{10,26},{12,28},{14,30},{16,0},... | collective-permute-start | bytes 552968 | tf_op jit(solution)/shard_map/ppermute | solution.py:703
  93.3 7.9 %collective-permute-start.32 = (bf16[2,72,384]{2,1,0:T(8,128)(2,1)S(1)}, bf16[2,72,384]{2,1,0:T(8,128)(2,1)S(1)}, u32[]{:S(2)}, u32[]{:S(2)}) collective-permute-start(bf16[2,72,384]{2,1,0:T(8,128)(2,1)S(1)} %get-tuple-element.160.refs_3_), channel_id=1, source_target_pairs={{0,8},{2,10},{4,12},{6,14},{8,0},{10,2},{12,4},{14,6},{16,24},{18,... | collective-permute-start | bytes 331784 | tf_op jit(solution)/shard_map/ppermute | solution.py:703
  101.4 9.1 %collective-permute-start.34 = (bf16[3,2,72,384]{3,2,1,0:T(8,128)(2,1)S(1)}, bf16[3,2,72,384]{3,2,1,0:T(8,128)(2,1)S(1)}, u32[]{:S(2)}, u32[]{:S(2)}) collective-permute-start(bf16[3,2,72,384]{3,2,1,0:T(8,128)(2,1)S(1)} %get-tuple-element.161.refs_3_.refs_0_), channel_id=1, source_target_pairs={{0,4},{2,6},{4,0},{6,2},{8,12},{10,14},{12,8},{14,10},{16,20},{18,... | collective-permute-start | bytes 995336 | tf_op jit(solution)/shard_map/ppermute | solution.py:703
  103.7 5.5 %collective-permute-start.33 = (bf16[80,384]{1,0:T(8,128)(2,1)S(1)}, bf16[80,384]{1,0:T(8,128)(2,1)S(1)}, u32[]{:S(2)}, u32[]{:S(2)}) collective-permute-start(bf16[80,384]{1,0:T(8,128)(2,1)S(1)} %get-tuple-element.163.refs_0_), channel_id=1, source_target_pairs={{0,16},{2,18},{4,20},{6,22},{8,24},{10,26},{12,28},{14,30},{16,0},... | collective-permute-start | bytes 184328 | tf_op jit(solution)/shard_map/ppermute | solution.py:703
  104.7 5.5 %collective-permute-start.35 = (bf16[2,72,384]{2,1,0:T(8,128)(2,1)S(1)}, bf16[2,72,384]{2,1,0:T(8,128)(2,1)S(1)}, u32[]{:S(2)}, u32[]{:S(2)}) collective-permute-start(bf16[2,72,384]{2,1,0:T(8,128)(2,1)S(1)} %get-tuple-element.164.refs_2_), channel_id=1, source_target_pairs={{0,8},{2,10},{4,12},{6,14},{8,0},{10,2},{12,4},{14,6},{16,24},{18,... | collective-permute-start | bytes 331784 | tf_op jit(solution)/shard_map/ppermute | solution.py:703
  110.6 8.9 %collective-permute-start.40 = (bf16[2,2,72,384]{3,2,1,0:T(8,128)(2,1)S(1)}, bf16[2,2,72,384]{3,2,1,0:T(8,128)(2,1)S(1)}, u32[]{:S(2)}, u32[]{:S(2)}) collective-permute-start(bf16[2,2,72,384]{3,2,1,0:T(8,128)(2,1)S(1)} %get-tuple-element.166.refs_2_), channel_id=1, source_target_pairs={{0,4},{2,6},{4,0},{6,2},{8,12},{10,14},{12,8},{14,10},{16,20},{18,... | collective-permute-start | bytes 663560 | tf_op jit(solution)/shard_map/ppermute | solution.py:703
  112.4 7.9 %collective-permute-start.39 = (bf16[2,2,72,384]{3,2,1,0:T(8,128)(2,1)S(1)}, bf16[2,2,72,384]{3,2,1,0:T(8,128)(2,1)S(1)}, u32[]{:S(2)}, u32[]{:S(2)}) collective-permute-start(bf16[2,2,72,384]{3,2,1,0:T(8,128)(2,1)S(1)} %get-tuple-element.165.refs_2_.refs_0_), channel_id=1, source_target_pairs={{0,8},{2,10},{4,12},{6,14},{8,0},{10,2},{12,4},{14,6},{16,24},{18,... | collective-permute-start | bytes 663560 | tf_op jit(solution)/shard_map/ppermute | solution.py:703
  112.5 2.8 %collective-permute-start.41 = (bf16[1,2,4,72,384]{4,3,2,1,0:T(8,128)(2,1)S(1)}, bf16[1,2,4,72,384]{4,3,2,1,0:T(8,128)(2,1)S(1)}, u32[]{:S(2)}, u32[]{:S(2)}) collective-permute-start(bf16[1,2,4,72,384]{4,3,2,1,0:T(8,128)(2,1)S(1)} %get-tuple-element.167.refs_0_), channel_id=1, source_target_pairs={{0,2},{2,0},{4,6},{6,4},{8,10},{10,8},{12,14},{14,12},{16,18},{18,... | collective-permute-start | bytes 1327112 | tf_op jit(solution)/shard_map/ppermute | solution.py:703
  112.5 11.2 %collective-permute-start.38 = (bf16[2,80,384]{2,1,0:T(8,128)(2,1)S(1)}, bf16[2,80,384]{2,1,0:T(8,128)(2,1)S(1)}, u32[]{:S(2)}, u32[]{:S(2)}) collective-permute-start(bf16[2,80,384]{2,1,0:T(8,128)(2,1)S(1)} %share_qkv_out_high.1.refs_5_.refs_0_), channel_id=1, source_target_pairs={{0,12},{2,14},{4,8},{6,10},{8,4},{10,6},{12,0},{14,2},{16,28},{18,... | collective-permute-start | bytes 368648 | tf_op jit(solution)/shard_map/ppermute | solution.py:703
  114.2 9.6 %collective-permute-start.37 = (bf16[2,80,384]{2,1,0:T(8,128)(2,1)S(1)}, bf16[2,80,384]{2,1,0:T(8,128)(2,1)S(1)}, u32[]{:S(2)}, u32[]{:S(2)}) collective-permute-start(bf16[2,80,384]{2,1,0:T(8,128)(2,1)S(1)} %share_qkv_out_high.1.refs_5_.refs_0_), channel_id=1, source_target_pairs={{0,8},{2,10},{4,12},{6,14},{8,0},{10,2},{12,4},{14,6},{16,24},{18,... | collective-permute-start | bytes 368648 | tf_op jit(solution)/shard_map/ppermute | solution.py:703
  115.4 8.4 %collective-permute-start.36 = (bf16[2,80,384]{2,1,0:T(8,128)(2,1)S(1)}, bf16[2,80,384]{2,1,0:T(8,128)(2,1)S(1)}, u32[]{:S(2)}, u32[]{:S(2)}) collective-permute-start(bf16[2,80,384]{2,1,0:T(8,128)(2,1)S(1)} %share_qkv_out_high.1.refs_5_.refs_0_), channel_id=1, source_target_pairs={{0,4},{2,6},{4,0},{6,2},{8,12},{10,14},{12,8},{14,10},{16,20},{18,... | collective-permute-start | bytes 368648 | tf_op jit(solution)/shard_map/ppermute | solution.py:703
  120.3 4.1 %collective-permute-start.43 = (bf16[2,2,4,72,384]{4,3,2,1,0:T(8,128)(2,1)S(1)}, bf16[2,2,4,72,384]{4,3,2,1,0:T(8,128)(2,1)S(1)}, u32[]{:S(2)}, u32[]{:S(2)}) collective-permute-start(bf16[2,2,4,72,384]{4,3,2,1,0:T(8,128)(2,1)S(1)} %share_gate_up.1.refs_0_), channel_id=1, source_target_pairs={{0,2},{2,0},{4,6},{6,4},{8,10},{10,8},{12,14},{14,12},{16,18},{18,... | collective-permute-start | bytes 2654216 | tf_op jit(solution)/shard_map/ppermute | solution.py:703
  123.9 3.9 %collective-permute-start.42 = (bf16[1,2,4,80,384]{4,3,2,1,0:T(8,128)(2,1)S(1)}, bf16[1,2,4,80,384]{4,3,2,1,0:T(8,128)(2,1)S(1)}, u32[]{:S(2)}, u32[]{:S(2)}) collective-permute-start(bf16[1,2,4,80,384]{4,3,2,1,0:T(8,128)(2,1)S(1)} %share_qkv_out.1.refs_7_.refs_0_), channel_id=1, source_target_pairs={{0,2},{2,0},{4,6},{6,4},{8,10},{10,8},{12,14},{14,12},{16,18},{18,... | collective-permute-start | bytes 1474568 | tf_op jit(solution)/shard_map/ppermute | solution.py:703
  (20 other events, 167.3 us)

commit v12 on v11

--- a/solution.py
+++ b/solution.py
@@ -590,7 +590,7 @@
     keep_ref[...] = low
 
 
-def add_step(jobs, name, after):
+def add_step(jobs, name, after, busy=20):
     arrays, outs = [], []
     for keep, arrived, axis in jobs:
         arrays += [keep, arrived]
@@ -601,7 +601,7 @@
         for i, (_, _, axis) in enumerate(jobs):
             add_split(ins[2 * i], ins[2 * i + 1], axis, out_refs[2 * i], out_refs[2 * i + 1])
 
-    flat = step(body, arrays, outs, name, after)
+    flat = step(body, arrays, outs, name, after, busy)
     return [(flat[2 * i], flat[2 * i + 1]) for i in range(len(jobs))]
 
 
@@ -874,21 +874,22 @@
             [(cut(keep_down, 2, 4), cut(arrived_down, 2, 4), 0)], "down_y", (grad_qkv_out[2],)
         )
         arrived_down = over_x(send)
+        ((send, keep_qkv_out),) = add_step(
+            [(grad_qkv_out[1][0], arrived_qkv_out[0], 0)], "qkv_out_core", (keep_down,), 0.1
+        )
+        arrived_qkv_out = over_y(send)
         (send_up, keep_up), (send_low, keep_low) = add_step(
             [
                 (cut(keep_up, 2, 2, 2), cut(arrived_up, 2, 2, 2), 1),
                 (cut(keep_low, 2, 2, 2), cut(arrived_low, 2, 2, 2), 1),
             ],
             "up_x_low_z",
-            (keep_down,),
+            (keep_qkv_out,),
+            20,
         )
         arrived_up, arrived_low = over_z_low(send_up), over_x(send_low)
-        ((send, keep_qkv_out),) = add_step(
-            [(grad_qkv_out[1][0], arrived_qkv_out[0], 0)], "qkv_out_core", (keep_up,)
-        )
-        arrived_qkv_out = over_y(send)
         ((send, keep_down),) = add_step(
-            [(cut(keep_down, 2, 2), cut(arrived_down, 2, 2), 0)], "down_x", (keep_qkv_out,)
+            [(cut(keep_down, 2, 2), cut(arrived_down, 2, 2), 0)], "down_x", (keep_up,), 0.1
         )
         arrived_down = over_z_low(send)
 
@@ -900,29 +901,28 @@
             outs[2][0], outs[2][1] = total[0, 1].astype(BF16), total[1, 1].astype(BF16)
             outs[3][...] = total[:, 0]
             total = ins[4][...] + ins[5][...].astype(F32)
-            outs[4][...] = total[1].astype(BF16)
-            outs[5][...] = total[0]
-            total = ins[6][...] + ins[7][...].astype(F32)
             outs[2][2] = total[1].astype(BF16)
-            outs[6][...] = total[0]
-
-        send_up, keep_up, send, keep_low, send_qkv_out, keep_qkv_out, keep_down = step(
+            outs[4][...] = total[0]
+
+        ((send, keep_qkv_out),) = add_step(
+            [(cut(keep_qkv_out, 2, 4), cut(arrived_qkv_out, 2, 4), 0)],
+            "qkv_out_y",
+            (keep_down,),
+            0.1,
+        )
+        arrived_qkv_out = over_x(send)
+        send_up, keep_up, send, keep_low, keep_down = step(
             columns,
-            [
-                *(keep_up, arrived_up, keep_low, arrived_low),
-                *(cut(keep_qkv_out, 2, 4), cut(arrived_qkv_out, 2, 4)),
-                *(keep_down, arrived_down),
-            ],
+            [keep_up, arrived_up, keep_low, arrived_low, keep_down, arrived_down],
             [
                 *(sds((2, *piece), BF16), sds((2, *piece), F32)),
                 *(sds((3, *piece), BF16), sds((2, *piece), F32)),
-                *(sds((4, *taller), BF16), sds((4, *taller), F32)),
                 sds(piece, F32),
             ],
             "columns",
-        )
-        arrived_up, arrived_qkv_out = over_y(send_up), over_x(send_qkv_out)
-        arrived = over_z_high(send)
+            (keep_qkv_out,),
+        )
+        arrived_up, arrived = over_y(send_up), over_z_high(send)
 
         def planes(ins, outs):
             keep_up, arrived_up, keep_low, arrived, keep_down, keep_qkv_out, arrived_qkv_out = ins

time: 132 us -> 129 us (0.977)
  starting transfers between devices: 48.7 us -> 42.5 us
  waiting for transfers between devices: 44.6 us -> 47.3 us
    ppermute x44, starting transfers between devices: 48.7 us -> 42.5 us  [swap(): return lax.ppermute(values, axis, [(i, i ^ mask) for i in range(size)])]
    ppermute x44, waiting for transfers between devices: 44.6 us -> 47.3 us  [swap(): return lax.ppermute(values, axis, [(i, i ^ mask) for i in range(size)])]
    pallas_call x17 -> x18, Pallas kernels: 3.32 us -> 3.25 us  [step(): pl.pallas_call(kernel, out_shape=tuple(outs), in_specs=[pl.BlockSpec(memo...]
  transfers between devices with their start and end apart: 44 -> 44, of which waited for: 20 -> 20; matrix products, arithmetic and copies ran while one was open for 0% -> 0% of each run, Pallas kernels for 22% -> 23%
where the time goes in v12:
time: 129 us
  waiting for transfers between devices  47.3 us (37%)
  starting transfers between devices  42.5 us (33%)
  Pallas kernels  36.3 us (28%)
  between operations  1.38 us (1%)
    ppermute x44, waiting for transfers between devices, swap(): return lax.ppermute(values, axis, [(i, i ^ mask) for i in range(size)])  47.3 us
    ppermute x44, starting transfers between devices, swap(): return lax.ppermute(values, axis, [(i, i ^ mask) for i in range(size)])  42.5 us
    pallas_call x5, Pallas kernels, call(): pl.pallas_call(kernel, out_shape=tuple(outs), in_specs=[pl.BlockSpec(memo...  15.7 us
    pallas_call x4, Pallas kernels, update_rows(): pl.pallas_call(kernel, out_shape=tuple((sds(a.shape, F32) for a in [*stat...  14.3 us
    pallas_call x18, Pallas kernels, step(): pl.pallas_call(kernel, out_shape=tuple(outs), in_specs=[pl.BlockSpec(memo...  3.25 us
    pallas_call x2, Pallas kernels, pack_kernel(): pl.pallas_call(kernel, out_shape=tuple(outs), in_specs=[pl.BlockSpec(memo...  2.97 us
  transfers between devices with their start and end apart: 44, of which 20 were waited for; matrix products, arithmetic and copies ran while one was open for 0% of the time, Pallas kernels for 23%

profile of v12, /device:TPU:0, one launch (start us, length us, event | category | flops | bytes accessed | tf_op | source)
XLA Modules:
  0.0 128.8 jit_solution(15585143707062513649)
XLA Ops:
  1.4 2.2 %pack_first.1 = (bf16[160,768]{1,0:T(8,128)(2,1)S(1)}, bf16[144,768]{1,0:T(8,128)(2,1)S(1)}, bf16[144,768]{1,0:T(8,128)(2,1)S(1)}) custom-call(s32[4]{0:T(128)S(1)} %pad_add_fusion.idx_ref.refs_0_, f32[288,960]{1,0:T(8,128)} %refs_2_.9, f32[288,576]{1,0:T(8,128)} %refs_3_.8, f32[2,288]{1,0:T(2,128)S(1)} %copy-done.16, f32[288,3072]{1,0:T(8,128)} %refs_1_.5, ...), custom_call_target="tpu_custom_call" | custom-call | flops 10000000000 | tf_op jit(solution)/shard_map/pack_first/pallas_call | solution.py:242
  3.6 3.0 %collective-permute-start = (bf16[160,768]{1,0:T(8,128)(2,1)S(1)}, bf16[160,768]{1,0:T(8,128)(2,1)S(1)}, u32[]{:S(2)}, u32[]{:S(2)}) collective-permute-start(bf16[160,768]{1,0:T(8,128)(2,1)S(1)} %get-tuple-element.103), channel_id=1, source_target_pairs={{0,1},{1,0},{2,3},{3,2},{4,5},{5,4},{6,7},{7,6},{8,9},{9,8},{10,11... | collective-permute-start | bytes 737288 | tf_op jit(solution)/shard_map/ppermute | solution.py:703
  6.7 1.9 %collective-permute-start.4 = (bf16[144,768]{1,0:T(8,128)(2,1)S(1)}, bf16[144,768]{1,0:T(8,128)(2,1)S(1)}, u32[]{:S(2)}, u32[]{:S(2)}) collective-permute-start(bf16[144,768]{1,0:T(8,128)(2,1)S(1)} %get-tuple-element.107), channel_id=1, source_target_pairs={{0,1},{1,0},{2,3},{3,2},{4,5},{5,4},{6,7},{7,6},{8,9},{9,8},{10,11... | collective-permute-start | bytes 663560 | tf_op jit(solution)/shard_map/ppermute | solution.py:703
  8.7 9.5 %collective-permute-done.8.refs_11_.refs_1_ = bf16[144,768]{1,0:T(8,128)(2,1)S(1)} collective-permute-done((bf16[144,768]{1,0:T(8,128)(2,1)S(1)}, bf16[144,768]{1,0:T(8,128)(2,1)S(1)}, u32[]{:S(2)}, u32[]{:S(2)}) %collective-permute-start.8) | collective-permute-done | bytes 221216 | tf_op jit(solution)/shard_map/ppermute | solution.py:703
  18.2 2.1 %collective-permute-start.9 = (bf16[144,768]{1,0:T(8,128)(2,1)S(1)}, bf16[144,768]{1,0:T(8,128)(2,1)S(1)}, u32[]{:S(2)}, u32[]{:S(2)}) collective-permute-start(bf16[144,768]{1,0:T(8,128)(2,1)S(1)} %collective-permute-done.8.refs_11_.refs_1_), channel_id=1, source_target_pairs={{0,8},{2,10},{4,12},{6,14},{8,0},{10,2},{12,4},{14,6},{16,24},{18,... | collective-permute-start | bytes 663560 | tf_op jit(solution)/shard_map/ppermute | solution.py:703
  21.2 2.0 %collective-permute-start.12 = (bf16[288,768]{1,0:T(8,128)(2,1)S(1)}, bf16[288,768]{1,0:T(8,128)(2,1)S(1)}, u32[]{:S(2)}, u32[]{:S(2)}) collective-permute-start(bf16[288,768]{1,0:T(8,128)(2,1)S(1)} %pack_down.1), channel_id=1, source_target_pairs={{0,1},{1,0},{2,3},{3,2},{4,5},{5,4},{6,7},{7,6},{8,9},{9,8},{10,11... | collective-permute-start | bytes 1327112 | tf_op jit(solution)/shard_map/ppermute | solution.py:703
  23.2 1.5 %collective-permute-start.5 = (bf16[144,768]{1,0:T(8,128)(2,1)S(1)}, bf16[144,768]{1,0:T(8,128)(2,1)S(1)}, u32[]{:S(2)}, u32[]{:S(2)}) collective-permute-start(bf16[144,768]{1,0:T(8,128)(2,1)S(1)} %collective-permute-done.4.refs_7_), channel_id=1, source_target_pairs={{0,4},{2,6},{4,0},{6,2},{8,12},{10,14},{12,8},{14,10},{16,20},{18,... | collective-permute-start | bytes 663560 | tf_op jit(solution)/shard_map/ppermute | solution.py:703
  24.7 1.4 %collective-permute-done.9.refs_12_ = bf16[144,768]{1,0:T(8,128)(2,1)S(1)} collective-permute-done((bf16[144,768]{1,0:T(8,128)(2,1)S(1)}, bf16[144,768]{1,0:T(8,128)(2,1)S(1)}, u32[]{:S(2)}, u32[]{:S(2)}) %collective-permute-start.9) | collective-permute-done | bytes 221216 | tf_op jit(solution)/shard_map/ppermute | solution.py:703
  26.1 3.4 %collective-permute-done.1.refs_9_ = bf16[160,768]{1,0:T(8,128)(2,1)S(1)} collective-permute-done((bf16[160,768]{1,0:T(8,128)(2,1)S(1)}, bf16[160,768]{1,0:T(8,128)(2,1)S(1)}, u32[]{:S(2)}, u32[]{:S(2)}) %collective-permute-start.1) | collective-permute-done | bytes 245792 | tf_op jit(solution)/shard_map/ppermute | solution.py:703
  29.5 1.0 collective-permute-done.5.refs_8_
  31.2 2.5 %attention.1 = (bf16[128,960]{1,0:T(8,128)(2,1)S(1)}, bf16[128,576]{1,0:T(8,128)(2,1)S(1)}, f32[128,128]{1,0:T(8,128)S(1)}, f32[128,128]{1,0:T(8,128)S(1)}, f32[...) custom-call(s32[4]{0:T(128)S(1)} %pad_add_fusion.idx_ref.refs_0_, ...), custom_call_target="tpu_custom_call" | custom-call | flops 1000000000 | tf_op jit(solution)/shard_map/attention/pallas_call | solution.py:152
  34.3 2.8 %feed_forward.1 = (f32[128,576]{1,0:T(8,128)S(1)}, bf16[128,576]{1,0:T(8,128)(2,1)S(1)}, f32[128,3072]{1,0:T(8,128)S(1)}, bf16[128,1536]{1,0:T(8,128)(2,1)S(1)},...) custom-call(s32[4]{0:T(128)S(1)} %pad_add_fusion.idx_ref.refs_0_, ...), custom_call_target="tpu_custom_call" | custom-call | flops 5000000000 | tf_op jit(solution)/shard_map/feed_forward/pallas_call | solution.py:152
  37.4 2.6 %feed_back.1 = (bf16[128,3072]{1,0:T(8,128)(2,1)S(1)}, bf16[2,2,8,72,384]{4,3,2,1,0:T(8,128)(2,1)S(1)}, bf16[2,2,8,72,384]{4,3,2,1,0:T(8,128)(2,1)S(1)}, bf16[576,1536]{1,0:T(8,128)(2,1)S(1)}) custom-call(s32[4]{0:T(128)S(1)} %pad_add_fusion.idx_ref.refs_0_, f32[128,3072]{1,0:T(8,128)S(1)} %get-tuple-element.111.refs_1_, ...), custom_call_target="tpu_custom_call" | custom-call | flops 20000000000 | tf_op jit(solution)/shard_map/feed_back/pallas_call | solution.py:152
  40.8 1.6 %collective-permute-start.19 = (bf16[8,72,384]{2,1,0:T(8,128)(2,1)S(1)}, bf16[8,72,384]{2,1,0:T(8,128)(2,1)S(1)}, u32[]{:S(2)}, u32[]{:S(2)}) collective-permute-start(bf16[8,72,384]{2,1,0:T(8,128)(2,1)S(1)} %get-tuple-element.134), channel_id=1, source_target_pairs={{0,1},{1,0},{2,3},{3,2},{4,5},{5,4},{6,7},{7,6},{8,9},{9,8},{10,11... | collective-permute-start | bytes 1327112 | tf_op jit(solution)/shard_map/ppermute | solution.py:703
  42.4 2.7 %middle_back.1 = (f32[128,576]{1,0:T(8,128)S(1)}, bf16[128,576]{1,0:T(8,128)(2,1)S(1)}, f32[1,576]{1,0:T(1,128)S(1)}) custom-call(s32[4]{0:T(128)S(1)} %pad_add_fusion.idx_ref.refs_0_, bf16[576,128]{1,0:T(8,128)(2,1)S(1)} %bitcast.68, f32[128,576]{1,0:T(8,128)S(1)} %get-tuple-element.109.refs_2_.refs_0_, ...), custom_call_target="tpu_custom_call" | custom-call | flops 20000000000 | tf_op jit(solution)/shard_map/middle_back/pallas_call | solution.py:152
  45.7 1.6 %collective-permute-start.16 = (bf16[2,4,72,384]{3,2,1,0:T(8,128)(2,1)S(1)}, bf16[2,4,72,384]{3,2,1,0:T(8,128)(2,1)S(1)}, u32[]{:S(2)}, u32[]{:S(2)}) collective-permute-start(bf16[2,4,72,384]{3,2,1,0:T(8,128)(2,1)S(1)} %get-tuple-element.123), channel_id=1, source_target_pairs={{0,4},{2,6},{4,0},{6,2},{8,12},{10,14},{12,8},{14,10},{16,20},{18,... | collective-permute-start | bytes 1327112 | tf_op jit(solution)/shard_map/ppermute | solution.py:703
  47.3 1.6 %collective-permute-start.17 = (bf16[4,2,72,384]{3,2,1,0:T(8,128)(2,1)S(1)}, bf16[4,2,72,384]{3,2,1,0:T(8,128)(2,1)S(1)}, u32[]{:S(2)}, u32[]{:S(2)}) collective-permute-start(bf16[4,2,72,384]{3,2,1,0:T(8,128)(2,1)S(1)} %get-tuple-element.125), channel_id=1, source_target_pairs={{0,8},{2,10},{4,12},{6,14},{8,0},{10,2},{12,4},{14,6},{16,24},{18,... | collective-permute-start | bytes 1327112 | tf_op jit(solution)/shard_map/ppermute | solution.py:703
  48.9 5.1 %attention_back.1 = (bf16[576,128]{1,0:T(8,128)(2,1)}, bf16[1,2,8,80,384]{4,3,2,1,0:T(8,128)(2,1)S(1)}, bf16[1,2,8,80,384]{4,3,2,1,0:T(8,128)(2,1)S(1)}, f32[8,128]{1,0:T(8,128)S(1)}) custom-call(s32[4]{0:T(128)S(1)} %pad_add_fusion.idx_ref.refs_0_, bf16[576,128]{1,0:T(8,128)(2,1)S(1)} %bitcast.71, f32[128,576]{1,0:T(8,128)S(1)} %get-tuple-element.121.refs_4_.refs_2_, ...), custom_call_target="tpu_custom_call" | custom-call | flops 20000000000 | tf_op jit(solution)/shard_map/attention_back/pallas_call | solution.py:152
  54.0 0.9 collective-permute-start.22
  55.0 1.5 %collective-permute-done.18 = bf16[1,2,8,80,384]{4,3,2,1,0:T(8,128)(2,1)S(1)} collective-permute-done((bf16[1,2,8,80,384]{4,3,2,1,0:T(8,128)(2,1)S(1)}, bf16[1,2,8,80,384]{4,3,2,1,0:T(8,128)(2,1)S(1)}, u32[]{:S(2)}, u32[]{:S(2)}) %collective-permute-start.18) | collective-permute-done | bytes 983072 | tf_op jit(solution)/shard_map/ppermute | solution.py:703
  57.3 1.3 %collective-permute-done.16 = bf16[2,4,72,384]{3,2,1,0:T(8,128)(2,1)S(1)} collective-permute-done((bf16[2,4,72,384]{3,2,1,0:T(8,128)(2,1)S(1)}, bf16[2,4,72,384]{3,2,1,0:T(8,128)(2,1)S(1)}, u32[]{:S(2)}, u32[]{:S(2)}) %collective-permute-start.16) | collective-permute-done | bytes 442400 | tf_op jit(solution)/shard_map/ppermute | solution.py:703
  59.3 1.6 %collective-permute-start.20 = (bf16[2,2,72,384]{3,2,1,0:T(8,128)(2,1)S(1)}, bf16[2,2,72,384]{3,2,1,0:T(8,128)(2,1)S(1)}, u32[]{:S(2)}, u32[]{:S(2)}) collective-permute-start(bf16[2,2,72,384]{3,2,1,0:T(8,128)(2,1)S(1)} %get-tuple-element.139), channel_id=1, source_target_pairs={{0,8},{2,10},{4,12},{6,14},{8,0},{10,2},{12,4},{14,6},{16,24},{18,... | collective-permute-start | bytes 663560 | tf_op jit(solution)/shard_map/ppermute | solution.py:703
  61.0 1.2 collective-permute-start.21
  62.1 1.0 collective-permute-done.22
  63.2 2.1 %collective-permute-start.23 = (bf16[2,72,384]{2,1,0:T(8,128)(2,1)S(1)}, bf16[2,72,384]{2,1,0:T(8,128)(2,1)S(1)}, u32[]{:S(2)}, u32[]{:S(2)}) collective-permute-start(bf16[2,72,384]{2,1,0:T(8,128)(2,1)S(1)} %get-tuple-element.144), channel_id=1, source_target_pairs={{0,8},{2,10},{4,12},{6,14},{8,0},{10,2},{12,4},{14,6},{16,24},{18,... | collective-permute-start | bytes 331784 | tf_op jit(solution)/shard_map/ppermute | solution.py:703
  65.2 4.8 %collective-permute-done.24 = bf16[8,80,384]{2,1,0:T(8,128)(2,1)S(1)} collective-permute-done((bf16[8,80,384]{2,1,0:T(8,128)(2,1)S(1)}, bf16[8,80,384]{2,1,0:T(8,128)(2,1)S(1)}, u32[]{:S(2)}, u32[]{:S(2)}) %collective-permute-start.24) | collective-permute-done | bytes 491552 | tf_op jit(solution)/shard_map/ppermute | solution.py:703
  70.9 2.6 %collective-permute-start.26 = (bf16[3,72,384]{2,1,0:T(8,128)(2,1)S(1)}, bf16[3,72,384]{2,1,0:T(8,128)(2,1)S(1)}, u32[]{:S(2)}, u32[]{:S(2)}) collective-permute-start(bf16[3,72,384]{2,1,0:T(8,128)(2,1)S(1)} %get-tuple-element.150), channel_id=1, source_target_pairs={{0,16},{2,18},{4,20},{6,22},{8,24},{10,26},{12,28},{14,30},{16,0},... | collective-permute-start | bytes 497672 | tf_op jit(solution)/shard_map/ppermute | solution.py:703
  74.0 4.2 %collective-permute-done.25.refs_1_ = bf16[2,72,384]{2,1,0:T(8,128)(2,1)S(1)} collective-permute-done((bf16[2,72,384]{2,1,0:T(8,128)(2,1)S(1)}, bf16[2,72,384]{2,1,0:T(8,128)(2,1)S(1)}, u32[]{:S(2)}, u32[]{:S(2)}) %collective-permute-start.25) | collective-permute-done | bytes 110624 | tf_op jit(solution)/shard_map/ppermute | solution.py:703
  78.3 2.2 %collective-permute-done.26.refs_3_ = bf16[3,72,384]{2,1,0:T(8,128)(2,1)S(1)} collective-permute-done((bf16[3,72,384]{2,1,0:T(8,128)(2,1)S(1)}, bf16[3,72,384]{2,1,0:T(8,128)(2,1)S(1)}, u32[]{:S(2)}, u32[]{:S(2)}) %collective-permute-start.26) | collective-permute-done | bytes 165920 | tf_op jit(solution)/shard_map/ppermute | solution.py:703
  80.6 3.1 %collective-permute-start.28 = (bf16[2,72,384]{2,1,0:T(8,128)(2,1)S(1)}, bf16[2,72,384]{2,1,0:T(8,128)(2,1)S(1)}, u32[]{:S(2)}, u32[]{:S(2)}) collective-permute-start(bf16[2,72,384]{2,1,0:T(8,128)(2,1)S(1)} %get-tuple-element.153.refs_0_), channel_id=1, source_target_pairs={{0,16},{2,18},{4,20},{6,22},{8,24},{10,26},{12,28},{14,30},{16,0},... | collective-permute-start | bytes 331784 | tf_op jit(solution)/shard_map/ppermute | solution.py:703
  83.8 4.2 %collective-permute-done.29.refs_3_ = bf16[72,384]{1,0:T(8,128)(2,1)S(1)} collective-permute-done((bf16[72,384]{1,0:T(8,128)(2,1)S(1)}, bf16[72,384]{1,0:T(8,128)(2,1)S(1)}, u32[]{:S(2)}, u32[]{:S(2)}) %collective-permute-start.29) | collective-permute-done | bytes 55328 | tf_op jit(solution)/shard_map/ppermute | solution.py:703
  87.9 1.0 collective-permute-done.28.refs_2_
  89.7 2.1 %collective-permute-start.32 = (bf16[2,72,384]{2,1,0:T(8,128)(2,1)S(1)}, bf16[2,72,384]{2,1,0:T(8,128)(2,1)S(1)}, u32[]{:S(2)}, u32[]{:S(2)}) collective-permute-start(bf16[2,72,384]{2,1,0:T(8,128)(2,1)S(1)} %get-tuple-element.160.refs_3_), channel_id=1, source_target_pairs={{0,8},{2,10},{4,12},{6,14},{8,0},{10,2},{12,4},{14,6},{16,24},{18,... | collective-permute-start | bytes 331784 | tf_op jit(solution)/shard_map/ppermute | solution.py:703
  91.9 3.5 %collective-permute-done.32.refs_4_ = bf16[2,72,384]{2,1,0:T(8,128)(2,1)S(1)} collective-permute-done((bf16[2,72,384]{2,1,0:T(8,128)(2,1)S(1)}, bf16[2,72,384]{2,1,0:T(8,128)(2,1)S(1)}, u32[]{:S(2)}, u32[]{:S(2)}) %collective-permute-start.32) | collective-permute-done | bytes 110624 | tf_op jit(solution)/shard_map/ppermute | solution.py:703
  95.4 2.7 %collective-permute-done.31.refs_1_ = bf16[3,80,384]{2,1,0:T(8,128)(2,1)S(1)} collective-permute-done((bf16[3,80,384]{2,1,0:T(8,128)(2,1)S(1)}, bf16[3,80,384]{2,1,0:T(8,128)(2,1)S(1)}, u32[]{:S(2)}, u32[]{:S(2)}) %collective-permute-start.31) | collective-permute-done | bytes 184352 | tf_op jit(solution)/shard_map/ppermute | solution.py:703
  98.3 1.6 %collective-permute-start.34 = (bf16[3,2,72,384]{3,2,1,0:T(8,128)(2,1)S(1)}, bf16[3,2,72,384]{3,2,1,0:T(8,128)(2,1)S(1)}, u32[]{:S(2)}, u32[]{:S(2)}) collective-permute-start(bf16[3,2,72,384]{3,2,1,0:T(8,128)(2,1)S(1)} %get-tuple-element.161.refs_3_.refs_0_), channel_id=1, source_target_pairs={{0,4},{2,6},{4,0},{6,2},{8,12},{10,14},{12,8},{14,10},{16,20},{18,... | collective-permute-start | bytes 995336 | tf_op jit(solution)/shard_map/ppermute | solution.py:703
  100.1 1.8 %collective-permute-start.35 = (bf16[2,72,384]{2,1,0:T(8,128)(2,1)S(1)}, bf16[2,72,384]{2,1,0:T(8,128)(2,1)S(1)}, u32[]{:S(2)}, u32[]{:S(2)}) collective-permute-start(bf16[2,72,384]{2,1,0:T(8,128)(2,1)S(1)} %get-tuple-element.164.refs_2_), channel_id=1, source_target_pairs={{0,8},{2,10},{4,12},{6,14},{8,0},{10,2},{12,4},{14,6},{16,24},{18,... | collective-permute-start | bytes 331784 | tf_op jit(solution)/shard_map/ppermute | solution.py:703
  101.9 1.5 %layer_output.1 = bf16[576,128]{1,0:T(8,128)(2,1)} custom-call(f32[128,576]{1,0:T(8,128)S(1)} %copy-done.23, bf16[128,1536]{1,0:T(8,128)(2,1)S(1)} %get-tuple-element.110.refs_1_, bf16[576,1536]{1,0:T(8,128)(2,1)S(1)} %get-tuple-element.113.refs_2_, bf16[3,2,72,384]{3,2,1,0:T(8,128)(2,1)S(1)} %get-tuple-element.161.refs_3_.refs_0_), custom_call_target="tpu_custom_call" | custom-call | flops 2000000000 | tf_op jit(solution)/shard_map/layer_output/pallas_call | solution.py:570
  103.4 1.7 %collective-permute-done.33.refs_4_.refs_1_ = bf16[80,384]{1,0:T(8,128)(2,1)S(1)} collective-permute-done((bf16[80,384]{1,0:T(8,128)(2,1)S(1)}, bf16[80,384]{1,0:T(8,128)(2,1)S(1)}, u32[]{:S(2)}, u32[]{:S(2)}) %collective-permute-start.33) | collective-permute-done | bytes 61472 | tf_op jit(solution)/shard_map/ppermute | solution.py:703
  105.5 1.3 %collective-permute-done.34.refs_1_ = bf16[3,2,72,384]{3,2,1,0:T(8,128)(2,1)S(1)} collective-permute-done((bf16[3,2,72,384]{3,2,1,0:T(8,128)(2,1)S(1)}, bf16[3,2,72,384]{3,2,1,0:T(8,128)(2,1)S(1)}, u32[]{:S(2)}, u32[]{:S(2)}) %collective-permute-start.34) | collective-permute-done | bytes 331808 | tf_op jit(solution)/shard_map/ppermute | solution.py:703
  106.9 1.6 %collective-permute-start.40 = (bf16[2,2,72,384]{3,2,1,0:T(8,128)(2,1)S(1)}, bf16[2,2,72,384]{3,2,1,0:T(8,128)(2,1)S(1)}, u32[]{:S(2)}, u32[]{:S(2)}) collective-permute-start(bf16[2,2,72,384]{3,2,1,0:T(8,128)(2,1)S(1)} %get-tuple-element.166.refs_2_), channel_id=1, source_target_pairs={{0,4},{2,6},{4,0},{6,2},{8,12},{10,14},{12,8},{14,10},{16,20},{18,... | collective-permute-start | bytes 663560 | tf_op jit(solution)/shard_map/ppermute | solution.py:703
  108.5 2.0 %collective-permute-start.38 = (bf16[2,80,384]{2,1,0:T(8,128)(2,1)S(1)}, bf16[2,80,384]{2,1,0:T(8,128)(2,1)S(1)}, u32[]{:S(2)}, u32[]{:S(2)}) collective-permute-start(bf16[2,80,384]{2,1,0:T(8,128)(2,1)S(1)} %share_qkv_out_high.1.refs_5_.refs_0_), channel_id=1, source_target_pairs={{0,12},{2,14},{4,8},{6,10},{8,4},{10,6},{12,0},{14,2},{16,28},{18,... | collective-permute-start | bytes 368648 | tf_op jit(solution)/shard_map/ppermute | solution.py:703
  110.7 1.4 %collective-permute-start.36 = (bf16[2,80,384]{2,1,0:T(8,128)(2,1)S(1)}, bf16[2,80,384]{2,1,0:T(8,128)(2,1)S(1)}, u32[]{:S(2)}, u32[]{:S(2)}) collective-permute-start(bf16[2,80,384]{2,1,0:T(8,128)(2,1)S(1)} %share_qkv_out_high.1.refs_5_.refs_0_), channel_id=1, source_target_pairs={{0,4},{2,6},{4,0},{6,2},{8,12},{10,14},{12,8},{14,10},{16,20},{18,... | collective-permute-start | bytes 368648 | tf_op jit(solution)/shard_map/ppermute | solution.py:703
  112.0 3.3 %update_down.1 = (f32[576,768]{1,0:T(8,128)}, f32[576,768]{1,0:T(8,128)}, f32[576,768]{1,0:T(8,128)}, f32[8,128]{1,0:T(8,128)S(1)}) custom-call(s32[4]{0:T(128)S(1)} %pad_add_fusion.idx_ref.refs_0_, bf16[1,2,4,72,384]{4,3,2,1,0:T(8,128)(2,1)S(1)} %get-tuple-element.167.refs_0_, bf16[1,2,4,72,384]{4,3,2,1,0:T(8,128)(2,1)S(1)} %collective-permute-done.41.refs_1_, ...), custom_call_target="tpu_custom_call" | custom-call | flops 100000000 | tf_op jit(solution)/shard_map/update_down/pallas_call | solution.py:684
  115.4 1.4 %collective-permute-done.39.refs_1_ = bf16[2,2,72,384]{3,2,1,0:T(8,128)(2,1)S(1)} collective-permute-done((bf16[2,2,72,384]{3,2,1,0:T(8,128)(2,1)S(1)}, bf16[2,2,72,384]{3,2,1,0:T(8,128)(2,1)S(1)}, u32[]{:S(2)}, u32[]{:S(2)}) %collective-permute-start.39) | collective-permute-done | bytes 221216 | tf_op jit(solution)/shard_map/ppermute | solution.py:703
  116.9 3.4 %update_gate_up_near.1 = (f32[288,3072]{1,0:T(8,128)}, f32[288,3072]{1,0:T(8,128)}, f32[288,3072]{1,0:T(8,128)}, f32[8,128]{1,0:T(8,128)S(1)}) custom-call(s32[4]{0:T(128)S(1)} %pad_add_fusion.idx_ref.refs_0_, bf16[2,2,4,72,384]{4,3,2,1,0:T(8,128)(2,1)S(1)} %share_gate_up.1.refs_0_, f32[288,3072]{1,0:T(8,128)S(1)} %copy-done.3, f32[288,3072]{1,0:T(8,128)S(1)} %copy-done.4, ...), custom_call_target="tpu_custom_call" | custom-call | flops 20000000000 | tf_op jit(solution)/shard_map/update_gate_up_near/pallas_call | solution.py:684
  120.9 3.3 %update_gate_up_far.1 = (f32[288,3072]{1,0:T(8,128)}, f32[288,3072]{1,0:T(8,128)}, f32[288,3072]{1,0:T(8,128)}, f32[8,128]{1,0:T(8,128)S(1)}) custom-call(s32[4]{0:T(128)S(1)} %pad_add_fusion.idx_ref.refs_0_, bf16[2,2,4,72,384]{4,3,2,1,0:T(8,128)(2,1)S(1)} %collective-permute-done.43.refs_0_, ...), custom_call_target="tpu_custom_call", output_to_operand_aliasing={{0}: (5, {}), {1}: (6, {}), {2}: (7, {})} | custom-call | flops 20000000000 | tf_op jit(solution)/shard_map/update_gate_up_far/pallas_call | solution.py:684
  124.3 4.3 %update_qkv_out.1 = (f32[288,960]{1,0:T(8,128)}, f32[288,576]{1,0:T(8,128)}, f32[288,960]{1,0:T(8,128)}, f32[288,576]{1,0:T(8,128)}, f32[288,960]{1,0:T(8,128)},...) custom-call(s32[4]{0:T(128)S(1)} %pad_add_fusion.idx_ref.refs_0_, ...), custom_call_target="tpu_custom_call" | custom-call | flops 20000000000 | tf_op jit(solution)/shard_map/update_qkv_out/pallas_call | solution.py:684
  (120 shorter events, 10.1 us)
Async XLA Ops:
  1.4 19.0 %copy-start = (f32[768,576]{0,1:T(8,128)S(1)}, f32[768,576]{0,1:T(8,128)}, u32[]{:S(2)}) copy-start(f32[768,576]{0,1:T(8,128)} %param.25) | copy-start | bytes 5308420
  3.6 16.7 %collective-permute-start = (bf16[160,768]{1,0:T(8,128)(2,1)S(1)}, bf16[160,768]{1,0:T(8,128)(2,1)S(1)}, u32[]{:S(2)}, u32[]{:S(2)}) collective-permute-start(bf16[160,768]{1,0:T(8,128)(2,1)S(1)} %get-tuple-element.103), channel_id=1, source_target_pairs={{0,1},{1,0},{2,3},{3,2},{4,5},{5,4},{6,7},{7,6},{8,9},{9,8},{10,11... | collective-permute-start | bytes 737288 | tf_op jit(solution)/shard_map/ppermute | solution.py:703
  6.7 11.5 %collective-permute-start.8 = (bf16[144,768]{1,0:T(8,128)(2,1)S(1)}, bf16[144,768]{1,0:T(8,128)(2,1)S(1)}, u32[]{:S(2)}, u32[]{:S(2)}) collective-permute-start(bf16[144,768]{1,0:T(8,128)(2,1)S(1)} %get-tuple-element.108), channel_id=1, source_target_pairs={{0,1},{1,0},{2,3},{3,2},{4,5},{5,4},{6,7},{7,6},{8,9},{9,8},{10,11... | collective-permute-start | bytes 663560 | tf_op jit(solution)/shard_map/ppermute | solution.py:703
  6.7 16.5 %collective-permute-start.4 = (bf16[144,768]{1,0:T(8,128)(2,1)S(1)}, bf16[144,768]{1,0:T(8,128)(2,1)S(1)}, u32[]{:S(2)}, u32[]{:S(2)}) collective-permute-start(bf16[144,768]{1,0:T(8,128)(2,1)S(1)} %get-tuple-element.107), channel_id=1, source_target_pairs={{0,1},{1,0},{2,3},{3,2},{4,5},{5,4},{6,7},{7,6},{8,9},{9,8},{10,11... | collective-permute-start | bytes 663560 | tf_op jit(solution)/shard_map/ppermute | solution.py:703
  18.2 7.9 %collective-permute-start.9 = (bf16[144,768]{1,0:T(8,128)(2,1)S(1)}, bf16[144,768]{1,0:T(8,128)(2,1)S(1)}, u32[]{:S(2)}, u32[]{:S(2)}) collective-permute-start(bf16[144,768]{1,0:T(8,128)(2,1)S(1)} %collective-permute-done.8.refs_11_.refs_1_), channel_id=1, source_target_pairs={{0,8},{2,10},{4,12},{6,14},{8,0},{10,2},{12,4},{14,6},{16,24},{18,... | collective-permute-start | bytes 663560 | tf_op jit(solution)/shard_map/ppermute | solution.py:703
  20.3 10.2 %collective-permute-start.2 = (bf16[160,768]{1,0:T(8,128)(2,1)S(1)}, bf16[160,768]{1,0:T(8,128)(2,1)S(1)}, u32[]{:S(2)}, u32[]{:S(2)}) collective-permute-start(bf16[160,768]{1,0:T(8,128)(2,1)S(1)} %collective-permute-done.refs_5_.refs_8_), channel_id=1, source_target_pairs={{0,2},{2,0},{4,6},{6,4},{8,10},{10,8},{12,14},{14,12},{16,18},{18,... | collective-permute-start | bytes 737288 | tf_op jit(solution)/shard_map/ppermute | solution.py:703
  20.3 9.2 %collective-permute-start.1 = (bf16[160,768]{1,0:T(8,128)(2,1)S(1)}, bf16[160,768]{1,0:T(8,128)(2,1)S(1)}, u32[]{:S(2)}, u32[]{:S(2)}) collective-permute-start(bf16[160,768]{1,0:T(8,128)(2,1)S(1)} %collective-permute-done.refs_5_.refs_8_), channel_id=1, source_target_pairs={{0,8},{2,10},{4,12},{6,14},{8,0},{10,2},{12,4},{14,6},{16,24},{18,... | collective-permute-start | bytes 737288 | tf_op jit(solution)/shard_map/ppermute | solution.py:703
  21.2 9.9 %copy-start.6 = (f32[288,960]{1,0:T(8,128)S(1)}, f32[288,960]{1,0:T(8,128)}, u32[]{:S(2)}) copy-start(f32[288,960]{1,0:T(8,128)} %refs_2_.9) | copy-start | bytes 3317764
  21.2 9.9 %copy-start.10 = (f32[288,576]{1,0:T(8,128)S(1)}, f32[288,576]{1,0:T(8,128)}, u32[]{:S(2)}) copy-start(f32[288,576]{1,0:T(8,128)} %refs_3_.8) | copy-start | bytes 1990660
  21.2 9.9 %copy-start.15 = (bf16[1,128,576]{1,2,0:T(8,128)(2,1)S(1)}, bf16[1,128,576]{1,2,0:T(8,128)(2,1)}, u32[]{:S(2)}) copy-start(bf16[1,128,576]{1,2,0:T(8,128)(2,1)} %param.19) | copy-start | bytes 442372
  21.2 12.6 %collective-permute-start.12 = (bf16[288,768]{1,0:T(8,128)(2,1)S(1)}, bf16[288,768]{1,0:T(8,128)(2,1)S(1)}, u32[]{:S(2)}, u32[]{:S(2)}) collective-permute-start(bf16[288,768]{1,0:T(8,128)(2,1)S(1)} %pack_down.1), channel_id=1, source_target_pairs={{0,1},{1,0},{2,3},{3,2},{4,5},{5,4},{6,7},{7,6},{8,9},{9,8},{10,11... | collective-permute-start | bytes 1327112 | tf_op jit(solution)/shard_map/ppermute | solution.py:703
  23.2 7.3 %collective-permute-start.5 = (bf16[144,768]{1,0:T(8,128)(2,1)S(1)}, bf16[144,768]{1,0:T(8,128)(2,1)S(1)}, u32[]{:S(2)}, u32[]{:S(2)}) collective-permute-start(bf16[144,768]{1,0:T(8,128)(2,1)S(1)} %collective-permute-done.4.refs_7_), channel_id=1, source_target_pairs={{0,4},{2,6},{4,0},{6,2},{8,12},{10,14},{12,8},{14,10},{16,20},{18,... | collective-permute-start | bytes 663560 | tf_op jit(solution)/shard_map/ppermute | solution.py:703
  26.1 4.9 %collective-permute-start.11 = (bf16[144,768]{1,0:T(8,128)(2,1)S(1)}, bf16[144,768]{1,0:T(8,128)(2,1)S(1)}, u32[]{:S(2)}, u32[]{:S(2)}) collective-permute-start(bf16[144,768]{1,0:T(8,128)(2,1)S(1)} %collective-permute-done.9.refs_12_), channel_id=1, source_target_pairs={{0,2},{2,0},{4,6},{6,4},{8,10},{10,8},{12,14},{14,12},{16,18},{18,... | collective-permute-start | bytes 663560 | tf_op jit(solution)/shard_map/ppermute | solution.py:703
  29.5 1.6 %collective-permute-start.3 = (bf16[160,768]{1,0:T(8,128)(2,1)S(1)}, bf16[160,768]{1,0:T(8,128)(2,1)S(1)}, u32[]{:S(2)}, u32[]{:S(2)}) collective-permute-start(bf16[160,768]{1,0:T(8,128)(2,1)S(1)} %collective-permute-done.1.refs_9_), channel_id=1, source_target_pairs={{0,2},{2,0},{4,6},{6,4},{8,10},{10,8},{12,14},{14,12},{16,18},{18,... | collective-permute-start | bytes 737288 | tf_op jit(solution)/shard_map/ppermute | solution.py:703
  30.5 3.8 %collective-permute-start.6 = (bf16[144,768]{1,0:T(8,128)(2,1)S(1)}, bf16[144,768]{1,0:T(8,128)(2,1)S(1)}, u32[]{:S(2)}, u32[]{:S(2)}) collective-permute-start(bf16[144,768]{1,0:T(8,128)(2,1)S(1)} %collective-permute-done.4.refs_7_), channel_id=1, source_target_pairs={{0,2},{2,0},{4,6},{6,4},{8,10},{10,8},{12,14},{14,12},{16,18},{18,... | collective-permute-start | bytes 663560 | tf_op jit(solution)/shard_map/ppermute | solution.py:703
  30.5 3.8 %collective-permute-start.10 = (bf16[144,768]{1,0:T(8,128)(2,1)S(1)}, bf16[144,768]{1,0:T(8,128)(2,1)S(1)}, u32[]{:S(2)}, u32[]{:S(2)}) collective-permute-start(bf16[144,768]{1,0:T(8,128)(2,1)S(1)} %collective-permute-done.8.refs_11_.refs_1_), channel_id=1, source_target_pairs={{0,2},{2,0},{4,6},{6,4},{8,10},{10,8},{12,14},{14,12},{16,18},{18,... | collective-permute-start | bytes 663560 | tf_op jit(solution)/shard_map/ppermute | solution.py:703
  31.0 3.3 %collective-permute-start.7 = (bf16[144,768]{1,0:T(8,128)(2,1)S(1)}, bf16[144,768]{1,0:T(8,128)(2,1)S(1)}, u32[]{:S(2)}, u32[]{:S(2)}) collective-permute-start(bf16[144,768]{1,0:T(8,128)(2,1)S(1)} %collective-permute-done.5.refs_8_), channel_id=1, source_target_pairs={{0,2},{2,0},{4,6},{6,4},{8,10},{10,8},{12,14},{14,12},{16,18},{18,... | collective-permute-start | bytes 663560 | tf_op jit(solution)/shard_map/ppermute | solution.py:703
  33.8 3.5 %collective-permute-start.13 = (bf16[288,768]{1,0:T(8,128)(2,1)S(1)}, bf16[288,768]{1,0:T(8,128)(2,1)S(1)}, u32[]{:S(2)}, u32[]{:S(2)}) collective-permute-start(bf16[288,768]{1,0:T(8,128)(2,1)S(1)} %pass_on.1.refs_5_), channel_id=1, source_target_pairs={{0,2},{2,0},{4,6},{6,4},{8,10},{10,8},{12,14},{14,12},{16,18},{18,... | collective-permute-start | bytes 1327112 | tf_op jit(solution)/shard_map/ppermute | solution.py:703
  37.1 3.5 %collective-permute-start.15 = (bf16[1,2,8,72,384]{4,3,2,1,0:T(8,128)(2,1)S(1)}, bf16[1,2,8,72,384]{4,3,2,1,0:T(8,128)(2,1)S(1)}, u32[]{:S(2)}, u32[]{:S(2)}) collective-permute-start(bf16[1,2,8,72,384]{4,3,2,1,0:T(8,128)(2,1)S(1)} %get-tuple-element.119), channel_id=1, source_target_pairs={{0,2},{2,0},{4,6},{6,4},{8,10},{10,8},{12,14},{14,12},{16,18},{18,... | collective-permute-start | bytes 2654216 | tf_op jit(solution)/shard_map/ppermute | solution.py:703
  40.0 5.1 %collective-permute-start.14 = (bf16[2,2,8,72,384]{4,3,2,1,0:T(8,128)(2,1)S(1)}, bf16[2,2,8,72,384]{4,3,2,1,0:T(8,128)(2,1)S(1)}, u32[]{:S(2)}, u32[]{:S(2)}) collective-permute-start(bf16[2,2,8,72,384]{4,3,2,1,0:T(8,128)(2,1)S(1)} %get-tuple-element.115), channel_id=1, source_target_pairs={{0,2},{2,0},{4,6},{6,4},{8,10},{10,8},{12,14},{14,12},{16,18},{18,... | collective-permute-start | bytes 5308424 | tf_op jit(solution)/shard_map/ppermute | solution.py:703
  40.8 13.1 %collective-permute-start.19 = (bf16[8,72,384]{2,1,0:T(8,128)(2,1)S(1)}, bf16[8,72,384]{2,1,0:T(8,128)(2,1)S(1)}, u32[]{:S(2)}, u32[]{:S(2)}) collective-permute-start(bf16[8,72,384]{2,1,0:T(8,128)(2,1)S(1)} %get-tuple-element.134), channel_id=1, source_target_pairs={{0,1},{1,0},{2,3},{3,2},{4,5},{5,4},{6,7},{7,6},{8,9},{9,8},{10,11... | collective-permute-start | bytes 1327112 | tf_op jit(solution)/shard_map/ppermute | solution.py:703
  45.7 12.9 %collective-permute-start.16 = (bf16[2,4,72,384]{3,2,1,0:T(8,128)(2,1)S(1)}, bf16[2,4,72,384]{3,2,1,0:T(8,128)(2,1)S(1)}, u32[]{:S(2)}, u32[]{:S(2)}) collective-permute-start(bf16[2,4,72,384]{3,2,1,0:T(8,128)(2,1)S(1)} %get-tuple-element.123), channel_id=1, source_target_pairs={{0,4},{2,6},{4,0},{6,2},{8,12},{10,14},{12,8},{14,10},{16,20},{18,... | collective-permute-start | bytes 1327112 | tf_op jit(solution)/shard_map/ppermute | solution.py:703
  47.3 11.9 %collective-permute-start.17 = (bf16[4,2,72,384]{3,2,1,0:T(8,128)(2,1)S(1)}, bf16[4,2,72,384]{3,2,1,0:T(8,128)(2,1)S(1)}, u32[]{:S(2)}, u32[]{:S(2)}) collective-permute-start(bf16[4,2,72,384]{3,2,1,0:T(8,128)(2,1)S(1)} %get-tuple-element.125), channel_id=1, source_target_pairs={{0,8},{2,10},{4,12},{6,14},{8,0},{10,2},{12,4},{14,6},{16,24},{18,... | collective-permute-start | bytes 1327112 | tf_op jit(solution)/shard_map/ppermute | solution.py:703
  53.9 2.6 %collective-permute-start.18 = (bf16[1,2,8,80,384]{4,3,2,1,0:T(8,128)(2,1)S(1)}, bf16[1,2,8,80,384]{4,3,2,1,0:T(8,128)(2,1)S(1)}, u32[]{:S(2)}, u32[]{:S(2)}) collective-permute-start(bf16[1,2,8,80,384]{4,3,2,1,0:T(8,128)(2,1)S(1)} %get-tuple-element.133), channel_id=1, source_target_pairs={{0,2},{2,0},{4,6},{6,4},{8,10},{10,8},{12,14},{14,12},{16,18},{18,... | collective-permute-start | bytes 2949128 | tf_op jit(solution)/shard_map/ppermute | solution.py:703
  54.0 9.1 %collective-permute-start.22 = (bf16[4,72,384]{2,1,0:T(8,128)(2,1)S(1)}, bf16[4,72,384]{2,1,0:T(8,128)(2,1)S(1)}, u32[]{:S(2)}, u32[]{:S(2)}) collective-permute-start(bf16[4,72,384]{2,1,0:T(8,128)(2,1)S(1)} %get-tuple-element.142), channel_id=1, source_target_pairs={{0,4},{2,6},{4,0},{6,2},{8,12},{10,14},{12,8},{14,10},{16,20},{18,... | collective-permute-start | bytes 663560 | tf_op jit(solution)/shard_map/ppermute | solution.py:703
  56.7 13.3 %collective-permute-start.24 = (bf16[8,80,384]{2,1,0:T(8,128)(2,1)S(1)}, bf16[8,80,384]{2,1,0:T(8,128)(2,1)S(1)}, u32[]{:S(2)}, u32[]{:S(2)}) collective-permute-start(bf16[8,80,384]{2,1,0:T(8,128)(2,1)S(1)} %get-tuple-element.145), channel_id=1, source_target_pairs={{0,1},{1,0},{2,3},{3,2},{4,5},{5,4},{6,7},{7,6},{8,9},{9,8},{10,11... | collective-permute-start | bytes 1474568 | tf_op jit(solution)/shard_map/ppermute | solution.py:703
  59.3 11.4 %collective-permute-start.20 = (bf16[2,2,72,384]{3,2,1,0:T(8,128)(2,1)S(1)}, bf16[2,2,72,384]{3,2,1,0:T(8,128)(2,1)S(1)}, u32[]{:S(2)}, u32[]{:S(2)}) collective-permute-start(bf16[2,2,72,384]{3,2,1,0:T(8,128)(2,1)S(1)} %get-tuple-element.139), channel_id=1, source_target_pairs={{0,8},{2,10},{4,12},{6,14},{8,0},{10,2},{12,4},{14,6},{16,24},{18,... | collective-permute-start | bytes 663560 | tf_op jit(solution)/shard_map/ppermute | solution.py:703
  61.0 9.8 %collective-permute-start.21 = (bf16[2,2,72,384]{3,2,1,0:T(8,128)(2,1)S(1)}, bf16[2,2,72,384]{3,2,1,0:T(8,128)(2,1)S(1)}, u32[]{:S(2)}, u32[]{:S(2)}) collective-permute-start(bf16[2,2,72,384]{3,2,1,0:T(8,128)(2,1)S(1)} %get-tuple-element.141), channel_id=1, source_target_pairs={{0,4},{2,6},{4,0},{6,2},{8,12},{10,14},{12,8},{14,10},{16,20},{18,... | collective-permute-start | bytes 663560 | tf_op jit(solution)/shard_map/ppermute | solution.py:703
  63.2 7.6 %collective-permute-start.23 = (bf16[2,72,384]{2,1,0:T(8,128)(2,1)S(1)}, bf16[2,72,384]{2,1,0:T(8,128)(2,1)S(1)}, u32[]{:S(2)}, u32[]{:S(2)}) collective-permute-start(bf16[2,72,384]{2,1,0:T(8,128)(2,1)S(1)} %get-tuple-element.144), channel_id=1, source_target_pairs={{0,8},{2,10},{4,12},{6,14},{8,0},{10,2},{12,4},{14,6},{16,24},{18,... | collective-permute-start | bytes 331784 | tf_op jit(solution)/shard_map/ppermute | solution.py:703
  70.1 10.3 %collective-permute-start.27 = (bf16[4,80,384]{2,1,0:T(8,128)(2,1)S(1)}, bf16[4,80,384]{2,1,0:T(8,128)(2,1)S(1)}, u32[]{:S(2)}, u32[]{:S(2)}) collective-permute-start(bf16[4,80,384]{2,1,0:T(8,128)(2,1)S(1)} %get-tuple-element.152), channel_id=1, source_target_pairs={{0,4},{2,6},{4,0},{6,2},{8,12},{10,14},{12,8},{14,10},{16,20},{18,... | collective-permute-start | bytes 737288 | tf_op jit(solution)/shard_map/ppermute | solution.py:703
  70.9 9.6 %collective-permute-start.26 = (bf16[3,72,384]{2,1,0:T(8,128)(2,1)S(1)}, bf16[3,72,384]{2,1,0:T(8,128)(2,1)S(1)}, u32[]{:S(2)}, u32[]{:S(2)}) collective-permute-start(bf16[3,72,384]{2,1,0:T(8,128)(2,1)S(1)} %get-tuple-element.150), channel_id=1, source_target_pairs={{0,16},{2,18},{4,20},{6,22},{8,24},{10,26},{12,28},{14,30},{16,0},... | collective-permute-start | bytes 497672 | tf_op jit(solution)/shard_map/ppermute | solution.py:703
  73.5 4.7 %collective-permute-start.25 = (bf16[2,72,384]{2,1,0:T(8,128)(2,1)S(1)}, bf16[2,72,384]{2,1,0:T(8,128)(2,1)S(1)}, u32[]{:S(2)}, u32[]{:S(2)}) collective-permute-start(bf16[2,72,384]{2,1,0:T(8,128)(2,1)S(1)} %get-tuple-element.148), channel_id=1, source_target_pairs={{0,1},{1,0},{2,3},{3,2},{4,5},{5,4},{6,7},{7,6},{8,9},{9,8},{10,11... | collective-permute-start | bytes 331784 | tf_op jit(solution)/shard_map/ppermute | solution.py:703
  80.6 8.4 %collective-permute-start.30 = (bf16[2,80,384]{2,1,0:T(8,128)(2,1)S(1)}, bf16[2,80,384]{2,1,0:T(8,128)(2,1)S(1)}, u32[]{:S(2)}, u32[]{:S(2)}) collective-permute-start(bf16[2,80,384]{2,1,0:T(8,128)(2,1)S(1)} %get-tuple-element.157), channel_id=1, source_target_pairs={{0,8},{2,10},{4,12},{6,14},{8,0},{10,2},{12,4},{14,6},{16,24},{18,... | collective-permute-start | bytes 368648 | tf_op jit(solution)/shard_map/ppermute | solution.py:703
  80.6 8.3 %collective-permute-start.28 = (bf16[2,72,384]{2,1,0:T(8,128)(2,1)S(1)}, bf16[2,72,384]{2,1,0:T(8,128)(2,1)S(1)}, u32[]{:S(2)}, u32[]{:S(2)}) collective-permute-start(bf16[2,72,384]{2,1,0:T(8,128)(2,1)S(1)} %get-tuple-element.153.refs_0_), channel_id=1, source_target_pairs={{0,16},{2,18},{4,20},{6,22},{8,24},{10,26},{12,28},{14,30},{16,0},... | collective-permute-start | bytes 331784 | tf_op jit(solution)/shard_map/ppermute | solution.py:703
  83.8 4.2 %collective-permute-start.29 = (bf16[72,384]{1,0:T(8,128)(2,1)S(1)}, bf16[72,384]{1,0:T(8,128)(2,1)S(1)}, u32[]{:S(2)}, u32[]{:S(2)}) collective-permute-start(bf16[72,384]{1,0:T(8,128)(2,1)S(1)} %get-tuple-element.155), channel_id=1, source_target_pairs={{0,1},{1,0},{2,3},{3,2},{4,5},{5,4},{6,7},{7,6},{8,9},{9,8},{10,11... | collective-permute-start | bytes 165896 | tf_op jit(solution)/shard_map/ppermute | solution.py:703
  89.1 9.0 %collective-permute-start.31 = (bf16[3,80,384]{2,1,0:T(8,128)(2,1)S(1)}, bf16[3,80,384]{2,1,0:T(8,128)(2,1)S(1)}, u32[]{:S(2)}, u32[]{:S(2)}) collective-permute-start(bf16[3,80,384]{2,1,0:T(8,128)(2,1)S(1)} %get-tuple-element.158.refs_0_), channel_id=1, source_target_pairs={{0,16},{2,18},{4,20},{6,22},{8,24},{10,26},{12,28},{14,30},{16,0},... | collective-permute-start | bytes 552968 | tf_op jit(solution)/shard_map/ppermute | solution.py:703
  89.7 5.7 %collective-permute-start.32 = (bf16[2,72,384]{2,1,0:T(8,128)(2,1)S(1)}, bf16[2,72,384]{2,1,0:T(8,128)(2,1)S(1)}, u32[]{:S(2)}, u32[]{:S(2)}) collective-permute-start(bf16[2,72,384]{2,1,0:T(8,128)(2,1)S(1)} %get-tuple-element.160.refs_3_), channel_id=1, source_target_pairs={{0,8},{2,10},{4,12},{6,14},{8,0},{10,2},{12,4},{14,6},{16,24},{18,... | collective-permute-start | bytes 331784 | tf_op jit(solution)/shard_map/ppermute | solution.py:703
  98.3 8.5 %collective-permute-start.34 = (bf16[3,2,72,384]{3,2,1,0:T(8,128)(2,1)S(1)}, bf16[3,2,72,384]{3,2,1,0:T(8,128)(2,1)S(1)}, u32[]{:S(2)}, u32[]{:S(2)}) collective-permute-start(bf16[3,2,72,384]{3,2,1,0:T(8,128)(2,1)S(1)} %get-tuple-element.161.refs_3_.refs_0_), channel_id=1, source_target_pairs={{0,4},{2,6},{4,0},{6,2},{8,12},{10,14},{12,8},{14,10},{16,20},{18,... | collective-permute-start | bytes 995336 | tf_op jit(solution)/shard_map/ppermute | solution.py:703
  99.9 5.2 %collective-permute-start.33 = (bf16[80,384]{1,0:T(8,128)(2,1)S(1)}, bf16[80,384]{1,0:T(8,128)(2,1)S(1)}, u32[]{:S(2)}, u32[]{:S(2)}) collective-permute-start(bf16[80,384]{1,0:T(8,128)(2,1)S(1)} %get-tuple-element.163.refs_0_), channel_id=1, source_target_pairs={{0,16},{2,18},{4,20},{6,22},{8,24},{10,26},{12,28},{14,30},{16,0},... | collective-permute-start | bytes 184328 | tf_op jit(solution)/shard_map/ppermute | solution.py:703
  100.1 5.4 %collective-permute-start.35 = (bf16[2,72,384]{2,1,0:T(8,128)(2,1)S(1)}, bf16[2,72,384]{2,1,0:T(8,128)(2,1)S(1)}, u32[]{:S(2)}, u32[]{:S(2)}) collective-permute-start(bf16[2,72,384]{2,1,0:T(8,128)(2,1)S(1)} %get-tuple-element.164.refs_2_), channel_id=1, source_target_pairs={{0,8},{2,10},{4,12},{6,14},{8,0},{10,2},{12,4},{14,6},{16,24},{18,... | collective-permute-start | bytes 331784 | tf_op jit(solution)/shard_map/ppermute | solution.py:703
  106.9 8.5 %collective-permute-start.40 = (bf16[2,2,72,384]{3,2,1,0:T(8,128)(2,1)S(1)}, bf16[2,2,72,384]{3,2,1,0:T(8,128)(2,1)S(1)}, u32[]{:S(2)}, u32[]{:S(2)}) collective-permute-start(bf16[2,2,72,384]{3,2,1,0:T(8,128)(2,1)S(1)} %get-tuple-element.166.refs_2_), channel_id=1, source_target_pairs={{0,4},{2,6},{4,0},{6,2},{8,12},{10,14},{12,8},{14,10},{16,20},{18,... | collective-permute-start | bytes 663560 | tf_op jit(solution)/shard_map/ppermute | solution.py:703
  108.5 8.3 %collective-permute-start.39 = (bf16[2,2,72,384]{3,2,1,0:T(8,128)(2,1)S(1)}, bf16[2,2,72,384]{3,2,1,0:T(8,128)(2,1)S(1)}, u32[]{:S(2)}, u32[]{:S(2)}) collective-permute-start(bf16[2,2,72,384]{3,2,1,0:T(8,128)(2,1)S(1)} %get-tuple-element.165.refs_2_.refs_0_), channel_id=1, source_target_pairs={{0,8},{2,10},{4,12},{6,14},{8,0},{10,2},{12,4},{14,6},{16,24},{18,... | collective-permute-start | bytes 663560 | tf_op jit(solution)/shard_map/ppermute | solution.py:703
  108.5 2.2 %collective-permute-start.41 = (bf16[1,2,4,72,384]{4,3,2,1,0:T(8,128)(2,1)S(1)}, bf16[1,2,4,72,384]{4,3,2,1,0:T(8,128)(2,1)S(1)}, u32[]{:S(2)}, u32[]{:S(2)}) collective-permute-start(bf16[1,2,4,72,384]{4,3,2,1,0:T(8,128)(2,1)S(1)} %get-tuple-element.167.refs_0_), channel_id=1, source_target_pairs={{0,2},{2,0},{4,6},{6,4},{8,10},{10,8},{12,14},{14,12},{16,18},{18,... | collective-permute-start | bytes 1327112 | tf_op jit(solution)/shard_map/ppermute | solution.py:703
  108.5 11.8 %collective-permute-start.38 = (bf16[2,80,384]{2,1,0:T(8,128)(2,1)S(1)}, bf16[2,80,384]{2,1,0:T(8,128)(2,1)S(1)}, u32[]{:S(2)}, u32[]{:S(2)}) collective-permute-start(bf16[2,80,384]{2,1,0:T(8,128)(2,1)S(1)} %share_qkv_out_high.1.refs_5_.refs_0_), channel_id=1, source_target_pairs={{0,12},{2,14},{4,8},{6,10},{8,4},{10,6},{12,0},{14,2},{16,28},{18,... | collective-permute-start | bytes 368648 | tf_op jit(solution)/shard_map/ppermute | solution.py:703
  110.5 9.8 %collective-permute-start.37 = (bf16[2,80,384]{2,1,0:T(8,128)(2,1)S(1)}, bf16[2,80,384]{2,1,0:T(8,128)(2,1)S(1)}, u32[]{:S(2)}, u32[]{:S(2)}) collective-permute-start(bf16[2,80,384]{2,1,0:T(8,128)(2,1)S(1)} %share_qkv_out_high.1.refs_5_.refs_0_), channel_id=1, source_target_pairs={{0,8},{2,10},{4,12},{6,14},{8,0},{10,2},{12,4},{14,6},{16,24},{18,... | collective-permute-start | bytes 368648 | tf_op jit(solution)/shard_map/ppermute | solution.py:703
  110.7 9.6 %collective-permute-start.36 = (bf16[2,80,384]{2,1,0:T(8,128)(2,1)S(1)}, bf16[2,80,384]{2,1,0:T(8,128)(2,1)S(1)}, u32[]{:S(2)}, u32[]{:S(2)}) collective-permute-start(bf16[2,80,384]{2,1,0:T(8,128)(2,1)S(1)} %share_qkv_out_high.1.refs_5_.refs_0_), channel_id=1, source_target_pairs={{0,4},{2,6},{4,0},{6,2},{8,12},{10,14},{12,8},{14,10},{16,20},{18,... | collective-permute-start | bytes 368648 | tf_op jit(solution)/shard_map/ppermute | solution.py:703
  116.8 4.1 %collective-permute-start.43 = (bf16[2,2,4,72,384]{4,3,2,1,0:T(8,128)(2,1)S(1)}, bf16[2,2,4,72,384]{4,3,2,1,0:T(8,128)(2,1)S(1)}, u32[]{:S(2)}, u32[]{:S(2)}) collective-permute-start(bf16[2,2,4,72,384]{4,3,2,1,0:T(8,128)(2,1)S(1)} %share_gate_up.1.refs_0_), channel_id=1, source_target_pairs={{0,2},{2,0},{4,6},{6,4},{8,10},{10,8},{12,14},{14,12},{16,18},{18,... | collective-permute-start | bytes 2654216 | tf_op jit(solution)/shard_map/ppermute | solution.py:703
  120.4 3.9 %collective-permute-start.42 = (bf16[1,2,4,80,384]{4,3,2,1,0:T(8,128)(2,1)S(1)}, bf16[1,2,4,80,384]{4,3,2,1,0:T(8,128)(2,1)S(1)}, u32[]{:S(2)}, u32[]{:S(2)}) collective-permute-start(bf16[1,2,4,80,384]{4,3,2,1,0:T(8,128)(2,1)S(1)} %share_qkv_out.1.refs_7_.refs_0_), channel_id=1, source_target_pairs={{0,2},{2,0},{4,6},{6,4},{8,10},{10,8},{12,14},{14,12},{16,18},{18,... | collective-permute-start | bytes 1474568 | tf_op jit(solution)/shard_map/ppermute | solution.py:703
  (20 other events, 154.3 us)

commit v13 on v12

--- a/solution.py
+++ b/solution.py
@@ -295,7 +295,7 @@
 
     def body(idx_ref, arrays, loads, outs, scratch):
         x_ref, seg_ref, freq_ref = arrays[:3]
-        qkv_ref, o_ref, cos_ref, sin_ref, allowed_ref, gains_ref = outs
+        qkv_ref, o_ref, cos_ref, sin_ref, probs_ref, normed_ref, scale_ref, gains_ref = outs
         if split_gains:
             own = arrays[3][...].astype(BF16).astype(F32)
             other = arrays[4][HALF : HALF + 8, : width // 2].astype(F32)[:2]
@@ -317,10 +317,11 @@
         cos_ref[...] = cosine
         sin_ref[...] = sine
         allowed = ((seen_doc == own_doc) & (token >= seen)).astype(F32)
-        allowed_ref[...] = allowed
         allowed = jnp.concatenate([allowed] * GROUP, axis=0) > 0.5
         x = x_ref[...].astype(F32).T
-        h1 = (x * norm_scale(x) * gains_ref[0:1, :]).astype(BF16)
+        scale_ref[...] = norm_scale(x)
+        normed_ref[...] = x * scale_ref[...]
+        h1 = (normed_ref[...] * gains_ref[0:1, :]).astype(BF16)
         projected = dot(h1, loads[0]()[:, :QKV])
         for start in range(0, ROPED, LANES):
             block = projected[:, start : start + LANES]
@@ -330,15 +331,17 @@
         for kv in range(KV_HEADS):
             key = qkv[:, QUERY + kv * HEAD : QUERY + (kv + 1) * HEAD]
             value = qkv[:, ROPED + kv * HEAD : ROPED + (kv + 1) * HEAD]
-            probs = softmax_rows(head_stack(qkv, kv), key, allowed).astype(BF16)
-            attended = dot(probs, value).astype(BF16)
+            probs = softmax_rows(head_stack(qkv, kv), key, allowed)
+            probs_ref[kv] = probs
+            attended = dot(probs.astype(BF16), value).astype(BF16)
             for i in range(GROUP):
                 start = (kv * GROUP + i) * HEAD
                 o_ref[:, start : start + HEAD] = attended[i * seq_length : (i + 1) * seq_length]
 
     square = sds((seq_length, seq_length), F32)
     outs = [sds((seq_length, QKV), BF16), sds((seq_length, QUERY), BF16)]
-    outs += [square, square, square, sds((2, width), F32)]
+    outs += [square, square, sds((KV_HEADS, GROUP * seq_length, seq_length), F32)]
+    outs += [sds((seq_length, width), F32), sds((seq_length, 1), F32), sds((2, width), F32)]
     return call(
         body,
         idx,
@@ -430,15 +433,19 @@
     )
 
 
-def layer_output(middle, hidden, down_t, after):
+def finish_tokens(middle, hidden, down_t, grad_middle, grad_normed, normed, scale, gains, after):
     seq_length, width = middle.shape
 
     def body(ins, outs):
-        outs[0][...] = (ins[0][...] + dot_right_t(ins[1][...], ins[2][...])).T.astype(BF16)
-
-    return step(
-        body, [middle, hidden, down_t], [sds((width, seq_length), BF16)], "layer_output", after, 2
-    )[0]
+        u_ref, z_ref, down_ref, gu_ref, grad_ref, normed_ref, scale_ref, gains_ref = ins
+        outs[0][...] = (u_ref[...] + dot_right_t(z_ref[...], down_ref[...])).T.astype(BF16)
+        grad = grad_ref[...] * gains_ref[0:1, :]
+        grad = gu_ref[...] + norm_back(grad, normed_ref[...], scale_ref[...])
+        outs[1][...] = grad.T.astype(BF16)
+
+    arrays = [middle, hidden, down_t, grad_middle, grad_normed, normed, scale, gains]
+    outs = [sds((width, seq_length), BF16)] * 2
+    return step(body, arrays, outs, "finish_tokens", after, 2)
 
 
 def middle_back(idx, cotangent_t, middle, gated, gains, w_gate_up, w_qkv_out, after):
@@ -473,26 +480,25 @@
 
 
 def attention_back(
-    idx, tokens_t, grad_middle, grad_attended, gain_two, qkv, attended, tables, gains, w_qkv, pieces, after
+    idx, grad_middle, grad_attended, gain_two, qkv, attended, tables, gains, w_qkv, pieces, after
 ):
-    width, seq_length = tokens_t.shape
+    seq_length, width = grad_middle.shape
 
     def body(idx_ref, arrays, loads, outs, scratch):
-        x_ref, gu_ref, go_ref, gain_two_ref, qkv_ref, o_ref = arrays[:6]
-        cos_ref, sin_ref, allowed_ref, gains_ref = arrays[6:]
+        gu_ref, go_ref, gain_two_ref, qkv_ref, o_ref = arrays[:5]
+        cos_ref, sin_ref, probs_ref, normed_ref, gains_ref = arrays[5:]
         grad_ref = outs[0]
         grad_proj, gp_ref, gain_rows, *blocks = scratch
         gu, go = gu_ref[...], go_ref[...]
         gu_low = gu.astype(BF16)
         grad_gain_two = gain_two_ref[...]
-        allowed = jnp.concatenate([allowed_ref[...]] * GROUP, axis=0) > 0.5
         qkv_values = qkv_ref[...]
         for kv in range(KV_HEADS):
             key = qkv_values[:, QUERY + kv * HEAD : QUERY + (kv + 1) * HEAD]
             value = qkv_values[:, ROPED + kv * HEAD : ROPED + (kv + 1) * HEAD]
             query = head_stack(qkv_values, kv)
             grad_out = head_stack(go, kv)
-            probs = softmax_rows(query, key, allowed)
+            probs = probs_ref[kv]
             grad_probs = dot_right_t(grad_out, value)
             row_delta = jnp.sum(probs * grad_probs, axis=-1, keepdims=True)
             gs = (probs * (grad_probs - row_delta)).astype(BF16)
@@ -511,9 +517,7 @@
                 grad_proj[:, start : start + LANES], cos_ref[...], -sin_ref[...]
             ).astype(BF16)
         gp_ref[:, ROPED:QKV] = grad_proj[:, ROPED:QKV].astype(BF16)
-        x = x_ref[...].astype(F32).T
-        scale_one = norm_scale(x)
-        normed = x * scale_one
+        normed = normed_ref[...]
         h1 = (normed * gains_ref[0:1, :]).astype(BF16)
         grad_qkv = dot_left_t(h1, gp_ref[...])
         grad_out = dot_left_t(o_ref[...], gu_low)
@@ -535,11 +539,9 @@
                 gain_rows[owner, 1:2, :half] = grad_gain_two[:, columns]
             pieces.emit(idx_ref, blocks[0], outs[1:3], gain_rows)
             outs[3][...] = jnp.zeros_like(outs[3])
-        grad_ref[...] = (
-            (gu + norm_back(grad_normed * gains_ref[0:1, :], normed, scale_one)).T
-        ).astype(BF16)
-
-    outs = [sds((width, seq_length), BF16)]
+        grad_ref[...] = grad_normed
+
+    outs = [sds((seq_length, width), F32)]
     scratch = [
         pltpu.VMEM((seq_length, QKV), F32),
         pltpu.VMEM((seq_length, QKV), BF16),
@@ -553,7 +555,7 @@
     return call(
         body,
         idx,
-        [tokens_t, grad_middle, grad_attended, gain_two, qkv, attended, *tables, gains],
+        [grad_middle, grad_attended, gain_two, qkv, attended, *tables, gains],
         [w_qkv],
         outs,
         scratch,
@@ -799,7 +801,7 @@
         ]
         cut_qkv_out = cut_gate_up = cut_down = None
 
-    qkv, attended, *tables, gains, whole = attention_forward(
+    qkv, attended, *tables, scale, gains, whole = attention_forward(
         idx, x_t, segments, frequency, gains, mat_qkv_out
     ) + (() if fast else (None,))
     if fast:
@@ -827,8 +829,6 @@
     if fast:
         arrived_down = over_core(grad_down[0])
     gated, *grad_gate_up = feed_back(idx, ab, normed_low, y_t, mat_down, cut_gate_up)
-    if not fast:
-        output = layer_output(middle, hidden, mat_down.arrays[0], ())
     if fast:
         down_whole = grad_gate_up.pop()
         cut = lambda a, *lead: a.reshape(*lead, *a.shape[-2:])
@@ -851,9 +851,8 @@
         )
         arrived_up, arrived_low = over_x(send_up), over_z_low(send_low)
         after = (keep_up,)
-    token_grad, *grad_qkv_out = attention_back(
+    grad_normed, *grad_qkv_out = attention_back(
         idx,
-        x_t,
         grad_middle,
         grad_attended,
         gain_two,
@@ -865,6 +864,9 @@
         cut_qkv_out,
         after,
     )
+    finish = (grad_middle, grad_normed, tables[3], scale, gains)
+    if not fast:
+        output, token_grad = finish_tokens(middle, hidden, mat_down.arrays[0], *finish, ())
     if fast:
 
         arrived_qkv_out = over_core(grad_qkv_out[0])
@@ -889,9 +891,9 @@
         )
         arrived_up, arrived_low = over_z_low(send_up), over_x(send_low)
         ((send, keep_down),) = add_step(
-            [(cut(keep_down, 2, 2), cut(arrived_down, 2, 2), 0)], "down_x", (keep_up,), 0.1
-        )
-        arrived_down = over_z_low(send)
+            [(cut(keep_down, 2, 2), cut(arrived_down, 2, 2), 1)], "down_x", (keep_up,), 0.1
+        )
+        arrived_down = over_z_high(send)
 
         def columns(ins, outs):
             total = ins[0][...] + ins[1][...].astype(F32)
@@ -901,8 +903,8 @@
             outs[2][0], outs[2][1] = total[0, 1].astype(BF16), total[1, 1].astype(BF16)
             outs[3][...] = total[:, 0]
             total = ins[4][...] + ins[5][...].astype(F32)
-            outs[2][2] = total[1].astype(BF16)
-            outs[4][...] = total[0]
+            outs[4][...] = total[1].astype(BF16)
+            outs[5][...] = total[0]
 
         ((send, keep_qkv_out),) = add_step(
             [(cut(keep_qkv_out, 2, 4), cut(arrived_qkv_out, 2, 4), 0)],
@@ -911,25 +913,27 @@
             0.1,
         )
         arrived_qkv_out = over_x(send)
-        send_up, keep_up, send, keep_low, keep_down = step(
+        send_up, keep_up, send, keep_low, send_down, keep_down = step(
             columns,
             [keep_up, arrived_up, keep_low, arrived_low, keep_down, arrived_down],
             [
                 *(sds((2, *piece), BF16), sds((2, *piece), F32)),
-                *(sds((3, *piece), BF16), sds((2, *piece), F32)),
-                sds(piece, F32),
+                *(sds((2, *piece), BF16), sds((2, *piece), F32)),
+                *(sds(piece, BF16), sds(piece, F32)),
             ],
             "columns",
             (keep_qkv_out,),
         )
         arrived_up, arrived = over_y(send_up), over_z_high(send)
+        arrived_down = over_z_low(send_down)
 
         def planes(ins, outs):
-            keep_up, arrived_up, keep_low, arrived, keep_down, keep_qkv_out, arrived_qkv_out = ins
+            keep_up, arrived_up, keep_low, arrived, keep_down, arrived_down = ins[:6]
+            keep_qkv_out, arrived_qkv_out = ins[6:]
             total = keep_up[...] + arrived_up[...].astype(F32)
             outs[0][0] = total[1].astype(BF16)
             outs[1][0] = total[0]
-            outs[0][1] = (keep_down[...] + arrived[2].astype(F32)).astype(BF16)
+            outs[0][1] = (keep_down[...] + arrived_down[...].astype(F32)).astype(BF16)
             outs[2][...] = (keep_low[1] + arrived[1].astype(F32)).astype(BF16)
             outs[1][1] = keep_low[0] + arrived[0].astype(F32)
             total = keep_qkv_out[...] + arrived_qkv_out[...].astype(F32)
@@ -939,7 +943,7 @@
         send, keep, send_low, send_qkv_out, keep_qkv_out = step(
             planes,
             [
-                *(keep_up, arrived_up, keep_low, arrived, keep_down),
+                *(keep_up, arrived_up, keep_low, arrived, keep_down, arrived_down),
                 *(cut(keep_qkv_out, 2, 2), cut(arrived_qkv_out, 2, 2)),
             ],
             [
@@ -991,7 +995,7 @@
         )
         arrived_x, low_low = over_x(near_x), over_z_low(near_low)
         qkv_out_high = over_z_high(piece_qkv_out)
-        output = layer_output(middle, hidden, down_whole, (near_x,))
+        output, token_grad = finish_tokens(middle, hidden, down_whole, *finish, (near_x,))
 
         def share_next(ins, outs):
             near_x, arrived_x, near_low, low_low = ins

time: 129 us -> 129 us (level)
  starting transfers between devices: 42.5 us -> 46 us
  waiting for transfers between devices: 47.3 us -> 45.7 us
  Pallas kernels: 36.3 us -> 34.9 us
    ppermute x44 -> x45, starting transfers between devices: 42.5 us -> 46 us  [swap(): return lax.ppermute(values, axis, [(i, i ^ mask) for i in range(size)])]
    pallas_call x5, Pallas kernels: 15.7 us -> 14.1 us  [call(): pl.pallas_call(kernel, out_shape=tuple(outs), in_specs=[pl.BlockSpec(memo...]
    ppermute x44 -> x45, waiting for transfers between devices: 47.3 us -> 45.7 us  [swap(): return lax.ppermute(values, axis, [(i, i ^ mask) for i in range(size)])]
  transfers between devices with their start and end apart: 44 -> 45, of which waited for: 20 -> 21; matrix products, arithmetic and copies ran while one was open for 0% -> 0% of each run, Pallas kernels for 23% -> 22%
where the time goes in v13:
time: 129 us
  starting transfers between devices  46 us (36%)
  waiting for transfers between devices  45.7 us (35%)
  Pallas kernels  34.9 us (27%)
  between operations  1.4 us (1%)
    ppermute x45, starting transfers between devices, swap(): return lax.ppermute(values, axis, [(i, i ^ mask) for i in range(size)])  46 us
    ppermute x45, waiting for transfers between devices, swap(): return lax.ppermute(values, axis, [(i, i ^ mask) for i in range(size)])  45.7 us
    pallas_call x4, Pallas kernels, update_rows(): pl.pallas_call(kernel, out_shape=tuple((sds(a.shape, F32) for a in [*stat...  14.3 us
    pallas_call x5, Pallas kernels, call(): pl.pallas_call(kernel, out_shape=tuple(outs), in_specs=[pl.BlockSpec(memo...  14.1 us
    pallas_call x18, Pallas kernels, step(): pl.pallas_call(kernel, out_shape=tuple(outs), in_specs=[pl.BlockSpec(memo...  3.52 us
    pallas_call x2, Pallas kernels, pack_kernel(): pl.pallas_call(kernel, out_shape=tuple(outs), in_specs=[pl.BlockSpec(memo...  2.97 us
  transfers between devices with their start and end apart: 45, of which 21 were waited for; matrix products, arithmetic and copies ran while one was open for 0% of the time, Pallas kernels for 22%

profile of v13, /device:TPU:0, one launch (start us, length us, event | category | flops | bytes accessed | tf_op | source)
XLA Modules:
  0.0 129.2 jit_solution(17530895230435278211)
XLA Ops:
  1.4 2.2 %pack_first.1 = (bf16[160,768]{1,0:T(8,128)(2,1)S(1)}, bf16[144,768]{1,0:T(8,128)(2,1)S(1)}, bf16[144,768]{1,0:T(8,128)(2,1)S(1)}) custom-call(s32[4]{0:T(128)S(1)} %pad_add_fusion.idx_ref.refs_0_, f32[288,960]{1,0:T(8,128)} %refs_2_.9, f32[288,576]{1,0:T(8,128)} %refs_3_.8, f32[2,288]{1,0:T(2,128)S(1)} %copy-done.16, f32[288,3072]{1,0:T(8,128)} %refs_1_.5, ...), custom_call_target="tpu_custom_call" | custom-call | flops 10000000000 | tf_op jit(solution)/shard_map/pack_first/pallas_call | solution.py:242
  3.6 3.0 %collective-permute-start = (bf16[160,768]{1,0:T(8,128)(2,1)S(1)}, bf16[160,768]{1,0:T(8,128)(2,1)S(1)}, u32[]{:S(2)}, u32[]{:S(2)}) collective-permute-start(bf16[160,768]{1,0:T(8,128)(2,1)S(1)} %get-tuple-element.108), channel_id=1, source_target_pairs={{0,1},{1,0},{2,3},{3,2},{4,5},{5,4},{6,7},{7,6},{8,9},{9,8},{10,11... | collective-permute-start | bytes 737288 | tf_op jit(solution)/shard_map/ppermute | solution.py:705
  6.7 1.9 %collective-permute-start.4 = (bf16[144,768]{1,0:T(8,128)(2,1)S(1)}, bf16[144,768]{1,0:T(8,128)(2,1)S(1)}, u32[]{:S(2)}, u32[]{:S(2)}) collective-permute-start(bf16[144,768]{1,0:T(8,128)(2,1)S(1)} %get-tuple-element.112), channel_id=1, source_target_pairs={{0,1},{1,0},{2,3},{3,2},{4,5},{5,4},{6,7},{7,6},{8,9},{9,8},{10,11... | collective-permute-start | bytes 663560 | tf_op jit(solution)/shard_map/ppermute | solution.py:705
  8.7 9.5 %collective-permute-done.8.refs_11_.refs_1_ = bf16[144,768]{1,0:T(8,128)(2,1)S(1)} collective-permute-done((bf16[144,768]{1,0:T(8,128)(2,1)S(1)}, bf16[144,768]{1,0:T(8,128)(2,1)S(1)}, u32[]{:S(2)}, u32[]{:S(2)}) %collective-permute-start.8) | collective-permute-done | bytes 221216 | tf_op jit(solution)/shard_map/ppermute | solution.py:705
  18.2 2.1 %collective-permute-start.9 = (bf16[144,768]{1,0:T(8,128)(2,1)S(1)}, bf16[144,768]{1,0:T(8,128)(2,1)S(1)}, u32[]{:S(2)}, u32[]{:S(2)}) collective-permute-start(bf16[144,768]{1,0:T(8,128)(2,1)S(1)} %collective-permute-done.8.refs_11_.refs_1_), channel_id=1, source_target_pairs={{0,8},{2,10},{4,12},{6,14},{8,0},{10,2},{12,4},{14,6},{16,24},{18,... | collective-permute-start | bytes 663560 | tf_op jit(solution)/shard_map/ppermute | solution.py:705
  21.2 2.0 %collective-permute-start.12 = (bf16[288,768]{1,0:T(8,128)(2,1)S(1)}, bf16[288,768]{1,0:T(8,128)(2,1)S(1)}, u32[]{:S(2)}, u32[]{:S(2)}) collective-permute-start(bf16[288,768]{1,0:T(8,128)(2,1)S(1)} %pack_down.1), channel_id=1, source_target_pairs={{0,1},{1,0},{2,3},{3,2},{4,5},{5,4},{6,7},{7,6},{8,9},{9,8},{10,11... | collective-permute-start | bytes 1327112 | tf_op jit(solution)/shard_map/ppermute | solution.py:705
  23.2 1.5 %collective-permute-start.5 = (bf16[144,768]{1,0:T(8,128)(2,1)S(1)}, bf16[144,768]{1,0:T(8,128)(2,1)S(1)}, u32[]{:S(2)}, u32[]{:S(2)}) collective-permute-start(bf16[144,768]{1,0:T(8,128)(2,1)S(1)} %collective-permute-done.4.refs_7_), channel_id=1, source_target_pairs={{0,4},{2,6},{4,0},{6,2},{8,12},{10,14},{12,8},{14,10},{16,20},{18,... | collective-permute-start | bytes 663560 | tf_op jit(solution)/shard_map/ppermute | solution.py:705
  24.7 1.4 %collective-permute-done.9.refs_12_ = bf16[144,768]{1,0:T(8,128)(2,1)S(1)} collective-permute-done((bf16[144,768]{1,0:T(8,128)(2,1)S(1)}, bf16[144,768]{1,0:T(8,128)(2,1)S(1)}, u32[]{:S(2)}, u32[]{:S(2)}) %collective-permute-start.9) | collective-permute-done | bytes 221216 | tf_op jit(solution)/shard_map/ppermute | solution.py:705
  26.1 3.4 %collective-permute-done.1.refs_9_ = bf16[160,768]{1,0:T(8,128)(2,1)S(1)} collective-permute-done((bf16[160,768]{1,0:T(8,128)(2,1)S(1)}, bf16[160,768]{1,0:T(8,128)(2,1)S(1)}, u32[]{:S(2)}, u32[]{:S(2)}) %collective-permute-start.1) | collective-permute-done | bytes 245792 | tf_op jit(solution)/shard_map/ppermute | solution.py:705
  29.5 1.0 collective-permute-done.5.refs_8_
  31.2 2.6 %attention.1 = (bf16[128,960]{1,0:T(8,128)(2,1)S(1)}, bf16[128,576]{1,0:T(8,128)(2,1)S(1)}, f32[128,128]{1,0:T(8,128)S(1)}, f32[128,128]{1,0:T(8,128)S(1)}, f32[...) custom-call(s32[4]{0:T(128)S(1)} %pad_add_fusion.idx_ref.refs_0_, ...), custom_call_target="tpu_custom_call" | custom-call | flops 1000000000 | tf_op jit(solution)/shard_map/attention/pallas_call | solution.py:152
  34.3 2.8 %feed_forward.1 = (f32[128,576]{1,0:T(8,128)S(1)}, bf16[128,576]{1,0:T(8,128)(2,1)S(1)}, f32[128,3072]{1,0:T(8,128)S(1)}, bf16[128,1536]{1,0:T(8,128)(2,1)S(1)},...) custom-call(s32[4]{0:T(128)S(1)} %pad_add_fusion.idx_ref.refs_0_, ...), custom_call_target="tpu_custom_call" | custom-call | flops 5000000000 | tf_op jit(solution)/shard_map/feed_forward/pallas_call | solution.py:152
  37.4 2.6 %feed_back.1 = (bf16[128,3072]{1,0:T(8,128)(2,1)S(1)}, bf16[2,2,8,72,384]{4,3,2,1,0:T(8,128)(2,1)S(1)}, bf16[2,2,8,72,384]{4,3,2,1,0:T(8,128)(2,1)S(1)}, bf16[576,1536]{1,0:T(8,128)(2,1)S(1)}) custom-call(s32[4]{0:T(128)S(1)} %pad_add_fusion.idx_ref.refs_0_, f32[128,3072]{1,0:T(8,128)S(1)} %get-tuple-element.116.refs_1_, ...), custom_call_target="tpu_custom_call" | custom-call | flops 20000000000 | tf_op jit(solution)/shard_map/feed_back/pallas_call | solution.py:152
  40.9 1.6 %collective-permute-start.19 = (bf16[8,72,384]{2,1,0:T(8,128)(2,1)S(1)}, bf16[8,72,384]{2,1,0:T(8,128)(2,1)S(1)}, u32[]{:S(2)}, u32[]{:S(2)}) collective-permute-start(bf16[8,72,384]{2,1,0:T(8,128)(2,1)S(1)} %get-tuple-element.142), channel_id=1, source_target_pairs={{0,1},{1,0},{2,3},{3,2},{4,5},{5,4},{6,7},{7,6},{8,9},{9,8},{10,11... | collective-permute-start | bytes 1327112 | tf_op jit(solution)/shard_map/ppermute | solution.py:705
  42.5 2.7 %middle_back.1 = (f32[128,576]{1,0:T(8,128)S(1)}, bf16[128,576]{1,0:T(8,128)(2,1)S(1)}, f32[1,576]{1,0:T(1,128)S(1)}) custom-call(s32[4]{0:T(128)S(1)} %pad_add_fusion.idx_ref.refs_0_, bf16[576,128]{1,0:T(8,128)(2,1)S(1)} %bitcast.70, f32[128,576]{1,0:T(8,128)S(1)} %get-tuple-element.114.refs_2_.refs_0_, ...), custom_call_target="tpu_custom_call" | custom-call | flops 20000000000 | tf_op jit(solution)/shard_map/middle_back/pallas_call | solution.py:152
  45.8 1.6 %collective-permute-start.16 = (bf16[2,4,72,384]{3,2,1,0:T(8,128)(2,1)S(1)}, bf16[2,4,72,384]{3,2,1,0:T(8,128)(2,1)S(1)}, u32[]{:S(2)}, u32[]{:S(2)}) collective-permute-start(bf16[2,4,72,384]{3,2,1,0:T(8,128)(2,1)S(1)} %get-tuple-element.137), channel_id=1, source_target_pairs={{0,4},{2,6},{4,0},{6,2},{8,12},{10,14},{12,8},{14,10},{16,20},{18,... | collective-permute-start | bytes 1327112 | tf_op jit(solution)/shard_map/ppermute | solution.py:705
  47.3 1.6 %collective-permute-start.17 = (bf16[4,2,72,384]{3,2,1,0:T(8,128)(2,1)S(1)}, bf16[4,2,72,384]{3,2,1,0:T(8,128)(2,1)S(1)}, u32[]{:S(2)}, u32[]{:S(2)}) collective-permute-start(bf16[4,2,72,384]{3,2,1,0:T(8,128)(2,1)S(1)} %get-tuple-element.139), channel_id=1, source_target_pairs={{0,8},{2,10},{4,12},{6,14},{8,0},{10,2},{12,4},{14,6},{16,24},{18,... | collective-permute-start | bytes 1327112 | tf_op jit(solution)/shard_map/ppermute | solution.py:705
  48.9 3.3 %attention_back.1 = (f32[128,576]{1,0:T(8,128)S(1)}, bf16[1,2,8,80,384]{4,3,2,1,0:T(8,128)(2,1)S(1)}, bf16[1,2,8,80,384]{4,3,2,1,0:T(8,128)(2,1)S(1)}, f32[8,128]{1,0:T(8,128)S(1)}) custom-call(s32[4]{0:T(128)S(1)} %pad_add_fusion.idx_ref.refs_0_, f32[128,576]{1,0:T(8,128)S(1)} %get-tuple-element.124.refs_4_.refs_1_.refs_3_, ...), custom_call_target="tpu_custom_call" | custom-call | flops 20000000000 | tf_op jit(solution)/shard_map/attention_back/pallas_call | solution.py:152
  53.3 1.8 %collective-permute-start.22 = (bf16[4,72,384]{2,1,0:T(8,128)(2,1)S(1)}, bf16[4,72,384]{2,1,0:T(8,128)(2,1)S(1)}, u32[]{:S(2)}, u32[]{:S(2)}) collective-permute-start(bf16[4,72,384]{2,1,0:T(8,128)(2,1)S(1)} %get-tuple-element.150), channel_id=1, source_target_pairs={{0,4},{2,6},{4,0},{6,2},{8,12},{10,14},{12,8},{14,10},{16,20},{18,... | collective-permute-start | bytes 663560 | tf_op jit(solution)/shard_map/ppermute | solution.py:705
  55.4 1.6 %collective-permute-start.24 = (bf16[8,80,384]{2,1,0:T(8,128)(2,1)S(1)}, bf16[8,80,384]{2,1,0:T(8,128)(2,1)S(1)}, u32[]{:S(2)}, u32[]{:S(2)}) collective-permute-start(bf16[8,80,384]{2,1,0:T(8,128)(2,1)S(1)} %get-tuple-element.153), channel_id=1, source_target_pairs={{0,1},{1,0},{2,3},{3,2},{4,5},{5,4},{6,7},{7,6},{8,9},{9,8},{10,11... | collective-permute-start | bytes 1474568 | tf_op jit(solution)/shard_map/ppermute | solution.py:705
  57.0 1.9 %collective-permute-done.16 = bf16[2,4,72,384]{3,2,1,0:T(8,128)(2,1)S(1)} collective-permute-done((bf16[2,4,72,384]{3,2,1,0:T(8,128)(2,1)S(1)}, bf16[2,4,72,384]{3,2,1,0:T(8,128)(2,1)S(1)}, u32[]{:S(2)}, u32[]{:S(2)}) %collective-permute-start.16) | collective-permute-done | bytes 442400 | tf_op jit(solution)/shard_map/ppermute | solution.py:705
  59.4 1.6 %collective-permute-start.20 = (bf16[2,2,72,384]{3,2,1,0:T(8,128)(2,1)S(1)}, bf16[2,2,72,384]{3,2,1,0:T(8,128)(2,1)S(1)}, u32[]{:S(2)}, u32[]{:S(2)}) collective-permute-start(bf16[2,2,72,384]{3,2,1,0:T(8,128)(2,1)S(1)} %get-tuple-element.147), channel_id=1, source_target_pairs={{0,8},{2,10},{4,12},{6,14},{8,0},{10,2},{12,4},{14,6},{16,24},{18,... | collective-permute-start | bytes 663560 | tf_op jit(solution)/shard_map/ppermute | solution.py:705
  61.0 1.2 collective-permute-start.21
  62.2 1.0 collective-permute-done.22
  63.2 2.6 %collective-permute-start.23 = (bf16[2,72,384]{2,1,0:T(8,128)(2,1)S(1)}, bf16[2,72,384]{2,1,0:T(8,128)(2,1)S(1)}, u32[]{:S(2)}, u32[]{:S(2)}) collective-permute-start(bf16[2,72,384]{2,1,0:T(8,128)(2,1)S(1)} %get-tuple-element.152), channel_id=1, source_target_pairs={{0,16},{2,18},{4,20},{6,22},{8,24},{10,26},{12,28},{14,30},{16,0},... | collective-permute-start | bytes 331784 | tf_op jit(solution)/shard_map/ppermute | solution.py:705
  65.9 2.8 %collective-permute-done.24 = bf16[8,80,384]{2,1,0:T(8,128)(2,1)S(1)} collective-permute-done((bf16[8,80,384]{2,1,0:T(8,128)(2,1)S(1)}, bf16[8,80,384]{2,1,0:T(8,128)(2,1)S(1)}, u32[]{:S(2)}, u32[]{:S(2)}) %collective-permute-start.24) | collective-permute-done | bytes 491552 | tf_op jit(solution)/shard_map/ppermute | solution.py:705
  69.3 1.4 %collective-permute-done.23.refs_5_ = bf16[2,72,384]{2,1,0:T(8,128)(2,1)S(1)} collective-permute-done((bf16[2,72,384]{2,1,0:T(8,128)(2,1)S(1)}, bf16[2,72,384]{2,1,0:T(8,128)(2,1)S(1)}, u32[]{:S(2)}, u32[]{:S(2)}) %collective-permute-start.23) | collective-permute-done | bytes 110624 | tf_op jit(solution)/shard_map/ppermute | solution.py:705
  71.3 1.6 %collective-permute-start.26 = (bf16[2,72,384]{2,1,0:T(8,128)(2,1)S(1)}, bf16[2,72,384]{2,1,0:T(8,128)(2,1)S(1)}, u32[]{:S(2)}, u32[]{:S(2)}) collective-permute-start(bf16[2,72,384]{2,1,0:T(8,128)(2,1)S(1)} %get-tuple-element.158), channel_id=1, source_target_pairs={{0,16},{2,18},{4,20},{6,22},{8,24},{10,26},{12,28},{14,30},{16,0},... | collective-permute-start | bytes 331784 | tf_op jit(solution)/shard_map/ppermute | solution.py:705
  72.9 2.2 %collective-permute-start.27 = (bf16[72,384]{1,0:T(8,128)(2,1)S(1)}, bf16[72,384]{1,0:T(8,128)(2,1)S(1)}, u32[]{:S(2)}, u32[]{:S(2)}) collective-permute-start(bf16[72,384]{1,0:T(8,128)(2,1)S(1)} %get-tuple-element.160), channel_id=1, source_target_pairs={{0,8},{2,10},{4,12},{6,14},{8,0},{10,2},{12,4},{14,6},{16,24},{18,... | collective-permute-start | bytes 165896 | tf_op jit(solution)/shard_map/ppermute | solution.py:705
  75.1 2.1 %collective-permute-done.27.refs_5_ = bf16[72,384]{1,0:T(8,128)(2,1)S(1)} collective-permute-done((bf16[72,384]{1,0:T(8,128)(2,1)S(1)}, bf16[72,384]{1,0:T(8,128)(2,1)S(1)}, u32[]{:S(2)}, u32[]{:S(2)}) %collective-permute-start.27) | collective-permute-done | bytes 55328 | tf_op jit(solution)/shard_map/ppermute | solution.py:705
  78.2 1.2 collective-permute-start.31
  79.5 2.2 %collective-permute-start.29 = (bf16[2,72,384]{2,1,0:T(8,128)(2,1)S(1)}, bf16[2,72,384]{2,1,0:T(8,128)(2,1)S(1)}, u32[]{:S(2)}, u32[]{:S(2)}) collective-permute-start(bf16[2,72,384]{2,1,0:T(8,128)(2,1)S(1)} %get-tuple-element.162.refs_0_), channel_id=1, source_target_pairs={{0,16},{2,18},{4,20},{6,22},{8,24},{10,26},{12,28},{14,30},{16,0},... | collective-permute-start | bytes 331784 | tf_op jit(solution)/shard_map/ppermute | solution.py:705
  81.6 1.5 %collective-permute-start.30 = (bf16[72,384]{1,0:T(8,128)(2,1)S(1)}, bf16[72,384]{1,0:T(8,128)(2,1)S(1)}, u32[]{:S(2)}, u32[]{:S(2)}) collective-permute-start(bf16[72,384]{1,0:T(8,128)(2,1)S(1)} %get-tuple-element.164), channel_id=1, source_target_pairs={{0,1},{1,0},{2,3},{3,2},{4,5},{5,4},{6,7},{7,6},{8,9},{9,8},{10,11... | collective-permute-start | bytes 165896 | tf_op jit(solution)/shard_map/ppermute | solution.py:705
  83.1 2.7 %collective-permute-done.30.refs_3_ = bf16[72,384]{1,0:T(8,128)(2,1)S(1)} collective-permute-done((bf16[72,384]{1,0:T(8,128)(2,1)S(1)}, bf16[72,384]{1,0:T(8,128)(2,1)S(1)}, u32[]{:S(2)}, u32[]{:S(2)}) %collective-permute-start.30) | collective-permute-done | bytes 55328 | tf_op jit(solution)/shard_map/ppermute | solution.py:705
  85.8 3.2 %collective-permute-done.29.refs_2_ = bf16[2,72,384]{2,1,0:T(8,128)(2,1)S(1)} collective-permute-done((bf16[2,72,384]{2,1,0:T(8,128)(2,1)S(1)}, bf16[2,72,384]{2,1,0:T(8,128)(2,1)S(1)}, u32[]{:S(2)}, u32[]{:S(2)}) %collective-permute-start.29) | collective-permute-done | bytes 110624 | tf_op jit(solution)/shard_map/ppermute | solution.py:705
  89.3 5.2 %collective-permute-done.33.refs_4_ = bf16[2,72,384]{2,1,0:T(8,128)(2,1)S(1)} collective-permute-done((bf16[2,72,384]{2,1,0:T(8,128)(2,1)S(1)}, bf16[2,72,384]{2,1,0:T(8,128)(2,1)S(1)}, u32[]{:S(2)}, u32[]{:S(2)}) %collective-permute-start.33) | collective-permute-done | bytes 110624 | tf_op jit(solution)/shard_map/ppermute | solution.py:705
  94.6 2.5 %collective-permute-done.32.refs_1_ = bf16[3,80,384]{2,1,0:T(8,128)(2,1)S(1)} collective-permute-done((bf16[3,80,384]{2,1,0:T(8,128)(2,1)S(1)}, bf16[3,80,384]{2,1,0:T(8,128)(2,1)S(1)}, u32[]{:S(2)}, u32[]{:S(2)}) %collective-permute-start.32) | collective-permute-done | bytes 184352 | tf_op jit(solution)/shard_map/ppermute | solution.py:705
  97.2 3.3 %collective-permute-start.35 = (bf16[3,2,72,384]{3,2,1,0:T(8,128)(2,1)S(1)}, bf16[3,2,72,384]{3,2,1,0:T(8,128)(2,1)S(1)}, u32[]{:S(2)}, u32[]{:S(2)}) collective-permute-start(bf16[3,2,72,384]{3,2,1,0:T(8,128)(2,1)S(1)} %get-tuple-element.170.refs_8_.refs_0_), channel_id=1, source_target_pairs={{0,4},{2,6},{4,0},{6,2},{8,12},{10,14},{12,8},{14,10},{16,20},{18,... | collective-permute-start | bytes 995336 | tf_op jit(solution)/shard_map/ppermute | solution.py:705
  101.3 1.6 %finish_tokens.1 = (bf16[576,128]{1,0:T(8,128)(2,1)}, bf16[576,128]{1,0:T(8,128)(2,1)}) custom-call(f32[128,576]{1,0:T(8,128)S(1)} %copy-done.23, bf16[128,1536]{1,0:T(8,128)(2,1)S(1)} %get-tuple-element.115.refs_1_, bf16[576,1536]{1,0:T(8,128)(2,1)S(1)} %get-tuple-element.118.refs_2_, f32[128,576]{1,0:T(8,128)S(1)} %get-tuple-element.124.refs_4_.refs_1_.refs_3_, ...), custom_call_target="tpu_custom_call" | custom-call | flops 2000000000 | tf_op jit(solution)/shard_map/finish_tokens/pallas_call | solution.py:572
  102.9 3.1 %collective-permute-done.34.refs_4_.refs_1_ = bf16[80,384]{1,0:T(8,128)(2,1)S(1)} collective-permute-done((bf16[80,384]{1,0:T(8,128)(2,1)S(1)}, bf16[80,384]{1,0:T(8,128)(2,1)S(1)}, u32[]{:S(2)}, u32[]{:S(2)}) %collective-permute-start.34) | collective-permute-done | bytes 61472 | tf_op jit(solution)/shard_map/ppermute | solution.py:705
  107.1 1.8 %collective-permute-start.41 = (bf16[2,2,72,384]{3,2,1,0:T(8,128)(2,1)S(1)}, bf16[2,2,72,384]{3,2,1,0:T(8,128)(2,1)S(1)}, u32[]{:S(2)}, u32[]{:S(2)}) collective-permute-start(bf16[2,2,72,384]{3,2,1,0:T(8,128)(2,1)S(1)} %get-tuple-element.176.refs_2_), channel_id=1, source_target_pairs={{0,4},{2,6},{4,0},{6,2},{8,12},{10,14},{12,8},{14,10},{16,20},{18,... | collective-permute-start | bytes 663560 | tf_op jit(solution)/shard_map/ppermute | solution.py:705
  108.9 1.8 %collective-permute-start.39 = (bf16[2,80,384]{2,1,0:T(8,128)(2,1)S(1)}, bf16[2,80,384]{2,1,0:T(8,128)(2,1)S(1)}, u32[]{:S(2)}, u32[]{:S(2)}) collective-permute-start(bf16[2,80,384]{2,1,0:T(8,128)(2,1)S(1)} %share_qkv_out_high.1.refs_5_.refs_0_), channel_id=1, source_target_pairs={{0,12},{2,14},{4,8},{6,10},{8,4},{10,6},{12,0},{14,2},{16,28},{18,... | collective-permute-start | bytes 368648 | tf_op jit(solution)/shard_map/ppermute | solution.py:705
  111.0 1.4 %collective-permute-start.37 = (bf16[2,80,384]{2,1,0:T(8,128)(2,1)S(1)}, bf16[2,80,384]{2,1,0:T(8,128)(2,1)S(1)}, u32[]{:S(2)}, u32[]{:S(2)}) collective-permute-start(bf16[2,80,384]{2,1,0:T(8,128)(2,1)S(1)} %share_qkv_out_high.1.refs_5_.refs_0_), channel_id=1, source_target_pairs={{0,4},{2,6},{4,0},{6,2},{8,12},{10,14},{12,8},{14,10},{16,20},{18,... | collective-permute-start | bytes 368648 | tf_op jit(solution)/shard_map/ppermute | solution.py:705
  112.4 3.3 %update_down.1 = (f32[576,768]{1,0:T(8,128)}, f32[576,768]{1,0:T(8,128)}, f32[576,768]{1,0:T(8,128)}, f32[8,128]{1,0:T(8,128)S(1)}) custom-call(s32[4]{0:T(128)S(1)} %pad_add_fusion.idx_ref.refs_0_, bf16[1,2,4,72,384]{4,3,2,1,0:T(8,128)(2,1)S(1)} %get-tuple-element.177.refs_0_, bf16[1,2,4,72,384]{4,3,2,1,0:T(8,128)(2,1)S(1)} %collective-permute-done.42.refs_1_, ...), custom_call_target="tpu_custom_call" | custom-call | flops 100000000 | tf_op jit(solution)/shard_map/update_down/pallas_call | solution.py:686
  115.8 1.4 %collective-permute-done.40.refs_1_ = bf16[2,2,72,384]{3,2,1,0:T(8,128)(2,1)S(1)} collective-permute-done((bf16[2,2,72,384]{3,2,1,0:T(8,128)(2,1)S(1)}, bf16[2,2,72,384]{3,2,1,0:T(8,128)(2,1)S(1)}, u32[]{:S(2)}, u32[]{:S(2)}) %collective-permute-start.40) | collective-permute-done | bytes 221216 | tf_op jit(solution)/shard_map/ppermute | solution.py:705
  117.3 3.4 %update_gate_up_near.1 = (f32[288,3072]{1,0:T(8,128)}, f32[288,3072]{1,0:T(8,128)}, f32[288,3072]{1,0:T(8,128)}, f32[8,128]{1,0:T(8,128)S(1)}) custom-call(s32[4]{0:T(128)S(1)} %pad_add_fusion.idx_ref.refs_0_, bf16[2,2,4,72,384]{4,3,2,1,0:T(8,128)(2,1)S(1)} %share_gate_up.1.refs_0_, f32[288,3072]{1,0:T(8,128)S(1)} %copy-done.3, f32[288,3072]{1,0:T(8,128)S(1)} %copy-done.4, ...), custom_call_target="tpu_custom_call" | custom-call | flops 20000000000 | tf_op jit(solution)/shard_map/update_gate_up_near/pallas_call | solution.py:686
  121.3 3.3 %update_gate_up_far.1 = (f32[288,3072]{1,0:T(8,128)}, f32[288,3072]{1,0:T(8,128)}, f32[288,3072]{1,0:T(8,128)}, f32[8,128]{1,0:T(8,128)S(1)}) custom-call(s32[4]{0:T(128)S(1)} %pad_add_fusion.idx_ref.refs_0_, bf16[2,2,4,72,384]{4,3,2,1,0:T(8,128)(2,1)S(1)} %collective-permute-done.44.refs_0_, ...), custom_call_target="tpu_custom_call", output_to_operand_aliasing={{0}: (5, {}), {1}: (6, {}), {2}: (7, {})} | custom-call | flops 20000000000 | tf_op jit(solution)/shard_map/update_gate_up_far/pallas_call | solution.py:686
  124.7 4.3 %update_qkv_out.1 = (f32[288,960]{1,0:T(8,128)}, f32[288,576]{1,0:T(8,128)}, f32[288,960]{1,0:T(8,128)}, f32[288,576]{1,0:T(8,128)}, f32[288,960]{1,0:T(8,128)},...) custom-call(s32[4]{0:T(128)S(1)} %pad_add_fusion.idx_ref.refs_0_, ...), custom_call_target="tpu_custom_call" | custom-call | flops 20000000000 | tf_op jit(solution)/shard_map/update_qkv_out/pallas_call | solution.py:686
  (122 shorter events, 12.1 us)
Async XLA Ops:
  1.4 19.0 %copy-start = (f32[768,576]{0,1:T(8,128)S(1)}, f32[768,576]{0,1:T(8,128)}, u32[]{:S(2)}) copy-start(f32[768,576]{0,1:T(8,128)} %param.25) | copy-start | bytes 5308420
  3.6 16.7 %collective-permute-start = (bf16[160,768]{1,0:T(8,128)(2,1)S(1)}, bf16[160,768]{1,0:T(8,128)(2,1)S(1)}, u32[]{:S(2)}, u32[]{:S(2)}) collective-permute-start(bf16[160,768]{1,0:T(8,128)(2,1)S(1)} %get-tuple-element.108), channel_id=1, source_target_pairs={{0,1},{1,0},{2,3},{3,2},{4,5},{5,4},{6,7},{7,6},{8,9},{9,8},{10,11... | collective-permute-start | bytes 737288 | tf_op jit(solution)/shard_map/ppermute | solution.py:705
  6.7 11.5 %collective-permute-start.8 = (bf16[144,768]{1,0:T(8,128)(2,1)S(1)}, bf16[144,768]{1,0:T(8,128)(2,1)S(1)}, u32[]{:S(2)}, u32[]{:S(2)}) collective-permute-start(bf16[144,768]{1,0:T(8,128)(2,1)S(1)} %get-tuple-element.113), channel_id=1, source_target_pairs={{0,1},{1,0},{2,3},{3,2},{4,5},{5,4},{6,7},{7,6},{8,9},{9,8},{10,11... | collective-permute-start | bytes 663560 | tf_op jit(solution)/shard_map/ppermute | solution.py:705
  6.7 16.5 %collective-permute-start.4 = (bf16[144,768]{1,0:T(8,128)(2,1)S(1)}, bf16[144,768]{1,0:T(8,128)(2,1)S(1)}, u32[]{:S(2)}, u32[]{:S(2)}) collective-permute-start(bf16[144,768]{1,0:T(8,128)(2,1)S(1)} %get-tuple-element.112), channel_id=1, source_target_pairs={{0,1},{1,0},{2,3},{3,2},{4,5},{5,4},{6,7},{7,6},{8,9},{9,8},{10,11... | collective-permute-start | bytes 663560 | tf_op jit(solution)/shard_map/ppermute | solution.py:705
  18.2 7.9 %collective-permute-start.9 = (bf16[144,768]{1,0:T(8,128)(2,1)S(1)}, bf16[144,768]{1,0:T(8,128)(2,1)S(1)}, u32[]{:S(2)}, u32[]{:S(2)}) collective-permute-start(bf16[144,768]{1,0:T(8,128)(2,1)S(1)} %collective-permute-done.8.refs_11_.refs_1_), channel_id=1, source_target_pairs={{0,8},{2,10},{4,12},{6,14},{8,0},{10,2},{12,4},{14,6},{16,24},{18,... | collective-permute-start | bytes 663560 | tf_op jit(solution)/shard_map/ppermute | solution.py:705
  20.3 10.2 %collective-permute-start.2 = (bf16[160,768]{1,0:T(8,128)(2,1)S(1)}, bf16[160,768]{1,0:T(8,128)(2,1)S(1)}, u32[]{:S(2)}, u32[]{:S(2)}) collective-permute-start(bf16[160,768]{1,0:T(8,128)(2,1)S(1)} %collective-permute-done.refs_5_.refs_8_), channel_id=1, source_target_pairs={{0,2},{2,0},{4,6},{6,4},{8,10},{10,8},{12,14},{14,12},{16,18},{18,... | collective-permute-start | bytes 737288 | tf_op jit(solution)/shard_map/ppermute | solution.py:705
  20.3 9.2 %collective-permute-start.1 = (bf16[160,768]{1,0:T(8,128)(2,1)S(1)}, bf16[160,768]{1,0:T(8,128)(2,1)S(1)}, u32[]{:S(2)}, u32[]{:S(2)}) collective-permute-start(bf16[160,768]{1,0:T(8,128)(2,1)S(1)} %collective-permute-done.refs_5_.refs_8_), channel_id=1, source_target_pairs={{0,8},{2,10},{4,12},{6,14},{8,0},{10,2},{12,4},{14,6},{16,24},{18,... | collective-permute-start | bytes 737288 | tf_op jit(solution)/shard_map/ppermute | solution.py:705
  21.2 12.6 %collective-permute-start.12 = (bf16[288,768]{1,0:T(8,128)(2,1)S(1)}, bf16[288,768]{1,0:T(8,128)(2,1)S(1)}, u32[]{:S(2)}, u32[]{:S(2)}) collective-permute-start(bf16[288,768]{1,0:T(8,128)(2,1)S(1)} %pack_down.1), channel_id=1, source_target_pairs={{0,1},{1,0},{2,3},{3,2},{4,5},{5,4},{6,7},{7,6},{8,9},{9,8},{10,11... | collective-permute-start | bytes 1327112 | tf_op jit(solution)/shard_map/ppermute | solution.py:705
  23.2 7.3 %collective-permute-start.5 = (bf16[144,768]{1,0:T(8,128)(2,1)S(1)}, bf16[144,768]{1,0:T(8,128)(2,1)S(1)}, u32[]{:S(2)}, u32[]{:S(2)}) collective-permute-start(bf16[144,768]{1,0:T(8,128)(2,1)S(1)} %collective-permute-done.4.refs_7_), channel_id=1, source_target_pairs={{0,4},{2,6},{4,0},{6,2},{8,12},{10,14},{12,8},{14,10},{16,20},{18,... | collective-permute-start | bytes 663560 | tf_op jit(solution)/shard_map/ppermute | solution.py:705
  26.1 4.9 %collective-permute-start.11 = (bf16[144,768]{1,0:T(8,128)(2,1)S(1)}, bf16[144,768]{1,0:T(8,128)(2,1)S(1)}, u32[]{:S(2)}, u32[]{:S(2)}) collective-permute-start(bf16[144,768]{1,0:T(8,128)(2,1)S(1)} %collective-permute-done.9.refs_12_), channel_id=1, source_target_pairs={{0,2},{2,0},{4,6},{6,4},{8,10},{10,8},{12,14},{14,12},{16,18},{18,... | collective-permute-start | bytes 663560 | tf_op jit(solution)/shard_map/ppermute | solution.py:705
  29.5 1.6 %collective-permute-start.3 = (bf16[160,768]{1,0:T(8,128)(2,1)S(1)}, bf16[160,768]{1,0:T(8,128)(2,1)S(1)}, u32[]{:S(2)}, u32[]{:S(2)}) collective-permute-start(bf16[160,768]{1,0:T(8,128)(2,1)S(1)} %collective-permute-done.1.refs_9_), channel_id=1, source_target_pairs={{0,2},{2,0},{4,6},{6,4},{8,10},{10,8},{12,14},{14,12},{16,18},{18,... | collective-permute-start | bytes 737288 | tf_op jit(solution)/shard_map/ppermute | solution.py:705
  30.5 3.8 %collective-permute-start.6 = (bf16[144,768]{1,0:T(8,128)(2,1)S(1)}, bf16[144,768]{1,0:T(8,128)(2,1)S(1)}, u32[]{:S(2)}, u32[]{:S(2)}) collective-permute-start(bf16[144,768]{1,0:T(8,128)(2,1)S(1)} %collective-permute-done.4.refs_7_), channel_id=1, source_target_pairs={{0,2},{2,0},{4,6},{6,4},{8,10},{10,8},{12,14},{14,12},{16,18},{18,... | collective-permute-start | bytes 663560 | tf_op jit(solution)/shard_map/ppermute | solution.py:705
  30.5 3.8 %collective-permute-start.10 = (bf16[144,768]{1,0:T(8,128)(2,1)S(1)}, bf16[144,768]{1,0:T(8,128)(2,1)S(1)}, u32[]{:S(2)}, u32[]{:S(2)}) collective-permute-start(bf16[144,768]{1,0:T(8,128)(2,1)S(1)} %collective-permute-done.8.refs_11_.refs_1_), channel_id=1, source_target_pairs={{0,2},{2,0},{4,6},{6,4},{8,10},{10,8},{12,14},{14,12},{16,18},{18,... | collective-permute-start | bytes 663560 | tf_op jit(solution)/shard_map/ppermute | solution.py:705
  31.0 3.3 %collective-permute-start.7 = (bf16[144,768]{1,0:T(8,128)(2,1)S(1)}, bf16[144,768]{1,0:T(8,128)(2,1)S(1)}, u32[]{:S(2)}, u32[]{:S(2)}) collective-permute-start(bf16[144,768]{1,0:T(8,128)(2,1)S(1)} %collective-permute-done.5.refs_8_), channel_id=1, source_target_pairs={{0,2},{2,0},{4,6},{6,4},{8,10},{10,8},{12,14},{14,12},{16,18},{18,... | collective-permute-start | bytes 663560 | tf_op jit(solution)/shard_map/ppermute | solution.py:705
  33.8 3.5 %collective-permute-start.13 = (bf16[288,768]{1,0:T(8,128)(2,1)S(1)}, bf16[288,768]{1,0:T(8,128)(2,1)S(1)}, u32[]{:S(2)}, u32[]{:S(2)}) collective-permute-start(bf16[288,768]{1,0:T(8,128)(2,1)S(1)} %pass_on.1.refs_5_), channel_id=1, source_target_pairs={{0,2},{2,0},{4,6},{6,4},{8,10},{10,8},{12,14},{14,12},{16,18},{18,... | collective-permute-start | bytes 1327112 | tf_op jit(solution)/shard_map/ppermute | solution.py:705
  37.2 3.5 %collective-permute-start.14 = (bf16[1,2,8,72,384]{4,3,2,1,0:T(8,128)(2,1)S(1)}, bf16[1,2,8,72,384]{4,3,2,1,0:T(8,128)(2,1)S(1)}, u32[]{:S(2)}, u32[]{:S(2)}) collective-permute-start(bf16[1,2,8,72,384]{4,3,2,1,0:T(8,128)(2,1)S(1)} %get-tuple-element.122), channel_id=1, source_target_pairs={{0,2},{2,0},{4,6},{6,4},{8,10},{10,8},{12,14},{14,12},{16,18},{18,... | collective-permute-start | bytes 2654216 | tf_op jit(solution)/shard_map/ppermute | solution.py:705
  40.0 5.2 %collective-permute-start.15 = (bf16[2,2,8,72,384]{4,3,2,1,0:T(8,128)(2,1)S(1)}, bf16[2,2,8,72,384]{4,3,2,1,0:T(8,128)(2,1)S(1)}, u32[]{:S(2)}, u32[]{:S(2)}) collective-permute-start(bf16[2,2,8,72,384]{4,3,2,1,0:T(8,128)(2,1)S(1)} %get-tuple-element.133), channel_id=1, source_target_pairs={{0,2},{2,0},{4,6},{6,4},{8,10},{10,8},{12,14},{14,12},{16,18},{18,... | collective-permute-start | bytes 5308424 | tf_op jit(solution)/shard_map/ppermute | solution.py:705
  40.9 12.3 %collective-permute-start.19 = (bf16[8,72,384]{2,1,0:T(8,128)(2,1)S(1)}, bf16[8,72,384]{2,1,0:T(8,128)(2,1)S(1)}, u32[]{:S(2)}, u32[]{:S(2)}) collective-permute-start(bf16[8,72,384]{2,1,0:T(8,128)(2,1)S(1)} %get-tuple-element.142), channel_id=1, source_target_pairs={{0,1},{1,0},{2,3},{3,2},{4,5},{5,4},{6,7},{7,6},{8,9},{9,8},{10,11... | collective-permute-start | bytes 1327112 | tf_op jit(solution)/shard_map/ppermute | solution.py:705
  45.8 13.1 %collective-permute-start.16 = (bf16[2,4,72,384]{3,2,1,0:T(8,128)(2,1)S(1)}, bf16[2,4,72,384]{3,2,1,0:T(8,128)(2,1)S(1)}, u32[]{:S(2)}, u32[]{:S(2)}) collective-permute-start(bf16[2,4,72,384]{3,2,1,0:T(8,128)(2,1)S(1)} %get-tuple-element.137), channel_id=1, source_target_pairs={{0,4},{2,6},{4,0},{6,2},{8,12},{10,14},{12,8},{14,10},{16,20},{18,... | collective-permute-start | bytes 1327112 | tf_op jit(solution)/shard_map/ppermute | solution.py:705
  47.3 11.9 %collective-permute-start.17 = (bf16[4,2,72,384]{3,2,1,0:T(8,128)(2,1)S(1)}, bf16[4,2,72,384]{3,2,1,0:T(8,128)(2,1)S(1)}, u32[]{:S(2)}, u32[]{:S(2)}) collective-permute-start(bf16[4,2,72,384]{3,2,1,0:T(8,128)(2,1)S(1)} %get-tuple-element.139), channel_id=1, source_target_pairs={{0,8},{2,10},{4,12},{6,14},{8,0},{10,2},{12,4},{14,6},{16,24},{18,... | collective-permute-start | bytes 1327112 | tf_op jit(solution)/shard_map/ppermute | solution.py:705
  52.3 2.8 %collective-permute-start.18 = (bf16[1,2,8,80,384]{4,3,2,1,0:T(8,128)(2,1)S(1)}, bf16[1,2,8,80,384]{4,3,2,1,0:T(8,128)(2,1)S(1)}, u32[]{:S(2)}, u32[]{:S(2)}) collective-permute-start(bf16[1,2,8,80,384]{4,3,2,1,0:T(8,128)(2,1)S(1)} %get-tuple-element.141), channel_id=1, source_target_pairs={{0,2},{2,0},{4,6},{6,4},{8,10},{10,8},{12,14},{14,12},{16,18},{18,... | collective-permute-start | bytes 2949128 | tf_op jit(solution)/shard_map/ppermute | solution.py:705
  53.3 9.9 %collective-permute-start.22 = (bf16[4,72,384]{2,1,0:T(8,128)(2,1)S(1)}, bf16[4,72,384]{2,1,0:T(8,128)(2,1)S(1)}, u32[]{:S(2)}, u32[]{:S(2)}) collective-permute-start(bf16[4,72,384]{2,1,0:T(8,128)(2,1)S(1)} %get-tuple-element.150), channel_id=1, source_target_pairs={{0,4},{2,6},{4,0},{6,2},{8,12},{10,14},{12,8},{14,10},{16,20},{18,... | collective-permute-start | bytes 663560 | tf_op jit(solution)/shard_map/ppermute | solution.py:705
  55.4 13.2 %collective-permute-start.24 = (bf16[8,80,384]{2,1,0:T(8,128)(2,1)S(1)}, bf16[8,80,384]{2,1,0:T(8,128)(2,1)S(1)}, u32[]{:S(2)}, u32[]{:S(2)}) collective-permute-start(bf16[8,80,384]{2,1,0:T(8,128)(2,1)S(1)} %get-tuple-element.153), channel_id=1, source_target_pairs={{0,1},{1,0},{2,3},{3,2},{4,5},{5,4},{6,7},{7,6},{8,9},{9,8},{10,11... | collective-permute-start | bytes 1474568 | tf_op jit(solution)/shard_map/ppermute | solution.py:705
  59.4 11.4 %collective-permute-start.20 = (bf16[2,2,72,384]{3,2,1,0:T(8,128)(2,1)S(1)}, bf16[2,2,72,384]{3,2,1,0:T(8,128)(2,1)S(1)}, u32[]{:S(2)}, u32[]{:S(2)}) collective-permute-start(bf16[2,2,72,384]{3,2,1,0:T(8,128)(2,1)S(1)} %get-tuple-element.147), channel_id=1, source_target_pairs={{0,8},{2,10},{4,12},{6,14},{8,0},{10,2},{12,4},{14,6},{16,24},{18,... | collective-permute-start | bytes 663560 | tf_op jit(solution)/shard_map/ppermute | solution.py:705
  61.0 9.7 %collective-permute-start.21 = (bf16[2,2,72,384]{3,2,1,0:T(8,128)(2,1)S(1)}, bf16[2,2,72,384]{3,2,1,0:T(8,128)(2,1)S(1)}, u32[]{:S(2)}, u32[]{:S(2)}) collective-permute-start(bf16[2,2,72,384]{3,2,1,0:T(8,128)(2,1)S(1)} %get-tuple-element.149), channel_id=1, source_target_pairs={{0,4},{2,6},{4,0},{6,2},{8,12},{10,14},{12,8},{14,10},{16,20},{18,... | collective-permute-start | bytes 663560 | tf_op jit(solution)/shard_map/ppermute | solution.py:705
  63.2 7.5 %collective-permute-start.23 = (bf16[2,72,384]{2,1,0:T(8,128)(2,1)S(1)}, bf16[2,72,384]{2,1,0:T(8,128)(2,1)S(1)}, u32[]{:S(2)}, u32[]{:S(2)}) collective-permute-start(bf16[2,72,384]{2,1,0:T(8,128)(2,1)S(1)} %get-tuple-element.152), channel_id=1, source_target_pairs={{0,16},{2,18},{4,20},{6,22},{8,24},{10,26},{12,28},{14,30},{16,0},... | collective-permute-start | bytes 331784 | tf_op jit(solution)/shard_map/ppermute | solution.py:705
  68.7 9.4 %collective-permute-start.28 = (bf16[4,80,384]{2,1,0:T(8,128)(2,1)S(1)}, bf16[4,80,384]{2,1,0:T(8,128)(2,1)S(1)}, u32[]{:S(2)}, u32[]{:S(2)}) collective-permute-start(bf16[4,80,384]{2,1,0:T(8,128)(2,1)S(1)} %get-tuple-element.161), channel_id=1, source_target_pairs={{0,4},{2,6},{4,0},{6,2},{8,12},{10,14},{12,8},{14,10},{16,20},{18,... | collective-permute-start | bytes 737288 | tf_op jit(solution)/shard_map/ppermute | solution.py:705
  70.9 6.4 %collective-permute-start.25 = (bf16[2,72,384]{2,1,0:T(8,128)(2,1)S(1)}, bf16[2,72,384]{2,1,0:T(8,128)(2,1)S(1)}, u32[]{:S(2)}, u32[]{:S(2)}) collective-permute-start(bf16[2,72,384]{2,1,0:T(8,128)(2,1)S(1)} %get-tuple-element.156), channel_id=1, source_target_pairs={{0,1},{1,0},{2,3},{3,2},{4,5},{5,4},{6,7},{7,6},{8,9},{9,8},{10,11... | collective-permute-start | bytes 331784 | tf_op jit(solution)/shard_map/ppermute | solution.py:705
  71.3 6.8 %collective-permute-start.26 = (bf16[2,72,384]{2,1,0:T(8,128)(2,1)S(1)}, bf16[2,72,384]{2,1,0:T(8,128)(2,1)S(1)}, u32[]{:S(2)}, u32[]{:S(2)}) collective-permute-start(bf16[2,72,384]{2,1,0:T(8,128)(2,1)S(1)} %get-tuple-element.158), channel_id=1, source_target_pairs={{0,16},{2,18},{4,20},{6,22},{8,24},{10,26},{12,28},{14,30},{16,0},... | collective-permute-start | bytes 331784 | tf_op jit(solution)/shard_map/ppermute | solution.py:705
  72.9 4.3 %collective-permute-start.27 = (bf16[72,384]{1,0:T(8,128)(2,1)S(1)}, bf16[72,384]{1,0:T(8,128)(2,1)S(1)}, u32[]{:S(2)}, u32[]{:S(2)}) collective-permute-start(bf16[72,384]{1,0:T(8,128)(2,1)S(1)} %get-tuple-element.160), channel_id=1, source_target_pairs={{0,8},{2,10},{4,12},{6,14},{8,0},{10,2},{12,4},{14,6},{16,24},{18,... | collective-permute-start | bytes 165896 | tf_op jit(solution)/shard_map/ppermute | solution.py:705
  78.1 10.9 %copy-start.4 = (f32[288,3072]{1,0:T(8,128)S(1)}, f32[288,3072]{1,0:T(8,128)}, u32[]{:S(2)}) copy-start(f32[288,3072]{1,0:T(8,128)} %refs_2_.8) | copy-start | bytes 10616836
  78.1 10.9 %copy-start.5 = (f32[288,3072]{1,0:T(8,128)S(1)}, f32[288,3072]{1,0:T(8,128)}, u32[]{:S(2)}) copy-start(f32[288,3072]{1,0:T(8,128)} %refs_3_.7) | copy-start | bytes 10616836
  78.2 10.7 %collective-permute-start.31 = (bf16[2,80,384]{2,1,0:T(8,128)(2,1)S(1)}, bf16[2,80,384]{2,1,0:T(8,128)(2,1)S(1)}, u32[]{:S(2)}, u32[]{:S(2)}) collective-permute-start(bf16[2,80,384]{2,1,0:T(8,128)(2,1)S(1)} %get-tuple-element.166), channel_id=1, source_target_pairs={{0,8},{2,10},{4,12},{6,14},{8,0},{10,2},{12,4},{14,6},{16,24},{18,... | collective-permute-start | bytes 368648 | tf_op jit(solution)/shard_map/ppermute | solution.py:705
  79.5 9.5 %collective-permute-start.29 = (bf16[2,72,384]{2,1,0:T(8,128)(2,1)S(1)}, bf16[2,72,384]{2,1,0:T(8,128)(2,1)S(1)}, u32[]{:S(2)}, u32[]{:S(2)}) collective-permute-start(bf16[2,72,384]{2,1,0:T(8,128)(2,1)S(1)} %get-tuple-element.162.refs_0_), channel_id=1, source_target_pairs={{0,16},{2,18},{4,20},{6,22},{8,24},{10,26},{12,28},{14,30},{16,0},... | collective-permute-start | bytes 331784 | tf_op jit(solution)/shard_map/ppermute | solution.py:705
  81.6 4.2 %collective-permute-start.30 = (bf16[72,384]{1,0:T(8,128)(2,1)S(1)}, bf16[72,384]{1,0:T(8,128)(2,1)S(1)}, u32[]{:S(2)}, u32[]{:S(2)}) collective-permute-start(bf16[72,384]{1,0:T(8,128)(2,1)S(1)} %get-tuple-element.164), channel_id=1, source_target_pairs={{0,1},{1,0},{2,3},{3,2},{4,5},{5,4},{6,7},{7,6},{8,9},{9,8},{10,11... | collective-permute-start | bytes 165896 | tf_op jit(solution)/shard_map/ppermute | solution.py:705
  89.2 7.9 %collective-permute-start.32 = (bf16[3,80,384]{2,1,0:T(8,128)(2,1)S(1)}, bf16[3,80,384]{2,1,0:T(8,128)(2,1)S(1)}, u32[]{:S(2)}, u32[]{:S(2)}) collective-permute-start(bf16[3,80,384]{2,1,0:T(8,128)(2,1)S(1)} %get-tuple-element.167.refs_0_), channel_id=1, source_target_pairs={{0,16},{2,18},{4,20},{6,22},{8,24},{10,26},{12,28},{14,30},{16,0},... | collective-permute-start | bytes 552968 | tf_op jit(solution)/shard_map/ppermute | solution.py:705
  89.3 5.3 %collective-permute-start.33 = (bf16[2,72,384]{2,1,0:T(8,128)(2,1)S(1)}, bf16[2,72,384]{2,1,0:T(8,128)(2,1)S(1)}, u32[]{:S(2)}, u32[]{:S(2)}) collective-permute-start(bf16[2,72,384]{2,1,0:T(8,128)(2,1)S(1)} %get-tuple-element.169.refs_3_), channel_id=1, source_target_pairs={{0,8},{2,10},{4,12},{6,14},{8,0},{10,2},{12,4},{14,6},{16,24},{18,... | collective-permute-start | bytes 331784 | tf_op jit(solution)/shard_map/ppermute | solution.py:705
  97.2 9.8 %collective-permute-start.35 = (bf16[3,2,72,384]{3,2,1,0:T(8,128)(2,1)S(1)}, bf16[3,2,72,384]{3,2,1,0:T(8,128)(2,1)S(1)}, u32[]{:S(2)}, u32[]{:S(2)}) collective-permute-start(bf16[3,2,72,384]{3,2,1,0:T(8,128)(2,1)S(1)} %get-tuple-element.170.refs_8_.refs_0_), channel_id=1, source_target_pairs={{0,4},{2,6},{4,0},{6,2},{8,12},{10,14},{12,8},{14,10},{16,20},{18,... | collective-permute-start | bytes 995336 | tf_op jit(solution)/shard_map/ppermute | solution.py:705
  100.4 5.5 %collective-permute-start.34 = (bf16[80,384]{1,0:T(8,128)(2,1)S(1)}, bf16[80,384]{1,0:T(8,128)(2,1)S(1)}, u32[]{:S(2)}, u32[]{:S(2)}) collective-permute-start(bf16[80,384]{1,0:T(8,128)(2,1)S(1)} %get-tuple-element.173.refs_0_), channel_id=1, source_target_pairs={{0,16},{2,18},{4,20},{6,22},{8,24},{10,26},{12,28},{14,30},{16,0},... | collective-permute-start | bytes 184328 | tf_op jit(solution)/shard_map/ppermute | solution.py:705
  100.5 6.3 %collective-permute-start.36 = (bf16[2,72,384]{2,1,0:T(8,128)(2,1)S(1)}, bf16[2,72,384]{2,1,0:T(8,128)(2,1)S(1)}, u32[]{:S(2)}, u32[]{:S(2)}) collective-permute-start(bf16[2,72,384]{2,1,0:T(8,128)(2,1)S(1)} %get-tuple-element.174.refs_2_), channel_id=1, source_target_pairs={{0,8},{2,10},{4,12},{6,14},{8,0},{10,2},{12,4},{14,6},{16,24},{18,... | collective-permute-start | bytes 331784 | tf_op jit(solution)/shard_map/ppermute | solution.py:705
  107.1 8.7 %collective-permute-start.41 = (bf16[2,2,72,384]{3,2,1,0:T(8,128)(2,1)S(1)}, bf16[2,2,72,384]{3,2,1,0:T(8,128)(2,1)S(1)}, u32[]{:S(2)}, u32[]{:S(2)}) collective-permute-start(bf16[2,2,72,384]{3,2,1,0:T(8,128)(2,1)S(1)} %get-tuple-element.176.refs_2_), channel_id=1, source_target_pairs={{0,4},{2,6},{4,0},{6,2},{8,12},{10,14},{12,8},{14,10},{16,20},{18,... | collective-permute-start | bytes 663560 | tf_op jit(solution)/shard_map/ppermute | solution.py:705
  108.9 8.3 %collective-permute-start.40 = (bf16[2,2,72,384]{3,2,1,0:T(8,128)(2,1)S(1)}, bf16[2,2,72,384]{3,2,1,0:T(8,128)(2,1)S(1)}, u32[]{:S(2)}, u32[]{:S(2)}) collective-permute-start(bf16[2,2,72,384]{3,2,1,0:T(8,128)(2,1)S(1)} %get-tuple-element.175.refs_2_.refs_0_), channel_id=1, source_target_pairs={{0,8},{2,10},{4,12},{6,14},{8,0},{10,2},{12,4},{14,6},{16,24},{18,... | collective-permute-start | bytes 663560 | tf_op jit(solution)/shard_map/ppermute | solution.py:705
  108.9 2.2 %collective-permute-start.42 = (bf16[1,2,4,72,384]{4,3,2,1,0:T(8,128)(2,1)S(1)}, bf16[1,2,4,72,384]{4,3,2,1,0:T(8,128)(2,1)S(1)}, u32[]{:S(2)}, u32[]{:S(2)}) collective-permute-start(bf16[1,2,4,72,384]{4,3,2,1,0:T(8,128)(2,1)S(1)} %get-tuple-element.177.refs_0_), channel_id=1, source_target_pairs={{0,2},{2,0},{4,6},{6,4},{8,10},{10,8},{12,14},{14,12},{16,18},{18,... | collective-permute-start | bytes 1327112 | tf_op jit(solution)/shard_map/ppermute | solution.py:705
  108.9 11.8 %collective-permute-start.39 = (bf16[2,80,384]{2,1,0:T(8,128)(2,1)S(1)}, bf16[2,80,384]{2,1,0:T(8,128)(2,1)S(1)}, u32[]{:S(2)}, u32[]{:S(2)}) collective-permute-start(bf16[2,80,384]{2,1,0:T(8,128)(2,1)S(1)} %share_qkv_out_high.1.refs_5_.refs_0_), channel_id=1, source_target_pairs={{0,12},{2,14},{4,8},{6,10},{8,4},{10,6},{12,0},{14,2},{16,28},{18,... | collective-permute-start | bytes 368648 | tf_op jit(solution)/shard_map/ppermute | solution.py:705
  110.7 10.0 %collective-permute-start.38 = (bf16[2,80,384]{2,1,0:T(8,128)(2,1)S(1)}, bf16[2,80,384]{2,1,0:T(8,128)(2,1)S(1)}, u32[]{:S(2)}, u32[]{:S(2)}) collective-permute-start(bf16[2,80,384]{2,1,0:T(8,128)(2,1)S(1)} %share_qkv_out_high.1.refs_5_.refs_0_), channel_id=1, source_target_pairs={{0,8},{2,10},{4,12},{6,14},{8,0},{10,2},{12,4},{14,6},{16,24},{18,... | collective-permute-start | bytes 368648 | tf_op jit(solution)/shard_map/ppermute | solution.py:705
  111.0 9.6 %collective-permute-start.37 = (bf16[2,80,384]{2,1,0:T(8,128)(2,1)S(1)}, bf16[2,80,384]{2,1,0:T(8,128)(2,1)S(1)}, u32[]{:S(2)}, u32[]{:S(2)}) collective-permute-start(bf16[2,80,384]{2,1,0:T(8,128)(2,1)S(1)} %share_qkv_out_high.1.refs_5_.refs_0_), channel_id=1, source_target_pairs={{0,4},{2,6},{4,0},{6,2},{8,12},{10,14},{12,8},{14,10},{16,20},{18,... | collective-permute-start | bytes 368648 | tf_op jit(solution)/shard_map/ppermute | solution.py:705
  117.2 4.1 %collective-permute-start.44 = (bf16[2,2,4,72,384]{4,3,2,1,0:T(8,128)(2,1)S(1)}, bf16[2,2,4,72,384]{4,3,2,1,0:T(8,128)(2,1)S(1)}, u32[]{:S(2)}, u32[]{:S(2)}) collective-permute-start(bf16[2,2,4,72,384]{4,3,2,1,0:T(8,128)(2,1)S(1)} %share_gate_up.1.refs_0_), channel_id=1, source_target_pairs={{0,2},{2,0},{4,6},{6,4},{8,10},{10,8},{12,14},{14,12},{16,18},{18,... | collective-permute-start | bytes 2654216 | tf_op jit(solution)/shard_map/ppermute | solution.py:705
  120.8 3.9 %collective-permute-start.43 = (bf16[1,2,4,80,384]{4,3,2,1,0:T(8,128)(2,1)S(1)}, bf16[1,2,4,80,384]{4,3,2,1,0:T(8,128)(2,1)S(1)}, u32[]{:S(2)}, u32[]{:S(2)}) collective-permute-start(bf16[1,2,4,80,384]{4,3,2,1,0:T(8,128)(2,1)S(1)} %share_qkv_out.1.refs_7_.refs_0_), channel_id=1, source_target_pairs={{0,2},{2,0},{4,6},{6,4},{8,10},{10,8},{12,14},{14,12},{16,18},{18,... | collective-permute-start | bytes 1474568 | tf_op jit(solution)/shard_map/ppermute | solution.py:705
  (21 other events, 156.3 us)

commit v14 on v13

--- a/solution.py
+++ b/solution.py
@@ -891,9 +891,9 @@
         )
         arrived_up, arrived_low = over_z_low(send_up), over_x(send_low)
         ((send, keep_down),) = add_step(
-            [(cut(keep_down, 2, 2), cut(arrived_down, 2, 2), 1)], "down_x", (keep_up,), 0.1
-        )
-        arrived_down = over_z_high(send)
+            [(cut(keep_down, 2, 2), cut(arrived_down, 2, 2), 0)], "down_x", (keep_up,), 0.1
+        )
+        arrived_down = over_z_low(send)
 
         def columns(ins, outs):
             total = ins[0][...] + ins[1][...].astype(F32)
@@ -903,8 +903,8 @@
             outs[2][0], outs[2][1] = total[0, 1].astype(BF16), total[1, 1].astype(BF16)
             outs[3][...] = total[:, 0]
             total = ins[4][...] + ins[5][...].astype(F32)
-            outs[4][...] = total[1].astype(BF16)
-            outs[5][...] = total[0]
+            outs[2][2] = total[1].astype(BF16)
+            outs[4][...] = total[0]
 
         ((send, keep_qkv_out),) = add_step(
             [(cut(keep_qkv_out, 2, 4), cut(arrived_qkv_out, 2, 4), 0)],
@@ -913,27 +913,25 @@
             0.1,
         )
         arrived_qkv_out = over_x(send)
-        send_up, keep_up, send, keep_low, send_down, keep_down = step(
+        send_up, keep_up, send, keep_low, keep_down = step(
             columns,
             [keep_up, arrived_up, keep_low, arrived_low, keep_down, arrived_down],
             [
                 *(sds((2, *piece), BF16), sds((2, *piece), F32)),
-                *(sds((2, *piece), BF16), sds((2, *piece), F32)),
-                *(sds(piece, BF16), sds(piece, F32)),
+                *(sds((3, *piece), BF16), sds((2, *piece), F32)),
+                sds(piece, F32),
             ],
             "columns",
             (keep_qkv_out,),
         )
         arrived_up, arrived = over_y(send_up), over_z_high(send)
-        arrived_down = over_z_low(send_down)
 
         def planes(ins, outs):
-            keep_up, arrived_up, keep_low, arrived, keep_down, arrived_down = ins[:6]
-            keep_qkv_out, arrived_qkv_out = ins[6:]
+            keep_up, arrived_up, keep_low, arrived, keep_down, keep_qkv_out, arrived_qkv_out = ins
             total = keep_up[...] + arrived_up[...].astype(F32)
             outs[0][0] = total[1].astype(BF16)
             outs[1][0] = total[0]
-            outs[0][1] = (keep_down[...] + arrived_down[...].astype(F32)).astype(BF16)
+            outs[0][1] = (keep_down[...] + arrived[2].astype(F32)).astype(BF16)
             outs[2][...] = (keep_low[1] + arrived[1].astype(F32)).astype(BF16)
             outs[1][1] = keep_low[0] + arrived[0].astype(F32)
             total = keep_qkv_out[...] + arrived_qkv_out[...].astype(F32)
@@ -943,7 +941,7 @@
         send, keep, send_low, send_qkv_out, keep_qkv_out = step(
             planes,
             [
-                *(keep_up, arrived_up, keep_low, arrived, keep_down, arrived_down),
+                *(keep_up, arrived_up, keep_low, arrived, keep_down),
                 *(cut(keep_qkv_out, 2, 2), cut(arrived_qkv_out, 2, 2)),
             ],
             [

time: 129 us -> 126 us (0.977)
  waiting for transfers between devices: 45.7 us -> 42.2 us
    ppermute x45 -> x44, waiting for transfers between devices: 45.7 us -> 42.2 us  [swap(): return lax.ppermute(values, axis, [(i, i ^ mask) for i in range(size)])]
    ppermute x45 -> x44, starting transfers between devices: 46 us -> 45.9 us  [swap(): return lax.ppermute(values, axis, [(i, i ^ mask) for i in range(size)])]
  transfers between devices with their start and end apart: 45 -> 44, of which waited for: 21 -> 19; matrix products, arithmetic and copies ran while one was open for 0% -> 0% of each run, Pallas kernels for 22% -> 22%
where the time goes in v14:
time: 126 us
  starting transfers between devices  45.9 us (36%)
  waiting for transfers between devices  42.2 us (33%)
  Pallas kernels  34.9 us (28%)
  between operations  1.4 us (1%)
    ppermute x44, starting transfers between devices, swap(): return lax.ppermute(values, axis, [(i, i ^ mask) for i in range(size)])  45.9 us
    ppermute x44, waiting for transfers between devices, swap(): return lax.ppermute(values, axis, [(i, i ^ mask) for i in range(size)])  42.2 us
    pallas_call x4, Pallas kernels, update_rows(): pl.pallas_call(kernel, out_shape=tuple((sds(a.shape, F32) for a in [*stat...  14.3 us
    pallas_call x5, Pallas kernels, call(): pl.pallas_call(kernel, out_shape=tuple(outs), in_specs=[pl.BlockSpec(memo...  14.1 us
    pallas_call x18, Pallas kernels, step(): pl.pallas_call(kernel, out_shape=tuple(outs), in_specs=[pl.BlockSpec(memo...  3.53 us
    pallas_call x2, Pallas kernels, pack_kernel(): pl.pallas_call(kernel, out_shape=tuple(outs), in_specs=[pl.BlockSpec(memo...  2.97 us
  transfers between devices with their start and end apart: 44, of which 19 were waited for; matrix products, arithmetic and copies ran while one was open for 0% of the time, Pallas kernels for 22%

profile of v14, /device:TPU:0, one launch (start us, length us, event | category | flops | bytes accessed | tf_op | source)
XLA Modules:
  0.0 125.6 jit_solution(11030961167185648711)
XLA Ops:
  1.4 2.2 %pack_first.1 = (bf16[160,768]{1,0:T(8,128)(2,1)S(1)}, bf16[144,768]{1,0:T(8,128)(2,1)S(1)}, bf16[144,768]{1,0:T(8,128)(2,1)S(1)}) custom-call(s32[4]{0:T(128)S(1)} %pad_add_fusion.idx_ref.refs_0_, f32[288,960]{1,0:T(8,128)} %refs_2_.9, f32[288,576]{1,0:T(8,128)} %refs_3_.8, f32[2,288]{1,0:T(2,128)S(1)} %copy-done.16, f32[288,3072]{1,0:T(8,128)} %refs_1_.5, ...), custom_call_target="tpu_custom_call" | custom-call | flops 10000000000 | tf_op jit(solution)/shard_map/pack_first/pallas_call | solution.py:242
  3.6 3.0 %collective-permute-start = (bf16[160,768]{1,0:T(8,128)(2,1)S(1)}, bf16[160,768]{1,0:T(8,128)(2,1)S(1)}, u32[]{:S(2)}, u32[]{:S(2)}) collective-permute-start(bf16[160,768]{1,0:T(8,128)(2,1)S(1)} %get-tuple-element.107), channel_id=1, source_target_pairs={{0,1},{1,0},{2,3},{3,2},{4,5},{5,4},{6,7},{7,6},{8,9},{9,8},{10,11... | collective-permute-start | bytes 737288 | tf_op jit(solution)/shard_map/ppermute | solution.py:705
  6.7 1.9 %collective-permute-start.4 = (bf16[144,768]{1,0:T(8,128)(2,1)S(1)}, bf16[144,768]{1,0:T(8,128)(2,1)S(1)}, u32[]{:S(2)}, u32[]{:S(2)}) collective-permute-start(bf16[144,768]{1,0:T(8,128)(2,1)S(1)} %get-tuple-element.111), channel_id=1, source_target_pairs={{0,1},{1,0},{2,3},{3,2},{4,5},{5,4},{6,7},{7,6},{8,9},{9,8},{10,11... | collective-permute-start | bytes 663560 | tf_op jit(solution)/shard_map/ppermute | solution.py:705
  8.7 9.5 %collective-permute-done.8.refs_11_.refs_1_ = bf16[144,768]{1,0:T(8,128)(2,1)S(1)} collective-permute-done((bf16[144,768]{1,0:T(8,128)(2,1)S(1)}, bf16[144,768]{1,0:T(8,128)(2,1)S(1)}, u32[]{:S(2)}, u32[]{:S(2)}) %collective-permute-start.8) | collective-permute-done | bytes 221216 | tf_op jit(solution)/shard_map/ppermute | solution.py:705
  18.2 2.1 %collective-permute-start.9 = (bf16[144,768]{1,0:T(8,128)(2,1)S(1)}, bf16[144,768]{1,0:T(8,128)(2,1)S(1)}, u32[]{:S(2)}, u32[]{:S(2)}) collective-permute-start(bf16[144,768]{1,0:T(8,128)(2,1)S(1)} %collective-permute-done.8.refs_11_.refs_1_), channel_id=1, source_target_pairs={{0,8},{2,10},{4,12},{6,14},{8,0},{10,2},{12,4},{14,6},{16,24},{18,... | collective-permute-start | bytes 663560 | tf_op jit(solution)/shard_map/ppermute | solution.py:705
  21.2 2.0 %collective-permute-start.12 = (bf16[288,768]{1,0:T(8,128)(2,1)S(1)}, bf16[288,768]{1,0:T(8,128)(2,1)S(1)}, u32[]{:S(2)}, u32[]{:S(2)}) collective-permute-start(bf16[288,768]{1,0:T(8,128)(2,1)S(1)} %pack_down.1), channel_id=1, source_target_pairs={{0,1},{1,0},{2,3},{3,2},{4,5},{5,4},{6,7},{7,6},{8,9},{9,8},{10,11... | collective-permute-start | bytes 1327112 | tf_op jit(solution)/shard_map/ppermute | solution.py:705
  23.2 1.5 %collective-permute-start.5 = (bf16[144,768]{1,0:T(8,128)(2,1)S(1)}, bf16[144,768]{1,0:T(8,128)(2,1)S(1)}, u32[]{:S(2)}, u32[]{:S(2)}) collective-permute-start(bf16[144,768]{1,0:T(8,128)(2,1)S(1)} %collective-permute-done.4.refs_7_), channel_id=1, source_target_pairs={{0,4},{2,6},{4,0},{6,2},{8,12},{10,14},{12,8},{14,10},{16,20},{18,... | collective-permute-start | bytes 663560 | tf_op jit(solution)/shard_map/ppermute | solution.py:705
  24.7 1.4 %collective-permute-done.9.refs_12_ = bf16[144,768]{1,0:T(8,128)(2,1)S(1)} collective-permute-done((bf16[144,768]{1,0:T(8,128)(2,1)S(1)}, bf16[144,768]{1,0:T(8,128)(2,1)S(1)}, u32[]{:S(2)}, u32[]{:S(2)}) %collective-permute-start.9) | collective-permute-done | bytes 221216 | tf_op jit(solution)/shard_map/ppermute | solution.py:705
  26.1 3.4 %collective-permute-done.1.refs_9_ = bf16[160,768]{1,0:T(8,128)(2,1)S(1)} collective-permute-done((bf16[160,768]{1,0:T(8,128)(2,1)S(1)}, bf16[160,768]{1,0:T(8,128)(2,1)S(1)}, u32[]{:S(2)}, u32[]{:S(2)}) %collective-permute-start.1) | collective-permute-done | bytes 245792 | tf_op jit(solution)/shard_map/ppermute | solution.py:705
  29.5 1.0 collective-permute-done.5.refs_8_
  31.2 2.6 %attention.1 = (bf16[128,960]{1,0:T(8,128)(2,1)S(1)}, bf16[128,576]{1,0:T(8,128)(2,1)S(1)}, f32[128,128]{1,0:T(8,128)S(1)}, f32[128,128]{1,0:T(8,128)S(1)}, f32[...) custom-call(s32[4]{0:T(128)S(1)} %pad_add_fusion.idx_ref.refs_0_, ...), custom_call_target="tpu_custom_call" | custom-call | flops 1000000000 | tf_op jit(solution)/shard_map/attention/pallas_call | solution.py:152
  34.3 2.8 %feed_forward.1 = (f32[128,576]{1,0:T(8,128)S(1)}, bf16[128,576]{1,0:T(8,128)(2,1)S(1)}, f32[128,3072]{1,0:T(8,128)S(1)}, bf16[128,1536]{1,0:T(8,128)(2,1)S(1)},...) custom-call(s32[4]{0:T(128)S(1)} %pad_add_fusion.idx_ref.refs_0_, ...), custom_call_target="tpu_custom_call" | custom-call | flops 5000000000 | tf_op jit(solution)/shard_map/feed_forward/pallas_call | solution.py:152
  37.4 2.6 %feed_back.1 = (bf16[128,3072]{1,0:T(8,128)(2,1)S(1)}, bf16[2,2,8,72,384]{4,3,2,1,0:T(8,128)(2,1)S(1)}, bf16[2,2,8,72,384]{4,3,2,1,0:T(8,128)(2,1)S(1)}, bf16[576,1536]{1,0:T(8,128)(2,1)S(1)}) custom-call(s32[4]{0:T(128)S(1)} %pad_add_fusion.idx_ref.refs_0_, f32[128,3072]{1,0:T(8,128)S(1)} %get-tuple-element.115.refs_1_, ...), custom_call_target="tpu_custom_call" | custom-call | flops 20000000000 | tf_op jit(solution)/shard_map/feed_back/pallas_call | solution.py:152
  40.9 1.6 %collective-permute-start.19 = (bf16[8,72,384]{2,1,0:T(8,128)(2,1)S(1)}, bf16[8,72,384]{2,1,0:T(8,128)(2,1)S(1)}, u32[]{:S(2)}, u32[]{:S(2)}) collective-permute-start(bf16[8,72,384]{2,1,0:T(8,128)(2,1)S(1)} %get-tuple-element.141), channel_id=1, source_target_pairs={{0,1},{1,0},{2,3},{3,2},{4,5},{5,4},{6,7},{7,6},{8,9},{9,8},{10,11... | collective-permute-start | bytes 1327112 | tf_op jit(solution)/shard_map/ppermute | solution.py:705
  42.5 2.7 %middle_back.1 = (f32[128,576]{1,0:T(8,128)S(1)}, bf16[128,576]{1,0:T(8,128)(2,1)S(1)}, f32[1,576]{1,0:T(1,128)S(1)}) custom-call(s32[4]{0:T(128)S(1)} %pad_add_fusion.idx_ref.refs_0_, bf16[576,128]{1,0:T(8,128)(2,1)S(1)} %bitcast.70, f32[128,576]{1,0:T(8,128)S(1)} %get-tuple-element.113.refs_2_.refs_0_, ...), custom_call_target="tpu_custom_call" | custom-call | flops 20000000000 | tf_op jit(solution)/shard_map/middle_back/pallas_call | solution.py:152
  45.8 1.6 %collective-permute-start.16 = (bf16[2,4,72,384]{3,2,1,0:T(8,128)(2,1)S(1)}, bf16[2,4,72,384]{3,2,1,0:T(8,128)(2,1)S(1)}, u32[]{:S(2)}, u32[]{:S(2)}) collective-permute-start(bf16[2,4,72,384]{3,2,1,0:T(8,128)(2,1)S(1)} %get-tuple-element.136), channel_id=1, source_target_pairs={{0,4},{2,6},{4,0},{6,2},{8,12},{10,14},{12,8},{14,10},{16,20},{18,... | collective-permute-start | bytes 1327112 | tf_op jit(solution)/shard_map/ppermute | solution.py:705
  47.3 1.6 %collective-permute-start.17 = (bf16[4,2,72,384]{3,2,1,0:T(8,128)(2,1)S(1)}, bf16[4,2,72,384]{3,2,1,0:T(8,128)(2,1)S(1)}, u32[]{:S(2)}, u32[]{:S(2)}) collective-permute-start(bf16[4,2,72,384]{3,2,1,0:T(8,128)(2,1)S(1)} %get-tuple-element.138), channel_id=1, source_target_pairs={{0,8},{2,10},{4,12},{6,14},{8,0},{10,2},{12,4},{14,6},{16,24},{18,... | collective-permute-start | bytes 1327112 | tf_op jit(solution)/shard_map/ppermute | solution.py:705
  48.9 3.3 %attention_back.1 = (f32[128,576]{1,0:T(8,128)S(1)}, bf16[1,2,8,80,384]{4,3,2,1,0:T(8,128)(2,1)S(1)}, bf16[1,2,8,80,384]{4,3,2,1,0:T(8,128)(2,1)S(1)}, f32[8,128]{1,0:T(8,128)S(1)}) custom-call(s32[4]{0:T(128)S(1)} %pad_add_fusion.idx_ref.refs_0_, f32[128,576]{1,0:T(8,128)S(1)} %get-tuple-element.123.refs_4_.refs_1_.refs_3_, ...), custom_call_target="tpu_custom_call" | custom-call | flops 20000000000 | tf_op jit(solution)/shard_map/attention_back/pallas_call | solution.py:152
  53.3 1.8 %collective-permute-start.22 = (bf16[4,72,384]{2,1,0:T(8,128)(2,1)S(1)}, bf16[4,72,384]{2,1,0:T(8,128)(2,1)S(1)}, u32[]{:S(2)}, u32[]{:S(2)}) collective-permute-start(bf16[4,72,384]{2,1,0:T(8,128)(2,1)S(1)} %get-tuple-element.149), channel_id=1, source_target_pairs={{0,4},{2,6},{4,0},{6,2},{8,12},{10,14},{12,8},{14,10},{16,20},{18,... | collective-permute-start | bytes 663560 | tf_op jit(solution)/shard_map/ppermute | solution.py:705
  55.4 1.6 %collective-permute-start.24 = (bf16[8,80,384]{2,1,0:T(8,128)(2,1)S(1)}, bf16[8,80,384]{2,1,0:T(8,128)(2,1)S(1)}, u32[]{:S(2)}, u32[]{:S(2)}) collective-permute-start(bf16[8,80,384]{2,1,0:T(8,128)(2,1)S(1)} %get-tuple-element.152), channel_id=1, source_target_pairs={{0,1},{1,0},{2,3},{3,2},{4,5},{5,4},{6,7},{7,6},{8,9},{9,8},{10,11... | collective-permute-start | bytes 1474568 | tf_op jit(solution)/shard_map/ppermute | solution.py:705
  57.0 1.8 %collective-permute-done.16 = bf16[2,4,72,384]{3,2,1,0:T(8,128)(2,1)S(1)} collective-permute-done((bf16[2,4,72,384]{3,2,1,0:T(8,128)(2,1)S(1)}, bf16[2,4,72,384]{3,2,1,0:T(8,128)(2,1)S(1)}, u32[]{:S(2)}, u32[]{:S(2)}) %collective-permute-start.16) | collective-permute-done | bytes 442400 | tf_op jit(solution)/shard_map/ppermute | solution.py:705
  59.4 1.6 %collective-permute-start.20 = (bf16[2,2,72,384]{3,2,1,0:T(8,128)(2,1)S(1)}, bf16[2,2,72,384]{3,2,1,0:T(8,128)(2,1)S(1)}, u32[]{:S(2)}, u32[]{:S(2)}) collective-permute-start(bf16[2,2,72,384]{3,2,1,0:T(8,128)(2,1)S(1)} %get-tuple-element.146), channel_id=1, source_target_pairs={{0,8},{2,10},{4,12},{6,14},{8,0},{10,2},{12,4},{14,6},{16,24},{18,... | collective-permute-start | bytes 663560 | tf_op jit(solution)/shard_map/ppermute | solution.py:705
  61.0 1.2 collective-permute-start.21
  62.2 1.0 collective-permute-done.22
  63.2 2.1 %collective-permute-start.23 = (bf16[2,72,384]{2,1,0:T(8,128)(2,1)S(1)}, bf16[2,72,384]{2,1,0:T(8,128)(2,1)S(1)}, u32[]{:S(2)}, u32[]{:S(2)}) collective-permute-start(bf16[2,72,384]{2,1,0:T(8,128)(2,1)S(1)} %get-tuple-element.151), channel_id=1, source_target_pairs={{0,8},{2,10},{4,12},{6,14},{8,0},{10,2},{12,4},{14,6},{16,24},{18,... | collective-permute-start | bytes 331784 | tf_op jit(solution)/shard_map/ppermute | solution.py:705
  65.3 3.3 %collective-permute-done.24 = bf16[8,80,384]{2,1,0:T(8,128)(2,1)S(1)} collective-permute-done((bf16[8,80,384]{2,1,0:T(8,128)(2,1)S(1)}, bf16[8,80,384]{2,1,0:T(8,128)(2,1)S(1)}, u32[]{:S(2)}, u32[]{:S(2)}) %collective-permute-start.24) | collective-permute-done | bytes 491552 | tf_op jit(solution)/shard_map/ppermute | solution.py:705
  69.4 2.7 %collective-permute-start.26 = (bf16[3,72,384]{2,1,0:T(8,128)(2,1)S(1)}, bf16[3,72,384]{2,1,0:T(8,128)(2,1)S(1)}, u32[]{:S(2)}, u32[]{:S(2)}) collective-permute-start(bf16[3,72,384]{2,1,0:T(8,128)(2,1)S(1)} %get-tuple-element.157), channel_id=1, source_target_pairs={{0,16},{2,18},{4,20},{6,22},{8,24},{10,26},{12,28},{14,30},{16,0},... | collective-permute-start | bytes 497672 | tf_op jit(solution)/shard_map/ppermute | solution.py:705
  72.9 3.9 %collective-permute-done.25.refs_1_ = bf16[2,72,384]{2,1,0:T(8,128)(2,1)S(1)} collective-permute-done((bf16[2,72,384]{2,1,0:T(8,128)(2,1)S(1)}, bf16[2,72,384]{2,1,0:T(8,128)(2,1)S(1)}, u32[]{:S(2)}, u32[]{:S(2)}) %collective-permute-start.25) | collective-permute-done | bytes 110624 | tf_op jit(solution)/shard_map/ppermute | solution.py:705
  76.8 2.0 %collective-permute-done.26.refs_3_ = bf16[3,72,384]{2,1,0:T(8,128)(2,1)S(1)} collective-permute-done((bf16[3,72,384]{2,1,0:T(8,128)(2,1)S(1)}, bf16[3,72,384]{2,1,0:T(8,128)(2,1)S(1)}, u32[]{:S(2)}, u32[]{:S(2)}) %collective-permute-start.26) | collective-permute-done | bytes 165920 | tf_op jit(solution)/shard_map/ppermute | solution.py:705
  79.0 3.2 %collective-permute-start.28 = (bf16[2,72,384]{2,1,0:T(8,128)(2,1)S(1)}, bf16[2,72,384]{2,1,0:T(8,128)(2,1)S(1)}, u32[]{:S(2)}, u32[]{:S(2)}) collective-permute-start(bf16[2,72,384]{2,1,0:T(8,128)(2,1)S(1)} %get-tuple-element.160.refs_0_), channel_id=1, source_target_pairs={{0,16},{2,18},{4,20},{6,22},{8,24},{10,26},{12,28},{14,30},{16,0},... | collective-permute-start | bytes 331784 | tf_op jit(solution)/shard_map/ppermute | solution.py:705
  82.1 1.1 collective-permute-start.29
  83.2 3.1 %collective-permute-done.29.refs_3_ = bf16[72,384]{1,0:T(8,128)(2,1)S(1)} collective-permute-done((bf16[72,384]{1,0:T(8,128)(2,1)S(1)}, bf16[72,384]{1,0:T(8,128)(2,1)S(1)}, u32[]{:S(2)}, u32[]{:S(2)}) %collective-permute-start.29) | collective-permute-done | bytes 55328 | tf_op jit(solution)/shard_map/ppermute | solution.py:705
  87.2 1.0 collective-permute-start.31
  88.2 1.9 %collective-permute-start.32 = (bf16[2,72,384]{2,1,0:T(8,128)(2,1)S(1)}, bf16[2,72,384]{2,1,0:T(8,128)(2,1)S(1)}, u32[]{:S(2)}, u32[]{:S(2)}) collective-permute-start(bf16[2,72,384]{2,1,0:T(8,128)(2,1)S(1)} %get-tuple-element.167.refs_3_), channel_id=1, source_target_pairs={{0,8},{2,10},{4,12},{6,14},{8,0},{10,2},{12,4},{14,6},{16,24},{18,... | collective-permute-start | bytes 331784 | tf_op jit(solution)/shard_map/ppermute | solution.py:705
  90.0 3.6 %collective-permute-done.32.refs_4_ = bf16[2,72,384]{2,1,0:T(8,128)(2,1)S(1)} collective-permute-done((bf16[2,72,384]{2,1,0:T(8,128)(2,1)S(1)}, bf16[2,72,384]{2,1,0:T(8,128)(2,1)S(1)}, u32[]{:S(2)}, u32[]{:S(2)}) %collective-permute-start.32) | collective-permute-done | bytes 110624 | tf_op jit(solution)/shard_map/ppermute | solution.py:705
  93.6 2.0 %collective-permute-done.31.refs_1_ = bf16[3,80,384]{2,1,0:T(8,128)(2,1)S(1)} collective-permute-done((bf16[3,80,384]{2,1,0:T(8,128)(2,1)S(1)}, bf16[3,80,384]{2,1,0:T(8,128)(2,1)S(1)}, u32[]{:S(2)}, u32[]{:S(2)}) %collective-permute-start.31) | collective-permute-done | bytes 184352 | tf_op jit(solution)/shard_map/ppermute | solution.py:705
  95.8 1.0 collective-permute-start.34
  97.0 2.5 %collective-permute-start.35 = (bf16[2,72,384]{2,1,0:T(8,128)(2,1)S(1)}, bf16[2,72,384]{2,1,0:T(8,128)(2,1)S(1)}, u32[]{:S(2)}, u32[]{:S(2)}) collective-permute-start(bf16[2,72,384]{2,1,0:T(8,128)(2,1)S(1)} %get-tuple-element.172.refs_2_), channel_id=1, source_target_pairs={{0,8},{2,10},{4,12},{6,14},{8,0},{10,2},{12,4},{14,6},{16,24},{18,... | collective-permute-start | bytes 331784 | tf_op jit(solution)/shard_map/ppermute | solution.py:705
  99.6 1.6 %finish_tokens.1 = (bf16[576,128]{1,0:T(8,128)(2,1)}, bf16[576,128]{1,0:T(8,128)(2,1)}) custom-call(f32[128,576]{1,0:T(8,128)S(1)} %copy-done.23, bf16[128,1536]{1,0:T(8,128)(2,1)S(1)} %get-tuple-element.114.refs_1_, bf16[576,1536]{1,0:T(8,128)(2,1)S(1)} %get-tuple-element.117.refs_2_, f32[128,576]{1,0:T(8,128)S(1)} %get-tuple-element.123.refs_4_.refs_1_.refs_3_, ...), custom_call_target="tpu_custom_call" | custom-call | flops 2000000000 | tf_op jit(solution)/shard_map/finish_tokens/pallas_call | solution.py:572
  101.1 0.9 collective-permute-done.33.refs_4_.refs_1_
  102.0 1.9 %collective-permute-done.35.refs_3_ = bf16[2,72,384]{2,1,0:T(8,128)(2,1)S(1)} collective-permute-done((bf16[2,72,384]{2,1,0:T(8,128)(2,1)S(1)}, bf16[2,72,384]{2,1,0:T(8,128)(2,1)S(1)}, u32[]{:S(2)}, u32[]{:S(2)}) %collective-permute-start.35) | collective-permute-done | bytes 110624 | tf_op jit(solution)/shard_map/ppermute | solution.py:705
  103.9 1.4 %collective-permute-done.34.refs_1_ = bf16[3,2,72,384]{3,2,1,0:T(8,128)(2,1)S(1)} collective-permute-done((bf16[3,2,72,384]{3,2,1,0:T(8,128)(2,1)S(1)}, bf16[3,2,72,384]{3,2,1,0:T(8,128)(2,1)S(1)}, u32[]{:S(2)}, u32[]{:S(2)}) %collective-permute-start.34) | collective-permute-done | bytes 331808 | tf_op jit(solution)/shard_map/ppermute | solution.py:705
  106.7 2.3 %collective-permute-start.38 = (bf16[2,80,384]{2,1,0:T(8,128)(2,1)S(1)}, bf16[2,80,384]{2,1,0:T(8,128)(2,1)S(1)}, u32[]{:S(2)}, u32[]{:S(2)}) collective-permute-start(bf16[2,80,384]{2,1,0:T(8,128)(2,1)S(1)} %share_qkv_out_high.1.refs_5_.refs_0_), channel_id=1, source_target_pairs={{0,12},{2,14},{4,8},{6,10},{8,4},{10,6},{12,0},{14,2},{16,28},{18,... | collective-permute-start | bytes 368648 | tf_op jit(solution)/shard_map/ppermute | solution.py:705
  109.2 1.1 collective-permute-start.36
  110.2 3.3 %update_down.1 = (f32[576,768]{1,0:T(8,128)}, f32[576,768]{1,0:T(8,128)}, f32[576,768]{1,0:T(8,128)}, f32[8,128]{1,0:T(8,128)S(1)}) custom-call(s32[4]{0:T(128)S(1)} %pad_add_fusion.idx_ref.refs_0_, bf16[1,2,4,72,384]{4,3,2,1,0:T(8,128)(2,1)S(1)} %get-tuple-element.175.refs_0_, bf16[1,2,4,72,384]{4,3,2,1,0:T(8,128)(2,1)S(1)} %collective-permute-done.41.refs_1_, ...), custom_call_target="tpu_custom_call" | custom-call | flops 100000000 | tf_op jit(solution)/shard_map/update_down/pallas_call | solution.py:686
  113.7 3.4 %update_gate_up_near.1 = (f32[288,3072]{1,0:T(8,128)}, f32[288,3072]{1,0:T(8,128)}, f32[288,3072]{1,0:T(8,128)}, f32[8,128]{1,0:T(8,128)S(1)}) custom-call(s32[4]{0:T(128)S(1)} %pad_add_fusion.idx_ref.refs_0_, bf16[2,2,4,72,384]{4,3,2,1,0:T(8,128)(2,1)S(1)} %share_gate_up.1.refs_0_, f32[288,3072]{1,0:T(8,128)S(1)} %copy-done.3, f32[288,3072]{1,0:T(8,128)S(1)} %copy-done.4, ...), custom_call_target="tpu_custom_call" | custom-call | flops 20000000000 | tf_op jit(solution)/shard_map/update_gate_up_near/pallas_call | solution.py:686
  117.7 3.3 %update_gate_up_far.1 = (f32[288,3072]{1,0:T(8,128)}, f32[288,3072]{1,0:T(8,128)}, f32[288,3072]{1,0:T(8,128)}, f32[8,128]{1,0:T(8,128)S(1)}) custom-call(s32[4]{0:T(128)S(1)} %pad_add_fusion.idx_ref.refs_0_, bf16[2,2,4,72,384]{4,3,2,1,0:T(8,128)(2,1)S(1)} %collective-permute-done.43.refs_0_, ...), custom_call_target="tpu_custom_call", output_to_operand_aliasing={{0}: (5, {}), {1}: (6, {}), {2}: (7, {})} | custom-call | flops 20000000000 | tf_op jit(solution)/shard_map/update_gate_up_far/pallas_call | solution.py:686
  121.1 4.3 %update_qkv_out.1 = (f32[288,960]{1,0:T(8,128)}, f32[288,576]{1,0:T(8,128)}, f32[288,960]{1,0:T(8,128)}, f32[288,576]{1,0:T(8,128)}, f32[288,960]{1,0:T(8,128)},...) custom-call(s32[4]{0:T(128)S(1)} %pad_add_fusion.idx_ref.refs_0_, ...), custom_call_target="tpu_custom_call" | custom-call | flops 20000000000 | tf_op jit(solution)/shard_map/update_qkv_out/pallas_call | solution.py:686
  (120 shorter events, 11.7 us)
Async XLA Ops:
  1.4 19.0 %copy-start = (f32[768,576]{0,1:T(8,128)S(1)}, f32[768,576]{0,1:T(8,128)}, u32[]{:S(2)}) copy-start(f32[768,576]{0,1:T(8,128)} %param.25) | copy-start | bytes 5308420
  3.6 16.7 %collective-permute-start = (bf16[160,768]{1,0:T(8,128)(2,1)S(1)}, bf16[160,768]{1,0:T(8,128)(2,1)S(1)}, u32[]{:S(2)}, u32[]{:S(2)}) collective-permute-start(bf16[160,768]{1,0:T(8,128)(2,1)S(1)} %get-tuple-element.107), channel_id=1, source_target_pairs={{0,1},{1,0},{2,3},{3,2},{4,5},{5,4},{6,7},{7,6},{8,9},{9,8},{10,11... | collective-permute-start | bytes 737288 | tf_op jit(solution)/shard_map/ppermute | solution.py:705
  6.7 11.5 %collective-permute-start.8 = (bf16[144,768]{1,0:T(8,128)(2,1)S(1)}, bf16[144,768]{1,0:T(8,128)(2,1)S(1)}, u32[]{:S(2)}, u32[]{:S(2)}) collective-permute-start(bf16[144,768]{1,0:T(8,128)(2,1)S(1)} %get-tuple-element.112), channel_id=1, source_target_pairs={{0,1},{1,0},{2,3},{3,2},{4,5},{5,4},{6,7},{7,6},{8,9},{9,8},{10,11... | collective-permute-start | bytes 663560 | tf_op jit(solution)/shard_map/ppermute | solution.py:705
  6.7 16.5 %collective-permute-start.4 = (bf16[144,768]{1,0:T(8,128)(2,1)S(1)}, bf16[144,768]{1,0:T(8,128)(2,1)S(1)}, u32[]{:S(2)}, u32[]{:S(2)}) collective-permute-start(bf16[144,768]{1,0:T(8,128)(2,1)S(1)} %get-tuple-element.111), channel_id=1, source_target_pairs={{0,1},{1,0},{2,3},{3,2},{4,5},{5,4},{6,7},{7,6},{8,9},{9,8},{10,11... | collective-permute-start | bytes 663560 | tf_op jit(solution)/shard_map/ppermute | solution.py:705
  18.2 7.9 %collective-permute-start.9 = (bf16[144,768]{1,0:T(8,128)(2,1)S(1)}, bf16[144,768]{1,0:T(8,128)(2,1)S(1)}, u32[]{:S(2)}, u32[]{:S(2)}) collective-permute-start(bf16[144,768]{1,0:T(8,128)(2,1)S(1)} %collective-permute-done.8.refs_11_.refs_1_), channel_id=1, source_target_pairs={{0,8},{2,10},{4,12},{6,14},{8,0},{10,2},{12,4},{14,6},{16,24},{18,... | collective-permute-start | bytes 663560 | tf_op jit(solution)/shard_map/ppermute | solution.py:705
  20.3 10.2 %collective-permute-start.2 = (bf16[160,768]{1,0:T(8,128)(2,1)S(1)}, bf16[160,768]{1,0:T(8,128)(2,1)S(1)}, u32[]{:S(2)}, u32[]{:S(2)}) collective-permute-start(bf16[160,768]{1,0:T(8,128)(2,1)S(1)} %collective-permute-done.refs_5_.refs_8_), channel_id=1, source_target_pairs={{0,2},{2,0},{4,6},{6,4},{8,10},{10,8},{12,14},{14,12},{16,18},{18,... | collective-permute-start | bytes 737288 | tf_op jit(solution)/shard_map/ppermute | solution.py:705
  20.3 9.2 %collective-permute-start.1 = (bf16[160,768]{1,0:T(8,128)(2,1)S(1)}, bf16[160,768]{1,0:T(8,128)(2,1)S(1)}, u32[]{:S(2)}, u32[]{:S(2)}) collective-permute-start(bf16[160,768]{1,0:T(8,128)(2,1)S(1)} %collective-permute-done.refs_5_.refs_8_), channel_id=1, source_target_pairs={{0,8},{2,10},{4,12},{6,14},{8,0},{10,2},{12,4},{14,6},{16,24},{18,... | collective-permute-start | bytes 737288 | tf_op jit(solution)/shard_map/ppermute | solution.py:705
  21.2 9.9 %copy-start.6 = (f32[288,960]{1,0:T(8,128)S(1)}, f32[288,960]{1,0:T(8,128)}, u32[]{:S(2)}) copy-start(f32[288,960]{1,0:T(8,128)} %refs_2_.9) | copy-start | bytes 3317764
  21.2 9.9 %copy-start.10 = (f32[288,576]{1,0:T(8,128)S(1)}, f32[288,576]{1,0:T(8,128)}, u32[]{:S(2)}) copy-start(f32[288,576]{1,0:T(8,128)} %refs_3_.8) | copy-start | bytes 1990660
  21.2 9.9 %copy-start.14 = (bf16[1,128,576]{1,2,0:T(8,128)(2,1)S(1)}, bf16[1,128,576]{1,2,0:T(8,128)(2,1)}, u32[]{:S(2)}) copy-start(bf16[1,128,576]{1,2,0:T(8,128)(2,1)} %param.19) | copy-start | bytes 442372
  21.2 12.6 %collective-permute-start.12 = (bf16[288,768]{1,0:T(8,128)(2,1)S(1)}, bf16[288,768]{1,0:T(8,128)(2,1)S(1)}, u32[]{:S(2)}, u32[]{:S(2)}) collective-permute-start(bf16[288,768]{1,0:T(8,128)(2,1)S(1)} %pack_down.1), channel_id=1, source_target_pairs={{0,1},{1,0},{2,3},{3,2},{4,5},{5,4},{6,7},{7,6},{8,9},{9,8},{10,11... | collective-permute-start | bytes 1327112 | tf_op jit(solution)/shard_map/ppermute | solution.py:705
  23.2 7.3 %collective-permute-start.5 = (bf16[144,768]{1,0:T(8,128)(2,1)S(1)}, bf16[144,768]{1,0:T(8,128)(2,1)S(1)}, u32[]{:S(2)}, u32[]{:S(2)}) collective-permute-start(bf16[144,768]{1,0:T(8,128)(2,1)S(1)} %collective-permute-done.4.refs_7_), channel_id=1, source_target_pairs={{0,4},{2,6},{4,0},{6,2},{8,12},{10,14},{12,8},{14,10},{16,20},{18,... | collective-permute-start | bytes 663560 | tf_op jit(solution)/shard_map/ppermute | solution.py:705
  26.1 4.9 %collective-permute-start.11 = (bf16[144,768]{1,0:T(8,128)(2,1)S(1)}, bf16[144,768]{1,0:T(8,128)(2,1)S(1)}, u32[]{:S(2)}, u32[]{:S(2)}) collective-permute-start(bf16[144,768]{1,0:T(8,128)(2,1)S(1)} %collective-permute-done.9.refs_12_), channel_id=1, source_target_pairs={{0,2},{2,0},{4,6},{6,4},{8,10},{10,8},{12,14},{14,12},{16,18},{18,... | collective-permute-start | bytes 663560 | tf_op jit(solution)/shard_map/ppermute | solution.py:705
  29.5 1.6 %collective-permute-start.3 = (bf16[160,768]{1,0:T(8,128)(2,1)S(1)}, bf16[160,768]{1,0:T(8,128)(2,1)S(1)}, u32[]{:S(2)}, u32[]{:S(2)}) collective-permute-start(bf16[160,768]{1,0:T(8,128)(2,1)S(1)} %collective-permute-done.1.refs_9_), channel_id=1, source_target_pairs={{0,2},{2,0},{4,6},{6,4},{8,10},{10,8},{12,14},{14,12},{16,18},{18,... | collective-permute-start | bytes 737288 | tf_op jit(solution)/shard_map/ppermute | solution.py:705
  30.5 3.8 %collective-permute-start.6 = (bf16[144,768]{1,0:T(8,128)(2,1)S(1)}, bf16[144,768]{1,0:T(8,128)(2,1)S(1)}, u32[]{:S(2)}, u32[]{:S(2)}) collective-permute-start(bf16[144,768]{1,0:T(8,128)(2,1)S(1)} %collective-permute-done.4.refs_7_), channel_id=1, source_target_pairs={{0,2},{2,0},{4,6},{6,4},{8,10},{10,8},{12,14},{14,12},{16,18},{18,... | collective-permute-start | bytes 663560 | tf_op jit(solution)/shard_map/ppermute | solution.py:705
  30.5 3.8 %collective-permute-start.10 = (bf16[144,768]{1,0:T(8,128)(2,1)S(1)}, bf16[144,768]{1,0:T(8,128)(2,1)S(1)}, u32[]{:S(2)}, u32[]{:S(2)}) collective-permute-start(bf16[144,768]{1,0:T(8,128)(2,1)S(1)} %collective-permute-done.8.refs_11_.refs_1_), channel_id=1, source_target_pairs={{0,2},{2,0},{4,6},{6,4},{8,10},{10,8},{12,14},{14,12},{16,18},{18,... | collective-permute-start | bytes 663560 | tf_op jit(solution)/shard_map/ppermute | solution.py:705
  31.0 3.3 %collective-permute-start.7 = (bf16[144,768]{1,0:T(8,128)(2,1)S(1)}, bf16[144,768]{1,0:T(8,128)(2,1)S(1)}, u32[]{:S(2)}, u32[]{:S(2)}) collective-permute-start(bf16[144,768]{1,0:T(8,128)(2,1)S(1)} %collective-permute-done.5.refs_8_), channel_id=1, source_target_pairs={{0,2},{2,0},{4,6},{6,4},{8,10},{10,8},{12,14},{14,12},{16,18},{18,... | collective-permute-start | bytes 663560 | tf_op jit(solution)/shard_map/ppermute | solution.py:705
  33.8 3.5 %collective-permute-start.13 = (bf16[288,768]{1,0:T(8,128)(2,1)S(1)}, bf16[288,768]{1,0:T(8,128)(2,1)S(1)}, u32[]{:S(2)}, u32[]{:S(2)}) collective-permute-start(bf16[288,768]{1,0:T(8,128)(2,1)S(1)} %pass_on.1.refs_5_), channel_id=1, source_target_pairs={{0,2},{2,0},{4,6},{6,4},{8,10},{10,8},{12,14},{14,12},{16,18},{18,... | collective-permute-start | bytes 1327112 | tf_op jit(solution)/shard_map/ppermute | solution.py:705
  37.2 3.5 %collective-permute-start.14 = (bf16[1,2,8,72,384]{4,3,2,1,0:T(8,128)(2,1)S(1)}, bf16[1,2,8,72,384]{4,3,2,1,0:T(8,128)(2,1)S(1)}, u32[]{:S(2)}, u32[]{:S(2)}) collective-permute-start(bf16[1,2,8,72,384]{4,3,2,1,0:T(8,128)(2,1)S(1)} %get-tuple-element.121), channel_id=1, source_target_pairs={{0,2},{2,0},{4,6},{6,4},{8,10},{10,8},{12,14},{14,12},{16,18},{18,... | collective-permute-start | bytes 2654216 | tf_op jit(solution)/shard_map/ppermute | solution.py:705
  40.0 5.2 %collective-permute-start.15 = (bf16[2,2,8,72,384]{4,3,2,1,0:T(8,128)(2,1)S(1)}, bf16[2,2,8,72,384]{4,3,2,1,0:T(8,128)(2,1)S(1)}, u32[]{:S(2)}, u32[]{:S(2)}) collective-permute-start(bf16[2,2,8,72,384]{4,3,2,1,0:T(8,128)(2,1)S(1)} %get-tuple-element.132), channel_id=1, source_target_pairs={{0,2},{2,0},{4,6},{6,4},{8,10},{10,8},{12,14},{14,12},{16,18},{18,... | collective-permute-start | bytes 5308424 | tf_op jit(solution)/shard_map/ppermute | solution.py:705
  40.9 12.3 %collective-permute-start.19 = (bf16[8,72,384]{2,1,0:T(8,128)(2,1)S(1)}, bf16[8,72,384]{2,1,0:T(8,128)(2,1)S(1)}, u32[]{:S(2)}, u32[]{:S(2)}) collective-permute-start(bf16[8,72,384]{2,1,0:T(8,128)(2,1)S(1)} %get-tuple-element.141), channel_id=1, source_target_pairs={{0,1},{1,0},{2,3},{3,2},{4,5},{5,4},{6,7},{7,6},{8,9},{9,8},{10,11... | collective-permute-start | bytes 1327112 | tf_op jit(solution)/shard_map/ppermute | solution.py:705
  45.8 13.1 %collective-permute-start.16 = (bf16[2,4,72,384]{3,2,1,0:T(8,128)(2,1)S(1)}, bf16[2,4,72,384]{3,2,1,0:T(8,128)(2,1)S(1)}, u32[]{:S(2)}, u32[]{:S(2)}) collective-permute-start(bf16[2,4,72,384]{3,2,1,0:T(8,128)(2,1)S(1)} %get-tuple-element.136), channel_id=1, source_target_pairs={{0,4},{2,6},{4,0},{6,2},{8,12},{10,14},{12,8},{14,10},{16,20},{18,... | collective-permute-start | bytes 1327112 | tf_op jit(solution)/shard_map/ppermute | solution.py:705
  47.3 11.9 %collective-permute-start.17 = (bf16[4,2,72,384]{3,2,1,0:T(8,128)(2,1)S(1)}, bf16[4,2,72,384]{3,2,1,0:T(8,128)(2,1)S(1)}, u32[]{:S(2)}, u32[]{:S(2)}) collective-permute-start(bf16[4,2,72,384]{3,2,1,0:T(8,128)(2,1)S(1)} %get-tuple-element.138), channel_id=1, source_target_pairs={{0,8},{2,10},{4,12},{6,14},{8,0},{10,2},{12,4},{14,6},{16,24},{18,... | collective-permute-start | bytes 1327112 | tf_op jit(solution)/shard_map/ppermute | solution.py:705
  52.3 2.8 %collective-permute-start.18 = (bf16[1,2,8,80,384]{4,3,2,1,0:T(8,128)(2,1)S(1)}, bf16[1,2,8,80,384]{4,3,2,1,0:T(8,128)(2,1)S(1)}, u32[]{:S(2)}, u32[]{:S(2)}) collective-permute-start(bf16[1,2,8,80,384]{4,3,2,1,0:T(8,128)(2,1)S(1)} %get-tuple-element.140), channel_id=1, source_target_pairs={{0,2},{2,0},{4,6},{6,4},{8,10},{10,8},{12,14},{14,12},{16,18},{18,... | collective-permute-start | bytes 2949128 | tf_op jit(solution)/shard_map/ppermute | solution.py:705
  53.3 9.9 %collective-permute-start.22 = (bf16[4,72,384]{2,1,0:T(8,128)(2,1)S(1)}, bf16[4,72,384]{2,1,0:T(8,128)(2,1)S(1)}, u32[]{:S(2)}, u32[]{:S(2)}) collective-permute-start(bf16[4,72,384]{2,1,0:T(8,128)(2,1)S(1)} %get-tuple-element.149), channel_id=1, source_target_pairs={{0,4},{2,6},{4,0},{6,2},{8,12},{10,14},{12,8},{14,10},{16,20},{18,... | collective-permute-start | bytes 663560 | tf_op jit(solution)/shard_map/ppermute | solution.py:705
  55.4 13.2 %collective-permute-start.24 = (bf16[8,80,384]{2,1,0:T(8,128)(2,1)S(1)}, bf16[8,80,384]{2,1,0:T(8,128)(2,1)S(1)}, u32[]{:S(2)}, u32[]{:S(2)}) collective-permute-start(bf16[8,80,384]{2,1,0:T(8,128)(2,1)S(1)} %get-tuple-element.152), channel_id=1, source_target_pairs={{0,1},{1,0},{2,3},{3,2},{4,5},{5,4},{6,7},{7,6},{8,9},{9,8},{10,11... | collective-permute-start | bytes 1474568 | tf_op jit(solution)/shard_map/ppermute | solution.py:705
  59.4 9.9 %collective-permute-start.20 = (bf16[2,2,72,384]{3,2,1,0:T(8,128)(2,1)S(1)}, bf16[2,2,72,384]{3,2,1,0:T(8,128)(2,1)S(1)}, u32[]{:S(2)}, u32[]{:S(2)}) collective-permute-start(bf16[2,2,72,384]{3,2,1,0:T(8,128)(2,1)S(1)} %get-tuple-element.146), channel_id=1, source_target_pairs={{0,8},{2,10},{4,12},{6,14},{8,0},{10,2},{12,4},{14,6},{16,24},{18,... | collective-permute-start | bytes 663560 | tf_op jit(solution)/shard_map/ppermute | solution.py:705
  61.0 8.3 %collective-permute-start.21 = (bf16[2,2,72,384]{3,2,1,0:T(8,128)(2,1)S(1)}, bf16[2,2,72,384]{3,2,1,0:T(8,128)(2,1)S(1)}, u32[]{:S(2)}, u32[]{:S(2)}) collective-permute-start(bf16[2,2,72,384]{3,2,1,0:T(8,128)(2,1)S(1)} %get-tuple-element.148), channel_id=1, source_target_pairs={{0,4},{2,6},{4,0},{6,2},{8,12},{10,14},{12,8},{14,10},{16,20},{18,... | collective-permute-start | bytes 663560 | tf_op jit(solution)/shard_map/ppermute | solution.py:705
  63.2 6.1 %collective-permute-start.23 = (bf16[2,72,384]{2,1,0:T(8,128)(2,1)S(1)}, bf16[2,72,384]{2,1,0:T(8,128)(2,1)S(1)}, u32[]{:S(2)}, u32[]{:S(2)}) collective-permute-start(bf16[2,72,384]{2,1,0:T(8,128)(2,1)S(1)} %get-tuple-element.151), channel_id=1, source_target_pairs={{0,8},{2,10},{4,12},{6,14},{8,0},{10,2},{12,4},{14,6},{16,24},{18,... | collective-permute-start | bytes 331784 | tf_op jit(solution)/shard_map/ppermute | solution.py:705
  68.7 10.1 %collective-permute-start.27 = (bf16[4,80,384]{2,1,0:T(8,128)(2,1)S(1)}, bf16[4,80,384]{2,1,0:T(8,128)(2,1)S(1)}, u32[]{:S(2)}, u32[]{:S(2)}) collective-permute-start(bf16[4,80,384]{2,1,0:T(8,128)(2,1)S(1)} %get-tuple-element.159), channel_id=1, source_target_pairs={{0,4},{2,6},{4,0},{6,2},{8,12},{10,14},{12,8},{14,10},{16,20},{18,... | collective-permute-start | bytes 737288 | tf_op jit(solution)/shard_map/ppermute | solution.py:705
  69.4 9.4 %collective-permute-start.26 = (bf16[3,72,384]{2,1,0:T(8,128)(2,1)S(1)}, bf16[3,72,384]{2,1,0:T(8,128)(2,1)S(1)}, u32[]{:S(2)}, u32[]{:S(2)}) collective-permute-start(bf16[3,72,384]{2,1,0:T(8,128)(2,1)S(1)} %get-tuple-element.157), channel_id=1, source_target_pairs={{0,16},{2,18},{4,20},{6,22},{8,24},{10,26},{12,28},{14,30},{16,0},... | collective-permute-start | bytes 497672 | tf_op jit(solution)/shard_map/ppermute | solution.py:705
  72.1 4.7 %collective-permute-start.25 = (bf16[2,72,384]{2,1,0:T(8,128)(2,1)S(1)}, bf16[2,72,384]{2,1,0:T(8,128)(2,1)S(1)}, u32[]{:S(2)}, u32[]{:S(2)}) collective-permute-start(bf16[2,72,384]{2,1,0:T(8,128)(2,1)S(1)} %get-tuple-element.155), channel_id=1, source_target_pairs={{0,1},{1,0},{2,3},{3,2},{4,5},{5,4},{6,7},{7,6},{8,9},{9,8},{10,11... | collective-permute-start | bytes 331784 | tf_op jit(solution)/shard_map/ppermute | solution.py:705
  78.9 8.1 %collective-permute-start.30 = (bf16[2,80,384]{2,1,0:T(8,128)(2,1)S(1)}, bf16[2,80,384]{2,1,0:T(8,128)(2,1)S(1)}, u32[]{:S(2)}, u32[]{:S(2)}) collective-permute-start(bf16[2,80,384]{2,1,0:T(8,128)(2,1)S(1)} %get-tuple-element.164), channel_id=1, source_target_pairs={{0,8},{2,10},{4,12},{6,14},{8,0},{10,2},{12,4},{14,6},{16,24},{18,... | collective-permute-start | bytes 368648 | tf_op jit(solution)/shard_map/ppermute | solution.py:705
  79.0 8.0 %collective-permute-start.28 = (bf16[2,72,384]{2,1,0:T(8,128)(2,1)S(1)}, bf16[2,72,384]{2,1,0:T(8,128)(2,1)S(1)}, u32[]{:S(2)}, u32[]{:S(2)}) collective-permute-start(bf16[2,72,384]{2,1,0:T(8,128)(2,1)S(1)} %get-tuple-element.160.refs_0_), channel_id=1, source_target_pairs={{0,16},{2,18},{4,20},{6,22},{8,24},{10,26},{12,28},{14,30},{16,0},... | collective-permute-start | bytes 331784 | tf_op jit(solution)/shard_map/ppermute | solution.py:705
  82.1 4.2 %collective-permute-start.29 = (bf16[72,384]{1,0:T(8,128)(2,1)S(1)}, bf16[72,384]{1,0:T(8,128)(2,1)S(1)}, u32[]{:S(2)}, u32[]{:S(2)}) collective-permute-start(bf16[72,384]{1,0:T(8,128)(2,1)S(1)} %get-tuple-element.162), channel_id=1, source_target_pairs={{0,1},{1,0},{2,3},{3,2},{4,5},{5,4},{6,7},{7,6},{8,9},{9,8},{10,11... | collective-permute-start | bytes 165896 | tf_op jit(solution)/shard_map/ppermute | solution.py:705
  87.2 8.5 %collective-permute-start.31 = (bf16[3,80,384]{2,1,0:T(8,128)(2,1)S(1)}, bf16[3,80,384]{2,1,0:T(8,128)(2,1)S(1)}, u32[]{:S(2)}, u32[]{:S(2)}) collective-permute-start(bf16[3,80,384]{2,1,0:T(8,128)(2,1)S(1)} %get-tuple-element.165.refs_0_), channel_id=1, source_target_pairs={{0,16},{2,18},{4,20},{6,22},{8,24},{10,26},{12,28},{14,30},{16,0},... | collective-permute-start | bytes 552968 | tf_op jit(solution)/shard_map/ppermute | solution.py:705
  88.2 5.5 %collective-permute-start.32 = (bf16[2,72,384]{2,1,0:T(8,128)(2,1)S(1)}, bf16[2,72,384]{2,1,0:T(8,128)(2,1)S(1)}, u32[]{:S(2)}, u32[]{:S(2)}) collective-permute-start(bf16[2,72,384]{2,1,0:T(8,128)(2,1)S(1)} %get-tuple-element.167.refs_3_), channel_id=1, source_target_pairs={{0,8},{2,10},{4,12},{6,14},{8,0},{10,2},{12,4},{14,6},{16,24},{18,... | collective-permute-start | bytes 331784 | tf_op jit(solution)/shard_map/ppermute | solution.py:705
  95.8 9.5 %collective-permute-start.34 = (bf16[3,2,72,384]{3,2,1,0:T(8,128)(2,1)S(1)}, bf16[3,2,72,384]{3,2,1,0:T(8,128)(2,1)S(1)}, u32[]{:S(2)}, u32[]{:S(2)}) collective-permute-start(bf16[3,2,72,384]{3,2,1,0:T(8,128)(2,1)S(1)} %get-tuple-element.168.refs_8_.refs_0_), channel_id=1, source_target_pairs={{0,4},{2,6},{4,0},{6,2},{8,12},{10,14},{12,8},{14,10},{16,20},{18,... | collective-permute-start | bytes 995336 | tf_op jit(solution)/shard_map/ppermute | solution.py:705
  96.8 5.2 %collective-permute-start.33 = (bf16[80,384]{1,0:T(8,128)(2,1)S(1)}, bf16[80,384]{1,0:T(8,128)(2,1)S(1)}, u32[]{:S(2)}, u32[]{:S(2)}) collective-permute-start(bf16[80,384]{1,0:T(8,128)(2,1)S(1)} %get-tuple-element.171.refs_0_), channel_id=1, source_target_pairs={{0,16},{2,18},{4,20},{6,22},{8,24},{10,26},{12,28},{14,30},{16,0},... | collective-permute-start | bytes 184328 | tf_op jit(solution)/shard_map/ppermute | solution.py:705
  97.0 6.9 %collective-permute-start.35 = (bf16[2,72,384]{2,1,0:T(8,128)(2,1)S(1)}, bf16[2,72,384]{2,1,0:T(8,128)(2,1)S(1)}, u32[]{:S(2)}, u32[]{:S(2)}) collective-permute-start(bf16[2,72,384]{2,1,0:T(8,128)(2,1)S(1)} %get-tuple-element.172.refs_2_), channel_id=1, source_target_pairs={{0,8},{2,10},{4,12},{6,14},{8,0},{10,2},{12,4},{14,6},{16,24},{18,... | collective-permute-start | bytes 331784 | tf_op jit(solution)/shard_map/ppermute | solution.py:705
  105.4 8.2 %collective-permute-start.40 = (bf16[2,2,72,384]{3,2,1,0:T(8,128)(2,1)S(1)}, bf16[2,2,72,384]{3,2,1,0:T(8,128)(2,1)S(1)}, u32[]{:S(2)}, u32[]{:S(2)}) collective-permute-start(bf16[2,2,72,384]{3,2,1,0:T(8,128)(2,1)S(1)} %get-tuple-element.174.refs_2_), channel_id=1, source_target_pairs={{0,4},{2,6},{4,0},{6,2},{8,12},{10,14},{12,8},{14,10},{16,20},{18,... | collective-permute-start | bytes 663560 | tf_op jit(solution)/shard_map/ppermute | solution.py:705
  105.9 7.7 %collective-permute-start.39 = (bf16[2,2,72,384]{3,2,1,0:T(8,128)(2,1)S(1)}, bf16[2,2,72,384]{3,2,1,0:T(8,128)(2,1)S(1)}, u32[]{:S(2)}, u32[]{:S(2)}) collective-permute-start(bf16[2,2,72,384]{3,2,1,0:T(8,128)(2,1)S(1)} %get-tuple-element.173.refs_2_.refs_0_), channel_id=1, source_target_pairs={{0,8},{2,10},{4,12},{6,14},{8,0},{10,2},{12,4},{14,6},{16,24},{18,... | collective-permute-start | bytes 663560 | tf_op jit(solution)/shard_map/ppermute | solution.py:705
  106.6 2.5 %collective-permute-start.41 = (bf16[1,2,4,72,384]{4,3,2,1,0:T(8,128)(2,1)S(1)}, bf16[1,2,4,72,384]{4,3,2,1,0:T(8,128)(2,1)S(1)}, u32[]{:S(2)}, u32[]{:S(2)}) collective-permute-start(bf16[1,2,4,72,384]{4,3,2,1,0:T(8,128)(2,1)S(1)} %get-tuple-element.175.refs_0_), channel_id=1, source_target_pairs={{0,2},{2,0},{4,6},{6,4},{8,10},{10,8},{12,14},{14,12},{16,18},{18,... | collective-permute-start | bytes 1327112 | tf_op jit(solution)/shard_map/ppermute | solution.py:705
  106.7 10.4 %collective-permute-start.38 = (bf16[2,80,384]{2,1,0:T(8,128)(2,1)S(1)}, bf16[2,80,384]{2,1,0:T(8,128)(2,1)S(1)}, u32[]{:S(2)}, u32[]{:S(2)}) collective-permute-start(bf16[2,80,384]{2,1,0:T(8,128)(2,1)S(1)} %share_qkv_out_high.1.refs_5_.refs_0_), channel_id=1, source_target_pairs={{0,12},{2,14},{4,8},{6,10},{8,4},{10,6},{12,0},{14,2},{16,28},{18,... | collective-permute-start | bytes 368648 | tf_op jit(solution)/shard_map/ppermute | solution.py:705
  109.0 8.1 %collective-permute-start.37 = (bf16[2,80,384]{2,1,0:T(8,128)(2,1)S(1)}, bf16[2,80,384]{2,1,0:T(8,128)(2,1)S(1)}, u32[]{:S(2)}, u32[]{:S(2)}) collective-permute-start(bf16[2,80,384]{2,1,0:T(8,128)(2,1)S(1)} %share_qkv_out_high.1.refs_5_.refs_0_), channel_id=1, source_target_pairs={{0,8},{2,10},{4,12},{6,14},{8,0},{10,2},{12,4},{14,6},{16,24},{18,... | collective-permute-start | bytes 368648 | tf_op jit(solution)/shard_map/ppermute | solution.py:705
  109.2 7.9 %collective-permute-start.36 = (bf16[2,80,384]{2,1,0:T(8,128)(2,1)S(1)}, bf16[2,80,384]{2,1,0:T(8,128)(2,1)S(1)}, u32[]{:S(2)}, u32[]{:S(2)}) collective-permute-start(bf16[2,80,384]{2,1,0:T(8,128)(2,1)S(1)} %share_qkv_out_high.1.refs_5_.refs_0_), channel_id=1, source_target_pairs={{0,4},{2,6},{4,0},{6,2},{8,12},{10,14},{12,8},{14,10},{16,20},{18,... | collective-permute-start | bytes 368648 | tf_op jit(solution)/shard_map/ppermute | solution.py:705
  113.6 4.1 %collective-permute-start.43 = (bf16[2,2,4,72,384]{4,3,2,1,0:T(8,128)(2,1)S(1)}, bf16[2,2,4,72,384]{4,3,2,1,0:T(8,128)(2,1)S(1)}, u32[]{:S(2)}, u32[]{:S(2)}) collective-permute-start(bf16[2,2,4,72,384]{4,3,2,1,0:T(8,128)(2,1)S(1)} %share_gate_up.1.refs_0_), channel_id=1, source_target_pairs={{0,2},{2,0},{4,6},{6,4},{8,10},{10,8},{12,14},{14,12},{16,18},{18,... | collective-permute-start | bytes 2654216 | tf_op jit(solution)/shard_map/ppermute | solution.py:705
  117.2 3.9 %collective-permute-start.42 = (bf16[1,2,4,80,384]{4,3,2,1,0:T(8,128)(2,1)S(1)}, bf16[1,2,4,80,384]{4,3,2,1,0:T(8,128)(2,1)S(1)}, u32[]{:S(2)}, u32[]{:S(2)}) collective-permute-start(bf16[1,2,4,80,384]{4,3,2,1,0:T(8,128)(2,1)S(1)} %share_qkv_out.1.refs_7_.refs_0_), channel_id=1, source_target_pairs={{0,2},{2,0},{4,6},{6,4},{8,10},{10,8},{12,14},{14,12},{16,18},{18,... | collective-permute-start | bytes 1474568 | tf_op jit(solution)/shard_map/ppermute | solution.py:705
  (20 other events, 148.7 us)

commit v15 on v14

--- a/solution.py
+++ b/solution.py
@@ -643,13 +643,13 @@
             base = (idx_ref[1] ^ far) * height
             for at_chunk in range(chunks):
 
-                def eight_rows(i, carry, at_chunk=at_chunk, share=share, base=base):
-                    at_row = at_chunk * chunk + i * 8
-                    near_rows = pl.ds(pl.multiple_of(share * height + at_row, 8), 8)
-                    rows = pl.ds(pl.multiple_of(base + at_row, 8), 8)
+                def some_rows(i, carry, at_chunk=at_chunk, share=share, base=base):
+                    at_row = at_chunk * chunk + i * 24
+                    near_rows = pl.ds(pl.multiple_of(share * height + at_row, 8), 24)
+                    rows = pl.ds(pl.multiple_of(base + at_row, 8), 24)
                     for k in range(count):
-                        for at in range(0, columns[k], 768):
-                            size = min(768, columns[k] - at)
+                        for at in range(0, columns[k], 384):
+                            size = min(384, columns[k] - at)
                             where = slice(at, at + size)
                             results = adamw_rows(
                                 *[state_refs[j][rows, where] for j in order[k]],
@@ -661,7 +661,7 @@
                                 buffers[j][near_rows, where] = result
                     return carry
 
-                lax.fori_loop(0, chunk // 8, eight_rows, 0, unroll=3)
+                lax.fori_loop(0, chunk // 24, some_rows, 0, unroll=2 if chunk > 24 else 1)
                 near_rows = pl.ds(share * height + at_chunk * chunk, chunk)
                 rows = pl.ds(pl.multiple_of(base + at_chunk * chunk, 8), chunk)
                 for j in range(3 * count):

time: 126 us -> 126 us (level)
  no operation moved by 1% of the time
where the time goes in v15:
time: 126 us
  starting transfers between devices  45.9 us (36%)
  waiting for transfers between devices  42.2 us (33%)
  Pallas kernels  34.9 us (28%)
  between operations  1.41 us (1%)
    ppermute x44, starting transfers between devices, swap(): return lax.ppermute(values, axis, [(i, i ^ mask) for i in range(size)])  45.9 us
    ppermute x44, waiting for transfers between devices, swap(): return lax.ppermute(values, axis, [(i, i ^ mask) for i in range(size)])  42.2 us
    pallas_call x4, Pallas kernels, update_rows(): pl.pallas_call(kernel, out_shape=tuple((sds(a.shape, F32) for a in [*stat...  14.3 us
    pallas_call x5, Pallas kernels, call(): pl.pallas_call(kernel, out_shape=tuple(outs), in_specs=[pl.BlockSpec(memo...  14.1 us
    pallas_call x18, Pallas kernels, step(): pl.pallas_call(kernel, out_shape=tuple(outs), in_specs=[pl.BlockSpec(memo...  3.53 us
    pallas_call x2, Pallas kernels, pack_kernel(): pl.pallas_call(kernel, out_shape=tuple(outs), in_specs=[pl.BlockSpec(memo...  2.97 us
  transfers between devices with their start and end apart: 44, of which 19 were waited for; matrix products, arithmetic and copies ran while one was open for 0% of the time, Pallas kernels for 22%

profile of v15, /device:TPU:0, one launch (start us, length us, event | category | flops | bytes accessed | tf_op | source)
XLA Modules:
  0.0 125.6 jit_solution(17099378200953764209)
XLA Ops:
  1.4 2.2 %pack_first.1 = (bf16[160,768]{1,0:T(8,128)(2,1)S(1)}, bf16[144,768]{1,0:T(8,128)(2,1)S(1)}, bf16[144,768]{1,0:T(8,128)(2,1)S(1)}) custom-call(s32[4]{0:T(128)S(1)} %pad_add_fusion.idx_ref.refs_0_, f32[288,960]{1,0:T(8,128)} %refs_2_.9, f32[288,576]{1,0:T(8,128)} %refs_3_.8, f32[2,288]{1,0:T(2,128)S(1)} %copy-done.16, f32[288,3072]{1,0:T(8,128)} %refs_1_.5, ...), custom_call_target="tpu_custom_call" | custom-call | flops 10000000000 | tf_op jit(solution)/shard_map/pack_first/pallas_call | solution.py:242
  3.6 3.0 %collective-permute-start = (bf16[160,768]{1,0:T(8,128)(2,1)S(1)}, bf16[160,768]{1,0:T(8,128)(2,1)S(1)}, u32[]{:S(2)}, u32[]{:S(2)}) collective-permute-start(bf16[160,768]{1,0:T(8,128)(2,1)S(1)} %get-tuple-element.107), channel_id=1, source_target_pairs={{0,1},{1,0},{2,3},{3,2},{4,5},{5,4},{6,7},{7,6},{8,9},{9,8},{10,11... | collective-permute-start | bytes 737288 | tf_op jit(solution)/shard_map/ppermute | solution.py:705
  6.7 1.9 %collective-permute-start.4 = (bf16[144,768]{1,0:T(8,128)(2,1)S(1)}, bf16[144,768]{1,0:T(8,128)(2,1)S(1)}, u32[]{:S(2)}, u32[]{:S(2)}) collective-permute-start(bf16[144,768]{1,0:T(8,128)(2,1)S(1)} %get-tuple-element.111), channel_id=1, source_target_pairs={{0,1},{1,0},{2,3},{3,2},{4,5},{5,4},{6,7},{7,6},{8,9},{9,8},{10,11... | collective-permute-start | bytes 663560 | tf_op jit(solution)/shard_map/ppermute | solution.py:705
  8.7 9.5 %collective-permute-done.8.refs_11_.refs_1_ = bf16[144,768]{1,0:T(8,128)(2,1)S(1)} collective-permute-done((bf16[144,768]{1,0:T(8,128)(2,1)S(1)}, bf16[144,768]{1,0:T(8,128)(2,1)S(1)}, u32[]{:S(2)}, u32[]{:S(2)}) %collective-permute-start.8) | collective-permute-done | bytes 221216 | tf_op jit(solution)/shard_map/ppermute | solution.py:705
  18.2 2.1 %collective-permute-start.9 = (bf16[144,768]{1,0:T(8,128)(2,1)S(1)}, bf16[144,768]{1,0:T(8,128)(2,1)S(1)}, u32[]{:S(2)}, u32[]{:S(2)}) collective-permute-start(bf16[144,768]{1,0:T(8,128)(2,1)S(1)} %collective-permute-done.8.refs_11_.refs_1_), channel_id=1, source_target_pairs={{0,8},{2,10},{4,12},{6,14},{8,0},{10,2},{12,4},{14,6},{16,24},{18,... | collective-permute-start | bytes 663560 | tf_op jit(solution)/shard_map/ppermute | solution.py:705
  21.2 2.0 %collective-permute-start.12 = (bf16[288,768]{1,0:T(8,128)(2,1)S(1)}, bf16[288,768]{1,0:T(8,128)(2,1)S(1)}, u32[]{:S(2)}, u32[]{:S(2)}) collective-permute-start(bf16[288,768]{1,0:T(8,128)(2,1)S(1)} %pack_down.1), channel_id=1, source_target_pairs={{0,1},{1,0},{2,3},{3,2},{4,5},{5,4},{6,7},{7,6},{8,9},{9,8},{10,11... | collective-permute-start | bytes 1327112 | tf_op jit(solution)/shard_map/ppermute | solution.py:705
  23.2 1.5 %collective-permute-start.5 = (bf16[144,768]{1,0:T(8,128)(2,1)S(1)}, bf16[144,768]{1,0:T(8,128)(2,1)S(1)}, u32[]{:S(2)}, u32[]{:S(2)}) collective-permute-start(bf16[144,768]{1,0:T(8,128)(2,1)S(1)} %collective-permute-done.4.refs_7_), channel_id=1, source_target_pairs={{0,4},{2,6},{4,0},{6,2},{8,12},{10,14},{12,8},{14,10},{16,20},{18,... | collective-permute-start | bytes 663560 | tf_op jit(solution)/shard_map/ppermute | solution.py:705
  24.7 1.4 %collective-permute-done.9.refs_12_ = bf16[144,768]{1,0:T(8,128)(2,1)S(1)} collective-permute-done((bf16[144,768]{1,0:T(8,128)(2,1)S(1)}, bf16[144,768]{1,0:T(8,128)(2,1)S(1)}, u32[]{:S(2)}, u32[]{:S(2)}) %collective-permute-start.9) | collective-permute-done | bytes 221216 | tf_op jit(solution)/shard_map/ppermute | solution.py:705
  26.1 3.4 %collective-permute-done.1.refs_9_ = bf16[160,768]{1,0:T(8,128)(2,1)S(1)} collective-permute-done((bf16[160,768]{1,0:T(8,128)(2,1)S(1)}, bf16[160,768]{1,0:T(8,128)(2,1)S(1)}, u32[]{:S(2)}, u32[]{:S(2)}) %collective-permute-start.1) | collective-permute-done | bytes 245792 | tf_op jit(solution)/shard_map/ppermute | solution.py:705
  29.5 1.0 collective-permute-done.5.refs_8_
  31.2 2.6 %attention.1 = (bf16[128,960]{1,0:T(8,128)(2,1)S(1)}, bf16[128,576]{1,0:T(8,128)(2,1)S(1)}, f32[128,128]{1,0:T(8,128)S(1)}, f32[128,128]{1,0:T(8,128)S(1)}, f32[...) custom-call(s32[4]{0:T(128)S(1)} %pad_add_fusion.idx_ref.refs_0_, ...), custom_call_target="tpu_custom_call" | custom-call | flops 1000000000 | tf_op jit(solution)/shard_map/attention/pallas_call | solution.py:152
  34.3 2.8 %feed_forward.1 = (f32[128,576]{1,0:T(8,128)S(1)}, bf16[128,576]{1,0:T(8,128)(2,1)S(1)}, f32[128,3072]{1,0:T(8,128)S(1)}, bf16[128,1536]{1,0:T(8,128)(2,1)S(1)},...) custom-call(s32[4]{0:T(128)S(1)} %pad_add_fusion.idx_ref.refs_0_, ...), custom_call_target="tpu_custom_call" | custom-call | flops 5000000000 | tf_op jit(solution)/shard_map/feed_forward/pallas_call | solution.py:152
  37.4 2.6 %feed_back.1 = (bf16[128,3072]{1,0:T(8,128)(2,1)S(1)}, bf16[2,2,8,72,384]{4,3,2,1,0:T(8,128)(2,1)S(1)}, bf16[2,2,8,72,384]{4,3,2,1,0:T(8,128)(2,1)S(1)}, bf16[576,1536]{1,0:T(8,128)(2,1)S(1)}) custom-call(s32[4]{0:T(128)S(1)} %pad_add_fusion.idx_ref.refs_0_, f32[128,3072]{1,0:T(8,128)S(1)} %get-tuple-element.115.refs_1_, ...), custom_call_target="tpu_custom_call" | custom-call | flops 20000000000 | tf_op jit(solution)/shard_map/feed_back/pallas_call | solution.py:152
  40.9 1.6 %collective-permute-start.19 = (bf16[8,72,384]{2,1,0:T(8,128)(2,1)S(1)}, bf16[8,72,384]{2,1,0:T(8,128)(2,1)S(1)}, u32[]{:S(2)}, u32[]{:S(2)}) collective-permute-start(bf16[8,72,384]{2,1,0:T(8,128)(2,1)S(1)} %get-tuple-element.141), channel_id=1, source_target_pairs={{0,1},{1,0},{2,3},{3,2},{4,5},{5,4},{6,7},{7,6},{8,9},{9,8},{10,11... | collective-permute-start | bytes 1327112 | tf_op jit(solution)/shard_map/ppermute | solution.py:705
  42.5 2.7 %middle_back.1 = (f32[128,576]{1,0:T(8,128)S(1)}, bf16[128,576]{1,0:T(8,128)(2,1)S(1)}, f32[1,576]{1,0:T(1,128)S(1)}) custom-call(s32[4]{0:T(128)S(1)} %pad_add_fusion.idx_ref.refs_0_, bf16[576,128]{1,0:T(8,128)(2,1)S(1)} %bitcast.70, f32[128,576]{1,0:T(8,128)S(1)} %get-tuple-element.113.refs_2_.refs_0_, ...), custom_call_target="tpu_custom_call" | custom-call | flops 20000000000 | tf_op jit(solution)/shard_map/middle_back/pallas_call | solution.py:152
  45.8 1.6 %collective-permute-start.16 = (bf16[2,4,72,384]{3,2,1,0:T(8,128)(2,1)S(1)}, bf16[2,4,72,384]{3,2,1,0:T(8,128)(2,1)S(1)}, u32[]{:S(2)}, u32[]{:S(2)}) collective-permute-start(bf16[2,4,72,384]{3,2,1,0:T(8,128)(2,1)S(1)} %get-tuple-element.136), channel_id=1, source_target_pairs={{0,4},{2,6},{4,0},{6,2},{8,12},{10,14},{12,8},{14,10},{16,20},{18,... | collective-permute-start | bytes 1327112 | tf_op jit(solution)/shard_map/ppermute | solution.py:705
  47.3 1.6 %collective-permute-start.17 = (bf16[4,2,72,384]{3,2,1,0:T(8,128)(2,1)S(1)}, bf16[4,2,72,384]{3,2,1,0:T(8,128)(2,1)S(1)}, u32[]{:S(2)}, u32[]{:S(2)}) collective-permute-start(bf16[4,2,72,384]{3,2,1,0:T(8,128)(2,1)S(1)} %get-tuple-element.138), channel_id=1, source_target_pairs={{0,8},{2,10},{4,12},{6,14},{8,0},{10,2},{12,4},{14,6},{16,24},{18,... | collective-permute-start | bytes 1327112 | tf_op jit(solution)/shard_map/ppermute | solution.py:705
  48.9 3.3 %attention_back.1 = (f32[128,576]{1,0:T(8,128)S(1)}, bf16[1,2,8,80,384]{4,3,2,1,0:T(8,128)(2,1)S(1)}, bf16[1,2,8,80,384]{4,3,2,1,0:T(8,128)(2,1)S(1)}, f32[8,128]{1,0:T(8,128)S(1)}) custom-call(s32[4]{0:T(128)S(1)} %pad_add_fusion.idx_ref.refs_0_, f32[128,576]{1,0:T(8,128)S(1)} %get-tuple-element.123.refs_4_.refs_1_.refs_3_, ...), custom_call_target="tpu_custom_call" | custom-call | flops 20000000000 | tf_op jit(solution)/shard_map/attention_back/pallas_call | solution.py:152
  53.3 1.8 %collective-permute-start.22 = (bf16[4,72,384]{2,1,0:T(8,128)(2,1)S(1)}, bf16[4,72,384]{2,1,0:T(8,128)(2,1)S(1)}, u32[]{:S(2)}, u32[]{:S(2)}) collective-permute-start(bf16[4,72,384]{2,1,0:T(8,128)(2,1)S(1)} %get-tuple-element.149), channel_id=1, source_target_pairs={{0,4},{2,6},{4,0},{6,2},{8,12},{10,14},{12,8},{14,10},{16,20},{18,... | collective-permute-start | bytes 663560 | tf_op jit(solution)/shard_map/ppermute | solution.py:705
  55.4 1.6 %collective-permute-start.24 = (bf16[8,80,384]{2,1,0:T(8,128)(2,1)S(1)}, bf16[8,80,384]{2,1,0:T(8,128)(2,1)S(1)}, u32[]{:S(2)}, u32[]{:S(2)}) collective-permute-start(bf16[8,80,384]{2,1,0:T(8,128)(2,1)S(1)} %get-tuple-element.152), channel_id=1, source_target_pairs={{0,1},{1,0},{2,3},{3,2},{4,5},{5,4},{6,7},{7,6},{8,9},{9,8},{10,11... | collective-permute-start | bytes 1474568 | tf_op jit(solution)/shard_map/ppermute | solution.py:705
  57.0 1.8 %collective-permute-done.16 = bf16[2,4,72,384]{3,2,1,0:T(8,128)(2,1)S(1)} collective-permute-done((bf16[2,4,72,384]{3,2,1,0:T(8,128)(2,1)S(1)}, bf16[2,4,72,384]{3,2,1,0:T(8,128)(2,1)S(1)}, u32[]{:S(2)}, u32[]{:S(2)}) %collective-permute-start.16) | collective-permute-done | bytes 442400 | tf_op jit(solution)/shard_map/ppermute | solution.py:705
  59.4 1.6 %collective-permute-start.20 = (bf16[2,2,72,384]{3,2,1,0:T(8,128)(2,1)S(1)}, bf16[2,2,72,384]{3,2,1,0:T(8,128)(2,1)S(1)}, u32[]{:S(2)}, u32[]{:S(2)}) collective-permute-start(bf16[2,2,72,384]{3,2,1,0:T(8,128)(2,1)S(1)} %get-tuple-element.146), channel_id=1, source_target_pairs={{0,8},{2,10},{4,12},{6,14},{8,0},{10,2},{12,4},{14,6},{16,24},{18,... | collective-permute-start | bytes 663560 | tf_op jit(solution)/shard_map/ppermute | solution.py:705
  61.0 1.2 collective-permute-start.21
  62.2 1.0 collective-permute-done.22
  63.2 2.1 %collective-permute-start.23 = (bf16[2,72,384]{2,1,0:T(8,128)(2,1)S(1)}, bf16[2,72,384]{2,1,0:T(8,128)(2,1)S(1)}, u32[]{:S(2)}, u32[]{:S(2)}) collective-permute-start(bf16[2,72,384]{2,1,0:T(8,128)(2,1)S(1)} %get-tuple-element.151), channel_id=1, source_target_pairs={{0,8},{2,10},{4,12},{6,14},{8,0},{10,2},{12,4},{14,6},{16,24},{18,... | collective-permute-start | bytes 331784 | tf_op jit(solution)/shard_map/ppermute | solution.py:705
  65.3 3.3 %collective-permute-done.24 = bf16[8,80,384]{2,1,0:T(8,128)(2,1)S(1)} collective-permute-done((bf16[8,80,384]{2,1,0:T(8,128)(2,1)S(1)}, bf16[8,80,384]{2,1,0:T(8,128)(2,1)S(1)}, u32[]{:S(2)}, u32[]{:S(2)}) %collective-permute-start.24) | collective-permute-done | bytes 491552 | tf_op jit(solution)/shard_map/ppermute | solution.py:705
  69.4 2.7 %collective-permute-start.26 = (bf16[3,72,384]{2,1,0:T(8,128)(2,1)S(1)}, bf16[3,72,384]{2,1,0:T(8,128)(2,1)S(1)}, u32[]{:S(2)}, u32[]{:S(2)}) collective-permute-start(bf16[3,72,384]{2,1,0:T(8,128)(2,1)S(1)} %get-tuple-element.157), channel_id=1, source_target_pairs={{0,16},{2,18},{4,20},{6,22},{8,24},{10,26},{12,28},{14,30},{16,0},... | collective-permute-start | bytes 497672 | tf_op jit(solution)/shard_map/ppermute | solution.py:705
  72.9 3.9 %collective-permute-done.25.refs_1_ = bf16[2,72,384]{2,1,0:T(8,128)(2,1)S(1)} collective-permute-done((bf16[2,72,384]{2,1,0:T(8,128)(2,1)S(1)}, bf16[2,72,384]{2,1,0:T(8,128)(2,1)S(1)}, u32[]{:S(2)}, u32[]{:S(2)}) %collective-permute-start.25) | collective-permute-done | bytes 110624 | tf_op jit(solution)/shard_map/ppermute | solution.py:705
  76.8 2.0 %collective-permute-done.26.refs_3_ = bf16[3,72,384]{2,1,0:T(8,128)(2,1)S(1)} collective-permute-done((bf16[3,72,384]{2,1,0:T(8,128)(2,1)S(1)}, bf16[3,72,384]{2,1,0:T(8,128)(2,1)S(1)}, u32[]{:S(2)}, u32[]{:S(2)}) %collective-permute-start.26) | collective-permute-done | bytes 165920 | tf_op jit(solution)/shard_map/ppermute | solution.py:705
  79.0 3.2 %collective-permute-start.28 = (bf16[2,72,384]{2,1,0:T(8,128)(2,1)S(1)}, bf16[2,72,384]{2,1,0:T(8,128)(2,1)S(1)}, u32[]{:S(2)}, u32[]{:S(2)}) collective-permute-start(bf16[2,72,384]{2,1,0:T(8,128)(2,1)S(1)} %get-tuple-element.160.refs_0_), channel_id=1, source_target_pairs={{0,16},{2,18},{4,20},{6,22},{8,24},{10,26},{12,28},{14,30},{16,0},... | collective-permute-start | bytes 331784 | tf_op jit(solution)/shard_map/ppermute | solution.py:705
  82.1 1.1 collective-permute-start.29
  83.2 3.1 %collective-permute-done.29.refs_3_ = bf16[72,384]{1,0:T(8,128)(2,1)S(1)} collective-permute-done((bf16[72,384]{1,0:T(8,128)(2,1)S(1)}, bf16[72,384]{1,0:T(8,128)(2,1)S(1)}, u32[]{:S(2)}, u32[]{:S(2)}) %collective-permute-start.29) | collective-permute-done | bytes 55328 | tf_op jit(solution)/shard_map/ppermute | solution.py:705
  87.2 1.0 collective-permute-start.31
  88.2 1.9 %collective-permute-start.32 = (bf16[2,72,384]{2,1,0:T(8,128)(2,1)S(1)}, bf16[2,72,384]{2,1,0:T(8,128)(2,1)S(1)}, u32[]{:S(2)}, u32[]{:S(2)}) collective-permute-start(bf16[2,72,384]{2,1,0:T(8,128)(2,1)S(1)} %get-tuple-element.167.refs_3_), channel_id=1, source_target_pairs={{0,8},{2,10},{4,12},{6,14},{8,0},{10,2},{12,4},{14,6},{16,24},{18,... | collective-permute-start | bytes 331784 | tf_op jit(solution)/shard_map/ppermute | solution.py:705
  90.0 3.6 %collective-permute-done.32.refs_4_ = bf16[2,72,384]{2,1,0:T(8,128)(2,1)S(1)} collective-permute-done((bf16[2,72,384]{2,1,0:T(8,128)(2,1)S(1)}, bf16[2,72,384]{2,1,0:T(8,128)(2,1)S(1)}, u32[]{:S(2)}, u32[]{:S(2)}) %collective-permute-start.32) | collective-permute-done | bytes 110624 | tf_op jit(solution)/shard_map/ppermute | solution.py:705
  93.6 2.0 %collective-permute-done.31.refs_1_ = bf16[3,80,384]{2,1,0:T(8,128)(2,1)S(1)} collective-permute-done((bf16[3,80,384]{2,1,0:T(8,128)(2,1)S(1)}, bf16[3,80,384]{2,1,0:T(8,128)(2,1)S(1)}, u32[]{:S(2)}, u32[]{:S(2)}) %collective-permute-start.31) | collective-permute-done | bytes 184352 | tf_op jit(solution)/shard_map/ppermute | solution.py:705
  95.8 1.0 collective-permute-start.34
  97.0 2.5 %collective-permute-start.35 = (bf16[2,72,384]{2,1,0:T(8,128)(2,1)S(1)}, bf16[2,72,384]{2,1,0:T(8,128)(2,1)S(1)}, u32[]{:S(2)}, u32[]{:S(2)}) collective-permute-start(bf16[2,72,384]{2,1,0:T(8,128)(2,1)S(1)} %get-tuple-element.172.refs_2_), channel_id=1, source_target_pairs={{0,8},{2,10},{4,12},{6,14},{8,0},{10,2},{12,4},{14,6},{16,24},{18,... | collective-permute-start | bytes 331784 | tf_op jit(solution)/shard_map/ppermute | solution.py:705
  99.6 1.6 %finish_tokens.1 = (bf16[576,128]{1,0:T(8,128)(2,1)}, bf16[576,128]{1,0:T(8,128)(2,1)}) custom-call(f32[128,576]{1,0:T(8,128)S(1)} %copy-done.23, bf16[128,1536]{1,0:T(8,128)(2,1)S(1)} %get-tuple-element.114.refs_1_, bf16[576,1536]{1,0:T(8,128)(2,1)S(1)} %get-tuple-element.117.refs_2_, f32[128,576]{1,0:T(8,128)S(1)} %get-tuple-element.123.refs_4_.refs_1_.refs_3_, ...), custom_call_target="tpu_custom_call" | custom-call | flops 2000000000 | tf_op jit(solution)/shard_map/finish_tokens/pallas_call | solution.py:572
  101.1 0.9 collective-permute-done.33.refs_4_.refs_1_
  102.0 1.9 %collective-permute-done.35.refs_3_ = bf16[2,72,384]{2,1,0:T(8,128)(2,1)S(1)} collective-permute-done((bf16[2,72,384]{2,1,0:T(8,128)(2,1)S(1)}, bf16[2,72,384]{2,1,0:T(8,128)(2,1)S(1)}, u32[]{:S(2)}, u32[]{:S(2)}) %collective-permute-start.35) | collective-permute-done | bytes 110624 | tf_op jit(solution)/shard_map/ppermute | solution.py:705
  103.9 1.4 %collective-permute-done.34.refs_1_ = bf16[3,2,72,384]{3,2,1,0:T(8,128)(2,1)S(1)} collective-permute-done((bf16[3,2,72,384]{3,2,1,0:T(8,128)(2,1)S(1)}, bf16[3,2,72,384]{3,2,1,0:T(8,128)(2,1)S(1)}, u32[]{:S(2)}, u32[]{:S(2)}) %collective-permute-start.34) | collective-permute-done | bytes 331808 | tf_op jit(solution)/shard_map/ppermute | solution.py:705
  106.7 2.3 %collective-permute-start.38 = (bf16[2,80,384]{2,1,0:T(8,128)(2,1)S(1)}, bf16[2,80,384]{2,1,0:T(8,128)(2,1)S(1)}, u32[]{:S(2)}, u32[]{:S(2)}) collective-permute-start(bf16[2,80,384]{2,1,0:T(8,128)(2,1)S(1)} %share_qkv_out_high.1.refs_5_.refs_0_), channel_id=1, source_target_pairs={{0,12},{2,14},{4,8},{6,10},{8,4},{10,6},{12,0},{14,2},{16,28},{18,... | collective-permute-start | bytes 368648 | tf_op jit(solution)/shard_map/ppermute | solution.py:705
  109.2 1.1 collective-permute-start.36
  110.2 3.3 %update_down.1 = (f32[576,768]{1,0:T(8,128)}, f32[576,768]{1,0:T(8,128)}, f32[576,768]{1,0:T(8,128)}, f32[8,128]{1,0:T(8,128)S(1)}) custom-call(s32[4]{0:T(128)S(1)} %pad_add_fusion.idx_ref.refs_0_, bf16[1,2,4,72,384]{4,3,2,1,0:T(8,128)(2,1)S(1)} %get-tuple-element.175.refs_0_, bf16[1,2,4,72,384]{4,3,2,1,0:T(8,128)(2,1)S(1)} %collective-permute-done.41.refs_1_, ...), custom_call_target="tpu_custom_call" | custom-call | flops 100000000 | tf_op jit(solution)/shard_map/update_down/pallas_call | solution.py:686
  113.7 3.4 %update_gate_up_near.1 = (f32[288,3072]{1,0:T(8,128)}, f32[288,3072]{1,0:T(8,128)}, f32[288,3072]{1,0:T(8,128)}, f32[8,128]{1,0:T(8,128)S(1)}) custom-call(s32[4]{0:T(128)S(1)} %pad_add_fusion.idx_ref.refs_0_, bf16[2,2,4,72,384]{4,3,2,1,0:T(8,128)(2,1)S(1)} %share_gate_up.1.refs_0_, f32[288,3072]{1,0:T(8,128)S(1)} %copy-done.3, f32[288,3072]{1,0:T(8,128)S(1)} %copy-done.4, ...), custom_call_target="tpu_custom_call" | custom-call | flops 20000000000 | tf_op jit(solution)/shard_map/update_gate_up_near/pallas_call | solution.py:686
  117.8 3.4 %update_gate_up_far.1 = (f32[288,3072]{1,0:T(8,128)}, f32[288,3072]{1,0:T(8,128)}, f32[288,3072]{1,0:T(8,128)}, f32[8,128]{1,0:T(8,128)S(1)}) custom-call(s32[4]{0:T(128)S(1)} %pad_add_fusion.idx_ref.refs_0_, bf16[2,2,4,72,384]{4,3,2,1,0:T(8,128)(2,1)S(1)} %collective-permute-done.43.refs_0_, ...), custom_call_target="tpu_custom_call", output_to_operand_aliasing={{0}: (5, {}), {1}: (6, {}), {2}: (7, {})} | custom-call | flops 20000000000 | tf_op jit(solution)/shard_map/update_gate_up_far/pallas_call | solution.py:686
  121.1 4.3 %update_qkv_out.1 = (f32[288,960]{1,0:T(8,128)}, f32[288,576]{1,0:T(8,128)}, f32[288,960]{1,0:T(8,128)}, f32[288,576]{1,0:T(8,128)}, f32[288,960]{1,0:T(8,128)},...) custom-call(s32[4]{0:T(128)S(1)} %pad_add_fusion.idx_ref.refs_0_, ...), custom_call_target="tpu_custom_call" | custom-call | flops 20000000000 | tf_op jit(solution)/shard_map/update_qkv_out/pallas_call | solution.py:686
  (120 shorter events, 11.7 us)
Async XLA Ops:
  1.4 19.0 %copy-start = (f32[768,576]{0,1:T(8,128)S(1)}, f32[768,576]{0,1:T(8,128)}, u32[]{:S(2)}) copy-start(f32[768,576]{0,1:T(8,128)} %param.25) | copy-start | bytes 5308420
  3.6 16.7 %collective-permute-start = (bf16[160,768]{1,0:T(8,128)(2,1)S(1)}, bf16[160,768]{1,0:T(8,128)(2,1)S(1)}, u32[]{:S(2)}, u32[]{:S(2)}) collective-permute-start(bf16[160,768]{1,0:T(8,128)(2,1)S(1)} %get-tuple-element.107), channel_id=1, source_target_pairs={{0,1},{1,0},{2,3},{3,2},{4,5},{5,4},{6,7},{7,6},{8,9},{9,8},{10,11... | collective-permute-start | bytes 737288 | tf_op jit(solution)/shard_map/ppermute | solution.py:705
  6.7 11.5 %collective-permute-start.8 = (bf16[144,768]{1,0:T(8,128)(2,1)S(1)}, bf16[144,768]{1,0:T(8,128)(2,1)S(1)}, u32[]{:S(2)}, u32[]{:S(2)}) collective-permute-start(bf16[144,768]{1,0:T(8,128)(2,1)S(1)} %get-tuple-element.112), channel_id=1, source_target_pairs={{0,1},{1,0},{2,3},{3,2},{4,5},{5,4},{6,7},{7,6},{8,9},{9,8},{10,11... | collective-permute-start | bytes 663560 | tf_op jit(solution)/shard_map/ppermute | solution.py:705
  6.7 16.5 %collective-permute-start.4 = (bf16[144,768]{1,0:T(8,128)(2,1)S(1)}, bf16[144,768]{1,0:T(8,128)(2,1)S(1)}, u32[]{:S(2)}, u32[]{:S(2)}) collective-permute-start(bf16[144,768]{1,0:T(8,128)(2,1)S(1)} %get-tuple-element.111), channel_id=1, source_target_pairs={{0,1},{1,0},{2,3},{3,2},{4,5},{5,4},{6,7},{7,6},{8,9},{9,8},{10,11... | collective-permute-start | bytes 663560 | tf_op jit(solution)/shard_map/ppermute | solution.py:705
  18.2 7.9 %collective-permute-start.9 = (bf16[144,768]{1,0:T(8,128)(2,1)S(1)}, bf16[144,768]{1,0:T(8,128)(2,1)S(1)}, u32[]{:S(2)}, u32[]{:S(2)}) collective-permute-start(bf16[144,768]{1,0:T(8,128)(2,1)S(1)} %collective-permute-done.8.refs_11_.refs_1_), channel_id=1, source_target_pairs={{0,8},{2,10},{4,12},{6,14},{8,0},{10,2},{12,4},{14,6},{16,24},{18,... | collective-permute-start | bytes 663560 | tf_op jit(solution)/shard_map/ppermute | solution.py:705
  20.3 10.2 %collective-permute-start.2 = (bf16[160,768]{1,0:T(8,128)(2,1)S(1)}, bf16[160,768]{1,0:T(8,128)(2,1)S(1)}, u32[]{:S(2)}, u32[]{:S(2)}) collective-permute-start(bf16[160,768]{1,0:T(8,128)(2,1)S(1)} %collective-permute-done.refs_5_.refs_8_), channel_id=1, source_target_pairs={{0,2},{2,0},{4,6},{6,4},{8,10},{10,8},{12,14},{14,12},{16,18},{18,... | collective-permute-start | bytes 737288 | tf_op jit(solution)/shard_map/ppermute | solution.py:705
  20.3 9.2 %collective-permute-start.1 = (bf16[160,768]{1,0:T(8,128)(2,1)S(1)}, bf16[160,768]{1,0:T(8,128)(2,1)S(1)}, u32[]{:S(2)}, u32[]{:S(2)}) collective-permute-start(bf16[160,768]{1,0:T(8,128)(2,1)S(1)} %collective-permute-done.refs_5_.refs_8_), channel_id=1, source_target_pairs={{0,8},{2,10},{4,12},{6,14},{8,0},{10,2},{12,4},{14,6},{16,24},{18,... | collective-permute-start | bytes 737288 | tf_op jit(solution)/shard_map/ppermute | solution.py:705
  21.2 9.9 %copy-start.6 = (f32[288,960]{1,0:T(8,128)S(1)}, f32[288,960]{1,0:T(8,128)}, u32[]{:S(2)}) copy-start(f32[288,960]{1,0:T(8,128)} %refs_2_.9) | copy-start | bytes 3317764
  21.2 9.9 %copy-start.10 = (f32[288,576]{1,0:T(8,128)S(1)}, f32[288,576]{1,0:T(8,128)}, u32[]{:S(2)}) copy-start(f32[288,576]{1,0:T(8,128)} %refs_3_.8) | copy-start | bytes 1990660
  21.2 9.9 %copy-start.14 = (bf16[1,128,576]{1,2,0:T(8,128)(2,1)S(1)}, bf16[1,128,576]{1,2,0:T(8,128)(2,1)}, u32[]{:S(2)}) copy-start(bf16[1,128,576]{1,2,0:T(8,128)(2,1)} %param.19) | copy-start | bytes 442372
  21.2 12.6 %collective-permute-start.12 = (bf16[288,768]{1,0:T(8,128)(2,1)S(1)}, bf16[288,768]{1,0:T(8,128)(2,1)S(1)}, u32[]{:S(2)}, u32[]{:S(2)}) collective-permute-start(bf16[288,768]{1,0:T(8,128)(2,1)S(1)} %pack_down.1), channel_id=1, source_target_pairs={{0,1},{1,0},{2,3},{3,2},{4,5},{5,4},{6,7},{7,6},{8,9},{9,8},{10,11... | collective-permute-start | bytes 1327112 | tf_op jit(solution)/shard_map/ppermute | solution.py:705
  23.2 7.3 %collective-permute-start.5 = (bf16[144,768]{1,0:T(8,128)(2,1)S(1)}, bf16[144,768]{1,0:T(8,128)(2,1)S(1)}, u32[]{:S(2)}, u32[]{:S(2)}) collective-permute-start(bf16[144,768]{1,0:T(8,128)(2,1)S(1)} %collective-permute-done.4.refs_7_), channel_id=1, source_target_pairs={{0,4},{2,6},{4,0},{6,2},{8,12},{10,14},{12,8},{14,10},{16,20},{18,... | collective-permute-start | bytes 663560 | tf_op jit(solution)/shard_map/ppermute | solution.py:705
  26.1 4.9 %collective-permute-start.11 = (bf16[144,768]{1,0:T(8,128)(2,1)S(1)}, bf16[144,768]{1,0:T(8,128)(2,1)S(1)}, u32[]{:S(2)}, u32[]{:S(2)}) collective-permute-start(bf16[144,768]{1,0:T(8,128)(2,1)S(1)} %collective-permute-done.9.refs_12_), channel_id=1, source_target_pairs={{0,2},{2,0},{4,6},{6,4},{8,10},{10,8},{12,14},{14,12},{16,18},{18,... | collective-permute-start | bytes 663560 | tf_op jit(solution)/shard_map/ppermute | solution.py:705
  29.5 1.6 %collective-permute-start.3 = (bf16[160,768]{1,0:T(8,128)(2,1)S(1)}, bf16[160,768]{1,0:T(8,128)(2,1)S(1)}, u32[]{:S(2)}, u32[]{:S(2)}) collective-permute-start(bf16[160,768]{1,0:T(8,128)(2,1)S(1)} %collective-permute-done.1.refs_9_), channel_id=1, source_target_pairs={{0,2},{2,0},{4,6},{6,4},{8,10},{10,8},{12,14},{14,12},{16,18},{18,... | collective-permute-start | bytes 737288 | tf_op jit(solution)/shard_map/ppermute | solution.py:705
  30.5 3.8 %collective-permute-start.6 = (bf16[144,768]{1,0:T(8,128)(2,1)S(1)}, bf16[144,768]{1,0:T(8,128)(2,1)S(1)}, u32[]{:S(2)}, u32[]{:S(2)}) collective-permute-start(bf16[144,768]{1,0:T(8,128)(2,1)S(1)} %collective-permute-done.4.refs_7_), channel_id=1, source_target_pairs={{0,2},{2,0},{4,6},{6,4},{8,10},{10,8},{12,14},{14,12},{16,18},{18,... | collective-permute-start | bytes 663560 | tf_op jit(solution)/shard_map/ppermute | solution.py:705
  30.5 3.8 %collective-permute-start.10 = (bf16[144,768]{1,0:T(8,128)(2,1)S(1)}, bf16[144,768]{1,0:T(8,128)(2,1)S(1)}, u32[]{:S(2)}, u32[]{:S(2)}) collective-permute-start(bf16[144,768]{1,0:T(8,128)(2,1)S(1)} %collective-permute-done.8.refs_11_.refs_1_), channel_id=1, source_target_pairs={{0,2},{2,0},{4,6},{6,4},{8,10},{10,8},{12,14},{14,12},{16,18},{18,... | collective-permute-start | bytes 663560 | tf_op jit(solution)/shard_map/ppermute | solution.py:705
  31.0 3.3 %collective-permute-start.7 = (bf16[144,768]{1,0:T(8,128)(2,1)S(1)}, bf16[144,768]{1,0:T(8,128)(2,1)S(1)}, u32[]{:S(2)}, u32[]{:S(2)}) collective-permute-start(bf16[144,768]{1,0:T(8,128)(2,1)S(1)} %collective-permute-done.5.refs_8_), channel_id=1, source_target_pairs={{0,2},{2,0},{4,6},{6,4},{8,10},{10,8},{12,14},{14,12},{16,18},{18,... | collective-permute-start | bytes 663560 | tf_op jit(solution)/shard_map/ppermute | solution.py:705
  33.8 3.5 %collective-permute-start.13 = (bf16[288,768]{1,0:T(8,128)(2,1)S(1)}, bf16[288,768]{1,0:T(8,128)(2,1)S(1)}, u32[]{:S(2)}, u32[]{:S(2)}) collective-permute-start(bf16[288,768]{1,0:T(8,128)(2,1)S(1)} %pass_on.1.refs_5_), channel_id=1, source_target_pairs={{0,2},{2,0},{4,6},{6,4},{8,10},{10,8},{12,14},{14,12},{16,18},{18,... | collective-permute-start | bytes 1327112 | tf_op jit(solution)/shard_map/ppermute | solution.py:705
  37.2 3.5 %collective-permute-start.14 = (bf16[1,2,8,72,384]{4,3,2,1,0:T(8,128)(2,1)S(1)}, bf16[1,2,8,72,384]{4,3,2,1,0:T(8,128)(2,1)S(1)}, u32[]{:S(2)}, u32[]{:S(2)}) collective-permute-start(bf16[1,2,8,72,384]{4,3,2,1,0:T(8,128)(2,1)S(1)} %get-tuple-element.121), channel_id=1, source_target_pairs={{0,2},{2,0},{4,6},{6,4},{8,10},{10,8},{12,14},{14,12},{16,18},{18,... | collective-permute-start | bytes 2654216 | tf_op jit(solution)/shard_map/ppermute | solution.py:705
  40.0 5.2 %collective-permute-start.15 = (bf16[2,2,8,72,384]{4,3,2,1,0:T(8,128)(2,1)S(1)}, bf16[2,2,8,72,384]{4,3,2,1,0:T(8,128)(2,1)S(1)}, u32[]{:S(2)}, u32[]{:S(2)}) collective-permute-start(bf16[2,2,8,72,384]{4,3,2,1,0:T(8,128)(2,1)S(1)} %get-tuple-element.132), channel_id=1, source_target_pairs={{0,2},{2,0},{4,6},{6,4},{8,10},{10,8},{12,14},{14,12},{16,18},{18,... | collective-permute-start | bytes 5308424 | tf_op jit(solution)/shard_map/ppermute | solution.py:705
  40.9 12.3 %collective-permute-start.19 = (bf16[8,72,384]{2,1,0:T(8,128)(2,1)S(1)}, bf16[8,72,384]{2,1,0:T(8,128)(2,1)S(1)}, u32[]{:S(2)}, u32[]{:S(2)}) collective-permute-start(bf16[8,72,384]{2,1,0:T(8,128)(2,1)S(1)} %get-tuple-element.141), channel_id=1, source_target_pairs={{0,1},{1,0},{2,3},{3,2},{4,5},{5,4},{6,7},{7,6},{8,9},{9,8},{10,11... | collective-permute-start | bytes 1327112 | tf_op jit(solution)/shard_map/ppermute | solution.py:705
  45.8 13.1 %collective-permute-start.16 = (bf16[2,4,72,384]{3,2,1,0:T(8,128)(2,1)S(1)}, bf16[2,4,72,384]{3,2,1,0:T(8,128)(2,1)S(1)}, u32[]{:S(2)}, u32[]{:S(2)}) collective-permute-start(bf16[2,4,72,384]{3,2,1,0:T(8,128)(2,1)S(1)} %get-tuple-element.136), channel_id=1, source_target_pairs={{0,4},{2,6},{4,0},{6,2},{8,12},{10,14},{12,8},{14,10},{16,20},{18,... | collective-permute-start | bytes 1327112 | tf_op jit(solution)/shard_map/ppermute | solution.py:705
  47.3 11.9 %collective-permute-start.17 = (bf16[4,2,72,384]{3,2,1,0:T(8,128)(2,1)S(1)}, bf16[4,2,72,384]{3,2,1,0:T(8,128)(2,1)S(1)}, u32[]{:S(2)}, u32[]{:S(2)}) collective-permute-start(bf16[4,2,72,384]{3,2,1,0:T(8,128)(2,1)S(1)} %get-tuple-element.138), channel_id=1, source_target_pairs={{0,8},{2,10},{4,12},{6,14},{8,0},{10,2},{12,4},{14,6},{16,24},{18,... | collective-permute-start | bytes 1327112 | tf_op jit(solution)/shard_map/ppermute | solution.py:705
  52.3 2.8 %collective-permute-start.18 = (bf16[1,2,8,80,384]{4,3,2,1,0:T(8,128)(2,1)S(1)}, bf16[1,2,8,80,384]{4,3,2,1,0:T(8,128)(2,1)S(1)}, u32[]{:S(2)}, u32[]{:S(2)}) collective-permute-start(bf16[1,2,8,80,384]{4,3,2,1,0:T(8,128)(2,1)S(1)} %get-tuple-element.140), channel_id=1, source_target_pairs={{0,2},{2,0},{4,6},{6,4},{8,10},{10,8},{12,14},{14,12},{16,18},{18,... | collective-permute-start | bytes 2949128 | tf_op jit(solution)/shard_map/ppermute | solution.py:705
  53.3 9.9 %collective-permute-start.22 = (bf16[4,72,384]{2,1,0:T(8,128)(2,1)S(1)}, bf16[4,72,384]{2,1,0:T(8,128)(2,1)S(1)}, u32[]{:S(2)}, u32[]{:S(2)}) collective-permute-start(bf16[4,72,384]{2,1,0:T(8,128)(2,1)S(1)} %get-tuple-element.149), channel_id=1, source_target_pairs={{0,4},{2,6},{4,0},{6,2},{8,12},{10,14},{12,8},{14,10},{16,20},{18,... | collective-permute-start | bytes 663560 | tf_op jit(solution)/shard_map/ppermute | solution.py:705
  55.4 13.2 %collective-permute-start.24 = (bf16[8,80,384]{2,1,0:T(8,128)(2,1)S(1)}, bf16[8,80,384]{2,1,0:T(8,128)(2,1)S(1)}, u32[]{:S(2)}, u32[]{:S(2)}) collective-permute-start(bf16[8,80,384]{2,1,0:T(8,128)(2,1)S(1)} %get-tuple-element.152), channel_id=1, source_target_pairs={{0,1},{1,0},{2,3},{3,2},{4,5},{5,4},{6,7},{7,6},{8,9},{9,8},{10,11... | collective-permute-start | bytes 1474568 | tf_op jit(solution)/shard_map/ppermute | solution.py:705
  59.4 9.9 %collective-permute-start.20 = (bf16[2,2,72,384]{3,2,1,0:T(8,128)(2,1)S(1)}, bf16[2,2,72,384]{3,2,1,0:T(8,128)(2,1)S(1)}, u32[]{:S(2)}, u32[]{:S(2)}) collective-permute-start(bf16[2,2,72,384]{3,2,1,0:T(8,128)(2,1)S(1)} %get-tuple-element.146), channel_id=1, source_target_pairs={{0,8},{2,10},{4,12},{6,14},{8,0},{10,2},{12,4},{14,6},{16,24},{18,... | collective-permute-start | bytes 663560 | tf_op jit(solution)/shard_map/ppermute | solution.py:705
  61.0 8.3 %collective-permute-start.21 = (bf16[2,2,72,384]{3,2,1,0:T(8,128)(2,1)S(1)}, bf16[2,2,72,384]{3,2,1,0:T(8,128)(2,1)S(1)}, u32[]{:S(2)}, u32[]{:S(2)}) collective-permute-start(bf16[2,2,72,384]{3,2,1,0:T(8,128)(2,1)S(1)} %get-tuple-element.148), channel_id=1, source_target_pairs={{0,4},{2,6},{4,0},{6,2},{8,12},{10,14},{12,8},{14,10},{16,20},{18,... | collective-permute-start | bytes 663560 | tf_op jit(solution)/shard_map/ppermute | solution.py:705
  63.2 6.1 %collective-permute-start.23 = (bf16[2,72,384]{2,1,0:T(8,128)(2,1)S(1)}, bf16[2,72,384]{2,1,0:T(8,128)(2,1)S(1)}, u32[]{:S(2)}, u32[]{:S(2)}) collective-permute-start(bf16[2,72,384]{2,1,0:T(8,128)(2,1)S(1)} %get-tuple-element.151), channel_id=1, source_target_pairs={{0,8},{2,10},{4,12},{6,14},{8,0},{10,2},{12,4},{14,6},{16,24},{18,... | collective-permute-start | bytes 331784 | tf_op jit(solution)/shard_map/ppermute | solution.py:705
  68.7 10.1 %collective-permute-start.27 = (bf16[4,80,384]{2,1,0:T(8,128)(2,1)S(1)}, bf16[4,80,384]{2,1,0:T(8,128)(2,1)S(1)}, u32[]{:S(2)}, u32[]{:S(2)}) collective-permute-start(bf16[4,80,384]{2,1,0:T(8,128)(2,1)S(1)} %get-tuple-element.159), channel_id=1, source_target_pairs={{0,4},{2,6},{4,0},{6,2},{8,12},{10,14},{12,8},{14,10},{16,20},{18,... | collective-permute-start | bytes 737288 | tf_op jit(solution)/shard_map/ppermute | solution.py:705
  69.4 9.4 %collective-permute-start.26 = (bf16[3,72,384]{2,1,0:T(8,128)(2,1)S(1)}, bf16[3,72,384]{2,1,0:T(8,128)(2,1)S(1)}, u32[]{:S(2)}, u32[]{:S(2)}) collective-permute-start(bf16[3,72,384]{2,1,0:T(8,128)(2,1)S(1)} %get-tuple-element.157), channel_id=1, source_target_pairs={{0,16},{2,18},{4,20},{6,22},{8,24},{10,26},{12,28},{14,30},{16,0},... | collective-permute-start | bytes 497672 | tf_op jit(solution)/shard_map/ppermute | solution.py:705
  72.1 4.7 %collective-permute-start.25 = (bf16[2,72,384]{2,1,0:T(8,128)(2,1)S(1)}, bf16[2,72,384]{2,1,0:T(8,128)(2,1)S(1)}, u32[]{:S(2)}, u32[]{:S(2)}) collective-permute-start(bf16[2,72,384]{2,1,0:T(8,128)(2,1)S(1)} %get-tuple-element.155), channel_id=1, source_target_pairs={{0,1},{1,0},{2,3},{3,2},{4,5},{5,4},{6,7},{7,6},{8,9},{9,8},{10,11... | collective-permute-start | bytes 331784 | tf_op jit(solution)/shard_map/ppermute | solution.py:705
  78.9 8.1 %collective-permute-start.30 = (bf16[2,80,384]{2,1,0:T(8,128)(2,1)S(1)}, bf16[2,80,384]{2,1,0:T(8,128)(2,1)S(1)}, u32[]{:S(2)}, u32[]{:S(2)}) collective-permute-start(bf16[2,80,384]{2,1,0:T(8,128)(2,1)S(1)} %get-tuple-element.164), channel_id=1, source_target_pairs={{0,8},{2,10},{4,12},{6,14},{8,0},{10,2},{12,4},{14,6},{16,24},{18,... | collective-permute-start | bytes 368648 | tf_op jit(solution)/shard_map/ppermute | solution.py:705
  79.0 8.0 %collective-permute-start.28 = (bf16[2,72,384]{2,1,0:T(8,128)(2,1)S(1)}, bf16[2,72,384]{2,1,0:T(8,128)(2,1)S(1)}, u32[]{:S(2)}, u32[]{:S(2)}) collective-permute-start(bf16[2,72,384]{2,1,0:T(8,128)(2,1)S(1)} %get-tuple-element.160.refs_0_), channel_id=1, source_target_pairs={{0,16},{2,18},{4,20},{6,22},{8,24},{10,26},{12,28},{14,30},{16,0},... | collective-permute-start | bytes 331784 | tf_op jit(solution)/shard_map/ppermute | solution.py:705
  82.1 4.2 %collective-permute-start.29 = (bf16[72,384]{1,0:T(8,128)(2,1)S(1)}, bf16[72,384]{1,0:T(8,128)(2,1)S(1)}, u32[]{:S(2)}, u32[]{:S(2)}) collective-permute-start(bf16[72,384]{1,0:T(8,128)(2,1)S(1)} %get-tuple-element.162), channel_id=1, source_target_pairs={{0,1},{1,0},{2,3},{3,2},{4,5},{5,4},{6,7},{7,6},{8,9},{9,8},{10,11... | collective-permute-start | bytes 165896 | tf_op jit(solution)/shard_map/ppermute | solution.py:705
  87.2 8.5 %collective-permute-start.31 = (bf16[3,80,384]{2,1,0:T(8,128)(2,1)S(1)}, bf16[3,80,384]{2,1,0:T(8,128)(2,1)S(1)}, u32[]{:S(2)}, u32[]{:S(2)}) collective-permute-start(bf16[3,80,384]{2,1,0:T(8,128)(2,1)S(1)} %get-tuple-element.165.refs_0_), channel_id=1, source_target_pairs={{0,16},{2,18},{4,20},{6,22},{8,24},{10,26},{12,28},{14,30},{16,0},... | collective-permute-start | bytes 552968 | tf_op jit(solution)/shard_map/ppermute | solution.py:705
  88.2 5.5 %collective-permute-start.32 = (bf16[2,72,384]{2,1,0:T(8,128)(2,1)S(1)}, bf16[2,72,384]{2,1,0:T(8,128)(2,1)S(1)}, u32[]{:S(2)}, u32[]{:S(2)}) collective-permute-start(bf16[2,72,384]{2,1,0:T(8,128)(2,1)S(1)} %get-tuple-element.167.refs_3_), channel_id=1, source_target_pairs={{0,8},{2,10},{4,12},{6,14},{8,0},{10,2},{12,4},{14,6},{16,24},{18,... | collective-permute-start | bytes 331784 | tf_op jit(solution)/shard_map/ppermute | solution.py:705
  95.8 9.5 %collective-permute-start.34 = (bf16[3,2,72,384]{3,2,1,0:T(8,128)(2,1)S(1)}, bf16[3,2,72,384]{3,2,1,0:T(8,128)(2,1)S(1)}, u32[]{:S(2)}, u32[]{:S(2)}) collective-permute-start(bf16[3,2,72,384]{3,2,1,0:T(8,128)(2,1)S(1)} %get-tuple-element.168.refs_8_.refs_0_), channel_id=1, source_target_pairs={{0,4},{2,6},{4,0},{6,2},{8,12},{10,14},{12,8},{14,10},{16,20},{18,... | collective-permute-start | bytes 995336 | tf_op jit(solution)/shard_map/ppermute | solution.py:705
  96.8 5.2 %collective-permute-start.33 = (bf16[80,384]{1,0:T(8,128)(2,1)S(1)}, bf16[80,384]{1,0:T(8,128)(2,1)S(1)}, u32[]{:S(2)}, u32[]{:S(2)}) collective-permute-start(bf16[80,384]{1,0:T(8,128)(2,1)S(1)} %get-tuple-element.171.refs_0_), channel_id=1, source_target_pairs={{0,16},{2,18},{4,20},{6,22},{8,24},{10,26},{12,28},{14,30},{16,0},... | collective-permute-start | bytes 184328 | tf_op jit(solution)/shard_map/ppermute | solution.py:705
  97.0 6.9 %collective-permute-start.35 = (bf16[2,72,384]{2,1,0:T(8,128)(2,1)S(1)}, bf16[2,72,384]{2,1,0:T(8,128)(2,1)S(1)}, u32[]{:S(2)}, u32[]{:S(2)}) collective-permute-start(bf16[2,72,384]{2,1,0:T(8,128)(2,1)S(1)} %get-tuple-element.172.refs_2_), channel_id=1, source_target_pairs={{0,8},{2,10},{4,12},{6,14},{8,0},{10,2},{12,4},{14,6},{16,24},{18,... | collective-permute-start | bytes 331784 | tf_op jit(solution)/shard_map/ppermute | solution.py:705
  105.4 8.2 %collective-permute-start.40 = (bf16[2,2,72,384]{3,2,1,0:T(8,128)(2,1)S(1)}, bf16[2,2,72,384]{3,2,1,0:T(8,128)(2,1)S(1)}, u32[]{:S(2)}, u32[]{:S(2)}) collective-permute-start(bf16[2,2,72,384]{3,2,1,0:T(8,128)(2,1)S(1)} %get-tuple-element.174.refs_2_), channel_id=1, source_target_pairs={{0,4},{2,6},{4,0},{6,2},{8,12},{10,14},{12,8},{14,10},{16,20},{18,... | collective-permute-start | bytes 663560 | tf_op jit(solution)/shard_map/ppermute | solution.py:705
  105.9 7.7 %collective-permute-start.39 = (bf16[2,2,72,384]{3,2,1,0:T(8,128)(2,1)S(1)}, bf16[2,2,72,384]{3,2,1,0:T(8,128)(2,1)S(1)}, u32[]{:S(2)}, u32[]{:S(2)}) collective-permute-start(bf16[2,2,72,384]{3,2,1,0:T(8,128)(2,1)S(1)} %get-tuple-element.173.refs_2_.refs_0_), channel_id=1, source_target_pairs={{0,8},{2,10},{4,12},{6,14},{8,0},{10,2},{12,4},{14,6},{16,24},{18,... | collective-permute-start | bytes 663560 | tf_op jit(solution)/shard_map/ppermute | solution.py:705
  106.6 2.5 %collective-permute-start.41 = (bf16[1,2,4,72,384]{4,3,2,1,0:T(8,128)(2,1)S(1)}, bf16[1,2,4,72,384]{4,3,2,1,0:T(8,128)(2,1)S(1)}, u32[]{:S(2)}, u32[]{:S(2)}) collective-permute-start(bf16[1,2,4,72,384]{4,3,2,1,0:T(8,128)(2,1)S(1)} %get-tuple-element.175.refs_0_), channel_id=1, source_target_pairs={{0,2},{2,0},{4,6},{6,4},{8,10},{10,8},{12,14},{14,12},{16,18},{18,... | collective-permute-start | bytes 1327112 | tf_op jit(solution)/shard_map/ppermute | solution.py:705
  106.7 10.5 %collective-permute-start.38 = (bf16[2,80,384]{2,1,0:T(8,128)(2,1)S(1)}, bf16[2,80,384]{2,1,0:T(8,128)(2,1)S(1)}, u32[]{:S(2)}, u32[]{:S(2)}) collective-permute-start(bf16[2,80,384]{2,1,0:T(8,128)(2,1)S(1)} %share_qkv_out_high.1.refs_5_.refs_0_), channel_id=1, source_target_pairs={{0,12},{2,14},{4,8},{6,10},{8,4},{10,6},{12,0},{14,2},{16,28},{18,... | collective-permute-start | bytes 368648 | tf_op jit(solution)/shard_map/ppermute | solution.py:705
  109.0 8.1 %collective-permute-start.37 = (bf16[2,80,384]{2,1,0:T(8,128)(2,1)S(1)}, bf16[2,80,384]{2,1,0:T(8,128)(2,1)S(1)}, u32[]{:S(2)}, u32[]{:S(2)}) collective-permute-start(bf16[2,80,384]{2,1,0:T(8,128)(2,1)S(1)} %share_qkv_out_high.1.refs_5_.refs_0_), channel_id=1, source_target_pairs={{0,8},{2,10},{4,12},{6,14},{8,0},{10,2},{12,4},{14,6},{16,24},{18,... | collective-permute-start | bytes 368648 | tf_op jit(solution)/shard_map/ppermute | solution.py:705
  109.2 8.0 %collective-permute-start.36 = (bf16[2,80,384]{2,1,0:T(8,128)(2,1)S(1)}, bf16[2,80,384]{2,1,0:T(8,128)(2,1)S(1)}, u32[]{:S(2)}, u32[]{:S(2)}) collective-permute-start(bf16[2,80,384]{2,1,0:T(8,128)(2,1)S(1)} %share_qkv_out_high.1.refs_5_.refs_0_), channel_id=1, source_target_pairs={{0,4},{2,6},{4,0},{6,2},{8,12},{10,14},{12,8},{14,10},{16,20},{18,... | collective-permute-start | bytes 368648 | tf_op jit(solution)/shard_map/ppermute | solution.py:705
  113.7 4.1 %collective-permute-start.43 = (bf16[2,2,4,72,384]{4,3,2,1,0:T(8,128)(2,1)S(1)}, bf16[2,2,4,72,384]{4,3,2,1,0:T(8,128)(2,1)S(1)}, u32[]{:S(2)}, u32[]{:S(2)}) collective-permute-start(bf16[2,2,4,72,384]{4,3,2,1,0:T(8,128)(2,1)S(1)} %share_gate_up.1.refs_0_), channel_id=1, source_target_pairs={{0,2},{2,0},{4,6},{6,4},{8,10},{10,8},{12,14},{14,12},{16,18},{18,... | collective-permute-start | bytes 2654216 | tf_op jit(solution)/shard_map/ppermute | solution.py:705
  117.2 3.9 %collective-permute-start.42 = (bf16[1,2,4,80,384]{4,3,2,1,0:T(8,128)(2,1)S(1)}, bf16[1,2,4,80,384]{4,3,2,1,0:T(8,128)(2,1)S(1)}, u32[]{:S(2)}, u32[]{:S(2)}) collective-permute-start(bf16[1,2,4,80,384]{4,3,2,1,0:T(8,128)(2,1)S(1)} %share_qkv_out.1.refs_7_.refs_0_), channel_id=1, source_target_pairs={{0,2},{2,0},{4,6},{6,4},{8,10},{10,8},{12,14},{14,12},{16,18},{18,... | collective-permute-start | bytes 1474568 | tf_op jit(solution)/shard_map/ppermute | solution.py:705
  (20 other events, 148.7 us)
